TPU v7x, 32 devices: a whole 2x2x4 slice. The times are simulated.
32 devices in a mesh: seq: 8 (over y, x, core), head: 4 (over z).
Axes of the slice: x: 2, y: 2, z: 4, core: 2. Of those that a mesh axis runs over, the one named last changes fastest.
Arguments:
- normed_input: bfloat16 [1024, 2304], P('seq'), may hold values from -6 to 6
- stored_queries: bfloat16 [1024, 2048], P('seq', 'head'), may hold values from -50 to 50
- stored_keys: bfloat16 [1024, 1024], P('seq', 'head'), may hold values from -4 to 4
- stored_values: bfloat16 [1024, 1024], P('seq', 'head'), may hold values from -6 to 6
- query_weight: bfloat16 [2304, 2048], P(None, 'head'), may hold values from -0.125 to 0.125
- key_matrix: bfloat16 [2304, 1024], P(None, 'head'), may hold values from -0.125 to 0.125
- value_matrix: bfloat16 [2304, 1024], P(None, 'head'), may hold values from -0.125 to 0.125
- output_weight: bfloat16 [2048, 2304], P('head'), may hold values from -0.125 to 0.125
- out_cotangent: bfloat16 [1024, 2304], P('seq'), may hold values from -48 to 48
Outputs:
- grad_input: bfloat16 [1024, 2304], P('seq', 'head')
- grad_wvalue: float32 [2304, 1024], P('seq', 'head')
- grad_woutput: float32 [2048, 2304], P('head', 'seq')
All inputs are finite; a program needn't handle non-finite values.
Results may differ from a plain program's by a relative error of at most 0.033.
Values may be sent and summed in bfloat16 or wider, within the bound.
No kernel may reach another device: no remote copies, remote signals or barrier semaphores. Data moves between devices by JAX's collectives and lax.ppermute only.
A program may use at most 128 MiB of HBM per device.

v0:
```python
import jax
import jax.numpy as jnp
from jax import lax
from jax.sharding import PartitionSpec as P

HEAD_SIZE = 128
WINDOW_LENGTH = 4096
QUERIES_PER_KEY = 2


logit_scale = 1.0 / 12.0


def passed_along(value, axis, steps):
    count = lax.axis_size(axis)
    leading, last = (max(0, -steps), min(count, count - steps))
    return lax.ppermute(value, axis, [(source, source + steps) for source in range(leading, last)])


def local(
    normed_input,
    stored_queries,
    stored_keys,
    stored_values,
    query_weight,
    key_matrix,
    value_matrix,
    output_weight,
    out_cotangent,
):
    tok_rows = normed_input.shape[0]
    blocks_seq = lax.axis_size("seq")
    seq_place = lax.axis_index("seq")
    reach_blocks = min(WINDOW_LENGTH // tok_rows, blocks_seq - 1)
    kv_heads = stored_keys.shape[1] // HEAD_SIZE
    output_gradient = jnp.dot(
        out_cotangent, output_weight.T, preferred_element_type=jnp.float32
    ).astype(jnp.bfloat16)
    pieces = [(stored_keys, stored_values)]
    current = (stored_keys, stored_values)
    for relay_step in range(reach_blocks):
        current = passed_along((current[0], current[1]), "seq", 1)
        pieces = [current] + pieces
    key_window = jnp.concatenate([piece[0] for piece in pieces], axis=0)
    value_window = jnp.concatenate([piece[1] for piece in pieces], axis=0)
    key_span = key_window.shape[0]
    query_pos = seq_place * tok_rows + jnp.arange(tok_rows, dtype=jnp.int32)
    key_pos = (seq_place - reach_blocks) * tok_rows + jnp.arange(key_span, dtype=jnp.int32)
    pos_gap = query_pos[:, None] - key_pos[None, :]
    allowed = (pos_gap >= 0) & (pos_gap < WINDOW_LENGTH) & (key_pos >= 0)[None, :]
    allowed_rows = jnp.tile(allowed, (QUERIES_PER_KEY, 1))
    query_stack = (
        stored_queries.reshape(tok_rows, kv_heads, QUERIES_PER_KEY, HEAD_SIZE)
        .transpose(1, 2, 0, 3)
        .reshape(kv_heads, QUERIES_PER_KEY * tok_rows, HEAD_SIZE)
    )
    grad_stack = (
        output_gradient.reshape(tok_rows, kv_heads, QUERIES_PER_KEY, HEAD_SIZE)
        .transpose(1, 2, 0, 3)
        .reshape(kv_heads, QUERIES_PER_KEY * tok_rows, HEAD_SIZE)
    )
    key_stack = key_window.reshape(key_span, kv_heads, HEAD_SIZE).transpose(1, 0, 2)
    value_stack = value_window.reshape(key_span, kv_heads, HEAD_SIZE).transpose(1, 0, 2)

    def per_head(head_items):
        query_head, key_head, value_head, grad_head = head_items
        attention_logits = logit_scale * jnp.dot(
            query_head, key_head.T, preferred_element_type=jnp.float32
        )
        masked = jnp.where(allowed_rows, attention_logits, -jnp.inf)
        row_top = jnp.max(masked, axis=1, keepdims=True)
        exp_scores = jnp.exp(masked - row_top)
        attn_prob = exp_scores / jnp.sum(exp_scores, axis=1, keepdims=True)
        probability_halfwidth = attn_prob.astype(jnp.bfloat16)
        attn_head = jnp.dot(
            probability_halfwidth, value_head, preferred_element_type=jnp.float32
        ).astype(jnp.bfloat16)
        row_delta = jnp.sum(
            grad_head.astype(jnp.float32) * attn_head.astype(jnp.float32), axis=1, keepdims=True
        )
        probability_gradient = jnp.dot(grad_head, value_head.T, preferred_element_type=jnp.float32)
        score_gradient = (attn_prob * (probability_gradient - row_delta)).astype(jnp.bfloat16)
        qgrad_head = (
            logit_scale * jnp.dot(score_gradient, key_head, preferred_element_type=jnp.float32)
        ).astype(jnp.bfloat16)
        key_partial = logit_scale * jnp.dot(
            score_gradient.T, query_head, preferred_element_type=jnp.float32
        )
        value_partial = jnp.dot(
            probability_halfwidth.T, grad_head, preferred_element_type=jnp.float32
        )
        return (attn_head, qgrad_head, key_partial, value_partial)

    attn_all, qgrad_all, key_all, value_all = lax.map(
        per_head, (query_stack, key_stack, value_stack, grad_stack)
    )
    attention_output = (
        attn_all.reshape(kv_heads, QUERIES_PER_KEY, tok_rows, HEAD_SIZE)
        .transpose(2, 0, 1, 3)
        .reshape(tok_rows, kv_heads * QUERIES_PER_KEY * HEAD_SIZE)
    )
    query_gradient = (
        qgrad_all.reshape(kv_heads, QUERIES_PER_KEY, tok_rows, HEAD_SIZE)
        .transpose(2, 0, 1, 3)
        .reshape(tok_rows, kv_heads * QUERIES_PER_KEY * HEAD_SIZE)
    )
    key_terms = key_all.transpose(1, 0, 2).reshape(key_span, kv_heads * HEAD_SIZE)
    value_terms = value_all.transpose(1, 0, 2).reshape(key_span, kv_heads * HEAD_SIZE)

    def take_slot(terms, slot_index):
        return terms[slot_index * tok_rows : (slot_index + 1) * tok_rows]

    key_sum = take_slot(key_terms, reach_blocks)
    value_sum = take_slot(value_terms, reach_blocks)
    for distance in range(1, reach_blocks + 1):
        received = passed_along(
            (
                take_slot(key_terms, reach_blocks - distance),
                take_slot(value_terms, reach_blocks - distance),
            ),
            "seq",
            -distance,
        )
        key_sum = key_sum + received[0]
        value_sum = value_sum + received[1]
    grad_key = key_sum.astype(jnp.bfloat16)
    grad_value = value_sum.astype(jnp.bfloat16)
    input_terms = jnp.dot(query_gradient, query_weight.T, preferred_element_type=jnp.float32)
    input_terms = input_terms + jnp.dot(grad_key, key_matrix.T, preferred_element_type=jnp.float32)
    input_terms = input_terms + jnp.dot(
        grad_value, value_matrix.T, preferred_element_type=jnp.float32
    )
    grad_input = lax.psum_scatter(input_terms, "head", scatter_dimension=1, tiled=True).astype(
        jnp.bfloat16
    )
    value_cols = grad_value.shape[1]
    input_cols = normed_input.T
    cot_cols = out_cotangent.T
    gathered = lax.psum_scatter(
        jnp.concatenate(
            [
                jnp.dot(input_cols, grad_value, preferred_element_type=jnp.float32),
                jnp.dot(cot_cols, attention_output, preferred_element_type=jnp.float32),
            ],
            axis=1,
        ),
        "seq",
        scatter_dimension=0,
        tiled=True,
    )
    grad_wvalue = gathered[:, :value_cols]
    grad_woutput = gathered[:, value_cols:].T
    return (grad_input, grad_wvalue, grad_woutput)


def solution(mesh):
    placed = (
        P("seq", None),
        P("seq", "head"),
        P("seq", "head"),
        P("seq", "head"),
        P(None, "head"),
        P(None, "head"),
        P(None, "head"),
        P("head", None),
        P("seq", None),
    )
    return jax.shard_map(
        local,
        mesh=mesh,
        in_specs=placed,
        out_specs=(P("seq", "head"), P("seq", "head"), P("head", "seq")),
        check_vma=False,
    )
```

profile of v0, /device:TPU:0, one launch (start us, length us, event | category | flops | bytes accessed | tf_op | source)
XLA Modules:
  0.0 226.6 jit_solution(141545560436078440)
XLA Ops:
  8.3 2.4 %collective-permute-start = (bf16[128,256]{0,1:T(8,128)(2,1)S(1)}, bf16[128,256]{0,1:T(8,128)(2,1)S(1)}, u32[]{:S(2)}, u32[]{:S(2)}) collective-permute-start(bf16[128,256]{0,1:T(8,128)(2,1)S(1)} %copy.47), channel_id=1, source_target_pairs={{0,4},{4,8},{8,12},{12,16},{16,20},{20,24},{24,28},{1,5},{5,9},{9,... | collective-permute-start | bytes 196616 | tf_op jit(solution)/shard_map/ppermute | solution.py:17
  11.7 4.5 %collective-permute-start.7 = (bf16[128,256]{0,1:T(8,128)(2,1)S(1)}, bf16[128,256]{0,1:T(8,128)(2,1)S(1)}, u32[]{:S(2)}, u32[]{:S(2)}) collective-permute-start(bf16[128,256]{0,1:T(8,128)(2,1)S(1)} %copy.49), channel_id=1, source_target_pairs={{0,4},{4,8},{8,12},{12,16},{16,20},{20,24},{24,28},{1,5},{5,9},{9,... | collective-permute-start | bytes 196616 | tf_op jit(solution)/shard_map/ppermute | solution.py:17
  16.2 1.9 collective-permute-start.1
  18.1 3.5 %collective-permute-start.8 = (bf16[128,256]{0,1:T(8,128)(2,1)S(1)}, bf16[128,256]{0,1:T(8,128)(2,1)S(1)}, u32[]{:S(2)}, u32[]{:S(2)}) collective-permute-start(bf16[128,256]{0,1:T(8,128)(2,1)S(1)} %collective-permute-done.7), channel_id=1, source_target_pairs={{0,4},{4,8},{8,12},{12,16},{16,20},{20,24},{24,28},{1,5},{5,9},{9,... | collective-permute-start | bytes 196616 | tf_op jit(solution)/shard_map/ppermute | solution.py:17
  21.7 2.0 collective-permute-start.2
  23.7 2.8 %convolution_convert_fusion.1 = bf16[128,512]{1,0:T(8,128)(2,1)S(1)} fusion(bf16[128,2304]{1,0:T(8,128)(2,1)} %param.19, bf16[512,2304]{1,0:T(8,128)(2,1)} %param.18), kind=kOutput, calls=%fused_computation.50 | convolution fusion | flops 302055424 | bytes 3080192 | tf_op jit(solution)/shard_map/dot_general | solution.py:36
  26.5 3.5 %collective-permute-start.9 = (bf16[128,256]{0,1:T(8,128)(2,1)S(1)}, bf16[128,256]{0,1:T(8,128)(2,1)S(1)}, u32[]{:S(2)}, u32[]{:S(2)}) collective-permute-start(bf16[128,256]{0,1:T(8,128)(2,1)S(1)} %collective-permute-done.8), channel_id=1, source_target_pairs={{0,4},{4,8},{8,12},{12,16},{16,20},{20,24},{24,28},{1,5},{5,9},{9,... | collective-permute-start | bytes 196616 | tf_op jit(solution)/shard_map/ppermute | solution.py:17
  30.0 2.8 %collective-permute-start.3 = (bf16[128,256]{0,1:T(8,128)(2,1)S(1)}, bf16[128,256]{0,1:T(8,128)(2,1)S(1)}, u32[]{:S(2)}, u32[]{:S(2)}) collective-permute-start(bf16[128,256]{0,1:T(8,128)(2,1)S(1)} %collective-permute-done.2), channel_id=1, source_target_pairs={{0,4},{4,8},{8,12},{12,16},{16,20},{20,24},{24,28},{1,5},{5,9},{9,... | collective-permute-start | bytes 196616 | tf_op jit(solution)/shard_map/ppermute | solution.py:17
  32.8 3.6 %collective-permute-start.10 = (bf16[128,256]{0,1:T(8,128)(2,1)S(1)}, bf16[128,256]{0,1:T(8,128)(2,1)S(1)}, u32[]{:S(2)}, u32[]{:S(2)}) collective-permute-start(bf16[128,256]{0,1:T(8,128)(2,1)S(1)} %collective-permute-done.9), channel_id=1, source_target_pairs={{0,4},{4,8},{8,12},{12,16},{16,20},{20,24},{24,28},{1,5},{5,9},{9,... | collective-permute-start | bytes 196616 | tf_op jit(solution)/shard_map/ppermute | solution.py:17
  36.4 2.0 collective-permute-start.4
  38.4 3.6 %collective-permute-start.11 = (bf16[128,256]{0,1:T(8,128)(2,1)S(1)}, bf16[128,256]{0,1:T(8,128)(2,1)S(1)}, u32[]{:S(2)}, u32[]{:S(2)}) collective-permute-start(bf16[128,256]{0,1:T(8,128)(2,1)S(1)} %collective-permute-done.10), channel_id=1, source_target_pairs={{0,4},{4,8},{8,12},{12,16},{16,20},{20,24},{24,28},{1,5},{5,9},{9,... | collective-permute-start | bytes 196616 | tf_op jit(solution)/shard_map/ppermute | solution.py:17
  42.0 3.4 %collective-permute-start.5 = (bf16[128,256]{0,1:T(8,128)(2,1)S(1)}, bf16[128,256]{0,1:T(8,128)(2,1)}, u32[]{:S(2)}, u32[]{:S(2)}) collective-permute-start(bf16[128,256]{0,1:T(8,128)(2,1)S(1)} %collective-permute-done.4), channel_id=1, source_target_pairs={{0,4},{4,8},{8,12},{12,16},{16,20},{20,24},{24,28},{1,5},{5,9},{9,... | collective-permute-start | bytes 196616 | tf_op jit(solution)/shard_map/ppermute | solution.py:17
  45.5 2.7 %collective-permute-start.12 = (bf16[128,256]{0,1:T(8,128)(2,1)S(1)}, bf16[128,256]{0,1:T(8,128)(2,1)}, u32[]{:S(2)}, u32[]{:S(2)}) collective-permute-start(bf16[128,256]{0,1:T(8,128)(2,1)S(1)} %collective-permute-done.11), channel_id=1, source_target_pairs={{0,4},{4,8},{8,12},{12,16},{16,20},{20,24},{24,28},{1,5},{5,9},{9,... | collective-permute-start | bytes 196616 | tf_op jit(solution)/shard_map/ppermute | solution.py:17
  48.2 3.7 %collective-permute-start.6 = (bf16[128,256]{0,1:T(8,128)(2,1)}, bf16[128,256]{0,1:T(8,128)(2,1)}, u32[]{:S(2)}, u32[]{:S(2)}) collective-permute-start(bf16[128,256]{0,1:T(8,128)(2,1)} %collective-permute-done.5), channel_id=1, source_target_pairs={{0,4},{4,8},{8,12},{12,16},{16,20},{20,24},{24,28},{1,5},{5,9},{9,... | collective-permute-start | bytes 196616 | tf_op jit(solution)/shard_map/ppermute | solution.py:17
  58.9 21.9 %while.17 = (s32[]{:T(128)}, bf16[2,256,128]{2,1,0:T(8,128)(2,1)}, bf16[2,256,128]{2,1,0:T(8,128)(2,1)}, f32[2,1024,128]{1,2,0:T(8,128)}, f32[2,1024,128]{1,2,0:...) while((s32[]{:T(128)}, bf16[2,256,128]{2,1,0:T(8,128)(2,1)}, ...), condition=%wide.region_4.5_spmd.clone, body=%wide.region_0.4_spmd.clone.sunk | while | flops 407207168 | bytes 28131736 | solution.py:94
  94.3 3.2 %collective-permute-done.18 = f32[128,256]{0,1:T(8,128)S(1)} collective-permute-done((f32[128,256]{0,1:T(8,128)S(1)}, f32[128,256]{0,1:T(8,128)S(1)}, u32[]{:S(2)}, u32[]{:S(2)}) %collective-permute-start.18) | collective-permute-done | bytes 131104 | tf_op jit(solution)/shard_map/ppermute | solution.py:17
  104.1 1.7 collective-permute-done.27
  110.0 2.4 %collective-permute-done.25 = f32[128,256]{0,1:T(8,128)S(1)} collective-permute-done((f32[128,256]{0,1:T(8,128)S(1)}, f32[128,256]{0,1:T(8,128)S(1)}, u32[]{:S(2)}, u32[]{:S(2)}) %collective-permute-start.25) | collective-permute-done | bytes 131104 | tf_op jit(solution)/shard_map/ppermute | solution.py:17
  117.0 3.4 %pad_maximum_fusion = f32[2304,768]{0,1:T(8,128)} fusion(f32[2304,512]{0,1:T(8,128)S(1)} %convolution_bitcast_fusion.1, f32[2304,256]{0,1:T(8,128)S(1)} %convolution_bitcast_fusion.2), kind=kLoop, calls=%fused_computation.45 | loop fusion | flops 1769472 | bytes 14155776 | tf_op jit(solution)/shard_map/concatenate | solution.py:140
  120.4 8.0 %copy.62 = f32[2304,768]{1,0:T(8,128)} copy(f32[2304,768]{0,1:T(8,128)} %pad_maximum_fusion) | data formatting | bytes 14155776
  128.4 19.9 %reduce-scatter.5.cloned.1.call-done = f32[128,576]{0,1:T(8,128)} async-done(((f32[128,2304]{0,1:T(8,128)}), f32[128,576]{0,1:T(8,128)}) %reduce-scatter.5.cloned.1.call-update) | async-done | bytes 294928 | tf_op jit(solution)/shard_map/reduce_scatter | solution.py:133
  150.0 66.1 %reduce-scatter.7.cloned.1.call-done = f32[288,768]{1,0:T(8,128)} async-done(((f32[2304,768]{1,0:T(8,128)}), f32[288,768]{1,0:T(8,128)}) %reduce-scatter.7.cloned.1.call-update) | async-done | bytes 884752
  216.1 1.7 slice.152
  217.8 1.9 slice_bitcast_fusion
  (171 shorter events, 60.9 us)
Async XLA Ops:
  7.2 141.1 %reduce-scatter.5.cloned.1.call-start = ((), (), s32[]{:S(2)}) async-start(), calls=%async_computation.2 | async-start | bytes 1474560 | tf_op jit(solution)/shard_map/reduce_scatter | solution.py:133
  8.3 7.8 %collective-permute-start = (bf16[128,256]{0,1:T(8,128)(2,1)S(1)}, bf16[128,256]{0,1:T(8,128)(2,1)S(1)}, u32[]{:S(2)}, u32[]{:S(2)}) collective-permute-start(bf16[128,256]{0,1:T(8,128)(2,1)S(1)} %copy.47), channel_id=1, source_target_pairs={{0,4},{4,8},{8,12},{12,16},{16,20},{20,24},{24,28},{1,5},{5,9},{9,... | collective-permute-start | bytes 196616 | tf_op jit(solution)/shard_map/ppermute | solution.py:17
  11.7 6.5 %collective-permute-start.7 = (bf16[128,256]{0,1:T(8,128)(2,1)S(1)}, bf16[128,256]{0,1:T(8,128)(2,1)S(1)}, u32[]{:S(2)}, u32[]{:S(2)}) collective-permute-start(bf16[128,256]{0,1:T(8,128)(2,1)S(1)} %copy.49), channel_id=1, source_target_pairs={{0,4},{4,8},{8,12},{12,16},{16,20},{20,24},{24,28},{1,5},{5,9},{9,... | collective-permute-start | bytes 196616 | tf_op jit(solution)/shard_map/ppermute | solution.py:17
  18.1 8.3 %collective-permute-start.8 = (bf16[128,256]{0,1:T(8,128)(2,1)S(1)}, bf16[128,256]{0,1:T(8,128)(2,1)S(1)}, u32[]{:S(2)}, u32[]{:S(2)}) collective-permute-start(bf16[128,256]{0,1:T(8,128)(2,1)S(1)} %collective-permute-done.7), channel_id=1, source_target_pairs={{0,4},{4,8},{8,12},{12,16},{16,20},{20,24},{24,28},{1,5},{5,9},{9,... | collective-permute-start | bytes 196616 | tf_op jit(solution)/shard_map/ppermute | solution.py:17
  21.7 8.3 %collective-permute-start.2 = (bf16[128,256]{0,1:T(8,128)(2,1)S(1)}, bf16[128,256]{0,1:T(8,128)(2,1)S(1)}, u32[]{:S(2)}, u32[]{:S(2)}) collective-permute-start(bf16[128,256]{0,1:T(8,128)(2,1)S(1)} %collective-permute-done.1), channel_id=1, source_target_pairs={{0,4},{4,8},{8,12},{12,16},{16,20},{20,24},{24,28},{1,5},{5,9},{9,... | collective-permute-start | bytes 196616 | tf_op jit(solution)/shard_map/ppermute | solution.py:17
  26.5 6.4 %collective-permute-start.9 = (bf16[128,256]{0,1:T(8,128)(2,1)S(1)}, bf16[128,256]{0,1:T(8,128)(2,1)S(1)}, u32[]{:S(2)}, u32[]{:S(2)}) collective-permute-start(bf16[128,256]{0,1:T(8,128)(2,1)S(1)} %collective-permute-done.8), channel_id=1, source_target_pairs={{0,4},{4,8},{8,12},{12,16},{16,20},{20,24},{24,28},{1,5},{5,9},{9,... | collective-permute-start | bytes 196616 | tf_op jit(solution)/shard_map/ppermute | solution.py:17
  30.0 6.4 %collective-permute-start.3 = (bf16[128,256]{0,1:T(8,128)(2,1)S(1)}, bf16[128,256]{0,1:T(8,128)(2,1)S(1)}, u32[]{:S(2)}, u32[]{:S(2)}) collective-permute-start(bf16[128,256]{0,1:T(8,128)(2,1)S(1)} %collective-permute-done.2), channel_id=1, source_target_pairs={{0,4},{4,8},{8,12},{12,16},{16,20},{20,24},{24,28},{1,5},{5,9},{9,... | collective-permute-start | bytes 196616 | tf_op jit(solution)/shard_map/ppermute | solution.py:17
  38.4 7.0 %collective-permute-start.11 = (bf16[128,256]{0,1:T(8,128)(2,1)S(1)}, bf16[128,256]{0,1:T(8,128)(2,1)S(1)}, u32[]{:S(2)}, u32[]{:S(2)}) collective-permute-start(bf16[128,256]{0,1:T(8,128)(2,1)S(1)} %collective-permute-done.10), channel_id=1, source_target_pairs={{0,4},{4,8},{8,12},{12,16},{16,20},{20,24},{24,28},{1,5},{5,9},{9,... | collective-permute-start | bytes 196616 | tf_op jit(solution)/shard_map/ppermute | solution.py:17
  45.5 8.3 %collective-permute-start.12 = (bf16[128,256]{0,1:T(8,128)(2,1)S(1)}, bf16[128,256]{0,1:T(8,128)(2,1)}, u32[]{:S(2)}, u32[]{:S(2)}) collective-permute-start(bf16[128,256]{0,1:T(8,128)(2,1)S(1)} %collective-permute-done.11), channel_id=1, source_target_pairs={{0,4},{4,8},{8,12},{12,16},{16,20},{20,24},{24,28},{1,5},{5,9},{9,... | collective-permute-start | bytes 196616 | tf_op jit(solution)/shard_map/ppermute | solution.py:17
  48.2 6.9 %collective-permute-start.6 = (bf16[128,256]{0,1:T(8,128)(2,1)}, bf16[128,256]{0,1:T(8,128)(2,1)}, u32[]{:S(2)}, u32[]{:S(2)}) collective-permute-start(bf16[128,256]{0,1:T(8,128)(2,1)} %collective-permute-done.5), channel_id=1, source_target_pairs={{0,4},{4,8},{8,12},{12,16},{16,20},{20,24},{24,28},{1,5},{5,9},{9,... | collective-permute-start | bytes 196616 | tf_op jit(solution)/shard_map/ppermute | solution.py:17
  83.3 7.3 %collective-permute-start.20 = (f32[128,256]{0,1:T(8,128)S(1)}, f32[128,256]{0,1:T(8,128)S(1)}, u32[]{:S(2)}, u32[]{:S(2)}) collective-permute-start(f32[128,256]{0,1:T(8,128)S(1)} %bitcast.188), channel_id=1, source_target_pairs={{28,0},{29,1},{30,2},{31,3}} | collective-permute-start | bytes 393224 | tf_op jit(solution)/shard_map/ppermute | solution.py:17
  84.6 8.3 %collective-permute-start.19 = (f32[128,256]{0,1:T(8,128)S(1)}, f32[128,256]{0,1:T(8,128)S(1)}, u32[]{:S(2)}, u32[]{:S(2)}) collective-permute-start(f32[128,256]{0,1:T(8,128)S(1)} %bitcast.187), channel_id=1, source_target_pairs={{24,0},{28,4},{25,1},{29,5},{26,2},{30,6},{27,3},{31,7}} | collective-permute-start | bytes 393224 | tf_op jit(solution)/shard_map/ppermute | solution.py:17
  85.9 11.6 %collective-permute-start.18 = (f32[128,256]{0,1:T(8,128)S(1)}, f32[128,256]{0,1:T(8,128)S(1)}, u32[]{:S(2)}, u32[]{:S(2)}) collective-permute-start(f32[128,256]{0,1:T(8,128)S(1)} %bitcast.186), channel_id=1, source_target_pairs={{20,0},{24,4},{28,8},{21,1},{25,5},{29,9},{22,2},{26,6},{30,10},{2... | collective-permute-start | bytes 393224 | tf_op jit(solution)/shard_map/ppermute | solution.py:17
  87.2 11.6 %collective-permute-start.17 = (f32[128,256]{0,1:T(8,128)S(1)}, f32[128,256]{0,1:T(8,128)S(1)}, u32[]{:S(2)}, u32[]{:S(2)}) collective-permute-start(f32[128,256]{0,1:T(8,128)S(1)} %bitcast.184), channel_id=1, source_target_pairs={{16,0},{20,4},{24,8},{28,12},{17,1},{21,5},{25,9},{29,13},{18,2},{... | collective-permute-start | bytes 393224 | tf_op jit(solution)/shard_map/ppermute | solution.py:17
  88.5 11.6 %collective-permute-start.16 = (f32[128,256]{0,1:T(8,128)S(1)}, f32[128,256]{0,1:T(8,128)S(1)}, u32[]{:S(2)}, u32[]{:S(2)}) collective-permute-start(f32[128,256]{0,1:T(8,128)S(1)} %bitcast.182), channel_id=1, source_target_pairs={{12,0},{16,4},{20,8},{24,12},{28,16},{13,1},{17,5},{21,9},{25,13},... | collective-permute-start | bytes 393224 | tf_op jit(solution)/shard_map/ppermute | solution.py:17
  90.6 10.8 %collective-permute-start.15 = (f32[128,256]{0,1:T(8,128)S(1)}, f32[128,256]{0,1:T(8,128)S(1)}, u32[]{:S(2)}, u32[]{:S(2)}) collective-permute-start(f32[128,256]{0,1:T(8,128)S(1)} %bitcast.180), channel_id=1, source_target_pairs={{8,0},{12,4},{16,8},{20,12},{24,16},{28,20},{9,1},{13,5},{17,9},{2... | collective-permute-start | bytes 393224 | tf_op jit(solution)/shard_map/ppermute | solution.py:17
  92.9 9.9 %collective-permute-start.14 = (f32[128,256]{0,1:T(8,128)S(1)}, f32[128,256]{0,1:T(8,128)S(1)}, u32[]{:S(2)}, u32[]{:S(2)}) collective-permute-start(f32[128,256]{0,1:T(8,128)S(1)} %bitcast.177), channel_id=1, source_target_pairs={{4,0},{8,4},{12,8},{16,12},{20,16},{24,20},{28,24},{5,1},{9,5},{13... | collective-permute-start | bytes 393224 | tf_op jit(solution)/shard_map/ppermute | solution.py:17
  97.5 8.3 %collective-permute-start.27 = (f32[128,256]{0,1:T(8,128)S(1)}, f32[128,256]{0,1:T(8,128)S(1)}, u32[]{:S(2)}, u32[]{:S(2)}) collective-permute-start(f32[128,256]{0,1:T(8,128)S(1)} %bitcast.185), channel_id=1, source_target_pairs={{28,0},{29,1},{30,2},{31,3}} | collective-permute-start | bytes 393224 | tf_op jit(solution)/shard_map/ppermute | solution.py:17
  98.8 9.3 %collective-permute-start.26 = (f32[128,256]{0,1:T(8,128)S(1)}, f32[128,256]{0,1:T(8,128)S(1)}, u32[]{:S(2)}, u32[]{:S(2)}) collective-permute-start(f32[128,256]{0,1:T(8,128)S(1)} %bitcast.183), channel_id=1, source_target_pairs={{24,0},{28,4},{25,1},{29,5},{26,2},{30,6},{27,3},{31,7}} | collective-permute-start | bytes 393224 | tf_op jit(solution)/shard_map/ppermute | solution.py:17
  100.1 12.3 %collective-permute-start.25 = (f32[128,256]{0,1:T(8,128)S(1)}, f32[128,256]{0,1:T(8,128)S(1)}, u32[]{:S(2)}, u32[]{:S(2)}) collective-permute-start(f32[128,256]{0,1:T(8,128)S(1)} %bitcast.181), channel_id=1, source_target_pairs={{20,0},{24,4},{28,8},{21,1},{25,5},{29,9},{22,2},{26,6},{30,10},{2... | collective-permute-start | bytes 393224 | tf_op jit(solution)/shard_map/ppermute | solution.py:17
  101.4 11.1 %collective-permute-start.24 = (f32[128,256]{0,1:T(8,128)S(1)}, f32[128,256]{0,1:T(8,128)S(1)}, u32[]{:S(2)}, u32[]{:S(2)}) collective-permute-start(f32[128,256]{0,1:T(8,128)S(1)} %bitcast.179), channel_id=1, source_target_pairs={{16,0},{20,4},{24,8},{28,12},{17,1},{21,5},{25,9},{29,13},{18,2},{... | collective-permute-start | bytes 393224 | tf_op jit(solution)/shard_map/ppermute | solution.py:17
  102.7 9.8 %collective-permute-start.23 = (f32[128,256]{0,1:T(8,128)S(1)}, f32[128,256]{0,1:T(8,128)S(1)}, u32[]{:S(2)}, u32[]{:S(2)}) collective-permute-start(f32[128,256]{0,1:T(8,128)S(1)} %bitcast.178), channel_id=1, source_target_pairs={{12,0},{16,4},{20,8},{24,12},{28,16},{13,1},{17,5},{21,9},{25,13},... | collective-permute-start | bytes 393224 | tf_op jit(solution)/shard_map/ppermute | solution.py:17
  105.8 7.8 %collective-permute-start.22 = (f32[128,256]{0,1:T(8,128)S(1)}, f32[128,256]{0,1:T(8,128)S(1)}, u32[]{:S(2)}, u32[]{:S(2)}) collective-permute-start(f32[128,256]{0,1:T(8,128)S(1)} %bitcast.176), channel_id=1, source_target_pairs={{8,0},{12,4},{16,8},{20,12},{24,16},{28,20},{9,1},{13,5},{17,9},{2... | collective-permute-start | bytes 393224 | tf_op jit(solution)/shard_map/ppermute | solution.py:17
  115.2 100.9 %reduce-scatter.7.cloned.1.call-start = ((), (), s32[]{:S(2)}) async-start(), calls=%async_computation.3 | async-start | bytes 7962624
  (36 other events, 232.1 us)
Sparse Core Ops, SparseCore 0:
  115.4 32.9 reduce-scatter.4
  151.8 64.2 reduce-scatter.6
where the time goes:
time: 228 us; the launch traced here: 227 us
  waiting for transfers between devices  96.5 us (42%)
  starting transfers between devices  59.3 us (26%)
  local copies, waits for them, and re-layouts  32.5 us (14%)
  matrix products  16.6 us (7%)
  between operations  14.7 us (6%)
  other arithmetic  6.61 us (3%)
    unnamed x3, waiting for transfers between devices  66.2 us
    ppermute x28, starting transfers between devices, passed_along(): lax.ppermute(value, axis, [(source, source + steps) for source in range(l...  59.2 us
    reduce_scatter x1, waiting for transfers between devices, local(): lax.psum_scatter(input_terms, 'head', scatter_dimension=1, tiled=True)  19.9 us
    unnamed x37, local copies, waits for them, and re-layouts  14.1 us
    ppermute x28, waiting for transfers between devices, passed_along(): lax.ppermute(value, axis, [(source, source + steps) for source in range(l...  10.4 us
    dynamic_update_slice x8, local copies, waits for them, and re-layouts, local(): lax.map(per_head, (query_stack, key_stack, value_stack, grad_stack))  5.27 us
  transfers between devices with their start and end apart: 30, of which 9 were waited for; matrix products, arithmetic and copies ran while one was open for 10% of the time, Pallas kernels for 0%

commit v1 on v0

--- a/solution.py
+++ b/solution.py
@@ -1,6 +1,10 @@
+import functools
+
 import jax
 import jax.numpy as jnp
 from jax import lax
+from jax.experimental import pallas as pl
+from jax.experimental.pallas import tpu as pltpu
 from jax.sharding import PartitionSpec as P
 
 HEAD_SIZE = 128
@@ -9,6 +13,8 @@
 
 
 logit_scale = 1.0 / 12.0
+log2_scale = 1.4426950408889634 / 12.0
+excluded = -1e30
 
 
 def passed_along(value, axis, steps):
@@ -17,7 +23,283 @@
     return lax.ppermute(value, axis, [(source, source + steps) for source in range(leading, last)])
 
 
-def local(
+NT = (((1,), (1,)), ((), ()))
+
+
+def dot_nt(left, right):
+    return lax.dot_general(left, right, NT, preferred_element_type=jnp.float32)
+
+
+def dot_nn(left, right):
+    return jnp.dot(left, right, preferred_element_type=jnp.float32)
+
+
+def out_grad_kernel(cot_ref, weight_ref, q_ref, k_ref, v_ref, packed_ref):
+    q_cols = q_ref.shape[1]
+    kv_cols = k_ref.shape[1]
+    packed_ref[:, :q_cols] = q_ref[...]
+    packed_ref[:, q_cols : q_cols + kv_cols] = k_ref[...]
+    packed_ref[:, q_cols + kv_cols : q_cols + 2 * kv_cols] = v_ref[...]
+    packed_ref[:, q_cols + 2 * kv_cols :] = dot_nt(cot_ref[...], weight_ref[...]).astype(
+        jnp.bfloat16
+    )
+
+
+def turn_kernel(parts, normed_ref, cot_ref, turned_ref):
+    cut = normed_ref.shape[1] // parts
+    for which, ref in enumerate((normed_ref, cot_ref)):
+        turned = ref[...].astype(jnp.float32).T.astype(jnp.bfloat16)
+        for part in range(parts):
+            turned_ref[part, which] = turned[part * cut : (part + 1) * cut]
+
+
+def attention_kernel(
+    gathered_ref,
+    wq_hbm,
+    wk_hbm,
+    wv_hbm,
+    terms_ref,
+    attn_ref,
+    dv_ref,
+    wq_ref,
+    wk_ref,
+    wv_ref,
+    score_ref,
+    prob_ref,
+    grad_ref,
+    value_t_ref,
+    key_t_ref,
+    dk_ref,
+    dx_ref,
+    weight_sem,
+):
+    me = lax.axis_index("seq")
+    copies = [
+        pltpu.make_async_copy(source, target, weight_sem.at[place])
+        for place, (source, target) in enumerate(
+            ((wq_hbm, wq_ref), (wk_hbm, wk_ref), (wv_hbm, wv_ref))
+        )
+    ]
+    for copy in copies:
+        copy.start()
+    tokens = gathered_ref.shape[0]
+    rows = dx_ref.shape[0]
+    blocks = tokens // rows
+    kv_cols = dv_ref.shape[1]
+    kv_heads = kv_cols // HEAD_SIZE
+    q_cols = attn_ref.shape[0]
+    key_base = q_cols
+    value_base = q_cols + kv_cols
+    grad_base = q_cols + 2 * kv_cols
+    wide = QUERIES_PER_KEY * rows
+
+    def stacked(block, base, kv_head):
+        return jnp.concatenate(
+            [
+                gathered_ref[
+                    block * rows : (block + 1) * rows,
+                    base + h * HEAD_SIZE : base + (h + 1) * HEAD_SIZE,
+                ]
+                for h in range(kv_head * QUERIES_PER_KEY, (kv_head + 1) * QUERIES_PER_KEY)
+            ],
+            axis=0,
+        )
+
+    def columns(base, kv_head):
+        return slice(base + kv_head * HEAD_SIZE, base + (kv_head + 1) * HEAD_SIZE)
+
+    dk_ref[...] = jnp.zeros_like(dk_ref)
+    for kv_head in range(kv_heads):
+        value_t_ref[kv_head] = gathered_ref[:, columns(value_base, kv_head)].T
+        key_t_ref[kv_head] = gathered_ref[:, columns(key_base, kv_head)].T
+    key_place = lax.broadcasted_iota(jnp.int32, (rows, wide), 0)
+    query_place = lax.broadcasted_iota(jnp.int32, (rows, wide), 1) % rows
+    allowed = key_place <= query_place
+
+    for block in range(blocks):
+        span = (block + 1) * rows
+        kept = []
+        for kv_head in range(kv_heads):
+            queries = stacked(block, 0, kv_head)
+            grads = stacked(block, grad_base, kv_head)
+            grad_ref[kv_head, block * wide : (block + 1) * wide] = grads
+            scores = dot_nt(gathered_ref[:span, columns(key_base, kv_head)], queries)
+            diagonal = jnp.where(allowed, scores[block * rows :], excluded)
+            if block:
+                scores = jnp.concatenate([scores[: block * rows], diagonal], axis=0)
+            else:
+                scores = diagonal
+            score_ref[kv_head, :span] = scores
+            top = jnp.max(scores, axis=0, keepdims=True)
+            weights = jnp.exp2((score_ref[kv_head, :span] - top) * log2_scale)
+            score_ref[kv_head, :span] = weights
+            inverse = 1.0 / jnp.sum(weights, axis=0, keepdims=True)
+            prob_b = (score_ref[kv_head, :span] * inverse).astype(jnp.bfloat16)
+            prob_ref[kv_head, :span, block * wide : (block + 1) * wide] = prob_b
+            attn = dot_nn(value_t_ref[kv_head, :, :span], prob_b).astype(jnp.bfloat16)
+            for h in range(QUERIES_PER_KEY):
+                first = (kv_head * QUERIES_PER_KEY + h) * HEAD_SIZE
+                attn_ref[first : first + HEAD_SIZE, block * rows : (block + 1) * rows] = attn[
+                    :, h * rows : (h + 1) * rows
+                ]
+            delta = jnp.sum(
+                grads.T.astype(jnp.float32) * attn.astype(jnp.float32), axis=0, keepdims=True
+            )
+            kept.append((queries, grads, inverse, delta))
+
+        @pl.when(me <= block)
+        def _():
+            own = pl.ds(pl.multiple_of(me * rows, rows), rows)
+            for kv_head, (queries, grads, inverse, delta) in enumerate(kept):
+                dprob = dot_nt(gathered_ref[own, columns(value_base, kv_head)], grads)
+                dscore = score_ref[kv_head, own] * inverse * (dprob - delta)
+                dk_ref[kv_head] += dot_nn(dscore.astype(jnp.bfloat16), queries)
+
+        @pl.when(me == block)
+        def _():
+            for kv_head, (queries, grads, inverse, delta) in enumerate(kept):
+                dprob = dot_nt(gathered_ref[:span, columns(value_base, kv_head)], grads)
+                dscore = score_ref[kv_head, :span] * inverse * (dprob - delta)
+                dq_t = logit_scale * dot_nn(
+                    key_t_ref[kv_head, :, :span], dscore.astype(jnp.bfloat16)
+                )
+                for h in range(QUERIES_PER_KEY):
+                    first = (kv_head * QUERIES_PER_KEY + h) * HEAD_SIZE
+                    dx_ref[:, first : first + HEAD_SIZE] = dq_t[
+                        :, h * rows : (h + 1) * rows
+                    ].T.astype(jnp.bfloat16)
+
+    for kv_head in range(kv_heads):
+        for block in range(blocks):
+            dv_ref[block * rows : (block + 1) * rows, columns(0, kv_head)] = dot_nn(
+                prob_ref[kv_head, block * rows : (block + 1) * rows, block * wide :],
+                grad_ref[kv_head, block * wide :],
+            ).astype(jnp.bfloat16)
+        dx_ref[:, columns(key_base, kv_head)] = (logit_scale * dk_ref[kv_head]).astype(
+            jnp.bfloat16
+        )
+    dx_ref[:, value_base : value_base + kv_cols] = dv_ref[
+        pl.ds(pl.multiple_of(me * rows, rows), rows)
+    ]
+    for copy in copies:
+        copy.wait()
+    parts, _, cut = terms_ref.shape
+    for part in range(parts):
+        out_rows = slice(part * cut, (part + 1) * cut)
+        terms_ref[part] = (
+            dot_nt(dx_ref[:, :key_base], wq_ref[out_rows])
+            + dot_nt(dx_ref[:, key_base:value_base], wk_ref[out_rows])
+            + dot_nt(dx_ref[:, value_base:], wv_ref[out_rows])
+        ).astype(jnp.bfloat16)
+
+
+def weight_grad_kernel(turned_ref, attn_ref, dv_ref, wvalue_ref, woutput_ref, joined_ref):
+    parts = turned_ref.shape[0]
+    rows = turned_ref.shape[3]
+    for part in range(parts):
+        joined_ref[:, :, part * rows : (part + 1) * rows] = turned_ref[part]
+    wvalue_ref[...] = dot_nn(joined_ref[0], dv_ref[...])
+    woutput_ref[...] = dot_nt(attn_ref[...], joined_ref[1])
+
+
+def kernel_call(body, outs, operands, in_specs=None, scratch=(), flops=0, moved=0):
+    vmem = pl.BlockSpec(memory_space=pltpu.VMEM)
+    return pl.pallas_call(
+        body,
+        out_shape=outs,
+        in_specs=in_specs or [vmem] * len(operands),
+        out_specs=jax.tree.map(lambda _: vmem, outs),
+        scratch_shapes=list(scratch),
+        compiler_params=pltpu.CompilerParams(vmem_limit_bytes=48 * 1024 * 1024),
+        cost_estimate=pl.CostEstimate(flops=flops, bytes_accessed=moved, transcendentals=0),
+    )(*operands)
+
+
+def gathered_plan(
+    normed_input,
+    stored_queries,
+    stored_keys,
+    stored_values,
+    query_weight,
+    key_matrix,
+    value_matrix,
+    output_weight,
+    out_cotangent,
+):
+    bf16, f32 = jnp.bfloat16, jnp.float32
+    rows, model = normed_input.shape
+    blocks = lax.axis_size("seq")
+    groups = lax.axis_size("head")
+    tokens = rows * blocks
+    q_cols = stored_queries.shape[1]
+    kv_cols = stored_keys.shape[1]
+    kv_heads = kv_cols // HEAD_SIZE
+    wide = QUERIES_PER_KEY * rows
+    packed_cols = 2 * q_cols + 2 * kv_cols
+    packed = kernel_call(
+        out_grad_kernel,
+        jax.ShapeDtypeStruct((rows, packed_cols), bf16),
+        (out_cotangent, output_weight, stored_queries, stored_keys, stored_values),
+        flops=2 * rows * model * q_cols,
+        moved=2 * model * (rows + q_cols),
+    )
+    gathered = lax.all_gather(packed, "seq", axis=0, tiled=True)
+    turned = kernel_call(
+        functools.partial(turn_kernel, blocks),
+        jax.ShapeDtypeStruct((blocks, 2, model // blocks, rows), bf16),
+        (normed_input, out_cotangent),
+        moved=8 * rows * model,
+    )
+    turned = lax.all_to_all(turned, "seq", 0, 0)
+    anywhere = pl.BlockSpec(memory_space=pl.ANY)
+    terms, attn, dv = kernel_call(
+        attention_kernel,
+        (
+            jax.ShapeDtypeStruct((groups, rows, model // groups), bf16),
+            jax.ShapeDtypeStruct((q_cols, tokens), bf16),
+            jax.ShapeDtypeStruct((tokens, kv_cols), bf16),
+        ),
+        (gathered, query_weight, key_matrix, value_matrix),
+        in_specs=[pl.BlockSpec(memory_space=pltpu.VMEM)] + [anywhere] * 3,
+        scratch=(
+            pltpu.VMEM(query_weight.shape, bf16),
+            pltpu.VMEM(key_matrix.shape, bf16),
+            pltpu.VMEM(value_matrix.shape, bf16),
+            pltpu.VMEM((kv_heads, tokens, wide), f32),
+            pltpu.VMEM((kv_heads, tokens, blocks * wide), bf16),
+            pltpu.VMEM((kv_heads, blocks * wide, HEAD_SIZE), bf16),
+            pltpu.VMEM((kv_heads, HEAD_SIZE, tokens), bf16),
+            pltpu.VMEM((kv_heads, HEAD_SIZE, tokens), bf16),
+            pltpu.VMEM((kv_heads, rows, HEAD_SIZE), f32),
+            pltpu.VMEM((rows, q_cols + 2 * kv_cols), bf16),
+            pltpu.SemaphoreType.DMA((3,)),
+        ),
+        flops=8 * tokens * tokens * q_cols,
+        moved=2 * (tokens * packed_cols + model * (q_cols + 2 * kv_cols)),
+    )
+    arrived = lax.all_to_all(terms, "head", 0, 0)
+    grad_wvalue, grad_woutput = kernel_call(
+        weight_grad_kernel,
+        (
+            jax.ShapeDtypeStruct((model // blocks, kv_cols), f32),
+            jax.ShapeDtypeStruct((q_cols, model // blocks), f32),
+        ),
+        (turned, attn, dv),
+        scratch=(pltpu.VMEM((2, model // blocks, tokens), bf16),),
+        flops=2 * tokens * (model // blocks) * (q_cols + kv_cols),
+        moved=4 * (model // blocks) * (tokens + q_cols + kv_cols),
+    )
+    grad_input = jnp.sum(arrived.astype(f32), axis=0).astype(bf16)
+    return (grad_input, grad_wvalue, grad_woutput)
+
+
+def local(normed_input, *others):
+    if normed_input.shape[0] * lax.axis_size("seq") <= WINDOW_LENGTH:
+        return gathered_plan(normed_input, *others)
+    return windowed_plan(normed_input, *others)
+
+
+def windowed_plan(
     normed_input,
     stored_queries,
     stored_keys,

time: 228 us -> 111 us (0.49)
  starting transfers between devices: 59.3 us -> 9.81 us
  waiting for transfers between devices: 96.5 us -> 50 us
  Pallas kernels: 0 us -> 24.2 us
  local copies, waits for them, and re-layouts: 32.5 us -> 9.97 us
  matrix products: 16.6 us -> 0 us
  other arithmetic: 6.61 us -> 1.85 us
    unnamed x3 -> x1, waiting for transfers between devices: 66.2 us -> 0.02 us
    ppermute x28 -> x0, starting transfers between devices: 59.2 us -> none  [passed_along(): lax.ppermute(value, axis, [(source, source + steps) for source in range(l...]
    all_gather x0 -> x1, waiting for transfers between devices: none -> 36.3 us  [gathered_plan(): gathered = lax.all_gather(packed, 'seq', axis=0, tiled=True)]
    pallas_call x0 -> x4, Pallas kernels: none -> 24.2 us  [kernel_call(): pl.pallas_call(body, out_shape=outs, in_specs=in_specs or [vmem] * len(op...]
    reduce_scatter x1 -> x0, waiting for transfers between devices: 19.9 us -> none  [local(): lax.psum_scatter(input_terms, 'head', scatter_dimension=1, tiled=True)]
    dot_general x18 -> x0, matrix products: 16.6 us -> none  [the longest x2 2.91 us: per_head(): jnp.dot(grad_head, value_head.T, preferred_element_type=jnp.float32)]
    all_to_all x0 -> x2, waiting for transfers between devices: none -> 13.8 us  [the longest x1 13.8 us: gathered_plan(): arrived = lax.all_to_all(terms, 'head', 0, 0)]
    ppermute x28 -> x0, waiting for transfers between devices: 10.4 us -> none  [passed_along(): lax.ppermute(value, axis, [(source, source + steps) for source in range(l...]
  transfers between devices with their start and end apart: 30 -> 3, of which waited for: 9 -> 2; matrix products, arithmetic and copies ran while one was open for 10% -> 2% of each run, Pallas kernels for 0% -> 21%
where the time goes in v1:
time: 111 us; the launch traced here: 110 us
  waiting for transfers between devices  50 us (45%)
  Pallas kernels  24.2 us (22%)
  between operations  14.1 us (13%)
  local copies, waits for them, and re-layouts  9.97 us (9%)
  starting transfers between devices  9.81 us (9%)
  other arithmetic  1.85 us (2%)
    all_gather x1, waiting for transfers between devices, gathered_plan(): gathered = lax.all_gather(packed, 'seq', axis=0, tiled=True)  36.3 us
    pallas_call x4, Pallas kernels, kernel_call(): pl.pallas_call(body, out_shape=outs, in_specs=in_specs or [vmem] * len(op...  24.2 us
    all_to_all x1, waiting for transfers between devices, gathered_plan(): arrived = lax.all_to_all(terms, 'head', 0, 0)  13.8 us
    unnamed x19, local copies, waits for them, and re-layouts  8.91 us
    all_to_all x1, starting transfers between devices, gathered_plan(): turned = lax.all_to_all(turned, 'seq', 0, 0)  5.16 us
    all_to_all x1, starting transfers between devices, gathered_plan(): arrived = lax.all_to_all(terms, 'head', 0, 0)  4.61 us
  transfers between devices with their start and end apart: 3, of which 2 were waited for; matrix products, arithmetic and copies ran while one was open for 2% of the time, Pallas kernels for 21%

profile of v1, /device:TPU:0, one launch (start us, length us, event | category | flops | bytes accessed | tf_op | source)
XLA Modules:
  0.0 110.0 jit_solution(13970058947378010204)
XLA Ops:
  7.2 0.0 all-gather.2.cloned.1.call-start
  7.2 0.0 copy-start
  7.2 1.7 %copy-done = bf16[512,2304]{1,0:T(8,128)(2,1)S(1)} copy-done((bf16[512,2304]{1,0:T(8,128)(2,1)S(1)}, bf16[512,2304]{1,0:T(8,128)(2,1)}, u32[]{:S(2)}) %copy-start) | copy-done | bytes 2359320
  8.9 1.1 copy-done.1
  9.9 0.9 copy-done.4
  10.8 0.8 copy-done.5
  11.7 0.8 copy-done.6
  12.5 1.6 %shard_map.112 = bf16[128,1536]{1,0:T(8,128)(2,1)} custom-call(bf16[128,2304]{1,0:T(8,128)(2,1)S(1)} %copy-done.1, bf16[512,2304]{1,0:T(8,128)(2,1)S(1)} %copy-done, bf16[128,512]{1,0:T(8,128)(2,1)S(1)} %copy-done.4, bf16[128,256]{1,0:T(8,128)(2,1)S(1)} %copy-done.5, bf16[128,256]{1,0:T(8,128)(2,1)S(1)} %copy-done.6), custom_call_target="tpu_custom_call" | custom-call | flops 301989888 | bytes 2949120 | tf_op jit(solution)/shard_map/pallas_call | solution.py:207
  14.2 0.0 all-gather.2.cloned.1.call-update
  14.2 0.0 copy-done.2
  14.2 0.0 copy-done.3
  14.2 1.4 %shard_map.114 = bf16[8,2,288,128]{3,2,1,0:T(8,128)(2,1)} custom-call(bf16[128,2304]{1,0:T(8,128)(2,1)S(1)} %copy-done.3, bf16[128,2304]{1,0:T(8,128)(2,1)S(1)} %copy-done.2), custom_call_target="tpu_custom_call" | custom-call | bytes 2359296 | tf_op jit(solution)/shard_map/pallas_call | solution.py:207
  15.6 5.2 %all-to-all-start.1 = ((bf16[8,2,288,128]{3,2,1,0:T(8,128)(2,1)}), bf16[8,2,288,128]{3,2,1,0:T(8,128)(2,1)S(1)}, u32[]{:S(2)}, u32[]{:S(2)}) async-start(bf16[8,2,288,128]{3,2,1,0:T(8,128)(2,1)} %shard_map.114), calls=%async_computation.1 | async-start | bytes 2359296 | tf_op jit(solution)/shard_map/all_to_all | solution.py:253
  20.8 36.3 %all-gather.2.cloned.1.call-done.gathered_ref = bf16[1024,1536]{1,0:T(8,128)(2,1)} async-done(((bf16[128,1536]{1,0:T(8,128)(2,1)}), bf16[1024,1536]{1,0:T(8,128)(2,1)}) %all-gather.2.cloned.1.call-update) | async-done | bytes 3145744 | tf_op jit(solution)/shard_map/all_gather | solution.py:246
  57.0 1.3 %copy-done.7 = bf16[2304,256]{1,0:T(8,128)(2,1)S(1)} copy-done((bf16[2304,256]{1,0:T(8,128)(2,1)S(1)}, bf16[2304,256]{1,0:T(8,128)(2,1)}, u32[]{:S(2)}) %copy-start.7) | copy-done | bytes 1179672
  58.3 1.3 %copy-done.8 = bf16[2304,256]{1,0:T(8,128)(2,1)S(1)} copy-done((bf16[2304,256]{1,0:T(8,128)(2,1)S(1)}, bf16[2304,256]{1,0:T(8,128)(2,1)}, u32[]{:S(2)}) %copy-start.8) | copy-done | bytes 1179672
  59.6 20.0 %shard_map.113 = (bf16[4,128,576]{2,1,0:T(8,128)(2,1)S(1)}, bf16[512,1024]{1,0:T(8,128)(2,1)S(1)}, bf16[1024,256]{1,0:T(8,128)(2,1)S(1)}) custom-call(bf16[1024,1536]{1,0:T(8,128)(2,1)} %all-gather.2.cloned.1.call-done.gathered_ref, bf16[2304,512]{1,0:T(8,128)(2,1)} %wq_hbm.1, bf16[2304,256]{1,0:T(8,128)(2,1)S(1)} %copy-done.7, bf16[2304,256]{1,0:T(8,128)(2,1)S(1)} %copy-done.8), custom_call_target="tpu_custom_call" | custom-call | flops 4294967296 | bytes 7864320 | tf_op jit(solution)/shard_map/pallas_call | solution.py:207
  79.6 1.1 copy.13
  80.6 0.0 all-to-all-done.1.turned_ref
  80.6 4.6 %all-to-all-start = ((bf16[4,128,576]{1,2,0:T(8,128)(2,1)}), bf16[4,128,576]{1,2,0:T(8,128)(2,1)}, u32[]{:S(2)}, u32[]{:S(2)}) async-start(bf16[4,128,576]{1,2,0:T(8,128)(2,1)} %copy.13), calls=%async_computation | async-start | bytes 1179648 | tf_op jit(solution)/shard_map/all_to_all | solution.py:280
  85.3 1.2 %shard_map.115 = (f32[288,256]{1,0:T(8,128)}, f32[512,288]{1,0:T(8,128)S(1)}) custom-call(bf16[8,2,288,128]{3,2,1,0:T(8,128)(2,1)S(1)} %all-to-all-done.1.turned_ref, bf16[512,1024]{1,0:T(8,128)(2,1)S(1)} %get-tuple-element.9.attn_ref, bf16[1024,256]{1,0:T(8,128)(2,1)S(1)} %get-tuple-element.10.dv_ref), custom_call_target="tpu_custom_call" | custom-call | flops 452984832 | bytes 2064384 | tf_op jit(solution)/shard_map/pallas_call | solution.py:207
  86.5 1.1 copy.16
  87.5 13.8 %all-to-all-done = bf16[4,128,576]{1,2,0:T(8,128)(2,1)} async-done(((bf16[4,128,576]{1,2,0:T(8,128)(2,1)}), bf16[4,128,576]{1,2,0:T(8,128)(2,1)}, u32[]{:S(2)}, u32[]{:S(2)}) %all-to-all-start) | async-done | bytes 589856 | tf_op jit(solution)/shard_map/all_to_all | solution.py:280
  101.3 1.8 %reduce_sum.12 = bf16[128,576]{0,1:T(8,128)(2,1)} reduce(bf16[4,128,576]{1,2,0:T(8,128)(2,1)} %all-to-all-done, bf16[]{:T(256)} %constant.2.clone.1), dimensions={0}, to_apply=%region_0.0 | reduce | flops 221184 | bytes 737282 | tf_op jit(solution)/shard_map/reduce_sum | solution.py:292
  (8 shorter events, 0.0 us)
Async XLA Ops:
  7.2 49.9 %all-gather.2.cloned.1.call-start = ((), (), s32[]{:S(2)}) async-start(), calls=%async_computation.2 | async-start | bytes 3538944 | tf_op jit(solution)/shard_map/all_gather | solution.py:246
  7.2 1.7 %copy-start = (bf16[512,2304]{1,0:T(8,128)(2,1)S(1)}, bf16[512,2304]{1,0:T(8,128)(2,1)}, u32[]{:S(2)}) copy-start(bf16[512,2304]{1,0:T(8,128)(2,1)} %weight_ref.1) | copy-start | bytes 7077892
  8.9 1.1 copy-start.1
  9.9 0.9 copy-start.4
  10.8 0.8 copy-start.5
  11.7 0.8 copy-start.6
  12.5 1.7 %copy-start.2 = (bf16[128,2304]{1,0:T(8,128)(2,1)S(1)}, bf16[128,2304]{1,0:T(8,128)(2,1)}, u32[]{:S(2)}) copy-start(bf16[128,2304]{1,0:T(8,128)(2,1)} %cot_ref.3) | copy-start | bytes 1769476
  12.5 1.7 %copy-start.3 = (bf16[128,2304]{1,0:T(8,128)(2,1)S(1)}, bf16[128,2304]{1,0:T(8,128)(2,1)}, u32[]{:S(2)}) copy-start(bf16[128,2304]{1,0:T(8,128)(2,1)} %normed_ref.1) | copy-start | bytes 1769476
  15.6 65.0 %all-to-all-start.1 = ((bf16[8,2,288,128]{3,2,1,0:T(8,128)(2,1)}), bf16[8,2,288,128]{3,2,1,0:T(8,128)(2,1)S(1)}, u32[]{:S(2)}, u32[]{:S(2)}) async-start(bf16[8,2,288,128]{3,2,1,0:T(8,128)(2,1)} %shard_map.114), calls=%async_computation.1 | async-start | bytes 2359296 | tf_op jit(solution)/shard_map/all_to_all | solution.py:253
  57.0 1.3 %copy-start.7 = (bf16[2304,256]{1,0:T(8,128)(2,1)S(1)}, bf16[2304,256]{1,0:T(8,128)(2,1)}, u32[]{:S(2)}) copy-start(bf16[2304,256]{1,0:T(8,128)(2,1)} %wk_hbm.1) | copy-start | bytes 3538948
  58.3 1.3 %copy-start.8 = (bf16[2304,256]{1,0:T(8,128)(2,1)S(1)}, bf16[2304,256]{1,0:T(8,128)(2,1)}, u32[]{:S(2)}) copy-start(bf16[2304,256]{1,0:T(8,128)(2,1)} %wv_hbm.1) | copy-start | bytes 3538948
  80.6 20.6 %all-to-all-start = ((bf16[4,128,576]{1,2,0:T(8,128)(2,1)}), bf16[4,128,576]{1,2,0:T(8,128)(2,1)}, u32[]{:S(2)}, u32[]{:S(2)}) async-start(bf16[4,128,576]{1,2,0:T(8,128)(2,1)} %copy.13), calls=%async_computation | async-start | bytes 1179648 | tf_op jit(solution)/shard_map/all_to_all | solution.py:280
Sparse Core Ops, SparseCore 0:
  14.3 42.6 all-gather.1

commit v2 on v1

--- a/solution.py
+++ b/solution.py
@@ -34,27 +34,68 @@
     return jnp.dot(left, right, preferred_element_type=jnp.float32)
 
 
-def out_grad_kernel(cot_ref, weight_ref, q_ref, k_ref, v_ref, packed_ref):
-    q_cols = q_ref.shape[1]
-    kv_cols = k_ref.shape[1]
-    packed_ref[:, :q_cols] = q_ref[...]
-    packed_ref[:, q_cols : q_cols + kv_cols] = k_ref[...]
-    packed_ref[:, q_cols + kv_cols : q_cols + 2 * kv_cols] = v_ref[...]
-    packed_ref[:, q_cols + 2 * kv_cols :] = dot_nt(cot_ref[...], weight_ref[...]).astype(
-        jnp.bfloat16
-    )
-
-
-def turn_kernel(parts, normed_ref, cot_ref, turned_ref):
+def out_grad_kernel(
+    cot_hbm, weight_hbm, q_hbm, k_hbm, v_hbm, packed_ref, cot_ref, weight_ref, sem
+):
+    q_cols = q_hbm.shape[1]
+    kv_cols = k_hbm.shape[1]
+    pieces = sem.shape[0] - 4
+    cut = weight_ref.shape[0] // pieces
+    cot_copy = pltpu.make_async_copy(cot_hbm, cot_ref, sem.at[pieces])
+    cot_copy.start()
+    weight_copies = [
+        pltpu.make_async_copy(
+            weight_hbm.at[pl.ds(piece * cut, cut)],
+            weight_ref.at[pl.ds(piece * cut, cut)],
+            sem.at[piece],
+        )
+        for piece in range(pieces)
+    ]
+    for copy in weight_copies:
+        copy.start()
+    first = 0
+    packed_copies = []
+    for place, source in enumerate((q_hbm, k_hbm, v_hbm)):
+        cols = source.shape[1]
+        packed_copies.append(
+            pltpu.make_async_copy(
+                source, packed_ref.at[:, pl.ds(first, cols)], sem.at[pieces + 1 + place]
+            )
+        )
+        packed_copies[-1].start()
+        first += cols
+    cot_copy.wait()
+    for piece, copy in enumerate(weight_copies):
+        copy.wait()
+        packed_ref[:, first + piece * cut : first + (piece + 1) * cut] = dot_nt(
+            cot_ref[...], weight_ref[piece * cut : (piece + 1) * cut]
+        ).astype(jnp.bfloat16)
+    for copy in packed_copies:
+        copy.wait()
+
+
+def turn_kernel(parts, normed_hbm, cot_hbm, turned_ref, normed_ref, cot_ref, sem):
     cut = normed_ref.shape[1] // parts
+    copies = []
+    for which, (source, target) in enumerate(((normed_hbm, normed_ref), (cot_hbm, cot_ref))):
+        copies.append(pltpu.make_async_copy(source, target, sem.at[which]))
+        copies[-1].start()
     for which, ref in enumerate((normed_ref, cot_ref)):
+        copies[which].wait()
         turned = ref[...].astype(jnp.float32).T.astype(jnp.bfloat16)
         for part in range(parts):
             turned_ref[part, which] = turned[part * cut : (part + 1) * cut]
 
 
 def attention_kernel(
-    gathered_ref,
+    blocks,
+    *refs,
+):
+    attention_body(refs[:blocks], *refs[blocks:])
+
+
+def attention_body(
+    block_refs,
     wq_hbm,
     wk_hbm,
     wv_hbm,
@@ -71,7 +112,9 @@
     key_t_ref,
     dk_ref,
     dx_ref,
+    gathered_ref,
     weight_sem,
+    block_sem,
 ):
     me = lax.axis_index("seq")
     copies = [
@@ -80,10 +123,19 @@
             ((wq_hbm, wq_ref), (wk_hbm, wk_ref), (wv_hbm, wv_ref))
         )
     ]
+    rows = dx_ref.shape[0]
+    arrivals = []
+    for apart, source in enumerate(block_refs):
+        place = pl.ds(pl.multiple_of((me ^ apart) * rows, rows), rows)
+        arrivals.append(
+            pltpu.make_async_copy(source, gathered_ref.at[place], block_sem.at[apart])
+        )
+        arrivals[-1].start()
     for copy in copies:
         copy.start()
+    for copy in arrivals:
+        copy.wait()
     tokens = gathered_ref.shape[0]
-    rows = dx_ref.shape[0]
     blocks = tokens // rows
     kv_cols = dv_ref.shape[1]
     kv_heads = kv_cols // HEAD_SIZE
@@ -183,13 +235,13 @@
     ]
     for copy in copies:
         copy.wait()
-    parts, _, cut = terms_ref.shape
+    parts, cut, _ = terms_ref.shape
     for part in range(parts):
         out_rows = slice(part * cut, (part + 1) * cut)
         terms_ref[part] = (
-            dot_nt(dx_ref[:, :key_base], wq_ref[out_rows])
-            + dot_nt(dx_ref[:, key_base:value_base], wk_ref[out_rows])
-            + dot_nt(dx_ref[:, value_base:], wv_ref[out_rows])
+            dot_nt(wq_ref[out_rows], dx_ref[:, :key_base])
+            + dot_nt(wk_ref[out_rows], dx_ref[:, key_base:value_base])
+            + dot_nt(wv_ref[out_rows], dx_ref[:, value_base:])
         ).astype(jnp.bfloat16)
 
 
@@ -199,20 +251,26 @@
     for part in range(parts):
         joined_ref[:, :, part * rows : (part + 1) * rows] = turned_ref[part]
     wvalue_ref[...] = dot_nn(joined_ref[0], dv_ref[...])
-    woutput_ref[...] = dot_nt(attn_ref[...], joined_ref[1])
-
-
-def kernel_call(body, outs, operands, in_specs=None, scratch=(), flops=0, moved=0):
+    woutput_ref[...] = dot_nt(joined_ref[1], attn_ref[...])
+
+
+def kernel_call(body, outs, operands, in_vmem=(), scratch=(), flops=0, moved=0, room=48):
     vmem = pl.BlockSpec(memory_space=pltpu.VMEM)
+    hbm = pl.BlockSpec(memory_space=pltpu.HBM)
     return pl.pallas_call(
         body,
         out_shape=outs,
-        in_specs=in_specs or [vmem] * len(operands),
+        in_specs=[vmem if place in in_vmem else hbm for place in range(len(operands))],
         out_specs=jax.tree.map(lambda _: vmem, outs),
         scratch_shapes=list(scratch),
-        compiler_params=pltpu.CompilerParams(vmem_limit_bytes=48 * 1024 * 1024),
+        compiler_params=pltpu.CompilerParams(vmem_limit_bytes=room * 1024 * 1024),
         cost_estimate=pl.CostEstimate(flops=flops, bytes_accessed=moved, transcendentals=0),
     )(*operands)
+
+
+def swapped(value, apart):
+    count = lax.axis_size("seq")
+    return lax.ppermute(value, "seq", [(place, place ^ apart) for place in range(count)])
 
 
 def gathered_plan(
@@ -240,27 +298,40 @@
         out_grad_kernel,
         jax.ShapeDtypeStruct((rows, packed_cols), bf16),
         (out_cotangent, output_weight, stored_queries, stored_keys, stored_values),
+        scratch=(
+            pltpu.VMEM(out_cotangent.shape, bf16),
+            pltpu.VMEM(output_weight.shape, bf16),
+            pltpu.SemaphoreType.DMA((q_cols // HEAD_SIZE + 4,)),
+        ),
         flops=2 * rows * model * q_cols,
         moved=2 * model * (rows + q_cols),
-    )
-    gathered = lax.all_gather(packed, "seq", axis=0, tiled=True)
+        room=63,
+    )
+    held = {0: packed}
+    for apart in range(2, blocks, 2):
+        held[apart] = swapped(packed, apart)
+    for apart in range(0, blocks, 2):
+        held[apart + 1] = swapped(held[apart], 1)
     turned = kernel_call(
         functools.partial(turn_kernel, blocks),
         jax.ShapeDtypeStruct((blocks, 2, model // blocks, rows), bf16),
         (normed_input, out_cotangent),
+        scratch=(
+            pltpu.VMEM(normed_input.shape, bf16),
+            pltpu.VMEM(out_cotangent.shape, bf16),
+            pltpu.SemaphoreType.DMA((2,)),
+        ),
         moved=8 * rows * model,
     )
     turned = lax.all_to_all(turned, "seq", 0, 0)
-    anywhere = pl.BlockSpec(memory_space=pl.ANY)
     terms, attn, dv = kernel_call(
-        attention_kernel,
+        functools.partial(attention_kernel, blocks),
         (
-            jax.ShapeDtypeStruct((groups, rows, model // groups), bf16),
+            jax.ShapeDtypeStruct((groups, model // groups, rows), bf16),
             jax.ShapeDtypeStruct((q_cols, tokens), bf16),
             jax.ShapeDtypeStruct((tokens, kv_cols), bf16),
         ),
-        (gathered, query_weight, key_matrix, value_matrix),
-        in_specs=[pl.BlockSpec(memory_space=pltpu.VMEM)] + [anywhere] * 3,
+        (*(held[apart] for apart in range(blocks)), query_weight, key_matrix, value_matrix),
         scratch=(
             pltpu.VMEM(query_weight.shape, bf16),
             pltpu.VMEM(key_matrix.shape, bf16),
@@ -272,7 +343,9 @@
             pltpu.VMEM((kv_heads, HEAD_SIZE, tokens), bf16),
             pltpu.VMEM((kv_heads, rows, HEAD_SIZE), f32),
             pltpu.VMEM((rows, q_cols + 2 * kv_cols), bf16),
+            pltpu.VMEM((tokens, packed_cols), bf16),
             pltpu.SemaphoreType.DMA((3,)),
+            pltpu.SemaphoreType.DMA((blocks,)),
         ),
         flops=8 * tokens * tokens * q_cols,
         moved=2 * (tokens * packed_cols + model * (q_cols + 2 * kv_cols)),
@@ -282,19 +355,22 @@
         weight_grad_kernel,
         (
             jax.ShapeDtypeStruct((model // blocks, kv_cols), f32),
-            jax.ShapeDtypeStruct((q_cols, model // blocks), f32),
+            jax.ShapeDtypeStruct((model // blocks, q_cols), f32),
         ),
         (turned, attn, dv),
+        in_vmem=(0, 1, 2),
         scratch=(pltpu.VMEM((2, model // blocks, tokens), bf16),),
         flops=2 * tokens * (model // blocks) * (q_cols + kv_cols),
         moved=4 * (model // blocks) * (tokens + q_cols + kv_cols),
     )
     grad_input = jnp.sum(arrived.astype(f32), axis=0).astype(bf16)
-    return (grad_input, grad_wvalue, grad_woutput)
+    return (grad_input.T, grad_wvalue, grad_woutput.T)
 
 
 def local(normed_input, *others):
-    if normed_input.shape[0] * lax.axis_size("seq") <= WINDOW_LENGTH:
+    blocks = lax.axis_size("seq")
+    fits = normed_input.shape[0] * blocks <= WINDOW_LENGTH
+    if fits and blocks % 2 == 0 and blocks & (blocks - 1) == 0:
         return gathered_plan(normed_input, *others)
     return windowed_plan(normed_input, *others)
 

time: 111 us -> 73.1 us (0.66)
  waiting for transfers between devices: 50 us -> 25.5 us
  between operations: 14.1 us -> 0.7 us
  local copies, waits for them, and re-layouts: 9.97 us -> 4.56 us
  starting transfers between devices: 9.81 us -> 14.3 us
  Pallas kernels: 24.2 us -> 27 us
    all_gather x1 -> x0, waiting for transfers between devices: 36.3 us -> none  [gathered_plan(): gathered = lax.all_gather(packed, 'seq', axis=0, tiled=True)]
    ppermute x0 -> x7, waiting for transfers between devices: none -> 11.1 us  [swapped(): lax.ppermute(value, 'seq', [(place, place ^ apart) for place in range(cou...]
    ppermute x0 -> x7, starting transfers between devices: none -> 5.11 us  [swapped(): lax.ppermute(value, 'seq', [(place, place ^ apart) for place in range(cou...]
    unnamed x19 -> x14, local copies, waits for them, and re-layouts: 8.91 us -> 4.56 us
    pallas_call x4, Pallas kernels: 24.2 us -> 27 us  [kernel_call(): pl.pallas_call(body, out_shape=outs, in_specs=[vmem if place in in_vmem e...]
  transfers between devices with their start and end apart: 3 -> 9, of which waited for: 2 -> 5; matrix products, arithmetic and copies ran while one was open for 2% -> 0% of each run, Pallas kernels for 21% -> 32%
where the time goes in v2:
time: 73.1 us; the launch traced here: 72.7 us
  Pallas kernels  27 us (37%)
  waiting for transfers between devices  25.5 us (35%)
  starting transfers between devices  14.3 us (20%)
  local copies, waits for them, and re-layouts  4.56 us (6%)
  other arithmetic  0.76 us (1%)
    pallas_call x4, Pallas kernels, kernel_call(): pl.pallas_call(body, out_shape=outs, in_specs=[vmem if place in in_vmem e...  27 us
    all_to_all x1, waiting for transfers between devices, gathered_plan(): arrived = lax.all_to_all(terms, 'head', 0, 0)  14.3 us
    ppermute x7, waiting for transfers between devices, swapped(): lax.ppermute(value, 'seq', [(place, place ^ apart) for place in range(cou...  11.1 us
    ppermute x7, starting transfers between devices, swapped(): lax.ppermute(value, 'seq', [(place, place ^ apart) for place in range(cou...  5.11 us
    all_to_all x1, starting transfers between devices, gathered_plan(): arrived = lax.all_to_all(terms, 'head', 0, 0)  4.89 us
    unnamed x14, local copies, waits for them, and re-layouts  4.56 us
    all_to_all x1, starting transfers between devices, gathered_plan(): turned = lax.all_to_all(turned, 'seq', 0, 0)  4.27 us
  transfers between devices with their start and end apart: 9, of which 5 were waited for; matrix products, arithmetic and copies ran while one was open for 0% of the time, Pallas kernels for 32%

profile of v2, /device:TPU:0, one launch (start us, length us, event | category | flops | bytes accessed | tf_op | source)
XLA Modules:
  0.0 72.7 jit_solution(5727999316340372374)
XLA Ops:
  0.6 3.9 %shard_map.112.refs_0_ = bf16[128,1536]{1,0:T(8,128)(2,1)} custom-call(bf16[128,2304]{1,0:T(8,128)(2,1)} %cot_hbm.3, bf16[512,2304]{1,0:T(8,128)(2,1)} %weight_hbm.1, bf16[128,512]{1,0:T(8,128)(2,1)} %q_hbm.1, bf16[128,256]{1,0:T(8,128)(2,1)} %k_hbm.1, bf16[128,256]{1,0:T(8,128)(2,1)} %v_hbm.1), custom_call_target="tpu_custom_call" | custom-call | flops 301989888 | bytes 2949120 | tf_op jit(solution)/shard_map/pallas_call | solution.py:260
  4.6 4.0 %collective-permute-start.5 = (bf16[128,1536]{1,0:T(8,128)(2,1)}, bf16[128,1536]{1,0:T(8,128)(2,1)S(1)}, u32[]{:S(2)}, u32[]{:S(2)}) collective-permute-start(bf16[128,1536]{1,0:T(8,128)(2,1)} %shard_map.112.refs_0_), channel_id=1, source_target_pairs={{0,24},{4,28},{8,16},{12,20},{16,8},{20,12},{24,0},{28,4},{1,25},{... | collective-permute-start | bytes 1179656 | tf_op jit(solution)/shard_map/ppermute | solution.py:273
  8.5 0.5 collective-permute-start.3
  9.0 0.1 collective-permute-start.1
  9.2 1.1 %copy-done.1 = bf16[128,2304]{1,0:T(8,128)(2,1)S(1)} copy-done((bf16[128,2304]{1,0:T(8,128)(2,1)S(1)}, bf16[128,2304]{1,0:T(8,128)(2,1)}, u32[]{:S(2)}) %copy-start.1) | copy-done | bytes 589848
  10.3 1.8 %shard_map.114 = bf16[8,2,288,128]{3,2,1,0:T(8,128)(2,1)} custom-call(bf16[128,2304]{1,0:T(8,128)(2,1)S(1)} %copy-done.1, bf16[128,2304]{1,0:T(8,128)(2,1)S(1)} %copy-done), custom_call_target="tpu_custom_call" | custom-call | bytes 2359296 | tf_op jit(solution)/shard_map/pallas_call | solution.py:260
  12.0 0.0 copy-start.2
  12.0 4.3 %all-to-all-start.1 = ((bf16[8,2,288,128]{3,2,1,0:T(8,128)(2,1)}), bf16[8,2,288,128]{3,2,1,0:T(8,128)(2,1)S(1)}, u32[]{:S(2)}, u32[]{:S(2)}) async-start(bf16[8,2,288,128]{3,2,1,0:T(8,128)(2,1)} %shard_map.114), calls=%async_computation.1 | async-start | bytes 2359296 | tf_op jit(solution)/shard_map/all_to_all | solution.py:326
  16.3 0.5 collective-permute-start
  16.8 1.9 %collective-permute-done.5.refs_6_ = bf16[128,1536]{1,0:T(8,128)(2,1)S(1)} collective-permute-done((bf16[128,1536]{1,0:T(8,128)(2,1)}, bf16[128,1536]{1,0:T(8,128)(2,1)S(1)}, u32[]{:S(2)}, u32[]{:S(2)}) %collective-permute-start.5) | collective-permute-done | bytes 393248 | tf_op jit(solution)/shard_map/ppermute | solution.py:273
  18.7 7.6 %collective-permute-done.3.refs_4_ = bf16[128,1536]{1,0:T(8,128)(2,1)S(1)} collective-permute-done((bf16[128,1536]{1,0:T(8,128)(2,1)}, bf16[128,1536]{1,0:T(8,128)(2,1)S(1)}, u32[]{:S(2)}, u32[]{:S(2)}) %collective-permute-start.3) | collective-permute-done | bytes 393248 | tf_op jit(solution)/shard_map/ppermute | solution.py:273
  26.4 0.0 collective-permute-start.4
  26.4 0.7 %copy-done.3 = bf16[128,1536]{1,0:T(8,128)(2,1)} copy-done((bf16[128,1536]{1,0:T(8,128)(2,1)}, bf16[128,1536]{1,0:T(8,128)(2,1)S(1)}, u32[]{:S(2)}) %copy-start.3) | copy-done | bytes 393240
  27.1 0.6 collective-permute-done.1.refs_2_
  27.7 0.0 collective-permute-start.2
  27.7 0.7 %copy-done.5 = bf16[128,1536]{1,0:T(8,128)(2,1)} copy-done((bf16[128,1536]{1,0:T(8,128)(2,1)}, bf16[128,1536]{1,0:T(8,128)(2,1)S(1)}, u32[]{:S(2)}) %copy-start.5) | copy-done | bytes 393240
  28.5 1.0 %collective-permute-done.2.refs_3_ = bf16[128,1536]{1,0:T(8,128)(2,1)S(1)} collective-permute-done((bf16[128,1536]{1,0:T(8,128)(2,1)S(1)}, bf16[128,1536]{1,0:T(8,128)(2,1)S(1)}, u32[]{:S(2)}, u32[]{:S(2)}) %collective-permute-start.2) | collective-permute-done | bytes 393248 | tf_op jit(solution)/shard_map/ppermute | solution.py:273
  29.5 1.0 %copy-done.4 = bf16[128,1536]{1,0:T(8,128)(2,1)S(1)} copy-done((bf16[128,1536]{1,0:T(8,128)(2,1)S(1)}, bf16[128,1536]{1,0:T(8,128)(2,1)}, u32[]{:S(2)}) %copy-start.4) | copy-done | bytes 393240
  30.5 1.0 %copy-done.6 = bf16[128,1536]{1,0:T(8,128)(2,1)S(1)} copy-done((bf16[128,1536]{1,0:T(8,128)(2,1)S(1)}, bf16[128,1536]{1,0:T(8,128)(2,1)}, u32[]{:S(2)}) %copy-start.6) | copy-done | bytes 393240
  31.4 19.8 %shard_map.113 = (bf16[4,576,128]{2,1,0:T(8,128)(2,1)}, bf16[512,1024]{1,0:T(8,128)(2,1)S(1)}, bf16[1024,256]{1,0:T(8,128)(2,1)S(1)}) custom-call(bf16[128,1536]{1,0:T(8,128)(2,1)S(1)} %copy-done.2, bf16[128,1536]{1,0:T(8,128)(2,1)S(1)} %collective-permute-done.refs_1_, bf16[128,1536]{1,0:T(8,128)(2,1)S(1)} %copy-done.6, ...), custom_call_target="tpu_custom_call" | custom-call | flops 4294967296 | bytes 7864320 | tf_op jit(solution)/shard_map/pallas_call | solution.py:260
  51.3 4.9 %all-to-all-start = ((bf16[4,576,128]{2,1,0:T(8,128)(2,1)}), bf16[4,576,128]{2,1,0:T(8,128)(2,1)S(1)}, u32[]{:S(2)}, u32[]{:S(2)}) async-start(bf16[4,576,128]{2,1,0:T(8,128)(2,1)} %get-tuple-element.8), calls=%async_computation | async-start | bytes 1179648 | tf_op jit(solution)/shard_map/all_to_all | solution.py:353
  56.1 1.5 %shard_map.115 = (f32[288,256]{1,0:T(8,128)}, f32[288,512]{1,0:T(8,128)}) custom-call(bf16[8,2,288,128]{3,2,1,0:T(8,128)(2,1)S(1)} %all-to-all-done.1.turned_ref, bf16[512,1024]{1,0:T(8,128)(2,1)S(1)} %get-tuple-element.9.attn_ref, bf16[1024,256]{1,0:T(8,128)(2,1)S(1)} %get-tuple-element.10.dv_ref), custom_call_target="tpu_custom_call" | custom-call | flops 452984832 | bytes 2064384 | tf_op jit(solution)/shard_map/pallas_call | solution.py:260
  57.6 14.3 %all-to-all-done = bf16[4,576,128]{2,1,0:T(8,128)(2,1)S(1)} async-done(((bf16[4,576,128]{2,1,0:T(8,128)(2,1)}), bf16[4,576,128]{2,1,0:T(8,128)(2,1)S(1)}, u32[]{:S(2)}, u32[]{:S(2)}) %all-to-all-start) | async-done | bytes 589856 | tf_op jit(solution)/shard_map/all_to_all | solution.py:353
  72.0 0.8 %reduce_sum.12 = bf16[576,128]{1,0:T(8,128)(2,1)} reduce(bf16[4,576,128]{2,1,0:T(8,128)(2,1)S(1)} %all-to-all-done, bf16[]{:T(256)} %constant.2.clone.1), dimensions={0}, to_apply=%region_0.0 | reduce | flops 221184 | bytes 737282 | tf_op jit(solution)/shard_map/reduce_sum | solution.py:366
  (13 shorter events, 0.0 us)
Async XLA Ops:
  0.6 8.6 %copy-start = (bf16[128,2304]{1,0:T(8,128)(2,1)S(1)}, bf16[128,2304]{1,0:T(8,128)(2,1)}, u32[]{:S(2)}) copy-start(bf16[128,2304]{1,0:T(8,128)(2,1)} %cot_hbm.3) | copy-start | bytes 1769476
  4.6 14.2 %collective-permute-start.5 = (bf16[128,1536]{1,0:T(8,128)(2,1)}, bf16[128,1536]{1,0:T(8,128)(2,1)S(1)}, u32[]{:S(2)}, u32[]{:S(2)}) collective-permute-start(bf16[128,1536]{1,0:T(8,128)(2,1)} %shard_map.112.refs_0_), channel_id=1, source_target_pairs={{0,24},{4,28},{8,16},{12,20},{16,8},{20,12},{24,0},{28,4},{1,25},{... | collective-permute-start | bytes 1179656 | tf_op jit(solution)/shard_map/ppermute | solution.py:273
  8.5 17.8 %collective-permute-start.3 = (bf16[128,1536]{1,0:T(8,128)(2,1)}, bf16[128,1536]{1,0:T(8,128)(2,1)S(1)}, u32[]{:S(2)}, u32[]{:S(2)}) collective-permute-start(bf16[128,1536]{1,0:T(8,128)(2,1)} %shard_map.112.refs_0_), channel_id=1, source_target_pairs={{0,16},{4,20},{8,24},{12,28},{16,0},{20,4},{24,8},{28,12},{1,17},{... | collective-permute-start | bytes 1179656 | tf_op jit(solution)/shard_map/ppermute | solution.py:273
  9.0 18.7 %collective-permute-start.1 = (bf16[128,1536]{1,0:T(8,128)(2,1)}, bf16[128,1536]{1,0:T(8,128)(2,1)S(1)}, u32[]{:S(2)}, u32[]{:S(2)}) collective-permute-start(bf16[128,1536]{1,0:T(8,128)(2,1)} %shard_map.112.refs_0_), channel_id=1, source_target_pairs={{0,8},{4,12},{8,0},{12,4},{16,24},{20,28},{24,16},{28,20},{1,9},{5... | collective-permute-start | bytes 1179656 | tf_op jit(solution)/shard_map/ppermute | solution.py:273
  9.2 1.1 %copy-start.1 = (bf16[128,2304]{1,0:T(8,128)(2,1)S(1)}, bf16[128,2304]{1,0:T(8,128)(2,1)}, u32[]{:S(2)}) copy-start(bf16[128,2304]{1,0:T(8,128)(2,1)} %normed_hbm.1) | copy-start | bytes 1769476
  12.0 4.3 %copy-start.2 = (bf16[128,1536]{1,0:T(8,128)(2,1)S(1)}, bf16[128,1536]{1,0:T(8,128)(2,1)}, u32[]{:S(2)}) copy-start(bf16[128,1536]{1,0:T(8,128)(2,1)} %shard_map.112.refs_0_) | copy-start | bytes 1179652
  12.0 39.2 %all-to-all-start.1 = ((bf16[8,2,288,128]{3,2,1,0:T(8,128)(2,1)}), bf16[8,2,288,128]{3,2,1,0:T(8,128)(2,1)S(1)}, u32[]{:S(2)}, u32[]{:S(2)}) async-start(bf16[8,2,288,128]{3,2,1,0:T(8,128)(2,1)} %shard_map.114), calls=%async_computation.1 | async-start | bytes 2359296 | tf_op jit(solution)/shard_map/all_to_all | solution.py:326
  16.3 12.2 %collective-permute-start = (bf16[128,1536]{1,0:T(8,128)(2,1)S(1)}, bf16[128,1536]{1,0:T(8,128)(2,1)S(1)}, u32[]{:S(2)}, u32[]{:S(2)}) collective-permute-start(bf16[128,1536]{1,0:T(8,128)(2,1)S(1)} %copy-done.2), channel_id=1, source_target_pairs={{0,4},{4,0},{8,12},{12,8},{16,20},{20,16},{24,28},{28,24},{1,5},{5... | collective-permute-start | bytes 1179656 | tf_op jit(solution)/shard_map/ppermute | solution.py:273
  18.7 9.8 %collective-permute-start.6 = (bf16[128,1536]{1,0:T(8,128)(2,1)S(1)}, bf16[128,1536]{1,0:T(8,128)(2,1)S(1)}, u32[]{:S(2)}, u32[]{:S(2)}) collective-permute-start(bf16[128,1536]{1,0:T(8,128)(2,1)S(1)} %collective-permute-done.5.refs_6_), channel_id=1, source_target_pairs={{0,4},{4,0},{8,12},{12,8},{16,20},{20,16},{24,28},{28,24},{1,5},{5... | collective-permute-start | bytes 1179656 | tf_op jit(solution)/shard_map/ppermute | solution.py:273
  26.4 2.1 %collective-permute-start.4 = (bf16[128,1536]{1,0:T(8,128)(2,1)S(1)}, bf16[128,1536]{1,0:T(8,128)(2,1)S(1)}, u32[]{:S(2)}, u32[]{:S(2)}) collective-permute-start(bf16[128,1536]{1,0:T(8,128)(2,1)S(1)} %collective-permute-done.3.refs_4_), channel_id=1, source_target_pairs={{0,4},{4,0},{8,12},{12,8},{16,20},{20,16},{24,28},{28,24},{1,5},{5... | collective-permute-start | bytes 1179656 | tf_op jit(solution)/shard_map/ppermute | solution.py:273
  26.4 0.7 %copy-start.3 = (bf16[128,1536]{1,0:T(8,128)(2,1)}, bf16[128,1536]{1,0:T(8,128)(2,1)S(1)}, u32[]{:S(2)}) copy-start(bf16[128,1536]{1,0:T(8,128)(2,1)S(1)} %collective-permute-done.3.refs_4_) | copy-start | bytes 1179652
  27.7 1.7 %collective-permute-start.2 = (bf16[128,1536]{1,0:T(8,128)(2,1)S(1)}, bf16[128,1536]{1,0:T(8,128)(2,1)S(1)}, u32[]{:S(2)}, u32[]{:S(2)}) collective-permute-start(bf16[128,1536]{1,0:T(8,128)(2,1)S(1)} %collective-permute-done.1.refs_2_), channel_id=1, source_target_pairs={{0,4},{4,0},{8,12},{12,8},{16,20},{20,16},{24,28},{28,24},{1,5},{5... | collective-permute-start | bytes 1179656 | tf_op jit(solution)/shard_map/ppermute | solution.py:273
  27.7 0.7 %copy-start.5 = (bf16[128,1536]{1,0:T(8,128)(2,1)}, bf16[128,1536]{1,0:T(8,128)(2,1)S(1)}, u32[]{:S(2)}) copy-start(bf16[128,1536]{1,0:T(8,128)(2,1)S(1)} %collective-permute-done.1.refs_2_) | copy-start | bytes 1179652
  29.5 1.0 %copy-start.4 = (bf16[128,1536]{1,0:T(8,128)(2,1)S(1)}, bf16[128,1536]{1,0:T(8,128)(2,1)}, u32[]{:S(2)}) copy-start(bf16[128,1536]{1,0:T(8,128)(2,1)} %copy-done.3) | copy-start | bytes 1179652
  30.5 1.0 %copy-start.6 = (bf16[128,1536]{1,0:T(8,128)(2,1)S(1)}, bf16[128,1536]{1,0:T(8,128)(2,1)}, u32[]{:S(2)}) copy-start(bf16[128,1536]{1,0:T(8,128)(2,1)} %copy-done.5) | copy-start | bytes 1179652
  51.3 20.7 %all-to-all-start = ((bf16[4,576,128]{2,1,0:T(8,128)(2,1)}), bf16[4,576,128]{2,1,0:T(8,128)(2,1)S(1)}, u32[]{:S(2)}, u32[]{:S(2)}) async-start(bf16[4,576,128]{2,1,0:T(8,128)(2,1)} %get-tuple-element.8), calls=%async_computation | async-start | bytes 1179648 | tf_op jit(solution)/shard_map/all_to_all | solution.py:353

commit v3 on v0

--- a/solution.py
+++ b/solution.py
@@ -1,6 +1,10 @@
+import functools
+
 import jax
 import jax.numpy as jnp
 from jax import lax
+from jax.experimental import pallas as pl
+from jax.experimental.pallas import tpu as pltpu
 from jax.sharding import PartitionSpec as P
 
 HEAD_SIZE = 128
@@ -9,6 +13,8 @@
 
 
 logit_scale = 1.0 / 12.0
+log2_scale = 1.4426950408889634 / 12.0
+excluded = -1e30
 
 
 def passed_along(value, axis, steps):
@@ -17,7 +23,380 @@
     return lax.ppermute(value, axis, [(source, source + steps) for source in range(leading, last)])
 
 
-def local(
+NT = (((1,), (1,)), ((), ()))
+
+
+def dot_nt(left, right):
+    return lax.dot_general(left, right, NT, preferred_element_type=jnp.float32)
+
+
+def dot_nn(left, right):
+    return jnp.dot(left, right, preferred_element_type=jnp.float32)
+
+
+def at(place, size):
+    return pl.ds(pl.multiple_of(place * size, size), size)
+
+
+def out_grad_kernel(
+    cot_hbm, weight_hbm, q_hbm, k_hbm, v_hbm, same_ref, other_ref, cot_ref, weight_ref, sem
+):
+    core = lax.axis_index("seq") % 2
+    cut = weight_ref.shape[0] // 2
+    cot_copy = pltpu.make_async_copy(cot_hbm, cot_ref, sem.at[0])
+    cot_copy.start()
+    halves = ((other_ref, 1 - core), (same_ref, core))
+    weight_copies = []
+    for place, (_, half) in enumerate(halves):
+        weight_copies.append(
+            pltpu.make_async_copy(
+                weight_hbm.at[at(half, cut)], weight_ref.at[at(place, cut)], sem.at[1 + place]
+            )
+        )
+        weight_copies[-1].start()
+    plain_copies = []
+    for place, (target, half) in enumerate(halves):
+        first = 0
+        for which, source in enumerate((q_hbm, k_hbm, v_hbm)):
+            cols = source.shape[1] // 2
+            plain_copies.append(
+                pltpu.make_async_copy(
+                    source.at[:, at(half, cols)],
+                    target.at[:, pl.ds(first, cols)],
+                    sem.at[3 + 3 * place + which],
+                )
+            )
+            plain_copies[-1].start()
+            first += cols
+    cot_copy.wait()
+    for place, (target, _) in enumerate(halves):
+        weight_copies[place].wait()
+        target[:, first:] = dot_nt(
+            cot_ref[...], weight_ref[place * cut : (place + 1) * cut]
+        ).astype(jnp.bfloat16)
+    for copy in plain_copies:
+        copy.wait()
+
+
+def turn_kernel(parts, normed_hbm, cot_hbm, turned_ref, normed_ref, cot_ref, sem):
+    cut = normed_ref.shape[1] // parts
+    copies = []
+    for which, (source, target) in enumerate(((normed_hbm, normed_ref), (cot_hbm, cot_ref))):
+        copies.append(pltpu.make_async_copy(source, target, sem.at[which]))
+        copies[-1].start()
+    for which, ref in enumerate((normed_ref, cot_ref)):
+        copies[which].wait()
+        turned = ref[...].astype(jnp.float32).T.astype(jnp.bfloat16)
+        for part in range(parts):
+            turned_ref[part, which] = turned[part * cut : (part + 1) * cut]
+
+
+def attention_kernel(blocks, *refs):
+    attention_body(refs[:blocks], *refs[blocks:])
+
+
+def attention_body(
+    block_refs,
+    dx_own_ref,
+    dx_far_ref,
+    attn_ref,
+    dv_ref,
+    gathered_ref,
+    score_even_ref,
+    score_odd_ref,
+    prob_ref,
+    grad_t_ref,
+    delta_ref,
+    query_ref,
+    value_t_ref,
+    key_t_ref,
+    dq_t_ref,
+    dk_ref,
+    sem,
+):
+    me = lax.axis_index("seq")
+    core, chip = me % 2, me // 2
+    rows = dx_own_ref.shape[0]
+    arrivals = []
+    for apart, source in enumerate(block_refs):
+        arrivals.append(
+            pltpu.make_async_copy(source, gathered_ref.at[at(me ^ apart, rows)], sem.at[apart])
+        )
+        arrivals[-1].start()
+    for copy in arrivals:
+        copy.wait()
+    tokens = gathered_ref.shape[0]
+    size = 2 * rows
+    steps = tokens // size
+    wide = QUERIES_PER_KEY * size
+    heads = QUERIES_PER_KEY
+    key_cols = slice(heads * HEAD_SIZE, (heads + 1) * HEAD_SIZE)
+    value_cols = slice((heads + 1) * HEAD_SIZE, (heads + 2) * HEAD_SIZE)
+    grad_base = (heads + 2) * HEAD_SIZE
+    value_t_ref[...] = gathered_ref[:, value_cols].T
+    key_t_ref[...] = gathered_ref[:, key_cols].T
+    key_place = lax.broadcasted_iota(jnp.int32, (size, wide), 0)
+    query_place = lax.broadcasted_iota(jnp.int32, (size, wide), 1) % size
+    allowed = key_place <= query_place
+
+    for step in range(steps):
+        span = (step + 1) * size
+        own = slice(step * size, span)
+        lanes = slice(step * wide, (step + 1) * wide)
+        score_ref = score_odd_ref if step % 2 else score_even_ref
+        queries = jnp.concatenate(
+            [gathered_ref[own, h * HEAD_SIZE : (h + 1) * HEAD_SIZE] for h in range(heads)], axis=0
+        )
+        query_ref[lanes] = queries
+        top = None
+        for piece in range(step + 1):
+            part = slice(piece * size, (piece + 1) * size)
+            scores = dot_nt(gathered_ref[part, key_cols], queries)
+            if piece == step:
+                scores = jnp.where(allowed, scores, excluded)
+            score_ref[part] = scores
+            largest = jnp.max(scores.reshape(size // 8, 8, wide), axis=0)
+            top = largest if top is None else jnp.maximum(top, largest)
+        top = jnp.max(top, axis=0, keepdims=True)
+        total = None
+        for piece in range(step + 1):
+            part = slice(piece * size, (piece + 1) * size)
+            weights = jnp.exp2((score_ref[part] - top) * log2_scale)
+            prob_ref[part, lanes] = weights.astype(jnp.bfloat16)
+            summed = jnp.sum(weights.reshape(size // 8, 8, wide), axis=0)
+            total = summed if total is None else total + summed
+        inverse = 1.0 / jnp.sum(total, axis=0, keepdims=True)
+        attn = dot_nn(value_t_ref[:, :span], prob_ref[:span, lanes]) * inverse
+        for h in range(heads):
+            attn_ref[h * HEAD_SIZE : (h + 1) * HEAD_SIZE, own] = attn[
+                :, h * size : (h + 1) * size
+            ].astype(jnp.bfloat16)
+        grads_t = jnp.concatenate(
+            [
+                gathered_ref[
+                    own, grad_base + h * HEAD_SIZE : grad_base + (h + 1) * HEAD_SIZE
+                ].T
+                for h in range(heads)
+            ],
+            axis=1,
+        )
+        grads_t = (grads_t.astype(jnp.float32) * inverse).astype(jnp.bfloat16)
+        grad_t_ref[:, lanes] = grads_t
+        delta_ref[:, lanes] = jnp.sum(grads_t.astype(jnp.float32) * attn, axis=0, keepdims=True)
+
+    for step in range(steps):
+        own = slice(step * size, (step + 1) * size)
+        dv_ref[own] = dot_nt(prob_ref[own, step * wide :], grad_t_ref[:, step * wide :]).astype(
+            jnp.bfloat16
+        )
+
+    dq_t_ref[...] = jnp.zeros_like(dq_t_ref)
+    dk_ref[...] = jnp.zeros_like(dk_ref)
+    for step in range(steps):
+        key_step = jnp.minimum(chip, step)
+        query_step = jnp.maximum(chip, step)
+        dprob = dot_nn(
+            gathered_ref[at(key_step, size), value_cols], grad_t_ref[:, at(query_step, wide)]
+        )
+        dscore = (
+            prob_ref[at(key_step, size), at(query_step, wide)].astype(jnp.float32)
+            * (dprob - delta_ref[:, at(query_step, wide)])
+        ).astype(jnp.bfloat16)
+
+        @pl.when(step <= chip)
+        def _():
+            dq_t_ref[...] += dot_nn(key_t_ref[:, at(key_step, size)], dscore)
+
+        @pl.when(step >= chip)
+        def _():
+            dk_ref[...] += dot_nn(dscore, query_ref[at(query_step, wide)])
+
+    for target, half in ((dx_far_ref, 1 - core), (dx_own_ref, core)):
+        for h in range(heads):
+            target[:, h * HEAD_SIZE : (h + 1) * HEAD_SIZE] = (
+                (logit_scale * dq_t_ref[:, at(2 * h + half, rows)])
+                .T.astype(jnp.bfloat16)
+            )
+        target[:, key_cols] = (logit_scale * dk_ref[at(half, rows)]).astype(jnp.bfloat16)
+        target[:, value_cols] = dv_ref[at(2 * chip + half, rows)]
+
+
+def input_terms_kernel(
+    apart_groups, own_ref, far_ref, wq_ref, wk_ref, wv_ref, *refs
+):
+    terms, dx_ref = refs[:-1], refs[-1]
+    core = lax.axis_index("seq") % 2
+    group = lax.axis_index("head")
+    q_cols = wq_ref.shape[1] // 2
+    kv_cols = wk_ref.shape[1] // 2
+    for source, half in ((own_ref, core), (far_ref, 1 - core)):
+        dx_ref[:, at(half, q_cols)] = source[:, :q_cols]
+        dx_ref[:, pl.ds(pl.multiple_of(2 * q_cols + half * kv_cols, kv_cols), kv_cols)] = source[
+            :, q_cols : q_cols + kv_cols
+        ]
+        dx_ref[
+            :, pl.ds(pl.multiple_of(2 * q_cols + (2 + half) * kv_cols, kv_cols), kv_cols)
+        ] = source[:, q_cols + kv_cols :]
+    for apart, target in zip(apart_groups, terms):
+        cut = target.shape[0]
+        place = at(group ^ apart, cut)
+        target[...] = (
+            dot_nt(wq_ref[place], dx_ref[:, : 2 * q_cols])
+            + dot_nt(wk_ref[place], dx_ref[:, 2 * q_cols : 2 * q_cols + 2 * kv_cols])
+            + dot_nt(wv_ref[place], dx_ref[:, 2 * q_cols + 2 * kv_cols :])
+        ).astype(target.dtype)
+
+
+def weight_grad_kernel(
+    turned_ref, attn_ref, far_attn_ref, dv_ref, far_dv_ref, wvalue_ref, woutput_ref, joined_ref
+):
+    core = lax.axis_index("seq") % 2
+    parts = turned_ref.shape[0]
+    rows = turned_ref.shape[3]
+    for part in range(parts):
+        joined_ref[:, :, part * rows : (part + 1) * rows] = turned_ref[part]
+    for half, attn, dv in ((core, attn_ref, dv_ref), (1 - core, far_attn_ref, far_dv_ref)):
+        wvalue_ref[:, at(half, dv.shape[1])] = dot_nn(joined_ref[0], dv[...])
+        woutput_ref[:, at(half, attn.shape[0])] = dot_nt(joined_ref[1], attn[...])
+
+
+def kernel_call(body, outs, operands, in_vmem=(), scratch=(), flops=0, moved=0, room=32):
+    vmem = pl.BlockSpec(memory_space=pltpu.VMEM)
+    hbm = pl.BlockSpec(memory_space=pltpu.HBM)
+    return pl.pallas_call(
+        body,
+        out_shape=outs,
+        in_specs=[vmem if place in in_vmem else hbm for place in range(len(operands))],
+        out_specs=jax.tree.map(lambda _: vmem, outs),
+        scratch_shapes=list(scratch),
+        compiler_params=pltpu.CompilerParams(vmem_limit_bytes=room * 1024 * 1024),
+        cost_estimate=pl.CostEstimate(flops=flops, bytes_accessed=moved, transcendentals=0),
+    )(*operands)
+
+
+def swapped(value, axis, apart):
+    count = lax.axis_size(axis)
+    return lax.ppermute(value, axis, [(place, place ^ apart) for place in range(count)])
+
+
+def gathered_plan(
+    normed_input,
+    stored_queries,
+    stored_keys,
+    stored_values,
+    query_weight,
+    key_matrix,
+    value_matrix,
+    output_weight,
+    out_cotangent,
+):
+    bf16, f32 = jnp.bfloat16, jnp.float32
+    rows, model = normed_input.shape
+    blocks = lax.axis_size("seq")
+    groups = lax.axis_size("head")
+    tokens = rows * blocks
+    q_cols = stored_queries.shape[1] // 2
+    kv_cols = HEAD_SIZE
+    wide = 2 * QUERIES_PER_KEY * rows
+    packed_cols = 2 * q_cols + 2 * kv_cols
+    shape = jax.ShapeDtypeStruct
+    same, other = kernel_call(
+        out_grad_kernel,
+        (shape((rows, packed_cols), bf16),) * 2,
+        (out_cotangent, output_weight, stored_queries, stored_keys, stored_values),
+        scratch=(
+            pltpu.VMEM(out_cotangent.shape, bf16),
+            pltpu.VMEM(output_weight.shape, bf16),
+            pltpu.SemaphoreType.DMA((9,)),
+        ),
+        flops=4 * rows * model * q_cols,
+        moved=2 * model * (rows + 2 * q_cols),
+        room=63,
+    )
+    held = [same] + [
+        swapped(other if apart % 2 else same, "seq", apart) for apart in range(1, blocks)
+    ]
+    turned = kernel_call(
+        functools.partial(turn_kernel, blocks),
+        shape((blocks, 2, model // blocks, rows), bf16),
+        (normed_input, out_cotangent),
+        scratch=(
+            pltpu.VMEM(normed_input.shape, bf16),
+            pltpu.VMEM(out_cotangent.shape, bf16),
+            pltpu.SemaphoreType.DMA((2,)),
+        ),
+        moved=8 * rows * model,
+    )
+    turned = lax.all_to_all(turned, "seq", 0, 0)
+    dx_own, dx_far, attn, dv = kernel_call(
+        functools.partial(attention_kernel, blocks),
+        (
+            shape((rows, q_cols + 2 * kv_cols), bf16),
+            shape((rows, q_cols + 2 * kv_cols), bf16),
+            shape((q_cols, tokens), bf16),
+            shape((tokens, kv_cols), bf16),
+        ),
+        held,
+        scratch=(
+            pltpu.VMEM((tokens, packed_cols), bf16),
+            pltpu.VMEM((tokens, wide), f32),
+            pltpu.VMEM((tokens, wide), f32),
+            pltpu.VMEM((tokens, tokens * QUERIES_PER_KEY), bf16),
+            pltpu.VMEM((HEAD_SIZE, tokens * QUERIES_PER_KEY), bf16),
+            pltpu.VMEM((1, tokens * QUERIES_PER_KEY), f32),
+            pltpu.VMEM((tokens * QUERIES_PER_KEY, HEAD_SIZE), bf16),
+            pltpu.VMEM((HEAD_SIZE, tokens), bf16),
+            pltpu.VMEM((HEAD_SIZE, tokens), bf16),
+            pltpu.VMEM((HEAD_SIZE, wide), f32),
+            pltpu.VMEM((2 * rows, HEAD_SIZE), f32),
+            pltpu.SemaphoreType.DMA((blocks,)),
+        ),
+        flops=8 * tokens * tokens * q_cols,
+        moved=2 * tokens * packed_cols,
+    )
+    dx_got = swapped(dx_far, "seq", 1)
+    aparts = tuple(range(groups - 1, -1, -1))
+    terms = kernel_call(
+        functools.partial(input_terms_kernel, aparts),
+        tuple(shape((model // groups, rows), bf16 if apart else f32) for apart in aparts),
+        (dx_own, dx_got, query_weight, key_matrix, value_matrix),
+        in_vmem=range(5),
+        scratch=(pltpu.VMEM((rows, 2 * (q_cols + 2 * kv_cols)), bf16),),
+        flops=4 * rows * model * (q_cols + 2 * kv_cols),
+        moved=4 * model * (q_cols + 2 * kv_cols),
+    )
+    grad_input = terms[-1]
+    for apart, term in zip(aparts[:-1], terms[:-1]):
+        grad_input = grad_input + swapped(term, "head", apart).astype(f32)
+    grad_wvalue, grad_woutput = kernel_call(
+        weight_grad_kernel,
+        (
+            shape((model // blocks, 2 * kv_cols), f32),
+            shape((model // blocks, 2 * q_cols), f32),
+        ),
+        (turned, attn, swapped(attn, "seq", 1), dv, swapped(dv, "seq", 1)),
+        in_vmem=range(5),
+        scratch=(pltpu.VMEM((2, model // blocks, tokens), bf16),),
+        flops=4 * tokens * (model // blocks) * (q_cols + kv_cols),
+        moved=4 * (model // blocks) * (tokens + 2 * q_cols + 2 * kv_cols),
+    )
+    return (grad_input.astype(bf16).T, grad_wvalue, grad_woutput.T)
+
+
+def power_of_two(count):
+    return count & (count - 1) == 0
+
+
+def local(normed_input, stored_queries, stored_keys, *others):
+    blocks, groups = lax.axis_size("seq"), lax.axis_size("head")
+    whole_window = normed_input.shape[0] * blocks <= WINDOW_LENGTH
+    two_heads = stored_keys.shape[1] == 2 * HEAD_SIZE
+    paired = blocks > 1 and power_of_two(blocks) and power_of_two(groups)
+    plan = gathered_plan if whole_window and two_heads and paired else windowed_plan
+    return plan(normed_input, stored_queries, stored_keys, *others)
+
+
+def windowed_plan(
     normed_input,
     stored_queries,
     stored_keys,

time: 228 us -> 75.2 us (0.33)
  waiting for transfers between devices: 96.5 us -> 38 us
  starting transfers between devices: 59.3 us -> 17.9 us
  local copies, waits for them, and re-layouts: 32.5 us -> 1.1 us
  matrix products: 16.6 us -> 0 us
  Pallas kernels: 0 us -> 16.5 us
  between operations: 14.7 us -> 0.74 us
  other arithmetic: 6.61 us -> 0.73 us
    unnamed x3 -> x0, waiting for transfers between devices: 66.2 us -> none
    ppermute x28 -> x13, starting transfers between devices: 59.2 us -> 14.2 us  [swapped(): lax.ppermute(value, axis, [(place, place ^ apart) for place in range(coun...]
    ppermute x28 -> x13, waiting for transfers between devices: 10.4 us -> 38 us  [swapped(): lax.ppermute(value, axis, [(place, place ^ apart) for place in range(coun...]
    reduce_scatter x1 -> x0, waiting for transfers between devices: 19.9 us -> none  [local(): lax.psum_scatter(input_terms, 'head', scatter_dimension=1, tiled=True)]
    dot_general x18 -> x0, matrix products: 16.6 us -> none  [the longest x2 2.91 us: per_head(): jnp.dot(grad_head, value_head.T, preferred_element_type=jnp.float32)]
    pallas_call x0 -> x5, Pallas kernels: none -> 16.5 us  [kernel_call(): pl.pallas_call(body, out_shape=outs, in_specs=[vmem if place in in_vmem e...]
    unnamed x37 -> x14, local copies, waits for them, and re-layouts: 14.1 us -> 1.1 us
    dynamic_update_slice x8 -> x0, local copies, waits for them, and re-layouts: 5.27 us -> none  [local(): lax.map(per_head, (query_stack, key_stack, value_stack, grad_stack))]
  transfers between devices with their start and end apart: 30 -> 14, of which waited for: 9 -> 6; matrix products, arithmetic and copies ran while one was open for 10% -> 1% of each run, Pallas kernels for 0% -> 15%
where the time goes in v3:
time: 75.2 us; the launch traced here: 75 us
  waiting for transfers between devices  38 us (51%)
  starting transfers between devices  17.9 us (24%)
  Pallas kernels  16.5 us (22%)
  local copies, waits for them, and re-layouts  1.1 us (1%)
    ppermute x13, waiting for transfers between devices, swapped(): lax.ppermute(value, axis, [(place, place ^ apart) for place in range(coun...  38 us
    pallas_call x5, Pallas kernels, kernel_call(): pl.pallas_call(body, out_shape=outs, in_specs=[vmem if place in in_vmem e...  16.5 us
    ppermute x13, starting transfers between devices, swapped(): lax.ppermute(value, axis, [(place, place ^ apart) for place in range(coun...  14.2 us
    all_to_all x1, starting transfers between devices, gathered_plan(): turned = lax.all_to_all(turned, 'seq', 0, 0)  3.71 us
  transfers between devices with their start and end apart: 14, of which 6 were waited for; matrix products, arithmetic and copies ran while one was open for 1% of the time, Pallas kernels for 15%

profile of v3, /device:TPU:0, one launch (start us, length us, event | category | flops | bytes accessed | tf_op | source)
XLA Modules:
  0.0 75.0 jit_solution(4181432335670394457)
XLA Ops:
  0.6 3.9 %shard_map.112 = (bf16[128,768]{1,0:T(8,128)(2,1)}, bf16[128,768]{1,0:T(8,128)(2,1)}) custom-call(bf16[128,2304]{1,0:T(8,128)(2,1)} %cot_hbm.3, bf16[512,2304]{1,0:T(8,128)(2,1)} %weight_hbm.1, bf16[128,512]{1,0:T(8,128)(2,1)} %q_hbm.1, bf16[128,256]{1,0:T(8,128)(2,1)} %k_hbm.1, bf16[128,256]{1,0:T(8,128)(2,1)} %v_hbm.1), custom_call_target="tpu_custom_call" | custom-call | flops 301989888 | bytes 2949120 | tf_op jit(solution)/shard_map/pallas_call | solution.py:266
  4.5 0.5 collective-permute-start
  5.1 2.6 %collective-permute-start.1 = (bf16[128,768]{1,0:T(8,128)(2,1)}, bf16[128,768]{1,0:T(8,128)(2,1)S(1)}, u32[]{:S(2)}, u32[]{:S(2)}) collective-permute-start(bf16[128,768]{1,0:T(8,128)(2,1)} %get-tuple-element.15.refs_0_), channel_id=1, source_target_pairs={{0,8},{4,12},{8,0},{12,4},{16,24},{20,28},{24,16},{28,20},{1,9},{5... | collective-permute-start | bytes 589832 | tf_op jit(solution)/shard_map/ppermute | solution.py:279
  7.6 1.1 %copy-done.4 = bf16[128,2304]{1,0:T(8,128)(2,1)S(1)} copy-done((bf16[128,2304]{1,0:T(8,128)(2,1)S(1)}, bf16[128,2304]{1,0:T(8,128)(2,1)}, u32[]{:S(2)}) %copy-start.4) | copy-done | bytes 589848
  8.7 1.8 %shard_map.115 = bf16[8,2,288,128]{3,2,1,0:T(8,128)(2,1)} custom-call(bf16[128,2304]{1,0:T(8,128)(2,1)S(1)} %copy-done.4, bf16[128,2304]{1,0:T(8,128)(2,1)S(1)} %copy-done.1), custom_call_target="tpu_custom_call" | custom-call | bytes 2359296 | tf_op jit(solution)/shard_map/pallas_call | solution.py:266
  10.5 3.7 %all-to-all-start = ((bf16[8,2,288,128]{3,2,1,0:T(8,128)(2,1)}), bf16[8,2,288,128]{3,2,1,0:T(8,128)(2,1)S(1)}, u32[]{:S(2)}, u32[]{:S(2)}) async-start(bf16[8,2,288,128]{3,2,1,0:T(8,128)(2,1)} %shard_map.115), calls=%async_computation | async-start | bytes 2359296 | tf_op jit(solution)/shard_map/all_to_all | solution.py:330
  14.2 1.7 %collective-permute-start.2 = (bf16[128,768]{1,0:T(8,128)(2,1)S(1)}, bf16[128,768]{1,0:T(8,128)(2,1)S(1)}, u32[]{:S(2)}, u32[]{:S(2)}) collective-permute-start(bf16[128,768]{1,0:T(8,128)(2,1)S(1)} %copy-done.6), channel_id=1, source_target_pairs={{0,12},{4,8},{8,4},{12,0},{16,28},{20,24},{24,20},{28,16},{1,13},{... | collective-permute-start | bytes 589832 | tf_op jit(solution)/shard_map/ppermute | solution.py:279
  16.0 1.5 %collective-permute-start.3 = (bf16[128,768]{1,0:T(8,128)(2,1)S(1)}, bf16[128,768]{1,0:T(8,128)(2,1)S(1)}, u32[]{:S(2)}, u32[]{:S(2)}) collective-permute-start(bf16[128,768]{1,0:T(8,128)(2,1)S(1)} %copy-done.5), channel_id=1, source_target_pairs={{0,16},{4,20},{8,24},{12,28},{16,0},{20,4},{24,8},{28,12},{1,17},{... | collective-permute-start | bytes 589832 | tf_op jit(solution)/shard_map/ppermute | solution.py:279
  17.7 1.5 %collective-permute-start.5 = (bf16[128,768]{1,0:T(8,128)(2,1)S(1)}, bf16[128,768]{1,0:T(8,128)(2,1)S(1)}, u32[]{:S(2)}, u32[]{:S(2)}) collective-permute-start(bf16[128,768]{1,0:T(8,128)(2,1)S(1)} %copy-done.5), channel_id=1, source_target_pairs={{0,24},{4,28},{8,16},{12,20},{16,8},{20,12},{24,0},{28,4},{1,25},{... | collective-permute-start | bytes 589832 | tf_op jit(solution)/shard_map/ppermute | solution.py:279
  19.2 1.2 %collective-permute-start.6 = (bf16[128,768]{1,0:T(8,128)(2,1)S(1)}, bf16[128,768]{1,0:T(8,128)(2,1)S(1)}, u32[]{:S(2)}, u32[]{:S(2)}) collective-permute-start(bf16[128,768]{1,0:T(8,128)(2,1)S(1)} %copy-done.6), channel_id=1, source_target_pairs={{0,28},{4,24},{8,20},{12,16},{16,12},{20,8},{24,4},{28,0},{1,29},{... | collective-permute-start | bytes 589832 | tf_op jit(solution)/shard_map/ppermute | solution.py:279
  20.4 13.4 %collective-permute-done.2.refs_3_ = bf16[128,768]{1,0:T(8,128)(2,1)S(1)} collective-permute-done((bf16[128,768]{1,0:T(8,128)(2,1)S(1)}, bf16[128,768]{1,0:T(8,128)(2,1)S(1)}, u32[]{:S(2)}, u32[]{:S(2)}) %collective-permute-start.2) | collective-permute-done | bytes 196640 | tf_op jit(solution)/shard_map/ppermute | solution.py:279
  33.8 0.9 %collective-permute-done.3.refs_4_ = bf16[128,768]{1,0:T(8,128)(2,1)S(1)} collective-permute-done((bf16[128,768]{1,0:T(8,128)(2,1)S(1)}, bf16[128,768]{1,0:T(8,128)(2,1)S(1)}, u32[]{:S(2)}, u32[]{:S(2)}) %collective-permute-start.3) | collective-permute-done | bytes 196640 | tf_op jit(solution)/shard_map/ppermute | solution.py:279
  34.7 11.7 %collective-permute-done.4.refs_5_ = bf16[128,768]{1,0:T(8,128)(2,1)S(1)} collective-permute-done((bf16[128,768]{1,0:T(8,128)(2,1)S(1)}, bf16[128,768]{1,0:T(8,128)(2,1)S(1)}, u32[]{:S(2)}, u32[]{:S(2)}) %collective-permute-start.4) | collective-permute-done | bytes 196640 | tf_op jit(solution)/shard_map/ppermute | solution.py:279
  46.4 7.7 %shard_map.113 = (bf16[128,512]{1,0:T(8,128)(2,1)S(1)}, bf16[128,512]{1,0:T(8,128)(2,1)S(1)}, bf16[256,1024]{1,0:T(8,128)(2,1)S(1)}, bf16[1024,128]{1,0:T(8,128)(2,1)S(1)}) custom-call(bf16[128,768]{1,0:T(8,128)(2,1)S(1)} %copy-done.5, bf16[128,768]{1,0:T(8,128)(2,1)S(1)} %collective-permute-done.refs_1_, ...), custom_call_target="tpu_custom_call" | custom-call | flops 2147483648 | bytes 1572864 | tf_op jit(solution)/shard_map/pallas_call | solution.py:266
  54.1 0.4 collective-permute-start.7
  54.6 0.8 %collective-permute-done.7.far_ref = bf16[128,512]{1,0:T(8,128)(2,1)S(1)} collective-permute-done((bf16[128,512]{1,0:T(8,128)(2,1)S(1)}, bf16[128,512]{1,0:T(8,128)(2,1)S(1)}, u32[]{:S(2)}, u32[]{:S(2)}) %collective-permute-start.7) | collective-permute-done | bytes 131104 | tf_op jit(solution)/shard_map/ppermute | solution.py:279
  55.5 1.4 %shard_map.114 = (bf16[576,128]{1,0:T(8,128)(2,1)S(1)}, bf16[576,128]{1,0:T(8,128)(2,1)S(1)}, bf16[576,128]{1,0:T(8,128)(2,1)S(1)}, f32[576,128]{1,0:T(8,128)S(1)}) custom-call(bf16[128,512]{1,0:T(8,128)(2,1)S(1)} %get-tuple-element.17.own_ref, bf16[128,512]{1,0:T(8,128)(2,1)S(1)} %collective-permute-done.7.far_ref, bf16[2304,512]{1,0:T(8,128)(2,1)S(1)} %copy-done, ...), custom_call_target="tpu_custom_call" | custom-call | flops 603979776 | bytes 4718592 | tf_op jit(solution)/shard_map/pallas_call | solution.py:266
  56.9 1.6 %collective-permute-start.10 = (bf16[576,128]{1,0:T(8,128)(2,1)S(1)}, bf16[576,128]{1,0:T(8,128)(2,1)S(1)}, u32[]{:S(2)}, u32[]{:S(2)}) collective-permute-start(bf16[576,128]{1,0:T(8,128)(2,1)S(1)} %get-tuple-element.22), channel_id=1, source_target_pairs={{0,1},{1,0},{2,3},{3,2},{4,5},{5,4},{6,7},{7,6},{8,9},{9,8},{10,11... | collective-permute-start | bytes 442376 | tf_op jit(solution)/shard_map/ppermute | solution.py:279
  58.6 2.6 %collective-permute-start.9 = (bf16[576,128]{1,0:T(8,128)(2,1)S(1)}, bf16[576,128]{1,0:T(8,128)(2,1)S(1)}, u32[]{:S(2)}, u32[]{:S(2)}) collective-permute-start(bf16[576,128]{1,0:T(8,128)(2,1)S(1)} %get-tuple-element.21), channel_id=1, source_target_pairs={{0,2},{1,3},{2,0},{3,1},{4,6},{5,7},{6,4},{7,5},{8,10},{9,11},{10,... | collective-permute-start | bytes 442376 | tf_op jit(solution)/shard_map/ppermute | solution.py:279
  61.2 0.2 collective-permute-start.8
  61.4 4.2 %collective-permute-done.10 = bf16[576,128]{1,0:T(8,128)(2,1)S(1)} collective-permute-done((bf16[576,128]{1,0:T(8,128)(2,1)S(1)}, bf16[576,128]{1,0:T(8,128)(2,1)S(1)}, u32[]{:S(2)}, u32[]{:S(2)}) %collective-permute-start.10) | collective-permute-done | bytes 147488 | tf_op jit(solution)/shard_map/ppermute | solution.py:279
  65.6 7.0 %collective-permute-done.9 = bf16[576,128]{1,0:T(8,128)(2,1)S(1)} collective-permute-done((bf16[576,128]{1,0:T(8,128)(2,1)S(1)}, bf16[576,128]{1,0:T(8,128)(2,1)S(1)}, u32[]{:S(2)}, u32[]{:S(2)}) %collective-permute-start.9) | collective-permute-done | bytes 147488 | tf_op jit(solution)/shard_map/ppermute | solution.py:279
  72.6 0.7 fusion
  73.3 1.7 %shard_map.116 = (f32[288,256]{1,0:T(8,128)}, f32[288,512]{1,0:T(8,128)}) custom-call(bf16[8,2,288,128]{3,2,1,0:T(8,128)(2,1)S(1)} %all-to-all-done.turned_ref, bf16[256,1024]{1,0:T(8,128)(2,1)S(1)} %get-tuple-element.23.attn_ref, bf16[256,1024]{1,0:T(8,128)(2,1)S(1)} %collective-permute-done.11.far_attn_ref, ...), custom_call_target="tpu_custom_call" | custom-call | flops 452984832 | bytes 2064384 | tf_op jit(solution)/shard_map/pallas_call | solution.py:266
  (24 shorter events, 0.5 us)
Async XLA Ops:
  0.6 7.0 %copy-start.1 = (bf16[128,2304]{1,0:T(8,128)(2,1)S(1)}, bf16[128,2304]{1,0:T(8,128)(2,1)}, u32[]{:S(2)}) copy-start(bf16[128,2304]{1,0:T(8,128)(2,1)} %cot_hbm.3) | copy-start | bytes 1769476
  4.5 13.1 %collective-permute-start = (bf16[128,768]{1,0:T(8,128)(2,1)}, bf16[128,768]{1,0:T(8,128)(2,1)S(1)}, u32[]{:S(2)}, u32[]{:S(2)}) collective-permute-start(bf16[128,768]{1,0:T(8,128)(2,1)} %get-tuple-element.16), channel_id=1, source_target_pairs={{0,4},{4,0},{8,12},{12,8},{16,20},{20,16},{24,28},{28,24},{1,5},{5... | collective-permute-start | bytes 589832 | tf_op jit(solution)/shard_map/ppermute | solution.py:279
  5.1 14.1 %collective-permute-start.1 = (bf16[128,768]{1,0:T(8,128)(2,1)}, bf16[128,768]{1,0:T(8,128)(2,1)S(1)}, u32[]{:S(2)}, u32[]{:S(2)}) collective-permute-start(bf16[128,768]{1,0:T(8,128)(2,1)} %get-tuple-element.15.refs_0_), channel_id=1, source_target_pairs={{0,8},{4,12},{8,0},{12,4},{16,24},{20,28},{24,16},{28,20},{1,9},{5... | collective-permute-start | bytes 589832 | tf_op jit(solution)/shard_map/ppermute | solution.py:279
  7.6 1.1 %copy-start.4 = (bf16[128,2304]{1,0:T(8,128)(2,1)S(1)}, bf16[128,2304]{1,0:T(8,128)(2,1)}, u32[]{:S(2)}) copy-start(bf16[128,2304]{1,0:T(8,128)(2,1)} %normed_hbm.1) | copy-start | bytes 1769476
  10.5 3.7 %copy-start.6 = (bf16[128,768]{1,0:T(8,128)(2,1)S(1)}, bf16[128,768]{1,0:T(8,128)(2,1)}, u32[]{:S(2)}) copy-start(bf16[128,768]{1,0:T(8,128)(2,1)} %get-tuple-element.16) | copy-start | bytes 589828
  10.5 5.5 %copy-start.5 = (bf16[128,768]{1,0:T(8,128)(2,1)S(1)}, bf16[128,768]{1,0:T(8,128)(2,1)}, u32[]{:S(2)}) copy-start(bf16[128,768]{1,0:T(8,128)(2,1)} %get-tuple-element.15.refs_0_) | copy-start | bytes 589828
  10.5 62.8 %all-to-all-start = ((bf16[8,2,288,128]{3,2,1,0:T(8,128)(2,1)}), bf16[8,2,288,128]{3,2,1,0:T(8,128)(2,1)S(1)}, u32[]{:S(2)}, u32[]{:S(2)}) async-start(bf16[8,2,288,128]{3,2,1,0:T(8,128)(2,1)} %shard_map.115), calls=%async_computation | async-start | bytes 2359296 | tf_op jit(solution)/shard_map/all_to_all | solution.py:330
  14.2 41.3 %copy-start.2 = (bf16[2304,256]{1,0:T(8,128)(2,1)S(1)}, bf16[2304,256]{1,0:T(8,128)(2,1)}, u32[]{:S(2)}) copy-start(bf16[2304,256]{1,0:T(8,128)(2,1)} %wk_ref.1) | copy-start | bytes 3538948
  14.2 41.3 %copy-start.3 = (bf16[2304,256]{1,0:T(8,128)(2,1)S(1)}, bf16[2304,256]{1,0:T(8,128)(2,1)}, u32[]{:S(2)}) copy-start(bf16[2304,256]{1,0:T(8,128)(2,1)} %wv_ref.1) | copy-start | bytes 3538948
  14.2 19.6 %collective-permute-start.2 = (bf16[128,768]{1,0:T(8,128)(2,1)S(1)}, bf16[128,768]{1,0:T(8,128)(2,1)S(1)}, u32[]{:S(2)}, u32[]{:S(2)}) collective-permute-start(bf16[128,768]{1,0:T(8,128)(2,1)S(1)} %copy-done.6), channel_id=1, source_target_pairs={{0,12},{4,8},{8,4},{12,0},{16,28},{20,24},{24,20},{28,16},{1,13},{... | collective-permute-start | bytes 589832 | tf_op jit(solution)/shard_map/ppermute | solution.py:279
  16.0 18.7 %collective-permute-start.3 = (bf16[128,768]{1,0:T(8,128)(2,1)S(1)}, bf16[128,768]{1,0:T(8,128)(2,1)S(1)}, u32[]{:S(2)}, u32[]{:S(2)}) collective-permute-start(bf16[128,768]{1,0:T(8,128)(2,1)S(1)} %copy-done.5), channel_id=1, source_target_pairs={{0,16},{4,20},{8,24},{12,28},{16,0},{20,4},{24,8},{28,12},{1,17},{... | collective-permute-start | bytes 589832 | tf_op jit(solution)/shard_map/ppermute | solution.py:279
  17.5 28.9 %collective-permute-start.4 = (bf16[128,768]{1,0:T(8,128)(2,1)S(1)}, bf16[128,768]{1,0:T(8,128)(2,1)S(1)}, u32[]{:S(2)}, u32[]{:S(2)}) collective-permute-start(bf16[128,768]{1,0:T(8,128)(2,1)S(1)} %copy-done.6), channel_id=1, source_target_pairs={{0,20},{4,16},{8,28},{12,24},{16,4},{20,0},{24,12},{28,8},{1,21},{... | collective-permute-start | bytes 589832 | tf_op jit(solution)/shard_map/ppermute | solution.py:279
  17.7 28.7 %collective-permute-start.5 = (bf16[128,768]{1,0:T(8,128)(2,1)S(1)}, bf16[128,768]{1,0:T(8,128)(2,1)S(1)}, u32[]{:S(2)}, u32[]{:S(2)}) collective-permute-start(bf16[128,768]{1,0:T(8,128)(2,1)S(1)} %copy-done.5), channel_id=1, source_target_pairs={{0,24},{4,28},{8,16},{12,20},{16,8},{20,12},{24,0},{28,4},{1,25},{... | collective-permute-start | bytes 589832 | tf_op jit(solution)/shard_map/ppermute | solution.py:279
  19.2 27.2 %collective-permute-start.6 = (bf16[128,768]{1,0:T(8,128)(2,1)S(1)}, bf16[128,768]{1,0:T(8,128)(2,1)S(1)}, u32[]{:S(2)}, u32[]{:S(2)}) collective-permute-start(bf16[128,768]{1,0:T(8,128)(2,1)S(1)} %copy-done.6), channel_id=1, source_target_pairs={{0,28},{4,24},{8,20},{12,16},{16,12},{20,8},{24,4},{28,0},{1,29},{... | collective-permute-start | bytes 589832 | tf_op jit(solution)/shard_map/ppermute | solution.py:279
  46.4 9.1 %copy-start = (bf16[2304,512]{1,0:T(8,128)(2,1)S(1)}, bf16[2304,512]{1,0:T(8,128)(2,1)}, u32[]{:S(2)}) copy-start(bf16[2304,512]{1,0:T(8,128)(2,1)} %wq_ref.1) | copy-start | bytes 7077892
  54.1 1.4 %collective-permute-start.7 = (bf16[128,512]{1,0:T(8,128)(2,1)S(1)}, bf16[128,512]{1,0:T(8,128)(2,1)S(1)}, u32[]{:S(2)}, u32[]{:S(2)}) collective-permute-start(bf16[128,512]{1,0:T(8,128)(2,1)S(1)} %get-tuple-element.18), channel_id=1, source_target_pairs={{0,4},{4,0},{8,12},{12,8},{16,20},{20,16},{24,28},{28,24},{1,5},{5... | collective-permute-start | bytes 393224 | tf_op jit(solution)/shard_map/ppermute | solution.py:279
  54.4 18.9 %collective-permute-start.11 = (bf16[256,1024]{1,0:T(8,128)(2,1)S(1)}, bf16[256,1024]{1,0:T(8,128)(2,1)S(1)}, u32[]{:S(2)}, u32[]{:S(2)}) collective-permute-start(bf16[256,1024]{1,0:T(8,128)(2,1)S(1)} %get-tuple-element.23.attn_ref), channel_id=1, source_target_pairs={{0,4},{4,0},{8,12},{12,8},{16,20},{20,16},{24,28},{28,24},{1,5},{5... | collective-permute-start | bytes 1572872 | tf_op jit(solution)/shard_map/ppermute | solution.py:279
  56.9 8.7 %collective-permute-start.10 = (bf16[576,128]{1,0:T(8,128)(2,1)S(1)}, bf16[576,128]{1,0:T(8,128)(2,1)S(1)}, u32[]{:S(2)}, u32[]{:S(2)}) collective-permute-start(bf16[576,128]{1,0:T(8,128)(2,1)S(1)} %get-tuple-element.22), channel_id=1, source_target_pairs={{0,1},{1,0},{2,3},{3,2},{4,5},{5,4},{6,7},{7,6},{8,9},{9,8},{10,11... | collective-permute-start | bytes 442376 | tf_op jit(solution)/shard_map/ppermute | solution.py:279
  58.6 14.0 %collective-permute-start.9 = (bf16[576,128]{1,0:T(8,128)(2,1)S(1)}, bf16[576,128]{1,0:T(8,128)(2,1)S(1)}, u32[]{:S(2)}, u32[]{:S(2)}) collective-permute-start(bf16[576,128]{1,0:T(8,128)(2,1)S(1)} %get-tuple-element.21), channel_id=1, source_target_pairs={{0,2},{1,3},{2,0},{3,1},{4,6},{5,7},{6,4},{7,5},{8,10},{9,11},{10,... | collective-permute-start | bytes 442376 | tf_op jit(solution)/shard_map/ppermute | solution.py:279
  61.2 11.4 %collective-permute-start.8 = (bf16[576,128]{1,0:T(8,128)(2,1)S(1)}, bf16[576,128]{1,0:T(8,128)(2,1)S(1)}, u32[]{:S(2)}, u32[]{:S(2)}) collective-permute-start(bf16[576,128]{1,0:T(8,128)(2,1)S(1)} %get-tuple-element.20), channel_id=1, source_target_pairs={{0,3},{1,2},{2,1},{3,0},{4,7},{5,6},{6,5},{7,4},{8,11},{9,10},{10,... | collective-permute-start | bytes 442376 | tf_op jit(solution)/shard_map/ppermute | solution.py:279
  61.4 11.9 %collective-permute-start.12 = (bf16[1024,128]{1,0:T(8,128)(2,1)S(1)}, bf16[1024,128]{1,0:T(8,128)(2,1)S(1)}, u32[]{:S(2)}, u32[]{:S(2)}) collective-permute-start(bf16[1024,128]{1,0:T(8,128)(2,1)S(1)} %get-tuple-element.24.dv_ref), channel_id=1, source_target_pairs={{0,4},{4,0},{8,12},{12,8},{16,20},{20,16},{24,28},{28,24},{1,5},{5... | collective-permute-start | bytes 786440 | tf_op jit(solution)/shard_map/ppermute | solution.py:279

commit v4 on v3

--- a/solution.py
+++ b/solution.py
@@ -71,15 +71,18 @@
     cot_copy.wait()
     for place, (target, _) in enumerate(halves):
         weight_copies[place].wait()
-        target[:, first:] = dot_nt(
-            cot_ref[...], weight_ref[place * cut : (place + 1) * cut]
-        ).astype(jnp.bfloat16)
+        grads_t = dot_nt(weight_ref[place * cut : (place + 1) * cut], cot_ref[...])
+        for h in range(cut // HEAD_SIZE):
+            target[:, first + h * HEAD_SIZE : first + (h + 1) * HEAD_SIZE] = grads_t[
+                h * HEAD_SIZE : (h + 1) * HEAD_SIZE
+            ].astype(jnp.bfloat16)
     for copy in plain_copies:
         copy.wait()
 
 
-def turn_kernel(parts, normed_hbm, cot_hbm, turned_ref, normed_ref, cot_ref, sem):
+def turn_kernel(parts, normed_hbm, cot_hbm, _, __, turned_ref, done_ref, normed_ref, cot_ref, sem):
     cut = normed_ref.shape[1] // parts
+    done_ref[...] = jnp.zeros_like(done_ref)
     copies = []
     for which, (source, target) in enumerate(((normed_hbm, normed_ref), (cot_hbm, cot_ref))):
         copies.append(pltpu.make_async_copy(source, target, sem.at[which]))
@@ -92,7 +95,7 @@
 
 
 def attention_kernel(blocks, *refs):
-    attention_body(refs[:blocks], *refs[blocks:])
+    attention_body(refs[:blocks], *refs[blocks + 1 :])
 
 
 def attention_body(
@@ -174,9 +177,11 @@
         grads_t = jnp.concatenate(
             [
                 gathered_ref[
-                    own, grad_base + h * HEAD_SIZE : grad_base + (h + 1) * HEAD_SIZE
-                ].T
+                    block * rows : (block + 1) * rows,
+                    grad_base + h * HEAD_SIZE : grad_base + (h + 1) * HEAD_SIZE,
+                ]
                 for h in range(heads)
+                for block in (2 * step, 2 * step + 1)
             ],
             axis=1,
         )
@@ -248,8 +253,9 @@
 
 
 def weight_grad_kernel(
-    turned_ref, attn_ref, far_attn_ref, dv_ref, far_dv_ref, wvalue_ref, woutput_ref, joined_ref
+    turned_ref, attn_ref, far_attn_ref, dv_ref, far_dv_ref, wvalue_ref, woutput_ref, done_ref, joined_ref
 ):
+    done_ref[...] = jnp.zeros_like(done_ref)
     core = lax.axis_index("seq") % 2
     parts = turned_ref.shape[0]
     rows = turned_ref.shape[3]
@@ -258,6 +264,13 @@
     for half, attn, dv in ((core, attn_ref, dv_ref), (1 - core, far_attn_ref, far_dv_ref)):
         wvalue_ref[:, at(half, dv.shape[1])] = dot_nn(joined_ref[0], dv[...])
         woutput_ref[:, at(half, attn.shape[0])] = dot_nt(joined_ref[1], attn[...])
+
+
+def sum_kernel(_, own_ref, *refs):
+    total = own_ref[...]
+    for arrived_ref in refs[:-1]:
+        total = total + arrived_ref[...].astype(jnp.float32)
+    refs[-1][...] = total.astype(jnp.bfloat16)
 
 
 def kernel_call(body, outs, operands, in_vmem=(), scratch=(), flops=0, moved=0, room=32):
@@ -313,13 +326,13 @@
         moved=2 * model * (rows + 2 * q_cols),
         room=63,
     )
-    held = [same] + [
-        swapped(other if apart % 2 else same, "seq", apart) for apart in range(1, blocks)
-    ]
-    turned = kernel_call(
+    held = {0: same}
+    for apart in range(blocks - 1, 0, -1):
+        held[apart] = swapped(other if apart % 2 else same, "seq", apart)
+    turned, turn_done = kernel_call(
         functools.partial(turn_kernel, blocks),
-        shape((blocks, 2, model // blocks, rows), bf16),
-        (normed_input, out_cotangent),
+        (shape((blocks, 2, model // blocks, rows), bf16), shape((8, HEAD_SIZE), f32)),
+        (normed_input, out_cotangent, held[1], held[2]),
         scratch=(
             pltpu.VMEM(normed_input.shape, bf16),
             pltpu.VMEM(out_cotangent.shape, bf16),
@@ -336,7 +349,7 @@
             shape((q_cols, tokens), bf16),
             shape((tokens, kv_cols), bf16),
         ),
-        held,
+        [held[apart] for apart in range(blocks)] + [turn_done],
         scratch=(
             pltpu.VMEM((tokens, packed_cols), bf16),
             pltpu.VMEM((tokens, wide), f32),
@@ -365,14 +378,13 @@
         flops=4 * rows * model * (q_cols + 2 * kv_cols),
         moved=4 * model * (q_cols + 2 * kv_cols),
     )
-    grad_input = terms[-1]
-    for apart, term in zip(aparts[:-1], terms[:-1]):
-        grad_input = grad_input + swapped(term, "head", apart).astype(f32)
-    grad_wvalue, grad_woutput = kernel_call(
+    arrived = [swapped(term, "head", apart) for apart, term in zip(aparts[:-1], terms[:-1])]
+    grad_wvalue, grad_woutput, weights_done = kernel_call(
         weight_grad_kernel,
         (
             shape((model // blocks, 2 * kv_cols), f32),
             shape((model // blocks, 2 * q_cols), f32),
+            shape((8, HEAD_SIZE), f32),
         ),
         (turned, attn, swapped(attn, "seq", 1), dv, swapped(dv, "seq", 1)),
         in_vmem=range(5),
@@ -380,7 +392,14 @@
         flops=4 * tokens * (model // blocks) * (q_cols + kv_cols),
         moved=4 * (model // blocks) * (tokens + 2 * q_cols + 2 * kv_cols),
     )
-    return (grad_input.astype(bf16).T, grad_wvalue, grad_woutput.T)
+    grad_input = kernel_call(
+        sum_kernel,
+        shape((model // groups, rows), bf16),
+        (weights_done, terms[-1], *arrived),
+        in_vmem=range(1, groups + 1),
+        moved=4 * groups * (model // groups) * rows,
+    )
+    return (grad_input.T, grad_wvalue, grad_woutput.T)
 
 
 def power_of_two(count):

time: 75.2 us -> 82.2 us (1.093)
  waiting for transfers between devices: 38 us -> 43.7 us
  Pallas kernels: 16.5 us -> 17.7 us
    ppermute x13, waiting for transfers between devices: 38 us -> 43.7 us  [swapped(): lax.ppermute(value, axis, [(place, place ^ apart) for place in range(coun...]
    pallas_call x5 -> x6, Pallas kernels: 16.5 us -> 17.7 us  [kernel_call(): pl.pallas_call(body, out_shape=outs, in_specs=[vmem if place in in_vmem e...]
  transfers between devices with their start and end apart: 14 -> 14, of which waited for: 6 -> 7; matrix products, arithmetic and copies ran while one was open for 1% -> 0% of each run, Pallas kernels for 15% -> 14%
where the time goes in v4:
time: 82.2 us; the launch traced here: 81.9 us
  waiting for transfers between devices  43.7 us (53%)
  starting transfers between devices  18.7 us (23%)
  Pallas kernels  17.7 us (22%)
  local copies, waits for them, and re-layouts  1.1 us (1%)
    ppermute x13, waiting for transfers between devices, swapped(): lax.ppermute(value, axis, [(place, place ^ apart) for place in range(coun...  43.7 us
    pallas_call x6, Pallas kernels, kernel_call(): pl.pallas_call(body, out_shape=outs, in_specs=[vmem if place in in_vmem e...  17.7 us
    ppermute x13, starting transfers between devices, swapped(): lax.ppermute(value, axis, [(place, place ^ apart) for place in range(coun...  14.5 us
    all_to_all x1, starting transfers between devices, gathered_plan(): turned = lax.all_to_all(turned, 'seq', 0, 0)  4.13 us
  transfers between devices with their start and end apart: 14, of which 7 were waited for; matrix products, arithmetic and copies ran while one was open for 0% of the time, Pallas kernels for 14%

profile of v4, /device:TPU:0, one launch (start us, length us, event | category | flops | bytes accessed | tf_op | source)
XLA Modules:
  0.0 81.9 jit_solution(8671746385400076655)
XLA Ops:
  0.6 3.8 %shard_map.112 = (bf16[128,768]{1,0:T(8,128)(2,1)}, bf16[128,768]{1,0:T(8,128)(2,1)}) custom-call(bf16[128,2304]{1,0:T(8,128)(2,1)} %cot_hbm.3, bf16[512,2304]{1,0:T(8,128)(2,1)} %weight_hbm.1, bf16[128,512]{1,0:T(8,128)(2,1)} %q_hbm.1, bf16[128,256]{1,0:T(8,128)(2,1)} %k_hbm.1, bf16[128,256]{1,0:T(8,128)(2,1)} %v_hbm.1), custom_call_target="tpu_custom_call" | custom-call | flops 301989888 | bytes 2949120 | tf_op jit(solution)/shard_map/pallas_call | solution.py:279
  4.5 0.5 collective-permute-start
  5.0 2.6 %collective-permute-start.1 = (bf16[128,768]{1,0:T(8,128)(2,1)}, bf16[128,768]{1,0:T(8,128)(2,1)S(1)}, u32[]{:S(2)}, u32[]{:S(2)}) collective-permute-start(bf16[128,768]{1,0:T(8,128)(2,1)} %get-tuple-element.19.refs_0_), channel_id=1, source_target_pairs={{0,8},{4,12},{8,0},{12,4},{16,24},{20,28},{24,16},{28,20},{1,9},{5... | collective-permute-start | bytes 589832 | tf_op jit(solution)/shard_map/ppermute | solution.py:292
  7.6 5.7 %collective-permute-done.1.__.refs_2_ = bf16[128,768]{1,0:T(8,128)(2,1)S(1)} collective-permute-done((bf16[128,768]{1,0:T(8,128)(2,1)}, bf16[128,768]{1,0:T(8,128)(2,1)S(1)}, u32[]{:S(2)}, u32[]{:S(2)}) %collective-permute-start.1) | collective-permute-done | bytes 196640 | tf_op jit(solution)/shard_map/ppermute | solution.py:292
  13.3 1.1 %copy-done.4 = bf16[128,2304]{1,0:T(8,128)(2,1)S(1)} copy-done((bf16[128,2304]{1,0:T(8,128)(2,1)S(1)}, bf16[128,2304]{1,0:T(8,128)(2,1)}, u32[]{:S(2)}) %copy-start.4) | copy-done | bytes 589848
  14.4 1.8 %shard_map.113 = (bf16[8,2,288,128]{3,2,1,0:T(8,128)(2,1)}, f32[8,128]{1,0:T(8,128)S(1)}) custom-call(bf16[128,2304]{1,0:T(8,128)(2,1)S(1)} %copy-done.4, bf16[128,2304]{1,0:T(8,128)(2,1)S(1)} %copy-done.1, bf16[128,768]{1,0:T(8,128)(2,1)S(1)} %collective-permute-done._.refs_1_, bf16[128,768]{1,0:T(8,128)(2,1)S(1)} %collective-permute-done.1.__.refs_2_), custom_call_target="tpu_custom_call" | custom-call | bytes 2359296 | tf_op jit(solution)/shard_map/pallas_call | solution.py:279
  16.2 4.1 %all-to-all-start = ((bf16[8,2,288,128]{3,2,1,0:T(8,128)(2,1)}), bf16[8,2,288,128]{3,2,1,0:T(8,128)(2,1)S(1)}, u32[]{:S(2)}, u32[]{:S(2)}) async-start(bf16[8,2,288,128]{3,2,1,0:T(8,128)(2,1)} %get-tuple-element.20), calls=%async_computation | async-start | bytes 2359296 | tf_op jit(solution)/shard_map/all_to_all | solution.py:343
  20.3 1.8 %collective-permute-start.2 = (bf16[128,768]{1,0:T(8,128)(2,1)S(1)}, bf16[128,768]{1,0:T(8,128)(2,1)S(1)}, u32[]{:S(2)}, u32[]{:S(2)}) collective-permute-start(bf16[128,768]{1,0:T(8,128)(2,1)S(1)} %copy-done.6), channel_id=1, source_target_pairs={{0,12},{4,8},{8,4},{12,0},{16,28},{20,24},{24,20},{28,16},{1,13},{... | collective-permute-start | bytes 589832 | tf_op jit(solution)/shard_map/ppermute | solution.py:292
  22.1 1.5 %collective-permute-start.3 = (bf16[128,768]{1,0:T(8,128)(2,1)S(1)}, bf16[128,768]{1,0:T(8,128)(2,1)S(1)}, u32[]{:S(2)}, u32[]{:S(2)}) collective-permute-start(bf16[128,768]{1,0:T(8,128)(2,1)S(1)} %copy-done.5), channel_id=1, source_target_pairs={{0,16},{4,20},{8,24},{12,28},{16,0},{20,4},{24,8},{28,12},{1,17},{... | collective-permute-start | bytes 589832 | tf_op jit(solution)/shard_map/ppermute | solution.py:292
  23.8 1.5 %collective-permute-start.5 = (bf16[128,768]{1,0:T(8,128)(2,1)S(1)}, bf16[128,768]{1,0:T(8,128)(2,1)S(1)}, u32[]{:S(2)}, u32[]{:S(2)}) collective-permute-start(bf16[128,768]{1,0:T(8,128)(2,1)S(1)} %copy-done.5), channel_id=1, source_target_pairs={{0,24},{4,28},{8,16},{12,20},{16,8},{20,12},{24,0},{28,4},{1,25},{... | collective-permute-start | bytes 589832 | tf_op jit(solution)/shard_map/ppermute | solution.py:292
  25.3 1.2 %collective-permute-start.6 = (bf16[128,768]{1,0:T(8,128)(2,1)S(1)}, bf16[128,768]{1,0:T(8,128)(2,1)S(1)}, u32[]{:S(2)}, u32[]{:S(2)}) collective-permute-start(bf16[128,768]{1,0:T(8,128)(2,1)S(1)} %copy-done.6), channel_id=1, source_target_pairs={{0,28},{4,24},{8,20},{12,16},{16,12},{20,8},{24,4},{28,0},{1,29},{... | collective-permute-start | bytes 589832 | tf_op jit(solution)/shard_map/ppermute | solution.py:292
  26.5 13.5 %collective-permute-done.2.refs_3_ = bf16[128,768]{1,0:T(8,128)(2,1)S(1)} collective-permute-done((bf16[128,768]{1,0:T(8,128)(2,1)S(1)}, bf16[128,768]{1,0:T(8,128)(2,1)S(1)}, u32[]{:S(2)}, u32[]{:S(2)}) %collective-permute-start.2) | collective-permute-done | bytes 196640 | tf_op jit(solution)/shard_map/ppermute | solution.py:292
  40.0 0.9 %collective-permute-done.3.refs_4_ = bf16[128,768]{1,0:T(8,128)(2,1)S(1)} collective-permute-done((bf16[128,768]{1,0:T(8,128)(2,1)S(1)}, bf16[128,768]{1,0:T(8,128)(2,1)S(1)}, u32[]{:S(2)}, u32[]{:S(2)}) %collective-permute-start.3) | collective-permute-done | bytes 196640 | tf_op jit(solution)/shard_map/ppermute | solution.py:292
  40.9 11.7 %collective-permute-done.4.refs_5_ = bf16[128,768]{1,0:T(8,128)(2,1)S(1)} collective-permute-done((bf16[128,768]{1,0:T(8,128)(2,1)S(1)}, bf16[128,768]{1,0:T(8,128)(2,1)S(1)}, u32[]{:S(2)}, u32[]{:S(2)}) %collective-permute-start.4) | collective-permute-done | bytes 196640 | tf_op jit(solution)/shard_map/ppermute | solution.py:292
  52.6 7.6 %shard_map.114 = (bf16[128,512]{1,0:T(8,128)(2,1)S(1)}, bf16[128,512]{1,0:T(8,128)(2,1)S(1)}, bf16[256,1024]{1,0:T(8,128)(2,1)S(1)}, bf16[1024,128]{1,0:T(8,128)(2,1)S(1)}) custom-call(bf16[128,768]{1,0:T(8,128)(2,1)S(1)} %copy-done.5, bf16[128,768]{1,0:T(8,128)(2,1)S(1)} %collective-permute-done._.refs_1_, ...), custom_call_target="tpu_custom_call" | custom-call | flops 2147483648 | bytes 1572864 | tf_op jit(solution)/shard_map/pallas_call | solution.py:279
  60.2 0.4 collective-permute-start.7
  61.0 1.3 %collective-permute-done.9.far_ref = bf16[128,512]{1,0:T(8,128)(2,1)S(1)} collective-permute-done((bf16[128,512]{1,0:T(8,128)(2,1)S(1)}, bf16[128,512]{1,0:T(8,128)(2,1)S(1)}, u32[]{:S(2)}, u32[]{:S(2)}) %collective-permute-start.9) | collective-permute-done | bytes 131104 | tf_op jit(solution)/shard_map/ppermute | solution.py:292
  62.3 2.1 %shard_map.116 = (bf16[576,128]{1,0:T(8,128)(2,1)}, bf16[576,128]{1,0:T(8,128)(2,1)}, bf16[576,128]{1,0:T(8,128)(2,1)}, f32[576,128]{1,0:T(8,128)S(1)}) custom-call(bf16[128,512]{1,0:T(8,128)(2,1)S(1)} %get-tuple-element.25.own_ref, bf16[128,512]{1,0:T(8,128)(2,1)S(1)} %collective-permute-done.9.far_ref, bf16[2304,512]{1,0:T(8,128)(2,1)S(1)} %copy-done, ...), custom_call_target="tpu_custom_call" | custom-call | flops 603979776 | bytes 4718592 | tf_op jit(solution)/shard_map/pallas_call | solution.py:279
  64.4 3.6 %collective-permute-start.10 = (bf16[576,128]{1,0:T(8,128)(2,1)}, bf16[576,128]{1,0:T(8,128)(2,1)S(1)}, u32[]{:S(2)}, u32[]{:S(2)}) collective-permute-start(bf16[576,128]{1,0:T(8,128)(2,1)} %get-tuple-element.28), channel_id=1, source_target_pairs={{0,3},{1,2},{2,1},{3,0},{4,7},{5,6},{6,5},{7,4},{8,11},{9,10},{10,... | collective-permute-start | bytes 442376 | tf_op jit(solution)/shard_map/ppermute | solution.py:292
  68.1 0.8 collective-permute-start.12
  68.8 1.7 %shard_map.115 = (f32[288,256]{1,0:T(8,128)}, f32[288,512]{1,0:T(8,128)}, f32[8,128]{1,0:T(8,128)S(1)}) custom-call(bf16[8,2,288,128]{3,2,1,0:T(8,128)(2,1)S(1)} %all-to-all-done.turned_ref, bf16[256,1024]{1,0:T(8,128)(2,1)S(1)} %get-tuple-element.22.attn_ref, bf16[256,1024]{1,0:T(8,128)(2,1)S(1)} %collective-permute-done.7.far_attn_ref, ...), custom_call_target="tpu_custom_call" | custom-call | flops 452984832 | bytes 2064384 | tf_op jit(solution)/shard_map/pallas_call | solution.py:279
  70.5 2.7 %collective-permute-done.10.refs_0_ = bf16[576,128]{1,0:T(8,128)(2,1)S(1)} collective-permute-done((bf16[576,128]{1,0:T(8,128)(2,1)}, bf16[576,128]{1,0:T(8,128)(2,1)S(1)}, u32[]{:S(2)}, u32[]{:S(2)}) %collective-permute-start.10) | collective-permute-done | bytes 147488 | tf_op jit(solution)/shard_map/ppermute | solution.py:292
  73.2 8.0 %collective-permute-done.11.refs_1_ = bf16[576,128]{1,0:T(8,128)(2,1)S(1)} collective-permute-done((bf16[576,128]{1,0:T(8,128)(2,1)}, bf16[576,128]{1,0:T(8,128)(2,1)S(1)}, u32[]{:S(2)}, u32[]{:S(2)}) %collective-permute-start.11) | collective-permute-done | bytes 147488 | tf_op jit(solution)/shard_map/ppermute | solution.py:292
  81.2 0.7 shard_map.117
  (24 shorter events, 0.8 us)
Async XLA Ops:
  0.6 12.7 %copy-start.1 = (bf16[128,2304]{1,0:T(8,128)(2,1)S(1)}, bf16[128,2304]{1,0:T(8,128)(2,1)}, u32[]{:S(2)}) copy-start(bf16[128,2304]{1,0:T(8,128)(2,1)} %cot_hbm.3) | copy-start | bytes 1769476
  4.5 3.1 %collective-permute-start = (bf16[128,768]{1,0:T(8,128)(2,1)}, bf16[128,768]{1,0:T(8,128)(2,1)S(1)}, u32[]{:S(2)}, u32[]{:S(2)}) collective-permute-start(bf16[128,768]{1,0:T(8,128)(2,1)} %get-tuple-element.18), channel_id=1, source_target_pairs={{0,4},{4,0},{8,12},{12,8},{16,20},{20,16},{24,28},{28,24},{1,5},{5... | collective-permute-start | bytes 589832 | tf_op jit(solution)/shard_map/ppermute | solution.py:292
  5.0 8.3 %collective-permute-start.1 = (bf16[128,768]{1,0:T(8,128)(2,1)}, bf16[128,768]{1,0:T(8,128)(2,1)S(1)}, u32[]{:S(2)}, u32[]{:S(2)}) collective-permute-start(bf16[128,768]{1,0:T(8,128)(2,1)} %get-tuple-element.19.refs_0_), channel_id=1, source_target_pairs={{0,8},{4,12},{8,0},{12,4},{16,24},{20,28},{24,16},{28,20},{1,9},{5... | collective-permute-start | bytes 589832 | tf_op jit(solution)/shard_map/ppermute | solution.py:292
  13.3 1.1 %copy-start.4 = (bf16[128,2304]{1,0:T(8,128)(2,1)S(1)}, bf16[128,2304]{1,0:T(8,128)(2,1)}, u32[]{:S(2)}) copy-start(bf16[128,2304]{1,0:T(8,128)(2,1)} %normed_hbm.1) | copy-start | bytes 1769476
  16.2 4.2 %copy-start.6 = (bf16[128,768]{1,0:T(8,128)(2,1)S(1)}, bf16[128,768]{1,0:T(8,128)(2,1)}, u32[]{:S(2)}) copy-start(bf16[128,768]{1,0:T(8,128)(2,1)} %get-tuple-element.18) | copy-start | bytes 589828
  16.2 5.9 %copy-start.5 = (bf16[128,768]{1,0:T(8,128)(2,1)S(1)}, bf16[128,768]{1,0:T(8,128)(2,1)}, u32[]{:S(2)}) copy-start(bf16[128,768]{1,0:T(8,128)(2,1)} %get-tuple-element.19.refs_0_) | copy-start | bytes 589828
  16.2 52.7 %all-to-all-start = ((bf16[8,2,288,128]{3,2,1,0:T(8,128)(2,1)}), bf16[8,2,288,128]{3,2,1,0:T(8,128)(2,1)S(1)}, u32[]{:S(2)}, u32[]{:S(2)}) async-start(bf16[8,2,288,128]{3,2,1,0:T(8,128)(2,1)} %get-tuple-element.20), calls=%async_computation | async-start | bytes 2359296 | tf_op jit(solution)/shard_map/all_to_all | solution.py:343
  20.3 19.7 %collective-permute-start.2 = (bf16[128,768]{1,0:T(8,128)(2,1)S(1)}, bf16[128,768]{1,0:T(8,128)(2,1)S(1)}, u32[]{:S(2)}, u32[]{:S(2)}) collective-permute-start(bf16[128,768]{1,0:T(8,128)(2,1)S(1)} %copy-done.6), channel_id=1, source_target_pairs={{0,12},{4,8},{8,4},{12,0},{16,28},{20,24},{24,20},{28,16},{1,13},{... | collective-permute-start | bytes 589832 | tf_op jit(solution)/shard_map/ppermute | solution.py:292
  22.1 18.8 %collective-permute-start.3 = (bf16[128,768]{1,0:T(8,128)(2,1)S(1)}, bf16[128,768]{1,0:T(8,128)(2,1)S(1)}, u32[]{:S(2)}, u32[]{:S(2)}) collective-permute-start(bf16[128,768]{1,0:T(8,128)(2,1)S(1)} %copy-done.5), channel_id=1, source_target_pairs={{0,16},{4,20},{8,24},{12,28},{16,0},{20,4},{24,8},{28,12},{1,17},{... | collective-permute-start | bytes 589832 | tf_op jit(solution)/shard_map/ppermute | solution.py:292
  23.6 29.0 %collective-permute-start.4 = (bf16[128,768]{1,0:T(8,128)(2,1)S(1)}, bf16[128,768]{1,0:T(8,128)(2,1)S(1)}, u32[]{:S(2)}, u32[]{:S(2)}) collective-permute-start(bf16[128,768]{1,0:T(8,128)(2,1)S(1)} %copy-done.6), channel_id=1, source_target_pairs={{0,20},{4,16},{8,28},{12,24},{16,4},{20,0},{24,12},{28,8},{1,21},{... | collective-permute-start | bytes 589832 | tf_op jit(solution)/shard_map/ppermute | solution.py:292
  23.8 28.8 %collective-permute-start.5 = (bf16[128,768]{1,0:T(8,128)(2,1)S(1)}, bf16[128,768]{1,0:T(8,128)(2,1)S(1)}, u32[]{:S(2)}, u32[]{:S(2)}) collective-permute-start(bf16[128,768]{1,0:T(8,128)(2,1)S(1)} %copy-done.5), channel_id=1, source_target_pairs={{0,24},{4,28},{8,16},{12,20},{16,8},{20,12},{24,0},{28,4},{1,25},{... | collective-permute-start | bytes 589832 | tf_op jit(solution)/shard_map/ppermute | solution.py:292
  25.3 27.3 %collective-permute-start.6 = (bf16[128,768]{1,0:T(8,128)(2,1)S(1)}, bf16[128,768]{1,0:T(8,128)(2,1)S(1)}, u32[]{:S(2)}, u32[]{:S(2)}) collective-permute-start(bf16[128,768]{1,0:T(8,128)(2,1)S(1)} %copy-done.6), channel_id=1, source_target_pairs={{0,28},{4,24},{8,20},{12,16},{16,12},{20,8},{24,4},{28,0},{1,29},{... | collective-permute-start | bytes 589832 | tf_op jit(solution)/shard_map/ppermute | solution.py:292
  52.6 9.8 %copy-start = (bf16[2304,512]{1,0:T(8,128)(2,1)S(1)}, bf16[2304,512]{1,0:T(8,128)(2,1)}, u32[]{:S(2)}) copy-start(bf16[2304,512]{1,0:T(8,128)(2,1)} %wq_ref.1) | copy-start | bytes 7077892
  52.6 9.8 %copy-start.2 = (bf16[2304,256]{1,0:T(8,128)(2,1)S(1)}, bf16[2304,256]{1,0:T(8,128)(2,1)}, u32[]{:S(2)}) copy-start(bf16[2304,256]{1,0:T(8,128)(2,1)} %wk_ref.1) | copy-start | bytes 3538948
  52.6 9.8 %copy-start.3 = (bf16[2304,256]{1,0:T(8,128)(2,1)S(1)}, bf16[2304,256]{1,0:T(8,128)(2,1)}, u32[]{:S(2)}) copy-start(bf16[2304,256]{1,0:T(8,128)(2,1)} %wv_ref.1) | copy-start | bytes 3538948
  60.2 8.7 %collective-permute-start.7 = (bf16[256,1024]{1,0:T(8,128)(2,1)S(1)}, bf16[256,1024]{1,0:T(8,128)(2,1)S(1)}, u32[]{:S(2)}, u32[]{:S(2)}) collective-permute-start(bf16[256,1024]{1,0:T(8,128)(2,1)S(1)} %get-tuple-element.22.attn_ref), channel_id=1, source_target_pairs={{0,4},{4,0},{8,12},{12,8},{16,20},{20,16},{24,28},{28,24},{1,5},{5... | collective-permute-start | bytes 1572872 | tf_op jit(solution)/shard_map/ppermute | solution.py:292
  60.5 1.8 %collective-permute-start.9 = (bf16[128,512]{1,0:T(8,128)(2,1)S(1)}, bf16[128,512]{1,0:T(8,128)(2,1)S(1)}, u32[]{:S(2)}, u32[]{:S(2)}) collective-permute-start(bf16[128,512]{1,0:T(8,128)(2,1)S(1)} %get-tuple-element.26), channel_id=1, source_target_pairs={{0,4},{4,0},{8,12},{12,8},{16,20},{20,16},{24,28},{28,24},{1,5},{5... | collective-permute-start | bytes 393224 | tf_op jit(solution)/shard_map/ppermute | solution.py:292
  60.7 8.1 %collective-permute-start.8 = (bf16[1024,128]{1,0:T(8,128)(2,1)S(1)}, bf16[1024,128]{1,0:T(8,128)(2,1)S(1)}, u32[]{:S(2)}, u32[]{:S(2)}) collective-permute-start(bf16[1024,128]{1,0:T(8,128)(2,1)S(1)} %get-tuple-element.23.dv_ref), channel_id=1, source_target_pairs={{0,4},{4,0},{8,12},{12,8},{16,20},{20,16},{24,28},{28,24},{1,5},{5... | collective-permute-start | bytes 786440 | tf_op jit(solution)/shard_map/ppermute | solution.py:292
  64.4 8.8 %collective-permute-start.10 = (bf16[576,128]{1,0:T(8,128)(2,1)}, bf16[576,128]{1,0:T(8,128)(2,1)S(1)}, u32[]{:S(2)}, u32[]{:S(2)}) collective-permute-start(bf16[576,128]{1,0:T(8,128)(2,1)} %get-tuple-element.28), channel_id=1, source_target_pairs={{0,3},{1,2},{2,1},{3,0},{4,7},{5,6},{6,5},{7,4},{8,11},{9,10},{10,... | collective-permute-start | bytes 442376 | tf_op jit(solution)/shard_map/ppermute | solution.py:292
  68.1 13.2 %collective-permute-start.11 = (bf16[576,128]{1,0:T(8,128)(2,1)}, bf16[576,128]{1,0:T(8,128)(2,1)S(1)}, u32[]{:S(2)}, u32[]{:S(2)}) collective-permute-start(bf16[576,128]{1,0:T(8,128)(2,1)} %get-tuple-element.29), channel_id=1, source_target_pairs={{0,2},{1,3},{2,0},{3,1},{4,6},{5,7},{6,4},{7,5},{8,10},{9,11},{10,... | collective-permute-start | bytes 442376 | tf_op jit(solution)/shard_map/ppermute | solution.py:292
  68.1 13.2 %collective-permute-start.12 = (bf16[576,128]{1,0:T(8,128)(2,1)}, bf16[576,128]{1,0:T(8,128)(2,1)S(1)}, u32[]{:S(2)}, u32[]{:S(2)}) collective-permute-start(bf16[576,128]{1,0:T(8,128)(2,1)} %get-tuple-element.30), channel_id=1, source_target_pairs={{0,1},{1,0},{2,3},{3,2},{4,5},{5,4},{6,7},{7,6},{8,9},{9,8},{10,11... | collective-permute-start | bytes 442376 | tf_op jit(solution)/shard_map/ppermute | solution.py:292

commit v5 on v4

--- a/solution.py
+++ b/solution.py
@@ -39,48 +39,48 @@
 
 
 def out_grad_kernel(
-    cot_hbm, weight_hbm, q_hbm, k_hbm, v_hbm, same_ref, other_ref, cot_ref, weight_ref, sem
+    cot_hbm, weight_hbm, q_hbm, k_hbm, v_hbm, sent_ref, done_ref, cot_ref, weight_ref, half_ref, sem
 ):
-    core = lax.axis_index("seq") % 2
+    done_ref[...] = jnp.zeros_like(done_ref)
     cut = weight_ref.shape[0] // 2
     cot_copy = pltpu.make_async_copy(cot_hbm, cot_ref, sem.at[0])
     cot_copy.start()
-    halves = ((other_ref, 1 - core), (same_ref, core))
     weight_copies = []
-    for place, (_, half) in enumerate(halves):
+    for half in range(2):
+        part = pl.ds(half * cut, cut)
         weight_copies.append(
-            pltpu.make_async_copy(
-                weight_hbm.at[at(half, cut)], weight_ref.at[at(place, cut)], sem.at[1 + place]
-            )
+            pltpu.make_async_copy(weight_hbm.at[part], weight_ref.at[part], sem.at[1 + half])
         )
         weight_copies[-1].start()
     plain_copies = []
-    for place, (target, half) in enumerate(halves):
+    for half in range(2):
         first = 0
         for which, source in enumerate((q_hbm, k_hbm, v_hbm)):
             cols = source.shape[1] // 2
             plain_copies.append(
                 pltpu.make_async_copy(
-                    source.at[:, at(half, cols)],
-                    target.at[:, pl.ds(first, cols)],
-                    sem.at[3 + 3 * place + which],
+                    source.at[:, pl.ds(half * cols, cols)],
+                    half_ref.at[half, :, pl.ds(first, cols)],
+                    sem.at[3 + 3 * half + which],
                 )
             )
             plain_copies[-1].start()
             first += cols
     cot_copy.wait()
-    for place, (target, _) in enumerate(halves):
-        weight_copies[place].wait()
-        grads_t = dot_nt(weight_ref[place * cut : (place + 1) * cut], cot_ref[...])
+    for half in range(2):
+        weight_copies[half].wait()
+        grads_t = dot_nt(weight_ref[half * cut : (half + 1) * cut], cot_ref[...])
         for h in range(cut // HEAD_SIZE):
-            target[:, first + h * HEAD_SIZE : first + (h + 1) * HEAD_SIZE] = grads_t[
+            half_ref[half, :, first + h * HEAD_SIZE : first + (h + 1) * HEAD_SIZE] = grads_t[
                 h * HEAD_SIZE : (h + 1) * HEAD_SIZE
             ].astype(jnp.bfloat16)
     for copy in plain_copies:
         copy.wait()
-
-
-def turn_kernel(parts, normed_hbm, cot_hbm, _, __, turned_ref, done_ref, normed_ref, cot_ref, sem):
+    for target in range(sent_ref.shape[0]):
+        sent_ref[target] = half_ref[target % 2]
+
+
+def turn_kernel(parts, normed_hbm, cot_hbm, _, turned_ref, done_ref, normed_ref, cot_ref, sem):
     cut = normed_ref.shape[1] // parts
     done_ref[...] = jnp.zeros_like(done_ref)
     copies = []
@@ -94,17 +94,13 @@
             turned_ref[part, which] = turned[part * cut : (part + 1) * cut]
 
 
-def attention_kernel(blocks, *refs):
-    attention_body(refs[:blocks], *refs[blocks + 1 :])
-
-
-def attention_body(
-    block_refs,
+def attention_kernel(
+    gathered_ref,
+    _,
     dx_own_ref,
     dx_far_ref,
     attn_ref,
     dv_ref,
-    gathered_ref,
     score_even_ref,
     score_odd_ref,
     prob_ref,
@@ -115,19 +111,10 @@
     key_t_ref,
     dq_t_ref,
     dk_ref,
-    sem,
 ):
     me = lax.axis_index("seq")
     core, chip = me % 2, me // 2
     rows = dx_own_ref.shape[0]
-    arrivals = []
-    for apart, source in enumerate(block_refs):
-        arrivals.append(
-            pltpu.make_async_copy(source, gathered_ref.at[at(me ^ apart, rows)], sem.at[apart])
-        )
-        arrivals[-1].start()
-    for copy in arrivals:
-        copy.wait()
     tokens = gathered_ref.shape[0]
     size = 2 * rows
     steps = tokens // size
@@ -313,26 +300,25 @@
     wide = 2 * QUERIES_PER_KEY * rows
     packed_cols = 2 * q_cols + 2 * kv_cols
     shape = jax.ShapeDtypeStruct
-    same, other = kernel_call(
+    sent, sent_done = kernel_call(
         out_grad_kernel,
-        (shape((rows, packed_cols), bf16),) * 2,
+        (shape((blocks, rows, packed_cols), bf16), shape((8, HEAD_SIZE), f32)),
         (out_cotangent, output_weight, stored_queries, stored_keys, stored_values),
         scratch=(
             pltpu.VMEM(out_cotangent.shape, bf16),
             pltpu.VMEM(output_weight.shape, bf16),
+            pltpu.VMEM((2, rows, packed_cols), bf16),
             pltpu.SemaphoreType.DMA((9,)),
         ),
         flops=4 * rows * model * q_cols,
         moved=2 * model * (rows + 2 * q_cols),
         room=63,
     )
-    held = {0: same}
-    for apart in range(blocks - 1, 0, -1):
-        held[apart] = swapped(other if apart % 2 else same, "seq", apart)
+    gathered = lax.all_to_all(sent, "seq", 0, 0).reshape(tokens, packed_cols)
     turned, turn_done = kernel_call(
         functools.partial(turn_kernel, blocks),
         (shape((blocks, 2, model // blocks, rows), bf16), shape((8, HEAD_SIZE), f32)),
-        (normed_input, out_cotangent, held[1], held[2]),
+        (normed_input, out_cotangent, sent_done),
         scratch=(
             pltpu.VMEM(normed_input.shape, bf16),
             pltpu.VMEM(out_cotangent.shape, bf16),
@@ -342,16 +328,16 @@
     )
     turned = lax.all_to_all(turned, "seq", 0, 0)
     dx_own, dx_far, attn, dv = kernel_call(
-        functools.partial(attention_kernel, blocks),
+        attention_kernel,
         (
             shape((rows, q_cols + 2 * kv_cols), bf16),
             shape((rows, q_cols + 2 * kv_cols), bf16),
             shape((q_cols, tokens), bf16),
             shape((tokens, kv_cols), bf16),
         ),
-        [held[apart] for apart in range(blocks)] + [turn_done],
+        (gathered, turn_done),
+        in_vmem=(0,),
         scratch=(
-            pltpu.VMEM((tokens, packed_cols), bf16),
             pltpu.VMEM((tokens, wide), f32),
             pltpu.VMEM((tokens, wide), f32),
             pltpu.VMEM((tokens, tokens * QUERIES_PER_KEY), bf16),
@@ -362,7 +348,6 @@
             pltpu.VMEM((HEAD_SIZE, tokens), bf16),
             pltpu.VMEM((HEAD_SIZE, wide), f32),
             pltpu.VMEM((2 * rows, HEAD_SIZE), f32),
-            pltpu.SemaphoreType.DMA((blocks,)),
         ),
         flops=8 * tokens * tokens * q_cols,
         moved=2 * tokens * packed_cols,

time: 82.2 us -> 62.5 us (0.76)
  waiting for transfers between devices: 43.7 us -> 31.2 us
  starting transfers between devices: 18.7 us -> 14.2 us
  Pallas kernels: 17.7 us -> 15 us
    ppermute x13 -> x6, waiting for transfers between devices: 43.7 us -> 9.38 us  [swapped(): lax.ppermute(value, axis, [(place, place ^ apart) for place in range(coun...]
    all_to_all x0 -> x1, waiting for transfers between devices: none -> 19.2 us  [gathered_plan(): gathered = lax.all_to_all(sent, 'seq', 0, 0).reshape(tokens, packed_cols)]
    ppermute x13 -> x6, starting transfers between devices: 14.5 us -> 5.34 us  [swapped(): lax.ppermute(value, axis, [(place, place ^ apart) for place in range(coun...]
    all_to_all x0 -> x1, starting transfers between devices: none -> 5.32 us  [gathered_plan(): gathered = lax.all_to_all(sent, 'seq', 0, 0).reshape(tokens, packed_cols)]
    pallas_call x6, Pallas kernels: 17.7 us -> 15 us  [kernel_call(): pl.pallas_call(body, out_shape=outs, in_specs=[vmem if place in in_vmem e...]
    all_to_all x1, waiting for transfers between devices: 0.01 us -> 2.59 us  [gathered_plan(): turned = lax.all_to_all(turned, 'seq', 0, 0)]
  transfers between devices with their start and end apart: 14 -> 8, of which waited for: 7 -> 5; matrix products, arithmetic and copies ran while one was open for 0% -> 0% of each run, Pallas kernels for 14% -> 16%
where the time goes in v5:
time: 62.5 us; the launch traced here: 62.2 us
  waiting for transfers between devices  31.2 us (50%)
  Pallas kernels  15 us (24%)
  starting transfers between devices  14.2 us (23%)
  local copies, waits for them, and re-layouts  1.06 us (2%)
  between operations  0.75 us (1%)
    all_to_all x1, waiting for transfers between devices, gathered_plan(): gathered = lax.all_to_all(sent, 'seq', 0, 0).reshape(tokens, packed_cols)  19.2 us
    pallas_call x6, Pallas kernels, kernel_call(): pl.pallas_call(body, out_shape=outs, in_specs=[vmem if place in in_vmem e...  15 us
    ppermute x6, waiting for transfers between devices, swapped(): lax.ppermute(value, axis, [(place, place ^ apart) for place in range(coun...  9.38 us
    ppermute x6, starting transfers between devices, swapped(): lax.ppermute(value, axis, [(place, place ^ apart) for place in range(coun...  5.34 us
    all_to_all x1, starting transfers between devices, gathered_plan(): gathered = lax.all_to_all(sent, 'seq', 0, 0).reshape(tokens, packed_cols)  5.32 us
    all_to_all x1, starting transfers between devices, gathered_plan(): turned = lax.all_to_all(turned, 'seq', 0, 0)  3.56 us
    all_to_all x1, waiting for transfers between devices, gathered_plan(): turned = lax.all_to_all(turned, 'seq', 0, 0)  2.59 us
  transfers between devices with their start and end apart: 8, of which 5 were waited for; matrix products, arithmetic and copies ran while one was open for 0% of the time, Pallas kernels for 16%

profile of v5, /device:TPU:0, one launch (start us, length us, event | category | flops | bytes accessed | tf_op | source)
XLA Modules:
  0.0 62.2 jit_solution(4484715767649503123)
XLA Ops:
  0.6 4.3 %shard_map.112 = (bf16[8,128,768]{2,1,0:T(8,128)(2,1)}, f32[8,128]{1,0:T(8,128)}) custom-call(bf16[128,2304]{1,0:T(8,128)(2,1)} %cot_hbm.3, bf16[512,2304]{1,0:T(8,128)(2,1)} %weight_hbm.1, bf16[128,512]{1,0:T(8,128)(2,1)} %q_hbm.1, bf16[128,256]{1,0:T(8,128)(2,1)} %k_hbm.1, bf16[128,256]{1,0:T(8,128)(2,1)} %v_hbm.1), custom_call_target="tpu_custom_call" | custom-call | flops 301989888 | bytes 2949120 | tf_op jit(solution)/shard_map/pallas_call | solution.py:266
  5.0 0.0 copy-start.1
  5.0 0.0 copy-start.5
  5.0 0.0 copy-start.6
  5.0 5.3 %all-to-all-start.1 = ((bf16[8,128,768]{2,1,0:T(8,128)(2,1)}), bf16[8,128,768]{2,1,0:T(8,128)(2,1)S(1)}, u32[]{:S(2)}, u32[]{:S(2)}) async-start(bf16[8,128,768]{2,1,0:T(8,128)(2,1)} %get-tuple-element.20), calls=%async_computation.1 | async-start | bytes 3145728 | tf_op jit(solution)/shard_map/all_to_all | solution.py:317
  10.3 0.7 %shard_map.113 = (bf16[8,2,288,128]{3,2,1,0:T(8,128)(2,1)S(1)}, f32[8,128]{1,0:T(8,128)S(1)}) custom-call(bf16[128,2304]{1,0:T(8,128)(2,1)S(1)} %copy-done.5, bf16[128,2304]{1,0:T(8,128)(2,1)S(1)} %copy-done.1, f32[8,128]{1,0:T(8,128)S(1)} %copy-done.6), custom_call_target="tpu_custom_call" | custom-call | bytes 2359296 | tf_op jit(solution)/shard_map/pallas_call | solution.py:266
  11.1 1.0 %copy-done.4 = bf16[8,2,288,128]{3,2,1,0:T(8,128)(2,1)} copy-done((bf16[8,2,288,128]{3,2,1,0:T(8,128)(2,1)}, bf16[8,2,288,128]{3,2,1,0:T(8,128)(2,1)S(1)}, u32[]{:S(2)}) %copy-start.4) | copy-done | bytes 1179672
  12.1 19.2 %all-to-all-done.1 = bf16[8,128,768]{2,1,0:T(8,128)(2,1)S(1)} async-done(((bf16[8,128,768]{2,1,0:T(8,128)(2,1)}), bf16[8,128,768]{2,1,0:T(8,128)(2,1)S(1)}, u32[]{:S(2)}, u32[]{:S(2)}) %all-to-all-start.1) | async-done | bytes 1572896 | tf_op jit(solution)/shard_map/all_to_all | solution.py:317
  31.3 3.6 %all-to-all-start = ((bf16[8,2,288,128]{3,2,1,0:T(8,128)(2,1)}), bf16[8,2,288,128]{3,2,1,0:T(8,128)(2,1)S(1)}, u32[]{:S(2)}, u32[]{:S(2)}) async-start(bf16[8,2,288,128]{3,2,1,0:T(8,128)(2,1)} %copy-done.4), calls=%async_computation | async-start | bytes 2359296 | tf_op jit(solution)/shard_map/all_to_all | solution.py:329
  34.9 0.0 copy-start
  34.9 0.0 copy-start.2
  35.0 5.4 %shard_map.114 = (bf16[128,512]{1,0:T(8,128)(2,1)S(1)}, bf16[128,512]{1,0:T(8,128)(2,1)S(1)}, bf16[256,1024]{1,0:T(8,128)(2,1)S(1)}, bf16[1024,128]{1,0:T(8,128)(2,1)S(1)}) custom-call(bf16[1024,768]{1,0:T(8,128)(2,1)S(1)} %bitcast.3, f32[8,128]{1,0:T(8,128)S(1)} %get-tuple-element.21._), custom_call_target="tpu_custom_call" | custom-call | flops 2147483648 | bytes 1572864 | tf_op jit(solution)/shard_map/pallas_call | solution.py:266
  40.4 0.4 collective-permute-start
  40.8 0.1 collective-permute-start.2
  41.0 0.4 collective-permute-start.1
  41.3 1.2 %collective-permute-done.2.far_ref = bf16[128,512]{1,0:T(8,128)(2,1)S(1)} collective-permute-done((bf16[128,512]{1,0:T(8,128)(2,1)S(1)}, bf16[128,512]{1,0:T(8,128)(2,1)S(1)}, u32[]{:S(2)}, u32[]{:S(2)}) %collective-permute-start.2) | collective-permute-done | bytes 131104 | tf_op jit(solution)/shard_map/ppermute | solution.py:279
  42.6 2.1 %shard_map.116 = (bf16[576,128]{1,0:T(8,128)(2,1)}, bf16[576,128]{1,0:T(8,128)(2,1)}, bf16[576,128]{1,0:T(8,128)(2,1)}, f32[576,128]{1,0:T(8,128)S(1)}) custom-call(bf16[128,512]{1,0:T(8,128)(2,1)S(1)} %get-tuple-element.25.own_ref, bf16[128,512]{1,0:T(8,128)(2,1)S(1)} %collective-permute-done.2.far_ref, bf16[2304,512]{1,0:T(8,128)(2,1)S(1)} %copy-done, ...), custom_call_target="tpu_custom_call" | custom-call | flops 603979776 | bytes 4718592 | tf_op jit(solution)/shard_map/pallas_call | solution.py:266
  44.7 3.6 %collective-permute-start.3 = (bf16[576,128]{1,0:T(8,128)(2,1)}, bf16[576,128]{1,0:T(8,128)(2,1)S(1)}, u32[]{:S(2)}, u32[]{:S(2)}) collective-permute-start(bf16[576,128]{1,0:T(8,128)(2,1)} %get-tuple-element.28), channel_id=1, source_target_pairs={{0,3},{1,2},{2,1},{3,0},{4,7},{5,6},{6,5},{7,4},{8,11},{9,10},{10,... | collective-permute-start | bytes 442376 | tf_op jit(solution)/shard_map/ppermute | solution.py:279
  48.3 0.8 %collective-permute-start.5 = (bf16[576,128]{1,0:T(8,128)(2,1)}, bf16[576,128]{1,0:T(8,128)(2,1)S(1)}, u32[]{:S(2)}, u32[]{:S(2)}) collective-permute-start(bf16[576,128]{1,0:T(8,128)(2,1)} %get-tuple-element.30), channel_id=1, source_target_pairs={{0,1},{1,0},{2,3},{3,2},{4,5},{5,4},{6,7},{7,6},{8,9},{9,8},{10,11... | collective-permute-start | bytes 442376 | tf_op jit(solution)/shard_map/ppermute | solution.py:279
  49.1 2.6 %all-to-all-done.turned_ref = bf16[8,2,288,128]{3,2,1,0:T(8,128)(2,1)S(1)} async-done(((bf16[8,2,288,128]{3,2,1,0:T(8,128)(2,1)}), bf16[8,2,288,128]{3,2,1,0:T(8,128)(2,1)S(1)}, u32[]{:S(2)}, u32[]{:S(2)}) %all-to-all-start) | async-done | bytes 1179680 | tf_op jit(solution)/shard_map/all_to_all | solution.py:329
  51.7 1.7 %shard_map.115 = (f32[288,256]{1,0:T(8,128)}, f32[288,512]{1,0:T(8,128)}, f32[8,128]{1,0:T(8,128)S(1)}) custom-call(bf16[8,2,288,128]{3,2,1,0:T(8,128)(2,1)S(1)} %all-to-all-done.turned_ref, bf16[256,1024]{1,0:T(8,128)(2,1)S(1)} %get-tuple-element.22.attn_ref, bf16[256,1024]{1,0:T(8,128)(2,1)S(1)} %collective-permute-done.far_attn_ref, ...), custom_call_target="tpu_custom_call" | custom-call | flops 452984832 | bytes 2064384 | tf_op jit(solution)/shard_map/pallas_call | solution.py:266
  53.4 0.1 collective-permute-done.3.refs_0_
  53.5 8.1 %collective-permute-done.4.refs_1_ = bf16[576,128]{1,0:T(8,128)(2,1)S(1)} collective-permute-done((bf16[576,128]{1,0:T(8,128)(2,1)}, bf16[576,128]{1,0:T(8,128)(2,1)S(1)}, u32[]{:S(2)}, u32[]{:S(2)}) %collective-permute-start.4) | collective-permute-done | bytes 147488 | tf_op jit(solution)/shard_map/ppermute | solution.py:279
  61.5 0.7 %shard_map.117 = bf16[576,128]{1,0:T(8,128)(2,1)} custom-call(f32[8,128]{1,0:T(8,128)S(1)} %get-tuple-element.24._, f32[576,128]{1,0:T(8,128)S(1)} %get-tuple-element.27.own_ref, bf16[576,128]{1,0:T(8,128)(2,1)S(1)} %collective-permute-done.3.refs_0_, bf16[576,128]{1,0:T(8,128)(2,1)S(1)} %collective-permute-done.4.refs_1_, ...), custom_call_target="tpu_custom_call" | custom-call | bytes 1179648 | tf_op jit(solution)/shard_map/pallas_call | solution.py:266
  (12 shorter events, 0.0 us)
Async XLA Ops:
  5.0 5.4 %copy-start.1 = (bf16[128,2304]{1,0:T(8,128)(2,1)S(1)}, bf16[128,2304]{1,0:T(8,128)(2,1)}, u32[]{:S(2)}) copy-start(bf16[128,2304]{1,0:T(8,128)(2,1)} %cot_hbm.3) | copy-start | bytes 1769476
  5.0 5.3 %copy-start.5 = (bf16[128,2304]{1,0:T(8,128)(2,1)S(1)}, bf16[128,2304]{1,0:T(8,128)(2,1)}, u32[]{:S(2)}) copy-start(bf16[128,2304]{1,0:T(8,128)(2,1)} %normed_hbm.1) | copy-start | bytes 1769476
  5.0 5.3 %copy-start.6 = (f32[8,128]{1,0:T(8,128)S(1)}, f32[8,128]{1,0:T(8,128)}, u32[]{:S(2)}) copy-start(f32[8,128]{1,0:T(8,128)} %get-tuple-element.18._) | copy-start | bytes 12292
  5.0 26.3 %all-to-all-start.1 = ((bf16[8,128,768]{2,1,0:T(8,128)(2,1)}), bf16[8,128,768]{2,1,0:T(8,128)(2,1)S(1)}, u32[]{:S(2)}, u32[]{:S(2)}) async-start(bf16[8,128,768]{2,1,0:T(8,128)(2,1)} %get-tuple-element.20), calls=%async_computation.1 | async-start | bytes 3145728 | tf_op jit(solution)/shard_map/all_to_all | solution.py:317
  11.1 1.0 %copy-start.4 = (bf16[8,2,288,128]{3,2,1,0:T(8,128)(2,1)}, bf16[8,2,288,128]{3,2,1,0:T(8,128)(2,1)S(1)}, u32[]{:S(2)}) copy-start(bf16[8,2,288,128]{3,2,1,0:T(8,128)(2,1)S(1)} %get-tuple-element.19) | copy-start | bytes 3538948
  31.3 20.3 %all-to-all-start = ((bf16[8,2,288,128]{3,2,1,0:T(8,128)(2,1)}), bf16[8,2,288,128]{3,2,1,0:T(8,128)(2,1)S(1)}, u32[]{:S(2)}, u32[]{:S(2)}) async-start(bf16[8,2,288,128]{3,2,1,0:T(8,128)(2,1)} %copy-done.4), calls=%async_computation | async-start | bytes 2359296 | tf_op jit(solution)/shard_map/all_to_all | solution.py:329
  34.9 7.6 %copy-start = (bf16[2304,512]{1,0:T(8,128)(2,1)S(1)}, bf16[2304,512]{1,0:T(8,128)(2,1)}, u32[]{:S(2)}) copy-start(bf16[2304,512]{1,0:T(8,128)(2,1)} %wq_ref.1) | copy-start | bytes 7077892
  34.9 7.6 %copy-start.2 = (bf16[2304,256]{1,0:T(8,128)(2,1)S(1)}, bf16[2304,256]{1,0:T(8,128)(2,1)}, u32[]{:S(2)}) copy-start(bf16[2304,256]{1,0:T(8,128)(2,1)} %wk_ref.1) | copy-start | bytes 3538948
  34.9 7.6 %copy-start.3 = (bf16[2304,256]{1,0:T(8,128)(2,1)S(1)}, bf16[2304,256]{1,0:T(8,128)(2,1)}, u32[]{:S(2)}) copy-start(bf16[2304,256]{1,0:T(8,128)(2,1)} %wv_ref.1) | copy-start | bytes 3538948
  40.4 11.3 %collective-permute-start = (bf16[256,1024]{1,0:T(8,128)(2,1)S(1)}, bf16[256,1024]{1,0:T(8,128)(2,1)S(1)}, u32[]{:S(2)}, u32[]{:S(2)}) collective-permute-start(bf16[256,1024]{1,0:T(8,128)(2,1)S(1)} %get-tuple-element.22.attn_ref), channel_id=1, source_target_pairs={{0,4},{4,0},{8,12},{12,8},{16,20},{20,16},{24,28},{28,24},{1,5},{5... | collective-permute-start | bytes 1572872 | tf_op jit(solution)/shard_map/ppermute | solution.py:279
  40.8 1.7 %collective-permute-start.2 = (bf16[128,512]{1,0:T(8,128)(2,1)S(1)}, bf16[128,512]{1,0:T(8,128)(2,1)S(1)}, u32[]{:S(2)}, u32[]{:S(2)}) collective-permute-start(bf16[128,512]{1,0:T(8,128)(2,1)S(1)} %get-tuple-element.26), channel_id=1, source_target_pairs={{0,4},{4,0},{8,12},{12,8},{16,20},{20,16},{24,28},{28,24},{1,5},{5... | collective-permute-start | bytes 393224 | tf_op jit(solution)/shard_map/ppermute | solution.py:279
  41.0 10.7 %collective-permute-start.1 = (bf16[1024,128]{1,0:T(8,128)(2,1)S(1)}, bf16[1024,128]{1,0:T(8,128)(2,1)S(1)}, u32[]{:S(2)}, u32[]{:S(2)}) collective-permute-start(bf16[1024,128]{1,0:T(8,128)(2,1)S(1)} %get-tuple-element.23.dv_ref), channel_id=1, source_target_pairs={{0,4},{4,0},{8,12},{12,8},{16,20},{20,16},{24,28},{28,24},{1,5},{5... | collective-permute-start | bytes 786440 | tf_op jit(solution)/shard_map/ppermute | solution.py:279
  44.7 8.8 %collective-permute-start.3 = (bf16[576,128]{1,0:T(8,128)(2,1)}, bf16[576,128]{1,0:T(8,128)(2,1)S(1)}, u32[]{:S(2)}, u32[]{:S(2)}) collective-permute-start(bf16[576,128]{1,0:T(8,128)(2,1)} %get-tuple-element.28), channel_id=1, source_target_pairs={{0,3},{1,2},{2,1},{3,0},{4,7},{5,6},{6,5},{7,4},{8,11},{9,10},{10,... | collective-permute-start | bytes 442376 | tf_op jit(solution)/shard_map/ppermute | solution.py:279
  48.3 13.2 %collective-permute-start.4 = (bf16[576,128]{1,0:T(8,128)(2,1)}, bf16[576,128]{1,0:T(8,128)(2,1)S(1)}, u32[]{:S(2)}, u32[]{:S(2)}) collective-permute-start(bf16[576,128]{1,0:T(8,128)(2,1)} %get-tuple-element.29), channel_id=1, source_target_pairs={{0,2},{1,3},{2,0},{3,1},{4,6},{5,7},{6,4},{7,5},{8,10},{9,11},{10,... | collective-permute-start | bytes 442376 | tf_op jit(solution)/shard_map/ppermute | solution.py:279
  48.3 13.2 %collective-permute-start.5 = (bf16[576,128]{1,0:T(8,128)(2,1)}, bf16[576,128]{1,0:T(8,128)(2,1)S(1)}, u32[]{:S(2)}, u32[]{:S(2)}) collective-permute-start(bf16[576,128]{1,0:T(8,128)(2,1)} %get-tuple-element.30), channel_id=1, source_target_pairs={{0,1},{1,0},{2,3},{3,2},{4,5},{5,4},{6,7},{7,6},{8,9},{9,8},{10,11... | collective-permute-start | bytes 442376 | tf_op jit(solution)/shard_map/ppermute | solution.py:279

commit v6 on v4

--- a/solution.py
+++ b/solution.py
@@ -38,8 +38,28 @@
     return pl.ds(pl.multiple_of(place * size, size), size)
 
 
+def pack_kernel(q_hbm, k_hbm, v_hbm, sent_hbm, done_ref, sem):
+    done_ref[...] = jnp.zeros_like(done_ref)
+    copies = []
+    for target in range(sent_hbm.shape[0]):
+        first = 0
+        for which, source in enumerate((q_hbm, k_hbm, v_hbm)):
+            cols = source.shape[1] // 2
+            copies.append(
+                pltpu.make_async_copy(
+                    source.at[:, pl.ds(target % 2 * cols, cols)],
+                    sent_hbm.at[target, :, pl.ds(first, cols)],
+                    sem.at[3 * target + which],
+                )
+            )
+            copies[-1].start()
+            first += cols
+    for copy in copies:
+        copy.wait()
+
+
 def out_grad_kernel(
-    cot_hbm, weight_hbm, q_hbm, k_hbm, v_hbm, same_ref, other_ref, cot_ref, weight_ref, sem
+    cot_hbm, weight_hbm, _, same_ref, other_ref, cot_ref, weight_ref, sem
 ):
     core = lax.axis_index("seq") % 2
     cut = weight_ref.shape[0] // 2
@@ -54,33 +74,15 @@
             )
         )
         weight_copies[-1].start()
-    plain_copies = []
-    for place, (target, half) in enumerate(halves):
-        first = 0
-        for which, source in enumerate((q_hbm, k_hbm, v_hbm)):
-            cols = source.shape[1] // 2
-            plain_copies.append(
-                pltpu.make_async_copy(
-                    source.at[:, at(half, cols)],
-                    target.at[:, pl.ds(first, cols)],
-                    sem.at[3 + 3 * place + which],
-                )
-            )
-            plain_copies[-1].start()
-            first += cols
     cot_copy.wait()
     for place, (target, _) in enumerate(halves):
         weight_copies[place].wait()
-        grads_t = dot_nt(weight_ref[place * cut : (place + 1) * cut], cot_ref[...])
-        for h in range(cut // HEAD_SIZE):
-            target[:, first + h * HEAD_SIZE : first + (h + 1) * HEAD_SIZE] = grads_t[
-                h * HEAD_SIZE : (h + 1) * HEAD_SIZE
-            ].astype(jnp.bfloat16)
-    for copy in plain_copies:
-        copy.wait()
-
-
-def turn_kernel(parts, normed_hbm, cot_hbm, _, __, turned_ref, done_ref, normed_ref, cot_ref, sem):
+        target[...] = dot_nt(
+            weight_ref[place * cut : (place + 1) * cut], cot_ref[...]
+        ).astype(jnp.bfloat16)
+
+
+def turn_kernel(parts, normed_hbm, cot_hbm, _, turned_ref, done_ref, normed_ref, cot_ref, sem):
     cut = normed_ref.shape[1] // parts
     done_ref[...] = jnp.zeros_like(done_ref)
     copies = []
@@ -94,55 +96,21 @@
             turned_ref[part, which] = turned[part * cut : (part + 1) * cut]
 
 
-def attention_kernel(blocks, *refs):
-    attention_body(refs[:blocks], *refs[blocks + 1 :])
-
-
-def attention_body(
-    block_refs,
-    dx_own_ref,
-    dx_far_ref,
-    attn_ref,
-    dv_ref,
-    gathered_ref,
-    score_even_ref,
-    score_odd_ref,
-    prob_ref,
-    grad_t_ref,
-    delta_ref,
-    query_ref,
-    value_t_ref,
-    key_t_ref,
-    dq_t_ref,
-    dk_ref,
-    sem,
-):
-    me = lax.axis_index("seq")
-    core, chip = me % 2, me // 2
-    rows = dx_own_ref.shape[0]
-    arrivals = []
-    for apart, source in enumerate(block_refs):
-        arrivals.append(
-            pltpu.make_async_copy(source, gathered_ref.at[at(me ^ apart, rows)], sem.at[apart])
-        )
-        arrivals[-1].start()
-    for copy in arrivals:
-        copy.wait()
+def probability_kernel(
+    gathered_ref, prob_ref, inverse_ref, attn_ref, done_ref, score_even_ref, score_odd_ref, value_t_ref
+):
+    done_ref[...] = jnp.zeros_like(done_ref)
     tokens = gathered_ref.shape[0]
-    size = 2 * rows
-    steps = tokens // size
-    wide = QUERIES_PER_KEY * size
     heads = QUERIES_PER_KEY
+    wide = score_even_ref.shape[1]
+    size = wide // heads
     key_cols = slice(heads * HEAD_SIZE, (heads + 1) * HEAD_SIZE)
     value_cols = slice((heads + 1) * HEAD_SIZE, (heads + 2) * HEAD_SIZE)
-    grad_base = (heads + 2) * HEAD_SIZE
     value_t_ref[...] = gathered_ref[:, value_cols].T
-    key_t_ref[...] = gathered_ref[:, key_cols].T
     key_place = lax.broadcasted_iota(jnp.int32, (size, wide), 0)
     query_place = lax.broadcasted_iota(jnp.int32, (size, wide), 1) % size
     allowed = key_place <= query_place
-
-    for step in range(steps):
+    for step in range(tokens // size):
         span = (step + 1) * size
         own = slice(step * size, span)
         lanes = slice(step * wide, (step + 1) * wide)
@@ -150,7 +118,6 @@
         queries = jnp.concatenate(
             [gathered_ref[own, h * HEAD_SIZE : (h + 1) * HEAD_SIZE] for h in range(heads)], axis=0
         )
-        query_ref[lanes] = queries
         top = None
         for piece in range(step + 1):
             part = slice(piece * size, (piece + 1) * size)
@@ -169,61 +136,117 @@
             summed = jnp.sum(weights.reshape(size // 8, 8, wide), axis=0)
             total = summed if total is None else total + summed
         inverse = 1.0 / jnp.sum(total, axis=0, keepdims=True)
+        inverse_ref[:, lanes] = inverse
         attn = dot_nn(value_t_ref[:, :span], prob_ref[:span, lanes]) * inverse
         for h in range(heads):
             attn_ref[h * HEAD_SIZE : (h + 1) * HEAD_SIZE, own] = attn[
                 :, h * size : (h + 1) * size
             ].astype(jnp.bfloat16)
+
+
+def gradient_kernel(
+    gathered_ref,
+    prob_ref,
+    inverse_ref,
+    attn_ref,
+    _,
+    *refs,
+):
+    blocks = len(refs) - 9
+    og_refs = refs[:blocks]
+    (
+        dx_own_ref,
+        dx_far_ref,
+        grad_t_ref,
+        og_ref,
+        delta_ref,
+        dq_t_ref,
+        dk_ref,
+        dv_ref,
+        sem,
+    ) = refs[blocks:]
+    me = lax.axis_index("seq")
+    core, chip = me % 2, me // 2
+    rows = dx_own_ref.shape[0]
+    arrivals = []
+    for apart, source in enumerate(og_refs):
+        arrivals.append(pltpu.make_async_copy(source, og_ref.at[me ^ apart], sem.at[apart]))
+        arrivals[-1].start()
+    dq_t_ref[...] = jnp.zeros_like(dq_t_ref)
+    dk_ref[...] = jnp.zeros_like(dk_ref)
+    dv_ref[...] = jnp.zeros_like(dv_ref)
+    for copy in arrivals:
+        copy.wait()
+    tokens = gathered_ref.shape[0]
+    heads = QUERIES_PER_KEY
+    size = 2 * rows
+    wide = heads * size
+    steps = tokens // size
+    key_cols = slice(heads * HEAD_SIZE, (heads + 1) * HEAD_SIZE)
+    value_cols = slice((heads + 1) * HEAD_SIZE, (heads + 2) * HEAD_SIZE)
+    for step in range(steps):
+        lanes = slice(step * wide, (step + 1) * wide)
         grads_t = jnp.concatenate(
             [
-                gathered_ref[
-                    block * rows : (block + 1) * rows,
-                    grad_base + h * HEAD_SIZE : grad_base + (h + 1) * HEAD_SIZE,
-                ]
+                og_ref[block, h * HEAD_SIZE : (h + 1) * HEAD_SIZE]
                 for h in range(heads)
                 for block in (2 * step, 2 * step + 1)
             ],
             axis=1,
         )
-        grads_t = (grads_t.astype(jnp.float32) * inverse).astype(jnp.bfloat16)
+        grads_t = (grads_t.astype(jnp.float32) * inverse_ref[:, lanes]).astype(jnp.bfloat16)
         grad_t_ref[:, lanes] = grads_t
-        delta_ref[:, lanes] = jnp.sum(grads_t.astype(jnp.float32) * attn, axis=0, keepdims=True)
-
+        attn = jnp.concatenate(
+            [
+                attn_ref[h * HEAD_SIZE : (h + 1) * HEAD_SIZE, step * size : (step + 1) * size]
+                for h in range(heads)
+            ],
+            axis=1,
+        )
+        delta_ref[:, lanes] = jnp.sum(
+            grads_t.astype(jnp.float32) * attn.astype(jnp.float32), axis=0, keepdims=True
+        )
+    for step in range(steps):
+        key_rows = at(jnp.minimum(chip, step), size)
+        query_step = jnp.maximum(chip, step)
+        lanes = at(query_step, wide)
+        prob = prob_ref[key_rows, lanes]
+        dprob = dot_nn(gathered_ref[key_rows, value_cols], grad_t_ref[:, lanes])
+        dscore = (prob.astype(jnp.float32) * (dprob - delta_ref[:, lanes])).astype(jnp.bfloat16)
+
+        @pl.when(step <= chip)
+        def _():
+            dq_t_ref[...] += dot_nn(gathered_ref[key_rows, key_cols].T, dscore)
+
+        @pl.when(step >= chip)
+        def _():
+            queries = jnp.concatenate(
+                [
+                    gathered_ref[at(query_step, size), h * HEAD_SIZE : (h + 1) * HEAD_SIZE]
+                    for h in range(heads)
+                ],
+                axis=0,
+            )
+            dk_ref[...] += dot_nn(dscore, queries)
+            dv_ref[...] += dot_nt(prob, grad_t_ref[:, lanes])
+
+    for target, half in ((dx_far_ref, 1 - core), (dx_own_ref, core)):
+        for h in range(heads):
+            target[:, h * HEAD_SIZE : (h + 1) * HEAD_SIZE] = (
+                logit_scale * dq_t_ref[:, at(2 * h + half, rows)]
+            ).T.astype(jnp.bfloat16)
+        target[:, key_cols] = (logit_scale * dk_ref[at(half, rows)]).astype(jnp.bfloat16)
+        target[:, value_cols] = dv_ref[at(half, rows)].astype(jnp.bfloat16)
+
+
+def value_grad_kernel(size, prob_ref, grad_t_ref, dv_ref):
+    steps = prob_ref.shape[0] // size
+    wide = grad_t_ref.shape[1] // steps
     for step in range(steps):
         own = slice(step * size, (step + 1) * size)
         dv_ref[own] = dot_nt(prob_ref[own, step * wide :], grad_t_ref[:, step * wide :]).astype(
             jnp.bfloat16
         )
-
-    dq_t_ref[...] = jnp.zeros_like(dq_t_ref)
-    dk_ref[...] = jnp.zeros_like(dk_ref)
-    for step in range(steps):
-        key_step = jnp.minimum(chip, step)
-        query_step = jnp.maximum(chip, step)
-        dprob = dot_nn(
-            gathered_ref[at(key_step, size), value_cols], grad_t_ref[:, at(query_step, wide)]
-        )
-        dscore = (
-            prob_ref[at(key_step, size), at(query_step, wide)].astype(jnp.float32)
-            * (dprob - delta_ref[:, at(query_step, wide)])
-        ).astype(jnp.bfloat16)
-
-        @pl.when(step <= chip)
-        def _():
-            dq_t_ref[...] += dot_nn(key_t_ref[:, at(key_step, size)], dscore)
-
-        @pl.when(step >= chip)
-        def _():
-            dk_ref[...] += dot_nn(dscore, query_ref[at(query_step, wide)])
-
-    for target, half in ((dx_far_ref, 1 - core), (dx_own_ref, core)):
-        for h in range(heads):
-            target[:, h * HEAD_SIZE : (h + 1) * HEAD_SIZE] = (
-                (logit_scale * dq_t_ref[:, at(2 * h + half, rows)])
-                .T.astype(jnp.bfloat16)
-            )
-        target[:, key_cols] = (logit_scale * dk_ref[at(half, rows)]).astype(jnp.bfloat16)
-        target[:, value_cols] = dv_ref[at(2 * chip + half, rows)]
 
 
 def input_terms_kernel(
@@ -273,14 +296,16 @@
     refs[-1][...] = total.astype(jnp.bfloat16)
 
 
-def kernel_call(body, outs, operands, in_vmem=(), scratch=(), flops=0, moved=0, room=32):
+def kernel_call(
+    body, outs, operands, in_vmem=(), scratch=(), flops=0, moved=0, room=16, out_hbm=()
+):
     vmem = pl.BlockSpec(memory_space=pltpu.VMEM)
     hbm = pl.BlockSpec(memory_space=pltpu.HBM)
     return pl.pallas_call(
         body,
         out_shape=outs,
         in_specs=[vmem if place in in_vmem else hbm for place in range(len(operands))],
-        out_specs=jax.tree.map(lambda _: vmem, outs),
+        out_specs=tuple(hbm if place in out_hbm else vmem for place in range(len(outs))),
         scratch_shapes=list(scratch),
         compiler_params=pltpu.CompilerParams(vmem_limit_bytes=room * 1024 * 1024),
         cost_estimate=pl.CostEstimate(flops=flops, bytes_accessed=moved, transcendentals=0),
@@ -311,28 +336,56 @@
     q_cols = stored_queries.shape[1] // 2
     kv_cols = HEAD_SIZE
     wide = 2 * QUERIES_PER_KEY * rows
-    packed_cols = 2 * q_cols + 2 * kv_cols
+    packed_cols = q_cols + 2 * kv_cols
     shape = jax.ShapeDtypeStruct
+    sent, sent_done = kernel_call(
+        pack_kernel,
+        (shape((blocks, rows, packed_cols), bf16), shape((8, HEAD_SIZE), f32)),
+        (stored_queries, stored_keys, stored_values),
+        scratch=(pltpu.SemaphoreType.DMA((3 * blocks,)),),
+        moved=4 * blocks * rows * packed_cols,
+        room=63,
+        out_hbm=(0,),
+    )
+    gathered = lax.all_to_all(sent, "seq", 0, 0).reshape(tokens, packed_cols)
     same, other = kernel_call(
         out_grad_kernel,
-        (shape((rows, packed_cols), bf16),) * 2,
-        (out_cotangent, output_weight, stored_queries, stored_keys, stored_values),
+        (shape((q_cols, rows), bf16),) * 2,
+        (out_cotangent, output_weight, sent_done),
         scratch=(
             pltpu.VMEM(out_cotangent.shape, bf16),
             pltpu.VMEM(output_weight.shape, bf16),
-            pltpu.SemaphoreType.DMA((9,)),
+            pltpu.SemaphoreType.DMA((3,)),
         ),
         flops=4 * rows * model * q_cols,
         moved=2 * model * (rows + 2 * q_cols),
         room=63,
     )
-    held = {0: same}
-    for apart in range(blocks - 1, 0, -1):
-        held[apart] = swapped(other if apart % 2 else same, "seq", apart)
+    held = [same] + [
+        swapped(other if apart % 2 else same, "seq", apart) for apart in range(1, blocks)
+    ]
+    prob, inverse, attn, prob_done = kernel_call(
+        probability_kernel,
+        (
+            shape((tokens, tokens * QUERIES_PER_KEY), bf16),
+            shape((1, tokens * QUERIES_PER_KEY), f32),
+            shape((q_cols, tokens), bf16),
+            shape((8, HEAD_SIZE), f32),
+        ),
+        (gathered,),
+        in_vmem=(0,),
+        scratch=(
+            pltpu.VMEM((tokens, wide), f32),
+            pltpu.VMEM((tokens, wide), f32),
+            pltpu.VMEM((HEAD_SIZE, tokens), bf16),
+        ),
+        flops=3 * tokens * tokens * q_cols,
+        moved=2 * tokens * (packed_cols + q_cols + tokens * QUERIES_PER_KEY),
+    )
     turned, turn_done = kernel_call(
         functools.partial(turn_kernel, blocks),
         (shape((blocks, 2, model // blocks, rows), bf16), shape((8, HEAD_SIZE), f32)),
-        (normed_input, out_cotangent, held[1], held[2]),
+        (normed_input, out_cotangent, prob_done),
         scratch=(
             pltpu.VMEM(normed_input.shape, bf16),
             pltpu.VMEM(out_cotangent.shape, bf16),
@@ -341,44 +394,49 @@
         moved=8 * rows * model,
     )
     turned = lax.all_to_all(turned, "seq", 0, 0)
-    dx_own, dx_far, attn, dv = kernel_call(
-        functools.partial(attention_kernel, blocks),
+    dx_own, dx_far, grad_t = kernel_call(
+        gradient_kernel,
         (
             shape((rows, q_cols + 2 * kv_cols), bf16),
             shape((rows, q_cols + 2 * kv_cols), bf16),
-            shape((q_cols, tokens), bf16),
-            shape((tokens, kv_cols), bf16),
-        ),
-        [held[apart] for apart in range(blocks)] + [turn_done],
+            shape((HEAD_SIZE, tokens * QUERIES_PER_KEY), bf16),
+        ),
+        (gathered, prob, inverse, attn, turn_done, *held),
+        in_vmem=range(4),
         scratch=(
-            pltpu.VMEM((tokens, packed_cols), bf16),
-            pltpu.VMEM((tokens, wide), f32),
-            pltpu.VMEM((tokens, wide), f32),
-            pltpu.VMEM((tokens, tokens * QUERIES_PER_KEY), bf16),
-            pltpu.VMEM((HEAD_SIZE, tokens * QUERIES_PER_KEY), bf16),
+            pltpu.VMEM((blocks, q_cols, rows), bf16),
             pltpu.VMEM((1, tokens * QUERIES_PER_KEY), f32),
-            pltpu.VMEM((tokens * QUERIES_PER_KEY, HEAD_SIZE), bf16),
-            pltpu.VMEM((HEAD_SIZE, tokens), bf16),
-            pltpu.VMEM((HEAD_SIZE, tokens), bf16),
             pltpu.VMEM((HEAD_SIZE, wide), f32),
             pltpu.VMEM((2 * rows, HEAD_SIZE), f32),
+            pltpu.VMEM((2 * rows, HEAD_SIZE), f32),
             pltpu.SemaphoreType.DMA((blocks,)),
         ),
-        flops=8 * tokens * tokens * q_cols,
-        moved=2 * tokens * packed_cols,
+        flops=3 * tokens * tokens * q_cols,
+        moved=2 * tokens * (packed_cols + q_cols + tokens * QUERIES_PER_KEY),
+    )
+    (dv,) = kernel_call(
+        functools.partial(value_grad_kernel, 2 * rows),
+        (shape((tokens, kv_cols), bf16),),
+        (prob, grad_t),
+        in_vmem=range(2),
+        flops=tokens * tokens * q_cols,
+        moved=2 * tokens * tokens * QUERIES_PER_KEY,
     )
     dx_got = swapped(dx_far, "seq", 1)
+    terms = {}
     aparts = tuple(range(groups - 1, -1, -1))
-    terms = kernel_call(
-        functools.partial(input_terms_kernel, aparts),
-        tuple(shape((model // groups, rows), bf16 if apart else f32) for apart in aparts),
-        (dx_own, dx_got, query_weight, key_matrix, value_matrix),
-        in_vmem=range(5),
-        scratch=(pltpu.VMEM((rows, 2 * (q_cols + 2 * kv_cols)), bf16),),
-        flops=4 * rows * model * (q_cols + 2 * kv_cols),
-        moved=4 * model * (q_cols + 2 * kv_cols),
-    )
-    arrived = [swapped(term, "head", apart) for apart, term in zip(aparts[:-1], terms[:-1])]
+    for chosen in (aparts[: groups // 2], aparts[groups // 2 :]):
+        made = kernel_call(
+            functools.partial(input_terms_kernel, chosen),
+            tuple(shape((model // groups, rows), bf16 if apart else f32) for apart in chosen),
+            (dx_own, dx_got, query_weight, key_matrix, value_matrix),
+            in_vmem=range(5),
+            scratch=(pltpu.VMEM((rows, 2 * (q_cols + 2 * kv_cols)), bf16),),
+            flops=2 * rows * model * (q_cols + 2 * kv_cols),
+            moved=2 * model * (q_cols + 2 * kv_cols),
+        )
+        terms.update(zip(chosen, made))
+    arrived = [swapped(terms[apart], "head", apart) for apart in aparts[:-1]]
     grad_wvalue, grad_woutput, weights_done = kernel_call(
         weight_grad_kernel,
         (
@@ -392,10 +450,10 @@
         flops=4 * tokens * (model // blocks) * (q_cols + kv_cols),
         moved=4 * (model // blocks) * (tokens + 2 * q_cols + 2 * kv_cols),
     )
-    grad_input = kernel_call(
+    (grad_input,) = kernel_call(
         sum_kernel,
-        shape((model // groups, rows), bf16),
-        (weights_done, terms[-1], *arrived),
+        (shape((model // groups, rows), bf16),),
+        (weights_done, terms[0], *arrived),
         in_vmem=range(1, groups + 1),
         moved=4 * groups * (model // groups) * rows,
     )

time: 82.2 us -> 121 us (1.47)
  Pallas kernels: 17.7 us -> 53.6 us
  waiting for transfers between devices: 43.7 us -> 23.1 us
  blocking collectives: 0 us -> 20.5 us
  local copies, waits for them, and re-layouts: 1.1 us -> 7.17 us
  starting transfers between devices: 18.7 us -> 15.5 us
    pallas_call x6 -> x10, Pallas kernels: 17.7 us -> 53.6 us  [kernel_call(): pl.pallas_call(body, out_shape=outs, in_specs=[vmem if place in in_vmem e...]
    ppermute x13, waiting for transfers between devices: 43.7 us -> 23.1 us  [swapped(): lax.ppermute(value, axis, [(place, place ^ apart) for place in range(coun...]
    all_to_all x0 -> x1, blocking collectives: none -> 20.5 us  [gathered_plan(): gathered = lax.all_to_all(sent, 'seq', 0, 0).reshape(tokens, packed_cols)]
    unnamed x14 -> x22, local copies, waits for them, and re-layouts: 1.1 us -> 7.17 us
    ppermute x13, starting transfers between devices: 14.5 us -> 11.2 us  [swapped(): lax.ppermute(value, axis, [(place, place ^ apart) for place in range(coun...]
  transfers between devices with their start and end apart: 14 -> 14, of which waited for: 7 -> 5; matrix products, arithmetic and copies ran while one was open for 0% -> 0% of each run, Pallas kernels for 14% -> 11%
where the time goes in v6:
time: 121 us
  Pallas kernels  53.6 us (44%)
  waiting for transfers between devices  23.1 us (19%)
  blocking collectives  20.5 us (17%)
  starting transfers between devices  15.5 us (13%)
  local copies, waits for them, and re-layouts  7.17 us (6%)
    pallas_call x10, Pallas kernels, kernel_call(): pl.pallas_call(body, out_shape=outs, in_specs=[vmem if place in in_vmem e...  53.6 us
    ppermute x13, waiting for transfers between devices, swapped(): lax.ppermute(value, axis, [(place, place ^ apart) for place in range(coun...  23.1 us
    all_to_all x1, blocking collectives, gathered_plan(): gathered = lax.all_to_all(sent, 'seq', 0, 0).reshape(tokens, packed_cols)  20.5 us
    ppermute x13, starting transfers between devices, swapped(): lax.ppermute(value, axis, [(place, place ^ apart) for place in range(coun...  11.2 us
    unnamed x22, local copies, waits for them, and re-layouts  7.17 us
    all_to_all x1, starting transfers between devices, gathered_plan(): turned = lax.all_to_all(turned, 'seq', 0, 0)  4.27 us
  transfers between devices with their start and end apart: 14, of which 5 were waited for; matrix products, arithmetic and copies ran while one was open for 0% of the time, Pallas kernels for 11%

profile of v6, /device:TPU:0, one launch (start us, length us, event | category | flops | bytes accessed | tf_op | source)
XLA Modules:
  0.0 120.6 jit_solution(9752745153988007875)
XLA Ops:
  0.6 33.7 %shard_map.112 = (bf16[8,128,512]{2,1,0:T(8,128)(2,1)}, f32[8,128]{1,0:T(8,128)}) custom-call(bf16[128,512]{1,0:T(8,128)(2,1)} %q_hbm.1, bf16[128,256]{1,0:T(8,128)(2,1)} %k_hbm.1, bf16[128,256]{1,0:T(8,128)(2,1)} %v_hbm.1), custom_call_target="tpu_custom_call" | custom-call | bytes 2097152 | tf_op jit(solution)/shard_map/pallas_call | solution.py:304
  34.3 20.5 %all_to_all.10 = bf16[8,128,512]{2,1,0:T(8,128)(2,1)S(1)} all-to-all(bf16[8,128,512]{2,1,0:T(8,128)(2,1)} %get-tuple-element.23), channel_id=1, replica_groups=mesh['seq'=8,'head'=4] {'seq'}, dimensions={0} | all-to-all | bytes 2097152 | tf_op jit(solution)/shard_map/all_to_all | solution.py:350
  54.9 3.7 %shard_map.113 = (bf16[1024,2048]{1,0:T(8,128)(2,1)S(1)}, f32[1,2048]{1,0:T(1,128)S(1)}, bf16[256,1024]{1,0:T(8,128)(2,1)}, f32[8,128]{1,0:T(8,128)S(1)}) custom-call(bf16[1024,512]{1,0:T(8,128)(2,1)S(1)} %bitcast.3), custom_call_target="tpu_custom_call" | custom-call | flops 805306368 | bytes 5767168 | tf_op jit(solution)/shard_map/pallas_call | solution.py:304
  58.6 2.0 %copy-done = bf16[1024,2048]{1,0:T(8,128)(2,1)} copy-done((bf16[1024,2048]{1,0:T(8,128)(2,1)}, bf16[1024,2048]{1,0:T(8,128)(2,1)S(1)}, u32[]{:S(2)}) %copy-start) | copy-done | bytes 4194328
  60.5 1.8 %shard_map.114 = (bf16[8,2,288,128]{3,2,1,0:T(8,128)(2,1)}, f32[8,128]{1,0:T(8,128)S(1)}) custom-call(bf16[128,2304]{1,0:T(8,128)(2,1)S(1)} %copy-done.9, bf16[128,2304]{1,0:T(8,128)(2,1)S(1)} %copy-done.8, f32[8,128]{1,0:T(8,128)S(1)} %get-tuple-element.24._), custom_call_target="tpu_custom_call" | custom-call | bytes 2359296 | tf_op jit(solution)/shard_map/pallas_call | solution.py:304
  62.3 4.3 %all-to-all-start.1 = ((bf16[8,2,288,128]{3,2,1,0:T(8,128)(2,1)}), bf16[8,2,288,128]{3,2,1,0:T(8,128)(2,1)}, u32[]{:S(2)}, u32[]{:S(2)}) async-start(bf16[8,2,288,128]{3,2,1,0:T(8,128)(2,1)} %get-tuple-element.25), calls=%async_computation.1 | async-start | bytes 2359296 | tf_op jit(solution)/shard_map/all_to_all | solution.py:396
  67.0 3.6 %shard_map.115 = (bf16[256,128]{1,0:T(8,128)(2,1)}, bf16[256,128]{1,0:T(8,128)(2,1)}) custom-call(bf16[128,2304]{1,0:T(8,128)(2,1)} %cot_hbm.3, bf16[512,2304]{1,0:T(8,128)(2,1)} %weight_hbm.1, f32[8,128]{1,0:T(8,128)} %get-tuple-element.30._), custom_call_target="tpu_custom_call" | custom-call | flops 301989888 | bytes 2949120 | tf_op jit(solution)/shard_map/pallas_call | solution.py:304
  70.8 1.8 %collective-permute-start.2 = (bf16[256,128]{1,0:T(8,128)(2,1)}, bf16[256,128]{1,0:T(8,128)(2,1)S(1)}, u32[]{:S(2)}, u32[]{:S(2)}) collective-permute-start(bf16[256,128]{1,0:T(8,128)(2,1)} %get-tuple-element.31.refs_0_), channel_id=1, source_target_pairs={{0,8},{4,12},{8,0},{12,4},{16,24},{20,28},{24,16},{28,20},{1,9},{5... | collective-permute-start | bytes 196616 | tf_op jit(solution)/shard_map/ppermute | solution.py:317
  72.7 1.5 %collective-permute-start.4 = (bf16[256,128]{1,0:T(8,128)(2,1)}, bf16[256,128]{1,0:T(8,128)(2,1)S(1)}, u32[]{:S(2)}, u32[]{:S(2)}) collective-permute-start(bf16[256,128]{1,0:T(8,128)(2,1)} %get-tuple-element.31.refs_0_), channel_id=1, source_target_pairs={{0,16},{4,20},{8,24},{12,28},{16,0},{20,4},{24,8},{28,12},{1,17},{... | collective-permute-start | bytes 196616 | tf_op jit(solution)/shard_map/ppermute | solution.py:317
  74.5 9.8 %collective-permute-done.2.refs_2_ = bf16[256,128]{1,0:T(8,128)(2,1)S(1)} collective-permute-done((bf16[256,128]{1,0:T(8,128)(2,1)}, bf16[256,128]{1,0:T(8,128)(2,1)S(1)}, u32[]{:S(2)}, u32[]{:S(2)}) %collective-permute-start.2) | collective-permute-done | bytes 65568 | tf_op jit(solution)/shard_map/ppermute | solution.py:317
  84.3 1.5 %collective-permute-start.6 = (bf16[256,128]{1,0:T(8,128)(2,1)}, bf16[256,128]{1,0:T(8,128)(2,1)S(1)}, u32[]{:S(2)}, u32[]{:S(2)}) collective-permute-start(bf16[256,128]{1,0:T(8,128)(2,1)} %get-tuple-element.31.refs_0_), channel_id=1, source_target_pairs={{0,24},{4,28},{8,16},{12,20},{16,8},{20,12},{24,0},{28,4},{1,25},{... | collective-permute-start | bytes 196616 | tf_op jit(solution)/shard_map/ppermute | solution.py:317
  86.1 3.5 %collective-permute-done.6.refs_6_ = bf16[256,128]{1,0:T(8,128)(2,1)S(1)} collective-permute-done((bf16[256,128]{1,0:T(8,128)(2,1)}, bf16[256,128]{1,0:T(8,128)(2,1)S(1)}, u32[]{:S(2)}, u32[]{:S(2)}) %collective-permute-start.6) | collective-permute-done | bytes 65568 | tf_op jit(solution)/shard_map/ppermute | solution.py:317
  89.7 1.4 %collective-permute-done.7.refs_7_ = bf16[256,128]{1,0:T(8,128)(2,1)S(1)} collective-permute-done((bf16[256,128]{1,0:T(8,128)(2,1)}, bf16[256,128]{1,0:T(8,128)(2,1)S(1)}, u32[]{:S(2)}, u32[]{:S(2)}) %collective-permute-start.7) | collective-permute-done | bytes 65568 | tf_op jit(solution)/shard_map/ppermute | solution.py:317
  91.1 2.2 %copy-done.1 = bf16[1024,2048]{1,0:T(8,128)(2,1)S(1)} copy-done((bf16[1024,2048]{1,0:T(8,128)(2,1)S(1)}, bf16[1024,2048]{1,0:T(8,128)(2,1)}, u32[]{:S(2)}) %copy-start.1) | copy-done | bytes 4194328
  93.3 1.2 %copy-done.7 = bf16[8,128,512]{2,1,0:T(8,128)(2,1)S(1)} copy-done((bf16[8,128,512]{2,1,0:T(8,128)(2,1)S(1)}, bf16[8,128,512]{2,1,0:T(8,128)(2,1)}, u32[]{:S(2)}) %copy-start.7) | copy-done | bytes 1048600
  94.5 0.8 copy-done.10
  95.3 4.5 %shard_map.116 = (bf16[128,512]{1,0:T(8,128)(2,1)S(1)}, bf16[128,512]{1,0:T(8,128)(2,1)S(1)}, bf16[128,2048]{1,0:T(8,128)(2,1)S(1)}) custom-call(bf16[1024,512]{1,0:T(8,128)(2,1)S(1)} %bitcast.4, bf16[1024,2048]{1,0:T(8,128)(2,1)S(1)} %copy-done.1, f32[1,2048]{1,0:T(1,128)S(1)} %get-tuple-element.28.inverse_ref, ...), custom_call_target="tpu_custom_call" | custom-call | flops 805306368 | bytes 5767168 | tf_op jit(solution)/shard_map/pallas_call | solution.py:304
  100.0 0.8 shard_map.117.dv_ref
  102.3 0.8 shard_map.120
  103.1 3.7 %collective-permute-start.10 = (bf16[576,128]{1,0:T(8,128)(2,1)S(1)}, bf16[576,128]{1,0:T(8,128)(2,1)S(1)}, u32[]{:S(2)}, u32[]{:S(2)}) collective-permute-start(bf16[576,128]{1,0:T(8,128)(2,1)S(1)} %get-tuple-element.38), channel_id=1, source_target_pairs={{0,3},{1,2},{2,1},{3,0},{4,7},{5,6},{6,5},{7,4},{8,11},{9,10},{10,... | collective-permute-start | bytes 442376 | tf_op jit(solution)/shard_map/ppermute | solution.py:317
  106.8 0.8 shard_map.119
  107.6 0.9 collective-permute-start.12
  108.5 3.1 %shard_map.118 = (f32[288,256]{1,0:T(8,128)}, f32[288,512]{1,0:T(8,128)}, f32[8,128]{1,0:T(8,128)S(1)}) custom-call(bf16[8,2,288,128]{3,2,1,0:T(8,128)(2,1)} %all-to-all-done.1.turned_ref, bf16[256,1024]{1,0:T(8,128)(2,1)} %get-tuple-element.26.attn_ref, bf16[256,1024]{1,0:T(8,128)(2,1)S(1)} %collective-permute-done.far_attn_ref, ...), custom_call_target="tpu_custom_call" | custom-call | flops 452984832 | bytes 2064384 | tf_op jit(solution)/shard_map/pallas_call | solution.py:304
  111.7 8.2 %collective-permute-done.11.refs_1_ = bf16[576,128]{1,0:T(8,128)(2,1)S(1)} collective-permute-done((bf16[576,128]{1,0:T(8,128)(2,1)S(1)}, bf16[576,128]{1,0:T(8,128)(2,1)S(1)}, u32[]{:S(2)}, u32[]{:S(2)}) %collective-permute-start.11) | collective-permute-done | bytes 147488 | tf_op jit(solution)/shard_map/ppermute | solution.py:317
  (37 shorter events, 3.7 us)
Async XLA Ops:
  54.9 3.7 %copy-start.6 = (bf16[8,128,512]{2,1,0:T(8,128)(2,1)}, bf16[8,128,512]{2,1,0:T(8,128)(2,1)S(1)}, u32[]{:S(2)}) copy-start(bf16[8,128,512]{2,1,0:T(8,128)(2,1)S(1)} %all_to_all.10) | copy-start | bytes 3145732
  54.9 5.7 %copy-start.8 = (bf16[128,2304]{1,0:T(8,128)(2,1)S(1)}, bf16[128,2304]{1,0:T(8,128)(2,1)}, u32[]{:S(2)}) copy-start(bf16[128,2304]{1,0:T(8,128)(2,1)} %cot_hbm.3) | copy-start | bytes 1769476
  54.9 5.7 %copy-start.9 = (bf16[128,2304]{1,0:T(8,128)(2,1)S(1)}, bf16[128,2304]{1,0:T(8,128)(2,1)}, u32[]{:S(2)}) copy-start(bf16[128,2304]{1,0:T(8,128)(2,1)} %normed_hbm.1) | copy-start | bytes 1769476
  58.6 2.0 %copy-start = (bf16[1024,2048]{1,0:T(8,128)(2,1)}, bf16[1024,2048]{1,0:T(8,128)(2,1)S(1)}, u32[]{:S(2)}) copy-start(bf16[1024,2048]{1,0:T(8,128)(2,1)S(1)} %get-tuple-element.27.prob_ref) | copy-start | bytes 12582916
  62.3 46.2 %all-to-all-start.1 = ((bf16[8,2,288,128]{3,2,1,0:T(8,128)(2,1)}), bf16[8,2,288,128]{3,2,1,0:T(8,128)(2,1)}, u32[]{:S(2)}, u32[]{:S(2)}) async-start(bf16[8,2,288,128]{3,2,1,0:T(8,128)(2,1)} %get-tuple-element.25), calls=%async_computation.1 | async-start | bytes 2359296 | tf_op jit(solution)/shard_map/all_to_all | solution.py:396
  66.6 41.9 %collective-permute-start = (bf16[256,1024]{1,0:T(8,128)(2,1)}, bf16[256,1024]{1,0:T(8,128)(2,1)S(1)}, u32[]{:S(2)}, u32[]{:S(2)}) collective-permute-start(bf16[256,1024]{1,0:T(8,128)(2,1)} %get-tuple-element.26.attn_ref), channel_id=1, source_target_pairs={{0,4},{4,0},{8,12},{12,8},{16,20},{20,16},{24,28},{28,24},{1,5},{5... | collective-permute-start | bytes 1572872 | tf_op jit(solution)/shard_map/ppermute | solution.py:317
  70.6 3.6 %collective-permute-start.1 = (bf16[256,128]{1,0:T(8,128)(2,1)}, bf16[256,128]{1,0:T(8,128)(2,1)S(1)}, u32[]{:S(2)}, u32[]{:S(2)}) collective-permute-start(bf16[256,128]{1,0:T(8,128)(2,1)} %get-tuple-element.32), channel_id=1, source_target_pairs={{0,4},{4,0},{8,12},{12,8},{16,20},{20,16},{24,28},{28,24},{1,5},{5... | collective-permute-start | bytes 196616 | tf_op jit(solution)/shard_map/ppermute | solution.py:317
  70.8 13.4 %collective-permute-start.2 = (bf16[256,128]{1,0:T(8,128)(2,1)}, bf16[256,128]{1,0:T(8,128)(2,1)S(1)}, u32[]{:S(2)}, u32[]{:S(2)}) collective-permute-start(bf16[256,128]{1,0:T(8,128)(2,1)} %get-tuple-element.31.refs_0_), channel_id=1, source_target_pairs={{0,8},{4,12},{8,0},{12,4},{16,24},{20,28},{24,16},{28,20},{1,9},{5... | collective-permute-start | bytes 196616 | tf_op jit(solution)/shard_map/ppermute | solution.py:317
  72.7 13.1 %collective-permute-start.3 = (bf16[256,128]{1,0:T(8,128)(2,1)}, bf16[256,128]{1,0:T(8,128)(2,1)S(1)}, u32[]{:S(2)}, u32[]{:S(2)}) collective-permute-start(bf16[256,128]{1,0:T(8,128)(2,1)} %get-tuple-element.32), channel_id=1, source_target_pairs={{0,12},{4,8},{8,4},{12,0},{16,28},{20,24},{24,20},{28,16},{1,13},{... | collective-permute-start | bytes 196616 | tf_op jit(solution)/shard_map/ppermute | solution.py:317
  72.7 13.4 %collective-permute-start.4 = (bf16[256,128]{1,0:T(8,128)(2,1)}, bf16[256,128]{1,0:T(8,128)(2,1)S(1)}, u32[]{:S(2)}, u32[]{:S(2)}) collective-permute-start(bf16[256,128]{1,0:T(8,128)(2,1)} %get-tuple-element.31.refs_0_), channel_id=1, source_target_pairs={{0,16},{4,20},{8,24},{12,28},{16,0},{20,4},{24,8},{28,12},{1,17},{... | collective-permute-start | bytes 196616 | tf_op jit(solution)/shard_map/ppermute | solution.py:317
  74.2 11.9 %collective-permute-start.5 = (bf16[256,128]{1,0:T(8,128)(2,1)}, bf16[256,128]{1,0:T(8,128)(2,1)S(1)}, u32[]{:S(2)}, u32[]{:S(2)}) collective-permute-start(bf16[256,128]{1,0:T(8,128)(2,1)} %get-tuple-element.32), channel_id=1, source_target_pairs={{0,20},{4,16},{8,28},{12,24},{16,4},{20,0},{24,12},{28,8},{1,21},{... | collective-permute-start | bytes 196616 | tf_op jit(solution)/shard_map/ppermute | solution.py:317
  84.3 5.4 %collective-permute-start.6 = (bf16[256,128]{1,0:T(8,128)(2,1)}, bf16[256,128]{1,0:T(8,128)(2,1)S(1)}, u32[]{:S(2)}, u32[]{:S(2)}) collective-permute-start(bf16[256,128]{1,0:T(8,128)(2,1)} %get-tuple-element.31.refs_0_), channel_id=1, source_target_pairs={{0,24},{4,28},{8,16},{12,20},{16,8},{20,12},{24,0},{28,4},{1,25},{... | collective-permute-start | bytes 196616 | tf_op jit(solution)/shard_map/ppermute | solution.py:317
  85.8 5.3 %collective-permute-start.7 = (bf16[256,128]{1,0:T(8,128)(2,1)}, bf16[256,128]{1,0:T(8,128)(2,1)S(1)}, u32[]{:S(2)}, u32[]{:S(2)}) collective-permute-start(bf16[256,128]{1,0:T(8,128)(2,1)} %get-tuple-element.32), channel_id=1, source_target_pairs={{0,28},{4,24},{8,20},{12,16},{16,12},{20,8},{24,4},{28,0},{1,29},{... | collective-permute-start | bytes 196616 | tf_op jit(solution)/shard_map/ppermute | solution.py:317
  91.1 2.2 %copy-start.1 = (bf16[1024,2048]{1,0:T(8,128)(2,1)S(1)}, bf16[1024,2048]{1,0:T(8,128)(2,1)}, u32[]{:S(2)}) copy-start(bf16[1024,2048]{1,0:T(8,128)(2,1)} %copy-done) | copy-start | bytes 12582916
  93.3 1.2 %copy-start.7 = (bf16[8,128,512]{2,1,0:T(8,128)(2,1)S(1)}, bf16[8,128,512]{2,1,0:T(8,128)(2,1)}, u32[]{:S(2)}) copy-start(bf16[8,128,512]{2,1,0:T(8,128)(2,1)} %copy-done.6) | copy-start | bytes 3145732
  95.3 4.6 %copy-start.2 = (bf16[1024,2048]{1,0:T(8,128)(2,1)S(1)}, bf16[1024,2048]{1,0:T(8,128)(2,1)}, u32[]{:S(2)}) copy-start(bf16[1024,2048]{1,0:T(8,128)(2,1)} %copy-done) | copy-start | bytes 12582916
  99.9 1.5 %collective-permute-start.9 = (bf16[128,512]{1,0:T(8,128)(2,1)S(1)}, bf16[128,512]{1,0:T(8,128)(2,1)S(1)}, u32[]{:S(2)}, u32[]{:S(2)}) collective-permute-start(bf16[128,512]{1,0:T(8,128)(2,1)S(1)} %get-tuple-element.36), channel_id=1, source_target_pairs={{0,4},{4,0},{8,12},{12,8},{16,20},{20,16},{24,28},{28,24},{1,5},{5... | collective-permute-start | bytes 393224 | tf_op jit(solution)/shard_map/ppermute | solution.py:317
  100.0 1.7 %copy-start.3 = (bf16[2304,512]{1,0:T(8,128)(2,1)S(1)}, bf16[2304,512]{1,0:T(8,128)(2,1)}, u32[]{:S(2)}) copy-start(bf16[2304,512]{1,0:T(8,128)(2,1)} %wq_ref.3) | copy-start | bytes 7077892
  100.0 2.0 %copy-start.4 = (bf16[2304,256]{1,0:T(8,128)(2,1)S(1)}, bf16[2304,256]{1,0:T(8,128)(2,1)}, u32[]{:S(2)}) copy-start(bf16[2304,256]{1,0:T(8,128)(2,1)} %wk_ref.3) | copy-start | bytes 3538948
  100.0 2.3 %copy-start.5 = (bf16[2304,256]{1,0:T(8,128)(2,1)S(1)}, bf16[2304,256]{1,0:T(8,128)(2,1)}, u32[]{:S(2)}) copy-start(bf16[2304,256]{1,0:T(8,128)(2,1)} %wv_ref.3) | copy-start | bytes 3538948
  100.8 7.6 %collective-permute-start.8 = (bf16[1024,128]{1,0:T(8,128)(2,1)S(1)}, bf16[1024,128]{1,0:T(8,128)(2,1)S(1)}, u32[]{:S(2)}, u32[]{:S(2)}) collective-permute-start(bf16[1024,128]{1,0:T(8,128)(2,1)S(1)} %shard_map.117.dv_ref), channel_id=1, source_target_pairs={{0,4},{4,0},{8,12},{12,8},{16,20},{20,16},{24,28},{28,24},{1,5},{5... | collective-permute-start | bytes 786440 | tf_op jit(solution)/shard_map/ppermute | solution.py:317
  103.1 8.6 %collective-permute-start.10 = (bf16[576,128]{1,0:T(8,128)(2,1)S(1)}, bf16[576,128]{1,0:T(8,128)(2,1)S(1)}, u32[]{:S(2)}, u32[]{:S(2)}) collective-permute-start(bf16[576,128]{1,0:T(8,128)(2,1)S(1)} %get-tuple-element.38), channel_id=1, source_target_pairs={{0,3},{1,2},{2,1},{3,0},{4,7},{5,6},{6,5},{7,4},{8,11},{9,10},{10,... | collective-permute-start | bytes 442376 | tf_op jit(solution)/shard_map/ppermute | solution.py:317
  106.8 13.1 %collective-permute-start.11 = (bf16[576,128]{1,0:T(8,128)(2,1)S(1)}, bf16[576,128]{1,0:T(8,128)(2,1)S(1)}, u32[]{:S(2)}, u32[]{:S(2)}) collective-permute-start(bf16[576,128]{1,0:T(8,128)(2,1)S(1)} %get-tuple-element.39), channel_id=1, source_target_pairs={{0,2},{1,3},{2,0},{3,1},{4,6},{5,7},{6,4},{7,5},{8,10},{9,11},{10,... | collective-permute-start | bytes 442376 | tf_op jit(solution)/shard_map/ppermute | solution.py:317
  107.6 12.3 %collective-permute-start.12 = (bf16[576,128]{1,0:T(8,128)(2,1)S(1)}, bf16[576,128]{1,0:T(8,128)(2,1)S(1)}, u32[]{:S(2)}, u32[]{:S(2)}) collective-permute-start(bf16[576,128]{1,0:T(8,128)(2,1)S(1)} %get-tuple-element.40), channel_id=1, source_target_pairs={{0,1},{1,0},{2,3},{3,2},{4,5},{5,4},{6,7},{7,6},{8,9},{9,8},{10,11... | collective-permute-start | bytes 442376 | tf_op jit(solution)/shard_map/ppermute | solution.py:317
  (1 other events, 0.8 us)

commit v7 on v4

--- a/solution.py
+++ b/solution.py
@@ -95,11 +95,12 @@
 
 
 def attention_kernel(blocks, *refs):
-    attention_body(refs[:blocks], *refs[blocks + 1 :])
+    attention_body(refs[:blocks], *refs[blocks:])
 
 
 def attention_body(
     block_refs,
+    _,
     dx_own_ref,
     dx_far_ref,
     attn_ref,
@@ -120,14 +121,9 @@
     me = lax.axis_index("seq")
     core, chip = me % 2, me // 2
     rows = dx_own_ref.shape[0]
-    arrivals = []
     for apart, source in enumerate(block_refs):
-        arrivals.append(
-            pltpu.make_async_copy(source, gathered_ref.at[at(me ^ apart, rows)], sem.at[apart])
-        )
-        arrivals[-1].start()
-    for copy in arrivals:
-        copy.wait()
+        place = me ^ apart
+        pltpu.make_async_copy(source, gathered_ref.at[at(place, rows)], sem.at[place]).start()
     tokens = gathered_ref.shape[0]
     size = 2 * rows
     steps = tokens // size
@@ -136,8 +132,6 @@
     key_cols = slice(heads * HEAD_SIZE, (heads + 1) * HEAD_SIZE)
     value_cols = slice((heads + 1) * HEAD_SIZE, (heads + 2) * HEAD_SIZE)
     grad_base = (heads + 2) * HEAD_SIZE
-    value_t_ref[...] = gathered_ref[:, value_cols].T
-    key_t_ref[...] = gathered_ref[:, key_cols].T
     key_place = lax.broadcasted_iota(jnp.int32, (size, wide), 0)
     query_place = lax.broadcasted_iota(jnp.int32, (size, wide), 1) % size
     allowed = key_place <= query_place
@@ -147,6 +141,12 @@
         own = slice(step * size, span)
         lanes = slice(step * wide, (step + 1) * wide)
         score_ref = score_odd_ref if step % 2 else score_even_ref
+        for block in (2 * step, 2 * step + 1):
+            pltpu.make_async_copy(
+                block_refs[0], gathered_ref.at[pl.ds(block * rows, rows)], sem.at[block]
+            ).wait()
+        value_t_ref[:, own] = gathered_ref[own, value_cols].T
+        key_t_ref[:, own] = gathered_ref[own, key_cols].T
         queries = jnp.concatenate(
             [gathered_ref[own, h * HEAD_SIZE : (h + 1) * HEAD_SIZE] for h in range(heads)], axis=0
         )
@@ -273,7 +273,7 @@
     refs[-1][...] = total.astype(jnp.bfloat16)
 
 
-def kernel_call(body, outs, operands, in_vmem=(), scratch=(), flops=0, moved=0, room=32):
+def kernel_call(body, outs, operands, in_vmem=(), scratch=(), flops=0, moved=0, room=16):
     vmem = pl.BlockSpec(memory_space=pltpu.VMEM)
     hbm = pl.BlockSpec(memory_space=pltpu.HBM)
     return pl.pallas_call(
@@ -327,12 +327,20 @@
         room=63,
     )
     held = {0: same}
-    for apart in range(blocks - 1, 0, -1):
-        held[apart] = swapped(other if apart % 2 else same, "seq", apart)
+    for apart in range(2, blocks):
+        lowest, highest = 2, 1 << (apart.bit_length() - 1)
+        while not apart & lowest:
+            lowest *= 2
+        through = lowest if apart % 2 else highest
+        if lowest == highest:
+            held[apart] = swapped(other if apart % 2 else same, "seq", apart)
+        else:
+            held[apart] = swapped(held[apart ^ through], "seq", through)
+    held[1] = swapped(other, "seq", 1)
     turned, turn_done = kernel_call(
         functools.partial(turn_kernel, blocks),
         (shape((blocks, 2, model // blocks, rows), bf16), shape((8, HEAD_SIZE), f32)),
-        (normed_input, out_cotangent, held[1], held[2]),
+        (normed_input, out_cotangent, held[3], held[4]),
         scratch=(
             pltpu.VMEM(normed_input.shape, bf16),
             pltpu.VMEM(out_cotangent.shape, bf16),
@@ -369,16 +377,19 @@
     )
     dx_got = swapped(dx_far, "seq", 1)
     aparts = tuple(range(groups - 1, -1, -1))
-    terms = kernel_call(
-        functools.partial(input_terms_kernel, aparts),
-        tuple(shape((model // groups, rows), bf16 if apart else f32) for apart in aparts),
-        (dx_own, dx_got, query_weight, key_matrix, value_matrix),
-        in_vmem=range(5),
-        scratch=(pltpu.VMEM((rows, 2 * (q_cols + 2 * kv_cols)), bf16),),
-        flops=4 * rows * model * (q_cols + 2 * kv_cols),
-        moved=4 * model * (q_cols + 2 * kv_cols),
-    )
-    arrived = [swapped(term, "head", apart) for apart, term in zip(aparts[:-1], terms[:-1])]
+    terms = {}
+    for chosen in (aparts[: groups // 2], aparts[groups // 2 :]):
+        made = kernel_call(
+            functools.partial(input_terms_kernel, chosen),
+            tuple(shape((model // groups, rows), bf16 if apart else f32) for apart in chosen),
+            (dx_own, dx_got, query_weight, key_matrix, value_matrix),
+            in_vmem=range(5),
+            scratch=(pltpu.VMEM((rows, 2 * (q_cols + 2 * kv_cols)), bf16),),
+            flops=2 * rows * model * (q_cols + 2 * kv_cols),
+            moved=2 * model * (q_cols + 2 * kv_cols),
+        )
+        terms.update(zip(chosen, made))
+    arrived = [swapped(terms[apart], "head", apart) for apart in aparts[:-1]]
     grad_wvalue, grad_woutput, weights_done = kernel_call(
         weight_grad_kernel,
         (
@@ -395,7 +406,7 @@
     grad_input = kernel_call(
         sum_kernel,
         shape((model // groups, rows), bf16),
-        (weights_done, terms[-1], *arrived),
+        (weights_done, terms[0], *arrived),
         in_vmem=range(1, groups + 1),
         moved=4 * groups * (model // groups) * rows,
     )

time: 82.2 us -> 71 us (0.86)
  waiting for transfers between devices: 43.7 us -> 32.8 us
  starting transfers between devices: 18.7 us -> 16.9 us
  Pallas kernels: 17.7 us -> 19.2 us
    ppermute x13, waiting for transfers between devices: 43.7 us -> 32.8 us  [swapped(): lax.ppermute(value, axis, [(place, place ^ apart) for place in range(coun...]
    pallas_call x6 -> x7, Pallas kernels: 17.7 us -> 19.2 us  [kernel_call(): pl.pallas_call(body, out_shape=outs, in_specs=[vmem if place in in_vmem e...]
    ppermute x13, starting transfers between devices: 14.5 us -> 13.2 us  [swapped(): lax.ppermute(value, axis, [(place, place ^ apart) for place in range(coun...]
  transfers between devices with their start and end apart: 14 -> 14, of which waited for: 7 -> 7; matrix products, arithmetic and copies ran while one was open for 0% -> 0% of each run, Pallas kernels for 14% -> 21%
where the time goes in v7:
time: 71 us; the launch traced here: 70.8 us
  waiting for transfers between devices  32.8 us (46%)
  Pallas kernels  19.2 us (27%)
  starting transfers between devices  16.9 us (24%)
  local copies, waits for them, and re-layouts  1.09 us (2%)
  between operations  0.73 us (1%)
    ppermute x13, waiting for transfers between devices, swapped(): lax.ppermute(value, axis, [(place, place ^ apart) for place in range(coun...  32.8 us
    pallas_call x7, Pallas kernels, kernel_call(): pl.pallas_call(body, out_shape=outs, in_specs=[vmem if place in in_vmem e...  19.2 us
    ppermute x13, starting transfers between devices, swapped(): lax.ppermute(value, axis, [(place, place ^ apart) for place in range(coun...  13.2 us
    all_to_all x1, starting transfers between devices, gathered_plan(): turned = lax.all_to_all(turned, 'seq', 0, 0)  3.71 us
  transfers between devices with their start and end apart: 14, of which 7 were waited for; matrix products, arithmetic and copies ran while one was open for 0% of the time, Pallas kernels for 21%

profile of v7, /device:TPU:0, one launch (start us, length us, event | category | flops | bytes accessed | tf_op | source)
XLA Modules:
  0.0 70.8 jit_solution(7794149816885033349)
XLA Ops:
  0.6 3.8 %shard_map.112 = (bf16[128,768]{1,0:T(8,128)(2,1)}, bf16[128,768]{1,0:T(8,128)(2,1)}) custom-call(bf16[128,2304]{1,0:T(8,128)(2,1)} %cot_hbm.3, bf16[512,2304]{1,0:T(8,128)(2,1)} %weight_hbm.1, bf16[128,512]{1,0:T(8,128)(2,1)} %q_hbm.1, bf16[128,256]{1,0:T(8,128)(2,1)} %k_hbm.1, bf16[128,256]{1,0:T(8,128)(2,1)} %v_hbm.1), custom_call_target="tpu_custom_call" | custom-call | flops 301989888 | bytes 2949120 | tf_op jit(solution)/shard_map/pallas_call | solution.py:279
  4.5 2.4 %collective-permute-start = (bf16[128,768]{1,0:T(8,128)(2,1)}, bf16[128,768]{1,0:T(8,128)(2,1)S(1)}, u32[]{:S(2)}, u32[]{:S(2)}) collective-permute-start(bf16[128,768]{1,0:T(8,128)(2,1)} %get-tuple-element.18), channel_id=1, source_target_pairs={{0,12},{4,8},{8,4},{12,0},{16,28},{20,24},{24,20},{28,16},{1,13},{... | collective-permute-start | bytes 589832 | tf_op jit(solution)/shard_map/ppermute | solution.py:292
  6.9 1.5 %collective-permute-start.1 = (bf16[128,768]{1,0:T(8,128)(2,1)}, bf16[128,768]{1,0:T(8,128)(2,1)S(1)}, u32[]{:S(2)}, u32[]{:S(2)}) collective-permute-start(bf16[128,768]{1,0:T(8,128)(2,1)} %get-tuple-element.19.refs_0_), channel_id=1, source_target_pairs={{0,16},{4,20},{8,24},{12,28},{16,0},{20,4},{24,8},{28,12},{1,17},{... | collective-permute-start | bytes 589832 | tf_op jit(solution)/shard_map/ppermute | solution.py:292
  8.5 0.6 collective-permute-start.3
  9.1 3.4 %collective-permute-done._.refs_3_ = bf16[128,768]{1,0:T(8,128)(2,1)S(1)} collective-permute-done((bf16[128,768]{1,0:T(8,128)(2,1)}, bf16[128,768]{1,0:T(8,128)(2,1)S(1)}, u32[]{:S(2)}, u32[]{:S(2)}) %collective-permute-start) | collective-permute-done | bytes 196640 | tf_op jit(solution)/shard_map/ppermute | solution.py:292
  12.6 2.4 %collective-permute-done.1.__.refs_4_ = bf16[128,768]{1,0:T(8,128)(2,1)S(1)} collective-permute-done((bf16[128,768]{1,0:T(8,128)(2,1)}, bf16[128,768]{1,0:T(8,128)(2,1)S(1)}, u32[]{:S(2)}, u32[]{:S(2)}) %collective-permute-start.1) | collective-permute-done | bytes 196640 | tf_op jit(solution)/shard_map/ppermute | solution.py:292
  14.9 1.1 %copy-done.4 = bf16[128,2304]{1,0:T(8,128)(2,1)S(1)} copy-done((bf16[128,2304]{1,0:T(8,128)(2,1)S(1)}, bf16[128,2304]{1,0:T(8,128)(2,1)}, u32[]{:S(2)}) %copy-start.4) | copy-done | bytes 589848
  16.0 1.8 %shard_map.113 = (bf16[8,2,288,128]{3,2,1,0:T(8,128)(2,1)}, f32[8,128]{1,0:T(8,128)S(1)}) custom-call(bf16[128,2304]{1,0:T(8,128)(2,1)S(1)} %copy-done.4, bf16[128,2304]{1,0:T(8,128)(2,1)S(1)} %copy-done.3, bf16[128,768]{1,0:T(8,128)(2,1)S(1)} %collective-permute-done._.refs_3_, bf16[128,768]{1,0:T(8,128)(2,1)S(1)} %collective-permute-done.1.__.refs_4_), custom_call_target="tpu_custom_call" | custom-call | bytes 2359296 | tf_op jit(solution)/shard_map/pallas_call | solution.py:279
  17.8 3.7 %all-to-all-start = ((bf16[8,2,288,128]{3,2,1,0:T(8,128)(2,1)}), bf16[8,2,288,128]{3,2,1,0:T(8,128)(2,1)S(1)}, u32[]{:S(2)}, u32[]{:S(2)}) async-start(bf16[8,2,288,128]{3,2,1,0:T(8,128)(2,1)} %get-tuple-element.20), calls=%async_computation | async-start | bytes 2359296 | tf_op jit(solution)/shard_map/all_to_all | solution.py:351
  21.5 0.4 collective-permute-start.2
  21.9 1.7 %collective-permute-start.5 = (bf16[128,768]{1,0:T(8,128)(2,1)S(1)}, bf16[128,768]{1,0:T(8,128)(2,1)S(1)}, u32[]{:S(2)}, u32[]{:S(2)}) collective-permute-start(bf16[128,768]{1,0:T(8,128)(2,1)S(1)} %collective-permute-done.3.refs_2_), channel_id=1, source_target_pairs={{0,16},{4,20},{8,24},{12,28},{16,0},{20,4},{24,8},{28,12},{1,17},{... | collective-permute-start | bytes 589832 | tf_op jit(solution)/shard_map/ppermute | solution.py:292
  23.6 1.5 %collective-permute-start.6 = (bf16[128,768]{1,0:T(8,128)(2,1)S(1)}, bf16[128,768]{1,0:T(8,128)(2,1)S(1)}, u32[]{:S(2)}, u32[]{:S(2)}) collective-permute-start(bf16[128,768]{1,0:T(8,128)(2,1)S(1)} %collective-permute-done.4.refs_5_), channel_id=1, source_target_pairs={{0,8},{4,12},{8,0},{12,4},{16,24},{20,28},{24,16},{28,20},{1,9},{5... | collective-permute-start | bytes 589832 | tf_op jit(solution)/shard_map/ppermute | solution.py:292
  25.1 16.4 %collective-permute-done.5.refs_6_ = bf16[128,768]{1,0:T(8,128)(2,1)S(1)} collective-permute-done((bf16[128,768]{1,0:T(8,128)(2,1)S(1)}, bf16[128,768]{1,0:T(8,128)(2,1)S(1)}, u32[]{:S(2)}, u32[]{:S(2)}) %collective-permute-start.5) | collective-permute-done | bytes 196640 | tf_op jit(solution)/shard_map/ppermute | solution.py:292
  41.6 8.2 %shard_map.114 = (bf16[128,512]{1,0:T(8,128)(2,1)S(1)}, bf16[128,512]{1,0:T(8,128)(2,1)S(1)}, bf16[256,1024]{1,0:T(8,128)(2,1)S(1)}, bf16[1024,128]{1,0:T(8,128)(2,1)S(1)}) custom-call(bf16[128,768]{1,0:T(8,128)(2,1)S(1)} %copy-done.5, bf16[128,768]{1,0:T(8,128)(2,1)S(1)} %collective-permute-done.2.refs_1_, ...), custom_call_target="tpu_custom_call" | custom-call | flops 2147483648 | bytes 1572864 | tf_op jit(solution)/shard_map/pallas_call | solution.py:279
  49.9 0.5 collective-permute-start.9
  50.4 1.5 %collective-permute-done.9.far_ref = bf16[128,512]{1,0:T(8,128)(2,1)S(1)} collective-permute-done((bf16[128,512]{1,0:T(8,128)(2,1)S(1)}, bf16[128,512]{1,0:T(8,128)(2,1)S(1)}, u32[]{:S(2)}, u32[]{:S(2)}) %collective-permute-start.9) | collective-permute-done | bytes 131104 | tf_op jit(solution)/shard_map/ppermute | solution.py:292
  52.0 1.5 %shard_map.117 = (bf16[576,128]{1,0:T(8,128)(2,1)}, bf16[576,128]{1,0:T(8,128)(2,1)}) custom-call(bf16[128,512]{1,0:T(8,128)(2,1)S(1)} %get-tuple-element.25.own_ref, bf16[128,512]{1,0:T(8,128)(2,1)S(1)} %collective-permute-done.9.far_ref, bf16[2304,512]{1,0:T(8,128)(2,1)S(1)} %copy-done, bf16[2304,256]{1,0:T(8,128)(2,1)S(1)} %copy-done.1, ...), custom_call_target="tpu_custom_call" | custom-call | flops 301989888 | bytes 2359296 | tf_op jit(solution)/shard_map/pallas_call | solution.py:279
  53.5 3.6 %collective-permute-start.10 = (bf16[576,128]{1,0:T(8,128)(2,1)}, bf16[576,128]{1,0:T(8,128)(2,1)S(1)}, u32[]{:S(2)}, u32[]{:S(2)}) collective-permute-start(bf16[576,128]{1,0:T(8,128)(2,1)} %get-tuple-element.28), channel_id=1, source_target_pairs={{0,3},{1,2},{2,1},{3,0},{4,7},{5,6},{6,5},{7,4},{8,11},{9,10},{10,... | collective-permute-start | bytes 442376 | tf_op jit(solution)/shard_map/ppermute | solution.py:292
  57.1 1.5 %shard_map.116 = (bf16[576,128]{1,0:T(8,128)(2,1)}, f32[576,128]{1,0:T(8,128)S(1)}) custom-call(bf16[128,512]{1,0:T(8,128)(2,1)S(1)} %get-tuple-element.25.own_ref, bf16[128,512]{1,0:T(8,128)(2,1)S(1)} %collective-permute-done.9.far_ref, bf16[2304,512]{1,0:T(8,128)(2,1)S(1)} %copy-done, bf16[2304,256]{1,0:T(8,128)(2,1)S(1)} %copy-done.1, ...), custom_call_target="tpu_custom_call" | custom-call | flops 301989888 | bytes 2359296 | tf_op jit(solution)/shard_map/pallas_call | solution.py:279
  58.6 0.8 %collective-permute-start.12 = (bf16[576,128]{1,0:T(8,128)(2,1)}, bf16[576,128]{1,0:T(8,128)(2,1)S(1)}, u32[]{:S(2)}, u32[]{:S(2)}) collective-permute-start(bf16[576,128]{1,0:T(8,128)(2,1)} %get-tuple-element.30), channel_id=1, source_target_pairs={{0,1},{1,0},{2,3},{3,2},{4,5},{5,4},{6,7},{7,6},{8,9},{9,8},{10,11... | collective-permute-start | bytes 442376 | tf_op jit(solution)/shard_map/ppermute | solution.py:292
  59.4 1.7 %shard_map.115 = (f32[288,256]{1,0:T(8,128)}, f32[288,512]{1,0:T(8,128)}, f32[8,128]{1,0:T(8,128)S(1)}) custom-call(bf16[8,2,288,128]{3,2,1,0:T(8,128)(2,1)S(1)} %all-to-all-done.turned_ref, bf16[256,1024]{1,0:T(8,128)(2,1)S(1)} %get-tuple-element.22.attn_ref, bf16[256,1024]{1,0:T(8,128)(2,1)S(1)} %collective-permute-done.7.far_attn_ref, ...), custom_call_target="tpu_custom_call" | custom-call | flops 452984832 | bytes 2064384 | tf_op jit(solution)/shard_map/pallas_call | solution.py:279
  61.1 1.2 %collective-permute-done.10.refs_0_ = bf16[576,128]{1,0:T(8,128)(2,1)S(1)} collective-permute-done((bf16[576,128]{1,0:T(8,128)(2,1)}, bf16[576,128]{1,0:T(8,128)(2,1)S(1)}, u32[]{:S(2)}, u32[]{:S(2)}) %collective-permute-start.10) | collective-permute-done | bytes 147488 | tf_op jit(solution)/shard_map/ppermute | solution.py:292
  62.3 7.8 %collective-permute-done.11.refs_1_ = bf16[576,128]{1,0:T(8,128)(2,1)S(1)} collective-permute-done((bf16[576,128]{1,0:T(8,128)(2,1)}, bf16[576,128]{1,0:T(8,128)(2,1)S(1)}, u32[]{:S(2)}, u32[]{:S(2)}) %collective-permute-start.11) | collective-permute-done | bytes 147488 | tf_op jit(solution)/shard_map/ppermute | solution.py:292
  70.1 0.7 %shard_map.118 = bf16[576,128]{1,0:T(8,128)(2,1)} custom-call(f32[8,128]{1,0:T(8,128)S(1)} %get-tuple-element.24._, f32[576,128]{1,0:T(8,128)S(1)} %get-tuple-element.27.own_ref, bf16[576,128]{1,0:T(8,128)(2,1)S(1)} %collective-permute-done.10.refs_0_, bf16[576,128]{1,0:T(8,128)(2,1)S(1)} %collective-permute-done.11.refs_1_, ...), custom_call_target="tpu_custom_call" | custom-call | bytes 1179648 | tf_op jit(solution)/shard_map/pallas_call | solution.py:279
  (25 shorter events, 0.3 us)
Async XLA Ops:
  0.6 14.3 %copy-start.3 = (bf16[128,2304]{1,0:T(8,128)(2,1)S(1)}, bf16[128,2304]{1,0:T(8,128)(2,1)}, u32[]{:S(2)}) copy-start(bf16[128,2304]{1,0:T(8,128)(2,1)} %cot_hbm.3) | copy-start | bytes 1769476
  4.5 8.1 %collective-permute-start = (bf16[128,768]{1,0:T(8,128)(2,1)}, bf16[128,768]{1,0:T(8,128)(2,1)S(1)}, u32[]{:S(2)}, u32[]{:S(2)}) collective-permute-start(bf16[128,768]{1,0:T(8,128)(2,1)} %get-tuple-element.18), channel_id=1, source_target_pairs={{0,12},{4,8},{8,4},{12,0},{16,28},{20,24},{24,20},{28,16},{1,13},{... | collective-permute-start | bytes 589832 | tf_op jit(solution)/shard_map/ppermute | solution.py:292
  6.9 8.0 %collective-permute-start.1 = (bf16[128,768]{1,0:T(8,128)(2,1)}, bf16[128,768]{1,0:T(8,128)(2,1)S(1)}, u32[]{:S(2)}, u32[]{:S(2)}) collective-permute-start(bf16[128,768]{1,0:T(8,128)(2,1)} %get-tuple-element.19.refs_0_), channel_id=1, source_target_pairs={{0,16},{4,20},{8,24},{12,28},{16,0},{20,4},{24,8},{28,12},{1,17},{... | collective-permute-start | bytes 589832 | tf_op jit(solution)/shard_map/ppermute | solution.py:292
  8.5 13.5 %collective-permute-start.3 = (bf16[128,768]{1,0:T(8,128)(2,1)}, bf16[128,768]{1,0:T(8,128)(2,1)S(1)}, u32[]{:S(2)}, u32[]{:S(2)}) collective-permute-start(bf16[128,768]{1,0:T(8,128)(2,1)} %get-tuple-element.19.refs_0_), channel_id=1, source_target_pairs={{0,8},{4,12},{8,0},{12,4},{16,24},{20,28},{24,16},{28,20},{1,9},{5... | collective-permute-start | bytes 589832 | tf_op jit(solution)/shard_map/ppermute | solution.py:292
  9.1 14.5 %collective-permute-start.4 = (bf16[128,768]{1,0:T(8,128)(2,1)}, bf16[128,768]{1,0:T(8,128)(2,1)S(1)}, u32[]{:S(2)}, u32[]{:S(2)}) collective-permute-start(bf16[128,768]{1,0:T(8,128)(2,1)} %get-tuple-element.18), channel_id=1, source_target_pairs={{0,20},{4,16},{8,28},{12,24},{16,4},{20,0},{24,12},{28,8},{1,21},{... | collective-permute-start | bytes 589832 | tf_op jit(solution)/shard_map/ppermute | solution.py:292
  14.9 1.1 %copy-start.4 = (bf16[128,2304]{1,0:T(8,128)(2,1)S(1)}, bf16[128,2304]{1,0:T(8,128)(2,1)}, u32[]{:S(2)}) copy-start(bf16[128,2304]{1,0:T(8,128)(2,1)} %normed_hbm.1) | copy-start | bytes 1769476
  17.8 3.7 %copy-start.6 = (bf16[128,768]{1,0:T(8,128)(2,1)S(1)}, bf16[128,768]{1,0:T(8,128)(2,1)}, u32[]{:S(2)}) copy-start(bf16[128,768]{1,0:T(8,128)(2,1)} %get-tuple-element.18) | copy-start | bytes 589828
  17.8 23.8 %copy-start.5 = (bf16[128,768]{1,0:T(8,128)(2,1)S(1)}, bf16[128,768]{1,0:T(8,128)(2,1)}, u32[]{:S(2)}) copy-start(bf16[128,768]{1,0:T(8,128)(2,1)} %get-tuple-element.19.refs_0_) | copy-start | bytes 589828
  17.8 41.6 %all-to-all-start = ((bf16[8,2,288,128]{3,2,1,0:T(8,128)(2,1)}), bf16[8,2,288,128]{3,2,1,0:T(8,128)(2,1)S(1)}, u32[]{:S(2)}, u32[]{:S(2)}) async-start(bf16[8,2,288,128]{3,2,1,0:T(8,128)(2,1)} %get-tuple-element.20), calls=%async_computation | async-start | bytes 2359296 | tf_op jit(solution)/shard_map/all_to_all | solution.py:351
  21.5 3.6 %collective-permute-start.2 = (bf16[128,768]{1,0:T(8,128)(2,1)S(1)}, bf16[128,768]{1,0:T(8,128)(2,1)S(1)}, u32[]{:S(2)}, u32[]{:S(2)}) collective-permute-start(bf16[128,768]{1,0:T(8,128)(2,1)S(1)} %copy-done.6), channel_id=1, source_target_pairs={{0,4},{4,0},{8,12},{12,8},{16,20},{20,16},{24,28},{28,24},{1,5},{5... | collective-permute-start | bytes 589832 | tf_op jit(solution)/shard_map/ppermute | solution.py:292
  21.9 19.6 %collective-permute-start.5 = (bf16[128,768]{1,0:T(8,128)(2,1)S(1)}, bf16[128,768]{1,0:T(8,128)(2,1)S(1)}, u32[]{:S(2)}, u32[]{:S(2)}) collective-permute-start(bf16[128,768]{1,0:T(8,128)(2,1)S(1)} %collective-permute-done.3.refs_2_), channel_id=1, source_target_pairs={{0,16},{4,20},{8,24},{12,28},{16,0},{20,4},{24,8},{28,12},{1,17},{... | collective-permute-start | bytes 589832 | tf_op jit(solution)/shard_map/ppermute | solution.py:292
  23.6 18.0 %collective-permute-start.6 = (bf16[128,768]{1,0:T(8,128)(2,1)S(1)}, bf16[128,768]{1,0:T(8,128)(2,1)S(1)}, u32[]{:S(2)}, u32[]{:S(2)}) collective-permute-start(bf16[128,768]{1,0:T(8,128)(2,1)S(1)} %collective-permute-done.4.refs_5_), channel_id=1, source_target_pairs={{0,8},{4,12},{8,0},{12,4},{16,24},{20,28},{24,16},{28,20},{1,9},{5... | collective-permute-start | bytes 589832 | tf_op jit(solution)/shard_map/ppermute | solution.py:292
  41.6 10.3 %copy-start = (bf16[2304,512]{1,0:T(8,128)(2,1)S(1)}, bf16[2304,512]{1,0:T(8,128)(2,1)}, u32[]{:S(2)}) copy-start(bf16[2304,512]{1,0:T(8,128)(2,1)} %wq_ref.3) | copy-start | bytes 7077892
  41.6 10.3 %copy-start.1 = (bf16[2304,256]{1,0:T(8,128)(2,1)S(1)}, bf16[2304,256]{1,0:T(8,128)(2,1)}, u32[]{:S(2)}) copy-start(bf16[2304,256]{1,0:T(8,128)(2,1)} %wk_ref.3) | copy-start | bytes 3538948
  41.6 10.3 %copy-start.2 = (bf16[2304,256]{1,0:T(8,128)(2,1)S(1)}, bf16[2304,256]{1,0:T(8,128)(2,1)}, u32[]{:S(2)}) copy-start(bf16[2304,256]{1,0:T(8,128)(2,1)} %wv_ref.3) | copy-start | bytes 3538948
  49.8 9.6 %collective-permute-start.7 = (bf16[256,1024]{1,0:T(8,128)(2,1)S(1)}, bf16[256,1024]{1,0:T(8,128)(2,1)S(1)}, u32[]{:S(2)}, u32[]{:S(2)}) collective-permute-start(bf16[256,1024]{1,0:T(8,128)(2,1)S(1)} %get-tuple-element.22.attn_ref), channel_id=1, source_target_pairs={{0,4},{4,0},{8,12},{12,8},{16,20},{20,16},{24,28},{28,24},{1,5},{5... | collective-permute-start | bytes 1572872 | tf_op jit(solution)/shard_map/ppermute | solution.py:292
  49.9 2.1 %collective-permute-start.9 = (bf16[128,512]{1,0:T(8,128)(2,1)S(1)}, bf16[128,512]{1,0:T(8,128)(2,1)S(1)}, u32[]{:S(2)}, u32[]{:S(2)}) collective-permute-start(bf16[128,512]{1,0:T(8,128)(2,1)S(1)} %get-tuple-element.26), channel_id=1, source_target_pairs={{0,4},{4,0},{8,12},{12,8},{16,20},{20,16},{24,28},{28,24},{1,5},{5... | collective-permute-start | bytes 393224 | tf_op jit(solution)/shard_map/ppermute | solution.py:292
  50.4 9.0 %collective-permute-start.8 = (bf16[1024,128]{1,0:T(8,128)(2,1)S(1)}, bf16[1024,128]{1,0:T(8,128)(2,1)S(1)}, u32[]{:S(2)}, u32[]{:S(2)}) collective-permute-start(bf16[1024,128]{1,0:T(8,128)(2,1)S(1)} %get-tuple-element.23.dv_ref), channel_id=1, source_target_pairs={{0,4},{4,0},{8,12},{12,8},{16,20},{20,16},{24,28},{28,24},{1,5},{5... | collective-permute-start | bytes 786440 | tf_op jit(solution)/shard_map/ppermute | solution.py:292
  53.5 8.8 %collective-permute-start.10 = (bf16[576,128]{1,0:T(8,128)(2,1)}, bf16[576,128]{1,0:T(8,128)(2,1)S(1)}, u32[]{:S(2)}, u32[]{:S(2)}) collective-permute-start(bf16[576,128]{1,0:T(8,128)(2,1)} %get-tuple-element.28), channel_id=1, source_target_pairs={{0,3},{1,2},{2,1},{3,0},{4,7},{5,6},{6,5},{7,4},{8,11},{9,10},{10,... | collective-permute-start | bytes 442376 | tf_op jit(solution)/shard_map/ppermute | solution.py:292
  57.1 13.0 %collective-permute-start.11 = (bf16[576,128]{1,0:T(8,128)(2,1)}, bf16[576,128]{1,0:T(8,128)(2,1)S(1)}, u32[]{:S(2)}, u32[]{:S(2)}) collective-permute-start(bf16[576,128]{1,0:T(8,128)(2,1)} %get-tuple-element.29), channel_id=1, source_target_pairs={{0,2},{1,3},{2,0},{3,1},{4,6},{5,7},{6,4},{7,5},{8,10},{9,11},{10,... | collective-permute-start | bytes 442376 | tf_op jit(solution)/shard_map/ppermute | solution.py:292
  58.6 11.5 %collective-permute-start.12 = (bf16[576,128]{1,0:T(8,128)(2,1)}, bf16[576,128]{1,0:T(8,128)(2,1)S(1)}, u32[]{:S(2)}, u32[]{:S(2)}) collective-permute-start(bf16[576,128]{1,0:T(8,128)(2,1)} %get-tuple-element.30), channel_id=1, source_target_pairs={{0,1},{1,0},{2,3},{3,2},{4,5},{5,4},{6,7},{7,6},{8,9},{9,8},{10,11... | collective-permute-start | bytes 442376 | tf_op jit(solution)/shard_map/ppermute | solution.py:292

commit v8 on v7

--- a/solution.py
+++ b/solution.py
@@ -116,14 +116,12 @@
     key_t_ref,
     dq_t_ref,
     dk_ref,
-    sem,
 ):
     me = lax.axis_index("seq")
     core, chip = me % 2, me // 2
     rows = dx_own_ref.shape[0]
     for apart, source in enumerate(block_refs):
-        place = me ^ apart
-        pltpu.make_async_copy(source, gathered_ref.at[at(place, rows)], sem.at[place]).start()
+        gathered_ref[at(me ^ apart, rows)] = source[...]
     tokens = gathered_ref.shape[0]
     size = 2 * rows
     steps = tokens // size
@@ -132,6 +130,8 @@
     key_cols = slice(heads * HEAD_SIZE, (heads + 1) * HEAD_SIZE)
     value_cols = slice((heads + 1) * HEAD_SIZE, (heads + 2) * HEAD_SIZE)
     grad_base = (heads + 2) * HEAD_SIZE
+    value_t_ref[...] = gathered_ref[:, value_cols].T
+    key_t_ref[...] = gathered_ref[:, key_cols].T
     key_place = lax.broadcasted_iota(jnp.int32, (size, wide), 0)
     query_place = lax.broadcasted_iota(jnp.int32, (size, wide), 1) % size
     allowed = key_place <= query_place
@@ -141,12 +141,6 @@
         own = slice(step * size, span)
         lanes = slice(step * wide, (step + 1) * wide)
         score_ref = score_odd_ref if step % 2 else score_even_ref
-        for block in (2 * step, 2 * step + 1):
-            pltpu.make_async_copy(
-                block_refs[0], gathered_ref.at[pl.ds(block * rows, rows)], sem.at[block]
-            ).wait()
-        value_t_ref[:, own] = gathered_ref[own, value_cols].T
-        key_t_ref[:, own] = gathered_ref[own, key_cols].T
         queries = jnp.concatenate(
             [gathered_ref[own, h * HEAD_SIZE : (h + 1) * HEAD_SIZE] for h in range(heads)], axis=0
         )
@@ -340,13 +334,13 @@
     turned, turn_done = kernel_call(
         functools.partial(turn_kernel, blocks),
         (shape((blocks, 2, model // blocks, rows), bf16), shape((8, HEAD_SIZE), f32)),
-        (normed_input, out_cotangent, held[3], held[4]),
+        (normed_input, out_cotangent, held[2], held[blocks // 2 + 1]),
         scratch=(
             pltpu.VMEM(normed_input.shape, bf16),
             pltpu.VMEM(out_cotangent.shape, bf16),
             pltpu.SemaphoreType.DMA((2,)),
         ),
-        moved=8 * rows * model,
+        moved=256 * rows * model,
     )
     turned = lax.all_to_all(turned, "seq", 0, 0)
     dx_own, dx_far, attn, dv = kernel_call(
@@ -358,6 +352,7 @@
             shape((tokens, kv_cols), bf16),
         ),
         [held[apart] for apart in range(blocks)] + [turn_done],
+        in_vmem=range(blocks),
         scratch=(
             pltpu.VMEM((tokens, packed_cols), bf16),
             pltpu.VMEM((tokens, wide), f32),
@@ -370,7 +365,6 @@
             pltpu.VMEM((HEAD_SIZE, tokens), bf16),
             pltpu.VMEM((HEAD_SIZE, wide), f32),
             pltpu.VMEM((2 * rows, HEAD_SIZE), f32),
-            pltpu.SemaphoreType.DMA((blocks,)),
         ),
         flops=8 * tokens * tokens * q_cols,
         moved=2 * tokens * packed_cols,
@@ -387,6 +381,7 @@
             scratch=(pltpu.VMEM((rows, 2 * (q_cols + 2 * kv_cols)), bf16),),
             flops=2 * rows * model * (q_cols + 2 * kv_cols),
             moved=2 * model * (q_cols + 2 * kv_cols),
+            room=4,
         )
         terms.update(zip(chosen, made))
     arrived = [swapped(terms[apart], "head", apart) for apart in aparts[:-1]]

time: 71 us -> 72.5 us (1.021)
  waiting for transfers between devices: 32.8 us -> 37.2 us
  Pallas kernels: 19.2 us -> 16.6 us
    ppermute x13, waiting for transfers between devices: 32.8 us -> 37.2 us  [swapped(): lax.ppermute(value, axis, [(place, place ^ apart) for place in range(coun...]
    pallas_call x7, Pallas kernels: 19.2 us -> 16.6 us  [kernel_call(): pl.pallas_call(body, out_shape=outs, in_specs=[vmem if place in in_vmem e...]
  transfers between devices with their start and end apart: 14 -> 14, of which waited for: 7 -> 9; matrix products, arithmetic and copies ran while one was open for 0% -> 0% of each run, Pallas kernels for 21% -> 14%
where the time goes in v8:
time: 72.5 us; the launch traced here: 72.3 us
  waiting for transfers between devices  37.2 us (51%)
  starting transfers between devices  16.7 us (23%)
  Pallas kernels  16.6 us (23%)
  local copies, waits for them, and re-layouts  1.09 us (2%)
  between operations  0.73 us (1%)
    ppermute x13, waiting for transfers between devices, swapped(): lax.ppermute(value, axis, [(place, place ^ apart) for place in range(coun...  37.2 us
    pallas_call x7, Pallas kernels, kernel_call(): pl.pallas_call(body, out_shape=outs, in_specs=[vmem if place in in_vmem e...  16.6 us
    ppermute x13, starting transfers between devices, swapped(): lax.ppermute(value, axis, [(place, place ^ apart) for place in range(coun...  13 us
    all_to_all x1, starting transfers between devices, gathered_plan(): turned = lax.all_to_all(turned, 'seq', 0, 0)  3.71 us
  transfers between devices with their start and end apart: 14, of which 9 were waited for; matrix products, arithmetic and copies ran while one was open for 0% of the time, Pallas kernels for 14%

profile of v8, /device:TPU:0, one launch (start us, length us, event | category | flops | bytes accessed | tf_op | source)
XLA Modules:
  0.0 72.3 jit_solution(3074080263921101207)
XLA Ops:
  0.6 3.8 %shard_map.112 = (bf16[128,768]{1,0:T(8,128)(2,1)}, bf16[128,768]{1,0:T(8,128)(2,1)}) custom-call(bf16[128,2304]{1,0:T(8,128)(2,1)} %cot_hbm.3, bf16[512,2304]{1,0:T(8,128)(2,1)} %weight_hbm.1, bf16[128,512]{1,0:T(8,128)(2,1)} %q_hbm.1, bf16[128,256]{1,0:T(8,128)(2,1)} %k_hbm.1, bf16[128,256]{1,0:T(8,128)(2,1)} %v_hbm.1), custom_call_target="tpu_custom_call" | custom-call | flops 301989888 | bytes 2949120 | tf_op jit(solution)/shard_map/pallas_call | solution.py:273
  4.5 3.0 %collective-permute-start = (bf16[128,768]{1,0:T(8,128)(2,1)}, bf16[128,768]{1,0:T(8,128)(2,1)S(1)}, u32[]{:S(2)}, u32[]{:S(2)}) collective-permute-start(bf16[128,768]{1,0:T(8,128)(2,1)} %get-tuple-element.18.refs_0_), channel_id=1, source_target_pairs={{0,8},{4,12},{8,0},{12,4},{16,24},{20,28},{24,16},{28,20},{1,9},{5... | collective-permute-start | bytes 589832 | tf_op jit(solution)/shard_map/ppermute | solution.py:286
  7.5 0.7 collective-permute-start.1
  8.2 4.4 %collective-permute-done._.refs_2_ = bf16[128,768]{1,0:T(8,128)(2,1)S(1)} collective-permute-done((bf16[128,768]{1,0:T(8,128)(2,1)}, bf16[128,768]{1,0:T(8,128)(2,1)S(1)}, u32[]{:S(2)}, u32[]{:S(2)}) %collective-permute-start) | collective-permute-done | bytes 196640 | tf_op jit(solution)/shard_map/ppermute | solution.py:286
  12.6 2.2 %collective-permute-done.1.__.refs_5_ = bf16[128,768]{1,0:T(8,128)(2,1)S(1)} collective-permute-done((bf16[128,768]{1,0:T(8,128)(2,1)}, bf16[128,768]{1,0:T(8,128)(2,1)S(1)}, u32[]{:S(2)}, u32[]{:S(2)}) %collective-permute-start.1) | collective-permute-done | bytes 196640 | tf_op jit(solution)/shard_map/ppermute | solution.py:286
  14.9 1.1 %copy-done.4 = bf16[128,2304]{1,0:T(8,128)(2,1)S(1)} copy-done((bf16[128,2304]{1,0:T(8,128)(2,1)S(1)}, bf16[128,2304]{1,0:T(8,128)(2,1)}, u32[]{:S(2)}) %copy-start.4) | copy-done | bytes 589848
  15.9 1.8 %shard_map.113 = (bf16[8,2,288,128]{3,2,1,0:T(8,128)(2,1)}, f32[8,128]{1,0:T(8,128)S(1)}) custom-call(bf16[128,2304]{1,0:T(8,128)(2,1)S(1)} %copy-done.4, bf16[128,2304]{1,0:T(8,128)(2,1)S(1)} %copy-done.3, bf16[128,768]{1,0:T(8,128)(2,1)S(1)} %collective-permute-done._.refs_2_, bf16[128,768]{1,0:T(8,128)(2,1)S(1)} %collective-permute-done.1.__.refs_5_), custom_call_target="tpu_custom_call" | custom-call | bytes 75497472 | tf_op jit(solution)/shard_map/pallas_call | solution.py:273
  17.7 3.7 %all-to-all-start = ((bf16[8,2,288,128]{3,2,1,0:T(8,128)(2,1)}), bf16[8,2,288,128]{3,2,1,0:T(8,128)(2,1)S(1)}, u32[]{:S(2)}, u32[]{:S(2)}) async-start(bf16[8,2,288,128]{3,2,1,0:T(8,128)(2,1)} %get-tuple-element.20), calls=%async_computation | async-start | bytes 2359296 | tf_op jit(solution)/shard_map/all_to_all | solution.py:345
  21.9 1.6 %collective-permute-start.3 = (bf16[128,768]{1,0:T(8,128)(2,1)S(1)}, bf16[128,768]{1,0:T(8,128)(2,1)S(1)}, u32[]{:S(2)}, u32[]{:S(2)}) collective-permute-start(bf16[128,768]{1,0:T(8,128)(2,1)S(1)} %copy-done.6), channel_id=1, source_target_pairs={{0,12},{4,8},{8,4},{12,0},{16,28},{20,24},{24,20},{28,16},{1,13},{... | collective-permute-start | bytes 589832 | tf_op jit(solution)/shard_map/ppermute | solution.py:286
  23.5 1.5 %collective-permute-start.4 = (bf16[128,768]{1,0:T(8,128)(2,1)S(1)}, bf16[128,768]{1,0:T(8,128)(2,1)S(1)}, u32[]{:S(2)}, u32[]{:S(2)}) collective-permute-start(bf16[128,768]{1,0:T(8,128)(2,1)S(1)} %copy-done.5), channel_id=1, source_target_pairs={{0,16},{4,20},{8,24},{12,28},{16,0},{20,4},{24,8},{28,12},{1,17},{... | collective-permute-start | bytes 589832 | tf_op jit(solution)/shard_map/ppermute | solution.py:286
  25.0 0.5 collective-permute-start.5
  25.7 15.3 %collective-permute-done.3.refs_3_ = bf16[128,768]{1,0:T(8,128)(2,1)S(1)} collective-permute-done((bf16[128,768]{1,0:T(8,128)(2,1)S(1)}, bf16[128,768]{1,0:T(8,128)(2,1)S(1)}, u32[]{:S(2)}, u32[]{:S(2)}) %collective-permute-start.3) | collective-permute-done | bytes 196640 | tf_op jit(solution)/shard_map/ppermute | solution.py:286
  41.0 0.9 %collective-permute-done.4.refs_4_ = bf16[128,768]{1,0:T(8,128)(2,1)S(1)} collective-permute-done((bf16[128,768]{1,0:T(8,128)(2,1)S(1)}, bf16[128,768]{1,0:T(8,128)(2,1)S(1)}, u32[]{:S(2)}, u32[]{:S(2)}) %collective-permute-start.4) | collective-permute-done | bytes 196640 | tf_op jit(solution)/shard_map/ppermute | solution.py:286
  41.9 3.7 %collective-permute-done.5.refs_6_ = bf16[128,768]{1,0:T(8,128)(2,1)S(1)} collective-permute-done((bf16[128,768]{1,0:T(8,128)(2,1)S(1)}, bf16[128,768]{1,0:T(8,128)(2,1)S(1)}, u32[]{:S(2)}, u32[]{:S(2)}) %collective-permute-start.5) | collective-permute-done | bytes 196640 | tf_op jit(solution)/shard_map/ppermute | solution.py:286
  45.7 5.5 %shard_map.114 = (bf16[128,512]{1,0:T(8,128)(2,1)S(1)}, bf16[128,512]{1,0:T(8,128)(2,1)S(1)}, bf16[256,1024]{1,0:T(8,128)(2,1)S(1)}, bf16[1024,128]{1,0:T(8,128)(2,1)S(1)}) custom-call(bf16[128,768]{1,0:T(8,128)(2,1)S(1)} %copy-done.5, bf16[128,768]{1,0:T(8,128)(2,1)S(1)} %collective-permute-done.2.refs_1_, ...), custom_call_target="tpu_custom_call" | custom-call | flops 2147483648 | bytes 1572864 | tf_op jit(solution)/shard_map/pallas_call | solution.py:273
  51.9 1.5 %collective-permute-done.9.far_ref = bf16[128,512]{1,0:T(8,128)(2,1)S(1)} collective-permute-done((bf16[128,512]{1,0:T(8,128)(2,1)S(1)}, bf16[128,512]{1,0:T(8,128)(2,1)S(1)}, u32[]{:S(2)}, u32[]{:S(2)}) %collective-permute-start.9) | collective-permute-done | bytes 131104 | tf_op jit(solution)/shard_map/ppermute | solution.py:286
  53.4 1.5 %shard_map.117 = (bf16[576,128]{1,0:T(8,128)(2,1)}, bf16[576,128]{1,0:T(8,128)(2,1)}) custom-call(bf16[128,512]{1,0:T(8,128)(2,1)S(1)} %get-tuple-element.25.own_ref, bf16[128,512]{1,0:T(8,128)(2,1)S(1)} %collective-permute-done.9.far_ref, bf16[2304,512]{1,0:T(8,128)(2,1)S(1)} %copy-done, bf16[2304,256]{1,0:T(8,128)(2,1)S(1)} %copy-done.1, ...), custom_call_target="tpu_custom_call" | custom-call | flops 301989888 | bytes 2359296 | tf_op jit(solution)/shard_map/pallas_call | solution.py:273
  55.0 3.6 %collective-permute-start.10 = (bf16[576,128]{1,0:T(8,128)(2,1)}, bf16[576,128]{1,0:T(8,128)(2,1)S(1)}, u32[]{:S(2)}, u32[]{:S(2)}) collective-permute-start(bf16[576,128]{1,0:T(8,128)(2,1)} %get-tuple-element.28), channel_id=1, source_target_pairs={{0,3},{1,2},{2,1},{3,0},{4,7},{5,6},{6,5},{7,4},{8,11},{9,10},{10,... | collective-permute-start | bytes 442376 | tf_op jit(solution)/shard_map/ppermute | solution.py:286
  58.6 1.5 %shard_map.116 = (bf16[576,128]{1,0:T(8,128)(2,1)}, f32[576,128]{1,0:T(8,128)S(1)}) custom-call(bf16[128,512]{1,0:T(8,128)(2,1)S(1)} %get-tuple-element.25.own_ref, bf16[128,512]{1,0:T(8,128)(2,1)S(1)} %collective-permute-done.9.far_ref, bf16[2304,512]{1,0:T(8,128)(2,1)S(1)} %copy-done, bf16[2304,256]{1,0:T(8,128)(2,1)S(1)} %copy-done.1, ...), custom_call_target="tpu_custom_call" | custom-call | flops 301989888 | bytes 2359296 | tf_op jit(solution)/shard_map/pallas_call | solution.py:273
  60.1 0.8 %collective-permute-start.12 = (bf16[576,128]{1,0:T(8,128)(2,1)}, bf16[576,128]{1,0:T(8,128)(2,1)S(1)}, u32[]{:S(2)}, u32[]{:S(2)}) collective-permute-start(bf16[576,128]{1,0:T(8,128)(2,1)} %get-tuple-element.30), channel_id=1, source_target_pairs={{0,1},{1,0},{2,3},{3,2},{4,5},{5,4},{6,7},{7,6},{8,9},{9,8},{10,11... | collective-permute-start | bytes 442376 | tf_op jit(solution)/shard_map/ppermute | solution.py:286
  60.9 1.7 %shard_map.115 = (f32[288,256]{1,0:T(8,128)}, f32[288,512]{1,0:T(8,128)}, f32[8,128]{1,0:T(8,128)S(1)}) custom-call(bf16[8,2,288,128]{3,2,1,0:T(8,128)(2,1)S(1)} %all-to-all-done.turned_ref, bf16[256,1024]{1,0:T(8,128)(2,1)S(1)} %get-tuple-element.22.attn_ref, bf16[256,1024]{1,0:T(8,128)(2,1)S(1)} %collective-permute-done.7.far_attn_ref, ...), custom_call_target="tpu_custom_call" | custom-call | flops 452984832 | bytes 2064384 | tf_op jit(solution)/shard_map/pallas_call | solution.py:273
  62.6 1.2 %collective-permute-done.10.refs_0_ = bf16[576,128]{1,0:T(8,128)(2,1)S(1)} collective-permute-done((bf16[576,128]{1,0:T(8,128)(2,1)}, bf16[576,128]{1,0:T(8,128)(2,1)S(1)}, u32[]{:S(2)}, u32[]{:S(2)}) %collective-permute-start.10) | collective-permute-done | bytes 147488 | tf_op jit(solution)/shard_map/ppermute | solution.py:286
  63.8 7.8 %collective-permute-done.11.refs_1_ = bf16[576,128]{1,0:T(8,128)(2,1)S(1)} collective-permute-done((bf16[576,128]{1,0:T(8,128)(2,1)}, bf16[576,128]{1,0:T(8,128)(2,1)S(1)}, u32[]{:S(2)}, u32[]{:S(2)}) %collective-permute-start.11) | collective-permute-done | bytes 147488 | tf_op jit(solution)/shard_map/ppermute | solution.py:286
  71.6 0.7 %shard_map.118 = bf16[576,128]{1,0:T(8,128)(2,1)} custom-call(f32[8,128]{1,0:T(8,128)S(1)} %get-tuple-element.24._, f32[576,128]{1,0:T(8,128)S(1)} %get-tuple-element.27.own_ref, bf16[576,128]{1,0:T(8,128)(2,1)S(1)} %collective-permute-done.10.refs_0_, bf16[576,128]{1,0:T(8,128)(2,1)S(1)} %collective-permute-done.11.refs_1_, ...), custom_call_target="tpu_custom_call" | custom-call | bytes 1179648 | tf_op jit(solution)/shard_map/pallas_call | solution.py:273
  (25 shorter events, 1.3 us)
Async XLA Ops:
  0.6 14.2 %copy-start.3 = (bf16[128,2304]{1,0:T(8,128)(2,1)S(1)}, bf16[128,2304]{1,0:T(8,128)(2,1)}, u32[]{:S(2)}) copy-start(bf16[128,2304]{1,0:T(8,128)(2,1)} %cot_hbm.3) | copy-start | bytes 1769476
  4.5 8.1 %collective-permute-start = (bf16[128,768]{1,0:T(8,128)(2,1)}, bf16[128,768]{1,0:T(8,128)(2,1)S(1)}, u32[]{:S(2)}, u32[]{:S(2)}) collective-permute-start(bf16[128,768]{1,0:T(8,128)(2,1)} %get-tuple-element.18.refs_0_), channel_id=1, source_target_pairs={{0,8},{4,12},{8,0},{12,4},{16,24},{20,28},{24,16},{28,20},{1,9},{5... | collective-permute-start | bytes 589832 | tf_op jit(solution)/shard_map/ppermute | solution.py:286
  7.5 7.3 %collective-permute-start.1 = (bf16[128,768]{1,0:T(8,128)(2,1)}, bf16[128,768]{1,0:T(8,128)(2,1)S(1)}, u32[]{:S(2)}, u32[]{:S(2)}) collective-permute-start(bf16[128,768]{1,0:T(8,128)(2,1)} %get-tuple-element.19), channel_id=1, source_target_pairs={{0,20},{4,16},{8,28},{12,24},{16,4},{20,0},{24,12},{28,8},{1,21},{... | collective-permute-start | bytes 589832 | tf_op jit(solution)/shard_map/ppermute | solution.py:286
  14.8 1.1 %copy-start.4 = (bf16[128,2304]{1,0:T(8,128)(2,1)S(1)}, bf16[128,2304]{1,0:T(8,128)(2,1)}, u32[]{:S(2)}) copy-start(bf16[128,2304]{1,0:T(8,128)(2,1)} %normed_hbm.1) | copy-start | bytes 1769476
  17.7 3.7 %copy-start.6 = (bf16[128,768]{1,0:T(8,128)(2,1)S(1)}, bf16[128,768]{1,0:T(8,128)(2,1)}, u32[]{:S(2)}) copy-start(bf16[128,768]{1,0:T(8,128)(2,1)} %get-tuple-element.19) | copy-start | bytes 589828
  17.7 5.8 %copy-start.5 = (bf16[128,768]{1,0:T(8,128)(2,1)S(1)}, bf16[128,768]{1,0:T(8,128)(2,1)}, u32[]{:S(2)}) copy-start(bf16[128,768]{1,0:T(8,128)(2,1)} %get-tuple-element.18.refs_0_) | copy-start | bytes 589828
  17.7 43.2 %all-to-all-start = ((bf16[8,2,288,128]{3,2,1,0:T(8,128)(2,1)}), bf16[8,2,288,128]{3,2,1,0:T(8,128)(2,1)S(1)}, u32[]{:S(2)}, u32[]{:S(2)}) async-start(bf16[8,2,288,128]{3,2,1,0:T(8,128)(2,1)} %get-tuple-element.20), calls=%async_computation | async-start | bytes 2359296 | tf_op jit(solution)/shard_map/all_to_all | solution.py:345
  21.5 4.2 %collective-permute-start.2 = (bf16[128,768]{1,0:T(8,128)(2,1)S(1)}, bf16[128,768]{1,0:T(8,128)(2,1)S(1)}, u32[]{:S(2)}, u32[]{:S(2)}) collective-permute-start(bf16[128,768]{1,0:T(8,128)(2,1)S(1)} %copy-done.6), channel_id=1, source_target_pairs={{0,4},{4,0},{8,12},{12,8},{16,20},{20,16},{24,28},{28,24},{1,5},{5... | collective-permute-start | bytes 589832 | tf_op jit(solution)/shard_map/ppermute | solution.py:286
  21.9 19.2 %collective-permute-start.3 = (bf16[128,768]{1,0:T(8,128)(2,1)S(1)}, bf16[128,768]{1,0:T(8,128)(2,1)S(1)}, u32[]{:S(2)}, u32[]{:S(2)}) collective-permute-start(bf16[128,768]{1,0:T(8,128)(2,1)S(1)} %copy-done.6), channel_id=1, source_target_pairs={{0,12},{4,8},{8,4},{12,0},{16,28},{20,24},{24,20},{28,16},{1,13},{... | collective-permute-start | bytes 589832 | tf_op jit(solution)/shard_map/ppermute | solution.py:286
  23.5 18.4 %collective-permute-start.4 = (bf16[128,768]{1,0:T(8,128)(2,1)S(1)}, bf16[128,768]{1,0:T(8,128)(2,1)S(1)}, u32[]{:S(2)}, u32[]{:S(2)}) collective-permute-start(bf16[128,768]{1,0:T(8,128)(2,1)S(1)} %copy-done.5), channel_id=1, source_target_pairs={{0,16},{4,20},{8,24},{12,28},{16,0},{20,4},{24,8},{28,12},{1,17},{... | collective-permute-start | bytes 589832 | tf_op jit(solution)/shard_map/ppermute | solution.py:286
  25.0 20.7 %collective-permute-start.5 = (bf16[128,768]{1,0:T(8,128)(2,1)S(1)}, bf16[128,768]{1,0:T(8,128)(2,1)S(1)}, u32[]{:S(2)}, u32[]{:S(2)}) collective-permute-start(bf16[128,768]{1,0:T(8,128)(2,1)S(1)} %collective-permute-done._.refs_2_), channel_id=1, source_target_pairs={{0,16},{4,20},{8,24},{12,28},{16,0},{20,4},{24,8},{28,12},{1,17},{... | collective-permute-start | bytes 589832 | tf_op jit(solution)/shard_map/ppermute | solution.py:286
  25.5 20.2 %collective-permute-start.6 = (bf16[128,768]{1,0:T(8,128)(2,1)S(1)}, bf16[128,768]{1,0:T(8,128)(2,1)S(1)}, u32[]{:S(2)}, u32[]{:S(2)}) collective-permute-start(bf16[128,768]{1,0:T(8,128)(2,1)S(1)} %collective-permute-done.1.__.refs_5_), channel_id=1, source_target_pairs={{0,8},{4,12},{8,0},{12,4},{16,24},{20,28},{24,16},{28,20},{1,9},{5... | collective-permute-start | bytes 589832 | tf_op jit(solution)/shard_map/ppermute | solution.py:286
  45.7 7.7 %copy-start = (bf16[2304,512]{1,0:T(8,128)(2,1)S(1)}, bf16[2304,512]{1,0:T(8,128)(2,1)}, u32[]{:S(2)}) copy-start(bf16[2304,512]{1,0:T(8,128)(2,1)} %wq_ref.3) | copy-start | bytes 7077892
  45.7 7.7 %copy-start.1 = (bf16[2304,256]{1,0:T(8,128)(2,1)S(1)}, bf16[2304,256]{1,0:T(8,128)(2,1)}, u32[]{:S(2)}) copy-start(bf16[2304,256]{1,0:T(8,128)(2,1)} %wk_ref.3) | copy-start | bytes 3538948
  45.7 7.7 %copy-start.2 = (bf16[2304,256]{1,0:T(8,128)(2,1)S(1)}, bf16[2304,256]{1,0:T(8,128)(2,1)}, u32[]{:S(2)}) copy-start(bf16[2304,256]{1,0:T(8,128)(2,1)} %wv_ref.3) | copy-start | bytes 3538948
  51.3 9.6 %collective-permute-start.7 = (bf16[256,1024]{1,0:T(8,128)(2,1)S(1)}, bf16[256,1024]{1,0:T(8,128)(2,1)S(1)}, u32[]{:S(2)}, u32[]{:S(2)}) collective-permute-start(bf16[256,1024]{1,0:T(8,128)(2,1)S(1)} %get-tuple-element.22.attn_ref), channel_id=1, source_target_pairs={{0,4},{4,0},{8,12},{12,8},{16,20},{20,16},{24,28},{28,24},{1,5},{5... | collective-permute-start | bytes 1572872 | tf_op jit(solution)/shard_map/ppermute | solution.py:286
  51.4 2.1 %collective-permute-start.9 = (bf16[128,512]{1,0:T(8,128)(2,1)S(1)}, bf16[128,512]{1,0:T(8,128)(2,1)S(1)}, u32[]{:S(2)}, u32[]{:S(2)}) collective-permute-start(bf16[128,512]{1,0:T(8,128)(2,1)S(1)} %get-tuple-element.26), channel_id=1, source_target_pairs={{0,4},{4,0},{8,12},{12,8},{16,20},{20,16},{24,28},{28,24},{1,5},{5... | collective-permute-start | bytes 393224 | tf_op jit(solution)/shard_map/ppermute | solution.py:286
  51.9 9.0 %collective-permute-start.8 = (bf16[1024,128]{1,0:T(8,128)(2,1)S(1)}, bf16[1024,128]{1,0:T(8,128)(2,1)S(1)}, u32[]{:S(2)}, u32[]{:S(2)}) collective-permute-start(bf16[1024,128]{1,0:T(8,128)(2,1)S(1)} %get-tuple-element.23.dv_ref), channel_id=1, source_target_pairs={{0,4},{4,0},{8,12},{12,8},{16,20},{20,16},{24,28},{28,24},{1,5},{5... | collective-permute-start | bytes 786440 | tf_op jit(solution)/shard_map/ppermute | solution.py:286
  55.0 8.8 %collective-permute-start.10 = (bf16[576,128]{1,0:T(8,128)(2,1)}, bf16[576,128]{1,0:T(8,128)(2,1)S(1)}, u32[]{:S(2)}, u32[]{:S(2)}) collective-permute-start(bf16[576,128]{1,0:T(8,128)(2,1)} %get-tuple-element.28), channel_id=1, source_target_pairs={{0,3},{1,2},{2,1},{3,0},{4,7},{5,6},{6,5},{7,4},{8,11},{9,10},{10,... | collective-permute-start | bytes 442376 | tf_op jit(solution)/shard_map/ppermute | solution.py:286
  58.6 13.0 %collective-permute-start.11 = (bf16[576,128]{1,0:T(8,128)(2,1)}, bf16[576,128]{1,0:T(8,128)(2,1)S(1)}, u32[]{:S(2)}, u32[]{:S(2)}) collective-permute-start(bf16[576,128]{1,0:T(8,128)(2,1)} %get-tuple-element.29), channel_id=1, source_target_pairs={{0,2},{1,3},{2,0},{3,1},{4,6},{5,7},{6,4},{7,5},{8,10},{9,11},{10,... | collective-permute-start | bytes 442376 | tf_op jit(solution)/shard_map/ppermute | solution.py:286
  60.1 11.5 %collective-permute-start.12 = (bf16[576,128]{1,0:T(8,128)(2,1)}, bf16[576,128]{1,0:T(8,128)(2,1)S(1)}, u32[]{:S(2)}, u32[]{:S(2)}) collective-permute-start(bf16[576,128]{1,0:T(8,128)(2,1)} %get-tuple-element.30), channel_id=1, source_target_pairs={{0,1},{1,0},{2,3},{3,2},{4,5},{5,4},{6,7},{7,6},{8,9},{9,8},{10,11... | collective-permute-start | bytes 442376 | tf_op jit(solution)/shard_map/ppermute | solution.py:286

commit v9 on v8

--- a/solution.py
+++ b/solution.py
@@ -80,18 +80,20 @@
         copy.wait()
 
 
-def turn_kernel(parts, normed_hbm, cot_hbm, _, __, turned_ref, done_ref, normed_ref, cot_ref, sem):
-    cut = normed_ref.shape[1] // parts
+def turn_kernel(normed_hbm, cot_hbm, _, __, *refs):
+    turned_refs, (done_ref, normed_ref, cot_ref, turned_ref, sem) = refs[:-5], refs[-5:]
+    me = lax.axis_index("seq")
     done_ref[...] = jnp.zeros_like(done_ref)
+    cut = turned_refs[0].shape[1]
     copies = []
     for which, (source, target) in enumerate(((normed_hbm, normed_ref), (cot_hbm, cot_ref))):
         copies.append(pltpu.make_async_copy(source, target, sem.at[which]))
         copies[-1].start()
     for which, ref in enumerate((normed_ref, cot_ref)):
         copies[which].wait()
-        turned = ref[...].astype(jnp.float32).T.astype(jnp.bfloat16)
-        for part in range(parts):
-            turned_ref[part, which] = turned[part * cut : (part + 1) * cut]
+        turned_ref[which] = ref[...].astype(jnp.float32).T.astype(jnp.bfloat16)
+        for apart, target in enumerate(turned_refs):
+            target[which] = turned_ref[which, at(me ^ apart, cut)]
 
 
 def attention_kernel(blocks, *refs):
@@ -247,14 +249,14 @@
 
 
 def weight_grad_kernel(
-    turned_ref, attn_ref, far_attn_ref, dv_ref, far_dv_ref, wvalue_ref, woutput_ref, done_ref, joined_ref
+    attn_ref, far_attn_ref, dv_ref, far_dv_ref, *refs
 ):
+    column_refs, (wvalue_ref, woutput_ref, done_ref, joined_ref) = refs[:-4], refs[-4:]
     done_ref[...] = jnp.zeros_like(done_ref)
-    core = lax.axis_index("seq") % 2
-    parts = turned_ref.shape[0]
-    rows = turned_ref.shape[3]
-    for part in range(parts):
-        joined_ref[:, :, part * rows : (part + 1) * rows] = turned_ref[part]
+    me = lax.axis_index("seq")
+    core = me % 2
+    for apart, ref in enumerate(column_refs):
+        joined_ref[:, :, at(me ^ apart, ref.shape[2])] = ref[...]
     for half, attn, dv in ((core, attn_ref, dv_ref), (1 - core, far_attn_ref, far_dv_ref)):
         wvalue_ref[:, at(half, dv.shape[1])] = dot_nn(joined_ref[0], dv[...])
         woutput_ref[:, at(half, attn.shape[0])] = dot_nt(joined_ref[1], attn[...])
@@ -331,18 +333,21 @@
         else:
             held[apart] = swapped(held[apart ^ through], "seq", through)
     held[1] = swapped(other, "seq", 1)
-    turned, turn_done = kernel_call(
-        functools.partial(turn_kernel, blocks),
-        (shape((blocks, 2, model // blocks, rows), bf16), shape((8, HEAD_SIZE), f32)),
+    *turned, turn_done = kernel_call(
+        turn_kernel,
+        (shape((2, model // blocks, rows), bf16),) * blocks + (shape((8, HEAD_SIZE), f32),),
         (normed_input, out_cotangent, held[2], held[blocks // 2 + 1]),
         scratch=(
             pltpu.VMEM(normed_input.shape, bf16),
             pltpu.VMEM(out_cotangent.shape, bf16),
+            pltpu.VMEM((2, model, rows), bf16),
             pltpu.SemaphoreType.DMA((2,)),
         ),
-        moved=256 * rows * model,
-    )
-    turned = lax.all_to_all(turned, "seq", 0, 0)
+        moved=8 * rows * model,
+    )
+    columns = [turned[0]] + [
+        swapped(turned[apart], "seq", apart) for apart in range(1, blocks)
+    ]
     dx_own, dx_far, attn, dv = kernel_call(
         functools.partial(attention_kernel, blocks),
         (
@@ -392,8 +397,8 @@
             shape((model // blocks, 2 * q_cols), f32),
             shape((8, HEAD_SIZE), f32),
         ),
-        (turned, attn, swapped(attn, "seq", 1), dv, swapped(dv, "seq", 1)),
-        in_vmem=range(5),
+        (attn, swapped(attn, "seq", 1), dv, swapped(dv, "seq", 1), *columns),
+        in_vmem=range(4 + blocks),
         scratch=(pltpu.VMEM((2, model // blocks, tokens), bf16),),
         flops=4 * tokens * (model // blocks) * (q_cols + kv_cols),
         moved=4 * (model // blocks) * (tokens + 2 * q_cols + 2 * kv_cols),

time: 72.5 us -> 68.3 us (0.942)
  waiting for transfers between devices: 37.2 us -> 31 us
  starting transfers between devices: 16.7 us -> 19.7 us
  Pallas kernels: 16.6 us -> 14.6 us
  local copies, waits for them, and re-layouts: 1.09 us -> 2.01 us
    ppermute x13 -> x20, starting transfers between devices: 13 us -> 19.7 us  [swapped(): lax.ppermute(value, axis, [(place, place ^ apart) for place in range(coun...]
    ppermute x13 -> x20, waiting for transfers between devices: 37.2 us -> 31 us  [swapped(): lax.ppermute(value, axis, [(place, place ^ apart) for place in range(coun...]
    all_to_all x1 -> x0, starting transfers between devices: 3.71 us -> none  [gathered_plan(): turned = lax.all_to_all(turned, 'seq', 0, 0)]
    pallas_call x7, Pallas kernels: 16.6 us -> 14.6 us  [kernel_call(): pl.pallas_call(body, out_shape=outs, in_specs=[vmem if place in in_vmem e...]
    unnamed x14 -> x12, local copies, waits for them, and re-layouts: 1.09 us -> 2.01 us
  transfers between devices with their start and end apart: 14 -> 20, of which waited for: 9 -> 8; matrix products, arithmetic and copies ran while one was open for 0% -> 0% of each run, Pallas kernels for 14% -> 15%
where the time goes in v9:
time: 68.3 us; the launch traced here: 68.1 us
  waiting for transfers between devices  31 us (45%)
  starting transfers between devices  19.7 us (29%)
  Pallas kernels  14.6 us (21%)
  local copies, waits for them, and re-layouts  2.01 us (3%)
  between operations  0.72 us (1%)
    ppermute x20, waiting for transfers between devices, swapped(): lax.ppermute(value, axis, [(place, place ^ apart) for place in range(coun...  31 us
    ppermute x20, starting transfers between devices, swapped(): lax.ppermute(value, axis, [(place, place ^ apart) for place in range(coun...  19.7 us
    pallas_call x7, Pallas kernels, kernel_call(): pl.pallas_call(body, out_shape=outs, in_specs=[vmem if place in in_vmem e...  14.6 us
    unnamed x12, local copies, waits for them, and re-layouts  2.01 us
  transfers between devices with their start and end apart: 20, of which 8 were waited for; matrix products, arithmetic and copies ran while one was open for 0% of the time, Pallas kernels for 15%

profile of v9, /device:TPU:0, one launch (start us, length us, event | category | flops | bytes accessed | tf_op | source)
XLA Modules:
  0.0 68.1 jit_solution(15423580270147508180)
XLA Ops:
  0.6 3.8 %shard_map.112 = (bf16[128,768]{1,0:T(8,128)(2,1)}, bf16[128,768]{1,0:T(8,128)(2,1)}) custom-call(bf16[128,2304]{1,0:T(8,128)(2,1)} %cot_hbm.3, bf16[512,2304]{1,0:T(8,128)(2,1)} %weight_hbm.1, bf16[128,512]{1,0:T(8,128)(2,1)} %q_hbm.1, bf16[128,256]{1,0:T(8,128)(2,1)} %k_hbm.1, bf16[128,256]{1,0:T(8,128)(2,1)} %v_hbm.1), custom_call_target="tpu_custom_call" | custom-call | flops 301989888 | bytes 2949120 | tf_op jit(solution)/shard_map/pallas_call | solution.py:275
  4.5 3.0 %collective-permute-start.1 = (bf16[128,768]{1,0:T(8,128)(2,1)}, bf16[128,768]{1,0:T(8,128)(2,1)S(1)}, u32[]{:S(2)}, u32[]{:S(2)}) collective-permute-start(bf16[128,768]{1,0:T(8,128)(2,1)} %get-tuple-element.25.refs_0_), channel_id=1, source_target_pairs={{0,8},{4,12},{8,0},{12,4},{16,24},{20,28},{24,16},{28,20},{1,9},{5... | collective-permute-start | bytes 589832 | tf_op jit(solution)/shard_map/ppermute | solution.py:288
  8.2 1.0 %collective-permute-start = (bf16[128,768]{1,0:T(8,128)(2,1)}, bf16[128,768]{1,0:T(8,128)(2,1)S(1)}, u32[]{:S(2)}, u32[]{:S(2)}) collective-permute-start(bf16[128,768]{1,0:T(8,128)(2,1)} %get-tuple-element.26), channel_id=1, source_target_pairs={{0,4},{4,0},{8,12},{12,8},{16,20},{20,16},{24,28},{28,24},{1,5},{5... | collective-permute-start | bytes 589832 | tf_op jit(solution)/shard_map/ppermute | solution.py:288
  9.7 3.5 %collective-permute-done.1._.refs_2_ = bf16[128,768]{1,0:T(8,128)(2,1)S(1)} collective-permute-done((bf16[128,768]{1,0:T(8,128)(2,1)}, bf16[128,768]{1,0:T(8,128)(2,1)S(1)}, u32[]{:S(2)}, u32[]{:S(2)}) %collective-permute-start.1) | collective-permute-done | bytes 196640 | tf_op jit(solution)/shard_map/ppermute | solution.py:288
  13.1 2.4 %collective-permute-start.5 = (bf16[128,768]{1,0:T(8,128)(2,1)S(1)}, bf16[128,768]{1,0:T(8,128)(2,1)S(1)}, u32[]{:S(2)}, u32[]{:S(2)}) collective-permute-start(bf16[128,768]{1,0:T(8,128)(2,1)S(1)} %collective-permute-done.1._.refs_2_), channel_id=1, source_target_pairs={{0,16},{4,20},{8,24},{12,28},{16,0},{20,4},{24,8},{28,12},{1,17},{... | collective-permute-start | bytes 589832 | tf_op jit(solution)/shard_map/ppermute | solution.py:288
  15.5 1.5 %collective-permute-start.6 = (bf16[128,768]{1,0:T(8,128)(2,1)S(1)}, bf16[128,768]{1,0:T(8,128)(2,1)S(1)}, u32[]{:S(2)}, u32[]{:S(2)}) collective-permute-start(bf16[128,768]{1,0:T(8,128)(2,1)S(1)} %collective-permute-done.4.__.refs_5_), channel_id=1, source_target_pairs={{0,8},{4,12},{8,0},{12,4},{16,24},{20,28},{24,16},{28,20},{1,9},{5... | collective-permute-start | bytes 589832 | tf_op jit(solution)/shard_map/ppermute | solution.py:288
  17.0 1.1 %copy-done.4 = bf16[128,2304]{1,0:T(8,128)(2,1)S(1)} copy-done((bf16[128,2304]{1,0:T(8,128)(2,1)S(1)}, bf16[128,2304]{1,0:T(8,128)(2,1)}, u32[]{:S(2)}) %copy-start.4) | copy-done | bytes 589848
  18.1 0.8 %shard_map.113 = (bf16[2,288,128]{2,1,0:T(8,128)(2,1)S(1)}, bf16[2,288,128]{2,1,0:T(8,128)(2,1)S(1)}, bf16[2,288,128]{2,1,0:T(8,128)(2,1)S(1)}, bf16[2,288,128]{...) custom-call(bf16[128,2304]{1,0:T(8,128)(2,1)S(1)} %copy-done.4, ...), custom_call_target="tpu_custom_call" | custom-call | bytes 2359296 | tf_op jit(solution)/shard_map/pallas_call | solution.py:275
  19.2 4.1 %collective-permute-done.5.refs_6_ = bf16[128,768]{1,0:T(8,128)(2,1)S(1)} collective-permute-done((bf16[128,768]{1,0:T(8,128)(2,1)S(1)}, bf16[128,768]{1,0:T(8,128)(2,1)S(1)}, u32[]{:S(2)}, u32[]{:S(2)}) %collective-permute-start.5) | collective-permute-done | bytes 196640 | tf_op jit(solution)/shard_map/ppermute | solution.py:288
  23.3 0.9 %copy-done.5 = bf16[128,768]{1,0:T(8,128)(2,1)S(1)} copy-done((bf16[128,768]{1,0:T(8,128)(2,1)S(1)}, bf16[128,768]{1,0:T(8,128)(2,1)}, u32[]{:S(2)}) %copy-start.5) | copy-done | bytes 196632
  24.3 5.5 %shard_map.114 = (bf16[128,512]{1,0:T(8,128)(2,1)S(1)}, bf16[128,512]{1,0:T(8,128)(2,1)S(1)}, bf16[256,1024]{1,0:T(8,128)(2,1)S(1)}, bf16[1024,128]{1,0:T(8,128)(2,1)S(1)}) custom-call(bf16[128,768]{1,0:T(8,128)(2,1)S(1)} %copy-done.5, bf16[128,768]{1,0:T(8,128)(2,1)S(1)} %collective-permute-done.refs_1_, ...), custom_call_target="tpu_custom_call" | custom-call | flops 2147483648 | bytes 1572864 | tf_op jit(solution)/shard_map/pallas_call | solution.py:275
  30.0 1.7 %collective-permute-start.11 = (bf16[2,288,128]{2,1,0:T(8,128)(2,1)S(1)}, bf16[2,288,128]{2,1,0:T(8,128)(2,1)S(1)}, u32[]{:S(2)}, u32[]{:S(2)}) collective-permute-start(bf16[2,288,128]{2,1,0:T(8,128)(2,1)S(1)} %get-tuple-element.33), channel_id=1, source_target_pairs={{0,12},{4,8},{8,4},{12,0},{16,28},{20,24},{24,20},{28,16},{1,13},{... | collective-permute-start | bytes 442376 | tf_op jit(solution)/shard_map/ppermute | solution.py:288
  31.8 0.9 %collective-permute-start.12 = (bf16[2,288,128]{2,1,0:T(8,128)(2,1)S(1)}, bf16[2,288,128]{2,1,0:T(8,128)(2,1)S(1)}, u32[]{:S(2)}, u32[]{:S(2)}) collective-permute-start(bf16[2,288,128]{2,1,0:T(8,128)(2,1)S(1)} %get-tuple-element.34), channel_id=1, source_target_pairs={{0,16},{4,20},{8,24},{12,28},{16,0},{20,4},{24,8},{28,12},{1,17},{... | collective-permute-start | bytes 442376 | tf_op jit(solution)/shard_map/ppermute | solution.py:288
  32.8 3.8 %collective-permute-done.10.refs_2_ = bf16[2,288,128]{2,1,0:T(8,128)(2,1)S(1)} collective-permute-done((bf16[2,288,128]{2,1,0:T(8,128)(2,1)S(1)}, bf16[2,288,128]{2,1,0:T(8,128)(2,1)S(1)}, u32[]{:S(2)}, u32[]{:S(2)}) %collective-permute-start.10) | collective-permute-done | bytes 147488 | tf_op jit(solution)/shard_map/ppermute | solution.py:288
  36.6 2.3 %collective-permute-done.11.refs_3_ = bf16[2,288,128]{2,1,0:T(8,128)(2,1)S(1)} collective-permute-done((bf16[2,288,128]{2,1,0:T(8,128)(2,1)S(1)}, bf16[2,288,128]{2,1,0:T(8,128)(2,1)S(1)}, u32[]{:S(2)}, u32[]{:S(2)}) %collective-permute-start.11) | collective-permute-done | bytes 147488 | tf_op jit(solution)/shard_map/ppermute | solution.py:288
  39.7 0.8 %collective-permute-start.14 = (bf16[2,288,128]{2,1,0:T(8,128)(2,1)S(1)}, bf16[2,288,128]{2,1,0:T(8,128)(2,1)S(1)}, u32[]{:S(2)}, u32[]{:S(2)}) collective-permute-start(bf16[2,288,128]{2,1,0:T(8,128)(2,1)S(1)} %get-tuple-element.36), channel_id=1, source_target_pairs={{0,24},{4,28},{8,16},{12,20},{16,8},{20,12},{24,0},{28,4},{1,25},{... | collective-permute-start | bytes 442376 | tf_op jit(solution)/shard_map/ppermute | solution.py:288
  40.5 1.6 %collective-permute-start.15 = (bf16[2,288,128]{2,1,0:T(8,128)(2,1)S(1)}, bf16[2,288,128]{2,1,0:T(8,128)(2,1)S(1)}, u32[]{:S(2)}, u32[]{:S(2)}) collective-permute-start(bf16[2,288,128]{2,1,0:T(8,128)(2,1)S(1)} %get-tuple-element.37), channel_id=1, source_target_pairs={{0,28},{4,24},{8,20},{12,16},{16,12},{20,8},{24,4},{28,0},{1,29},{... | collective-permute-start | bytes 442376 | tf_op jit(solution)/shard_map/ppermute | solution.py:288
  42.2 0.8 %shard_map.116 = (bf16[576,128]{1,0:T(8,128)(2,1)S(1)}, f32[576,128]{1,0:T(8,128)S(1)}) custom-call(bf16[128,512]{1,0:T(8,128)(2,1)S(1)} %get-tuple-element.39.own_ref, bf16[128,512]{1,0:T(8,128)(2,1)S(1)} %collective-permute-done.16.far_ref, bf16[2304,512]{1,0:T(8,128)(2,1)S(1)} %copy-done, bf16[2304,256]{1,0:T(8,128)(2,1)S(1)} %copy-done.1, ...), custom_call_target="tpu_custom_call" | custom-call | flops 301989888 | bytes 2359296 | tf_op jit(solution)/shard_map/pallas_call | solution.py:275
  43.0 0.8 %shard_map.117 = (bf16[576,128]{1,0:T(8,128)(2,1)S(1)}, bf16[576,128]{1,0:T(8,128)(2,1)S(1)}) custom-call(bf16[128,512]{1,0:T(8,128)(2,1)S(1)} %get-tuple-element.39.own_ref, bf16[128,512]{1,0:T(8,128)(2,1)S(1)} %collective-permute-done.16.far_ref, bf16[2304,512]{1,0:T(8,128)(2,1)S(1)} %copy-done, bf16[2304,256]{1,0:T(8,128)(2,1)S(1)} %copy-done.1, ...), custom_call_target="tpu_custom_call" | custom-call | flops 301989888 | bytes 2359296 | tf_op jit(solution)/shard_map/pallas_call | solution.py:275
  43.8 7.1 %collective-permute-done.13.refs_5_ = bf16[2,288,128]{2,1,0:T(8,128)(2,1)S(1)} collective-permute-done((bf16[2,288,128]{2,1,0:T(8,128)(2,1)S(1)}, bf16[2,288,128]{2,1,0:T(8,128)(2,1)S(1)}, u32[]{:S(2)}, u32[]{:S(2)}) %collective-permute-start.13) | collective-permute-done | bytes 147488 | tf_op jit(solution)/shard_map/ppermute | solution.py:288
  51.0 3.6 %collective-permute-start.17 = (bf16[576,128]{1,0:T(8,128)(2,1)S(1)}, bf16[576,128]{1,0:T(8,128)(2,1)S(1)}, u32[]{:S(2)}, u32[]{:S(2)}) collective-permute-start(bf16[576,128]{1,0:T(8,128)(2,1)S(1)} %get-tuple-element.42), channel_id=1, source_target_pairs={{0,3},{1,2},{2,1},{3,0},{4,7},{5,6},{6,5},{7,4},{8,11},{9,10},{10,... | collective-permute-start | bytes 442376 | tf_op jit(solution)/shard_map/ppermute | solution.py:288
  55.4 2.0 %shard_map.115 = (f32[288,256]{1,0:T(8,128)}, f32[288,512]{1,0:T(8,128)}, f32[8,128]{1,0:T(8,128)S(1)}) custom-call(bf16[256,1024]{1,0:T(8,128)(2,1)S(1)} %get-tuple-element.28.attn_ref, bf16[256,1024]{1,0:T(8,128)(2,1)S(1)} %collective-permute-done.7.far_attn_ref, bf16[1024,128]{1,0:T(8,128)(2,1)S(1)} %get-tuple-element.29.dv_ref, ...), custom_call_target="tpu_custom_call" | custom-call | flops 452984832 | bytes 2064384 | tf_op jit(solution)/shard_map/pallas_call | solution.py:275
  57.4 2.1 %collective-permute-done.17.refs_0_ = bf16[576,128]{1,0:T(8,128)(2,1)S(1)} collective-permute-done((bf16[576,128]{1,0:T(8,128)(2,1)S(1)}, bf16[576,128]{1,0:T(8,128)(2,1)S(1)}, u32[]{:S(2)}, u32[]{:S(2)}) %collective-permute-start.17) | collective-permute-done | bytes 147488 | tf_op jit(solution)/shard_map/ppermute | solution.py:288
  59.5 7.9 %collective-permute-done.18.refs_1_ = bf16[576,128]{1,0:T(8,128)(2,1)S(1)} collective-permute-done((bf16[576,128]{1,0:T(8,128)(2,1)S(1)}, bf16[576,128]{1,0:T(8,128)(2,1)S(1)}, u32[]{:S(2)}, u32[]{:S(2)}) %collective-permute-start.18) | collective-permute-done | bytes 147488 | tf_op jit(solution)/shard_map/ppermute | solution.py:288
  (35 shorter events, 4.1 us)
Async XLA Ops:
  0.6 16.4 %copy-start.3 = (bf16[128,2304]{1,0:T(8,128)(2,1)S(1)}, bf16[128,2304]{1,0:T(8,128)(2,1)}, u32[]{:S(2)}) copy-start(bf16[128,2304]{1,0:T(8,128)(2,1)} %cot_hbm.3) | copy-start | bytes 1769476
  4.5 8.6 %collective-permute-start.1 = (bf16[128,768]{1,0:T(8,128)(2,1)}, bf16[128,768]{1,0:T(8,128)(2,1)S(1)}, u32[]{:S(2)}, u32[]{:S(2)}) collective-permute-start(bf16[128,768]{1,0:T(8,128)(2,1)} %get-tuple-element.25.refs_0_), channel_id=1, source_target_pairs={{0,8},{4,12},{8,0},{12,4},{16,24},{20,28},{24,16},{28,20},{1,9},{5... | collective-permute-start | bytes 589832 | tf_op jit(solution)/shard_map/ppermute | solution.py:288
  7.5 8.0 %collective-permute-start.4 = (bf16[128,768]{1,0:T(8,128)(2,1)}, bf16[128,768]{1,0:T(8,128)(2,1)S(1)}, u32[]{:S(2)}, u32[]{:S(2)}) collective-permute-start(bf16[128,768]{1,0:T(8,128)(2,1)} %get-tuple-element.26), channel_id=1, source_target_pairs={{0,20},{4,16},{8,28},{12,24},{16,4},{20,0},{24,12},{28,8},{1,21},{... | collective-permute-start | bytes 589832 | tf_op jit(solution)/shard_map/ppermute | solution.py:288
  8.2 10.7 %collective-permute-start = (bf16[128,768]{1,0:T(8,128)(2,1)}, bf16[128,768]{1,0:T(8,128)(2,1)S(1)}, u32[]{:S(2)}, u32[]{:S(2)}) collective-permute-start(bf16[128,768]{1,0:T(8,128)(2,1)} %get-tuple-element.26), channel_id=1, source_target_pairs={{0,4},{4,0},{8,12},{12,8},{16,20},{20,16},{24,28},{28,24},{1,5},{5... | collective-permute-start | bytes 589832 | tf_op jit(solution)/shard_map/ppermute | solution.py:288
  9.1 9.9 %collective-permute-start.2 = (bf16[128,768]{1,0:T(8,128)(2,1)}, bf16[128,768]{1,0:T(8,128)(2,1)S(1)}, u32[]{:S(2)}, u32[]{:S(2)}) collective-permute-start(bf16[128,768]{1,0:T(8,128)(2,1)} %get-tuple-element.26), channel_id=1, source_target_pairs={{0,12},{4,8},{8,4},{12,0},{16,28},{20,24},{24,20},{28,16},{1,13},{... | collective-permute-start | bytes 589832 | tf_op jit(solution)/shard_map/ppermute | solution.py:288
  9.3 9.9 %collective-permute-start.3 = (bf16[128,768]{1,0:T(8,128)(2,1)}, bf16[128,768]{1,0:T(8,128)(2,1)S(1)}, u32[]{:S(2)}, u32[]{:S(2)}) collective-permute-start(bf16[128,768]{1,0:T(8,128)(2,1)} %get-tuple-element.25.refs_0_), channel_id=1, source_target_pairs={{0,16},{4,20},{8,24},{12,28},{16,0},{20,4},{24,8},{28,12},{1,17},{... | collective-permute-start | bytes 589832 | tf_op jit(solution)/shard_map/ppermute | solution.py:288
  13.1 10.2 %collective-permute-start.5 = (bf16[128,768]{1,0:T(8,128)(2,1)S(1)}, bf16[128,768]{1,0:T(8,128)(2,1)S(1)}, u32[]{:S(2)}, u32[]{:S(2)}) collective-permute-start(bf16[128,768]{1,0:T(8,128)(2,1)S(1)} %collective-permute-done.1._.refs_2_), channel_id=1, source_target_pairs={{0,16},{4,20},{8,24},{12,28},{16,0},{20,4},{24,8},{28,12},{1,17},{... | collective-permute-start | bytes 589832 | tf_op jit(solution)/shard_map/ppermute | solution.py:288
  15.5 7.8 %collective-permute-start.6 = (bf16[128,768]{1,0:T(8,128)(2,1)S(1)}, bf16[128,768]{1,0:T(8,128)(2,1)S(1)}, u32[]{:S(2)}, u32[]{:S(2)}) collective-permute-start(bf16[128,768]{1,0:T(8,128)(2,1)S(1)} %collective-permute-done.4.__.refs_5_), channel_id=1, source_target_pairs={{0,8},{4,12},{8,0},{12,4},{16,24},{20,28},{24,16},{28,20},{1,9},{5... | collective-permute-start | bytes 589832 | tf_op jit(solution)/shard_map/ppermute | solution.py:288
  18.9 13.8 %collective-permute-start.9 = (bf16[2,288,128]{2,1,0:T(8,128)(2,1)S(1)}, bf16[2,288,128]{2,1,0:T(8,128)(2,1)S(1)}, u32[]{:S(2)}, u32[]{:S(2)}) collective-permute-start(bf16[2,288,128]{2,1,0:T(8,128)(2,1)S(1)} %get-tuple-element.31), channel_id=1, source_target_pairs={{0,4},{4,0},{8,12},{12,8},{16,20},{20,16},{24,28},{28,24},{1,5},{5... | collective-permute-start | bytes 442376 | tf_op jit(solution)/shard_map/ppermute | solution.py:288
  24.3 17.9 %copy-start = (bf16[2304,512]{1,0:T(8,128)(2,1)S(1)}, bf16[2304,512]{1,0:T(8,128)(2,1)}, u32[]{:S(2)}) copy-start(bf16[2304,512]{1,0:T(8,128)(2,1)} %wq_ref.3) | copy-start | bytes 7077892
  24.3 17.9 %copy-start.1 = (bf16[2304,256]{1,0:T(8,128)(2,1)S(1)}, bf16[2304,256]{1,0:T(8,128)(2,1)}, u32[]{:S(2)}) copy-start(bf16[2304,256]{1,0:T(8,128)(2,1)} %wk_ref.3) | copy-start | bytes 3538948
  24.3 17.9 %copy-start.2 = (bf16[2304,256]{1,0:T(8,128)(2,1)S(1)}, bf16[2304,256]{1,0:T(8,128)(2,1)}, u32[]{:S(2)}) copy-start(bf16[2304,256]{1,0:T(8,128)(2,1)} %wv_ref.3) | copy-start | bytes 3538948
  29.8 25.5 %collective-permute-start.7 = (bf16[256,1024]{1,0:T(8,128)(2,1)S(1)}, bf16[256,1024]{1,0:T(8,128)(2,1)S(1)}, u32[]{:S(2)}, u32[]{:S(2)}) collective-permute-start(bf16[256,1024]{1,0:T(8,128)(2,1)S(1)} %get-tuple-element.28.attn_ref), channel_id=1, source_target_pairs={{0,4},{4,0},{8,12},{12,8},{16,20},{20,16},{24,28},{28,24},{1,5},{5... | collective-permute-start | bytes 1572872 | tf_op jit(solution)/shard_map/ppermute | solution.py:288
  30.0 6.7 %collective-permute-start.10 = (bf16[2,288,128]{2,1,0:T(8,128)(2,1)S(1)}, bf16[2,288,128]{2,1,0:T(8,128)(2,1)S(1)}, u32[]{:S(2)}, u32[]{:S(2)}) collective-permute-start(bf16[2,288,128]{2,1,0:T(8,128)(2,1)S(1)} %get-tuple-element.32), channel_id=1, source_target_pairs={{0,8},{4,12},{8,0},{12,4},{16,24},{20,28},{24,16},{28,20},{1,9},{5... | collective-permute-start | bytes 442376 | tf_op jit(solution)/shard_map/ppermute | solution.py:288
  30.0 8.8 %collective-permute-start.11 = (bf16[2,288,128]{2,1,0:T(8,128)(2,1)S(1)}, bf16[2,288,128]{2,1,0:T(8,128)(2,1)S(1)}, u32[]{:S(2)}, u32[]{:S(2)}) collective-permute-start(bf16[2,288,128]{2,1,0:T(8,128)(2,1)S(1)} %get-tuple-element.33), channel_id=1, source_target_pairs={{0,12},{4,8},{8,4},{12,0},{16,28},{20,24},{24,20},{28,16},{1,13},{... | collective-permute-start | bytes 442376 | tf_op jit(solution)/shard_map/ppermute | solution.py:288
  31.8 7.9 %collective-permute-start.12 = (bf16[2,288,128]{2,1,0:T(8,128)(2,1)S(1)}, bf16[2,288,128]{2,1,0:T(8,128)(2,1)S(1)}, u32[]{:S(2)}, u32[]{:S(2)}) collective-permute-start(bf16[2,288,128]{2,1,0:T(8,128)(2,1)S(1)} %get-tuple-element.34), channel_id=1, source_target_pairs={{0,16},{4,20},{8,24},{12,28},{16,0},{20,4},{24,8},{28,12},{1,17},{... | collective-permute-start | bytes 442376 | tf_op jit(solution)/shard_map/ppermute | solution.py:288
  32.7 7.8 %collective-permute-start.16 = (bf16[128,512]{1,0:T(8,128)(2,1)S(1)}, bf16[128,512]{1,0:T(8,128)(2,1)S(1)}, u32[]{:S(2)}, u32[]{:S(2)}) collective-permute-start(bf16[128,512]{1,0:T(8,128)(2,1)S(1)} %get-tuple-element.40), channel_id=1, source_target_pairs={{0,4},{4,0},{8,12},{12,8},{16,20},{20,16},{24,28},{28,24},{1,5},{5... | collective-permute-start | bytes 393224 | tf_op jit(solution)/shard_map/ppermute | solution.py:288
  36.6 18.7 %collective-permute-start.8 = (bf16[1024,128]{1,0:T(8,128)(2,1)S(1)}, bf16[1024,128]{1,0:T(8,128)(2,1)S(1)}, u32[]{:S(2)}, u32[]{:S(2)}) collective-permute-start(bf16[1024,128]{1,0:T(8,128)(2,1)S(1)} %get-tuple-element.29.dv_ref), channel_id=1, source_target_pairs={{0,4},{4,0},{8,12},{12,8},{16,20},{20,16},{24,28},{28,24},{1,5},{5... | collective-permute-start | bytes 786440 | tf_op jit(solution)/shard_map/ppermute | solution.py:288
  38.9 12.1 %collective-permute-start.13 = (bf16[2,288,128]{2,1,0:T(8,128)(2,1)S(1)}, bf16[2,288,128]{2,1,0:T(8,128)(2,1)S(1)}, u32[]{:S(2)}, u32[]{:S(2)}) collective-permute-start(bf16[2,288,128]{2,1,0:T(8,128)(2,1)S(1)} %get-tuple-element.35), channel_id=1, source_target_pairs={{0,20},{4,16},{8,28},{12,24},{16,4},{20,0},{24,12},{28,8},{1,21},{... | collective-permute-start | bytes 442376 | tf_op jit(solution)/shard_map/ppermute | solution.py:288
  39.7 14.9 %collective-permute-start.14 = (bf16[2,288,128]{2,1,0:T(8,128)(2,1)S(1)}, bf16[2,288,128]{2,1,0:T(8,128)(2,1)S(1)}, u32[]{:S(2)}, u32[]{:S(2)}) collective-permute-start(bf16[2,288,128]{2,1,0:T(8,128)(2,1)S(1)} %get-tuple-element.36), channel_id=1, source_target_pairs={{0,24},{4,28},{8,16},{12,20},{16,8},{20,12},{24,0},{28,4},{1,25},{... | collective-permute-start | bytes 442376 | tf_op jit(solution)/shard_map/ppermute | solution.py:288
  40.5 14.1 %collective-permute-start.15 = (bf16[2,288,128]{2,1,0:T(8,128)(2,1)S(1)}, bf16[2,288,128]{2,1,0:T(8,128)(2,1)S(1)}, u32[]{:S(2)}, u32[]{:S(2)}) collective-permute-start(bf16[2,288,128]{2,1,0:T(8,128)(2,1)S(1)} %get-tuple-element.37), channel_id=1, source_target_pairs={{0,28},{4,24},{8,20},{12,16},{16,12},{20,8},{24,4},{28,0},{1,29},{... | collective-permute-start | bytes 442376 | tf_op jit(solution)/shard_map/ppermute | solution.py:288
  51.0 8.6 %collective-permute-start.17 = (bf16[576,128]{1,0:T(8,128)(2,1)S(1)}, bf16[576,128]{1,0:T(8,128)(2,1)S(1)}, u32[]{:S(2)}, u32[]{:S(2)}) collective-permute-start(bf16[576,128]{1,0:T(8,128)(2,1)S(1)} %get-tuple-element.42), channel_id=1, source_target_pairs={{0,3},{1,2},{2,1},{3,0},{4,7},{5,6},{6,5},{7,4},{8,11},{9,10},{10,... | collective-permute-start | bytes 442376 | tf_op jit(solution)/shard_map/ppermute | solution.py:288
  54.6 12.8 %collective-permute-start.18 = (bf16[576,128]{1,0:T(8,128)(2,1)S(1)}, bf16[576,128]{1,0:T(8,128)(2,1)S(1)}, u32[]{:S(2)}, u32[]{:S(2)}) collective-permute-start(bf16[576,128]{1,0:T(8,128)(2,1)S(1)} %get-tuple-element.43), channel_id=1, source_target_pairs={{0,2},{1,3},{2,0},{3,1},{4,6},{5,7},{6,4},{7,5},{8,10},{9,11},{10,... | collective-permute-start | bytes 442376 | tf_op jit(solution)/shard_map/ppermute | solution.py:288
  54.6 12.8 %collective-permute-start.19 = (bf16[576,128]{1,0:T(8,128)(2,1)S(1)}, bf16[576,128]{1,0:T(8,128)(2,1)S(1)}, u32[]{:S(2)}, u32[]{:S(2)}) collective-permute-start(bf16[576,128]{1,0:T(8,128)(2,1)S(1)} %get-tuple-element.44), channel_id=1, source_target_pairs={{0,1},{1,0},{2,3},{3,2},{4,5},{5,4},{6,7},{7,6},{8,9},{9,8},{10,11... | collective-permute-start | bytes 442376 | tf_op jit(solution)/shard_map/ppermute | solution.py:288
  (2 other events, 2.0 us)

commit v10 on v8

--- a/solution.py
+++ b/solution.py
@@ -80,11 +80,14 @@
         copy.wait()
 
 
-def turn_kernel(parts, normed_hbm, cot_hbm, _, __, turned_ref, done_ref, normed_ref, cot_ref, sem):
+def turn_kernel(
+    parts, normed_hbm, cot_hbm, block_hbm, _, turned_ref, own_ref, normed_ref, cot_ref, sem
+):
     cut = normed_ref.shape[1] // parts
-    done_ref[...] = jnp.zeros_like(done_ref)
     copies = []
-    for which, (source, target) in enumerate(((normed_hbm, normed_ref), (cot_hbm, cot_ref))):
+    for which, (source, target) in enumerate(
+        ((normed_hbm, normed_ref), (cot_hbm, cot_ref), (block_hbm, own_ref))
+    ):
         copies.append(pltpu.make_async_copy(source, target, sem.at[which]))
         copies[-1].start()
     for which, ref in enumerate((normed_ref, cot_ref)):
@@ -92,6 +95,7 @@
         turned = ref[...].astype(jnp.float32).T.astype(jnp.bfloat16)
         for part in range(parts):
             turned_ref[part, which] = turned[part * cut : (part + 1) * cut]
+    copies[2].wait()
 
 
 def attention_kernel(blocks, *refs):
@@ -103,8 +107,8 @@
     _,
     dx_own_ref,
     dx_far_ref,
-    attn_ref,
-    dv_ref,
+    parts_ref,
+    __,
     gathered_ref,
     score_even_ref,
     score_odd_ref,
@@ -165,7 +169,7 @@
         inverse = 1.0 / jnp.sum(total, axis=0, keepdims=True)
         attn = dot_nn(value_t_ref[:, :span], prob_ref[:span, lanes]) * inverse
         for h in range(heads):
-            attn_ref[h * HEAD_SIZE : (h + 1) * HEAD_SIZE, own] = attn[
+            parts_ref[h * HEAD_SIZE : (h + 1) * HEAD_SIZE, own] = attn[
                 :, h * size : (h + 1) * size
             ].astype(jnp.bfloat16)
         grads_t = jnp.concatenate(
@@ -185,9 +189,9 @@
 
     for step in range(steps):
         own = slice(step * size, (step + 1) * size)
-        dv_ref[own] = dot_nt(prob_ref[own, step * wide :], grad_t_ref[:, step * wide :]).astype(
-            jnp.bfloat16
-        )
+        parts_ref[heads * HEAD_SIZE :, own] = dot_nt(
+            grad_t_ref[:, step * wide :], prob_ref[own, step * wide :]
+        ).astype(jnp.bfloat16)
 
     dq_t_ref[...] = jnp.zeros_like(dq_t_ref)
     dk_ref[...] = jnp.zeros_like(dk_ref)
@@ -217,7 +221,7 @@
                 .T.astype(jnp.bfloat16)
             )
         target[:, key_cols] = (logit_scale * dk_ref[at(half, rows)]).astype(jnp.bfloat16)
-        target[:, value_cols] = dv_ref[at(2 * chip + half, rows)]
+        target[:, value_cols] = parts_ref[heads * HEAD_SIZE :, at(2 * chip + half, rows)].T
 
 
 def input_terms_kernel(
@@ -247,7 +251,7 @@
 
 
 def weight_grad_kernel(
-    turned_ref, attn_ref, far_attn_ref, dv_ref, far_dv_ref, wvalue_ref, woutput_ref, done_ref, joined_ref
+    turned_ref, own_ref, far_ref, wvalue_ref, woutput_ref, done_ref, joined_ref
 ):
     done_ref[...] = jnp.zeros_like(done_ref)
     core = lax.axis_index("seq") % 2
@@ -255,9 +259,11 @@
     rows = turned_ref.shape[3]
     for part in range(parts):
         joined_ref[:, :, part * rows : (part + 1) * rows] = turned_ref[part]
-    for half, attn, dv in ((core, attn_ref, dv_ref), (1 - core, far_attn_ref, far_dv_ref)):
-        wvalue_ref[:, at(half, dv.shape[1])] = dot_nn(joined_ref[0], dv[...])
-        woutput_ref[:, at(half, attn.shape[0])] = dot_nt(joined_ref[1], attn[...])
+    kv_cols = wvalue_ref.shape[1] // 2
+    q_cols = woutput_ref.shape[1] // 2
+    for half, ref in ((core, own_ref), (1 - core, far_ref)):
+        woutput_ref[:, at(half, q_cols)] = dot_nt(joined_ref[1], ref[:q_cols])
+        wvalue_ref[:, at(half, kv_cols)] = dot_nt(joined_ref[0], ref[q_cols:])
 
 
 def sum_kernel(_, own_ref, *refs):
@@ -267,14 +273,18 @@
     refs[-1][...] = total.astype(jnp.bfloat16)
 
 
-def kernel_call(body, outs, operands, in_vmem=(), scratch=(), flops=0, moved=0, room=16):
+def kernel_call(
+    body, outs, operands, in_vmem=(), scratch=(), flops=0, moved=0, room=16,
+    out_hbm=(), aliases={},
+):
     vmem = pl.BlockSpec(memory_space=pltpu.VMEM)
     hbm = pl.BlockSpec(memory_space=pltpu.HBM)
     return pl.pallas_call(
         body,
         out_shape=outs,
         in_specs=[vmem if place in in_vmem else hbm for place in range(len(operands))],
-        out_specs=jax.tree.map(lambda _: vmem, outs),
+        out_specs=tuple(hbm if place in out_hbm else vmem for place in range(len(outs))),
+        input_output_aliases=aliases,
         scratch_shapes=list(scratch),
         compiler_params=pltpu.CompilerParams(vmem_limit_bytes=room * 1024 * 1024),
         cost_estimate=pl.CostEstimate(flops=flops, bytes_accessed=moved, transcendentals=0),
@@ -331,28 +341,30 @@
         else:
             held[apart] = swapped(held[apart ^ through], "seq", through)
     held[1] = swapped(other, "seq", 1)
-    turned, turn_done = kernel_call(
+    turned, own_block = kernel_call(
         functools.partial(turn_kernel, blocks),
-        (shape((blocks, 2, model // blocks, rows), bf16), shape((8, HEAD_SIZE), f32)),
-        (normed_input, out_cotangent, held[2], held[blocks // 2 + 1]),
+        (shape((blocks, 2, model // blocks, rows), bf16), shape((rows, packed_cols), bf16)),
+        (normed_input, out_cotangent, same, held[2]),
         scratch=(
             pltpu.VMEM(normed_input.shape, bf16),
             pltpu.VMEM(out_cotangent.shape, bf16),
-            pltpu.SemaphoreType.DMA((2,)),
+            pltpu.SemaphoreType.DMA((3,)),
         ),
-        moved=256 * rows * model,
-    )
-    turned = lax.all_to_all(turned, "seq", 0, 0)
-    dx_own, dx_far, attn, dv = kernel_call(
+        moved=8 * rows * model,
+    )
+    held[0] = own_block
+    dx_own, dx_far, grad_parts, turned = kernel_call(
         functools.partial(attention_kernel, blocks),
         (
             shape((rows, q_cols + 2 * kv_cols), bf16),
             shape((rows, q_cols + 2 * kv_cols), bf16),
-            shape((q_cols, tokens), bf16),
-            shape((tokens, kv_cols), bf16),
+            shape((q_cols + kv_cols, tokens), bf16),
+            shape(turned.shape, bf16),
         ),
-        [held[apart] for apart in range(blocks)] + [turn_done],
+        [held[apart] for apart in range(blocks)] + [turned],
         in_vmem=range(blocks),
+        out_hbm=(3,),
+        aliases={blocks: 3},
         scratch=(
             pltpu.VMEM((tokens, packed_cols), bf16),
             pltpu.VMEM((tokens, wide), f32),
@@ -370,6 +382,7 @@
         moved=2 * tokens * packed_cols,
     )
     dx_got = swapped(dx_far, "seq", 1)
+    turned = lax.all_to_all(turned, "seq", 0, 0)
     aparts = tuple(range(groups - 1, -1, -1))
     terms = {}
     for chosen in (aparts[: groups // 2], aparts[groups // 2 :]):
@@ -392,15 +405,15 @@
             shape((model // blocks, 2 * q_cols), f32),
             shape((8, HEAD_SIZE), f32),
         ),
-        (turned, attn, swapped(attn, "seq", 1), dv, swapped(dv, "seq", 1)),
-        in_vmem=range(5),
+        (turned, grad_parts, swapped(grad_parts, "seq", 1)),
+        in_vmem=range(3),
         scratch=(pltpu.VMEM((2, model // blocks, tokens), bf16),),
         flops=4 * tokens * (model // blocks) * (q_cols + kv_cols),
         moved=4 * (model // blocks) * (tokens + 2 * q_cols + 2 * kv_cols),
     )
-    grad_input = kernel_call(
+    (grad_input,) = kernel_call(
         sum_kernel,
-        shape((model // groups, rows), bf16),
+        (shape((model // groups, rows), bf16),),
         (weights_done, terms[0], *arrived),
         in_vmem=range(1, groups + 1),
         moved=4 * groups * (model // groups) * rows,

time: 72.5 us -> 62.2 us (0.86)
  waiting for transfers between devices: 37.2 us -> 13 us
  local copies, waits for them, and re-layouts: 1.09 us -> 11.3 us
  Pallas kernels: 16.6 us -> 18.3 us
  starting transfers between devices: 16.7 us -> 18.4 us
    ppermute x13 -> x12, waiting for transfers between devices: 37.2 us -> 10.1 us  [swapped(): lax.ppermute(value, axis, [(place, place ^ apart) for place in range(coun...]
    unnamed x14 -> x34, local copies, waits for them, and re-layouts: 1.09 us -> 11.3 us
    all_to_all x1, waiting for transfers between devices: 0.01 us -> 2.85 us  [gathered_plan(): turned = lax.all_to_all(turned, 'seq', 0, 0)]
    pallas_call x7, Pallas kernels: 16.6 us -> 18.3 us  [kernel_call(): pl.pallas_call(body, out_shape=outs, in_specs=[vmem if place in in_vmem e...]
    ppermute x13 -> x12, starting transfers between devices: 13 us -> 14.1 us  [swapped(): lax.ppermute(value, axis, [(place, place ^ apart) for place in range(coun...]
  transfers between devices with their start and end apart: 14 -> 13, of which waited for: 9 -> 5; matrix products, arithmetic and copies ran while one was open for 0% -> 0% of each run, Pallas kernels for 14% -> 11%
where the time goes in v10:
time: 62.2 us; the launch traced here: 61.7 us
  starting transfers between devices  18.4 us (30%)
  Pallas kernels  18.3 us (29%)
  waiting for transfers between devices  13 us (21%)
  local copies, waits for them, and re-layouts  11.3 us (18%)
  between operations  0.73 us (1%)
    pallas_call x7, Pallas kernels, kernel_call(): pl.pallas_call(body, out_shape=outs, in_specs=[vmem if place in in_vmem e...  18.3 us
    ppermute x12, starting transfers between devices, swapped(): lax.ppermute(value, axis, [(place, place ^ apart) for place in range(coun...  14.1 us
    unnamed x34, local copies, waits for them, and re-layouts  11.3 us
    ppermute x12, waiting for transfers between devices, swapped(): lax.ppermute(value, axis, [(place, place ^ apart) for place in range(coun...  10.1 us
    all_to_all x1, starting transfers between devices, gathered_plan(): turned = lax.all_to_all(turned, 'seq', 0, 0)  4.38 us
    all_to_all x1, waiting for transfers between devices, gathered_plan(): turned = lax.all_to_all(turned, 'seq', 0, 0)  2.85 us
  transfers between devices with their start and end apart: 13, of which 5 were waited for; matrix products, arithmetic and copies ran while one was open for 0% of the time, Pallas kernels for 11%

profile of v10, /device:TPU:0, one launch (start us, length us, event | category | flops | bytes accessed | tf_op | source)
XLA Modules:
  0.0 61.7 jit_solution(16447779087038606967)
XLA Ops:
  0.6 3.8 %shard_map.112 = (bf16[128,768]{1,0:T(8,128)(2,1)}, bf16[128,768]{1,0:T(8,128)(2,1)}) custom-call(bf16[128,2304]{1,0:T(8,128)(2,1)} %cot_hbm.3, bf16[512,2304]{1,0:T(8,128)(2,1)} %weight_hbm.1, bf16[128,512]{1,0:T(8,128)(2,1)} %q_hbm.1, bf16[128,256]{1,0:T(8,128)(2,1)} %k_hbm.1, bf16[128,256]{1,0:T(8,128)(2,1)} %v_hbm.1), custom_call_target="tpu_custom_call" | custom-call | flops 301989888 | bytes 2949120 | tf_op jit(solution)/shard_map/pallas_call | solution.py:282
  4.5 3.0 %collective-permute-start = (bf16[128,768]{1,0:T(8,128)(2,1)}, bf16[128,768]{1,0:T(8,128)(2,1)S(1)}, u32[]{:S(2)}, u32[]{:S(2)}) collective-permute-start(bf16[128,768]{1,0:T(8,128)(2,1)} %get-tuple-element.18.block_hbm), channel_id=1, source_target_pairs={{0,8},{4,12},{8,0},{12,4},{16,24},{20,28},{24,16},{28,20},{1,9},{5... | collective-permute-start | bytes 589832 | tf_op jit(solution)/shard_map/ppermute | solution.py:296
  9.7 3.4 %collective-permute-done._.refs_2_ = bf16[128,768]{1,0:T(8,128)(2,1)S(1)} collective-permute-done((bf16[128,768]{1,0:T(8,128)(2,1)}, bf16[128,768]{1,0:T(8,128)(2,1)S(1)}, u32[]{:S(2)}, u32[]{:S(2)}) %collective-permute-start) | collective-permute-done | bytes 196640 | tf_op jit(solution)/shard_map/ppermute | solution.py:296
  13.1 2.2 %collective-permute-start.5 = (bf16[128,768]{1,0:T(8,128)(2,1)S(1)}, bf16[128,768]{1,0:T(8,128)(2,1)S(1)}, u32[]{:S(2)}, u32[]{:S(2)}) collective-permute-start(bf16[128,768]{1,0:T(8,128)(2,1)S(1)} %collective-permute-done._.refs_2_), channel_id=1, source_target_pairs={{0,16},{4,20},{8,24},{12,28},{16,0},{20,4},{24,8},{28,12},{1,17},{... | collective-permute-start | bytes 589832 | tf_op jit(solution)/shard_map/ppermute | solution.py:296
  15.3 1.7 %collective-permute-start.6 = (bf16[128,768]{1,0:T(8,128)(2,1)S(1)}, bf16[128,768]{1,0:T(8,128)(2,1)S(1)}, u32[]{:S(2)}, u32[]{:S(2)}) collective-permute-start(bf16[128,768]{1,0:T(8,128)(2,1)S(1)} %collective-permute-done.4.refs_5_), channel_id=1, source_target_pairs={{0,8},{4,12},{8,0},{12,4},{16,24},{20,28},{24,16},{28,20},{1,9},{5... | collective-permute-start | bytes 589832 | tf_op jit(solution)/shard_map/ppermute | solution.py:296
  17.0 1.1 %copy-done.9 = bf16[128,2304]{1,0:T(8,128)(2,1)S(1)} copy-done((bf16[128,2304]{1,0:T(8,128)(2,1)S(1)}, bf16[128,2304]{1,0:T(8,128)(2,1)}, u32[]{:S(2)}) %copy-start.9) | copy-done | bytes 589848
  18.1 0.9 %copy-done.15 = bf16[128,768]{1,0:T(8,128)(2,1)S(1)} copy-done((bf16[128,768]{1,0:T(8,128)(2,1)S(1)}, bf16[128,768]{1,0:T(8,128)(2,1)}, u32[]{:S(2)}) %copy-start.15) | copy-done | bytes 196632
  19.0 1.0 %shard_map.113 = (bf16[8,2,288,128]{3,2,1,0:T(8,128)(2,1)S(1)}, bf16[128,768]{1,0:T(8,128)(2,1)S(1)}) custom-call(bf16[128,2304]{1,0:T(8,128)(2,1)S(1)} %copy-done.9, bf16[128,2304]{1,0:T(8,128)(2,1)S(1)} %copy-done.3, bf16[128,768]{1,0:T(8,128)(2,1)S(1)} %copy-done.15, bf16[128,768]{1,0:T(8,128)(2,1)S(1)} %collective-permute-done._.refs_2_), custom_call_target="tpu_custom_call" | custom-call | bytes 2359296 | tf_op jit(solution)/shard_map/pallas_call | solution.py:282
  20.1 3.3 %collective-permute-done.5.refs_6_ = bf16[128,768]{1,0:T(8,128)(2,1)S(1)} collective-permute-done((bf16[128,768]{1,0:T(8,128)(2,1)S(1)}, bf16[128,768]{1,0:T(8,128)(2,1)S(1)}, u32[]{:S(2)}, u32[]{:S(2)}) %collective-permute-start.5) | collective-permute-done | bytes 196640 | tf_op jit(solution)/shard_map/ppermute | solution.py:296
  23.3 5.7 %shard_map.114 = (bf16[128,512]{1,0:T(8,128)(2,1)S(1)}, bf16[128,512]{1,0:T(8,128)(2,1)S(1)}, bf16[384,1024]{1,0:T(8,128)(2,1)S(1)}, bf16[8,2,288,128]{3,2,1,0:T(8,128)(2,1)S(1)}) custom-call(bf16[128,768]{1,0:T(8,128)(2,1)S(1)} %get-tuple-element.19.refs_0_, bf16[128,768]{1,0:T(8,128)(2,1)S(1)} %collective-permute-done.1.refs_1_, ...), custom_call_target="tpu_custom_call", output_to_operand_aliasing={{3}: (8, {})} | custom-call | flops 2147483648 | bytes 1572864 | tf_op jit(solution)/shard_map/pallas_call | solution.py:282
  29.1 1.0 %copy-done.4 = bf16[8,2,288,128]{3,2,1,0:T(8,128)(2,1)} copy-done((bf16[8,2,288,128]{3,2,1,0:T(8,128)(2,1)}, bf16[8,2,288,128]{3,2,1,0:T(8,128)(2,1)S(1)}, u32[]{:S(2)}) %copy-start.4) | copy-done | bytes 1179672
  32.3 4.4 %all-to-all-start = ((bf16[8,2,288,128]{3,2,1,0:T(8,128)(2,1)}), bf16[8,2,288,128]{3,2,1,0:T(8,128)(2,1)}, u32[]{:S(2)}, u32[]{:S(2)}) async-start(bf16[8,2,288,128]{3,2,1,0:T(8,128)(2,1)} %copy-done.4), calls=%async_computation | async-start | bytes 2359296 | tf_op jit(solution)/shard_map/all_to_all | solution.py:385
  37.2 2.2 %collective-permute-done.8.far_ref = bf16[128,512]{1,0:T(8,128)(2,1)S(1)} collective-permute-done((bf16[128,512]{1,0:T(8,128)(2,1)}, bf16[128,512]{1,0:T(8,128)(2,1)S(1)}, u32[]{:S(2)}, u32[]{:S(2)}) %collective-permute-start.8) | collective-permute-done | bytes 131104 | tf_op jit(solution)/shard_map/ppermute | solution.py:296
  39.4 1.3 %copy-done.2 = bf16[2304,256]{1,0:T(8,128)(2,1)S(1)} copy-done((bf16[2304,256]{1,0:T(8,128)(2,1)S(1)}, bf16[2304,256]{1,0:T(8,128)(2,1)}, u32[]{:S(2)}) %copy-start.2) | copy-done | bytes 1179672
  40.7 0.9 %copy-done.11 = bf16[128,512]{1,0:T(8,128)(2,1)S(1)} copy-done((bf16[128,512]{1,0:T(8,128)(2,1)S(1)}, bf16[128,512]{1,0:T(8,128)(2,1)}, u32[]{:S(2)}) %copy-start.11) | copy-done | bytes 131096
  41.6 1.5 %shard_map.117 = (bf16[576,128]{1,0:T(8,128)(2,1)}, bf16[576,128]{1,0:T(8,128)(2,1)}) custom-call(bf16[128,512]{1,0:T(8,128)(2,1)S(1)} %copy-done.11, bf16[128,512]{1,0:T(8,128)(2,1)S(1)} %collective-permute-done.8.far_ref, bf16[2304,512]{1,0:T(8,128)(2,1)S(1)} %copy-done, bf16[2304,256]{1,0:T(8,128)(2,1)S(1)} %copy-done.1, bf16[2304,256]{1,0:T(8,128)(2,1)S(1)} %copy-done.2), custom_call_target="tpu_custom_call" | custom-call | flops 301989888 | bytes 2359296 | tf_op jit(solution)/shard_map/pallas_call | solution.py:282
  43.1 3.6 %collective-permute-start.9 = (bf16[576,128]{1,0:T(8,128)(2,1)}, bf16[576,128]{1,0:T(8,128)(2,1)}, u32[]{:S(2)}, u32[]{:S(2)}) collective-permute-start(bf16[576,128]{1,0:T(8,128)(2,1)} %get-tuple-element.28), channel_id=1, source_target_pairs={{0,3},{1,2},{2,1},{3,0},{4,7},{5,6},{6,5},{7,4},{8,11},{9,10},{10,... | collective-permute-start | bytes 442376 | tf_op jit(solution)/shard_map/ppermute | solution.py:296
  46.8 1.5 %shard_map.116 = (bf16[576,128]{1,0:T(8,128)(2,1)}, f32[576,128]{1,0:T(8,128)S(1)}) custom-call(bf16[128,512]{1,0:T(8,128)(2,1)S(1)} %copy-done.12, bf16[128,512]{1,0:T(8,128)(2,1)S(1)} %collective-permute-done.8.far_ref, bf16[2304,512]{1,0:T(8,128)(2,1)S(1)} %copy-done, bf16[2304,256]{1,0:T(8,128)(2,1)S(1)} %copy-done.1, bf16[2304,256]{1,0:T(8,128)(2,1)S(1)} %copy-done.2), custom_call_target="tpu_custom_call" | custom-call | flops 301989888 | bytes 2359296 | tf_op jit(solution)/shard_map/pallas_call | solution.py:282
  50.6 2.8 %all-to-all-done.turned_ref = bf16[8,2,288,128]{3,2,1,0:T(8,128)(2,1)} async-done(((bf16[8,2,288,128]{3,2,1,0:T(8,128)(2,1)}), bf16[8,2,288,128]{3,2,1,0:T(8,128)(2,1)}, u32[]{:S(2)}, u32[]{:S(2)}) %all-to-all-start) | async-done | bytes 1179680 | tf_op jit(solution)/shard_map/all_to_all | solution.py:385
  53.5 1.1 %copy-done.6 = bf16[384,1024]{1,0:T(8,128)(2,1)S(1)} copy-done((bf16[384,1024]{1,0:T(8,128)(2,1)S(1)}, bf16[384,1024]{1,0:T(8,128)(2,1)}, u32[]{:S(2)}) %copy-start.6) | copy-done | bytes 786456
  54.6 1.1 %copy-done.8 = bf16[384,1024]{1,0:T(8,128)(2,1)S(1)} copy-done((bf16[384,1024]{1,0:T(8,128)(2,1)S(1)}, bf16[384,1024]{1,0:T(8,128)(2,1)}, u32[]{:S(2)}) %copy-start.8) | copy-done | bytes 786456
  55.8 3.0 %shard_map.115 = (f32[288,256]{1,0:T(8,128)}, f32[288,512]{1,0:T(8,128)}, f32[8,128]{1,0:T(8,128)S(1)}) custom-call(bf16[8,2,288,128]{3,2,1,0:T(8,128)(2,1)} %all-to-all-done.turned_ref, bf16[384,1024]{1,0:T(8,128)(2,1)S(1)} %copy-done.6, bf16[384,1024]{1,0:T(8,128)(2,1)S(1)} %copy-done.8), custom_call_target="tpu_custom_call" | custom-call | flops 452984832 | bytes 2064384 | tf_op jit(solution)/shard_map/pallas_call | solution.py:282
  58.8 1.2 %collective-permute-done.10.refs_1_ = bf16[576,128]{1,0:T(8,128)(2,1)} collective-permute-done((bf16[576,128]{1,0:T(8,128)(2,1)}, bf16[576,128]{1,0:T(8,128)(2,1)}, u32[]{:S(2)}, u32[]{:S(2)}) %collective-permute-start.10) | collective-permute-done | bytes 147488 | tf_op jit(solution)/shard_map/ppermute | solution.py:296
  60.0 1.7 %shard_map.118 = bf16[576,128]{1,0:T(8,128)(2,1)} custom-call(f32[8,128]{1,0:T(8,128)S(1)} %get-tuple-element.24._, f32[576,128]{1,0:T(8,128)S(1)} %copy-done.14, bf16[576,128]{1,0:T(8,128)(2,1)} %collective-permute-done.9.refs_0_, bf16[576,128]{1,0:T(8,128)(2,1)} %collective-permute-done.10.refs_1_, bf16[576,128]{1,0:T(8,128)(2,1)S(1)} %collective-permute-done.11.refs_2_), custom_call_target="tpu_custom_call" | custom-call | bytes 1179648 | tf_op jit(solution)/shard_map/pallas_call | solution.py:282
  (43 shorter events, 7.4 us)
Async XLA Ops:
  0.6 16.4 %copy-start.3 = (bf16[128,2304]{1,0:T(8,128)(2,1)S(1)}, bf16[128,2304]{1,0:T(8,128)(2,1)}, u32[]{:S(2)}) copy-start(bf16[128,2304]{1,0:T(8,128)(2,1)} %cot_hbm.3) | copy-start | bytes 1769476
  4.5 8.6 %collective-permute-start = (bf16[128,768]{1,0:T(8,128)(2,1)}, bf16[128,768]{1,0:T(8,128)(2,1)S(1)}, u32[]{:S(2)}, u32[]{:S(2)}) collective-permute-start(bf16[128,768]{1,0:T(8,128)(2,1)} %get-tuple-element.18.block_hbm), channel_id=1, source_target_pairs={{0,8},{4,12},{8,0},{12,4},{16,24},{20,28},{24,16},{28,20},{1,9},{5... | collective-permute-start | bytes 589832 | tf_op jit(solution)/shard_map/ppermute | solution.py:296
  7.5 7.8 %collective-permute-start.4 = (bf16[128,768]{1,0:T(8,128)(2,1)}, bf16[128,768]{1,0:T(8,128)(2,1)S(1)}, u32[]{:S(2)}, u32[]{:S(2)}) collective-permute-start(bf16[128,768]{1,0:T(8,128)(2,1)} %get-tuple-element.20), channel_id=1, source_target_pairs={{0,20},{4,16},{8,28},{12,24},{16,4},{20,0},{24,12},{28,8},{1,21},{... | collective-permute-start | bytes 589832 | tf_op jit(solution)/shard_map/ppermute | solution.py:296
  8.2 11.8 %collective-permute-start.3 = (bf16[128,768]{1,0:T(8,128)(2,1)}, bf16[128,768]{1,0:T(8,128)(2,1)S(1)}, u32[]{:S(2)}, u32[]{:S(2)}) collective-permute-start(bf16[128,768]{1,0:T(8,128)(2,1)} %get-tuple-element.18.block_hbm), channel_id=1, source_target_pairs={{0,16},{4,20},{8,24},{12,28},{16,0},{20,4},{24,8},{28,12},{1,17},{... | collective-permute-start | bytes 589832 | tf_op jit(solution)/shard_map/ppermute | solution.py:296
  9.1 11.0 %collective-permute-start.2 = (bf16[128,768]{1,0:T(8,128)(2,1)}, bf16[128,768]{1,0:T(8,128)(2,1)S(1)}, u32[]{:S(2)}, u32[]{:S(2)}) collective-permute-start(bf16[128,768]{1,0:T(8,128)(2,1)} %get-tuple-element.20), channel_id=1, source_target_pairs={{0,12},{4,8},{8,4},{12,0},{16,28},{20,24},{24,20},{28,16},{1,13},{... | collective-permute-start | bytes 589832 | tf_op jit(solution)/shard_map/ppermute | solution.py:296
  9.3 10.8 %collective-permute-start.1 = (bf16[128,768]{1,0:T(8,128)(2,1)}, bf16[128,768]{1,0:T(8,128)(2,1)S(1)}, u32[]{:S(2)}, u32[]{:S(2)}) collective-permute-start(bf16[128,768]{1,0:T(8,128)(2,1)} %get-tuple-element.20), channel_id=1, source_target_pairs={{0,4},{4,0},{8,12},{12,8},{16,20},{20,16},{24,28},{28,24},{1,5},{5... | collective-permute-start | bytes 589832 | tf_op jit(solution)/shard_map/ppermute | solution.py:296
  13.1 10.2 %collective-permute-start.5 = (bf16[128,768]{1,0:T(8,128)(2,1)S(1)}, bf16[128,768]{1,0:T(8,128)(2,1)S(1)}, u32[]{:S(2)}, u32[]{:S(2)}) collective-permute-start(bf16[128,768]{1,0:T(8,128)(2,1)S(1)} %collective-permute-done._.refs_2_), channel_id=1, source_target_pairs={{0,16},{4,20},{8,24},{12,28},{16,0},{20,4},{24,8},{28,12},{1,17},{... | collective-permute-start | bytes 589832 | tf_op jit(solution)/shard_map/ppermute | solution.py:296
  15.3 8.1 %collective-permute-start.6 = (bf16[128,768]{1,0:T(8,128)(2,1)S(1)}, bf16[128,768]{1,0:T(8,128)(2,1)S(1)}, u32[]{:S(2)}, u32[]{:S(2)}) collective-permute-start(bf16[128,768]{1,0:T(8,128)(2,1)S(1)} %collective-permute-done.4.refs_5_), channel_id=1, source_target_pairs={{0,8},{4,12},{8,0},{12,4},{16,24},{20,28},{24,16},{28,20},{1,9},{5... | collective-permute-start | bytes 589832 | tf_op jit(solution)/shard_map/ppermute | solution.py:296
  17.0 1.1 %copy-start.9 = (bf16[128,2304]{1,0:T(8,128)(2,1)S(1)}, bf16[128,2304]{1,0:T(8,128)(2,1)}, u32[]{:S(2)}) copy-start(bf16[128,2304]{1,0:T(8,128)(2,1)} %normed_hbm.1) | copy-start | bytes 1769476
  18.1 0.9 %copy-start.15 = (bf16[128,768]{1,0:T(8,128)(2,1)S(1)}, bf16[128,768]{1,0:T(8,128)(2,1)}, u32[]{:S(2)}) copy-start(bf16[128,768]{1,0:T(8,128)(2,1)} %get-tuple-element.18.block_hbm) | copy-start | bytes 589828
  23.3 16.1 %copy-start.1 = (bf16[2304,256]{1,0:T(8,128)(2,1)S(1)}, bf16[2304,256]{1,0:T(8,128)(2,1)}, u32[]{:S(2)}) copy-start(bf16[2304,256]{1,0:T(8,128)(2,1)} %wk_ref.3) | copy-start | bytes 3538948
  29.1 1.0 %copy-start.4 = (bf16[8,2,288,128]{3,2,1,0:T(8,128)(2,1)}, bf16[8,2,288,128]{3,2,1,0:T(8,128)(2,1)S(1)}, u32[]{:S(2)}) copy-start(bf16[8,2,288,128]{3,2,1,0:T(8,128)(2,1)S(1)} %get-tuple-element.22) | copy-start | bytes 3538948
  32.3 7.2 %copy-start = (bf16[2304,512]{1,0:T(8,128)(2,1)S(1)}, bf16[2304,512]{1,0:T(8,128)(2,1)}, u32[]{:S(2)}) copy-start(bf16[2304,512]{1,0:T(8,128)(2,1)} %wq_ref.3) | copy-start | bytes 7077892
  32.3 21.2 %all-to-all-start = ((bf16[8,2,288,128]{3,2,1,0:T(8,128)(2,1)}), bf16[8,2,288,128]{3,2,1,0:T(8,128)(2,1)}, u32[]{:S(2)}, u32[]{:S(2)}) async-start(bf16[8,2,288,128]{3,2,1,0:T(8,128)(2,1)} %copy-done.4), calls=%async_computation | async-start | bytes 2359296 | tf_op jit(solution)/shard_map/all_to_all | solution.py:385
  36.7 13.1 %collective-permute-start.7 = (bf16[384,1024]{1,0:T(8,128)(2,1)}, bf16[384,1024]{1,0:T(8,128)(2,1)S(1)}, u32[]{:S(2)}, u32[]{:S(2)}) collective-permute-start(bf16[384,1024]{1,0:T(8,128)(2,1)} %copy-done.5), channel_id=1, source_target_pairs={{0,4},{4,0},{8,12},{12,8},{16,20},{20,16},{24,28},{28,24},{1,5},{5... | collective-permute-start | bytes 2359304 | tf_op jit(solution)/shard_map/ppermute | solution.py:296
  37.0 2.4 %collective-permute-start.8 = (bf16[128,512]{1,0:T(8,128)(2,1)}, bf16[128,512]{1,0:T(8,128)(2,1)S(1)}, u32[]{:S(2)}, u32[]{:S(2)}) collective-permute-start(bf16[128,512]{1,0:T(8,128)(2,1)} %copy-done.16), channel_id=1, source_target_pairs={{0,4},{4,0},{8,12},{12,8},{16,20},{20,16},{24,28},{28,24},{1,5},{5... | collective-permute-start | bytes 393224 | tf_op jit(solution)/shard_map/ppermute | solution.py:296
  39.4 1.3 %copy-start.2 = (bf16[2304,256]{1,0:T(8,128)(2,1)S(1)}, bf16[2304,256]{1,0:T(8,128)(2,1)}, u32[]{:S(2)}) copy-start(bf16[2304,256]{1,0:T(8,128)(2,1)} %wv_ref.3) | copy-start | bytes 3538948
  41.6 5.2 %copy-start.12 = (bf16[128,512]{1,0:T(8,128)(2,1)S(1)}, bf16[128,512]{1,0:T(8,128)(2,1)}, u32[]{:S(2)}) copy-start(bf16[128,512]{1,0:T(8,128)(2,1)} %copy-done.10) | copy-start | bytes 393220
  43.1 15.6 %collective-permute-start.9 = (bf16[576,128]{1,0:T(8,128)(2,1)}, bf16[576,128]{1,0:T(8,128)(2,1)}, u32[]{:S(2)}, u32[]{:S(2)}) collective-permute-start(bf16[576,128]{1,0:T(8,128)(2,1)} %get-tuple-element.28), channel_id=1, source_target_pairs={{0,3},{1,2},{2,1},{3,0},{4,7},{5,6},{6,5},{7,4},{8,11},{9,10},{10,... | collective-permute-start | bytes 442376 | tf_op jit(solution)/shard_map/ppermute | solution.py:296
  46.7 13.3 %collective-permute-start.10 = (bf16[576,128]{1,0:T(8,128)(2,1)}, bf16[576,128]{1,0:T(8,128)(2,1)}, u32[]{:S(2)}, u32[]{:S(2)}) collective-permute-start(bf16[576,128]{1,0:T(8,128)(2,1)} %get-tuple-element.29), channel_id=1, source_target_pairs={{0,2},{1,3},{2,0},{3,1},{4,6},{5,7},{6,4},{7,5},{8,10},{9,11},{10,... | collective-permute-start | bytes 442376 | tf_op jit(solution)/shard_map/ppermute | solution.py:296
  49.0 11.0 %collective-permute-start.11 = (bf16[576,128]{1,0:T(8,128)(2,1)}, bf16[576,128]{1,0:T(8,128)(2,1)S(1)}, u32[]{:S(2)}, u32[]{:S(2)}) collective-permute-start(bf16[576,128]{1,0:T(8,128)(2,1)} %get-tuple-element.30), channel_id=1, source_target_pairs={{0,1},{1,0},{2,3},{3,2},{4,5},{5,4},{6,7},{7,6},{8,9},{9,8},{10,11... | collective-permute-start | bytes 442376 | tf_op jit(solution)/shard_map/ppermute | solution.py:296
  53.5 1.1 %copy-start.6 = (bf16[384,1024]{1,0:T(8,128)(2,1)S(1)}, bf16[384,1024]{1,0:T(8,128)(2,1)}, u32[]{:S(2)}) copy-start(bf16[384,1024]{1,0:T(8,128)(2,1)} %copy-done.5) | copy-start | bytes 2359300
  54.6 1.1 %copy-start.8 = (bf16[384,1024]{1,0:T(8,128)(2,1)S(1)}, bf16[384,1024]{1,0:T(8,128)(2,1)}, u32[]{:S(2)}) copy-start(bf16[384,1024]{1,0:T(8,128)(2,1)} %copy-done.7) | copy-start | bytes 2359300
  55.8 4.3 %copy-start.14 = (f32[576,128]{1,0:T(8,128)S(1)}, f32[576,128]{1,0:T(8,128)}, u32[]{:S(2)}) copy-start(f32[576,128]{1,0:T(8,128)} %copy-done.13) | copy-start | bytes 884740
  (6 other events, 4.7 us)

commit v11 on v10

--- a/solution.py
+++ b/solution.py
@@ -81,21 +81,28 @@
 
 
 def turn_kernel(
-    parts, normed_hbm, cot_hbm, block_hbm, _, turned_ref, own_ref, normed_ref, cot_ref, sem
+    normed_hbm, cot_hbm, _, keep_ref, give_ref, normed_ref, cot_ref, turned_ref, sem
 ):
-    cut = normed_ref.shape[1] // parts
+    me = lax.axis_index("seq")
+    cut = keep_ref.shape[2]
     copies = []
-    for which, (source, target) in enumerate(
-        ((normed_hbm, normed_ref), (cot_hbm, cot_ref), (block_hbm, own_ref))
-    ):
+    for which, (source, target) in enumerate(((normed_hbm, normed_ref), (cot_hbm, cot_ref))):
         copies.append(pltpu.make_async_copy(source, target, sem.at[which]))
         copies[-1].start()
     for which, ref in enumerate((normed_ref, cot_ref)):
         copies[which].wait()
-        turned = ref[...].astype(jnp.float32).T.astype(jnp.bfloat16)
-        for part in range(parts):
-            turned_ref[part, which] = turned[part * cut : (part + 1) * cut]
-    copies[2].wait()
+        turned_ref[which] = ref[...].astype(jnp.float32).T.astype(jnp.bfloat16)
+        for chip in range(keep_ref.shape[0]):
+            keep_ref[chip, which] = turned_ref[which, at(me ^ (2 * chip), cut)]
+            give_ref[chip, which] = turned_ref[which, at(me ^ (2 * chip + 1), cut)]
+
+
+def join_kernel(keep_ref, got_ref, block_ref, *joined_refs):
+    joined_refs, own_ref = joined_refs[:-1], joined_refs[-1]
+    own_ref[...] = block_ref[...]
+    for chip, ref in enumerate(joined_refs):
+        ref[0] = keep_ref[chip]
+        ref[1] = got_ref[chip]
 
 
 def attention_kernel(blocks, *refs):
@@ -104,11 +111,9 @@
 
 def attention_body(
     block_refs,
-    _,
     dx_own_ref,
     dx_far_ref,
     parts_ref,
-    __,
     gathered_ref,
     score_even_ref,
     score_odd_ref,
@@ -250,15 +255,14 @@
         ).astype(target.dtype)
 
 
-def weight_grad_kernel(
-    turned_ref, own_ref, far_ref, wvalue_ref, woutput_ref, done_ref, joined_ref
-):
+def weight_grad_kernel(own_ref, far_ref, *refs):
+    column_refs, (wvalue_ref, woutput_ref, done_ref, joined_ref) = refs[:-4], refs[-4:]
     done_ref[...] = jnp.zeros_like(done_ref)
-    core = lax.axis_index("seq") % 2
-    parts = turned_ref.shape[0]
-    rows = turned_ref.shape[3]
-    for part in range(parts):
-        joined_ref[:, :, part * rows : (part + 1) * rows] = turned_ref[part]
+    me = lax.axis_index("seq")
+    core = me % 2
+    for chip, ref in enumerate(column_refs):
+        for far in range(2):
+            joined_ref[:, :, at(me ^ (2 * chip + far), ref.shape[3])] = ref[far]
     kv_cols = wvalue_ref.shape[1] // 2
     q_cols = woutput_ref.shape[1] // 2
     for half, ref in ((core, own_ref), (1 - core, far_ref)):
@@ -274,8 +278,7 @@
 
 
 def kernel_call(
-    body, outs, operands, in_vmem=(), scratch=(), flops=0, moved=0, room=16,
-    out_hbm=(), aliases={},
+    body, outs, operands, in_vmem=(), scratch=(), flops=0, moved=0, room=16
 ):
     vmem = pl.BlockSpec(memory_space=pltpu.VMEM)
     hbm = pl.BlockSpec(memory_space=pltpu.HBM)
@@ -283,8 +286,7 @@
         body,
         out_shape=outs,
         in_specs=[vmem if place in in_vmem else hbm for place in range(len(operands))],
-        out_specs=tuple(hbm if place in out_hbm else vmem for place in range(len(outs))),
-        input_output_aliases=aliases,
+        out_specs=(vmem,) * len(outs),
         scratch_shapes=list(scratch),
         compiler_params=pltpu.CompilerParams(vmem_limit_bytes=room * 1024 * 1024),
         cost_estimate=pl.CostEstimate(flops=flops, bytes_accessed=moved, transcendentals=0),
@@ -341,30 +343,43 @@
         else:
             held[apart] = swapped(held[apart ^ through], "seq", through)
     held[1] = swapped(other, "seq", 1)
-    turned, own_block = kernel_call(
-        functools.partial(turn_kernel, blocks),
-        (shape((blocks, 2, model // blocks, rows), bf16), shape((rows, packed_cols), bf16)),
-        (normed_input, out_cotangent, same, held[2]),
+    cut = model // blocks
+    keep, give = kernel_call(
+        turn_kernel,
+        (
+            shape((blocks // 2, 2, cut, rows), bf16),
+            shape((blocks // 2, 2, cut, rows), bf16),
+        ),
+        (normed_input, out_cotangent, held[2]),
         scratch=(
             pltpu.VMEM(normed_input.shape, bf16),
             pltpu.VMEM(out_cotangent.shape, bf16),
-            pltpu.SemaphoreType.DMA((3,)),
+            pltpu.VMEM((2, model, rows), bf16),
+            pltpu.SemaphoreType.DMA((2,)),
         ),
         moved=8 * rows * model,
-    )
-    held[0] = own_block
-    dx_own, dx_far, grad_parts, turned = kernel_call(
+        room=8,
+    )
+    *columns, held[0] = kernel_call(
+        join_kernel,
+        (shape((2, 2, cut, rows), bf16),) * (blocks // 2) + (shape(same.shape, bf16),),
+        (keep, swapped(give, "seq", 1), same),
+        in_vmem=range(3),
+        moved=8 * rows * model,
+        room=4,
+    )
+    columns = [columns[0]] + [
+        swapped(columns[chip], "seq", 2 * chip) for chip in range(1, blocks // 2)
+    ]
+    dx_own, dx_far, grad_parts = kernel_call(
         functools.partial(attention_kernel, blocks),
         (
             shape((rows, q_cols + 2 * kv_cols), bf16),
             shape((rows, q_cols + 2 * kv_cols), bf16),
             shape((q_cols + kv_cols, tokens), bf16),
-            shape(turned.shape, bf16),
         ),
-        [held[apart] for apart in range(blocks)] + [turned],
+        [held[apart] for apart in range(blocks)],
         in_vmem=range(blocks),
-        out_hbm=(3,),
-        aliases={blocks: 3},
         scratch=(
             pltpu.VMEM((tokens, packed_cols), bf16),
             pltpu.VMEM((tokens, wide), f32),
@@ -382,7 +397,6 @@
         moved=2 * tokens * packed_cols,
     )
     dx_got = swapped(dx_far, "seq", 1)
-    turned = lax.all_to_all(turned, "seq", 0, 0)
     aparts = tuple(range(groups - 1, -1, -1))
     terms = {}
     for chosen in (aparts[: groups // 2], aparts[groups // 2 :]):
@@ -405,9 +419,10 @@
             shape((model // blocks, 2 * q_cols), f32),
             shape((8, HEAD_SIZE), f32),
         ),
-        (turned, grad_parts, swapped(grad_parts, "seq", 1)),
-        in_vmem=range(3),
+        (grad_parts, swapped(grad_parts, "seq", 1), *columns),
+        in_vmem=range(2 + blocks // 2),
         scratch=(pltpu.VMEM((2, model // blocks, tokens), bf16),),
+        room=8,
         flops=4 * tokens * (model // blocks) * (q_cols + kv_cols),
         moved=4 * (model // blocks) * (tokens + 2 * q_cols + 2 * kv_cols),
     )

time: 62.2 us -> 61.2 us (0.984)
  waiting for transfers between devices: 13 us -> 22.6 us
  local copies, waits for them, and re-layouts: 11.3 us -> 2.01 us
  Pallas kernels: 18.3 us -> 14.8 us
  starting transfers between devices: 18.4 us -> 20.9 us
    ppermute x12 -> x16, waiting for transfers between devices: 10.1 us -> 22.6 us  [swapped(): lax.ppermute(value, axis, [(place, place ^ apart) for place in range(coun...]
    unnamed x34 -> x12, local copies, waits for them, and re-layouts: 11.3 us -> 2.01 us
    ppermute x12 -> x16, starting transfers between devices: 14.1 us -> 20.9 us  [swapped(): lax.ppermute(value, axis, [(place, place ^ apart) for place in range(coun...]
    all_to_all x1 -> x0, starting transfers between devices: 4.38 us -> none  [gathered_plan(): turned = lax.all_to_all(turned, 'seq', 0, 0)]
    pallas_call x7 -> x8, Pallas kernels: 18.3 us -> 14.8 us  [kernel_call(): pl.pallas_call(body, out_shape=outs, in_specs=[vmem if place in in_vmem e...]
    all_to_all x1 -> x0, waiting for transfers between devices: 2.85 us -> none  [gathered_plan(): turned = lax.all_to_all(turned, 'seq', 0, 0)]
  transfers between devices with their start and end apart: 13 -> 16, of which waited for: 5 -> 9; matrix products, arithmetic and copies ran while one was open for 0% -> 0% of each run, Pallas kernels for 11% -> 6%
where the time goes in v11:
time: 61.2 us; the launch traced here: 61.1 us
  waiting for transfers between devices  22.6 us (37%)
  starting transfers between devices  20.9 us (34%)
  Pallas kernels  14.8 us (24%)
  local copies, waits for them, and re-layouts  2.01 us (3%)
  between operations  0.73 us (1%)
    ppermute x16, waiting for transfers between devices, swapped(): lax.ppermute(value, axis, [(place, place ^ apart) for place in range(coun...  22.6 us
    ppermute x16, starting transfers between devices, swapped(): lax.ppermute(value, axis, [(place, place ^ apart) for place in range(coun...  20.9 us
    pallas_call x8, Pallas kernels, kernel_call(): pl.pallas_call(body, out_shape=outs, in_specs=[vmem if place in in_vmem e...  14.8 us
    unnamed x12, local copies, waits for them, and re-layouts  2.01 us
  transfers between devices with their start and end apart: 16, of which 9 were waited for; matrix products, arithmetic and copies ran while one was open for 0% of the time, Pallas kernels for 6%

profile of v11, /device:TPU:0, one launch (start us, length us, event | category | flops | bytes accessed | tf_op | source)
XLA Modules:
  0.0 61.1 jit_solution(6280824741343095283)
XLA Ops:
  0.6 3.8 %shard_map.112 = (bf16[128,768]{1,0:T(8,128)(2,1)}, bf16[128,768]{1,0:T(8,128)(2,1)}) custom-call(bf16[128,2304]{1,0:T(8,128)(2,1)} %cot_hbm.3, bf16[512,2304]{1,0:T(8,128)(2,1)} %weight_hbm.1, bf16[128,512]{1,0:T(8,128)(2,1)} %q_hbm.1, bf16[128,256]{1,0:T(8,128)(2,1)} %k_hbm.1, bf16[128,256]{1,0:T(8,128)(2,1)} %v_hbm.1), custom_call_target="tpu_custom_call" | custom-call | flops 301989888 | bytes 2949120 | tf_op jit(solution)/shard_map/pallas_call | solution.py:285
  4.5 3.0 %collective-permute-start = (bf16[128,768]{1,0:T(8,128)(2,1)}, bf16[128,768]{1,0:T(8,128)(2,1)S(1)}, u32[]{:S(2)}, u32[]{:S(2)}) collective-permute-start(bf16[128,768]{1,0:T(8,128)(2,1)} %get-tuple-element.22.block_ref), channel_id=1, source_target_pairs={{0,8},{4,12},{8,0},{12,4},{16,24},{20,28},{24,16},{28,20},{1,9},{5... | collective-permute-start | bytes 589832 | tf_op jit(solution)/shard_map/ppermute | solution.py:298
  7.5 5.1 %collective-permute-done._.refs_2_ = bf16[128,768]{1,0:T(8,128)(2,1)S(1)} collective-permute-done((bf16[128,768]{1,0:T(8,128)(2,1)}, bf16[128,768]{1,0:T(8,128)(2,1)S(1)}, u32[]{:S(2)}, u32[]{:S(2)}) %collective-permute-start) | collective-permute-done | bytes 196640 | tf_op jit(solution)/shard_map/ppermute | solution.py:298
  12.6 1.1 %copy-done.4 = bf16[128,2304]{1,0:T(8,128)(2,1)S(1)} copy-done((bf16[128,2304]{1,0:T(8,128)(2,1)S(1)}, bf16[128,2304]{1,0:T(8,128)(2,1)}, u32[]{:S(2)}) %copy-start.4) | copy-done | bytes 589848
  14.6 1.9 %collective-permute-start.5 = (bf16[128,768]{1,0:T(8,128)(2,1)}, bf16[128,768]{1,0:T(8,128)(2,1)S(1)}, u32[]{:S(2)}, u32[]{:S(2)}) collective-permute-start(bf16[128,768]{1,0:T(8,128)(2,1)} %get-tuple-element.26), channel_id=1, source_target_pairs={{0,20},{4,16},{8,28},{12,24},{16,4},{20,0},{24,12},{28,8},{1,21},{... | collective-permute-start | bytes 589832 | tf_op jit(solution)/shard_map/ppermute | solution.py:298
  16.5 1.5 %collective-permute-start.3 = (bf16[128,768]{1,0:T(8,128)(2,1)}, bf16[128,768]{1,0:T(8,128)(2,1)S(1)}, u32[]{:S(2)}, u32[]{:S(2)}) collective-permute-start(bf16[128,768]{1,0:T(8,128)(2,1)} %get-tuple-element.26), channel_id=1, source_target_pairs={{0,12},{4,8},{8,4},{12,0},{16,28},{20,24},{24,20},{28,16},{1,13},{... | collective-permute-start | bytes 589832 | tf_op jit(solution)/shard_map/ppermute | solution.py:298
  18.6 3.4 %collective-permute-done.5.refs_5_ = bf16[128,768]{1,0:T(8,128)(2,1)S(1)} collective-permute-done((bf16[128,768]{1,0:T(8,128)(2,1)}, bf16[128,768]{1,0:T(8,128)(2,1)S(1)}, u32[]{:S(2)}, u32[]{:S(2)}) %collective-permute-start.5) | collective-permute-done | bytes 196640 | tf_op jit(solution)/shard_map/ppermute | solution.py:298
  22.0 1.2 %collective-permute-start.6 = (bf16[128,768]{1,0:T(8,128)(2,1)S(1)}, bf16[128,768]{1,0:T(8,128)(2,1)S(1)}, u32[]{:S(2)}, u32[]{:S(2)}) collective-permute-start(bf16[128,768]{1,0:T(8,128)(2,1)S(1)} %collective-permute-done._.refs_2_), channel_id=1, source_target_pairs={{0,16},{4,20},{8,24},{12,28},{16,0},{20,4},{24,8},{28,12},{1,17},{... | collective-permute-start | bytes 589832 | tf_op jit(solution)/shard_map/ppermute | solution.py:298
  23.3 1.5 %collective-permute-start.7 = (bf16[128,768]{1,0:T(8,128)(2,1)S(1)}, bf16[128,768]{1,0:T(8,128)(2,1)S(1)}, u32[]{:S(2)}, u32[]{:S(2)}) collective-permute-start(bf16[128,768]{1,0:T(8,128)(2,1)S(1)} %collective-permute-done.5.refs_5_), channel_id=1, source_target_pairs={{0,8},{4,12},{8,0},{12,4},{16,24},{20,28},{24,16},{28,20},{1,9},{5... | collective-permute-start | bytes 589832 | tf_op jit(solution)/shard_map/ppermute | solution.py:298
  24.8 0.9 %copy-done.5 = bf16[128,768]{1,0:T(8,128)(2,1)S(1)} copy-done((bf16[128,768]{1,0:T(8,128)(2,1)S(1)}, bf16[128,768]{1,0:T(8,128)(2,1)}, u32[]{:S(2)}) %copy-start.5) | copy-done | bytes 196632
  25.8 1.0 %collective-permute-done.4.refs_4_ = bf16[128,768]{1,0:T(8,128)(2,1)S(1)} collective-permute-done((bf16[128,768]{1,0:T(8,128)(2,1)}, bf16[128,768]{1,0:T(8,128)(2,1)S(1)}, u32[]{:S(2)}, u32[]{:S(2)}) %collective-permute-start.4) | collective-permute-done | bytes 196640 | tf_op jit(solution)/shard_map/ppermute | solution.py:298
  26.8 3.7 %collective-permute-done.6.refs_6_ = bf16[128,768]{1,0:T(8,128)(2,1)S(1)} collective-permute-done((bf16[128,768]{1,0:T(8,128)(2,1)S(1)}, bf16[128,768]{1,0:T(8,128)(2,1)S(1)}, u32[]{:S(2)}, u32[]{:S(2)}) %collective-permute-start.6) | collective-permute-done | bytes 196640 | tf_op jit(solution)/shard_map/ppermute | solution.py:298
  30.8 5.7 %shard_map.115 = (bf16[128,512]{1,0:T(8,128)(2,1)S(1)}, bf16[128,512]{1,0:T(8,128)(2,1)S(1)}, bf16[384,1024]{1,0:T(8,128)(2,1)S(1)}) custom-call(bf16[128,768]{1,0:T(8,128)(2,1)S(1)} %get-tuple-element.25.refs_0_, bf16[128,768]{1,0:T(8,128)(2,1)S(1)} %collective-permute-done.2.refs_1_, bf16[128,768]{1,0:T(8,128)(2,1)S(1)} %collective-permute-done._.refs_2_, ...), custom_call_target="tpu_custom_call" | custom-call | flops 2147483648 | bytes 1572864 | tf_op jit(solution)/shard_map/pallas_call | solution.py:285
  36.5 1.5 %collective-permute-start.9 = (bf16[2,2,288,128]{3,2,1,0:T(8,128)(2,1)S(1)}, bf16[2,2,288,128]{3,2,1,0:T(8,128)(2,1)S(1)}, u32[]{:S(2)}, u32[]{:S(2)}) collective-permute-start(bf16[2,2,288,128]{3,2,1,0:T(8,128)(2,1)S(1)} %get-tuple-element.29), channel_id=1, source_target_pairs={{0,8},{4,12},{8,0},{12,4},{16,24},{20,28},{24,16},{28,20},{1,9},{5... | collective-permute-start | bytes 884744 | tf_op jit(solution)/shard_map/ppermute | solution.py:298
  38.1 1.5 %collective-permute-start.10 = (bf16[2,2,288,128]{3,2,1,0:T(8,128)(2,1)S(1)}, bf16[2,2,288,128]{3,2,1,0:T(8,128)(2,1)S(1)}, u32[]{:S(2)}, u32[]{:S(2)}) collective-permute-start(bf16[2,2,288,128]{3,2,1,0:T(8,128)(2,1)S(1)} %get-tuple-element.30), channel_id=1, source_target_pairs={{0,16},{4,20},{8,24},{12,28},{16,0},{20,4},{24,8},{28,12},{1,17},{... | collective-permute-start | bytes 884744 | tf_op jit(solution)/shard_map/ppermute | solution.py:298
  40.1 1.3 %collective-permute-done.12.far_ref = bf16[128,512]{1,0:T(8,128)(2,1)S(1)} collective-permute-done((bf16[128,512]{1,0:T(8,128)(2,1)S(1)}, bf16[128,512]{1,0:T(8,128)(2,1)S(1)}, u32[]{:S(2)}, u32[]{:S(2)}) %collective-permute-start.12) | collective-permute-done | bytes 131104 | tf_op jit(solution)/shard_map/ppermute | solution.py:298
  41.4 0.8 %shard_map.118 = (bf16[576,128]{1,0:T(8,128)(2,1)S(1)}, bf16[576,128]{1,0:T(8,128)(2,1)S(1)}) custom-call(bf16[128,512]{1,0:T(8,128)(2,1)S(1)} %get-tuple-element.33.own_ref, bf16[128,512]{1,0:T(8,128)(2,1)S(1)} %collective-permute-done.12.far_ref, bf16[2304,512]{1,0:T(8,128)(2,1)S(1)} %copy-done, bf16[2304,256]{1,0:T(8,128)(2,1)S(1)} %copy-done.1, ...), custom_call_target="tpu_custom_call" | custom-call | flops 301989888 | bytes 2359296 | tf_op jit(solution)/shard_map/pallas_call | solution.py:285
  42.3 3.7 %collective-permute-start.13 = (bf16[576,128]{1,0:T(8,128)(2,1)S(1)}, bf16[576,128]{1,0:T(8,128)(2,1)S(1)}, u32[]{:S(2)}, u32[]{:S(2)}) collective-permute-start(bf16[576,128]{1,0:T(8,128)(2,1)S(1)} %get-tuple-element.36), channel_id=1, source_target_pairs={{0,3},{1,2},{2,1},{3,0},{4,7},{5,6},{6,5},{7,4},{8,11},{9,10},{10,... | collective-permute-start | bytes 442376 | tf_op jit(solution)/shard_map/ppermute | solution.py:298
  46.8 2.2 %collective-permute-start.14 = (bf16[576,128]{1,0:T(8,128)(2,1)S(1)}, bf16[576,128]{1,0:T(8,128)(2,1)S(1)}, u32[]{:S(2)}, u32[]{:S(2)}) collective-permute-start(bf16[576,128]{1,0:T(8,128)(2,1)S(1)} %get-tuple-element.37), channel_id=1, source_target_pairs={{0,2},{1,3},{2,0},{3,1},{4,6},{5,7},{6,4},{7,5},{8,10},{9,11},{10,... | collective-permute-start | bytes 442376 | tf_op jit(solution)/shard_map/ppermute | solution.py:298
  49.0 4.5 %collective-permute-done.10.refs_2_ = bf16[2,2,288,128]{3,2,1,0:T(8,128)(2,1)S(1)} collective-permute-done((bf16[2,2,288,128]{3,2,1,0:T(8,128)(2,1)S(1)}, bf16[2,2,288,128]{3,2,1,0:T(8,128)(2,1)S(1)}, u32[]{:S(2)}, u32[]{:S(2)}) %collective-permute-start.10) | collective-permute-done | bytes 294944 | tf_op jit(solution)/shard_map/ppermute | solution.py:298
  53.5 1.6 %collective-permute-start.15 = (bf16[576,128]{1,0:T(8,128)(2,1)S(1)}, bf16[576,128]{1,0:T(8,128)(2,1)S(1)}, u32[]{:S(2)}, u32[]{:S(2)}) collective-permute-start(bf16[576,128]{1,0:T(8,128)(2,1)S(1)} %get-tuple-element.38), channel_id=1, source_target_pairs={{0,1},{1,0},{2,3},{3,2},{4,5},{5,4},{6,7},{7,6},{8,9},{9,8},{10,11... | collective-permute-start | bytes 442376 | tf_op jit(solution)/shard_map/ppermute | solution.py:298
  55.0 2.0 %shard_map.116 = (f32[288,256]{1,0:T(8,128)}, f32[288,512]{1,0:T(8,128)}, f32[8,128]{1,0:T(8,128)S(1)}) custom-call(bf16[384,1024]{1,0:T(8,128)(2,1)S(1)} %get-tuple-element.27.own_ref, bf16[384,1024]{1,0:T(8,128)(2,1)S(1)} %collective-permute-done.8.far_ref, bf16[2,2,288,128]{3,2,1,0:T(8,128)(2,1)S(1)} %get-tuple-element.28.refs_0_, ...), custom_call_target="tpu_custom_call" | custom-call | flops 452984832 | bytes 2064384 | tf_op jit(solution)/shard_map/pallas_call | solution.py:285
  57.1 1.8 %collective-permute-done.14.refs_1_ = bf16[576,128]{1,0:T(8,128)(2,1)S(1)} collective-permute-done((bf16[576,128]{1,0:T(8,128)(2,1)S(1)}, bf16[576,128]{1,0:T(8,128)(2,1)S(1)}, u32[]{:S(2)}, u32[]{:S(2)}) %collective-permute-start.14) | collective-permute-done | bytes 147488 | tf_op jit(solution)/shard_map/ppermute | solution.py:298
  58.8 1.5 %collective-permute-done.15.refs_2_ = bf16[576,128]{1,0:T(8,128)(2,1)S(1)} collective-permute-done((bf16[576,128]{1,0:T(8,128)(2,1)S(1)}, bf16[576,128]{1,0:T(8,128)(2,1)S(1)}, u32[]{:S(2)}, u32[]{:S(2)}) %collective-permute-start.15) | collective-permute-done | bytes 147488 | tf_op jit(solution)/shard_map/ppermute | solution.py:298
  (28 shorter events, 4.0 us)
Async XLA Ops:
  0.6 12.0 %copy-start.3 = (bf16[128,2304]{1,0:T(8,128)(2,1)S(1)}, bf16[128,2304]{1,0:T(8,128)(2,1)}, u32[]{:S(2)}) copy-start(bf16[128,2304]{1,0:T(8,128)(2,1)} %cot_hbm.3) | copy-start | bytes 1769476
  4.5 8.1 %collective-permute-start = (bf16[128,768]{1,0:T(8,128)(2,1)}, bf16[128,768]{1,0:T(8,128)(2,1)S(1)}, u32[]{:S(2)}, u32[]{:S(2)}) collective-permute-start(bf16[128,768]{1,0:T(8,128)(2,1)} %get-tuple-element.22.block_ref), channel_id=1, source_target_pairs={{0,8},{4,12},{8,0},{12,4},{16,24},{20,28},{24,16},{28,20},{1,9},{5... | collective-permute-start | bytes 589832 | tf_op jit(solution)/shard_map/ppermute | solution.py:298
  12.6 1.1 %copy-start.4 = (bf16[128,2304]{1,0:T(8,128)(2,1)S(1)}, bf16[128,2304]{1,0:T(8,128)(2,1)}, u32[]{:S(2)}) copy-start(bf16[128,2304]{1,0:T(8,128)(2,1)} %normed_hbm.1) | copy-start | bytes 1769476
  14.5 8.8 %collective-permute-start.1 = (bf16[4,2,288,128]{3,2,1,0:T(8,128)(2,1)S(1)}, bf16[4,2,288,128]{3,2,1,0:T(8,128)(2,1)S(1)}, u32[]{:S(2)}, u32[]{:S(2)}) collective-permute-start(bf16[4,2,288,128]{3,2,1,0:T(8,128)(2,1)S(1)} %get-tuple-element.24), channel_id=1, source_target_pairs={{0,4},{4,0},{8,12},{12,8},{16,20},{20,16},{24,28},{28,24},{1,5},{5... | collective-permute-start | bytes 1769480 | tf_op jit(solution)/shard_map/ppermute | solution.py:298
  14.6 7.4 %collective-permute-start.5 = (bf16[128,768]{1,0:T(8,128)(2,1)}, bf16[128,768]{1,0:T(8,128)(2,1)S(1)}, u32[]{:S(2)}, u32[]{:S(2)}) collective-permute-start(bf16[128,768]{1,0:T(8,128)(2,1)} %get-tuple-element.26), channel_id=1, source_target_pairs={{0,20},{4,16},{8,28},{12,24},{16,4},{20,0},{24,12},{28,8},{1,21},{... | collective-permute-start | bytes 589832 | tf_op jit(solution)/shard_map/ppermute | solution.py:298
  16.5 9.3 %collective-permute-start.2 = (bf16[128,768]{1,0:T(8,128)(2,1)}, bf16[128,768]{1,0:T(8,128)(2,1)S(1)}, u32[]{:S(2)}, u32[]{:S(2)}) collective-permute-start(bf16[128,768]{1,0:T(8,128)(2,1)} %get-tuple-element.26), channel_id=1, source_target_pairs={{0,4},{4,0},{8,12},{12,8},{16,20},{20,16},{24,28},{28,24},{1,5},{5... | collective-permute-start | bytes 589832 | tf_op jit(solution)/shard_map/ppermute | solution.py:298
  16.5 9.3 %collective-permute-start.3 = (bf16[128,768]{1,0:T(8,128)(2,1)}, bf16[128,768]{1,0:T(8,128)(2,1)S(1)}, u32[]{:S(2)}, u32[]{:S(2)}) collective-permute-start(bf16[128,768]{1,0:T(8,128)(2,1)} %get-tuple-element.26), channel_id=1, source_target_pairs={{0,12},{4,8},{8,4},{12,0},{16,28},{20,24},{24,20},{28,16},{1,13},{... | collective-permute-start | bytes 589832 | tf_op jit(solution)/shard_map/ppermute | solution.py:298
  18.1 8.8 %collective-permute-start.4 = (bf16[128,768]{1,0:T(8,128)(2,1)}, bf16[128,768]{1,0:T(8,128)(2,1)S(1)}, u32[]{:S(2)}, u32[]{:S(2)}) collective-permute-start(bf16[128,768]{1,0:T(8,128)(2,1)} %get-tuple-element.22.block_ref), channel_id=1, source_target_pairs={{0,16},{4,20},{8,24},{12,28},{16,0},{20,4},{24,8},{28,12},{1,17},{... | collective-permute-start | bytes 589832 | tf_op jit(solution)/shard_map/ppermute | solution.py:298
  22.0 8.5 %collective-permute-start.6 = (bf16[128,768]{1,0:T(8,128)(2,1)S(1)}, bf16[128,768]{1,0:T(8,128)(2,1)S(1)}, u32[]{:S(2)}, u32[]{:S(2)}) collective-permute-start(bf16[128,768]{1,0:T(8,128)(2,1)S(1)} %collective-permute-done._.refs_2_), channel_id=1, source_target_pairs={{0,16},{4,20},{8,24},{12,28},{16,0},{20,4},{24,8},{28,12},{1,17},{... | collective-permute-start | bytes 589832 | tf_op jit(solution)/shard_map/ppermute | solution.py:298
  23.3 7.5 %collective-permute-start.7 = (bf16[128,768]{1,0:T(8,128)(2,1)S(1)}, bf16[128,768]{1,0:T(8,128)(2,1)S(1)}, u32[]{:S(2)}, u32[]{:S(2)}) collective-permute-start(bf16[128,768]{1,0:T(8,128)(2,1)S(1)} %collective-permute-done.5.refs_5_), channel_id=1, source_target_pairs={{0,8},{4,12},{8,0},{12,4},{16,24},{20,28},{24,16},{28,20},{1,9},{5... | collective-permute-start | bytes 589832 | tf_op jit(solution)/shard_map/ppermute | solution.py:298
  24.8 0.9 %copy-start.5 = (bf16[128,768]{1,0:T(8,128)(2,1)S(1)}, bf16[128,768]{1,0:T(8,128)(2,1)}, u32[]{:S(2)}) copy-start(bf16[128,768]{1,0:T(8,128)(2,1)} %get-tuple-element.22.block_ref) | copy-start | bytes 589828
  30.7 10.7 %copy-start = (bf16[2304,512]{1,0:T(8,128)(2,1)S(1)}, bf16[2304,512]{1,0:T(8,128)(2,1)}, u32[]{:S(2)}) copy-start(bf16[2304,512]{1,0:T(8,128)(2,1)} %wq_ref.3) | copy-start | bytes 7077892
  30.7 10.7 %copy-start.1 = (bf16[2304,256]{1,0:T(8,128)(2,1)S(1)}, bf16[2304,256]{1,0:T(8,128)(2,1)}, u32[]{:S(2)}) copy-start(bf16[2304,256]{1,0:T(8,128)(2,1)} %wk_ref.3) | copy-start | bytes 3538948
  30.8 10.7 %copy-start.2 = (bf16[2304,256]{1,0:T(8,128)(2,1)S(1)}, bf16[2304,256]{1,0:T(8,128)(2,1)}, u32[]{:S(2)}) copy-start(bf16[2304,256]{1,0:T(8,128)(2,1)} %wv_ref.3) | copy-start | bytes 3538948
  36.5 18.6 %collective-permute-start.8 = (bf16[384,1024]{1,0:T(8,128)(2,1)S(1)}, bf16[384,1024]{1,0:T(8,128)(2,1)S(1)}, u32[]{:S(2)}, u32[]{:S(2)}) collective-permute-start(bf16[384,1024]{1,0:T(8,128)(2,1)S(1)} %get-tuple-element.27.own_ref), channel_id=1, source_target_pairs={{0,4},{4,0},{8,12},{12,8},{16,20},{20,16},{24,28},{28,24},{1,5},{5... | collective-permute-start | bytes 2359304 | tf_op jit(solution)/shard_map/ppermute | solution.py:298
  36.5 10.2 %collective-permute-start.9 = (bf16[2,2,288,128]{3,2,1,0:T(8,128)(2,1)S(1)}, bf16[2,2,288,128]{3,2,1,0:T(8,128)(2,1)S(1)}, u32[]{:S(2)}, u32[]{:S(2)}) collective-permute-start(bf16[2,2,288,128]{3,2,1,0:T(8,128)(2,1)S(1)} %get-tuple-element.29), channel_id=1, source_target_pairs={{0,8},{4,12},{8,0},{12,4},{16,24},{20,28},{24,16},{28,20},{1,9},{5... | collective-permute-start | bytes 884744 | tf_op jit(solution)/shard_map/ppermute | solution.py:298
  38.1 15.4 %collective-permute-start.10 = (bf16[2,2,288,128]{3,2,1,0:T(8,128)(2,1)S(1)}, bf16[2,2,288,128]{3,2,1,0:T(8,128)(2,1)S(1)}, u32[]{:S(2)}, u32[]{:S(2)}) collective-permute-start(bf16[2,2,288,128]{3,2,1,0:T(8,128)(2,1)S(1)} %get-tuple-element.30), channel_id=1, source_target_pairs={{0,16},{4,20},{8,24},{12,28},{16,0},{20,4},{24,8},{28,12},{1,17},{... | collective-permute-start | bytes 884744 | tf_op jit(solution)/shard_map/ppermute | solution.py:298
  39.5 15.5 %collective-permute-start.11 = (bf16[2,2,288,128]{3,2,1,0:T(8,128)(2,1)S(1)}, bf16[2,2,288,128]{3,2,1,0:T(8,128)(2,1)S(1)}, u32[]{:S(2)}, u32[]{:S(2)}) collective-permute-start(bf16[2,2,288,128]{3,2,1,0:T(8,128)(2,1)S(1)} %get-tuple-element.31), channel_id=1, source_target_pairs={{0,24},{4,28},{8,16},{12,20},{16,8},{20,12},{24,0},{28,4},{1,25},{... | collective-permute-start | bytes 884744 | tf_op jit(solution)/shard_map/ppermute | solution.py:298
  40.1 1.3 %collective-permute-start.12 = (bf16[128,512]{1,0:T(8,128)(2,1)S(1)}, bf16[128,512]{1,0:T(8,128)(2,1)S(1)}, u32[]{:S(2)}, u32[]{:S(2)}) collective-permute-start(bf16[128,512]{1,0:T(8,128)(2,1)S(1)} %get-tuple-element.34), channel_id=1, source_target_pairs={{0,4},{4,0},{8,12},{12,8},{16,20},{20,16},{24,28},{28,24},{1,5},{5... | collective-permute-start | bytes 393224 | tf_op jit(solution)/shard_map/ppermute | solution.py:298
  42.3 14.8 %collective-permute-start.13 = (bf16[576,128]{1,0:T(8,128)(2,1)S(1)}, bf16[576,128]{1,0:T(8,128)(2,1)S(1)}, u32[]{:S(2)}, u32[]{:S(2)}) collective-permute-start(bf16[576,128]{1,0:T(8,128)(2,1)S(1)} %get-tuple-element.36), channel_id=1, source_target_pairs={{0,3},{1,2},{2,1},{3,0},{4,7},{5,6},{6,5},{7,4},{8,11},{9,10},{10,... | collective-permute-start | bytes 442376 | tf_op jit(solution)/shard_map/ppermute | solution.py:298
  46.8 12.1 %collective-permute-start.14 = (bf16[576,128]{1,0:T(8,128)(2,1)S(1)}, bf16[576,128]{1,0:T(8,128)(2,1)S(1)}, u32[]{:S(2)}, u32[]{:S(2)}) collective-permute-start(bf16[576,128]{1,0:T(8,128)(2,1)S(1)} %get-tuple-element.37), channel_id=1, source_target_pairs={{0,2},{1,3},{2,0},{3,1},{4,6},{5,7},{6,4},{7,5},{8,10},{9,11},{10,... | collective-permute-start | bytes 442376 | tf_op jit(solution)/shard_map/ppermute | solution.py:298
  53.5 6.9 %collective-permute-start.15 = (bf16[576,128]{1,0:T(8,128)(2,1)S(1)}, bf16[576,128]{1,0:T(8,128)(2,1)S(1)}, u32[]{:S(2)}, u32[]{:S(2)}) collective-permute-start(bf16[576,128]{1,0:T(8,128)(2,1)S(1)} %get-tuple-element.38), channel_id=1, source_target_pairs={{0,1},{1,0},{2,3},{3,2},{4,5},{5,4},{6,7},{7,6},{8,9},{9,8},{10,11... | collective-permute-start | bytes 442376 | tf_op jit(solution)/shard_map/ppermute | solution.py:298

commit v12 on v11

--- a/solution.py
+++ b/solution.py
@@ -42,15 +42,19 @@
     cot_hbm, weight_hbm, q_hbm, k_hbm, v_hbm, same_ref, other_ref, cot_ref, weight_ref, sem
 ):
     core = lax.axis_index("seq") % 2
-    cut = weight_ref.shape[0] // 2
     cot_copy = pltpu.make_async_copy(cot_hbm, cot_ref, sem.at[0])
     cot_copy.start()
+    heads = weight_ref.shape[0] // HEAD_SIZE
     halves = ((other_ref, 1 - core), (same_ref, core))
     weight_copies = []
-    for place, (_, half) in enumerate(halves):
+    for head in range(heads):
+        half = halves[2 * head // heads][1]
+        source = half * (heads // 2) + head % (heads // 2)
         weight_copies.append(
             pltpu.make_async_copy(
-                weight_hbm.at[at(half, cut)], weight_ref.at[at(place, cut)], sem.at[1 + place]
+                weight_hbm.at[at(source, HEAD_SIZE)],
+                weight_ref.at[pl.ds(head * HEAD_SIZE, HEAD_SIZE)],
+                sem.at[7 + head],
             )
         )
         weight_copies[-1].start()
@@ -63,30 +67,31 @@
                 pltpu.make_async_copy(
                     source.at[:, at(half, cols)],
                     target.at[:, pl.ds(first, cols)],
-                    sem.at[3 + 3 * place + which],
+                    sem.at[1 + 3 * place + which],
                 )
             )
             plain_copies[-1].start()
             first += cols
     cot_copy.wait()
-    for place, (target, _) in enumerate(halves):
-        weight_copies[place].wait()
-        grads_t = dot_nt(weight_ref[place * cut : (place + 1) * cut], cot_ref[...])
-        for h in range(cut // HEAD_SIZE):
-            target[:, first + h * HEAD_SIZE : first + (h + 1) * HEAD_SIZE] = grads_t[
-                h * HEAD_SIZE : (h + 1) * HEAD_SIZE
-            ].astype(jnp.bfloat16)
+    for head, copy in enumerate(weight_copies):
+        copy.wait()
+        place = first + head % (heads // 2) * HEAD_SIZE
+        halves[2 * head // heads][0][:, place : place + HEAD_SIZE] = dot_nt(
+            weight_ref[head * HEAD_SIZE : (head + 1) * HEAD_SIZE], cot_ref[...]
+        ).astype(jnp.bfloat16)
     for copy in plain_copies:
         copy.wait()
 
 
 def turn_kernel(
-    normed_hbm, cot_hbm, _, keep_ref, give_ref, normed_ref, cot_ref, turned_ref, sem
+    normed_hbm, cot_hbm, block_hbm, _, __, keep_ref, give_ref, own_ref, normed_ref, cot_ref, turned_ref, sem
 ):
     me = lax.axis_index("seq")
     cut = keep_ref.shape[2]
     copies = []
-    for which, (source, target) in enumerate(((normed_hbm, normed_ref), (cot_hbm, cot_ref))):
+    for which, (source, target) in enumerate(
+        ((normed_hbm, normed_ref), (cot_hbm, cot_ref), (block_hbm, own_ref))
+    ):
         copies.append(pltpu.make_async_copy(source, target, sem.at[which]))
         copies[-1].start()
     for which, ref in enumerate((normed_ref, cot_ref)):
@@ -95,11 +100,10 @@
         for chip in range(keep_ref.shape[0]):
             keep_ref[chip, which] = turned_ref[which, at(me ^ (2 * chip), cut)]
             give_ref[chip, which] = turned_ref[which, at(me ^ (2 * chip + 1), cut)]
-
-
-def join_kernel(keep_ref, got_ref, block_ref, *joined_refs):
-    joined_refs, own_ref = joined_refs[:-1], joined_refs[-1]
-    own_ref[...] = block_ref[...]
+    copies[2].wait()
+
+
+def join_kernel(keep_ref, got_ref, *joined_refs):
     for chip, ref in enumerate(joined_refs):
         ref[0] = keep_ref[chip]
         ref[1] = got_ref[chip]
@@ -270,6 +274,11 @@
         wvalue_ref[:, at(half, kv_cols)] = dot_nt(joined_ref[0], ref[q_cols:])
 
 
+def add_kernel(own_ref, arrived_ref, sum_ref):
+    total = own_ref[...].astype(jnp.float32) + arrived_ref[...].astype(jnp.float32)
+    sum_ref[...] = total.astype(jnp.bfloat16)
+
+
 def sum_kernel(_, own_ref, *refs):
     total = own_ref[...]
     for arrived_ref in refs[:-1]:
@@ -326,7 +335,7 @@
         scratch=(
             pltpu.VMEM(out_cotangent.shape, bf16),
             pltpu.VMEM(output_weight.shape, bf16),
-            pltpu.SemaphoreType.DMA((9,)),
+            pltpu.SemaphoreType.DMA((7 + 2 * q_cols // HEAD_SIZE,)),
         ),
         flops=4 * rows * model * q_cols,
         moved=2 * model * (rows + 2 * q_cols),
@@ -344,27 +353,28 @@
             held[apart] = swapped(held[apart ^ through], "seq", through)
     held[1] = swapped(other, "seq", 1)
     cut = model // blocks
-    keep, give = kernel_call(
+    keep, give, held[0] = kernel_call(
         turn_kernel,
         (
             shape((blocks // 2, 2, cut, rows), bf16),
             shape((blocks // 2, 2, cut, rows), bf16),
+            shape(same.shape, bf16),
         ),
-        (normed_input, out_cotangent, held[2]),
+        (normed_input, out_cotangent, same, held[2], held[blocks // 2 + 1]),
         scratch=(
             pltpu.VMEM(normed_input.shape, bf16),
             pltpu.VMEM(out_cotangent.shape, bf16),
             pltpu.VMEM((2, model, rows), bf16),
-            pltpu.SemaphoreType.DMA((2,)),
+            pltpu.SemaphoreType.DMA((3,)),
         ),
         moved=8 * rows * model,
         room=8,
     )
-    *columns, held[0] = kernel_call(
+    columns = kernel_call(
         join_kernel,
-        (shape((2, 2, cut, rows), bf16),) * (blocks // 2) + (shape(same.shape, bf16),),
-        (keep, swapped(give, "seq", 1), same),
-        in_vmem=range(3),
+        (shape((2, 2, cut, rows), bf16),) * (blocks // 2),
+        (keep, swapped(give, "seq", 1)),
+        in_vmem=range(2),
         moved=8 * rows * model,
         room=4,
     )
@@ -397,21 +407,28 @@
         moved=2 * tokens * packed_cols,
     )
     dx_got = swapped(dx_far, "seq", 1)
-    aparts = tuple(range(groups - 1, -1, -1))
     terms = {}
-    for chosen in (aparts[: groups // 2], aparts[groups // 2 :]):
+    for chosen in ((groups - 1,), tuple(range(groups - 2, -1, -1))):
         made = kernel_call(
             functools.partial(input_terms_kernel, chosen),
-            tuple(shape((model // groups, rows), bf16 if apart else f32) for apart in chosen),
+            tuple(shape((model // groups, rows), f32 if not apart else bf16) for apart in chosen),
             (dx_own, dx_got, query_weight, key_matrix, value_matrix),
             in_vmem=range(5),
             scratch=(pltpu.VMEM((rows, 2 * (q_cols + 2 * kv_cols)), bf16),),
-            flops=2 * rows * model * (q_cols + 2 * kv_cols),
-            moved=2 * model * (q_cols + 2 * kv_cols),
+            flops=2 * len(chosen) * rows * (model // groups) * 2 * (q_cols + 2 * kv_cols),
+            moved=2 * len(chosen) * (model // groups) * 2 * (q_cols + 2 * kv_cols),
             room=4,
         )
         terms.update(zip(chosen, made))
-    arrived = [swapped(terms[apart], "head", apart) for apart in aparts[:-1]]
+    (pair_sum,) = kernel_call(
+        add_kernel,
+        (shape(terms[2].shape, bf16),),
+        (terms[2], swapped(terms[3], "head", 1)),
+        in_vmem=range(2),
+        moved=6 * rows * (model // groups),
+        room=4,
+    )
+    arrived = [swapped(terms[1], "head", 1), swapped(pair_sum, "head", 2)]
     grad_wvalue, grad_woutput, weights_done = kernel_call(
         weight_grad_kernel,
         (
@@ -430,7 +447,7 @@
         sum_kernel,
         (shape((model // groups, rows), bf16),),
         (weights_done, terms[0], *arrived),
-        in_vmem=range(1, groups + 1),
+        in_vmem=range(1, 4),
         moved=4 * groups * (model // groups) * rows,
     )
     return (grad_input.T, grad_wvalue, grad_woutput.T)
@@ -444,7 +461,7 @@
     blocks, groups = lax.axis_size("seq"), lax.axis_size("head")
     whole_window = normed_input.shape[0] * blocks <= WINDOW_LENGTH
     two_heads = stored_keys.shape[1] == 2 * HEAD_SIZE
-    paired = blocks > 1 and power_of_two(blocks) and power_of_two(groups)
+    paired = blocks >= 4 and power_of_two(blocks) and groups == 4
     plan = gathered_plan if whole_window and two_heads and paired else windowed_plan
     return plan(normed_input, stored_queries, stored_keys, *others)
 

time: 61.2 us -> 50.3 us (0.82)
  waiting for transfers between devices: 22.6 us -> 13.2 us
  starting transfers between devices: 20.9 us -> 18.9 us
    ppermute x16, waiting for transfers between devices: 22.6 us -> 13.2 us  [swapped(): lax.ppermute(value, axis, [(place, place ^ apart) for place in range(coun...]
    ppermute x16, starting transfers between devices: 20.9 us -> 18.9 us  [swapped(): lax.ppermute(value, axis, [(place, place ^ apart) for place in range(coun...]
    pallas_call x8 -> x9, Pallas kernels: 14.8 us -> 15.3 us  [kernel_call(): pl.pallas_call(body, out_shape=outs, in_specs=[vmem if place in in_vmem e...]
  transfers between devices with their start and end apart: 16 -> 16, of which waited for: 9 -> 5; matrix products, arithmetic and copies ran while one was open for 0% -> 0% of each run, Pallas kernels for 6% -> 21%
where the time goes in v12:
time: 50.3 us; the launch traced here: 50.1 us
  starting transfers between devices  18.9 us (38%)
  Pallas kernels  15.3 us (30%)
  waiting for transfers between devices  13.2 us (26%)
  local copies, waits for them, and re-layouts  2.01 us (4%)
  between operations  0.75 us (1%)
    ppermute x16, starting transfers between devices, swapped(): lax.ppermute(value, axis, [(place, place ^ apart) for place in range(coun...  18.9 us
    pallas_call x9, Pallas kernels, kernel_call(): pl.pallas_call(body, out_shape=outs, in_specs=[vmem if place in in_vmem e...  15.3 us
    ppermute x16, waiting for transfers between devices, swapped(): lax.ppermute(value, axis, [(place, place ^ apart) for place in range(coun...  13.2 us
    unnamed x12, local copies, waits for them, and re-layouts  2.01 us
  transfers between devices with their start and end apart: 16, of which 5 were waited for; matrix products, arithmetic and copies ran while one was open for 0% of the time, Pallas kernels for 21%

profile of v12, /device:TPU:0, one launch (start us, length us, event | category | flops | bytes accessed | tf_op | source)
XLA Modules:
  0.0 50.1 jit_solution(1831605694646050530)
XLA Ops:
  0.6 4.0 %shard_map.112 = (bf16[128,768]{1,0:T(8,128)(2,1)}, bf16[128,768]{1,0:T(8,128)(2,1)}) custom-call(bf16[128,2304]{1,0:T(8,128)(2,1)} %cot_hbm.3, bf16[512,2304]{1,0:T(8,128)(2,1)} %weight_hbm.1, bf16[128,512]{1,0:T(8,128)(2,1)} %q_hbm.1, bf16[128,256]{1,0:T(8,128)(2,1)} %k_hbm.1, bf16[128,256]{1,0:T(8,128)(2,1)} %v_hbm.1), custom_call_target="tpu_custom_call" | custom-call | flops 301989888 | bytes 2949120 | tf_op jit(solution)/shard_map/pallas_call | solution.py:294
  4.6 3.0 %collective-permute-start = (bf16[128,768]{1,0:T(8,128)(2,1)}, bf16[128,768]{1,0:T(8,128)(2,1)S(1)}, u32[]{:S(2)}, u32[]{:S(2)}) collective-permute-start(bf16[128,768]{1,0:T(8,128)(2,1)} %get-tuple-element.21.block_hbm), channel_id=1, source_target_pairs={{0,8},{4,12},{8,0},{12,4},{16,24},{20,28},{24,16},{28,20},{1,9},{5... | collective-permute-start | bytes 589832 | tf_op jit(solution)/shard_map/ppermute | solution.py:307
  7.6 0.7 %collective-permute-start.1 = (bf16[128,768]{1,0:T(8,128)(2,1)}, bf16[128,768]{1,0:T(8,128)(2,1)S(1)}, u32[]{:S(2)}, u32[]{:S(2)}) collective-permute-start(bf16[128,768]{1,0:T(8,128)(2,1)} %get-tuple-element.22), channel_id=1, source_target_pairs={{0,20},{4,16},{8,28},{12,24},{16,4},{20,0},{24,12},{28,8},{1,21},{... | collective-permute-start | bytes 589832 | tf_op jit(solution)/shard_map/ppermute | solution.py:307
  8.3 1.0 %collective-permute-start.2 = (bf16[128,768]{1,0:T(8,128)(2,1)}, bf16[128,768]{1,0:T(8,128)(2,1)S(1)}, u32[]{:S(2)}, u32[]{:S(2)}) collective-permute-start(bf16[128,768]{1,0:T(8,128)(2,1)} %get-tuple-element.22), channel_id=1, source_target_pairs={{0,4},{4,0},{8,12},{12,8},{16,20},{20,16},{24,28},{28,24},{1,5},{5... | collective-permute-start | bytes 589832 | tf_op jit(solution)/shard_map/ppermute | solution.py:307
  9.8 3.4 %collective-permute-done._.refs_2_ = bf16[128,768]{1,0:T(8,128)(2,1)S(1)} collective-permute-done((bf16[128,768]{1,0:T(8,128)(2,1)}, bf16[128,768]{1,0:T(8,128)(2,1)S(1)}, u32[]{:S(2)}, u32[]{:S(2)}) %collective-permute-start) | collective-permute-done | bytes 196640 | tf_op jit(solution)/shard_map/ppermute | solution.py:307
  13.2 2.4 %collective-permute-start.5 = (bf16[128,768]{1,0:T(8,128)(2,1)S(1)}, bf16[128,768]{1,0:T(8,128)(2,1)S(1)}, u32[]{:S(2)}, u32[]{:S(2)}) collective-permute-start(bf16[128,768]{1,0:T(8,128)(2,1)S(1)} %collective-permute-done._.refs_2_), channel_id=1, source_target_pairs={{0,16},{4,20},{8,24},{12,28},{16,0},{20,4},{24,8},{28,12},{1,17},{... | collective-permute-start | bytes 589832 | tf_op jit(solution)/shard_map/ppermute | solution.py:307
  15.6 1.5 %collective-permute-start.6 = (bf16[128,768]{1,0:T(8,128)(2,1)S(1)}, bf16[128,768]{1,0:T(8,128)(2,1)S(1)}, u32[]{:S(2)}, u32[]{:S(2)}) collective-permute-start(bf16[128,768]{1,0:T(8,128)(2,1)S(1)} %collective-permute-done.1.__.refs_5_), channel_id=1, source_target_pairs={{0,8},{4,12},{8,0},{12,4},{16,24},{20,28},{24,16},{28,20},{1,9},{5... | collective-permute-start | bytes 589832 | tf_op jit(solution)/shard_map/ppermute | solution.py:307
  17.1 1.1 %copy-done.4 = bf16[128,2304]{1,0:T(8,128)(2,1)S(1)} copy-done((bf16[128,2304]{1,0:T(8,128)(2,1)S(1)}, bf16[128,2304]{1,0:T(8,128)(2,1)}, u32[]{:S(2)}) %copy-start.4) | copy-done | bytes 589848
  18.2 0.9 %copy-done.5 = bf16[128,768]{1,0:T(8,128)(2,1)S(1)} copy-done((bf16[128,768]{1,0:T(8,128)(2,1)S(1)}, bf16[128,768]{1,0:T(8,128)(2,1)}, u32[]{:S(2)}) %copy-start.5) | copy-done | bytes 196632
  19.1 1.1 %shard_map.113 = (bf16[4,2,288,128]{3,2,1,0:T(8,128)(2,1)S(1)}, bf16[4,2,288,128]{3,2,1,0:T(8,128)(2,1)S(1)}, bf16[128,768]{1,0:T(8,128)(2,1)S(1)}) custom-call(bf16[128,2304]{1,0:T(8,128)(2,1)S(1)} %copy-done.4, bf16[128,2304]{1,0:T(8,128)(2,1)S(1)} %copy-done.3, bf16[128,768]{1,0:T(8,128)(2,1)S(1)} %copy-done.5, ...), custom_call_target="tpu_custom_call" | custom-call | bytes 2359296 | tf_op jit(solution)/shard_map/pallas_call | solution.py:294
  20.3 3.1 %collective-permute-done.5.refs_6_ = bf16[128,768]{1,0:T(8,128)(2,1)S(1)} collective-permute-done((bf16[128,768]{1,0:T(8,128)(2,1)S(1)}, bf16[128,768]{1,0:T(8,128)(2,1)S(1)}, u32[]{:S(2)}, u32[]{:S(2)}) %collective-permute-start.5) | collective-permute-done | bytes 196640 | tf_op jit(solution)/shard_map/ppermute | solution.py:307
  23.5 5.7 %shard_map.114 = (bf16[128,512]{1,0:T(8,128)(2,1)S(1)}, bf16[128,512]{1,0:T(8,128)(2,1)S(1)}, bf16[384,1024]{1,0:T(8,128)(2,1)S(1)}) custom-call(bf16[128,768]{1,0:T(8,128)(2,1)S(1)} %get-tuple-element.23.refs_0_, bf16[128,768]{1,0:T(8,128)(2,1)S(1)} %collective-permute-done.2.refs_1_, bf16[128,768]{1,0:T(8,128)(2,1)S(1)} %collective-permute-done._.refs_2_, ...), custom_call_target="tpu_custom_call" | custom-call | flops 2147483648 | bytes 1572864 | tf_op jit(solution)/shard_map/pallas_call | solution.py:294
  30.0 1.1 %collective-permute-start.10 = (bf16[2,2,288,128]{3,2,1,0:T(8,128)(2,1)S(1)}, bf16[2,2,288,128]{3,2,1,0:T(8,128)(2,1)S(1)}, u32[]{:S(2)}, u32[]{:S(2)}) collective-permute-start(bf16[2,2,288,128]{3,2,1,0:T(8,128)(2,1)S(1)} %get-tuple-element.29), channel_id=1, source_target_pairs={{0,16},{4,20},{8,24},{12,28},{16,0},{20,4},{24,8},{28,12},{1,17},{... | collective-permute-start | bytes 884744 | tf_op jit(solution)/shard_map/ppermute | solution.py:307
  31.1 2.1 %collective-permute-start.11 = (bf16[2,2,288,128]{3,2,1,0:T(8,128)(2,1)S(1)}, bf16[2,2,288,128]{3,2,1,0:T(8,128)(2,1)S(1)}, u32[]{:S(2)}, u32[]{:S(2)}) collective-permute-start(bf16[2,2,288,128]{3,2,1,0:T(8,128)(2,1)S(1)} %get-tuple-element.30), channel_id=1, source_target_pairs={{0,24},{4,28},{8,16},{12,20},{16,8},{20,12},{24,0},{28,4},{1,25},{... | collective-permute-start | bytes 884744 | tf_op jit(solution)/shard_map/ppermute | solution.py:307
  33.1 0.5 %shard_map.118 = bf16[576,128]{1,0:T(8,128)(2,1)S(1)} custom-call(bf16[128,512]{1,0:T(8,128)(2,1)S(1)} %get-tuple-element.32.own_ref, bf16[128,512]{1,0:T(8,128)(2,1)S(1)} %collective-permute-done.12.far_ref, bf16[2304,512]{1,0:T(8,128)(2,1)S(1)} %copy-done, bf16[2304,256]{1,0:T(8,128)(2,1)S(1)} %copy-done.1, bf16[2304,256]{1,0:T(8,128)(2,1)S(1)} %copy-done.2), custom_call_target="tpu_custom_call" | custom-call | flops 150994944 | bytes 1179648 | tf_op jit(solution)/shard_map/pallas_call | solution.py:294
  33.7 1.6 %collective-permute-start.14 = (bf16[576,128]{1,0:T(8,128)(2,1)S(1)}, bf16[576,128]{1,0:T(8,128)(2,1)S(1)}, u32[]{:S(2)}, u32[]{:S(2)}) collective-permute-start(bf16[576,128]{1,0:T(8,128)(2,1)S(1)} %shard_map.118), channel_id=1, source_target_pairs={{0,1},{1,0},{2,3},{3,2},{4,5},{5,4},{6,7},{7,6},{8,9},{9,8},{10,11... | collective-permute-start | bytes 442376 | tf_op jit(solution)/shard_map/ppermute | solution.py:307
  35.3 1.1 %shard_map.117 = (bf16[576,128]{1,0:T(8,128)(2,1)S(1)}, bf16[576,128]{1,0:T(8,128)(2,1)S(1)}, f32[576,128]{1,0:T(8,128)S(1)}) custom-call(bf16[128,512]{1,0:T(8,128)(2,1)S(1)} %get-tuple-element.32.own_ref, bf16[128,512]{1,0:T(8,128)(2,1)S(1)} %collective-permute-done.12.far_ref, bf16[2304,512]{1,0:T(8,128)(2,1)S(1)} %copy-done, ...), custom_call_target="tpu_custom_call" | custom-call | flops 452984832 | bytes 3538944 | tf_op jit(solution)/shard_map/pallas_call | solution.py:294
  36.4 2.8 %collective-permute-done.14.arrived_ref = bf16[576,128]{1,0:T(8,128)(2,1)S(1)} collective-permute-done((bf16[576,128]{1,0:T(8,128)(2,1)S(1)}, bf16[576,128]{1,0:T(8,128)(2,1)S(1)}, u32[]{:S(2)}, u32[]{:S(2)}) %collective-permute-start.14) | collective-permute-done | bytes 147488 | tf_op jit(solution)/shard_map/ppermute | solution.py:307
  39.3 1.6 %collective-permute-start.13 = (bf16[576,128]{1,0:T(8,128)(2,1)S(1)}, bf16[576,128]{1,0:T(8,128)(2,1)S(1)}, u32[]{:S(2)}, u32[]{:S(2)}) collective-permute-start(bf16[576,128]{1,0:T(8,128)(2,1)S(1)} %get-tuple-element.35), channel_id=1, source_target_pairs={{0,1},{1,0},{2,3},{3,2},{4,5},{5,4},{6,7},{7,6},{8,9},{9,8},{10,11... | collective-permute-start | bytes 442376 | tf_op jit(solution)/shard_map/ppermute | solution.py:307
  40.9 2.7 %collective-permute-start.15 = (bf16[576,128]{1,0:T(8,128)(2,1)S(1)}, bf16[576,128]{1,0:T(8,128)(2,1)S(1)}, u32[]{:S(2)}, u32[]{:S(2)}) collective-permute-start(bf16[576,128]{1,0:T(8,128)(2,1)S(1)} %shard_map.119), channel_id=1, source_target_pairs={{0,2},{1,3},{2,0},{3,1},{4,6},{5,7},{6,4},{7,5},{8,10},{9,11},{10,... | collective-permute-start | bytes 442376 | tf_op jit(solution)/shard_map/ppermute | solution.py:307
  43.5 2.0 %collective-permute-done.11.refs_3_ = bf16[2,2,288,128]{3,2,1,0:T(8,128)(2,1)S(1)} collective-permute-done((bf16[2,2,288,128]{3,2,1,0:T(8,128)(2,1)S(1)}, bf16[2,2,288,128]{3,2,1,0:T(8,128)(2,1)S(1)}, u32[]{:S(2)}, u32[]{:S(2)}) %collective-permute-start.11) | collective-permute-done | bytes 294944 | tf_op jit(solution)/shard_map/ppermute | solution.py:307
  45.5 2.0 %shard_map.116 = (f32[288,256]{1,0:T(8,128)}, f32[288,512]{1,0:T(8,128)}, f32[8,128]{1,0:T(8,128)S(1)}) custom-call(bf16[384,1024]{1,0:T(8,128)(2,1)S(1)} %get-tuple-element.24.own_ref, bf16[384,1024]{1,0:T(8,128)(2,1)S(1)} %collective-permute-done.7.far_ref, bf16[2,2,288,128]{3,2,1,0:T(8,128)(2,1)S(1)} %get-tuple-element.27.refs_0_, ...), custom_call_target="tpu_custom_call" | custom-call | flops 452984832 | bytes 2064384 | tf_op jit(solution)/shard_map/pallas_call | solution.py:294
  47.6 1.8 %collective-permute-done.15.refs_1_ = bf16[576,128]{1,0:T(8,128)(2,1)S(1)} collective-permute-done((bf16[576,128]{1,0:T(8,128)(2,1)S(1)}, bf16[576,128]{1,0:T(8,128)(2,1)S(1)}, u32[]{:S(2)}, u32[]{:S(2)}) %collective-permute-start.15) | collective-permute-done | bytes 147488 | tf_op jit(solution)/shard_map/ppermute | solution.py:307
  49.4 0.7 %shard_map.120 = bf16[576,128]{1,0:T(8,128)(2,1)} custom-call(f32[8,128]{1,0:T(8,128)S(1)} %get-tuple-element.31._, f32[576,128]{1,0:T(8,128)S(1)} %get-tuple-element.34.own_ref, bf16[576,128]{1,0:T(8,128)(2,1)S(1)} %collective-permute-done.13.refs_0_, bf16[576,128]{1,0:T(8,128)(2,1)S(1)} %collective-permute-done.15.refs_1_), custom_call_target="tpu_custom_call" | custom-call | bytes 1179648 | tf_op jit(solution)/shard_map/pallas_call | solution.py:294
  (29 shorter events, 1.5 us)
Async XLA Ops:
  0.6 16.5 %copy-start.3 = (bf16[128,2304]{1,0:T(8,128)(2,1)S(1)}, bf16[128,2304]{1,0:T(8,128)(2,1)}, u32[]{:S(2)}) copy-start(bf16[128,2304]{1,0:T(8,128)(2,1)} %cot_hbm.3) | copy-start | bytes 1769476
  4.6 8.6 %collective-permute-start = (bf16[128,768]{1,0:T(8,128)(2,1)}, bf16[128,768]{1,0:T(8,128)(2,1)S(1)}, u32[]{:S(2)}, u32[]{:S(2)}) collective-permute-start(bf16[128,768]{1,0:T(8,128)(2,1)} %get-tuple-element.21.block_hbm), channel_id=1, source_target_pairs={{0,8},{4,12},{8,0},{12,4},{16,24},{20,28},{24,16},{28,20},{1,9},{5... | collective-permute-start | bytes 589832 | tf_op jit(solution)/shard_map/ppermute | solution.py:307
  7.6 8.0 %collective-permute-start.1 = (bf16[128,768]{1,0:T(8,128)(2,1)}, bf16[128,768]{1,0:T(8,128)(2,1)S(1)}, u32[]{:S(2)}, u32[]{:S(2)}) collective-permute-start(bf16[128,768]{1,0:T(8,128)(2,1)} %get-tuple-element.22), channel_id=1, source_target_pairs={{0,20},{4,16},{8,28},{12,24},{16,4},{20,0},{24,12},{28,8},{1,21},{... | collective-permute-start | bytes 589832 | tf_op jit(solution)/shard_map/ppermute | solution.py:307
  8.3 11.9 %collective-permute-start.2 = (bf16[128,768]{1,0:T(8,128)(2,1)}, bf16[128,768]{1,0:T(8,128)(2,1)S(1)}, u32[]{:S(2)}, u32[]{:S(2)}) collective-permute-start(bf16[128,768]{1,0:T(8,128)(2,1)} %get-tuple-element.22), channel_id=1, source_target_pairs={{0,4},{4,0},{8,12},{12,8},{16,20},{20,16},{24,28},{28,24},{1,5},{5... | collective-permute-start | bytes 589832 | tf_op jit(solution)/shard_map/ppermute | solution.py:307
  9.3 11.1 %collective-permute-start.3 = (bf16[128,768]{1,0:T(8,128)(2,1)}, bf16[128,768]{1,0:T(8,128)(2,1)S(1)}, u32[]{:S(2)}, u32[]{:S(2)}) collective-permute-start(bf16[128,768]{1,0:T(8,128)(2,1)} %get-tuple-element.22), channel_id=1, source_target_pairs={{0,12},{4,8},{8,4},{12,0},{16,28},{20,24},{24,20},{28,16},{1,13},{... | collective-permute-start | bytes 589832 | tf_op jit(solution)/shard_map/ppermute | solution.py:307
  9.4 10.9 %collective-permute-start.4 = (bf16[128,768]{1,0:T(8,128)(2,1)}, bf16[128,768]{1,0:T(8,128)(2,1)S(1)}, u32[]{:S(2)}, u32[]{:S(2)}) collective-permute-start(bf16[128,768]{1,0:T(8,128)(2,1)} %get-tuple-element.21.block_hbm), channel_id=1, source_target_pairs={{0,16},{4,20},{8,24},{12,28},{16,0},{20,4},{24,8},{28,12},{1,17},{... | collective-permute-start | bytes 589832 | tf_op jit(solution)/shard_map/ppermute | solution.py:307
  13.2 10.2 %collective-permute-start.5 = (bf16[128,768]{1,0:T(8,128)(2,1)S(1)}, bf16[128,768]{1,0:T(8,128)(2,1)S(1)}, u32[]{:S(2)}, u32[]{:S(2)}) collective-permute-start(bf16[128,768]{1,0:T(8,128)(2,1)S(1)} %collective-permute-done._.refs_2_), channel_id=1, source_target_pairs={{0,16},{4,20},{8,24},{12,28},{16,0},{20,4},{24,8},{28,12},{1,17},{... | collective-permute-start | bytes 589832 | tf_op jit(solution)/shard_map/ppermute | solution.py:307
  15.6 7.8 %collective-permute-start.6 = (bf16[128,768]{1,0:T(8,128)(2,1)S(1)}, bf16[128,768]{1,0:T(8,128)(2,1)S(1)}, u32[]{:S(2)}, u32[]{:S(2)}) collective-permute-start(bf16[128,768]{1,0:T(8,128)(2,1)S(1)} %collective-permute-done.1.__.refs_5_), channel_id=1, source_target_pairs={{0,8},{4,12},{8,0},{12,4},{16,24},{20,28},{24,16},{28,20},{1,9},{5... | collective-permute-start | bytes 589832 | tf_op jit(solution)/shard_map/ppermute | solution.py:307
  17.1 1.1 %copy-start.4 = (bf16[128,2304]{1,0:T(8,128)(2,1)S(1)}, bf16[128,2304]{1,0:T(8,128)(2,1)}, u32[]{:S(2)}) copy-start(bf16[128,2304]{1,0:T(8,128)(2,1)} %normed_hbm.1) | copy-start | bytes 1769476
  18.2 0.9 %copy-start.5 = (bf16[128,768]{1,0:T(8,128)(2,1)S(1)}, bf16[128,768]{1,0:T(8,128)(2,1)}, u32[]{:S(2)}) copy-start(bf16[128,768]{1,0:T(8,128)(2,1)} %get-tuple-element.21.block_hbm) | copy-start | bytes 589828
  20.2 9.1 %collective-permute-start.8 = (bf16[4,2,288,128]{3,2,1,0:T(8,128)(2,1)S(1)}, bf16[4,2,288,128]{3,2,1,0:T(8,128)(2,1)S(1)}, u32[]{:S(2)}, u32[]{:S(2)}) collective-permute-start(bf16[4,2,288,128]{3,2,1,0:T(8,128)(2,1)S(1)} %get-tuple-element.26), channel_id=1, source_target_pairs={{0,4},{4,0},{8,12},{12,8},{16,20},{20,16},{24,28},{28,24},{1,5},{5... | collective-permute-start | bytes 1769480 | tf_op jit(solution)/shard_map/ppermute | solution.py:307
  23.5 9.7 %copy-start = (bf16[2304,512]{1,0:T(8,128)(2,1)S(1)}, bf16[2304,512]{1,0:T(8,128)(2,1)}, u32[]{:S(2)}) copy-start(bf16[2304,512]{1,0:T(8,128)(2,1)} %wq_ref.3) | copy-start | bytes 7077892
  23.5 9.7 %copy-start.1 = (bf16[2304,256]{1,0:T(8,128)(2,1)S(1)}, bf16[2304,256]{1,0:T(8,128)(2,1)}, u32[]{:S(2)}) copy-start(bf16[2304,256]{1,0:T(8,128)(2,1)} %wk_ref.3) | copy-start | bytes 3538948
  23.5 9.7 %copy-start.2 = (bf16[2304,256]{1,0:T(8,128)(2,1)S(1)}, bf16[2304,256]{1,0:T(8,128)(2,1)}, u32[]{:S(2)}) copy-start(bf16[2304,256]{1,0:T(8,128)(2,1)} %wv_ref.3) | copy-start | bytes 3538948
  29.2 16.3 %collective-permute-start.7 = (bf16[384,1024]{1,0:T(8,128)(2,1)S(1)}, bf16[384,1024]{1,0:T(8,128)(2,1)S(1)}, u32[]{:S(2)}, u32[]{:S(2)}) collective-permute-start(bf16[384,1024]{1,0:T(8,128)(2,1)S(1)} %get-tuple-element.24.own_ref), channel_id=1, source_target_pairs={{0,4},{4,0},{8,12},{12,8},{16,20},{20,16},{24,28},{28,24},{1,5},{5... | collective-permute-start | bytes 2359304 | tf_op jit(solution)/shard_map/ppermute | solution.py:307
  29.4 11.5 %collective-permute-start.9 = (bf16[2,2,288,128]{3,2,1,0:T(8,128)(2,1)S(1)}, bf16[2,2,288,128]{3,2,1,0:T(8,128)(2,1)S(1)}, u32[]{:S(2)}, u32[]{:S(2)}) collective-permute-start(bf16[2,2,288,128]{3,2,1,0:T(8,128)(2,1)S(1)} %get-tuple-element.28), channel_id=1, source_target_pairs={{0,8},{4,12},{8,0},{12,4},{16,24},{20,28},{24,16},{28,20},{1,9},{5... | collective-permute-start | bytes 884744 | tf_op jit(solution)/shard_map/ppermute | solution.py:307
  29.5 3.6 %collective-permute-start.12 = (bf16[128,512]{1,0:T(8,128)(2,1)S(1)}, bf16[128,512]{1,0:T(8,128)(2,1)S(1)}, u32[]{:S(2)}, u32[]{:S(2)}) collective-permute-start(bf16[128,512]{1,0:T(8,128)(2,1)S(1)} %get-tuple-element.33), channel_id=1, source_target_pairs={{0,4},{4,0},{8,12},{12,8},{16,20},{20,16},{24,28},{28,24},{1,5},{5... | collective-permute-start | bytes 393224 | tf_op jit(solution)/shard_map/ppermute | solution.py:307
  30.0 13.6 %collective-permute-start.10 = (bf16[2,2,288,128]{3,2,1,0:T(8,128)(2,1)S(1)}, bf16[2,2,288,128]{3,2,1,0:T(8,128)(2,1)S(1)}, u32[]{:S(2)}, u32[]{:S(2)}) collective-permute-start(bf16[2,2,288,128]{3,2,1,0:T(8,128)(2,1)S(1)} %get-tuple-element.29), channel_id=1, source_target_pairs={{0,16},{4,20},{8,24},{12,28},{16,0},{20,4},{24,8},{28,12},{1,17},{... | collective-permute-start | bytes 884744 | tf_op jit(solution)/shard_map/ppermute | solution.py:307
  31.1 14.5 %collective-permute-start.11 = (bf16[2,2,288,128]{3,2,1,0:T(8,128)(2,1)S(1)}, bf16[2,2,288,128]{3,2,1,0:T(8,128)(2,1)S(1)}, u32[]{:S(2)}, u32[]{:S(2)}) collective-permute-start(bf16[2,2,288,128]{3,2,1,0:T(8,128)(2,1)S(1)} %get-tuple-element.30), channel_id=1, source_target_pairs={{0,24},{4,28},{8,16},{12,20},{16,8},{20,12},{24,0},{28,4},{1,25},{... | collective-permute-start | bytes 884744 | tf_op jit(solution)/shard_map/ppermute | solution.py:307
  33.7 5.6 %collective-permute-start.14 = (bf16[576,128]{1,0:T(8,128)(2,1)S(1)}, bf16[576,128]{1,0:T(8,128)(2,1)S(1)}, u32[]{:S(2)}, u32[]{:S(2)}) collective-permute-start(bf16[576,128]{1,0:T(8,128)(2,1)S(1)} %shard_map.118), channel_id=1, source_target_pairs={{0,1},{1,0},{2,3},{3,2},{4,5},{5,4},{6,7},{7,6},{8,9},{9,8},{10,11... | collective-permute-start | bytes 442376 | tf_op jit(solution)/shard_map/ppermute | solution.py:307
  39.3 8.3 %collective-permute-start.13 = (bf16[576,128]{1,0:T(8,128)(2,1)S(1)}, bf16[576,128]{1,0:T(8,128)(2,1)S(1)}, u32[]{:S(2)}, u32[]{:S(2)}) collective-permute-start(bf16[576,128]{1,0:T(8,128)(2,1)S(1)} %get-tuple-element.35), channel_id=1, source_target_pairs={{0,1},{1,0},{2,3},{3,2},{4,5},{5,4},{6,7},{7,6},{8,9},{9,8},{10,11... | collective-permute-start | bytes 442376 | tf_op jit(solution)/shard_map/ppermute | solution.py:307
  40.9 8.5 %collective-permute-start.15 = (bf16[576,128]{1,0:T(8,128)(2,1)S(1)}, bf16[576,128]{1,0:T(8,128)(2,1)S(1)}, u32[]{:S(2)}, u32[]{:S(2)}) collective-permute-start(bf16[576,128]{1,0:T(8,128)(2,1)S(1)} %shard_map.119), channel_id=1, source_target_pairs={{0,2},{1,3},{2,0},{3,1},{4,6},{5,7},{6,4},{7,5},{8,10},{9,11},{10,... | collective-permute-start | bytes 442376 | tf_op jit(solution)/shard_map/ppermute | solution.py:307

commit v13 on v12

--- a/solution.py
+++ b/solution.py
@@ -42,22 +42,30 @@
     cot_hbm, weight_hbm, q_hbm, k_hbm, v_hbm, same_ref, other_ref, cot_ref, weight_ref, sem
 ):
     core = lax.axis_index("seq") % 2
-    cot_copy = pltpu.make_async_copy(cot_hbm, cot_ref, sem.at[0])
-    cot_copy.start()
-    heads = weight_ref.shape[0] // HEAD_SIZE
     halves = ((other_ref, 1 - core), (same_ref, core))
-    weight_copies = []
-    for head in range(heads):
-        half = halves[2 * head // heads][1]
-        source = half * (heads // 2) + head % (heads // 2)
-        weight_copies.append(
-            pltpu.make_async_copy(
-                weight_hbm.at[at(source, HEAD_SIZE)],
-                weight_ref.at[pl.ds(head * HEAD_SIZE, HEAD_SIZE)],
-                sem.at[7 + head],
+    rows = weight_ref.shape[0] // 2
+    pieces = (sem.shape[0] - 6) // 3
+    cut = weight_ref.shape[1] // pieces
+    model_copies = []
+    for piece in range(pieces):
+        part = pl.ds(piece * cut, cut)
+        model_copies.append(
+            [
+                pltpu.make_async_copy(
+                    cot_hbm.at[:, part], cot_ref.at[:, part], sem.at[6 + 3 * piece]
+                )
+            ]
+        )
+        for place, (_, half) in enumerate(halves):
+            model_copies[-1].append(
+                pltpu.make_async_copy(
+                    weight_hbm.at[at(half, rows), part],
+                    weight_ref.at[pl.ds(place * rows, rows), part],
+                    sem.at[7 + 3 * piece + place],
+                )
             )
-        )
-        weight_copies[-1].start()
+        for copy in model_copies[-1]:
+            copy.start()
     plain_copies = []
     for place, (target, half) in enumerate(halves):
         first = 0
@@ -67,18 +75,24 @@
                 pltpu.make_async_copy(
                     source.at[:, at(half, cols)],
                     target.at[:, pl.ds(first, cols)],
-                    sem.at[1 + 3 * place + which],
+                    sem.at[3 * place + which],
                 )
             )
             plain_copies[-1].start()
             first += cols
-    cot_copy.wait()
-    for head, copy in enumerate(weight_copies):
-        copy.wait()
-        place = first + head % (heads // 2) * HEAD_SIZE
-        halves[2 * head // heads][0][:, place : place + HEAD_SIZE] = dot_nt(
-            weight_ref[head * HEAD_SIZE : (head + 1) * HEAD_SIZE], cot_ref[...]
-        ).astype(jnp.bfloat16)
+    total = None
+    for piece in range(pieces):
+        for copy in model_copies[piece]:
+            copy.wait()
+        part = slice(piece * cut, (piece + 1) * cut)
+        product = dot_nt(weight_ref[:, part], cot_ref[:, part])
+        total = product if total is None else total + product
+    for place, (target, _) in enumerate(halves):
+        for head in range(rows // HEAD_SIZE):
+            row = place * rows + head * HEAD_SIZE
+            target[:, first + head * HEAD_SIZE : first + (head + 1) * HEAD_SIZE] = total[
+                row : row + HEAD_SIZE
+            ].astype(jnp.bfloat16)
     for copy in plain_copies:
         copy.wait()
 
@@ -233,10 +247,8 @@
         target[:, value_cols] = parts_ref[heads * HEAD_SIZE :, at(2 * chip + half, rows)].T
 
 
-def input_terms_kernel(
-    apart_groups, own_ref, far_ref, wq_ref, wk_ref, wv_ref, *refs
-):
-    terms, dx_ref = refs[:-1], refs[-1]
+def input_terms_kernel(apart_groups, own_ref, far_ref, wq_ref, wk_ref, wv_ref, *refs):
+    terms, dx_ref = refs[-1 - len(apart_groups) : -1], refs[-1]
     core = lax.axis_index("seq") % 2
     group = lax.axis_index("head")
     q_cols = wq_ref.shape[1] // 2
@@ -327,6 +339,7 @@
     kv_cols = HEAD_SIZE
     wide = 2 * QUERIES_PER_KEY * rows
     packed_cols = 2 * q_cols + 2 * kv_cols
+    pieces = 3 if model % (6 * HEAD_SIZE) == 0 else 1
     shape = jax.ShapeDtypeStruct
     same, other = kernel_call(
         out_grad_kernel,
@@ -335,7 +348,7 @@
         scratch=(
             pltpu.VMEM(out_cotangent.shape, bf16),
             pltpu.VMEM(output_weight.shape, bf16),
-            pltpu.SemaphoreType.DMA((7 + 2 * q_cols // HEAD_SIZE,)),
+            pltpu.SemaphoreType.DMA((6 + 3 * pieces,)),
         ),
         flops=4 * rows * model * q_cols,
         moved=2 * model * (rows + 2 * q_cols),
@@ -403,16 +416,15 @@
             pltpu.VMEM((HEAD_SIZE, wide), f32),
             pltpu.VMEM((2 * rows, HEAD_SIZE), f32),
         ),
-        flops=8 * tokens * tokens * q_cols,
         moved=2 * tokens * packed_cols,
     )
     dx_got = swapped(dx_far, "seq", 1)
     terms = {}
-    for chosen in ((groups - 1,), tuple(range(groups - 2, -1, -1))):
+    for chosen, waited in (((3,), []), ((2, 1, 0), [columns[1], columns[blocks // 4]])):
         made = kernel_call(
             functools.partial(input_terms_kernel, chosen),
             tuple(shape((model // groups, rows), f32 if not apart else bf16) for apart in chosen),
-            (dx_own, dx_got, query_weight, key_matrix, value_matrix),
+            (dx_own, dx_got, query_weight, key_matrix, value_matrix, *waited),
             in_vmem=range(5),
             scratch=(pltpu.VMEM((rows, 2 * (q_cols + 2 * kv_cols)), bf16),),
             flops=2 * len(chosen) * rows * (model // groups) * 2 * (q_cols + 2 * kv_cols),

time: 50.3 us -> 64.1 us (1.27)
  waiting for transfers between devices: 13.2 us -> 26.3 us
  local copies, waits for them, and re-layouts: 2.01 us -> 3.28 us
    ppermute x16, waiting for transfers between devices: 13.2 us -> 26.3 us  [swapped(): lax.ppermute(value, axis, [(place, place ^ apart) for place in range(coun...]
    unnamed x12 -> x14, local copies, waits for them, and re-layouts: 2.01 us -> 3.28 us
  transfers between devices with their start and end apart: 16 -> 16, of which waited for: 5 -> 10; matrix products, arithmetic and copies ran while one was open for 0% -> 0% of each run, Pallas kernels for 21% -> 17%
where the time goes in v13:
time: 64.1 us; the launch traced here: 63.8 us
  waiting for transfers between devices  26.3 us (41%)
  starting transfers between devices  18.4 us (29%)
  Pallas kernels  15.1 us (24%)
  local copies, waits for them, and re-layouts  3.28 us (5%)
  between operations  0.74 us (1%)
    ppermute x16, waiting for transfers between devices, swapped(): lax.ppermute(value, axis, [(place, place ^ apart) for place in range(coun...  26.3 us
    ppermute x16, starting transfers between devices, swapped(): lax.ppermute(value, axis, [(place, place ^ apart) for place in range(coun...  18.4 us
    pallas_call x9, Pallas kernels, kernel_call(): pl.pallas_call(body, out_shape=outs, in_specs=[vmem if place in in_vmem e...  15.1 us
    unnamed x14, local copies, waits for them, and re-layouts  3.28 us
  transfers between devices with their start and end apart: 16, of which 10 were waited for; matrix products, arithmetic and copies ran while one was open for 0% of the time, Pallas kernels for 17%

profile of v13, /device:TPU:0, one launch (start us, length us, event | category | flops | bytes accessed | tf_op | source)
XLA Modules:
  0.0 63.8 jit_solution(1036641293511028500)
XLA Ops:
  0.6 3.8 %shard_map.112 = (bf16[128,768]{1,0:T(8,128)(2,1)}, bf16[128,768]{1,0:T(8,128)(2,1)}) custom-call(bf16[128,2304]{1,0:T(8,128)(2,1)} %cot_hbm.3, bf16[512,2304]{1,0:T(8,128)(2,1)} %weight_hbm.1, bf16[128,512]{1,0:T(8,128)(2,1)} %q_hbm.1, bf16[128,256]{1,0:T(8,128)(2,1)} %k_hbm.1, bf16[128,256]{1,0:T(8,128)(2,1)} %v_hbm.1), custom_call_target="tpu_custom_call" | custom-call | flops 301989888 | bytes 2949120 | tf_op jit(solution)/shard_map/pallas_call | solution.py:306
  4.5 3.0 %collective-permute-start = (bf16[128,768]{1,0:T(8,128)(2,1)}, bf16[128,768]{1,0:T(8,128)(2,1)S(1)}, u32[]{:S(2)}, u32[]{:S(2)}) collective-permute-start(bf16[128,768]{1,0:T(8,128)(2,1)} %get-tuple-element.21.block_hbm), channel_id=1, source_target_pairs={{0,8},{4,12},{8,0},{12,4},{16,24},{20,28},{24,16},{28,20},{1,9},{5... | collective-permute-start | bytes 589832 | tf_op jit(solution)/shard_map/ppermute | solution.py:319
  8.1 1.0 %collective-permute-start.2 = (bf16[128,768]{1,0:T(8,128)(2,1)}, bf16[128,768]{1,0:T(8,128)(2,1)S(1)}, u32[]{:S(2)}, u32[]{:S(2)}) collective-permute-start(bf16[128,768]{1,0:T(8,128)(2,1)} %get-tuple-element.22), channel_id=1, source_target_pairs={{0,4},{4,0},{8,12},{12,8},{16,20},{20,16},{24,28},{28,24},{1,5},{5... | collective-permute-start | bytes 589832 | tf_op jit(solution)/shard_map/ppermute | solution.py:319
  9.1 3.5 %collective-permute-done._.refs_2_ = bf16[128,768]{1,0:T(8,128)(2,1)S(1)} collective-permute-done((bf16[128,768]{1,0:T(8,128)(2,1)}, bf16[128,768]{1,0:T(8,128)(2,1)S(1)}, u32[]{:S(2)}, u32[]{:S(2)}) %collective-permute-start) | collective-permute-done | bytes 196640 | tf_op jit(solution)/shard_map/ppermute | solution.py:319
  12.6 2.2 %collective-permute-done.1.__.refs_5_ = bf16[128,768]{1,0:T(8,128)(2,1)S(1)} collective-permute-done((bf16[128,768]{1,0:T(8,128)(2,1)}, bf16[128,768]{1,0:T(8,128)(2,1)S(1)}, u32[]{:S(2)}, u32[]{:S(2)}) %collective-permute-start.1) | collective-permute-done | bytes 196640 | tf_op jit(solution)/shard_map/ppermute | solution.py:319
  14.8 1.1 %copy-done.5 = bf16[128,2304]{1,0:T(8,128)(2,1)S(1)} copy-done((bf16[128,2304]{1,0:T(8,128)(2,1)S(1)}, bf16[128,2304]{1,0:T(8,128)(2,1)}, u32[]{:S(2)}) %copy-start.5) | copy-done | bytes 589848
  15.9 0.9 %copy-done.6 = bf16[128,768]{1,0:T(8,128)(2,1)S(1)} copy-done((bf16[128,768]{1,0:T(8,128)(2,1)S(1)}, bf16[128,768]{1,0:T(8,128)(2,1)}, u32[]{:S(2)}) %copy-start.6) | copy-done | bytes 196632
  16.8 1.1 %shard_map.113 = (bf16[4,2,288,128]{3,2,1,0:T(8,128)(2,1)S(1)}, bf16[4,2,288,128]{3,2,1,0:T(8,128)(2,1)S(1)}, bf16[128,768]{1,0:T(8,128)(2,1)S(1)}) custom-call(bf16[128,2304]{1,0:T(8,128)(2,1)S(1)} %copy-done.5, bf16[128,2304]{1,0:T(8,128)(2,1)S(1)} %copy-done.4, bf16[128,768]{1,0:T(8,128)(2,1)S(1)} %copy-done.6, ...), custom_call_target="tpu_custom_call" | custom-call | bytes 2359296 | tf_op jit(solution)/shard_map/pallas_call | solution.py:306
  18.1 1.9 %collective-permute-start.4 = (bf16[128,768]{1,0:T(8,128)(2,1)S(1)}, bf16[128,768]{1,0:T(8,128)(2,1)S(1)}, u32[]{:S(2)}, u32[]{:S(2)}) collective-permute-start(bf16[128,768]{1,0:T(8,128)(2,1)S(1)} %copy-done.6), channel_id=1, source_target_pairs={{0,16},{4,20},{8,24},{12,28},{16,0},{20,4},{24,8},{28,12},{1,17},{... | collective-permute-start | bytes 589832 | tf_op jit(solution)/shard_map/ppermute | solution.py:319
  20.1 2.0 %collective-permute-start.6 = (bf16[128,768]{1,0:T(8,128)(2,1)S(1)}, bf16[128,768]{1,0:T(8,128)(2,1)S(1)}, u32[]{:S(2)}, u32[]{:S(2)}) collective-permute-start(bf16[128,768]{1,0:T(8,128)(2,1)S(1)} %collective-permute-done.1.__.refs_5_), channel_id=1, source_target_pairs={{0,8},{4,12},{8,0},{12,4},{16,24},{20,28},{24,16},{28,20},{1,9},{5... | collective-permute-start | bytes 589832 | tf_op jit(solution)/shard_map/ppermute | solution.py:319
  22.1 2.9 %collective-permute-done.3.refs_3_ = bf16[128,768]{1,0:T(8,128)(2,1)S(1)} collective-permute-done((bf16[128,768]{1,0:T(8,128)(2,1)}, bf16[128,768]{1,0:T(8,128)(2,1)S(1)}, u32[]{:S(2)}, u32[]{:S(2)}) %collective-permute-start.3) | collective-permute-done | bytes 196640 | tf_op jit(solution)/shard_map/ppermute | solution.py:319
  25.8 3.6 %collective-permute-done.5.refs_6_ = bf16[128,768]{1,0:T(8,128)(2,1)S(1)} collective-permute-done((bf16[128,768]{1,0:T(8,128)(2,1)S(1)}, bf16[128,768]{1,0:T(8,128)(2,1)S(1)}, u32[]{:S(2)}, u32[]{:S(2)}) %collective-permute-start.5) | collective-permute-done | bytes 196640 | tf_op jit(solution)/shard_map/ppermute | solution.py:319
  29.7 5.7 %shard_map.114 = (bf16[128,512]{1,0:T(8,128)(2,1)S(1)}, bf16[128,512]{1,0:T(8,128)(2,1)S(1)}, bf16[384,1024]{1,0:T(8,128)(2,1)S(1)}) custom-call(bf16[128,768]{1,0:T(8,128)(2,1)S(1)} %get-tuple-element.23.refs_0_, bf16[128,768]{1,0:T(8,128)(2,1)S(1)} %collective-permute-done.2.refs_1_, bf16[128,768]{1,0:T(8,128)(2,1)S(1)} %collective-permute-done._.refs_2_, ...), custom_call_target="tpu_custom_call" | custom-call | bytes 1572864 | tf_op jit(solution)/shard_map/pallas_call | solution.py:306
  35.6 1.6 %collective-permute-start.9 = (bf16[2,2,288,128]{3,2,1,0:T(8,128)(2,1)S(1)}, bf16[2,2,288,128]{3,2,1,0:T(8,128)(2,1)S(1)}, u32[]{:S(2)}, u32[]{:S(2)}) collective-permute-start(bf16[2,2,288,128]{3,2,1,0:T(8,128)(2,1)S(1)} %get-tuple-element.28), channel_id=1, source_target_pairs={{0,8},{4,12},{8,0},{12,4},{16,24},{20,28},{24,16},{28,20},{1,9},{5... | collective-permute-start | bytes 884744 | tf_op jit(solution)/shard_map/ppermute | solution.py:319
  37.2 1.2 %collective-permute-start.10 = (bf16[2,2,288,128]{3,2,1,0:T(8,128)(2,1)S(1)}, bf16[2,2,288,128]{3,2,1,0:T(8,128)(2,1)S(1)}, u32[]{:S(2)}, u32[]{:S(2)}) collective-permute-start(bf16[2,2,288,128]{3,2,1,0:T(8,128)(2,1)S(1)} %get-tuple-element.29), channel_id=1, source_target_pairs={{0,16},{4,20},{8,24},{12,28},{16,0},{20,4},{24,8},{28,12},{1,17},{... | collective-permute-start | bytes 884744 | tf_op jit(solution)/shard_map/ppermute | solution.py:319
  39.7 1.3 %copy-done.2 = bf16[2304,256]{1,0:T(8,128)(2,1)S(1)} copy-done((bf16[2304,256]{1,0:T(8,128)(2,1)S(1)}, bf16[2304,256]{1,0:T(8,128)(2,1)}, u32[]{:S(2)}) %copy-start.2) | copy-done | bytes 1179672
  41.5 1.6 %collective-permute-start.14 = (bf16[576,128]{1,0:T(8,128)(2,1)S(1)}, bf16[576,128]{1,0:T(8,128)(2,1)S(1)}, u32[]{:S(2)}, u32[]{:S(2)}) collective-permute-start(bf16[576,128]{1,0:T(8,128)(2,1)S(1)} %shard_map.118), channel_id=1, source_target_pairs={{0,1},{1,0},{2,3},{3,2},{4,5},{5,4},{6,7},{7,6},{8,9},{9,8},{10,11... | collective-permute-start | bytes 442376 | tf_op jit(solution)/shard_map/ppermute | solution.py:319
  43.2 2.3 %collective-permute-done.9.refs_1_.refs_0_ = bf16[2,2,288,128]{3,2,1,0:T(8,128)(2,1)S(1)} collective-permute-done((bf16[2,2,288,128]{3,2,1,0:T(8,128)(2,1)S(1)}, bf16[2,2,288,128]{3,2,1,0:T(8,128)(2,1)S(1)}, u32[]{:S(2)}, u32[]{:S(2)}) %collective-permute-start.9) | collective-permute-done | bytes 294944 | tf_op jit(solution)/shard_map/ppermute | solution.py:319
  45.5 7.1 %collective-permute-done.10.refs_2_.refs_1_ = bf16[2,2,288,128]{3,2,1,0:T(8,128)(2,1)S(1)} collective-permute-done((bf16[2,2,288,128]{3,2,1,0:T(8,128)(2,1)S(1)}, bf16[2,2,288,128]{3,2,1,0:T(8,128)(2,1)S(1)}, u32[]{:S(2)}, u32[]{:S(2)}) %collective-permute-start.10) | collective-permute-done | bytes 294944 | tf_op jit(solution)/shard_map/ppermute | solution.py:319
  52.6 1.1 %shard_map.117 = (bf16[576,128]{1,0:T(8,128)(2,1)S(1)}, bf16[576,128]{1,0:T(8,128)(2,1)S(1)}, f32[576,128]{1,0:T(8,128)S(1)}) custom-call(bf16[128,512]{1,0:T(8,128)(2,1)S(1)} %get-tuple-element.32.own_ref, bf16[128,512]{1,0:T(8,128)(2,1)S(1)} %collective-permute-done.12.far_ref, bf16[2304,512]{1,0:T(8,128)(2,1)S(1)} %copy-done, ...), custom_call_target="tpu_custom_call" | custom-call | flops 452984832 | bytes 3538944 | tf_op jit(solution)/shard_map/pallas_call | solution.py:306
  53.7 1.6 %collective-permute-start.13 = (bf16[576,128]{1,0:T(8,128)(2,1)S(1)}, bf16[576,128]{1,0:T(8,128)(2,1)S(1)}, u32[]{:S(2)}, u32[]{:S(2)}) collective-permute-start(bf16[576,128]{1,0:T(8,128)(2,1)S(1)} %get-tuple-element.35), channel_id=1, source_target_pairs={{0,1},{1,0},{2,3},{3,2},{4,5},{5,4},{6,7},{7,6},{8,9},{9,8},{10,11... | collective-permute-start | bytes 442376 | tf_op jit(solution)/shard_map/ppermute | solution.py:319
  55.4 2.6 %collective-permute-start.15 = (bf16[576,128]{1,0:T(8,128)(2,1)S(1)}, bf16[576,128]{1,0:T(8,128)(2,1)S(1)}, u32[]{:S(2)}, u32[]{:S(2)}) collective-permute-start(bf16[576,128]{1,0:T(8,128)(2,1)S(1)} %shard_map.119), channel_id=1, source_target_pairs={{0,2},{1,3},{2,0},{3,1},{4,6},{5,7},{6,4},{7,5},{8,10},{9,11},{10,... | collective-permute-start | bytes 442376 | tf_op jit(solution)/shard_map/ppermute | solution.py:319
  58.1 2.0 %shard_map.116 = (f32[288,256]{1,0:T(8,128)}, f32[288,512]{1,0:T(8,128)}, f32[8,128]{1,0:T(8,128)S(1)}) custom-call(bf16[384,1024]{1,0:T(8,128)(2,1)S(1)} %get-tuple-element.24.own_ref, bf16[384,1024]{1,0:T(8,128)(2,1)S(1)} %collective-permute-done.7.far_ref, bf16[2,2,288,128]{3,2,1,0:T(8,128)(2,1)S(1)} %get-tuple-element.27.refs_0_, ...), custom_call_target="tpu_custom_call" | custom-call | flops 452984832 | bytes 2064384 | tf_op jit(solution)/shard_map/pallas_call | solution.py:306
  60.1 3.0 %collective-permute-done.15.refs_1_ = bf16[576,128]{1,0:T(8,128)(2,1)S(1)} collective-permute-done((bf16[576,128]{1,0:T(8,128)(2,1)S(1)}, bf16[576,128]{1,0:T(8,128)(2,1)S(1)}, u32[]{:S(2)}, u32[]{:S(2)}) %collective-permute-start.15) | collective-permute-done | bytes 147488 | tf_op jit(solution)/shard_map/ppermute | solution.py:319
  (31 shorter events, 4.9 us)
Async XLA Ops:
  0.6 14.2 %copy-start.4 = (bf16[128,2304]{1,0:T(8,128)(2,1)S(1)}, bf16[128,2304]{1,0:T(8,128)(2,1)}, u32[]{:S(2)}) copy-start(bf16[128,2304]{1,0:T(8,128)(2,1)} %cot_hbm.3) | copy-start | bytes 1769476
  4.4 35.3 %copy-start = (bf16[2304,512]{1,0:T(8,128)(2,1)S(1)}, bf16[2304,512]{1,0:T(8,128)(2,1)}, u32[]{:S(2)}) copy-start(bf16[2304,512]{1,0:T(8,128)(2,1)} %wq_ref.3) | copy-start | bytes 7077892
  4.4 35.3 %copy-start.1 = (bf16[2304,256]{1,0:T(8,128)(2,1)S(1)}, bf16[2304,256]{1,0:T(8,128)(2,1)}, u32[]{:S(2)}) copy-start(bf16[2304,256]{1,0:T(8,128)(2,1)} %wk_ref.3) | copy-start | bytes 3538948
  4.5 8.1 %collective-permute-start = (bf16[128,768]{1,0:T(8,128)(2,1)}, bf16[128,768]{1,0:T(8,128)(2,1)S(1)}, u32[]{:S(2)}, u32[]{:S(2)}) collective-permute-start(bf16[128,768]{1,0:T(8,128)(2,1)} %get-tuple-element.21.block_hbm), channel_id=1, source_target_pairs={{0,8},{4,12},{8,0},{12,4},{16,24},{20,28},{24,16},{28,20},{1,9},{5... | collective-permute-start | bytes 589832 | tf_op jit(solution)/shard_map/ppermute | solution.py:319
  7.5 7.3 %collective-permute-start.1 = (bf16[128,768]{1,0:T(8,128)(2,1)}, bf16[128,768]{1,0:T(8,128)(2,1)S(1)}, u32[]{:S(2)}, u32[]{:S(2)}) collective-permute-start(bf16[128,768]{1,0:T(8,128)(2,1)} %get-tuple-element.22), channel_id=1, source_target_pairs={{0,20},{4,16},{8,28},{12,24},{16,4},{20,0},{24,12},{28,8},{1,21},{... | collective-permute-start | bytes 589832 | tf_op jit(solution)/shard_map/ppermute | solution.py:319
  8.1 12.0 %collective-permute-start.2 = (bf16[128,768]{1,0:T(8,128)(2,1)}, bf16[128,768]{1,0:T(8,128)(2,1)S(1)}, u32[]{:S(2)}, u32[]{:S(2)}) collective-permute-start(bf16[128,768]{1,0:T(8,128)(2,1)} %get-tuple-element.22), channel_id=1, source_target_pairs={{0,4},{4,0},{8,12},{12,8},{16,20},{20,16},{24,28},{28,24},{1,5},{5... | collective-permute-start | bytes 589832 | tf_op jit(solution)/shard_map/ppermute | solution.py:319
  14.8 1.1 %copy-start.5 = (bf16[128,2304]{1,0:T(8,128)(2,1)S(1)}, bf16[128,2304]{1,0:T(8,128)(2,1)}, u32[]{:S(2)}) copy-start(bf16[128,2304]{1,0:T(8,128)(2,1)} %normed_hbm.1) | copy-start | bytes 1769476
  15.9 0.9 %copy-start.6 = (bf16[128,768]{1,0:T(8,128)(2,1)S(1)}, bf16[128,768]{1,0:T(8,128)(2,1)}, u32[]{:S(2)}) copy-start(bf16[128,768]{1,0:T(8,128)(2,1)} %get-tuple-element.21.block_hbm) | copy-start | bytes 589828
  17.9 17.6 %collective-permute-start.8 = (bf16[4,2,288,128]{3,2,1,0:T(8,128)(2,1)S(1)}, bf16[4,2,288,128]{3,2,1,0:T(8,128)(2,1)S(1)}, u32[]{:S(2)}, u32[]{:S(2)}) collective-permute-start(bf16[4,2,288,128]{3,2,1,0:T(8,128)(2,1)S(1)} %get-tuple-element.26), channel_id=1, source_target_pairs={{0,4},{4,0},{8,12},{12,8},{16,20},{20,16},{24,28},{28,24},{1,5},{5... | collective-permute-start | bytes 1769480 | tf_op jit(solution)/shard_map/ppermute | solution.py:319
  18.1 7.0 %collective-permute-start.3 = (bf16[128,768]{1,0:T(8,128)(2,1)}, bf16[128,768]{1,0:T(8,128)(2,1)S(1)}, u32[]{:S(2)}, u32[]{:S(2)}) collective-permute-start(bf16[128,768]{1,0:T(8,128)(2,1)} %get-tuple-element.22), channel_id=1, source_target_pairs={{0,12},{4,8},{8,4},{12,0},{16,28},{20,24},{24,20},{28,16},{1,13},{... | collective-permute-start | bytes 589832 | tf_op jit(solution)/shard_map/ppermute | solution.py:319
  18.1 7.8 %collective-permute-start.4 = (bf16[128,768]{1,0:T(8,128)(2,1)S(1)}, bf16[128,768]{1,0:T(8,128)(2,1)S(1)}, u32[]{:S(2)}, u32[]{:S(2)}) collective-permute-start(bf16[128,768]{1,0:T(8,128)(2,1)S(1)} %copy-done.6), channel_id=1, source_target_pairs={{0,16},{4,20},{8,24},{12,28},{16,0},{20,4},{24,8},{28,12},{1,17},{... | collective-permute-start | bytes 589832 | tf_op jit(solution)/shard_map/ppermute | solution.py:319
  19.9 9.5 %collective-permute-start.5 = (bf16[128,768]{1,0:T(8,128)(2,1)S(1)}, bf16[128,768]{1,0:T(8,128)(2,1)S(1)}, u32[]{:S(2)}, u32[]{:S(2)}) collective-permute-start(bf16[128,768]{1,0:T(8,128)(2,1)S(1)} %collective-permute-done._.refs_2_), channel_id=1, source_target_pairs={{0,16},{4,20},{8,24},{12,28},{16,0},{20,4},{24,8},{28,12},{1,17},{... | collective-permute-start | bytes 589832 | tf_op jit(solution)/shard_map/ppermute | solution.py:319
  20.1 9.6 %collective-permute-start.6 = (bf16[128,768]{1,0:T(8,128)(2,1)S(1)}, bf16[128,768]{1,0:T(8,128)(2,1)S(1)}, u32[]{:S(2)}, u32[]{:S(2)}) collective-permute-start(bf16[128,768]{1,0:T(8,128)(2,1)S(1)} %collective-permute-done.1.__.refs_5_), channel_id=1, source_target_pairs={{0,8},{4,12},{8,0},{12,4},{16,24},{20,28},{24,16},{28,20},{1,9},{5... | collective-permute-start | bytes 589832 | tf_op jit(solution)/shard_map/ppermute | solution.py:319
  35.4 22.7 %collective-permute-start.7 = (bf16[384,1024]{1,0:T(8,128)(2,1)S(1)}, bf16[384,1024]{1,0:T(8,128)(2,1)S(1)}, u32[]{:S(2)}, u32[]{:S(2)}) collective-permute-start(bf16[384,1024]{1,0:T(8,128)(2,1)S(1)} %get-tuple-element.24.own_ref), channel_id=1, source_target_pairs={{0,4},{4,0},{8,12},{12,8},{16,20},{20,16},{24,28},{28,24},{1,5},{5... | collective-permute-start | bytes 2359304 | tf_op jit(solution)/shard_map/ppermute | solution.py:319
  35.6 9.9 %collective-permute-start.9 = (bf16[2,2,288,128]{3,2,1,0:T(8,128)(2,1)S(1)}, bf16[2,2,288,128]{3,2,1,0:T(8,128)(2,1)S(1)}, u32[]{:S(2)}, u32[]{:S(2)}) collective-permute-start(bf16[2,2,288,128]{3,2,1,0:T(8,128)(2,1)S(1)} %get-tuple-element.28), channel_id=1, source_target_pairs={{0,8},{4,12},{8,0},{12,4},{16,24},{20,28},{24,16},{28,20},{1,9},{5... | collective-permute-start | bytes 884744 | tf_op jit(solution)/shard_map/ppermute | solution.py:319
  37.2 15.4 %collective-permute-start.10 = (bf16[2,2,288,128]{3,2,1,0:T(8,128)(2,1)S(1)}, bf16[2,2,288,128]{3,2,1,0:T(8,128)(2,1)S(1)}, u32[]{:S(2)}, u32[]{:S(2)}) collective-permute-start(bf16[2,2,288,128]{3,2,1,0:T(8,128)(2,1)S(1)} %get-tuple-element.29), channel_id=1, source_target_pairs={{0,16},{4,20},{8,24},{12,28},{16,0},{20,4},{24,8},{28,12},{1,17},{... | collective-permute-start | bytes 884744 | tf_op jit(solution)/shard_map/ppermute | solution.py:319
  38.4 1.3 %collective-permute-start.12 = (bf16[128,512]{1,0:T(8,128)(2,1)S(1)}, bf16[128,512]{1,0:T(8,128)(2,1)S(1)}, u32[]{:S(2)}, u32[]{:S(2)}) collective-permute-start(bf16[128,512]{1,0:T(8,128)(2,1)S(1)} %get-tuple-element.33), channel_id=1, source_target_pairs={{0,4},{4,0},{8,12},{12,8},{16,20},{20,16},{24,28},{28,24},{1,5},{5... | collective-permute-start | bytes 393224 | tf_op jit(solution)/shard_map/ppermute | solution.py:319
  38.4 19.7 %collective-permute-start.11 = (bf16[2,2,288,128]{3,2,1,0:T(8,128)(2,1)S(1)}, bf16[2,2,288,128]{3,2,1,0:T(8,128)(2,1)S(1)}, u32[]{:S(2)}, u32[]{:S(2)}) collective-permute-start(bf16[2,2,288,128]{3,2,1,0:T(8,128)(2,1)S(1)} %get-tuple-element.30), channel_id=1, source_target_pairs={{0,24},{4,28},{8,16},{12,20},{16,8},{20,12},{24,0},{28,4},{1,25},{... | collective-permute-start | bytes 884744 | tf_op jit(solution)/shard_map/ppermute | solution.py:319
  39.7 1.3 %copy-start.2 = (bf16[2304,256]{1,0:T(8,128)(2,1)S(1)}, bf16[2304,256]{1,0:T(8,128)(2,1)}, u32[]{:S(2)}) copy-start(bf16[2304,256]{1,0:T(8,128)(2,1)} %wv_ref.3) | copy-start | bytes 3538948
  41.0 11.6 %copy-start.3 = (bf16[2304,256]{1,0:T(8,128)(2,1)S(1)}, bf16[2304,256]{1,0:T(8,128)(2,1)}, u32[]{:S(2)}) copy-start(bf16[2304,256]{1,0:T(8,128)(2,1)} %wv_ref.3) | copy-start | bytes 3538948
  41.5 13.9 %collective-permute-start.14 = (bf16[576,128]{1,0:T(8,128)(2,1)S(1)}, bf16[576,128]{1,0:T(8,128)(2,1)S(1)}, u32[]{:S(2)}, u32[]{:S(2)}) collective-permute-start(bf16[576,128]{1,0:T(8,128)(2,1)S(1)} %shard_map.118), channel_id=1, source_target_pairs={{0,1},{1,0},{2,3},{3,2},{4,5},{5,4},{6,7},{7,6},{8,9},{9,8},{10,11... | collective-permute-start | bytes 442376 | tf_op jit(solution)/shard_map/ppermute | solution.py:319
  53.7 6.4 %collective-permute-start.13 = (bf16[576,128]{1,0:T(8,128)(2,1)S(1)}, bf16[576,128]{1,0:T(8,128)(2,1)S(1)}, u32[]{:S(2)}, u32[]{:S(2)}) collective-permute-start(bf16[576,128]{1,0:T(8,128)(2,1)S(1)} %get-tuple-element.35), channel_id=1, source_target_pairs={{0,1},{1,0},{2,3},{3,2},{4,5},{5,4},{6,7},{7,6},{8,9},{9,8},{10,11... | collective-permute-start | bytes 442376 | tf_op jit(solution)/shard_map/ppermute | solution.py:319
  55.4 7.7 %collective-permute-start.15 = (bf16[576,128]{1,0:T(8,128)(2,1)S(1)}, bf16[576,128]{1,0:T(8,128)(2,1)S(1)}, u32[]{:S(2)}, u32[]{:S(2)}) collective-permute-start(bf16[576,128]{1,0:T(8,128)(2,1)S(1)} %shard_map.119), channel_id=1, source_target_pairs={{0,2},{1,3},{2,0},{3,1},{4,6},{5,7},{6,4},{7,5},{8,10},{9,11},{10,... | collective-permute-start | bytes 442376 | tf_op jit(solution)/shard_map/ppermute | solution.py:319

commit v14 on v13

--- a/solution.py
+++ b/solution.py
@@ -97,11 +97,10 @@
         copy.wait()
 
 
-def turn_kernel(
-    normed_hbm, cot_hbm, block_hbm, _, __, keep_ref, give_ref, own_ref, normed_ref, cot_ref, turned_ref, sem
-):
+def turn_kernel(normed_hbm, cot_hbm, block_hbm, _, __, *refs):
+    *column_refs, own_ref, normed_ref, cot_ref, turned_ref, sem = refs
     me = lax.axis_index("seq")
-    cut = keep_ref.shape[2]
+    cut = column_refs[0].shape[2]
     copies = []
     for which, (source, target) in enumerate(
         ((normed_hbm, normed_ref), (cot_hbm, cot_ref), (block_hbm, own_ref))
@@ -111,16 +110,16 @@
     for which, ref in enumerate((normed_ref, cot_ref)):
         copies[which].wait()
         turned_ref[which] = ref[...].astype(jnp.float32).T.astype(jnp.bfloat16)
-        for chip in range(keep_ref.shape[0]):
-            keep_ref[chip, which] = turned_ref[which, at(me ^ (2 * chip), cut)]
-            give_ref[chip, which] = turned_ref[which, at(me ^ (2 * chip + 1), cut)]
+        for chip, target in enumerate(column_refs):
+            for far in range(2):
+                target[far, which] = turned_ref[which, at(me ^ (2 * chip + far), cut)]
     copies[2].wait()
 
 
-def join_kernel(keep_ref, got_ref, *joined_refs):
-    for chip, ref in enumerate(joined_refs):
-        ref[0] = keep_ref[chip]
-        ref[1] = got_ref[chip]
+def pass_on_kernel(_, *refs):
+    *column_refs, give_ref = refs
+    for chip, ref in enumerate(column_refs):
+        give_ref[chip] = ref[1]
 
 
 def attention_kernel(blocks, *refs):
@@ -276,9 +275,10 @@
     done_ref[...] = jnp.zeros_like(done_ref)
     me = lax.axis_index("seq")
     core = me % 2
+    *column_refs, got_ref = column_refs
     for chip, ref in enumerate(column_refs):
-        for far in range(2):
-            joined_ref[:, :, at(me ^ (2 * chip + far), ref.shape[3])] = ref[far]
+        joined_ref[:, :, at(me ^ (2 * chip), ref.shape[3])] = ref[0]
+        joined_ref[:, :, at(me ^ (2 * chip + 1), ref.shape[3])] = got_ref[chip]
     kv_cols = wvalue_ref.shape[1] // 2
     q_cols = woutput_ref.shape[1] // 2
     for half, ref in ((core, own_ref), (1 - core, far_ref)):
@@ -366,13 +366,9 @@
             held[apart] = swapped(held[apart ^ through], "seq", through)
     held[1] = swapped(other, "seq", 1)
     cut = model // blocks
-    keep, give, held[0] = kernel_call(
+    *columns, held[0] = kernel_call(
         turn_kernel,
-        (
-            shape((blocks // 2, 2, cut, rows), bf16),
-            shape((blocks // 2, 2, cut, rows), bf16),
-            shape(same.shape, bf16),
-        ),
+        (shape((2, 2, cut, rows), bf16),) * (blocks // 2) + (shape(same.shape, bf16),),
         (normed_input, out_cotangent, same, held[2], held[blocks // 2 + 1]),
         scratch=(
             pltpu.VMEM(normed_input.shape, bf16),
@@ -382,14 +378,6 @@
         ),
         moved=8 * rows * model,
         room=8,
-    )
-    columns = kernel_call(
-        join_kernel,
-        (shape((2, 2, cut, rows), bf16),) * (blocks // 2),
-        (keep, swapped(give, "seq", 1)),
-        in_vmem=range(2),
-        moved=8 * rows * model,
-        room=4,
     )
     columns = [columns[0]] + [
         swapped(columns[chip], "seq", 2 * chip) for chip in range(1, blocks // 2)
@@ -416,15 +404,14 @@
             pltpu.VMEM((HEAD_SIZE, wide), f32),
             pltpu.VMEM((2 * rows, HEAD_SIZE), f32),
         ),
-        moved=2 * tokens * packed_cols,
     )
     dx_got = swapped(dx_far, "seq", 1)
     terms = {}
-    for chosen, waited in (((3,), []), ((2, 1, 0), [columns[1], columns[blocks // 4]])):
+    for chosen in ((3,), (2, 1, 0)):
         made = kernel_call(
             functools.partial(input_terms_kernel, chosen),
             tuple(shape((model // groups, rows), f32 if not apart else bf16) for apart in chosen),
-            (dx_own, dx_got, query_weight, key_matrix, value_matrix, *waited),
+            (dx_own, dx_got, query_weight, key_matrix, value_matrix),
             in_vmem=range(5),
             scratch=(pltpu.VMEM((rows, 2 * (q_cols + 2 * kv_cols)), bf16),),
             flops=2 * len(chosen) * rows * (model // groups) * 2 * (q_cols + 2 * kv_cols),
@@ -440,6 +427,14 @@
         moved=6 * rows * (model // groups),
         room=4,
     )
+    (give,) = kernel_call(
+        pass_on_kernel,
+        (shape((blocks // 2, 2, cut, rows), bf16),),
+        (pair_sum, *columns),
+        in_vmem=range(1, 1 + blocks // 2),
+        moved=8 * cut * rows * blocks // 2,
+        room=4,
+    )
     arrived = [swapped(terms[1], "head", 1), swapped(pair_sum, "head", 2)]
     grad_wvalue, grad_woutput, weights_done = kernel_call(
         weight_grad_kernel,
@@ -448,8 +443,8 @@
             shape((model // blocks, 2 * q_cols), f32),
             shape((8, HEAD_SIZE), f32),
         ),
-        (grad_parts, swapped(grad_parts, "seq", 1), *columns),
-        in_vmem=range(2 + blocks // 2),
+        (grad_parts, swapped(grad_parts, "seq", 1), *columns, swapped(give, "seq", 1)),
+        in_vmem=range(3 + blocks // 2),
         scratch=(pltpu.VMEM((2, model // blocks, tokens), bf16),),
         room=8,
         flops=4 * tokens * (model // blocks) * (q_cols + kv_cols),

time: 64.1 us -> 52.6 us (0.82)
  waiting for transfers between devices: 26.3 us -> 12.9 us
  local copies, waits for them, and re-layouts: 3.28 us -> 4.54 us
  starting transfers between devices: 18.4 us -> 19.2 us
    ppermute x16, waiting for transfers between devices: 26.3 us -> 12.9 us  [swapped(): lax.ppermute(value, axis, [(place, place ^ apart) for place in range(coun...]
    unnamed x14 -> x12, local copies, waits for them, and re-layouts: 3.28 us -> 4.54 us
    ppermute x16, starting transfers between devices: 18.4 us -> 19.2 us  [swapped(): lax.ppermute(value, axis, [(place, place ^ apart) for place in range(coun...]
  transfers between devices with their start and end apart: 16 -> 16, of which waited for: 10 -> 5; matrix products, arithmetic and copies ran while one was open for 0% -> 0% of each run, Pallas kernels for 17% -> 20%
where the time goes in v14:
time: 52.6 us; the launch traced here: 52.4 us
  starting transfers between devices  19.2 us (37%)
  Pallas kernels  15 us (29%)
  waiting for transfers between devices  12.9 us (25%)
  local copies, waits for them, and re-layouts  4.54 us (9%)
  between operations  0.76 us (1%)
    ppermute x16, starting transfers between devices, swapped(): lax.ppermute(value, axis, [(place, place ^ apart) for place in range(coun...  19.2 us
    pallas_call x9, Pallas kernels, kernel_call(): pl.pallas_call(body, out_shape=outs, in_specs=[vmem if place in in_vmem e...  15 us
    ppermute x16, waiting for transfers between devices, swapped(): lax.ppermute(value, axis, [(place, place ^ apart) for place in range(coun...  12.9 us
    unnamed x12, local copies, waits for them, and re-layouts  4.54 us
  transfers between devices with their start and end apart: 16, of which 5 were waited for; matrix products, arithmetic and copies ran while one was open for 0% of the time, Pallas kernels for 20%

profile of v14, /device:TPU:0, one launch (start us, length us, event | category | flops | bytes accessed | tf_op | source)
XLA Modules:
  0.0 52.4 jit_solution(10860893180577873235)
XLA Ops:
  0.6 3.8 %shard_map.112 = (bf16[128,768]{1,0:T(8,128)(2,1)}, bf16[128,768]{1,0:T(8,128)(2,1)}) custom-call(bf16[128,2304]{1,0:T(8,128)(2,1)} %cot_hbm.3, bf16[512,2304]{1,0:T(8,128)(2,1)} %weight_hbm.1, bf16[128,512]{1,0:T(8,128)(2,1)} %q_hbm.1, bf16[128,256]{1,0:T(8,128)(2,1)} %k_hbm.1, bf16[128,256]{1,0:T(8,128)(2,1)} %v_hbm.1), custom_call_target="tpu_custom_call" | custom-call | flops 301989888 | bytes 2949120 | tf_op jit(solution)/shard_map/pallas_call | solution.py:306
  4.4 3.0 %collective-permute-start = (bf16[128,768]{1,0:T(8,128)(2,1)}, bf16[128,768]{1,0:T(8,128)(2,1)S(1)}, u32[]{:S(2)}, u32[]{:S(2)}) collective-permute-start(bf16[128,768]{1,0:T(8,128)(2,1)} %get-tuple-element.19.block_hbm), channel_id=1, source_target_pairs={{0,8},{4,12},{8,0},{12,4},{16,24},{20,28},{24,16},{28,20},{1,9},{5... | collective-permute-start | bytes 589832 | tf_op jit(solution)/shard_map/ppermute | solution.py:319
  8.1 0.9 %collective-permute-start.4 = (bf16[128,768]{1,0:T(8,128)(2,1)}, bf16[128,768]{1,0:T(8,128)(2,1)S(1)}, u32[]{:S(2)}, u32[]{:S(2)}) collective-permute-start(bf16[128,768]{1,0:T(8,128)(2,1)} %get-tuple-element.19.block_hbm), channel_id=1, source_target_pairs={{0,16},{4,20},{8,24},{12,28},{16,0},{20,4},{24,8},{28,12},{1,17},{... | collective-permute-start | bytes 589832 | tf_op jit(solution)/shard_map/ppermute | solution.py:319
  9.6 3.4 %collective-permute-done._.refs_2_ = bf16[128,768]{1,0:T(8,128)(2,1)S(1)} collective-permute-done((bf16[128,768]{1,0:T(8,128)(2,1)}, bf16[128,768]{1,0:T(8,128)(2,1)S(1)}, u32[]{:S(2)}, u32[]{:S(2)}) %collective-permute-start) | collective-permute-done | bytes 196640 | tf_op jit(solution)/shard_map/ppermute | solution.py:319
  13.1 2.2 %collective-permute-start.5 = (bf16[128,768]{1,0:T(8,128)(2,1)S(1)}, bf16[128,768]{1,0:T(8,128)(2,1)S(1)}, u32[]{:S(2)}, u32[]{:S(2)}) collective-permute-start(bf16[128,768]{1,0:T(8,128)(2,1)S(1)} %collective-permute-done._.refs_2_), channel_id=1, source_target_pairs={{0,16},{4,20},{8,24},{12,28},{16,0},{20,4},{24,8},{28,12},{1,17},{... | collective-permute-start | bytes 589832 | tf_op jit(solution)/shard_map/ppermute | solution.py:319
  15.2 1.7 %collective-permute-start.6 = (bf16[128,768]{1,0:T(8,128)(2,1)S(1)}, bf16[128,768]{1,0:T(8,128)(2,1)S(1)}, u32[]{:S(2)}, u32[]{:S(2)}) collective-permute-start(bf16[128,768]{1,0:T(8,128)(2,1)S(1)} %collective-permute-done.1.__.refs_5_), channel_id=1, source_target_pairs={{0,8},{4,12},{8,0},{12,4},{16,24},{20,28},{24,16},{28,20},{1,9},{5... | collective-permute-start | bytes 589832 | tf_op jit(solution)/shard_map/ppermute | solution.py:319
  17.0 1.1 %copy-done.4 = bf16[128,2304]{1,0:T(8,128)(2,1)S(1)} copy-done((bf16[128,2304]{1,0:T(8,128)(2,1)S(1)}, bf16[128,2304]{1,0:T(8,128)(2,1)}, u32[]{:S(2)}) %copy-start.4) | copy-done | bytes 589848
  18.0 0.9 %copy-done.5 = bf16[128,768]{1,0:T(8,128)(2,1)S(1)} copy-done((bf16[128,768]{1,0:T(8,128)(2,1)S(1)}, bf16[128,768]{1,0:T(8,128)(2,1)}, u32[]{:S(2)}) %copy-start.5) | copy-done | bytes 196632
  19.0 1.1 %shard_map.113 = (bf16[2,2,288,128]{3,2,1,0:T(8,128)(2,1)S(1)}, bf16[2,2,288,128]{3,2,1,0:T(8,128)(2,1)S(1)}, bf16[2,2,288,128]{3,2,1,0:T(8,128)(2,1)S(1)}, bf16...) custom-call(bf16[128,2304]{1,0:T(8,128)(2,1)S(1)} %copy-done.4, bf16[128,2304]{1,0:T(8,128)(2,1)S(1)} %copy-done.3, ...), custom_call_target="tpu_custom_call" | custom-call | bytes 2359296 | tf_op jit(solution)/shard_map/pallas_call | solution.py:306
  20.4 1.1 %collective-permute-start.9 = (bf16[2,2,288,128]{3,2,1,0:T(8,128)(2,1)S(1)}, bf16[2,2,288,128]{3,2,1,0:T(8,128)(2,1)S(1)}, u32[]{:S(2)}, u32[]{:S(2)}) collective-permute-start(bf16[2,2,288,128]{3,2,1,0:T(8,128)(2,1)S(1)} %get-tuple-element.25), channel_id=1, source_target_pairs={{0,16},{4,20},{8,24},{12,28},{16,0},{20,4},{24,8},{28,12},{1,17},{... | collective-permute-start | bytes 884744 | tf_op jit(solution)/shard_map/ppermute | solution.py:319
  21.6 2.1 %collective-permute-start.10 = (bf16[2,2,288,128]{3,2,1,0:T(8,128)(2,1)S(1)}, bf16[2,2,288,128]{3,2,1,0:T(8,128)(2,1)S(1)}, u32[]{:S(2)}, u32[]{:S(2)}) collective-permute-start(bf16[2,2,288,128]{3,2,1,0:T(8,128)(2,1)S(1)} %get-tuple-element.26), channel_id=1, source_target_pairs={{0,24},{4,28},{8,16},{12,20},{16,8},{20,12},{24,0},{28,4},{1,25},{... | collective-permute-start | bytes 884744 | tf_op jit(solution)/shard_map/ppermute | solution.py:319
  23.6 5.7 %shard_map.114 = (bf16[128,512]{1,0:T(8,128)(2,1)S(1)}, bf16[128,512]{1,0:T(8,128)(2,1)S(1)}, bf16[384,1024]{1,0:T(8,128)(2,1)S(1)}) custom-call(bf16[128,768]{1,0:T(8,128)(2,1)S(1)} %get-tuple-element.21.refs_0_, bf16[128,768]{1,0:T(8,128)(2,1)S(1)} %collective-permute-done.2.refs_1_, bf16[128,768]{1,0:T(8,128)(2,1)S(1)} %collective-permute-done._.refs_2_, ...), custom_call_target="tpu_custom_call" | custom-call | tf_op jit(solution)/shard_map/pallas_call | solution.py:306
  29.9 0.8 %collective-permute-done.11.far_ref = bf16[128,512]{1,0:T(8,128)(2,1)S(1)} collective-permute-done((bf16[128,512]{1,0:T(8,128)(2,1)S(1)}, bf16[128,512]{1,0:T(8,128)(2,1)S(1)}, u32[]{:S(2)}, u32[]{:S(2)}) %collective-permute-start.11) | collective-permute-done | bytes 131104 | tf_op jit(solution)/shard_map/ppermute | solution.py:319
  30.7 1.3 %copy-done.1 = bf16[2304,256]{1,0:T(8,128)(2,1)S(1)} copy-done((bf16[2304,256]{1,0:T(8,128)(2,1)S(1)}, bf16[2304,256]{1,0:T(8,128)(2,1)}, u32[]{:S(2)}) %copy-start.1) | copy-done | bytes 1179672
  32.0 1.3 %copy-done.2 = bf16[2304,256]{1,0:T(8,128)(2,1)S(1)} copy-done((bf16[2304,256]{1,0:T(8,128)(2,1)S(1)}, bf16[2304,256]{1,0:T(8,128)(2,1)}, u32[]{:S(2)}) %copy-start.2) | copy-done | bytes 1179672
  33.8 1.6 %collective-permute-start.12 = (bf16[576,128]{1,0:T(8,128)(2,1)S(1)}, bf16[576,128]{1,0:T(8,128)(2,1)S(1)}, u32[]{:S(2)}, u32[]{:S(2)}) collective-permute-start(bf16[576,128]{1,0:T(8,128)(2,1)S(1)} %shard_map.116), channel_id=1, source_target_pairs={{0,1},{1,0},{2,3},{3,2},{4,5},{5,4},{6,7},{7,6},{8,9},{9,8},{10,11... | collective-permute-start | bytes 442376 | tf_op jit(solution)/shard_map/ppermute | solution.py:319
  35.5 1.1 %shard_map.115 = (bf16[576,128]{1,0:T(8,128)(2,1)S(1)}, bf16[576,128]{1,0:T(8,128)(2,1)S(1)}, f32[576,128]{1,0:T(8,128)S(1)}) custom-call(bf16[128,512]{1,0:T(8,128)(2,1)S(1)} %get-tuple-element.27.own_ref, bf16[128,512]{1,0:T(8,128)(2,1)S(1)} %collective-permute-done.11.far_ref, bf16[2304,512]{1,0:T(8,128)(2,1)S(1)} %copy-done, ...), custom_call_target="tpu_custom_call" | custom-call | flops 452984832 | bytes 3538944 | tf_op jit(solution)/shard_map/pallas_call | solution.py:306
  36.6 3.2 %collective-permute-done.12.arrived_ref = bf16[576,128]{1,0:T(8,128)(2,1)S(1)} collective-permute-done((bf16[576,128]{1,0:T(8,128)(2,1)S(1)}, bf16[576,128]{1,0:T(8,128)(2,1)S(1)}, u32[]{:S(2)}, u32[]{:S(2)}) %collective-permute-start.12) | collective-permute-done | bytes 147488 | tf_op jit(solution)/shard_map/ppermute | solution.py:319
  40.0 1.6 %collective-permute-start.14 = (bf16[576,128]{1,0:T(8,128)(2,1)S(1)}, bf16[576,128]{1,0:T(8,128)(2,1)S(1)}, u32[]{:S(2)}, u32[]{:S(2)}) collective-permute-start(bf16[576,128]{1,0:T(8,128)(2,1)S(1)} %get-tuple-element.32), channel_id=1, source_target_pairs={{0,1},{1,0},{2,3},{3,2},{4,5},{5,4},{6,7},{7,6},{8,9},{9,8},{10,11... | collective-permute-start | bytes 442376 | tf_op jit(solution)/shard_map/ppermute | solution.py:319
  41.6 2.6 %collective-permute-start.15 = (bf16[576,128]{1,0:T(8,128)(2,1)S(1)}, bf16[576,128]{1,0:T(8,128)(2,1)S(1)}, u32[]{:S(2)}, u32[]{:S(2)}) collective-permute-start(bf16[576,128]{1,0:T(8,128)(2,1)S(1)} %shard_map.117._), channel_id=1, source_target_pairs={{0,2},{1,3},{2,0},{3,1},{4,6},{5,7},{6,4},{7,5},{8,10},{9,11},{10,... | collective-permute-start | bytes 442376 | tf_op jit(solution)/shard_map/ppermute | solution.py:319
  44.2 2.0 %shard_map.119 = (f32[288,256]{1,0:T(8,128)}, f32[288,512]{1,0:T(8,128)}, f32[8,128]{1,0:T(8,128)S(1)}) custom-call(bf16[384,1024]{1,0:T(8,128)(2,1)S(1)} %get-tuple-element.22.own_ref, bf16[384,1024]{1,0:T(8,128)(2,1)S(1)} %collective-permute-done.7.far_ref, bf16[2,2,288,128]{3,2,1,0:T(8,128)(2,1)S(1)} %get-tuple-element.23.refs_0_, ...), custom_call_target="tpu_custom_call" | custom-call | flops 452984832 | bytes 2064384 | tf_op jit(solution)/shard_map/pallas_call | solution.py:306
  46.3 3.0 %collective-permute-done.14.refs_0_ = bf16[576,128]{1,0:T(8,128)(2,1)S(1)} collective-permute-done((bf16[576,128]{1,0:T(8,128)(2,1)S(1)}, bf16[576,128]{1,0:T(8,128)(2,1)S(1)}, u32[]{:S(2)}, u32[]{:S(2)}) %collective-permute-start.14) | collective-permute-done | bytes 147488 | tf_op jit(solution)/shard_map/ppermute | solution.py:319
  49.3 2.4 %collective-permute-done.15.refs_1_ = bf16[576,128]{1,0:T(8,128)(2,1)S(1)} collective-permute-done((bf16[576,128]{1,0:T(8,128)(2,1)S(1)}, bf16[576,128]{1,0:T(8,128)(2,1)S(1)}, u32[]{:S(2)}, u32[]{:S(2)}) %collective-permute-start.15) | collective-permute-done | bytes 147488 | tf_op jit(solution)/shard_map/ppermute | solution.py:319
  51.6 0.7 %shard_map.120 = bf16[576,128]{1,0:T(8,128)(2,1)} custom-call(f32[8,128]{1,0:T(8,128)S(1)} %get-tuple-element.30._, f32[576,128]{1,0:T(8,128)S(1)} %get-tuple-element.31.own_ref, bf16[576,128]{1,0:T(8,128)(2,1)S(1)} %collective-permute-done.14.refs_0_, bf16[576,128]{1,0:T(8,128)(2,1)S(1)} %collective-permute-done.15.refs_1_), custom_call_target="tpu_custom_call" | custom-call | bytes 1179648 | tf_op jit(solution)/shard_map/pallas_call | solution.py:306
  (29 shorter events, 3.0 us)
Async XLA Ops:
  0.6 16.3 %copy-start.3 = (bf16[128,2304]{1,0:T(8,128)(2,1)S(1)}, bf16[128,2304]{1,0:T(8,128)(2,1)}, u32[]{:S(2)}) copy-start(bf16[128,2304]{1,0:T(8,128)(2,1)} %cot_hbm.3) | copy-start | bytes 1769476
  4.4 26.3 %copy-start = (bf16[2304,512]{1,0:T(8,128)(2,1)S(1)}, bf16[2304,512]{1,0:T(8,128)(2,1)}, u32[]{:S(2)}) copy-start(bf16[2304,512]{1,0:T(8,128)(2,1)} %wq_ref.3) | copy-start | bytes 7077892
  4.4 8.6 %collective-permute-start = (bf16[128,768]{1,0:T(8,128)(2,1)}, bf16[128,768]{1,0:T(8,128)(2,1)S(1)}, u32[]{:S(2)}, u32[]{:S(2)}) collective-permute-start(bf16[128,768]{1,0:T(8,128)(2,1)} %get-tuple-element.19.block_hbm), channel_id=1, source_target_pairs={{0,8},{4,12},{8,0},{12,4},{16,24},{20,28},{24,16},{28,20},{1,9},{5... | collective-permute-start | bytes 589832 | tf_op jit(solution)/shard_map/ppermute | solution.py:319
  7.4 7.8 %collective-permute-start.1 = (bf16[128,768]{1,0:T(8,128)(2,1)}, bf16[128,768]{1,0:T(8,128)(2,1)S(1)}, u32[]{:S(2)}, u32[]{:S(2)}) collective-permute-start(bf16[128,768]{1,0:T(8,128)(2,1)} %get-tuple-element.20), channel_id=1, source_target_pairs={{0,20},{4,16},{8,28},{12,24},{16,4},{20,0},{24,12},{28,8},{1,21},{... | collective-permute-start | bytes 589832 | tf_op jit(solution)/shard_map/ppermute | solution.py:319
  8.1 11.9 %collective-permute-start.4 = (bf16[128,768]{1,0:T(8,128)(2,1)}, bf16[128,768]{1,0:T(8,128)(2,1)S(1)}, u32[]{:S(2)}, u32[]{:S(2)}) collective-permute-start(bf16[128,768]{1,0:T(8,128)(2,1)} %get-tuple-element.19.block_hbm), channel_id=1, source_target_pairs={{0,16},{4,20},{8,24},{12,28},{16,0},{20,4},{24,8},{28,12},{1,17},{... | collective-permute-start | bytes 589832 | tf_op jit(solution)/shard_map/ppermute | solution.py:319
  9.0 11.4 %collective-permute-start.3 = (bf16[128,768]{1,0:T(8,128)(2,1)}, bf16[128,768]{1,0:T(8,128)(2,1)S(1)}, u32[]{:S(2)}, u32[]{:S(2)}) collective-permute-start(bf16[128,768]{1,0:T(8,128)(2,1)} %get-tuple-element.20), channel_id=1, source_target_pairs={{0,12},{4,8},{8,4},{12,0},{16,28},{20,24},{24,20},{28,16},{1,13},{... | collective-permute-start | bytes 589832 | tf_op jit(solution)/shard_map/ppermute | solution.py:319
  9.2 12.3 %collective-permute-start.2 = (bf16[128,768]{1,0:T(8,128)(2,1)}, bf16[128,768]{1,0:T(8,128)(2,1)S(1)}, u32[]{:S(2)}, u32[]{:S(2)}) collective-permute-start(bf16[128,768]{1,0:T(8,128)(2,1)} %get-tuple-element.20), channel_id=1, source_target_pairs={{0,4},{4,0},{8,12},{12,8},{16,20},{20,16},{24,28},{28,24},{1,5},{5... | collective-permute-start | bytes 589832 | tf_op jit(solution)/shard_map/ppermute | solution.py:319
  13.1 10.6 %collective-permute-start.5 = (bf16[128,768]{1,0:T(8,128)(2,1)S(1)}, bf16[128,768]{1,0:T(8,128)(2,1)S(1)}, u32[]{:S(2)}, u32[]{:S(2)}) collective-permute-start(bf16[128,768]{1,0:T(8,128)(2,1)S(1)} %collective-permute-done._.refs_2_), channel_id=1, source_target_pairs={{0,16},{4,20},{8,24},{12,28},{16,0},{20,4},{24,8},{28,12},{1,17},{... | collective-permute-start | bytes 589832 | tf_op jit(solution)/shard_map/ppermute | solution.py:319
  15.2 8.4 %collective-permute-start.6 = (bf16[128,768]{1,0:T(8,128)(2,1)S(1)}, bf16[128,768]{1,0:T(8,128)(2,1)S(1)}, u32[]{:S(2)}, u32[]{:S(2)}) collective-permute-start(bf16[128,768]{1,0:T(8,128)(2,1)S(1)} %collective-permute-done.1.__.refs_5_), channel_id=1, source_target_pairs={{0,8},{4,12},{8,0},{12,4},{16,24},{20,28},{24,16},{28,20},{1,9},{5... | collective-permute-start | bytes 589832 | tf_op jit(solution)/shard_map/ppermute | solution.py:319
  17.0 1.1 %copy-start.4 = (bf16[128,2304]{1,0:T(8,128)(2,1)S(1)}, bf16[128,2304]{1,0:T(8,128)(2,1)}, u32[]{:S(2)}) copy-start(bf16[128,2304]{1,0:T(8,128)(2,1)} %normed_hbm.1) | copy-start | bytes 1769476
  18.0 0.9 %copy-start.5 = (bf16[128,768]{1,0:T(8,128)(2,1)S(1)}, bf16[128,768]{1,0:T(8,128)(2,1)}, u32[]{:S(2)}) copy-start(bf16[128,768]{1,0:T(8,128)(2,1)} %get-tuple-element.19.block_hbm) | copy-start | bytes 589828
  20.1 19.8 %collective-permute-start.8 = (bf16[2,2,288,128]{3,2,1,0:T(8,128)(2,1)S(1)}, bf16[2,2,288,128]{3,2,1,0:T(8,128)(2,1)S(1)}, u32[]{:S(2)}, u32[]{:S(2)}) collective-permute-start(bf16[2,2,288,128]{3,2,1,0:T(8,128)(2,1)S(1)} %get-tuple-element.24), channel_id=1, source_target_pairs={{0,8},{4,12},{8,0},{12,4},{16,24},{20,28},{24,16},{28,20},{1,9},{5... | collective-permute-start | bytes 884744 | tf_op jit(solution)/shard_map/ppermute | solution.py:319
  20.4 19.4 %collective-permute-start.9 = (bf16[2,2,288,128]{3,2,1,0:T(8,128)(2,1)S(1)}, bf16[2,2,288,128]{3,2,1,0:T(8,128)(2,1)S(1)}, u32[]{:S(2)}, u32[]{:S(2)}) collective-permute-start(bf16[2,2,288,128]{3,2,1,0:T(8,128)(2,1)S(1)} %get-tuple-element.25), channel_id=1, source_target_pairs={{0,16},{4,20},{8,24},{12,28},{16,0},{20,4},{24,8},{28,12},{1,17},{... | collective-permute-start | bytes 884744 | tf_op jit(solution)/shard_map/ppermute | solution.py:319
  21.6 18.3 %collective-permute-start.10 = (bf16[2,2,288,128]{3,2,1,0:T(8,128)(2,1)S(1)}, bf16[2,2,288,128]{3,2,1,0:T(8,128)(2,1)S(1)}, u32[]{:S(2)}, u32[]{:S(2)}) collective-permute-start(bf16[2,2,288,128]{3,2,1,0:T(8,128)(2,1)S(1)} %get-tuple-element.26), channel_id=1, source_target_pairs={{0,24},{4,28},{8,16},{12,20},{16,8},{20,12},{24,0},{28,4},{1,25},{... | collective-permute-start | bytes 884744 | tf_op jit(solution)/shard_map/ppermute | solution.py:319
  29.3 1.4 %collective-permute-start.11 = (bf16[128,512]{1,0:T(8,128)(2,1)S(1)}, bf16[128,512]{1,0:T(8,128)(2,1)S(1)}, u32[]{:S(2)}, u32[]{:S(2)}) collective-permute-start(bf16[128,512]{1,0:T(8,128)(2,1)S(1)} %get-tuple-element.28), channel_id=1, source_target_pairs={{0,4},{4,0},{8,12},{12,8},{16,20},{20,16},{24,28},{28,24},{1,5},{5... | collective-permute-start | bytes 393224 | tf_op jit(solution)/shard_map/ppermute | solution.py:319
  29.4 14.8 %collective-permute-start.7 = (bf16[384,1024]{1,0:T(8,128)(2,1)S(1)}, bf16[384,1024]{1,0:T(8,128)(2,1)S(1)}, u32[]{:S(2)}, u32[]{:S(2)}) collective-permute-start(bf16[384,1024]{1,0:T(8,128)(2,1)S(1)} %get-tuple-element.22.own_ref), channel_id=1, source_target_pairs={{0,4},{4,0},{8,12},{12,8},{16,20},{20,16},{24,28},{28,24},{1,5},{5... | collective-permute-start | bytes 2359304 | tf_op jit(solution)/shard_map/ppermute | solution.py:319
  30.7 1.3 %copy-start.1 = (bf16[2304,256]{1,0:T(8,128)(2,1)S(1)}, bf16[2304,256]{1,0:T(8,128)(2,1)}, u32[]{:S(2)}) copy-start(bf16[2304,256]{1,0:T(8,128)(2,1)} %wk_ref.3) | copy-start | bytes 3538948
  32.0 1.3 %copy-start.2 = (bf16[2304,256]{1,0:T(8,128)(2,1)S(1)}, bf16[2304,256]{1,0:T(8,128)(2,1)}, u32[]{:S(2)}) copy-start(bf16[2304,256]{1,0:T(8,128)(2,1)} %wv_ref.3) | copy-start | bytes 3538948
  33.8 6.0 %collective-permute-start.12 = (bf16[576,128]{1,0:T(8,128)(2,1)S(1)}, bf16[576,128]{1,0:T(8,128)(2,1)S(1)}, u32[]{:S(2)}, u32[]{:S(2)}) collective-permute-start(bf16[576,128]{1,0:T(8,128)(2,1)S(1)} %shard_map.116), channel_id=1, source_target_pairs={{0,1},{1,0},{2,3},{3,2},{4,5},{5,4},{6,7},{7,6},{8,9},{9,8},{10,11... | collective-permute-start | bytes 442376 | tf_op jit(solution)/shard_map/ppermute | solution.py:319
  39.9 4.3 %collective-permute-start.13 = (bf16[4,2,288,128]{3,2,1,0:T(8,128)(2,1)S(1)}, bf16[4,2,288,128]{3,2,1,0:T(8,128)(2,1)S(1)}, u32[]{:S(2)}, u32[]{:S(2)}) collective-permute-start(bf16[4,2,288,128]{3,2,1,0:T(8,128)(2,1)S(1)} %shard_map.118), channel_id=1, source_target_pairs={{0,4},{4,0},{8,12},{12,8},{16,20},{20,16},{24,28},{28,24},{1,5},{5... | collective-permute-start | bytes 1769480 | tf_op jit(solution)/shard_map/ppermute | solution.py:319
  40.0 9.3 %collective-permute-start.14 = (bf16[576,128]{1,0:T(8,128)(2,1)S(1)}, bf16[576,128]{1,0:T(8,128)(2,1)S(1)}, u32[]{:S(2)}, u32[]{:S(2)}) collective-permute-start(bf16[576,128]{1,0:T(8,128)(2,1)S(1)} %get-tuple-element.32), channel_id=1, source_target_pairs={{0,1},{1,0},{2,3},{3,2},{4,5},{5,4},{6,7},{7,6},{8,9},{9,8},{10,11... | collective-permute-start | bytes 442376 | tf_op jit(solution)/shard_map/ppermute | solution.py:319
  41.6 10.0 %collective-permute-start.15 = (bf16[576,128]{1,0:T(8,128)(2,1)S(1)}, bf16[576,128]{1,0:T(8,128)(2,1)S(1)}, u32[]{:S(2)}, u32[]{:S(2)}) collective-permute-start(bf16[576,128]{1,0:T(8,128)(2,1)S(1)} %shard_map.117._), channel_id=1, source_target_pairs={{0,2},{1,3},{2,0},{3,1},{4,6},{5,7},{6,4},{7,5},{8,10},{9,11},{10,... | collective-permute-start | bytes 442376 | tf_op jit(solution)/shard_map/ppermute | solution.py:319

commit v15 on v14

--- a/solution.py
+++ b/solution.py
@@ -128,9 +128,15 @@
 
 def attention_body(
     block_refs,
+    wq_hbm,
+    wk_hbm,
+    wv_hbm,
     dx_own_ref,
     dx_far_ref,
     parts_ref,
+    wq_ref,
+    wk_ref,
+    wv_ref,
     gathered_ref,
     score_even_ref,
     score_odd_ref,
@@ -142,7 +148,16 @@
     key_t_ref,
     dq_t_ref,
     dk_ref,
+    sem,
 ):
+    copies = [
+        pltpu.make_async_copy(source, target, sem.at[place])
+        for place, (source, target) in enumerate(
+            ((wq_hbm, wq_ref), (wk_hbm, wk_ref), (wv_hbm, wv_ref))
+        )
+    ]
+    for copy in copies:
+        copy.start()
     me = lax.axis_index("seq")
     core, chip = me % 2, me // 2
     rows = dx_own_ref.shape[0]
@@ -244,6 +259,8 @@
             )
         target[:, key_cols] = (logit_scale * dk_ref[at(half, rows)]).astype(jnp.bfloat16)
         target[:, value_cols] = parts_ref[heads * HEAD_SIZE :, at(2 * chip + half, rows)].T
+    for copy in copies:
+        copy.wait()
 
 
 def input_terms_kernel(apart_groups, own_ref, far_ref, wq_ref, wk_ref, wv_ref, *refs):
@@ -382,14 +399,16 @@
     columns = [columns[0]] + [
         swapped(columns[chip], "seq", 2 * chip) for chip in range(1, blocks // 2)
     ]
-    dx_own, dx_far, grad_parts = kernel_call(
+    weights = (query_weight, key_matrix, value_matrix)
+    dx_own, dx_far, grad_parts, *weights = kernel_call(
         functools.partial(attention_kernel, blocks),
         (
             shape((rows, q_cols + 2 * kv_cols), bf16),
             shape((rows, q_cols + 2 * kv_cols), bf16),
             shape((q_cols + kv_cols, tokens), bf16),
-        ),
-        [held[apart] for apart in range(blocks)],
+        )
+        + tuple(shape(weight.shape, bf16) for weight in weights),
+        [held[apart] for apart in range(blocks)] + list(weights),
         in_vmem=range(blocks),
         scratch=(
             pltpu.VMEM((tokens, packed_cols), bf16),
@@ -403,6 +422,7 @@
             pltpu.VMEM((HEAD_SIZE, tokens), bf16),
             pltpu.VMEM((HEAD_SIZE, wide), f32),
             pltpu.VMEM((2 * rows, HEAD_SIZE), f32),
+            pltpu.SemaphoreType.DMA((3,)),
         ),
     )
     dx_got = swapped(dx_far, "seq", 1)
@@ -411,7 +431,7 @@
         made = kernel_call(
             functools.partial(input_terms_kernel, chosen),
             tuple(shape((model // groups, rows), f32 if not apart else bf16) for apart in chosen),
-            (dx_own, dx_got, query_weight, key_matrix, value_matrix),
+            (dx_own, dx_got, *weights),
             in_vmem=range(5),
             scratch=(pltpu.VMEM((rows, 2 * (q_cols + 2 * kv_cols)), bf16),),
             flops=2 * len(chosen) * rows * (model // groups) * 2 * (q_cols + 2 * kv_cols),
@@ -435,7 +455,7 @@
         moved=8 * cut * rows * blocks // 2,
         room=4,
     )
-    arrived = [swapped(terms[1], "head", 1), swapped(pair_sum, "head", 2)]
+    arrived = [swapped(pair_sum, "head", 2), swapped(terms[1], "head", 1)]
     grad_wvalue, grad_woutput, weights_done = kernel_call(
         weight_grad_kernel,
         (

time: 52.6 us -> 53.7 us (1.021)
  Pallas kernels: 15 us -> 15.7 us
    pallas_call x9, Pallas kernels: 15 us -> 15.7 us  [kernel_call(): pl.pallas_call(body, out_shape=outs, in_specs=[vmem if place in in_vmem e...]
  transfers between devices with their start and end apart: 16 -> 16, of which waited for: 5 -> 5; matrix products, arithmetic and copies ran while one was open for 0% -> 0% of each run, Pallas kernels for 20% -> 21%
where the time goes in v15:
time: 53.7 us; the launch traced here: 53.4 us
  starting transfers between devices  19.2 us (36%)
  Pallas kernels  15.7 us (29%)
  waiting for transfers between devices  12.9 us (24%)
  local copies, waits for them, and re-layouts  4.93 us (9%)
  between operations  0.77 us (1%)
    ppermute x16, starting transfers between devices, swapped(): lax.ppermute(value, axis, [(place, place ^ apart) for place in range(coun...  19.2 us
    pallas_call x9, Pallas kernels, kernel_call(): pl.pallas_call(body, out_shape=outs, in_specs=[vmem if place in in_vmem e...  15.7 us
    ppermute x16, waiting for transfers between devices, swapped(): lax.ppermute(value, axis, [(place, place ^ apart) for place in range(coun...  12.9 us
    unnamed x12, local copies, waits for them, and re-layouts  4.93 us
  transfers between devices with their start and end apart: 16, of which 5 were waited for; matrix products, arithmetic and copies ran while one was open for 0% of the time, Pallas kernels for 21%

profile of v15, /device:TPU:0, one launch (start us, length us, event | category | flops | bytes accessed | tf_op | source)
XLA Modules:
  0.0 53.4 jit_solution(6779087754922814152)
XLA Ops:
  0.6 3.8 %shard_map.112 = (bf16[128,768]{1,0:T(8,128)(2,1)}, bf16[128,768]{1,0:T(8,128)(2,1)}) custom-call(bf16[128,2304]{1,0:T(8,128)(2,1)} %cot_hbm.3, bf16[512,2304]{1,0:T(8,128)(2,1)} %weight_hbm.1, bf16[128,512]{1,0:T(8,128)(2,1)} %q_hbm.1, bf16[128,256]{1,0:T(8,128)(2,1)} %k_hbm.1, bf16[128,256]{1,0:T(8,128)(2,1)} %v_hbm.1), custom_call_target="tpu_custom_call" | custom-call | flops 301989888 | bytes 2949120 | tf_op jit(solution)/shard_map/pallas_call | solution.py:323
  4.4 3.0 %collective-permute-start = (bf16[128,768]{1,0:T(8,128)(2,1)}, bf16[128,768]{1,0:T(8,128)(2,1)S(1)}, u32[]{:S(2)}, u32[]{:S(2)}) collective-permute-start(bf16[128,768]{1,0:T(8,128)(2,1)} %get-tuple-element.22.block_hbm), channel_id=1, source_target_pairs={{0,8},{4,12},{8,0},{12,4},{16,24},{20,28},{24,16},{28,20},{1,9},{5... | collective-permute-start | bytes 589832 | tf_op jit(solution)/shard_map/ppermute | solution.py:336
  8.1 0.9 %collective-permute-start.4 = (bf16[128,768]{1,0:T(8,128)(2,1)}, bf16[128,768]{1,0:T(8,128)(2,1)S(1)}, u32[]{:S(2)}, u32[]{:S(2)}) collective-permute-start(bf16[128,768]{1,0:T(8,128)(2,1)} %get-tuple-element.22.block_hbm), channel_id=1, source_target_pairs={{0,16},{4,20},{8,24},{12,28},{16,0},{20,4},{24,8},{28,12},{1,17},{... | collective-permute-start | bytes 589832 | tf_op jit(solution)/shard_map/ppermute | solution.py:336
  9.6 3.4 %collective-permute-done._.refs_2_ = bf16[128,768]{1,0:T(8,128)(2,1)S(1)} collective-permute-done((bf16[128,768]{1,0:T(8,128)(2,1)}, bf16[128,768]{1,0:T(8,128)(2,1)S(1)}, u32[]{:S(2)}, u32[]{:S(2)}) %collective-permute-start) | collective-permute-done | bytes 196640 | tf_op jit(solution)/shard_map/ppermute | solution.py:336
  13.1 2.2 %collective-permute-start.5 = (bf16[128,768]{1,0:T(8,128)(2,1)S(1)}, bf16[128,768]{1,0:T(8,128)(2,1)S(1)}, u32[]{:S(2)}, u32[]{:S(2)}) collective-permute-start(bf16[128,768]{1,0:T(8,128)(2,1)S(1)} %collective-permute-done._.refs_2_), channel_id=1, source_target_pairs={{0,16},{4,20},{8,24},{12,28},{16,0},{20,4},{24,8},{28,12},{1,17},{... | collective-permute-start | bytes 589832 | tf_op jit(solution)/shard_map/ppermute | solution.py:336
  15.2 1.7 %collective-permute-start.6 = (bf16[128,768]{1,0:T(8,128)(2,1)S(1)}, bf16[128,768]{1,0:T(8,128)(2,1)S(1)}, u32[]{:S(2)}, u32[]{:S(2)}) collective-permute-start(bf16[128,768]{1,0:T(8,128)(2,1)S(1)} %collective-permute-done.1.__.refs_5_), channel_id=1, source_target_pairs={{0,8},{4,12},{8,0},{12,4},{16,24},{20,28},{24,16},{28,20},{1,9},{5... | collective-permute-start | bytes 589832 | tf_op jit(solution)/shard_map/ppermute | solution.py:336
  17.0 1.1 %copy-done.4 = bf16[128,2304]{1,0:T(8,128)(2,1)S(1)} copy-done((bf16[128,2304]{1,0:T(8,128)(2,1)S(1)}, bf16[128,2304]{1,0:T(8,128)(2,1)}, u32[]{:S(2)}) %copy-start.4) | copy-done | bytes 589848
  18.0 0.9 %copy-done.5 = bf16[128,768]{1,0:T(8,128)(2,1)S(1)} copy-done((bf16[128,768]{1,0:T(8,128)(2,1)S(1)}, bf16[128,768]{1,0:T(8,128)(2,1)}, u32[]{:S(2)}) %copy-start.5) | copy-done | bytes 196632
  19.0 1.1 %shard_map.113 = (bf16[2,2,288,128]{3,2,1,0:T(8,128)(2,1)S(1)}, bf16[2,2,288,128]{3,2,1,0:T(8,128)(2,1)S(1)}, bf16[2,2,288,128]{3,2,1,0:T(8,128)(2,1)S(1)}, bf16...) custom-call(bf16[128,2304]{1,0:T(8,128)(2,1)S(1)} %copy-done.4, bf16[128,2304]{1,0:T(8,128)(2,1)S(1)} %copy-done.1, ...), custom_call_target="tpu_custom_call" | custom-call | bytes 2359296 | tf_op jit(solution)/shard_map/pallas_call | solution.py:323
  20.4 1.1 %collective-permute-start.9 = (bf16[2,2,288,128]{3,2,1,0:T(8,128)(2,1)S(1)}, bf16[2,2,288,128]{3,2,1,0:T(8,128)(2,1)S(1)}, u32[]{:S(2)}, u32[]{:S(2)}) collective-permute-start(bf16[2,2,288,128]{3,2,1,0:T(8,128)(2,1)S(1)} %get-tuple-element.28), channel_id=1, source_target_pairs={{0,16},{4,20},{8,24},{12,28},{16,0},{20,4},{24,8},{28,12},{1,17},{... | collective-permute-start | bytes 884744 | tf_op jit(solution)/shard_map/ppermute | solution.py:336
  21.6 2.1 %collective-permute-start.10 = (bf16[2,2,288,128]{3,2,1,0:T(8,128)(2,1)S(1)}, bf16[2,2,288,128]{3,2,1,0:T(8,128)(2,1)S(1)}, u32[]{:S(2)}, u32[]{:S(2)}) collective-permute-start(bf16[2,2,288,128]{3,2,1,0:T(8,128)(2,1)S(1)} %get-tuple-element.29), channel_id=1, source_target_pairs={{0,24},{4,28},{8,16},{12,20},{16,8},{20,12},{24,0},{28,4},{1,25},{... | collective-permute-start | bytes 884744 | tf_op jit(solution)/shard_map/ppermute | solution.py:336
  23.6 1.7 %copy-done = bf16[2304,512]{1,0:T(8,128)(2,1)S(1)} copy-done((bf16[2304,512]{1,0:T(8,128)(2,1)S(1)}, bf16[2304,512]{1,0:T(8,128)(2,1)}, u32[]{:S(2)}) %copy-start) | copy-done | bytes 2359320
  25.3 1.3 %copy-done.3 = bf16[2304,256]{1,0:T(8,128)(2,1)S(1)} copy-done((bf16[2304,256]{1,0:T(8,128)(2,1)S(1)}, bf16[2304,256]{1,0:T(8,128)(2,1)}, u32[]{:S(2)}) %copy-start.3) | copy-done | bytes 1179672
  26.6 6.4 %shard_map.114 = (bf16[128,512]{1,0:T(8,128)(2,1)S(1)}, bf16[128,512]{1,0:T(8,128)(2,1)S(1)}, bf16[384,1024]{1,0:T(8,128)(2,1)S(1)}, bf16[2304,512]{1,0:T(8,128)...) custom-call(bf16[128,768]{1,0:T(8,128)(2,1)S(1)} %get-tuple-element.24.refs_0_, ...), custom_call_target="tpu_custom_call" | custom-call | tf_op jit(solution)/shard_map/pallas_call | solution.py:323
  33.5 0.8 %collective-permute-done.11.far_ref = bf16[128,512]{1,0:T(8,128)(2,1)S(1)} collective-permute-done((bf16[128,512]{1,0:T(8,128)(2,1)S(1)}, bf16[128,512]{1,0:T(8,128)(2,1)S(1)}, u32[]{:S(2)}, u32[]{:S(2)}) %collective-permute-start.11) | collective-permute-done | bytes 131104 | tf_op jit(solution)/shard_map/ppermute | solution.py:336
  34.9 1.6 %collective-permute-start.12 = (bf16[576,128]{1,0:T(8,128)(2,1)S(1)}, bf16[576,128]{1,0:T(8,128)(2,1)S(1)}, u32[]{:S(2)}, u32[]{:S(2)}) collective-permute-start(bf16[576,128]{1,0:T(8,128)(2,1)S(1)} %shard_map.116), channel_id=1, source_target_pairs={{0,1},{1,0},{2,3},{3,2},{4,5},{5,4},{6,7},{7,6},{8,9},{9,8},{10,11... | collective-permute-start | bytes 442376 | tf_op jit(solution)/shard_map/ppermute | solution.py:336
  36.5 1.1 %shard_map.115 = (bf16[576,128]{1,0:T(8,128)(2,1)S(1)}, bf16[576,128]{1,0:T(8,128)(2,1)S(1)}, f32[576,128]{1,0:T(8,128)S(1)}) custom-call(bf16[128,512]{1,0:T(8,128)(2,1)S(1)} %get-tuple-element.30.own_ref, bf16[128,512]{1,0:T(8,128)(2,1)S(1)} %collective-permute-done.11.far_ref, bf16[2304,512]{1,0:T(8,128)(2,1)S(1)} %get-tuple-element.32.wq_ref, ...), custom_call_target="tpu_custom_call" | custom-call | flops 452984832 | bytes 3538944 | tf_op jit(solution)/shard_map/pallas_call | solution.py:323
  37.7 3.2 %collective-permute-done.12.arrived_ref = bf16[576,128]{1,0:T(8,128)(2,1)S(1)} collective-permute-done((bf16[576,128]{1,0:T(8,128)(2,1)S(1)}, bf16[576,128]{1,0:T(8,128)(2,1)S(1)}, u32[]{:S(2)}, u32[]{:S(2)}) %collective-permute-start.12) | collective-permute-done | bytes 147488 | tf_op jit(solution)/shard_map/ppermute | solution.py:336
  41.1 1.6 %collective-permute-start.15 = (bf16[576,128]{1,0:T(8,128)(2,1)S(1)}, bf16[576,128]{1,0:T(8,128)(2,1)S(1)}, u32[]{:S(2)}, u32[]{:S(2)}) collective-permute-start(bf16[576,128]{1,0:T(8,128)(2,1)S(1)} %get-tuple-element.38), channel_id=1, source_target_pairs={{0,1},{1,0},{2,3},{3,2},{4,5},{5,4},{6,7},{7,6},{8,9},{9,8},{10,11... | collective-permute-start | bytes 442376 | tf_op jit(solution)/shard_map/ppermute | solution.py:336
  42.7 2.6 %collective-permute-start.14 = (bf16[576,128]{1,0:T(8,128)(2,1)S(1)}, bf16[576,128]{1,0:T(8,128)(2,1)S(1)}, u32[]{:S(2)}, u32[]{:S(2)}) collective-permute-start(bf16[576,128]{1,0:T(8,128)(2,1)S(1)} %shard_map.117._), channel_id=1, source_target_pairs={{0,2},{1,3},{2,0},{3,1},{4,6},{5,7},{6,4},{7,5},{8,10},{9,11},{10,... | collective-permute-start | bytes 442376 | tf_op jit(solution)/shard_map/ppermute | solution.py:336
  45.3 2.0 %shard_map.119 = (f32[288,256]{1,0:T(8,128)}, f32[288,512]{1,0:T(8,128)}, f32[8,128]{1,0:T(8,128)S(1)}) custom-call(bf16[384,1024]{1,0:T(8,128)(2,1)S(1)} %get-tuple-element.25.own_ref, bf16[384,1024]{1,0:T(8,128)(2,1)S(1)} %collective-permute-done.7.far_ref, bf16[2,2,288,128]{3,2,1,0:T(8,128)(2,1)S(1)} %get-tuple-element.26.refs_0_, ...), custom_call_target="tpu_custom_call" | custom-call | flops 452984832 | bytes 2064384 | tf_op jit(solution)/shard_map/pallas_call | solution.py:323
  47.3 3.0 %collective-permute-done.15.refs_1_ = bf16[576,128]{1,0:T(8,128)(2,1)S(1)} collective-permute-done((bf16[576,128]{1,0:T(8,128)(2,1)S(1)}, bf16[576,128]{1,0:T(8,128)(2,1)S(1)}, u32[]{:S(2)}, u32[]{:S(2)}) %collective-permute-start.15) | collective-permute-done | bytes 147488 | tf_op jit(solution)/shard_map/ppermute | solution.py:336
  50.4 2.4 %collective-permute-done.14.refs_0_ = bf16[576,128]{1,0:T(8,128)(2,1)S(1)} collective-permute-done((bf16[576,128]{1,0:T(8,128)(2,1)S(1)}, bf16[576,128]{1,0:T(8,128)(2,1)S(1)}, u32[]{:S(2)}, u32[]{:S(2)}) %collective-permute-start.14) | collective-permute-done | bytes 147488 | tf_op jit(solution)/shard_map/ppermute | solution.py:336
  52.7 0.7 %shard_map.120 = bf16[576,128]{1,0:T(8,128)(2,1)} custom-call(f32[8,128]{1,0:T(8,128)S(1)} %get-tuple-element.36._, f32[576,128]{1,0:T(8,128)S(1)} %get-tuple-element.37.own_ref, bf16[576,128]{1,0:T(8,128)(2,1)S(1)} %collective-permute-done.14.refs_0_, bf16[576,128]{1,0:T(8,128)(2,1)S(1)} %collective-permute-done.15.refs_1_), custom_call_target="tpu_custom_call" | custom-call | bytes 1179648 | tf_op jit(solution)/shard_map/pallas_call | solution.py:323
  (29 shorter events, 3.0 us)
Async XLA Ops:
  0.6 16.3 %copy-start.1 = (bf16[128,2304]{1,0:T(8,128)(2,1)S(1)}, bf16[128,2304]{1,0:T(8,128)(2,1)}, u32[]{:S(2)}) copy-start(bf16[128,2304]{1,0:T(8,128)(2,1)} %cot_hbm.3) | copy-start | bytes 1769476
  4.4 19.2 %copy-start.2 = (bf16[2304,256]{1,0:T(8,128)(2,1)S(1)}, bf16[2304,256]{1,0:T(8,128)(2,1)}, u32[]{:S(2)}) copy-start(bf16[2304,256]{1,0:T(8,128)(2,1)} %refs_9_.1) | copy-start | bytes 3538948
  4.4 8.6 %collective-permute-start = (bf16[128,768]{1,0:T(8,128)(2,1)}, bf16[128,768]{1,0:T(8,128)(2,1)S(1)}, u32[]{:S(2)}, u32[]{:S(2)}) collective-permute-start(bf16[128,768]{1,0:T(8,128)(2,1)} %get-tuple-element.22.block_hbm), channel_id=1, source_target_pairs={{0,8},{4,12},{8,0},{12,4},{16,24},{20,28},{24,16},{28,20},{1,9},{5... | collective-permute-start | bytes 589832 | tf_op jit(solution)/shard_map/ppermute | solution.py:336
  7.4 7.8 %collective-permute-start.1 = (bf16[128,768]{1,0:T(8,128)(2,1)}, bf16[128,768]{1,0:T(8,128)(2,1)S(1)}, u32[]{:S(2)}, u32[]{:S(2)}) collective-permute-start(bf16[128,768]{1,0:T(8,128)(2,1)} %get-tuple-element.23), channel_id=1, source_target_pairs={{0,20},{4,16},{8,28},{12,24},{16,4},{20,0},{24,12},{28,8},{1,21},{... | collective-permute-start | bytes 589832 | tf_op jit(solution)/shard_map/ppermute | solution.py:336
  8.1 11.9 %collective-permute-start.4 = (bf16[128,768]{1,0:T(8,128)(2,1)}, bf16[128,768]{1,0:T(8,128)(2,1)S(1)}, u32[]{:S(2)}, u32[]{:S(2)}) collective-permute-start(bf16[128,768]{1,0:T(8,128)(2,1)} %get-tuple-element.22.block_hbm), channel_id=1, source_target_pairs={{0,16},{4,20},{8,24},{12,28},{16,0},{20,4},{24,8},{28,12},{1,17},{... | collective-permute-start | bytes 589832 | tf_op jit(solution)/shard_map/ppermute | solution.py:336
  9.0 11.4 %collective-permute-start.3 = (bf16[128,768]{1,0:T(8,128)(2,1)}, bf16[128,768]{1,0:T(8,128)(2,1)S(1)}, u32[]{:S(2)}, u32[]{:S(2)}) collective-permute-start(bf16[128,768]{1,0:T(8,128)(2,1)} %get-tuple-element.23), channel_id=1, source_target_pairs={{0,12},{4,8},{8,4},{12,0},{16,28},{20,24},{24,20},{28,16},{1,13},{... | collective-permute-start | bytes 589832 | tf_op jit(solution)/shard_map/ppermute | solution.py:336
  9.2 12.3 %collective-permute-start.2 = (bf16[128,768]{1,0:T(8,128)(2,1)}, bf16[128,768]{1,0:T(8,128)(2,1)S(1)}, u32[]{:S(2)}, u32[]{:S(2)}) collective-permute-start(bf16[128,768]{1,0:T(8,128)(2,1)} %get-tuple-element.23), channel_id=1, source_target_pairs={{0,4},{4,0},{8,12},{12,8},{16,20},{20,16},{24,28},{28,24},{1,5},{5... | collective-permute-start | bytes 589832 | tf_op jit(solution)/shard_map/ppermute | solution.py:336
  13.1 10.6 %collective-permute-start.5 = (bf16[128,768]{1,0:T(8,128)(2,1)S(1)}, bf16[128,768]{1,0:T(8,128)(2,1)S(1)}, u32[]{:S(2)}, u32[]{:S(2)}) collective-permute-start(bf16[128,768]{1,0:T(8,128)(2,1)S(1)} %collective-permute-done._.refs_2_), channel_id=1, source_target_pairs={{0,16},{4,20},{8,24},{12,28},{16,0},{20,4},{24,8},{28,12},{1,17},{... | collective-permute-start | bytes 589832 | tf_op jit(solution)/shard_map/ppermute | solution.py:336
  15.2 8.4 %collective-permute-start.6 = (bf16[128,768]{1,0:T(8,128)(2,1)S(1)}, bf16[128,768]{1,0:T(8,128)(2,1)S(1)}, u32[]{:S(2)}, u32[]{:S(2)}) collective-permute-start(bf16[128,768]{1,0:T(8,128)(2,1)S(1)} %collective-permute-done.1.__.refs_5_), channel_id=1, source_target_pairs={{0,8},{4,12},{8,0},{12,4},{16,24},{20,28},{24,16},{28,20},{1,9},{5... | collective-permute-start | bytes 589832 | tf_op jit(solution)/shard_map/ppermute | solution.py:336
  17.0 1.1 %copy-start.4 = (bf16[128,2304]{1,0:T(8,128)(2,1)S(1)}, bf16[128,2304]{1,0:T(8,128)(2,1)}, u32[]{:S(2)}) copy-start(bf16[128,2304]{1,0:T(8,128)(2,1)} %normed_hbm.1) | copy-start | bytes 1769476
  18.0 0.9 %copy-start.5 = (bf16[128,768]{1,0:T(8,128)(2,1)S(1)}, bf16[128,768]{1,0:T(8,128)(2,1)}, u32[]{:S(2)}) copy-start(bf16[128,768]{1,0:T(8,128)(2,1)} %get-tuple-element.22.block_hbm) | copy-start | bytes 589828
  20.1 20.8 %collective-permute-start.8 = (bf16[2,2,288,128]{3,2,1,0:T(8,128)(2,1)S(1)}, bf16[2,2,288,128]{3,2,1,0:T(8,128)(2,1)S(1)}, u32[]{:S(2)}, u32[]{:S(2)}) collective-permute-start(bf16[2,2,288,128]{3,2,1,0:T(8,128)(2,1)S(1)} %get-tuple-element.27), channel_id=1, source_target_pairs={{0,8},{4,12},{8,0},{12,4},{16,24},{20,28},{24,16},{28,20},{1,9},{5... | collective-permute-start | bytes 884744 | tf_op jit(solution)/shard_map/ppermute | solution.py:336
  20.4 20.5 %collective-permute-start.9 = (bf16[2,2,288,128]{3,2,1,0:T(8,128)(2,1)S(1)}, bf16[2,2,288,128]{3,2,1,0:T(8,128)(2,1)S(1)}, u32[]{:S(2)}, u32[]{:S(2)}) collective-permute-start(bf16[2,2,288,128]{3,2,1,0:T(8,128)(2,1)S(1)} %get-tuple-element.28), channel_id=1, source_target_pairs={{0,16},{4,20},{8,24},{12,28},{16,0},{20,4},{24,8},{28,12},{1,17},{... | collective-permute-start | bytes 884744 | tf_op jit(solution)/shard_map/ppermute | solution.py:336
  21.6 19.4 %collective-permute-start.10 = (bf16[2,2,288,128]{3,2,1,0:T(8,128)(2,1)S(1)}, bf16[2,2,288,128]{3,2,1,0:T(8,128)(2,1)S(1)}, u32[]{:S(2)}, u32[]{:S(2)}) collective-permute-start(bf16[2,2,288,128]{3,2,1,0:T(8,128)(2,1)S(1)} %get-tuple-element.29), channel_id=1, source_target_pairs={{0,24},{4,28},{8,16},{12,20},{16,8},{20,12},{24,0},{28,4},{1,25},{... | collective-permute-start | bytes 884744 | tf_op jit(solution)/shard_map/ppermute | solution.py:336
  23.6 1.7 %copy-start = (bf16[2304,512]{1,0:T(8,128)(2,1)S(1)}, bf16[2304,512]{1,0:T(8,128)(2,1)}, u32[]{:S(2)}) copy-start(bf16[2304,512]{1,0:T(8,128)(2,1)} %refs_8_.1) | copy-start | bytes 7077892
  25.3 1.3 %copy-start.3 = (bf16[2304,256]{1,0:T(8,128)(2,1)S(1)}, bf16[2304,256]{1,0:T(8,128)(2,1)}, u32[]{:S(2)}) copy-start(bf16[2304,256]{1,0:T(8,128)(2,1)} %refs_10_.1) | copy-start | bytes 3538948
  32.9 1.4 %collective-permute-start.11 = (bf16[128,512]{1,0:T(8,128)(2,1)S(1)}, bf16[128,512]{1,0:T(8,128)(2,1)S(1)}, u32[]{:S(2)}, u32[]{:S(2)}) collective-permute-start(bf16[128,512]{1,0:T(8,128)(2,1)S(1)} %get-tuple-element.31), channel_id=1, source_target_pairs={{0,4},{4,0},{8,12},{12,8},{16,20},{20,16},{24,28},{28,24},{1,5},{5... | collective-permute-start | bytes 393224 | tf_op jit(solution)/shard_map/ppermute | solution.py:336
  33.0 12.3 %collective-permute-start.7 = (bf16[384,1024]{1,0:T(8,128)(2,1)S(1)}, bf16[384,1024]{1,0:T(8,128)(2,1)S(1)}, u32[]{:S(2)}, u32[]{:S(2)}) collective-permute-start(bf16[384,1024]{1,0:T(8,128)(2,1)S(1)} %get-tuple-element.25.own_ref), channel_id=1, source_target_pairs={{0,4},{4,0},{8,12},{12,8},{16,20},{20,16},{24,28},{28,24},{1,5},{5... | collective-permute-start | bytes 2359304 | tf_op jit(solution)/shard_map/ppermute | solution.py:336
  34.9 6.0 %collective-permute-start.12 = (bf16[576,128]{1,0:T(8,128)(2,1)S(1)}, bf16[576,128]{1,0:T(8,128)(2,1)S(1)}, u32[]{:S(2)}, u32[]{:S(2)}) collective-permute-start(bf16[576,128]{1,0:T(8,128)(2,1)S(1)} %shard_map.116), channel_id=1, source_target_pairs={{0,1},{1,0},{2,3},{3,2},{4,5},{5,4},{6,7},{7,6},{8,9},{9,8},{10,11... | collective-permute-start | bytes 442376 | tf_op jit(solution)/shard_map/ppermute | solution.py:336
  41.0 4.3 %collective-permute-start.13 = (bf16[4,2,288,128]{3,2,1,0:T(8,128)(2,1)S(1)}, bf16[4,2,288,128]{3,2,1,0:T(8,128)(2,1)S(1)}, u32[]{:S(2)}, u32[]{:S(2)}) collective-permute-start(bf16[4,2,288,128]{3,2,1,0:T(8,128)(2,1)S(1)} %shard_map.118), channel_id=1, source_target_pairs={{0,4},{4,0},{8,12},{12,8},{16,20},{20,16},{24,28},{28,24},{1,5},{5... | collective-permute-start | bytes 1769480 | tf_op jit(solution)/shard_map/ppermute | solution.py:336
  41.1 9.3 %collective-permute-start.15 = (bf16[576,128]{1,0:T(8,128)(2,1)S(1)}, bf16[576,128]{1,0:T(8,128)(2,1)S(1)}, u32[]{:S(2)}, u32[]{:S(2)}) collective-permute-start(bf16[576,128]{1,0:T(8,128)(2,1)S(1)} %get-tuple-element.38), channel_id=1, source_target_pairs={{0,1},{1,0},{2,3},{3,2},{4,5},{5,4},{6,7},{7,6},{8,9},{9,8},{10,11... | collective-permute-start | bytes 442376 | tf_op jit(solution)/shard_map/ppermute | solution.py:336
  42.7 10.0 %collective-permute-start.14 = (bf16[576,128]{1,0:T(8,128)(2,1)S(1)}, bf16[576,128]{1,0:T(8,128)(2,1)S(1)}, u32[]{:S(2)}, u32[]{:S(2)}) collective-permute-start(bf16[576,128]{1,0:T(8,128)(2,1)S(1)} %shard_map.117._), channel_id=1, source_target_pairs={{0,2},{1,3},{2,0},{3,1},{4,6},{5,7},{6,4},{7,5},{8,10},{9,11},{10,... | collective-permute-start | bytes 442376 | tf_op jit(solution)/shard_map/ppermute | solution.py:336

commit v16 on v14

--- a/solution.py
+++ b/solution.py
@@ -97,23 +97,16 @@
         copy.wait()
 
 
-def turn_kernel(normed_hbm, cot_hbm, block_hbm, _, __, *refs):
-    *column_refs, own_ref, normed_ref, cot_ref, turned_ref, sem = refs
+def turn_kernel(normed_ref, cot_ref, block_ref, _, __, *refs):
+    *column_refs, own_ref, turned_ref = refs
     me = lax.axis_index("seq")
     cut = column_refs[0].shape[2]
-    copies = []
-    for which, (source, target) in enumerate(
-        ((normed_hbm, normed_ref), (cot_hbm, cot_ref), (block_hbm, own_ref))
-    ):
-        copies.append(pltpu.make_async_copy(source, target, sem.at[which]))
-        copies[-1].start()
+    own_ref[...] = block_ref[...]
     for which, ref in enumerate((normed_ref, cot_ref)):
-        copies[which].wait()
         turned_ref[which] = ref[...].astype(jnp.float32).T.astype(jnp.bfloat16)
         for chip, target in enumerate(column_refs):
             for far in range(2):
                 target[far, which] = turned_ref[which, at(me ^ (2 * chip + far), cut)]
-    copies[2].wait()
 
 
 def pass_on_kernel(_, *refs):
@@ -370,12 +363,8 @@
         turn_kernel,
         (shape((2, 2, cut, rows), bf16),) * (blocks // 2) + (shape(same.shape, bf16),),
         (normed_input, out_cotangent, same, held[2], held[blocks // 2 + 1]),
-        scratch=(
-            pltpu.VMEM(normed_input.shape, bf16),
-            pltpu.VMEM(out_cotangent.shape, bf16),
-            pltpu.VMEM((2, model, rows), bf16),
-            pltpu.SemaphoreType.DMA((3,)),
-        ),
+        in_vmem=range(3),
+        scratch=(pltpu.VMEM((2, model, rows), bf16),),
         moved=8 * rows * model,
         room=8,
     )
@@ -404,38 +393,38 @@
             pltpu.VMEM((HEAD_SIZE, wide), f32),
             pltpu.VMEM((2 * rows, HEAD_SIZE), f32),
         ),
+        flops=8 * tokens * tokens * q_cols,
+        moved=2 * tokens * packed_cols,
     )
     dx_got = swapped(dx_far, "seq", 1)
-    terms = {}
-    for chosen in ((3,), (2, 1, 0)):
-        made = kernel_call(
+    def terms_of(chosen, after):
+        return kernel_call(
             functools.partial(input_terms_kernel, chosen),
             tuple(shape((model // groups, rows), f32 if not apart else bf16) for apart in chosen),
-            (dx_own, dx_got, query_weight, key_matrix, value_matrix),
+            (dx_own, dx_got, query_weight, key_matrix, value_matrix, *after),
             in_vmem=range(5),
             scratch=(pltpu.VMEM((rows, 2 * (q_cols + 2 * kv_cols)), bf16),),
-            flops=2 * len(chosen) * rows * (model // groups) * 2 * (q_cols + 2 * kv_cols),
-            moved=2 * len(chosen) * (model // groups) * 2 * (q_cols + 2 * kv_cols),
             room=4,
         )
-        terms.update(zip(chosen, made))
+
+    (far_term,) = terms_of((3,), ())
+    pair_term, own_term = terms_of((2, 0), (far_term,))
     (pair_sum,) = kernel_call(
         add_kernel,
-        (shape(terms[2].shape, bf16),),
-        (terms[2], swapped(terms[3], "head", 1)),
+        (shape(pair_term.shape, bf16),),
+        (pair_term, swapped(far_term, "head", 1)),
         in_vmem=range(2),
-        moved=6 * rows * (model // groups),
         room=4,
     )
+    (near_term,) = terms_of((1,), (pair_sum,))
     (give,) = kernel_call(
         pass_on_kernel,
         (shape((blocks // 2, 2, cut, rows), bf16),),
-        (pair_sum, *columns),
+        (pair_term, *columns),
         in_vmem=range(1, 1 + blocks // 2),
-        moved=8 * cut * rows * blocks // 2,
         room=4,
     )
-    arrived = [swapped(terms[1], "head", 1), swapped(pair_sum, "head", 2)]
+    arrived = [swapped(pair_sum, "head", 2), swapped(near_term, "head", 1)]
     grad_wvalue, grad_woutput, weights_done = kernel_call(
         weight_grad_kernel,
         (
@@ -447,13 +436,11 @@
         in_vmem=range(3 + blocks // 2),
         scratch=(pltpu.VMEM((2, model // blocks, tokens), bf16),),
         room=8,
-        flops=4 * tokens * (model // blocks) * (q_cols + kv_cols),
-        moved=4 * (model // blocks) * (tokens + 2 * q_cols + 2 * kv_cols),
     )
     (grad_input,) = kernel_call(
         sum_kernel,
         (shape((model // groups, rows), bf16),),
-        (weights_done, terms[0], *arrived),
+        (weights_done, own_term, *arrived),
         in_vmem=range(1, 4),
         moved=4 * groups * (model // groups) * rows,
     )

time: 52.6 us -> 54.7 us (1.040)
  waiting for transfers between devices: 12.9 us -> 17.9 us
  local copies, waits for them, and re-layouts: 4.54 us -> 2.01 us
    ppermute x16, waiting for transfers between devices: 12.9 us -> 17.9 us  [swapped(): lax.ppermute(value, axis, [(place, place ^ apart) for place in range(coun...]
    unnamed x12, local copies, waits for them, and re-layouts: 4.54 us -> 2.01 us
    pallas_call x9 -> x10, Pallas kernels: 15 us -> 14.7 us  [kernel_call(): pl.pallas_call(body, out_shape=outs, in_specs=[vmem if place in in_vmem e...]
  transfers between devices with their start and end apart: 16 -> 16, of which waited for: 5 -> 7; matrix products, arithmetic and copies ran while one was open for 0% -> 0% of each run, Pallas kernels for 20% -> 19%
where the time goes in v16:
time: 54.7 us; the launch traced here: 54.5 us
  starting transfers between devices  19.2 us (35%)
  waiting for transfers between devices  17.9 us (33%)
  Pallas kernels  14.7 us (27%)
  local copies, waits for them, and re-layouts  2.01 us (4%)
  between operations  0.75 us (1%)
    ppermute x16, starting transfers between devices, swapped(): lax.ppermute(value, axis, [(place, place ^ apart) for place in range(coun...  19.2 us
    ppermute x16, waiting for transfers between devices, swapped(): lax.ppermute(value, axis, [(place, place ^ apart) for place in range(coun...  17.9 us
    pallas_call x10, Pallas kernels, kernel_call(): pl.pallas_call(body, out_shape=outs, in_specs=[vmem if place in in_vmem e...  14.7 us
    unnamed x12, local copies, waits for them, and re-layouts  2.01 us
  transfers between devices with their start and end apart: 16, of which 7 were waited for; matrix products, arithmetic and copies ran while one was open for 0% of the time, Pallas kernels for 19%

profile of v16, /device:TPU:0, one launch (start us, length us, event | category | flops | bytes accessed | tf_op | source)
XLA Modules:
  0.0 54.5 jit_solution(15257038274512963272)
XLA Ops:
  0.6 3.8 %shard_map.112 = (bf16[128,768]{1,0:T(8,128)(2,1)}, bf16[128,768]{1,0:T(8,128)(2,1)}) custom-call(bf16[128,2304]{1,0:T(8,128)(2,1)} %cot_ref.1, bf16[512,2304]{1,0:T(8,128)(2,1)} %weight_hbm.1, bf16[128,512]{1,0:T(8,128)(2,1)} %q_hbm.1, bf16[128,256]{1,0:T(8,128)(2,1)} %k_hbm.1, bf16[128,256]{1,0:T(8,128)(2,1)} %v_hbm.1), custom_call_target="tpu_custom_call" | custom-call | flops 301989888 | bytes 2949120 | tf_op jit(solution)/shard_map/pallas_call | solution.py:299
  4.4 3.0 %collective-permute-start = (bf16[128,768]{1,0:T(8,128)(2,1)}, bf16[128,768]{1,0:T(8,128)(2,1)S(1)}, u32[]{:S(2)}, u32[]{:S(2)}) collective-permute-start(bf16[128,768]{1,0:T(8,128)(2,1)} %get-tuple-element.18.block_ref), channel_id=1, source_target_pairs={{0,8},{4,12},{8,0},{12,4},{16,24},{20,28},{24,16},{28,20},{1,9},{5... | collective-permute-start | bytes 589832 | tf_op jit(solution)/shard_map/ppermute | solution.py:312
  7.4 0.7 %collective-permute-start.1 = (bf16[128,768]{1,0:T(8,128)(2,1)}, bf16[128,768]{1,0:T(8,128)(2,1)S(1)}, u32[]{:S(2)}, u32[]{:S(2)}) collective-permute-start(bf16[128,768]{1,0:T(8,128)(2,1)} %get-tuple-element.19), channel_id=1, source_target_pairs={{0,20},{4,16},{8,28},{12,24},{16,4},{20,0},{24,12},{28,8},{1,21},{... | collective-permute-start | bytes 589832 | tf_op jit(solution)/shard_map/ppermute | solution.py:312
  8.1 0.9 %collective-permute-start.4 = (bf16[128,768]{1,0:T(8,128)(2,1)}, bf16[128,768]{1,0:T(8,128)(2,1)S(1)}, u32[]{:S(2)}, u32[]{:S(2)}) collective-permute-start(bf16[128,768]{1,0:T(8,128)(2,1)} %get-tuple-element.18.block_ref), channel_id=1, source_target_pairs={{0,16},{4,20},{8,24},{12,28},{16,0},{20,4},{24,8},{28,12},{1,17},{... | collective-permute-start | bytes 589832 | tf_op jit(solution)/shard_map/ppermute | solution.py:312
  9.6 3.4 %collective-permute-done._.refs_2_ = bf16[128,768]{1,0:T(8,128)(2,1)S(1)} collective-permute-done((bf16[128,768]{1,0:T(8,128)(2,1)}, bf16[128,768]{1,0:T(8,128)(2,1)S(1)}, u32[]{:S(2)}, u32[]{:S(2)}) %collective-permute-start) | collective-permute-done | bytes 196640 | tf_op jit(solution)/shard_map/ppermute | solution.py:312
  13.1 2.2 %collective-permute-start.5 = (bf16[128,768]{1,0:T(8,128)(2,1)S(1)}, bf16[128,768]{1,0:T(8,128)(2,1)S(1)}, u32[]{:S(2)}, u32[]{:S(2)}) collective-permute-start(bf16[128,768]{1,0:T(8,128)(2,1)S(1)} %collective-permute-done._.refs_2_), channel_id=1, source_target_pairs={{0,16},{4,20},{8,24},{12,28},{16,0},{20,4},{24,8},{28,12},{1,17},{... | collective-permute-start | bytes 589832 | tf_op jit(solution)/shard_map/ppermute | solution.py:312
  15.2 1.7 %collective-permute-start.6 = (bf16[128,768]{1,0:T(8,128)(2,1)S(1)}, bf16[128,768]{1,0:T(8,128)(2,1)S(1)}, u32[]{:S(2)}, u32[]{:S(2)}) collective-permute-start(bf16[128,768]{1,0:T(8,128)(2,1)S(1)} %collective-permute-done.1.__.refs_5_), channel_id=1, source_target_pairs={{0,8},{4,12},{8,0},{12,4},{16,24},{20,28},{24,16},{28,20},{1,9},{5... | collective-permute-start | bytes 589832 | tf_op jit(solution)/shard_map/ppermute | solution.py:312
  17.0 1.1 %copy-done.4 = bf16[128,2304]{1,0:T(8,128)(2,1)S(1)} copy-done((bf16[128,2304]{1,0:T(8,128)(2,1)S(1)}, bf16[128,2304]{1,0:T(8,128)(2,1)}, u32[]{:S(2)}) %copy-start.4) | copy-done | bytes 589848
  18.0 0.9 %copy-done.5 = bf16[128,768]{1,0:T(8,128)(2,1)S(1)} copy-done((bf16[128,768]{1,0:T(8,128)(2,1)S(1)}, bf16[128,768]{1,0:T(8,128)(2,1)}, u32[]{:S(2)}) %copy-start.5) | copy-done | bytes 196632
  19.8 1.1 %collective-permute-start.9 = (bf16[2,2,288,128]{3,2,1,0:T(8,128)(2,1)S(1)}, bf16[2,2,288,128]{3,2,1,0:T(8,128)(2,1)S(1)}, u32[]{:S(2)}, u32[]{:S(2)}) collective-permute-start(bf16[2,2,288,128]{3,2,1,0:T(8,128)(2,1)S(1)} %get-tuple-element.24), channel_id=1, source_target_pairs={{0,16},{4,20},{8,24},{12,28},{16,0},{20,4},{24,8},{28,12},{1,17},{... | collective-permute-start | bytes 884744 | tf_op jit(solution)/shard_map/ppermute | solution.py:312
  21.0 2.1 %collective-permute-start.10 = (bf16[2,2,288,128]{3,2,1,0:T(8,128)(2,1)S(1)}, bf16[2,2,288,128]{3,2,1,0:T(8,128)(2,1)S(1)}, u32[]{:S(2)}, u32[]{:S(2)}) collective-permute-start(bf16[2,2,288,128]{3,2,1,0:T(8,128)(2,1)S(1)} %get-tuple-element.25), channel_id=1, source_target_pairs={{0,24},{4,28},{8,16},{12,20},{16,8},{20,12},{24,0},{28,4},{1,25},{... | collective-permute-start | bytes 884744 | tf_op jit(solution)/shard_map/ppermute | solution.py:312
  23.4 5.7 %shard_map.114 = (bf16[128,512]{1,0:T(8,128)(2,1)S(1)}, bf16[128,512]{1,0:T(8,128)(2,1)S(1)}, bf16[384,1024]{1,0:T(8,128)(2,1)S(1)}) custom-call(bf16[128,768]{1,0:T(8,128)(2,1)S(1)} %get-tuple-element.20.refs_0_, bf16[128,768]{1,0:T(8,128)(2,1)S(1)} %collective-permute-done.2.refs_1_, bf16[128,768]{1,0:T(8,128)(2,1)S(1)} %collective-permute-done._.refs_2_, ...), custom_call_target="tpu_custom_call" | custom-call | flops 2147483648 | bytes 1572864 | tf_op jit(solution)/shard_map/pallas_call | solution.py:299
  29.6 2.0 %collective-permute-done.11.far_ref = bf16[128,512]{1,0:T(8,128)(2,1)S(1)} collective-permute-done((bf16[128,512]{1,0:T(8,128)(2,1)S(1)}, bf16[128,512]{1,0:T(8,128)(2,1)S(1)}, u32[]{:S(2)}, u32[]{:S(2)}) %collective-permute-start.11) | collective-permute-done | bytes 131104 | tf_op jit(solution)/shard_map/ppermute | solution.py:312
  31.6 0.5 shard_map.115.refs_0_
  32.1 0.8 %shard_map.116 = (bf16[576,128]{1,0:T(8,128)(2,1)S(1)}, f32[576,128]{1,0:T(8,128)S(1)}) custom-call(bf16[128,512]{1,0:T(8,128)(2,1)S(1)} %get-tuple-element.26.own_ref, bf16[128,512]{1,0:T(8,128)(2,1)S(1)} %collective-permute-done.11.far_ref, bf16[2304,512]{1,0:T(8,128)(2,1)S(1)} %copy-done, bf16[2304,256]{1,0:T(8,128)(2,1)S(1)} %copy-done.1, ...), custom_call_target="tpu_custom_call" | custom-call | tf_op jit(solution)/shard_map/pallas_call | solution.py:299
  33.0 2.9 %collective-permute-done.9.refs_2_ = bf16[2,2,288,128]{3,2,1,0:T(8,128)(2,1)S(1)} collective-permute-done((bf16[2,2,288,128]{3,2,1,0:T(8,128)(2,1)S(1)}, bf16[2,2,288,128]{3,2,1,0:T(8,128)(2,1)S(1)}, u32[]{:S(2)}, u32[]{:S(2)}) %collective-permute-start.9) | collective-permute-done | bytes 294944 | tf_op jit(solution)/shard_map/ppermute | solution.py:312
  36.0 1.6 %collective-permute-start.13 = (bf16[576,128]{1,0:T(8,128)(2,1)S(1)}, bf16[576,128]{1,0:T(8,128)(2,1)S(1)}, u32[]{:S(2)}, u32[]{:S(2)}) collective-permute-start(bf16[576,128]{1,0:T(8,128)(2,1)S(1)} %shard_map.115.refs_0_), channel_id=1, source_target_pairs={{0,1},{1,0},{2,3},{3,2},{4,5},{5,4},{6,7},{7,6},{8,9},{9,8},{10,11... | collective-permute-start | bytes 442376 | tf_op jit(solution)/shard_map/ppermute | solution.py:312
  37.7 4.6 %collective-permute-done.13.arrived_ref = bf16[576,128]{1,0:T(8,128)(2,1)S(1)} collective-permute-done((bf16[576,128]{1,0:T(8,128)(2,1)S(1)}, bf16[576,128]{1,0:T(8,128)(2,1)S(1)}, u32[]{:S(2)}, u32[]{:S(2)}) %collective-permute-start.13) | collective-permute-done | bytes 147488 | tf_op jit(solution)/shard_map/ppermute | solution.py:312
  42.9 1.6 %collective-permute-start.15 = (bf16[576,128]{1,0:T(8,128)(2,1)S(1)}, bf16[576,128]{1,0:T(8,128)(2,1)S(1)}, u32[]{:S(2)}, u32[]{:S(2)}) collective-permute-start(bf16[576,128]{1,0:T(8,128)(2,1)S(1)} %shard_map.120), channel_id=1, source_target_pairs={{0,1},{1,0},{2,3},{3,2},{4,5},{5,4},{6,7},{7,6},{8,9},{9,8},{10,11... | collective-permute-start | bytes 442376 | tf_op jit(solution)/shard_map/ppermute | solution.py:312
  44.5 2.6 %collective-permute-start.14 = (bf16[576,128]{1,0:T(8,128)(2,1)S(1)}, bf16[576,128]{1,0:T(8,128)(2,1)S(1)}, u32[]{:S(2)}, u32[]{:S(2)}) collective-permute-start(bf16[576,128]{1,0:T(8,128)(2,1)S(1)} %shard_map.119.refs_0_), channel_id=1, source_target_pairs={{0,2},{1,3},{2,0},{3,1},{4,6},{5,7},{6,4},{7,5},{8,10},{9,11},{10,... | collective-permute-start | bytes 442376 | tf_op jit(solution)/shard_map/ppermute | solution.py:312
  47.1 2.0 %shard_map.118 = (f32[288,256]{1,0:T(8,128)}, f32[288,512]{1,0:T(8,128)}, f32[8,128]{1,0:T(8,128)S(1)}) custom-call(bf16[384,1024]{1,0:T(8,128)(2,1)S(1)} %get-tuple-element.21.own_ref, bf16[384,1024]{1,0:T(8,128)(2,1)S(1)} %collective-permute-done.7.far_ref, bf16[2,2,288,128]{3,2,1,0:T(8,128)(2,1)S(1)} %get-tuple-element.22.refs_0_, ...), custom_call_target="tpu_custom_call" | custom-call | tf_op jit(solution)/shard_map/pallas_call | solution.py:299
  49.1 1.7 %collective-permute-done.15.refs_1_ = bf16[576,128]{1,0:T(8,128)(2,1)S(1)} collective-permute-done((bf16[576,128]{1,0:T(8,128)(2,1)S(1)}, bf16[576,128]{1,0:T(8,128)(2,1)S(1)}, u32[]{:S(2)}, u32[]{:S(2)}) %collective-permute-start.15) | collective-permute-done | bytes 147488 | tf_op jit(solution)/shard_map/ppermute | solution.py:312
  50.9 2.9 %collective-permute-done.14.refs_0_ = bf16[576,128]{1,0:T(8,128)(2,1)S(1)} collective-permute-done((bf16[576,128]{1,0:T(8,128)(2,1)S(1)}, bf16[576,128]{1,0:T(8,128)(2,1)S(1)}, u32[]{:S(2)}, u32[]{:S(2)}) %collective-permute-start.14) | collective-permute-done | bytes 147488 | tf_op jit(solution)/shard_map/ppermute | solution.py:312
  53.8 0.7 %shard_map.121 = bf16[576,128]{1,0:T(8,128)(2,1)} custom-call(f32[8,128]{1,0:T(8,128)S(1)} %get-tuple-element.29._, f32[576,128]{1,0:T(8,128)S(1)} %get-tuple-element.30.own_ref, bf16[576,128]{1,0:T(8,128)(2,1)S(1)} %collective-permute-done.14.refs_0_, bf16[576,128]{1,0:T(8,128)(2,1)S(1)} %collective-permute-done.15.refs_1_), custom_call_target="tpu_custom_call" | custom-call | bytes 1179648 | tf_op jit(solution)/shard_map/pallas_call | solution.py:299
  (30 shorter events, 3.1 us)
Async XLA Ops:
  0.6 16.3 %copy-start.3 = (bf16[128,2304]{1,0:T(8,128)(2,1)S(1)}, bf16[128,2304]{1,0:T(8,128)(2,1)}, u32[]{:S(2)}) copy-start(bf16[128,2304]{1,0:T(8,128)(2,1)} %cot_ref.1) | copy-start | bytes 1769476
  4.4 8.6 %collective-permute-start = (bf16[128,768]{1,0:T(8,128)(2,1)}, bf16[128,768]{1,0:T(8,128)(2,1)S(1)}, u32[]{:S(2)}, u32[]{:S(2)}) collective-permute-start(bf16[128,768]{1,0:T(8,128)(2,1)} %get-tuple-element.18.block_ref), channel_id=1, source_target_pairs={{0,8},{4,12},{8,0},{12,4},{16,24},{20,28},{24,16},{28,20},{1,9},{5... | collective-permute-start | bytes 589832 | tf_op jit(solution)/shard_map/ppermute | solution.py:312
  7.4 7.8 %collective-permute-start.1 = (bf16[128,768]{1,0:T(8,128)(2,1)}, bf16[128,768]{1,0:T(8,128)(2,1)S(1)}, u32[]{:S(2)}, u32[]{:S(2)}) collective-permute-start(bf16[128,768]{1,0:T(8,128)(2,1)} %get-tuple-element.19), channel_id=1, source_target_pairs={{0,20},{4,16},{8,28},{12,24},{16,4},{20,0},{24,12},{28,8},{1,21},{... | collective-permute-start | bytes 589832 | tf_op jit(solution)/shard_map/ppermute | solution.py:312
  8.1 11.3 %collective-permute-start.4 = (bf16[128,768]{1,0:T(8,128)(2,1)}, bf16[128,768]{1,0:T(8,128)(2,1)S(1)}, u32[]{:S(2)}, u32[]{:S(2)}) collective-permute-start(bf16[128,768]{1,0:T(8,128)(2,1)} %get-tuple-element.18.block_ref), channel_id=1, source_target_pairs={{0,16},{4,20},{8,24},{12,28},{16,0},{20,4},{24,8},{28,12},{1,17},{... | collective-permute-start | bytes 589832 | tf_op jit(solution)/shard_map/ppermute | solution.py:312
  9.0 10.8 %collective-permute-start.3 = (bf16[128,768]{1,0:T(8,128)(2,1)}, bf16[128,768]{1,0:T(8,128)(2,1)S(1)}, u32[]{:S(2)}, u32[]{:S(2)}) collective-permute-start(bf16[128,768]{1,0:T(8,128)(2,1)} %get-tuple-element.19), channel_id=1, source_target_pairs={{0,12},{4,8},{8,4},{12,0},{16,28},{20,24},{24,20},{28,16},{1,13},{... | collective-permute-start | bytes 589832 | tf_op jit(solution)/shard_map/ppermute | solution.py:312
  9.2 11.8 %collective-permute-start.2 = (bf16[128,768]{1,0:T(8,128)(2,1)}, bf16[128,768]{1,0:T(8,128)(2,1)S(1)}, u32[]{:S(2)}, u32[]{:S(2)}) collective-permute-start(bf16[128,768]{1,0:T(8,128)(2,1)} %get-tuple-element.19), channel_id=1, source_target_pairs={{0,4},{4,0},{8,12},{12,8},{16,20},{20,16},{24,28},{28,24},{1,5},{5... | collective-permute-start | bytes 589832 | tf_op jit(solution)/shard_map/ppermute | solution.py:312
  13.1 10.3 %collective-permute-start.5 = (bf16[128,768]{1,0:T(8,128)(2,1)S(1)}, bf16[128,768]{1,0:T(8,128)(2,1)S(1)}, u32[]{:S(2)}, u32[]{:S(2)}) collective-permute-start(bf16[128,768]{1,0:T(8,128)(2,1)S(1)} %collective-permute-done._.refs_2_), channel_id=1, source_target_pairs={{0,16},{4,20},{8,24},{12,28},{16,0},{20,4},{24,8},{28,12},{1,17},{... | collective-permute-start | bytes 589832 | tf_op jit(solution)/shard_map/ppermute | solution.py:312
  15.2 8.1 %collective-permute-start.6 = (bf16[128,768]{1,0:T(8,128)(2,1)S(1)}, bf16[128,768]{1,0:T(8,128)(2,1)S(1)}, u32[]{:S(2)}, u32[]{:S(2)}) collective-permute-start(bf16[128,768]{1,0:T(8,128)(2,1)S(1)} %collective-permute-done.1.__.refs_5_), channel_id=1, source_target_pairs={{0,8},{4,12},{8,0},{12,4},{16,24},{20,28},{24,16},{28,20},{1,9},{5... | collective-permute-start | bytes 589832 | tf_op jit(solution)/shard_map/ppermute | solution.py:312
  17.0 1.1 %copy-start.4 = (bf16[128,2304]{1,0:T(8,128)(2,1)S(1)}, bf16[128,2304]{1,0:T(8,128)(2,1)}, u32[]{:S(2)}) copy-start(bf16[128,2304]{1,0:T(8,128)(2,1)} %normed_ref.1) | copy-start | bytes 1769476
  18.0 0.9 %copy-start.5 = (bf16[128,768]{1,0:T(8,128)(2,1)S(1)}, bf16[128,768]{1,0:T(8,128)(2,1)}, u32[]{:S(2)}) copy-start(bf16[128,768]{1,0:T(8,128)(2,1)} %get-tuple-element.18.block_ref) | copy-start | bytes 589828
  19.5 13.5 %collective-permute-start.8 = (bf16[2,2,288,128]{3,2,1,0:T(8,128)(2,1)S(1)}, bf16[2,2,288,128]{3,2,1,0:T(8,128)(2,1)S(1)}, u32[]{:S(2)}, u32[]{:S(2)}) collective-permute-start(bf16[2,2,288,128]{3,2,1,0:T(8,128)(2,1)S(1)} %get-tuple-element.23), channel_id=1, source_target_pairs={{0,8},{4,12},{8,0},{12,4},{16,24},{20,28},{24,16},{28,20},{1,9},{5... | collective-permute-start | bytes 884744 | tf_op jit(solution)/shard_map/ppermute | solution.py:312
  19.8 16.1 %collective-permute-start.9 = (bf16[2,2,288,128]{3,2,1,0:T(8,128)(2,1)S(1)}, bf16[2,2,288,128]{3,2,1,0:T(8,128)(2,1)S(1)}, u32[]{:S(2)}, u32[]{:S(2)}) collective-permute-start(bf16[2,2,288,128]{3,2,1,0:T(8,128)(2,1)S(1)} %get-tuple-element.24), channel_id=1, source_target_pairs={{0,16},{4,20},{8,24},{12,28},{16,0},{20,4},{24,8},{28,12},{1,17},{... | collective-permute-start | bytes 884744 | tf_op jit(solution)/shard_map/ppermute | solution.py:312
  21.0 14.9 %collective-permute-start.10 = (bf16[2,2,288,128]{3,2,1,0:T(8,128)(2,1)S(1)}, bf16[2,2,288,128]{3,2,1,0:T(8,128)(2,1)S(1)}, u32[]{:S(2)}, u32[]{:S(2)}) collective-permute-start(bf16[2,2,288,128]{3,2,1,0:T(8,128)(2,1)S(1)} %get-tuple-element.25), channel_id=1, source_target_pairs={{0,24},{4,28},{8,16},{12,20},{16,8},{20,12},{24,0},{28,4},{1,25},{... | collective-permute-start | bytes 884744 | tf_op jit(solution)/shard_map/ppermute | solution.py:312
  23.3 8.3 %copy-start = (bf16[2304,512]{1,0:T(8,128)(2,1)S(1)}, bf16[2304,512]{1,0:T(8,128)(2,1)}, u32[]{:S(2)}) copy-start(bf16[2304,512]{1,0:T(8,128)(2,1)} %wq_ref.5) | copy-start | bytes 7077892
  23.3 8.3 %copy-start.1 = (bf16[2304,256]{1,0:T(8,128)(2,1)S(1)}, bf16[2304,256]{1,0:T(8,128)(2,1)}, u32[]{:S(2)}) copy-start(bf16[2304,256]{1,0:T(8,128)(2,1)} %wk_ref.5) | copy-start | bytes 3538948
  23.3 8.3 %copy-start.2 = (bf16[2304,256]{1,0:T(8,128)(2,1)S(1)}, bf16[2304,256]{1,0:T(8,128)(2,1)}, u32[]{:S(2)}) copy-start(bf16[2304,256]{1,0:T(8,128)(2,1)} %wv_ref.5) | copy-start | bytes 3538948
  29.1 18.1 %collective-permute-start.7 = (bf16[384,1024]{1,0:T(8,128)(2,1)S(1)}, bf16[384,1024]{1,0:T(8,128)(2,1)S(1)}, u32[]{:S(2)}, u32[]{:S(2)}) collective-permute-start(bf16[384,1024]{1,0:T(8,128)(2,1)S(1)} %get-tuple-element.21.own_ref), channel_id=1, source_target_pairs={{0,4},{4,0},{8,12},{12,8},{16,20},{20,16},{24,28},{28,24},{1,5},{5... | collective-permute-start | bytes 2359304 | tf_op jit(solution)/shard_map/ppermute | solution.py:312
  29.1 2.5 %collective-permute-start.11 = (bf16[128,512]{1,0:T(8,128)(2,1)S(1)}, bf16[128,512]{1,0:T(8,128)(2,1)S(1)}, u32[]{:S(2)}, u32[]{:S(2)}) collective-permute-start(bf16[128,512]{1,0:T(8,128)(2,1)S(1)} %get-tuple-element.27), channel_id=1, source_target_pairs={{0,4},{4,0},{8,12},{12,8},{16,20},{20,16},{24,28},{28,24},{1,5},{5... | collective-permute-start | bytes 393224 | tf_op jit(solution)/shard_map/ppermute | solution.py:312
  36.0 11.2 %collective-permute-start.12 = (bf16[4,2,288,128]{3,2,1,0:T(8,128)(2,1)S(1)}, bf16[4,2,288,128]{3,2,1,0:T(8,128)(2,1)S(1)}, u32[]{:S(2)}, u32[]{:S(2)}) collective-permute-start(bf16[4,2,288,128]{3,2,1,0:T(8,128)(2,1)S(1)} %shard_map.117), channel_id=1, source_target_pairs={{0,4},{4,0},{8,12},{12,8},{16,20},{20,16},{24,28},{28,24},{1,5},{5... | collective-permute-start | bytes 1769480 | tf_op jit(solution)/shard_map/ppermute | solution.py:312
  36.0 6.3 %collective-permute-start.13 = (bf16[576,128]{1,0:T(8,128)(2,1)S(1)}, bf16[576,128]{1,0:T(8,128)(2,1)S(1)}, u32[]{:S(2)}, u32[]{:S(2)}) collective-permute-start(bf16[576,128]{1,0:T(8,128)(2,1)S(1)} %shard_map.115.refs_0_), channel_id=1, source_target_pairs={{0,1},{1,0},{2,3},{3,2},{4,5},{5,4},{6,7},{7,6},{8,9},{9,8},{10,11... | collective-permute-start | bytes 442376 | tf_op jit(solution)/shard_map/ppermute | solution.py:312
  42.9 8.0 %collective-permute-start.15 = (bf16[576,128]{1,0:T(8,128)(2,1)S(1)}, bf16[576,128]{1,0:T(8,128)(2,1)S(1)}, u32[]{:S(2)}, u32[]{:S(2)}) collective-permute-start(bf16[576,128]{1,0:T(8,128)(2,1)S(1)} %shard_map.120), channel_id=1, source_target_pairs={{0,1},{1,0},{2,3},{3,2},{4,5},{5,4},{6,7},{7,6},{8,9},{9,8},{10,11... | collective-permute-start | bytes 442376 | tf_op jit(solution)/shard_map/ppermute | solution.py:312
  44.5 9.2 %collective-permute-start.14 = (bf16[576,128]{1,0:T(8,128)(2,1)S(1)}, bf16[576,128]{1,0:T(8,128)(2,1)S(1)}, u32[]{:S(2)}, u32[]{:S(2)}) collective-permute-start(bf16[576,128]{1,0:T(8,128)(2,1)S(1)} %shard_map.119.refs_0_), channel_id=1, source_target_pairs={{0,2},{1,3},{2,0},{3,1},{4,6},{5,7},{6,4},{7,5},{8,10},{9,11},{10,... | collective-permute-start | bytes 442376 | tf_op jit(solution)/shard_map/ppermute | solution.py:312

commit v17 on v16

--- a/solution.py
+++ b/solution.py
@@ -109,10 +109,18 @@
                 target[far, which] = turned_ref[which, at(me ^ (2 * chip + far), cut)]
 
 
-def pass_on_kernel(_, *refs):
+def pass_on_kernel(_, parts_ref, *refs):
     *column_refs, give_ref = refs
+    cut, rows = column_refs[0].shape[2:]
     for chip, ref in enumerate(column_refs):
-        give_ref[chip] = ref[1]
+        for which in range(2):
+            first = (2 * chip + which) * cut
+            give_ref[first : first + cut] = ref[1, which]
+    first = 2 * len(column_refs) * cut
+    part_rows = parts_ref.shape[0]
+    for block in range(parts_ref.shape[1] // rows):
+        give_ref[first : first + part_rows] = parts_ref[:, block * rows : (block + 1) * rows]
+        first += part_rows
 
 
 def attention_kernel(blocks, *refs):
@@ -263,15 +271,23 @@
         ).astype(target.dtype)
 
 
-def weight_grad_kernel(own_ref, far_ref, *refs):
-    column_refs, (wvalue_ref, woutput_ref, done_ref, joined_ref) = refs[:-4], refs[-4:]
+def weight_grad_kernel(own_ref, got_ref, *refs):
+    column_refs, refs = refs[:-5], refs[-5:]
+    wvalue_ref, woutput_ref, done_ref, joined_ref, far_ref = refs
     done_ref[...] = jnp.zeros_like(done_ref)
     me = lax.axis_index("seq")
     core = me % 2
-    *column_refs, got_ref = column_refs
+    cut, rows = column_refs[0].shape[2:]
     for chip, ref in enumerate(column_refs):
-        joined_ref[:, :, at(me ^ (2 * chip), ref.shape[3])] = ref[0]
-        joined_ref[:, :, at(me ^ (2 * chip + 1), ref.shape[3])] = got_ref[chip]
+        joined_ref[:, :, at(me ^ (2 * chip), rows)] = ref[0]
+        for which in range(2):
+            first = (2 * chip + which) * cut
+            joined_ref[which, :, at(me ^ (2 * chip + 1), rows)] = got_ref[first : first + cut]
+    first = 2 * len(column_refs) * cut
+    part_rows = far_ref.shape[0]
+    for block in range(far_ref.shape[1] // rows):
+        far_ref[:, block * rows : (block + 1) * rows] = got_ref[first : first + part_rows]
+        first += part_rows
     kv_cols = wvalue_ref.shape[1] // 2
     q_cols = woutput_ref.shape[1] // 2
     for half, ref in ((core, own_ref), (1 - core, far_ref)):
@@ -397,18 +413,20 @@
         moved=2 * tokens * packed_cols,
     )
     dx_got = swapped(dx_far, "seq", 1)
-    def terms_of(chosen, after):
+    def terms_of(chosen):
         return kernel_call(
             functools.partial(input_terms_kernel, chosen),
             tuple(shape((model // groups, rows), f32 if not apart else bf16) for apart in chosen),
-            (dx_own, dx_got, query_weight, key_matrix, value_matrix, *after),
+            (dx_own, dx_got, query_weight, key_matrix, value_matrix),
             in_vmem=range(5),
             scratch=(pltpu.VMEM((rows, 2 * (q_cols + 2 * kv_cols)), bf16),),
+            flops=2 * len(chosen) * rows * (model // groups) * 2 * (q_cols + 2 * kv_cols),
+            moved=2 * len(chosen) * (model // groups) * 2 * (q_cols + 2 * kv_cols),
             room=4,
         )
 
-    (far_term,) = terms_of((3,), ())
-    pair_term, own_term = terms_of((2, 0), (far_term,))
+    (far_term,) = terms_of((3,))
+    pair_term, near_term, own_term = terms_of((2, 1, 0))
     (pair_sum,) = kernel_call(
         add_kernel,
         (shape(pair_term.shape, bf16),),
@@ -416,12 +434,12 @@
         in_vmem=range(2),
         room=4,
     )
-    (near_term,) = terms_of((1,), (pair_sum,))
+    part_rows = q_cols + kv_cols
     (give,) = kernel_call(
         pass_on_kernel,
-        (shape((blocks // 2, 2, cut, rows), bf16),),
-        (pair_term, *columns),
-        in_vmem=range(1, 1 + blocks // 2),
+        (shape((blocks * (cut + part_rows), rows), bf16),),
+        (pair_sum, grad_parts, *columns),
+        in_vmem=range(1, 2 + blocks // 2),
         room=4,
     )
     arrived = [swapped(pair_sum, "head", 2), swapped(near_term, "head", 1)]
@@ -432,9 +450,12 @@
             shape((model // blocks, 2 * q_cols), f32),
             shape((8, HEAD_SIZE), f32),
         ),
-        (grad_parts, swapped(grad_parts, "seq", 1), *columns, swapped(give, "seq", 1)),
-        in_vmem=range(3 + blocks // 2),
-        scratch=(pltpu.VMEM((2, model // blocks, tokens), bf16),),
+        (grad_parts, swapped(give, "seq", 1), *columns),
+        in_vmem=range(2 + blocks // 2),
+        scratch=(
+            pltpu.VMEM((2, model // blocks, tokens), bf16),
+            pltpu.VMEM((part_rows, tokens), bf16),
+        ),
         room=8,
     )
     (grad_input,) = kernel_call(

time: 54.7 us -> 49.9 us (0.912)
  waiting for transfers between devices: 17.9 us -> 13.7 us
    ppermute x16 -> x15, waiting for transfers between devices: 17.9 us -> 13.7 us  [swapped(): lax.ppermute(value, axis, [(place, place ^ apart) for place in range(coun...]
    ppermute x16 -> x15, starting transfers between devices: 19.2 us -> 18.7 us  [swapped(): lax.ppermute(value, axis, [(place, place ^ apart) for place in range(coun...]
    pallas_call x10 -> x9, Pallas kernels: 14.7 us -> 14.6 us  [kernel_call(): pl.pallas_call(body, out_shape=outs, in_specs=[vmem if place in in_vmem e...]
  transfers between devices with their start and end apart: 16 -> 15, of which waited for: 7 -> 6; matrix products, arithmetic and copies ran while one was open for 0% -> 0% of each run, Pallas kernels for 19% -> 20%
where the time goes in v17:
time: 49.9 us; the launch traced here: 49.7 us
  starting transfers between devices  18.7 us (37%)
  Pallas kernels  14.6 us (29%)
  waiting for transfers between devices  13.7 us (27%)
  local copies, waits for them, and re-layouts  2.01 us (4%)
  between operations  0.76 us (2%)
    ppermute x15, starting transfers between devices, swapped(): lax.ppermute(value, axis, [(place, place ^ apart) for place in range(coun...  18.7 us
    pallas_call x9, Pallas kernels, kernel_call(): pl.pallas_call(body, out_shape=outs, in_specs=[vmem if place in in_vmem e...  14.6 us
    ppermute x15, waiting for transfers between devices, swapped(): lax.ppermute(value, axis, [(place, place ^ apart) for place in range(coun...  13.7 us
    unnamed x12, local copies, waits for them, and re-layouts  2.01 us
  transfers between devices with their start and end apart: 15, of which 6 were waited for; matrix products, arithmetic and copies ran while one was open for 0% of the time, Pallas kernels for 20%

profile of v17, /device:TPU:0, one launch (start us, length us, event | category | flops | bytes accessed | tf_op | source)
XLA Modules:
  0.0 49.7 jit_solution(7479203928232570894)
XLA Ops:
  0.6 3.8 %shard_map.112 = (bf16[128,768]{1,0:T(8,128)(2,1)}, bf16[128,768]{1,0:T(8,128)(2,1)}) custom-call(bf16[128,2304]{1,0:T(8,128)(2,1)} %cot_ref.1, bf16[512,2304]{1,0:T(8,128)(2,1)} %weight_hbm.1, bf16[128,512]{1,0:T(8,128)(2,1)} %q_hbm.1, bf16[128,256]{1,0:T(8,128)(2,1)} %k_hbm.1, bf16[128,256]{1,0:T(8,128)(2,1)} %v_hbm.1), custom_call_target="tpu_custom_call" | custom-call | flops 301989888 | bytes 2949120 | tf_op jit(solution)/shard_map/pallas_call | solution.py:315
  4.4 3.0 %collective-permute-start = (bf16[128,768]{1,0:T(8,128)(2,1)}, bf16[128,768]{1,0:T(8,128)(2,1)S(1)}, u32[]{:S(2)}, u32[]{:S(2)}) collective-permute-start(bf16[128,768]{1,0:T(8,128)(2,1)} %get-tuple-element.19.block_ref), channel_id=1, source_target_pairs={{0,8},{4,12},{8,0},{12,4},{16,24},{20,28},{24,16},{28,20},{1,9},{5... | collective-permute-start | bytes 589832 | tf_op jit(solution)/shard_map/ppermute | solution.py:328
  7.4 0.7 %collective-permute-start.1 = (bf16[128,768]{1,0:T(8,128)(2,1)}, bf16[128,768]{1,0:T(8,128)(2,1)S(1)}, u32[]{:S(2)}, u32[]{:S(2)}) collective-permute-start(bf16[128,768]{1,0:T(8,128)(2,1)} %get-tuple-element.20), channel_id=1, source_target_pairs={{0,20},{4,16},{8,28},{12,24},{16,4},{20,0},{24,12},{28,8},{1,21},{... | collective-permute-start | bytes 589832 | tf_op jit(solution)/shard_map/ppermute | solution.py:328
  8.1 0.9 %collective-permute-start.4 = (bf16[128,768]{1,0:T(8,128)(2,1)}, bf16[128,768]{1,0:T(8,128)(2,1)S(1)}, u32[]{:S(2)}, u32[]{:S(2)}) collective-permute-start(bf16[128,768]{1,0:T(8,128)(2,1)} %get-tuple-element.19.block_ref), channel_id=1, source_target_pairs={{0,16},{4,20},{8,24},{12,28},{16,0},{20,4},{24,8},{28,12},{1,17},{... | collective-permute-start | bytes 589832 | tf_op jit(solution)/shard_map/ppermute | solution.py:328
  9.6 3.4 %collective-permute-done._.refs_2_ = bf16[128,768]{1,0:T(8,128)(2,1)S(1)} collective-permute-done((bf16[128,768]{1,0:T(8,128)(2,1)}, bf16[128,768]{1,0:T(8,128)(2,1)S(1)}, u32[]{:S(2)}, u32[]{:S(2)}) %collective-permute-start) | collective-permute-done | bytes 196640 | tf_op jit(solution)/shard_map/ppermute | solution.py:328
  13.1 2.2 %collective-permute-start.5 = (bf16[128,768]{1,0:T(8,128)(2,1)S(1)}, bf16[128,768]{1,0:T(8,128)(2,1)S(1)}, u32[]{:S(2)}, u32[]{:S(2)}) collective-permute-start(bf16[128,768]{1,0:T(8,128)(2,1)S(1)} %collective-permute-done._.refs_2_), channel_id=1, source_target_pairs={{0,16},{4,20},{8,24},{12,28},{16,0},{20,4},{24,8},{28,12},{1,17},{... | collective-permute-start | bytes 589832 | tf_op jit(solution)/shard_map/ppermute | solution.py:328
  15.2 1.7 %collective-permute-start.6 = (bf16[128,768]{1,0:T(8,128)(2,1)S(1)}, bf16[128,768]{1,0:T(8,128)(2,1)S(1)}, u32[]{:S(2)}, u32[]{:S(2)}) collective-permute-start(bf16[128,768]{1,0:T(8,128)(2,1)S(1)} %collective-permute-done.1.__.refs_5_), channel_id=1, source_target_pairs={{0,8},{4,12},{8,0},{12,4},{16,24},{20,28},{24,16},{28,20},{1,9},{5... | collective-permute-start | bytes 589832 | tf_op jit(solution)/shard_map/ppermute | solution.py:328
  17.0 1.1 %copy-done.4 = bf16[128,2304]{1,0:T(8,128)(2,1)S(1)} copy-done((bf16[128,2304]{1,0:T(8,128)(2,1)S(1)}, bf16[128,2304]{1,0:T(8,128)(2,1)}, u32[]{:S(2)}) %copy-start.4) | copy-done | bytes 589848
  18.0 0.9 %copy-done.5 = bf16[128,768]{1,0:T(8,128)(2,1)S(1)} copy-done((bf16[128,768]{1,0:T(8,128)(2,1)S(1)}, bf16[128,768]{1,0:T(8,128)(2,1)}, u32[]{:S(2)}) %copy-start.5) | copy-done | bytes 196632
  19.0 0.5 shard_map.113
  19.8 1.1 %collective-permute-start.10 = (bf16[2,2,288,128]{3,2,1,0:T(8,128)(2,1)S(1)}, bf16[2,2,288,128]{3,2,1,0:T(8,128)(2,1)S(1)}, u32[]{:S(2)}, u32[]{:S(2)}) collective-permute-start(bf16[2,2,288,128]{3,2,1,0:T(8,128)(2,1)S(1)} %get-tuple-element.28), channel_id=1, source_target_pairs={{0,16},{4,20},{8,24},{12,28},{16,0},{20,4},{24,8},{28,12},{1,17},{... | collective-permute-start | bytes 884744 | tf_op jit(solution)/shard_map/ppermute | solution.py:328
  21.0 2.1 %collective-permute-start.11 = (bf16[2,2,288,128]{3,2,1,0:T(8,128)(2,1)S(1)}, bf16[2,2,288,128]{3,2,1,0:T(8,128)(2,1)S(1)}, u32[]{:S(2)}, u32[]{:S(2)}) collective-permute-start(bf16[2,2,288,128]{3,2,1,0:T(8,128)(2,1)S(1)} %get-tuple-element.29), channel_id=1, source_target_pairs={{0,24},{4,28},{8,16},{12,20},{16,8},{20,12},{24,0},{28,4},{1,25},{... | collective-permute-start | bytes 884744 | tf_op jit(solution)/shard_map/ppermute | solution.py:328
  23.4 5.7 %shard_map.114 = (bf16[128,512]{1,0:T(8,128)(2,1)S(1)}, bf16[128,512]{1,0:T(8,128)(2,1)S(1)}, bf16[384,1024]{1,0:T(8,128)(2,1)S(1)}) custom-call(bf16[128,768]{1,0:T(8,128)(2,1)S(1)} %get-tuple-element.21.refs_0_, bf16[128,768]{1,0:T(8,128)(2,1)S(1)} %collective-permute-done.2.refs_1_, bf16[128,768]{1,0:T(8,128)(2,1)S(1)} %collective-permute-done._.refs_2_, ...), custom_call_target="tpu_custom_call" | custom-call | flops 2147483648 | bytes 1572864 | tf_op jit(solution)/shard_map/pallas_call | solution.py:315
  29.1 1.3 %collective-permute-done.7.far_ref = bf16[128,512]{1,0:T(8,128)(2,1)S(1)} collective-permute-done((bf16[128,512]{1,0:T(8,128)(2,1)S(1)}, bf16[128,512]{1,0:T(8,128)(2,1)S(1)}, u32[]{:S(2)}, u32[]{:S(2)}) %collective-permute-start.7) | collective-permute-done | bytes 131104 | tf_op jit(solution)/shard_map/ppermute | solution.py:328
  30.5 0.5 %shard_map.116 = bf16[576,128]{1,0:T(8,128)(2,1)S(1)} custom-call(bf16[128,512]{1,0:T(8,128)(2,1)S(1)} %get-tuple-element.23.own_ref, bf16[128,512]{1,0:T(8,128)(2,1)S(1)} %collective-permute-done.7.far_ref, bf16[2304,512]{1,0:T(8,128)(2,1)S(1)} %copy-done, bf16[2304,256]{1,0:T(8,128)(2,1)S(1)} %copy-done.1, bf16[2304,256]{1,0:T(8,128)(2,1)S(1)} %copy-done.2), custom_call_target="tpu_custom_call" | custom-call | flops 150994944 | bytes 1179648 | tf_op jit(solution)/shard_map/pallas_call | solution.py:315
  31.0 1.6 %collective-permute-start.8 = (bf16[576,128]{1,0:T(8,128)(2,1)S(1)}, bf16[576,128]{1,0:T(8,128)(2,1)S(1)}, u32[]{:S(2)}, u32[]{:S(2)}) collective-permute-start(bf16[576,128]{1,0:T(8,128)(2,1)S(1)} %shard_map.116), channel_id=1, source_target_pairs={{0,1},{1,0},{2,3},{3,2},{4,5},{5,4},{6,7},{7,6},{8,9},{9,8},{10,11... | collective-permute-start | bytes 442376 | tf_op jit(solution)/shard_map/ppermute | solution.py:328
  32.7 1.1 %shard_map.115 = (bf16[576,128]{1,0:T(8,128)(2,1)S(1)}, bf16[576,128]{1,0:T(8,128)(2,1)S(1)}, f32[576,128]{1,0:T(8,128)S(1)}) custom-call(bf16[128,512]{1,0:T(8,128)(2,1)S(1)} %get-tuple-element.23.own_ref, bf16[128,512]{1,0:T(8,128)(2,1)S(1)} %collective-permute-done.7.far_ref, bf16[2304,512]{1,0:T(8,128)(2,1)S(1)} %copy-done, ...), custom_call_target="tpu_custom_call" | custom-call | flops 452984832 | bytes 3538944 | tf_op jit(solution)/shard_map/pallas_call | solution.py:315
  33.8 3.2 %collective-permute-done.8.arrived_ref = bf16[576,128]{1,0:T(8,128)(2,1)S(1)} collective-permute-done((bf16[576,128]{1,0:T(8,128)(2,1)S(1)}, bf16[576,128]{1,0:T(8,128)(2,1)S(1)}, u32[]{:S(2)}, u32[]{:S(2)}) %collective-permute-start.8) | collective-permute-done | bytes 147488 | tf_op jit(solution)/shard_map/ppermute | solution.py:328
  37.3 1.6 %collective-permute-start.14 = (bf16[576,128]{1,0:T(8,128)(2,1)S(1)}, bf16[576,128]{1,0:T(8,128)(2,1)S(1)}, u32[]{:S(2)}, u32[]{:S(2)}) collective-permute-start(bf16[576,128]{1,0:T(8,128)(2,1)S(1)} %get-tuple-element.32), channel_id=1, source_target_pairs={{0,1},{1,0},{2,3},{3,2},{4,5},{5,4},{6,7},{7,6},{8,9},{9,8},{10,11... | collective-permute-start | bytes 442376 | tf_op jit(solution)/shard_map/ppermute | solution.py:328
  39.0 2.6 %collective-permute-start.13 = (bf16[576,128]{1,0:T(8,128)(2,1)S(1)}, bf16[576,128]{1,0:T(8,128)(2,1)S(1)}, u32[]{:S(2)}, u32[]{:S(2)}) collective-permute-start(bf16[576,128]{1,0:T(8,128)(2,1)S(1)} %shard_map.117._), channel_id=1, source_target_pairs={{0,2},{1,3},{2,0},{3,1},{4,6},{5,7},{6,4},{7,5},{8,10},{9,11},{10,... | collective-permute-start | bytes 442376 | tf_op jit(solution)/shard_map/ppermute | solution.py:328
  41.6 2.1 %shard_map.119 = (f32[288,256]{1,0:T(8,128)}, f32[288,512]{1,0:T(8,128)}, f32[8,128]{1,0:T(8,128)S(1)}) custom-call(bf16[384,1024]{1,0:T(8,128)(2,1)S(1)} %get-tuple-element.22.parts_ref.own_ref, bf16[5376,128]{1,0:T(8,128)(2,1)S(1)} %collective-permute-done.12.got_ref, bf16[2,2,288,128]{3,2,1,0:T(8,128)(2,1)S(1)} %get-tuple-element.26.refs_0_, ...), custom_call_target="tpu_custom_call" | custom-call | tf_op jit(solution)/shard_map/pallas_call | solution.py:315
  43.6 3.0 %collective-permute-done.14.refs_1_ = bf16[576,128]{1,0:T(8,128)(2,1)S(1)} collective-permute-done((bf16[576,128]{1,0:T(8,128)(2,1)S(1)}, bf16[576,128]{1,0:T(8,128)(2,1)S(1)}, u32[]{:S(2)}, u32[]{:S(2)}) %collective-permute-start.14) | collective-permute-done | bytes 147488 | tf_op jit(solution)/shard_map/ppermute | solution.py:328
  46.6 2.4 %collective-permute-done.13.refs_0_ = bf16[576,128]{1,0:T(8,128)(2,1)S(1)} collective-permute-done((bf16[576,128]{1,0:T(8,128)(2,1)S(1)}, bf16[576,128]{1,0:T(8,128)(2,1)S(1)}, u32[]{:S(2)}, u32[]{:S(2)}) %collective-permute-start.13) | collective-permute-done | bytes 147488 | tf_op jit(solution)/shard_map/ppermute | solution.py:328
  49.0 0.7 %shard_map.120 = bf16[576,128]{1,0:T(8,128)(2,1)} custom-call(f32[8,128]{1,0:T(8,128)S(1)} %get-tuple-element.30._, f32[576,128]{1,0:T(8,128)S(1)} %get-tuple-element.31.own_ref, bf16[576,128]{1,0:T(8,128)(2,1)S(1)} %collective-permute-done.13.refs_0_, bf16[576,128]{1,0:T(8,128)(2,1)S(1)} %collective-permute-done.14.refs_1_), custom_call_target="tpu_custom_call" | custom-call | bytes 1179648 | tf_op jit(solution)/shard_map/pallas_call | solution.py:315
  (27 shorter events, 1.7 us)
Async XLA Ops:
  0.6 16.3 %copy-start.3 = (bf16[128,2304]{1,0:T(8,128)(2,1)S(1)}, bf16[128,2304]{1,0:T(8,128)(2,1)}, u32[]{:S(2)}) copy-start(bf16[128,2304]{1,0:T(8,128)(2,1)} %cot_ref.1) | copy-start | bytes 1769476
  4.4 8.6 %collective-permute-start = (bf16[128,768]{1,0:T(8,128)(2,1)}, bf16[128,768]{1,0:T(8,128)(2,1)S(1)}, u32[]{:S(2)}, u32[]{:S(2)}) collective-permute-start(bf16[128,768]{1,0:T(8,128)(2,1)} %get-tuple-element.19.block_ref), channel_id=1, source_target_pairs={{0,8},{4,12},{8,0},{12,4},{16,24},{20,28},{24,16},{28,20},{1,9},{5... | collective-permute-start | bytes 589832 | tf_op jit(solution)/shard_map/ppermute | solution.py:328
  7.4 7.8 %collective-permute-start.1 = (bf16[128,768]{1,0:T(8,128)(2,1)}, bf16[128,768]{1,0:T(8,128)(2,1)S(1)}, u32[]{:S(2)}, u32[]{:S(2)}) collective-permute-start(bf16[128,768]{1,0:T(8,128)(2,1)} %get-tuple-element.20), channel_id=1, source_target_pairs={{0,20},{4,16},{8,28},{12,24},{16,4},{20,0},{24,12},{28,8},{1,21},{... | collective-permute-start | bytes 589832 | tf_op jit(solution)/shard_map/ppermute | solution.py:328
  8.1 11.3 %collective-permute-start.4 = (bf16[128,768]{1,0:T(8,128)(2,1)}, bf16[128,768]{1,0:T(8,128)(2,1)S(1)}, u32[]{:S(2)}, u32[]{:S(2)}) collective-permute-start(bf16[128,768]{1,0:T(8,128)(2,1)} %get-tuple-element.19.block_ref), channel_id=1, source_target_pairs={{0,16},{4,20},{8,24},{12,28},{16,0},{20,4},{24,8},{28,12},{1,17},{... | collective-permute-start | bytes 589832 | tf_op jit(solution)/shard_map/ppermute | solution.py:328
  9.0 10.8 %collective-permute-start.3 = (bf16[128,768]{1,0:T(8,128)(2,1)}, bf16[128,768]{1,0:T(8,128)(2,1)S(1)}, u32[]{:S(2)}, u32[]{:S(2)}) collective-permute-start(bf16[128,768]{1,0:T(8,128)(2,1)} %get-tuple-element.20), channel_id=1, source_target_pairs={{0,12},{4,8},{8,4},{12,0},{16,28},{20,24},{24,20},{28,16},{1,13},{... | collective-permute-start | bytes 589832 | tf_op jit(solution)/shard_map/ppermute | solution.py:328
  9.2 11.8 %collective-permute-start.2 = (bf16[128,768]{1,0:T(8,128)(2,1)}, bf16[128,768]{1,0:T(8,128)(2,1)S(1)}, u32[]{:S(2)}, u32[]{:S(2)}) collective-permute-start(bf16[128,768]{1,0:T(8,128)(2,1)} %get-tuple-element.20), channel_id=1, source_target_pairs={{0,4},{4,0},{8,12},{12,8},{16,20},{20,16},{24,28},{28,24},{1,5},{5... | collective-permute-start | bytes 589832 | tf_op jit(solution)/shard_map/ppermute | solution.py:328
  13.1 10.3 %collective-permute-start.5 = (bf16[128,768]{1,0:T(8,128)(2,1)S(1)}, bf16[128,768]{1,0:T(8,128)(2,1)S(1)}, u32[]{:S(2)}, u32[]{:S(2)}) collective-permute-start(bf16[128,768]{1,0:T(8,128)(2,1)S(1)} %collective-permute-done._.refs_2_), channel_id=1, source_target_pairs={{0,16},{4,20},{8,24},{12,28},{16,0},{20,4},{24,8},{28,12},{1,17},{... | collective-permute-start | bytes 589832 | tf_op jit(solution)/shard_map/ppermute | solution.py:328
  15.2 8.1 %collective-permute-start.6 = (bf16[128,768]{1,0:T(8,128)(2,1)S(1)}, bf16[128,768]{1,0:T(8,128)(2,1)S(1)}, u32[]{:S(2)}, u32[]{:S(2)}) collective-permute-start(bf16[128,768]{1,0:T(8,128)(2,1)S(1)} %collective-permute-done.1.__.refs_5_), channel_id=1, source_target_pairs={{0,8},{4,12},{8,0},{12,4},{16,24},{20,28},{24,16},{28,20},{1,9},{5... | collective-permute-start | bytes 589832 | tf_op jit(solution)/shard_map/ppermute | solution.py:328
  17.0 1.1 %copy-start.4 = (bf16[128,2304]{1,0:T(8,128)(2,1)S(1)}, bf16[128,2304]{1,0:T(8,128)(2,1)}, u32[]{:S(2)}) copy-start(bf16[128,2304]{1,0:T(8,128)(2,1)} %normed_ref.1) | copy-start | bytes 1769476
  18.0 0.9 %copy-start.5 = (bf16[128,768]{1,0:T(8,128)(2,1)S(1)}, bf16[128,768]{1,0:T(8,128)(2,1)}, u32[]{:S(2)}) copy-start(bf16[128,768]{1,0:T(8,128)(2,1)} %get-tuple-element.19.block_ref) | copy-start | bytes 589828
  19.5 17.6 %collective-permute-start.9 = (bf16[2,2,288,128]{3,2,1,0:T(8,128)(2,1)S(1)}, bf16[2,2,288,128]{3,2,1,0:T(8,128)(2,1)S(1)}, u32[]{:S(2)}, u32[]{:S(2)}) collective-permute-start(bf16[2,2,288,128]{3,2,1,0:T(8,128)(2,1)S(1)} %get-tuple-element.27), channel_id=1, source_target_pairs={{0,8},{4,12},{8,0},{12,4},{16,24},{20,28},{24,16},{28,20},{1,9},{5... | collective-permute-start | bytes 884744 | tf_op jit(solution)/shard_map/ppermute | solution.py:328
  19.8 17.2 %collective-permute-start.10 = (bf16[2,2,288,128]{3,2,1,0:T(8,128)(2,1)S(1)}, bf16[2,2,288,128]{3,2,1,0:T(8,128)(2,1)S(1)}, u32[]{:S(2)}, u32[]{:S(2)}) collective-permute-start(bf16[2,2,288,128]{3,2,1,0:T(8,128)(2,1)S(1)} %get-tuple-element.28), channel_id=1, source_target_pairs={{0,16},{4,20},{8,24},{12,28},{16,0},{20,4},{24,8},{28,12},{1,17},{... | collective-permute-start | bytes 884744 | tf_op jit(solution)/shard_map/ppermute | solution.py:328
  21.0 16.1 %collective-permute-start.11 = (bf16[2,2,288,128]{3,2,1,0:T(8,128)(2,1)S(1)}, bf16[2,2,288,128]{3,2,1,0:T(8,128)(2,1)S(1)}, u32[]{:S(2)}, u32[]{:S(2)}) collective-permute-start(bf16[2,2,288,128]{3,2,1,0:T(8,128)(2,1)S(1)} %get-tuple-element.29), channel_id=1, source_target_pairs={{0,24},{4,28},{8,16},{12,20},{16,8},{20,12},{24,0},{28,4},{1,25},{... | collective-permute-start | bytes 884744 | tf_op jit(solution)/shard_map/ppermute | solution.py:328
  23.3 7.1 %copy-start = (bf16[2304,512]{1,0:T(8,128)(2,1)S(1)}, bf16[2304,512]{1,0:T(8,128)(2,1)}, u32[]{:S(2)}) copy-start(bf16[2304,512]{1,0:T(8,128)(2,1)} %wq_ref.3) | copy-start | bytes 7077892
  23.3 7.1 %copy-start.1 = (bf16[2304,256]{1,0:T(8,128)(2,1)S(1)}, bf16[2304,256]{1,0:T(8,128)(2,1)}, u32[]{:S(2)}) copy-start(bf16[2304,256]{1,0:T(8,128)(2,1)} %wk_ref.3) | copy-start | bytes 3538948
  23.3 7.1 %copy-start.2 = (bf16[2304,256]{1,0:T(8,128)(2,1)S(1)}, bf16[2304,256]{1,0:T(8,128)(2,1)}, u32[]{:S(2)}) copy-start(bf16[2304,256]{1,0:T(8,128)(2,1)} %wv_ref.3) | copy-start | bytes 3538948
  29.1 1.4 %collective-permute-start.7 = (bf16[128,512]{1,0:T(8,128)(2,1)S(1)}, bf16[128,512]{1,0:T(8,128)(2,1)S(1)}, u32[]{:S(2)}, u32[]{:S(2)}) collective-permute-start(bf16[128,512]{1,0:T(8,128)(2,1)S(1)} %get-tuple-element.24), channel_id=1, source_target_pairs={{0,4},{4,0},{8,12},{12,8},{16,20},{20,16},{24,28},{28,24},{1,5},{5... | collective-permute-start | bytes 393224 | tf_op jit(solution)/shard_map/ppermute | solution.py:328
  31.0 6.0 %collective-permute-start.8 = (bf16[576,128]{1,0:T(8,128)(2,1)S(1)}, bf16[576,128]{1,0:T(8,128)(2,1)S(1)}, u32[]{:S(2)}, u32[]{:S(2)}) collective-permute-start(bf16[576,128]{1,0:T(8,128)(2,1)S(1)} %shard_map.116), channel_id=1, source_target_pairs={{0,1},{1,0},{2,3},{3,2},{4,5},{5,4},{6,7},{7,6},{8,9},{9,8},{10,11... | collective-permute-start | bytes 442376 | tf_op jit(solution)/shard_map/ppermute | solution.py:328
  37.2 4.3 %collective-permute-start.12 = (bf16[5376,128]{1,0:T(8,128)(2,1)S(1)}, bf16[5376,128]{1,0:T(8,128)(2,1)S(1)}, u32[]{:S(2)}, u32[]{:S(2)}) collective-permute-start(bf16[5376,128]{1,0:T(8,128)(2,1)S(1)} %shard_map.118), channel_id=1, source_target_pairs={{0,4},{4,0},{8,12},{12,8},{16,20},{20,16},{24,28},{28,24},{1,5},{5... | collective-permute-start | bytes 4128776 | tf_op jit(solution)/shard_map/ppermute | solution.py:328
  37.3 9.3 %collective-permute-start.14 = (bf16[576,128]{1,0:T(8,128)(2,1)S(1)}, bf16[576,128]{1,0:T(8,128)(2,1)S(1)}, u32[]{:S(2)}, u32[]{:S(2)}) collective-permute-start(bf16[576,128]{1,0:T(8,128)(2,1)S(1)} %get-tuple-element.32), channel_id=1, source_target_pairs={{0,1},{1,0},{2,3},{3,2},{4,5},{5,4},{6,7},{7,6},{8,9},{9,8},{10,11... | collective-permute-start | bytes 442376 | tf_op jit(solution)/shard_map/ppermute | solution.py:328
  39.0 10.0 %collective-permute-start.13 = (bf16[576,128]{1,0:T(8,128)(2,1)S(1)}, bf16[576,128]{1,0:T(8,128)(2,1)S(1)}, u32[]{:S(2)}, u32[]{:S(2)}) collective-permute-start(bf16[576,128]{1,0:T(8,128)(2,1)S(1)} %shard_map.117._), channel_id=1, source_target_pairs={{0,2},{1,3},{2,0},{3,1},{4,6},{5,7},{6,4},{7,5},{8,10},{9,11},{10,... | collective-permute-start | bytes 442376 | tf_op jit(solution)/shard_map/ppermute | solution.py:328

commit v18 on v17

--- a/solution.py
+++ b/solution.py
@@ -109,7 +109,7 @@
                 target[far, which] = turned_ref[which, at(me ^ (2 * chip + far), cut)]
 
 
-def pass_on_kernel(_, parts_ref, *refs):
+def pass_on_kernel(_, attn_ref, dv_t_ref, *refs):
     *column_refs, give_ref = refs
     cut, rows = column_refs[0].shape[2:]
     for chip, ref in enumerate(column_refs):
@@ -117,10 +117,10 @@
             first = (2 * chip + which) * cut
             give_ref[first : first + cut] = ref[1, which]
     first = 2 * len(column_refs) * cut
-    part_rows = parts_ref.shape[0]
-    for block in range(parts_ref.shape[1] // rows):
-        give_ref[first : first + part_rows] = parts_ref[:, block * rows : (block + 1) * rows]
-        first += part_rows
+    for ref in (attn_ref, dv_t_ref):
+        for block in range(ref.shape[1] // rows):
+            give_ref[first : first + ref.shape[0]] = ref[:, block * rows : (block + 1) * rows]
+            first += ref.shape[0]
 
 
 def attention_kernel(blocks, *refs):
@@ -131,18 +131,19 @@
     block_refs,
     dx_own_ref,
     dx_far_ref,
-    parts_ref,
+    attn_ref,
+    prob_ref,
+    grad_t_ref,
     gathered_ref,
     score_even_ref,
     score_odd_ref,
-    prob_ref,
-    grad_t_ref,
     delta_ref,
     query_ref,
     value_t_ref,
     key_t_ref,
     dq_t_ref,
     dk_ref,
+    dv_ref,
 ):
     me = lax.axis_index("seq")
     core, chip = me % 2, me // 2
@@ -192,7 +193,7 @@
         inverse = 1.0 / jnp.sum(total, axis=0, keepdims=True)
         attn = dot_nn(value_t_ref[:, :span], prob_ref[:span, lanes]) * inverse
         for h in range(heads):
-            parts_ref[h * HEAD_SIZE : (h + 1) * HEAD_SIZE, own] = attn[
+            attn_ref[h * HEAD_SIZE : (h + 1) * HEAD_SIZE, own] = attn[
                 :, h * size : (h + 1) * size
             ].astype(jnp.bfloat16)
         grads_t = jnp.concatenate(
@@ -210,22 +211,18 @@
         grad_t_ref[:, lanes] = grads_t
         delta_ref[:, lanes] = jnp.sum(grads_t.astype(jnp.float32) * attn, axis=0, keepdims=True)
 
-    for step in range(steps):
-        own = slice(step * size, (step + 1) * size)
-        parts_ref[heads * HEAD_SIZE :, own] = dot_nt(
-            grad_t_ref[:, step * wide :], prob_ref[own, step * wide :]
-        ).astype(jnp.bfloat16)
-
     dq_t_ref[...] = jnp.zeros_like(dq_t_ref)
     dk_ref[...] = jnp.zeros_like(dk_ref)
+    dv_ref[...] = jnp.zeros_like(dv_ref)
     for step in range(steps):
         key_step = jnp.minimum(chip, step)
         query_step = jnp.maximum(chip, step)
         dprob = dot_nn(
             gathered_ref[at(key_step, size), value_cols], grad_t_ref[:, at(query_step, wide)]
         )
+        prob = prob_ref[at(key_step, size), at(query_step, wide)]
         dscore = (
-            prob_ref[at(key_step, size), at(query_step, wide)].astype(jnp.float32)
+            prob.astype(jnp.float32)
             * (dprob - delta_ref[:, at(query_step, wide)])
         ).astype(jnp.bfloat16)
 
@@ -236,6 +233,7 @@
         @pl.when(step >= chip)
         def _():
             dk_ref[...] += dot_nn(dscore, query_ref[at(query_step, wide)])
+            dv_ref[...] += dot_nt(prob, grad_t_ref[:, at(query_step, wide)])
 
     for target, half in ((dx_far_ref, 1 - core), (dx_own_ref, core)):
         for h in range(heads):
@@ -244,7 +242,17 @@
                 .T.astype(jnp.bfloat16)
             )
         target[:, key_cols] = (logit_scale * dk_ref[at(half, rows)]).astype(jnp.bfloat16)
-        target[:, value_cols] = parts_ref[heads * HEAD_SIZE :, at(2 * chip + half, rows)].T
+        target[:, value_cols] = dv_ref[at(half, rows)].astype(jnp.bfloat16)
+
+
+def value_grad_kernel(prob_ref, grad_t_ref, dv_t_ref):
+    size = 2 * HEAD_SIZE
+    wide = QUERIES_PER_KEY * size
+    for step in range(prob_ref.shape[0] // size):
+        own = slice(step * size, (step + 1) * size)
+        dv_t_ref[:, own] = dot_nt(grad_t_ref[:, step * wide :], prob_ref[own, step * wide :]).astype(
+            jnp.bfloat16
+        )
 
 
 def input_terms_kernel(apart_groups, own_ref, far_ref, wq_ref, wk_ref, wv_ref, *refs):
@@ -271,9 +279,9 @@
         ).astype(target.dtype)
 
 
-def weight_grad_kernel(own_ref, got_ref, *refs):
-    column_refs, refs = refs[:-5], refs[-5:]
-    wvalue_ref, woutput_ref, done_ref, joined_ref, far_ref = refs
+def weight_grad_kernel(attn_ref, dv_t_ref, got_ref, *refs):
+    column_refs, refs = refs[:-6], refs[-6:]
+    wvalue_ref, woutput_ref, done_ref, joined_ref, far_attn_ref, far_dv_ref = refs
     done_ref[...] = jnp.zeros_like(done_ref)
     me = lax.axis_index("seq")
     core = me % 2
@@ -284,23 +292,25 @@
             first = (2 * chip + which) * cut
             joined_ref[which, :, at(me ^ (2 * chip + 1), rows)] = got_ref[first : first + cut]
     first = 2 * len(column_refs) * cut
-    part_rows = far_ref.shape[0]
-    for block in range(far_ref.shape[1] // rows):
-        far_ref[:, block * rows : (block + 1) * rows] = got_ref[first : first + part_rows]
-        first += part_rows
-    kv_cols = wvalue_ref.shape[1] // 2
-    q_cols = woutput_ref.shape[1] // 2
-    for half, ref in ((core, own_ref), (1 - core, far_ref)):
-        woutput_ref[:, at(half, q_cols)] = dot_nt(joined_ref[1], ref[:q_cols])
-        wvalue_ref[:, at(half, kv_cols)] = dot_nt(joined_ref[0], ref[q_cols:])
-
-
-def add_kernel(own_ref, arrived_ref, sum_ref):
+    for ref in (far_attn_ref, far_dv_ref):
+        for block in range(ref.shape[1] // rows):
+            ref[:, block * rows : (block + 1) * rows] = got_ref[first : first + ref.shape[0]]
+            first += ref.shape[0]
+    for half, attn, dv_t in ((core, attn_ref, dv_t_ref), (1 - core, far_attn_ref, far_dv_ref)):
+        woutput_ref[:, at(half, attn.shape[0])] = dot_nt(joined_ref[1], attn[...])
+        wvalue_ref[:, at(half, dv_t.shape[0])] = dot_nt(joined_ref[0], dv_t[...])
+
+
+def add_kernel(own_ref, arrived_ref, _, sum_ref):
     total = own_ref[...].astype(jnp.float32) + arrived_ref[...].astype(jnp.float32)
     sum_ref[...] = total.astype(jnp.bfloat16)
 
 
-def sum_kernel(_, own_ref, *refs):
+def far_sum_kernel(_, own_ref, arrived_ref, sum_ref):
+    sum_ref[...] = own_ref[...] + arrived_ref[...].astype(jnp.float32)
+
+
+def sum_kernel(own_ref, *refs):
     total = own_ref[...]
     for arrived_ref in refs[:-1]:
         total = total + arrived_ref[...].astype(jnp.float32)
@@ -387,12 +397,14 @@
     columns = [columns[0]] + [
         swapped(columns[chip], "seq", 2 * chip) for chip in range(1, blocks // 2)
     ]
-    dx_own, dx_far, grad_parts = kernel_call(
+    dx_own, dx_far, attn, prob, grad_t = kernel_call(
         functools.partial(attention_kernel, blocks),
         (
             shape((rows, q_cols + 2 * kv_cols), bf16),
             shape((rows, q_cols + 2 * kv_cols), bf16),
-            shape((q_cols + kv_cols, tokens), bf16),
+            shape((q_cols, tokens), bf16),
+            shape((tokens, tokens * QUERIES_PER_KEY), bf16),
+            shape((HEAD_SIZE, tokens * QUERIES_PER_KEY), bf16),
         ),
         [held[apart] for apart in range(blocks)],
         in_vmem=range(blocks),
@@ -400,13 +412,12 @@
             pltpu.VMEM((tokens, packed_cols), bf16),
             pltpu.VMEM((tokens, wide), f32),
             pltpu.VMEM((tokens, wide), f32),
-            pltpu.VMEM((tokens, tokens * QUERIES_PER_KEY), bf16),
-            pltpu.VMEM((HEAD_SIZE, tokens * QUERIES_PER_KEY), bf16),
             pltpu.VMEM((1, tokens * QUERIES_PER_KEY), f32),
             pltpu.VMEM((tokens * QUERIES_PER_KEY, HEAD_SIZE), bf16),
             pltpu.VMEM((HEAD_SIZE, tokens), bf16),
             pltpu.VMEM((HEAD_SIZE, tokens), bf16),
             pltpu.VMEM((HEAD_SIZE, wide), f32),
+            pltpu.VMEM((2 * rows, HEAD_SIZE), f32),
             pltpu.VMEM((2 * rows, HEAD_SIZE), f32),
         ),
         flops=8 * tokens * tokens * q_cols,
@@ -427,10 +438,19 @@
 
     (far_term,) = terms_of((3,))
     pair_term, near_term, own_term = terms_of((2, 1, 0))
+    (dv_t,) = kernel_call(
+        value_grad_kernel,
+        (shape((kv_cols, tokens), bf16),),
+        (prob, grad_t),
+        in_vmem=range(2),
+        flops=tokens * tokens * q_cols,
+        moved=2 * tokens * tokens * QUERIES_PER_KEY,
+        room=4,
+    )
     (pair_sum,) = kernel_call(
         add_kernel,
         (shape(pair_term.shape, bf16),),
-        (pair_term, swapped(far_term, "head", 1)),
+        (pair_term, swapped(far_term, "head", 1), dv_t),
         in_vmem=range(2),
         room=4,
     )
@@ -438,11 +458,10 @@
     (give,) = kernel_call(
         pass_on_kernel,
         (shape((blocks * (cut + part_rows), rows), bf16),),
-        (pair_sum, grad_parts, *columns),
-        in_vmem=range(1, 2 + blocks // 2),
+        (pair_sum, attn, dv_t, *columns),
+        in_vmem=range(1, 3 + blocks // 2),
         room=4,
     )
-    arrived = [swapped(pair_sum, "head", 2), swapped(near_term, "head", 1)]
     grad_wvalue, grad_woutput, weights_done = kernel_call(
         weight_grad_kernel,
         (
@@ -450,19 +469,28 @@
             shape((model // blocks, 2 * q_cols), f32),
             shape((8, HEAD_SIZE), f32),
         ),
-        (grad_parts, swapped(give, "seq", 1), *columns),
-        in_vmem=range(2 + blocks // 2),
+        (attn, dv_t, swapped(give, "seq", 1), *columns),
+        in_vmem=range(3 + blocks // 2),
         scratch=(
             pltpu.VMEM((2, model // blocks, tokens), bf16),
-            pltpu.VMEM((part_rows, tokens), bf16),
+            pltpu.VMEM((q_cols, tokens), bf16),
+            pltpu.VMEM((kv_cols, tokens), bf16),
         ),
         room=8,
+    )
+    (far_sum,) = kernel_call(
+        far_sum_kernel,
+        (shape((model // groups, rows), f32),),
+        (weights_done, own_term, swapped(pair_sum, "head", 2)),
+        in_vmem=range(1, 3),
+        moved=10 * rows * (model // groups),
+        room=4,
     )
     (grad_input,) = kernel_call(
         sum_kernel,
         (shape((model // groups, rows), bf16),),
-        (weights_done, own_term, *arrived),
-        in_vmem=range(1, 4),
+        (far_sum, swapped(near_term, "head", 1)),
+        in_vmem=range(2),
         moved=4 * groups * (model // groups) * rows,
     )
     return (grad_input.T, grad_wvalue, grad_woutput.T)

time: 49.9 us -> 48.4 us (0.970)
  waiting for transfers between devices: 13.7 us -> 11.6 us
  Pallas kernels: 14.6 us -> 15.1 us
    ppermute x15, waiting for transfers between devices: 13.7 us -> 11.6 us  [swapped(): lax.ppermute(value, axis, [(place, place ^ apart) for place in range(coun...]
    pallas_call x9 -> x11, Pallas kernels: 14.6 us -> 15.1 us  [kernel_call(): pl.pallas_call(body, out_shape=outs, in_specs=[vmem if place in in_vmem e...]
  transfers between devices with their start and end apart: 15 -> 15, of which waited for: 6 -> 6; matrix products, arithmetic and copies ran while one was open for 0% -> 0% of each run, Pallas kernels for 20% -> 22%
where the time goes in v18:
time: 48.4 us; the launch traced here: 48.2 us
  starting transfers between devices  18.7 us (39%)
  Pallas kernels  15.1 us (31%)
  waiting for transfers between devices  11.6 us (24%)
  local copies, waits for them, and re-layouts  2.01 us (4%)
  between operations  0.77 us (2%)
    ppermute x15, starting transfers between devices, swapped(): lax.ppermute(value, axis, [(place, place ^ apart) for place in range(coun...  18.7 us
    pallas_call x11, Pallas kernels, kernel_call(): pl.pallas_call(body, out_shape=outs, in_specs=[vmem if place in in_vmem e...  15.1 us
    ppermute x15, waiting for transfers between devices, swapped(): lax.ppermute(value, axis, [(place, place ^ apart) for place in range(coun...  11.6 us
    unnamed x12, local copies, waits for them, and re-layouts  2.01 us
  transfers between devices with their start and end apart: 15, of which 6 were waited for; matrix products, arithmetic and copies ran while one was open for 0% of the time, Pallas kernels for 22%

profile of v18, /device:TPU:0, one launch (start us, length us, event | category | flops | bytes accessed | tf_op | source)
XLA Modules:
  0.0 48.2 jit_solution(1947979161098328108)
XLA Ops:
  0.6 3.8 %shard_map.112 = (bf16[128,768]{1,0:T(8,128)(2,1)}, bf16[128,768]{1,0:T(8,128)(2,1)}) custom-call(bf16[128,2304]{1,0:T(8,128)(2,1)} %cot_ref.1, bf16[512,2304]{1,0:T(8,128)(2,1)} %weight_hbm.1, bf16[128,512]{1,0:T(8,128)(2,1)} %q_hbm.1, bf16[128,256]{1,0:T(8,128)(2,1)} %k_hbm.1, bf16[128,256]{1,0:T(8,128)(2,1)} %v_hbm.1), custom_call_target="tpu_custom_call" | custom-call | flops 301989888 | bytes 2949120 | tf_op jit(solution)/shard_map/pallas_call | solution.py:325
  4.4 3.0 %collective-permute-start = (bf16[128,768]{1,0:T(8,128)(2,1)}, bf16[128,768]{1,0:T(8,128)(2,1)S(1)}, u32[]{:S(2)}, u32[]{:S(2)}) collective-permute-start(bf16[128,768]{1,0:T(8,128)(2,1)} %get-tuple-element.21.block_ref), channel_id=1, source_target_pairs={{0,8},{4,12},{8,0},{12,4},{16,24},{20,28},{24,16},{28,20},{1,9},{5... | collective-permute-start | bytes 589832 | tf_op jit(solution)/shard_map/ppermute | solution.py:338
  7.4 0.7 %collective-permute-start.1 = (bf16[128,768]{1,0:T(8,128)(2,1)}, bf16[128,768]{1,0:T(8,128)(2,1)S(1)}, u32[]{:S(2)}, u32[]{:S(2)}) collective-permute-start(bf16[128,768]{1,0:T(8,128)(2,1)} %get-tuple-element.22), channel_id=1, source_target_pairs={{0,20},{4,16},{8,28},{12,24},{16,4},{20,0},{24,12},{28,8},{1,21},{... | collective-permute-start | bytes 589832 | tf_op jit(solution)/shard_map/ppermute | solution.py:338
  8.1 0.9 %collective-permute-start.4 = (bf16[128,768]{1,0:T(8,128)(2,1)}, bf16[128,768]{1,0:T(8,128)(2,1)S(1)}, u32[]{:S(2)}, u32[]{:S(2)}) collective-permute-start(bf16[128,768]{1,0:T(8,128)(2,1)} %get-tuple-element.21.block_ref), channel_id=1, source_target_pairs={{0,16},{4,20},{8,24},{12,28},{16,0},{20,4},{24,8},{28,12},{1,17},{... | collective-permute-start | bytes 589832 | tf_op jit(solution)/shard_map/ppermute | solution.py:338
  9.6 3.4 %collective-permute-done._.refs_2_ = bf16[128,768]{1,0:T(8,128)(2,1)S(1)} collective-permute-done((bf16[128,768]{1,0:T(8,128)(2,1)}, bf16[128,768]{1,0:T(8,128)(2,1)S(1)}, u32[]{:S(2)}, u32[]{:S(2)}) %collective-permute-start) | collective-permute-done | bytes 196640 | tf_op jit(solution)/shard_map/ppermute | solution.py:338
  13.1 2.2 %collective-permute-start.5 = (bf16[128,768]{1,0:T(8,128)(2,1)S(1)}, bf16[128,768]{1,0:T(8,128)(2,1)S(1)}, u32[]{:S(2)}, u32[]{:S(2)}) collective-permute-start(bf16[128,768]{1,0:T(8,128)(2,1)S(1)} %collective-permute-done._.refs_2_), channel_id=1, source_target_pairs={{0,16},{4,20},{8,24},{12,28},{16,0},{20,4},{24,8},{28,12},{1,17},{... | collective-permute-start | bytes 589832 | tf_op jit(solution)/shard_map/ppermute | solution.py:338
  15.2 1.7 %collective-permute-start.6 = (bf16[128,768]{1,0:T(8,128)(2,1)S(1)}, bf16[128,768]{1,0:T(8,128)(2,1)S(1)}, u32[]{:S(2)}, u32[]{:S(2)}) collective-permute-start(bf16[128,768]{1,0:T(8,128)(2,1)S(1)} %collective-permute-done.1.__.refs_5_), channel_id=1, source_target_pairs={{0,8},{4,12},{8,0},{12,4},{16,24},{20,28},{24,16},{28,20},{1,9},{5... | collective-permute-start | bytes 589832 | tf_op jit(solution)/shard_map/ppermute | solution.py:338
  17.0 1.1 %copy-done.4 = bf16[128,2304]{1,0:T(8,128)(2,1)S(1)} copy-done((bf16[128,2304]{1,0:T(8,128)(2,1)S(1)}, bf16[128,2304]{1,0:T(8,128)(2,1)}, u32[]{:S(2)}) %copy-start.4) | copy-done | bytes 589848
  18.0 0.9 %copy-done.5 = bf16[128,768]{1,0:T(8,128)(2,1)S(1)} copy-done((bf16[128,768]{1,0:T(8,128)(2,1)S(1)}, bf16[128,768]{1,0:T(8,128)(2,1)}, u32[]{:S(2)}) %copy-start.5) | copy-done | bytes 196632
  19.0 0.5 %shard_map.113 = (bf16[2,2,288,128]{3,2,1,0:T(8,128)(2,1)S(1)}, bf16[2,2,288,128]{3,2,1,0:T(8,128)(2,1)S(1)}, bf16[2,2,288,128]{3,2,1,0:T(8,128)(2,1)S(1)}, bf16...) custom-call(bf16[128,2304]{1,0:T(8,128)(2,1)S(1)} %copy-done.4, bf16[128,2304]{1,0:T(8,128)(2,1)S(1)} %copy-done.3, ...), custom_call_target="tpu_custom_call" | custom-call | bytes 2359296 | tf_op jit(solution)/shard_map/pallas_call | solution.py:325
  19.8 1.1 %collective-permute-start.10 = (bf16[2,2,288,128]{3,2,1,0:T(8,128)(2,1)S(1)}, bf16[2,2,288,128]{3,2,1,0:T(8,128)(2,1)S(1)}, u32[]{:S(2)}, u32[]{:S(2)}) collective-permute-start(bf16[2,2,288,128]{3,2,1,0:T(8,128)(2,1)S(1)} %get-tuple-element.32), channel_id=1, source_target_pairs={{0,16},{4,20},{8,24},{12,28},{16,0},{20,4},{24,8},{28,12},{1,17},{... | collective-permute-start | bytes 884744 | tf_op jit(solution)/shard_map/ppermute | solution.py:338
  21.0 2.1 %collective-permute-start.11 = (bf16[2,2,288,128]{3,2,1,0:T(8,128)(2,1)S(1)}, bf16[2,2,288,128]{3,2,1,0:T(8,128)(2,1)S(1)}, u32[]{:S(2)}, u32[]{:S(2)}) collective-permute-start(bf16[2,2,288,128]{3,2,1,0:T(8,128)(2,1)S(1)} %get-tuple-element.33), channel_id=1, source_target_pairs={{0,24},{4,28},{8,16},{12,20},{16,8},{20,12},{24,0},{28,4},{1,25},{... | collective-permute-start | bytes 884744 | tf_op jit(solution)/shard_map/ppermute | solution.py:338
  23.4 5.2 %shard_map.114 = (bf16[128,512]{1,0:T(8,128)(2,1)S(1)}, bf16[128,512]{1,0:T(8,128)(2,1)S(1)}, bf16[256,1024]{1,0:T(8,128)(2,1)S(1)}, bf16[1024,2048]{1,0:T(8,128)(2,1)S(1)}, bf16[128,2048]{1,0:T(8,128)(2,1)S(1)}) custom-call(bf16[128,768]{1,0:T(8,128)(2,1)S(1)} %get-tuple-element.23.refs_0_, bf16[128,768]{1,0:T(8,128)(2,1)S(1)} %collective-permute-done.2.refs_1_, ...), custom_call_target="tpu_custom_call" | custom-call | flops 2147483648 | bytes 1572864 | tf_op jit(solution)/shard_map/pallas_call | solution.py:325
  28.7 1.3 %collective-permute-done.7.far_ref = bf16[128,512]{1,0:T(8,128)(2,1)S(1)} collective-permute-done((bf16[128,512]{1,0:T(8,128)(2,1)S(1)}, bf16[128,512]{1,0:T(8,128)(2,1)S(1)}, u32[]{:S(2)}, u32[]{:S(2)}) %collective-permute-start.7) | collective-permute-done | bytes 131104 | tf_op jit(solution)/shard_map/ppermute | solution.py:338
  30.0 0.5 %shard_map.117 = bf16[576,128]{1,0:T(8,128)(2,1)S(1)} custom-call(bf16[128,512]{1,0:T(8,128)(2,1)S(1)} %get-tuple-element.27.own_ref, bf16[128,512]{1,0:T(8,128)(2,1)S(1)} %collective-permute-done.7.far_ref, bf16[2304,512]{1,0:T(8,128)(2,1)S(1)} %copy-done, bf16[2304,256]{1,0:T(8,128)(2,1)S(1)} %copy-done.1, bf16[2304,256]{1,0:T(8,128)(2,1)S(1)} %copy-done.2), custom_call_target="tpu_custom_call" | custom-call | flops 150994944 | bytes 1179648 | tf_op jit(solution)/shard_map/pallas_call | solution.py:325
  30.6 1.6 %collective-permute-start.8 = (bf16[576,128]{1,0:T(8,128)(2,1)S(1)}, bf16[576,128]{1,0:T(8,128)(2,1)S(1)}, u32[]{:S(2)}, u32[]{:S(2)}) collective-permute-start(bf16[576,128]{1,0:T(8,128)(2,1)S(1)} %shard_map.117), channel_id=1, source_target_pairs={{0,1},{1,0},{2,3},{3,2},{4,5},{5,4},{6,7},{7,6},{8,9},{9,8},{10,11... | collective-permute-start | bytes 442376 | tf_op jit(solution)/shard_map/ppermute | solution.py:338
  32.2 1.0 %shard_map.115._.dv_t_ref = bf16[128,1024]{1,0:T(8,128)(2,1)S(1)} custom-call(bf16[1024,2048]{1,0:T(8,128)(2,1)S(1)} %get-tuple-element.25.prob_ref, bf16[128,2048]{1,0:T(8,128)(2,1)S(1)} %get-tuple-element.26.grad_t_ref), custom_call_target="tpu_custom_call" | custom-call | flops 268435456 | bytes 4194304 | tf_op jit(solution)/shard_map/pallas_call | solution.py:325
  33.2 1.1 %shard_map.116 = (bf16[576,128]{1,0:T(8,128)(2,1)S(1)}, bf16[576,128]{1,0:T(8,128)(2,1)S(1)}, f32[576,128]{1,0:T(8,128)S(1)}) custom-call(bf16[128,512]{1,0:T(8,128)(2,1)S(1)} %get-tuple-element.27.own_ref, bf16[128,512]{1,0:T(8,128)(2,1)S(1)} %collective-permute-done.7.far_ref, bf16[2304,512]{1,0:T(8,128)(2,1)S(1)} %copy-done, ...), custom_call_target="tpu_custom_call" | custom-call | flops 452984832 | bytes 3538944 | tf_op jit(solution)/shard_map/pallas_call | solution.py:325
  34.3 2.2 %collective-permute-done.8.arrived_ref = bf16[576,128]{1,0:T(8,128)(2,1)S(1)} collective-permute-done((bf16[576,128]{1,0:T(8,128)(2,1)S(1)}, bf16[576,128]{1,0:T(8,128)(2,1)S(1)}, u32[]{:S(2)}, u32[]{:S(2)}) %collective-permute-start.8) | collective-permute-done | bytes 147488 | tf_op jit(solution)/shard_map/ppermute | solution.py:338
  36.9 2.7 %collective-permute-start.13 = (bf16[576,128]{1,0:T(8,128)(2,1)S(1)}, bf16[576,128]{1,0:T(8,128)(2,1)S(1)}, u32[]{:S(2)}, u32[]{:S(2)}) collective-permute-start(bf16[576,128]{1,0:T(8,128)(2,1)S(1)} %shard_map.118._), channel_id=1, source_target_pairs={{0,2},{1,3},{2,0},{3,1},{4,6},{5,7},{6,4},{7,5},{8,10},{9,11},{10,... | collective-permute-start | bytes 442376 | tf_op jit(solution)/shard_map/ppermute | solution.py:338
  39.5 1.6 %collective-permute-start.14 = (bf16[576,128]{1,0:T(8,128)(2,1)S(1)}, bf16[576,128]{1,0:T(8,128)(2,1)S(1)}, u32[]{:S(2)}, u32[]{:S(2)}) collective-permute-start(bf16[576,128]{1,0:T(8,128)(2,1)S(1)} %get-tuple-element.36), channel_id=1, source_target_pairs={{0,1},{1,0},{2,3},{3,2},{4,5},{5,4},{6,7},{7,6},{8,9},{9,8},{10,11... | collective-permute-start | bytes 442376 | tf_op jit(solution)/shard_map/ppermute | solution.py:338
  41.1 2.0 %shard_map.120 = (f32[288,256]{1,0:T(8,128)}, f32[288,512]{1,0:T(8,128)}, f32[8,128]{1,0:T(8,128)S(1)}) custom-call(bf16[256,1024]{1,0:T(8,128)(2,1)S(1)} %get-tuple-element.24.attn_ref, bf16[128,1024]{1,0:T(8,128)(2,1)S(1)} %shard_map.115._.dv_t_ref, bf16[5376,128]{1,0:T(8,128)(2,1)S(1)} %collective-permute-done.12.got_ref, ...), custom_call_target="tpu_custom_call" | custom-call | tf_op jit(solution)/shard_map/pallas_call | solution.py:325
  43.1 4.2 %collective-permute-done.13.arrived_ref = bf16[576,128]{1,0:T(8,128)(2,1)S(1)} collective-permute-done((bf16[576,128]{1,0:T(8,128)(2,1)S(1)}, bf16[576,128]{1,0:T(8,128)(2,1)S(1)}, u32[]{:S(2)}, u32[]{:S(2)}) %collective-permute-start.13) | collective-permute-done | bytes 147488 | tf_op jit(solution)/shard_map/ppermute | solution.py:338
  47.5 0.7 %shard_map.122 = bf16[576,128]{1,0:T(8,128)(2,1)} custom-call(f32[576,128]{1,0:T(8,128)S(1)} %shard_map.121.own_ref, bf16[576,128]{1,0:T(8,128)(2,1)S(1)} %collective-permute-done.14.refs_0_), custom_call_target="tpu_custom_call" | custom-call | bytes 1179648 | tf_op jit(solution)/shard_map/pallas_call | solution.py:325
  (29 shorter events, 1.9 us)
Async XLA Ops:
  0.6 16.3 %copy-start.3 = (bf16[128,2304]{1,0:T(8,128)(2,1)S(1)}, bf16[128,2304]{1,0:T(8,128)(2,1)}, u32[]{:S(2)}) copy-start(bf16[128,2304]{1,0:T(8,128)(2,1)} %cot_ref.1) | copy-start | bytes 1769476
  4.4 8.6 %collective-permute-start = (bf16[128,768]{1,0:T(8,128)(2,1)}, bf16[128,768]{1,0:T(8,128)(2,1)S(1)}, u32[]{:S(2)}, u32[]{:S(2)}) collective-permute-start(bf16[128,768]{1,0:T(8,128)(2,1)} %get-tuple-element.21.block_ref), channel_id=1, source_target_pairs={{0,8},{4,12},{8,0},{12,4},{16,24},{20,28},{24,16},{28,20},{1,9},{5... | collective-permute-start | bytes 589832 | tf_op jit(solution)/shard_map/ppermute | solution.py:338
  7.4 7.8 %collective-permute-start.1 = (bf16[128,768]{1,0:T(8,128)(2,1)}, bf16[128,768]{1,0:T(8,128)(2,1)S(1)}, u32[]{:S(2)}, u32[]{:S(2)}) collective-permute-start(bf16[128,768]{1,0:T(8,128)(2,1)} %get-tuple-element.22), channel_id=1, source_target_pairs={{0,20},{4,16},{8,28},{12,24},{16,4},{20,0},{24,12},{28,8},{1,21},{... | collective-permute-start | bytes 589832 | tf_op jit(solution)/shard_map/ppermute | solution.py:338
  8.1 11.3 %collective-permute-start.4 = (bf16[128,768]{1,0:T(8,128)(2,1)}, bf16[128,768]{1,0:T(8,128)(2,1)S(1)}, u32[]{:S(2)}, u32[]{:S(2)}) collective-permute-start(bf16[128,768]{1,0:T(8,128)(2,1)} %get-tuple-element.21.block_ref), channel_id=1, source_target_pairs={{0,16},{4,20},{8,24},{12,28},{16,0},{20,4},{24,8},{28,12},{1,17},{... | collective-permute-start | bytes 589832 | tf_op jit(solution)/shard_map/ppermute | solution.py:338
  9.0 10.8 %collective-permute-start.3 = (bf16[128,768]{1,0:T(8,128)(2,1)}, bf16[128,768]{1,0:T(8,128)(2,1)S(1)}, u32[]{:S(2)}, u32[]{:S(2)}) collective-permute-start(bf16[128,768]{1,0:T(8,128)(2,1)} %get-tuple-element.22), channel_id=1, source_target_pairs={{0,12},{4,8},{8,4},{12,0},{16,28},{20,24},{24,20},{28,16},{1,13},{... | collective-permute-start | bytes 589832 | tf_op jit(solution)/shard_map/ppermute | solution.py:338
  9.2 11.8 %collective-permute-start.2 = (bf16[128,768]{1,0:T(8,128)(2,1)}, bf16[128,768]{1,0:T(8,128)(2,1)S(1)}, u32[]{:S(2)}, u32[]{:S(2)}) collective-permute-start(bf16[128,768]{1,0:T(8,128)(2,1)} %get-tuple-element.22), channel_id=1, source_target_pairs={{0,4},{4,0},{8,12},{12,8},{16,20},{20,16},{24,28},{28,24},{1,5},{5... | collective-permute-start | bytes 589832 | tf_op jit(solution)/shard_map/ppermute | solution.py:338
  13.1 10.3 %collective-permute-start.5 = (bf16[128,768]{1,0:T(8,128)(2,1)S(1)}, bf16[128,768]{1,0:T(8,128)(2,1)S(1)}, u32[]{:S(2)}, u32[]{:S(2)}) collective-permute-start(bf16[128,768]{1,0:T(8,128)(2,1)S(1)} %collective-permute-done._.refs_2_), channel_id=1, source_target_pairs={{0,16},{4,20},{8,24},{12,28},{16,0},{20,4},{24,8},{28,12},{1,17},{... | collective-permute-start | bytes 589832 | tf_op jit(solution)/shard_map/ppermute | solution.py:338
  15.2 8.1 %collective-permute-start.6 = (bf16[128,768]{1,0:T(8,128)(2,1)S(1)}, bf16[128,768]{1,0:T(8,128)(2,1)S(1)}, u32[]{:S(2)}, u32[]{:S(2)}) collective-permute-start(bf16[128,768]{1,0:T(8,128)(2,1)S(1)} %collective-permute-done.1.__.refs_5_), channel_id=1, source_target_pairs={{0,8},{4,12},{8,0},{12,4},{16,24},{20,28},{24,16},{28,20},{1,9},{5... | collective-permute-start | bytes 589832 | tf_op jit(solution)/shard_map/ppermute | solution.py:338
  17.0 1.1 %copy-start.4 = (bf16[128,2304]{1,0:T(8,128)(2,1)S(1)}, bf16[128,2304]{1,0:T(8,128)(2,1)}, u32[]{:S(2)}) copy-start(bf16[128,2304]{1,0:T(8,128)(2,1)} %normed_ref.1) | copy-start | bytes 1769476
  18.0 0.9 %copy-start.5 = (bf16[128,768]{1,0:T(8,128)(2,1)S(1)}, bf16[128,768]{1,0:T(8,128)(2,1)}, u32[]{:S(2)}) copy-start(bf16[128,768]{1,0:T(8,128)(2,1)} %get-tuple-element.21.block_ref) | copy-start | bytes 589828
  19.5 17.1 %collective-permute-start.9 = (bf16[2,2,288,128]{3,2,1,0:T(8,128)(2,1)S(1)}, bf16[2,2,288,128]{3,2,1,0:T(8,128)(2,1)S(1)}, u32[]{:S(2)}, u32[]{:S(2)}) collective-permute-start(bf16[2,2,288,128]{3,2,1,0:T(8,128)(2,1)S(1)} %get-tuple-element.31), channel_id=1, source_target_pairs={{0,8},{4,12},{8,0},{12,4},{16,24},{20,28},{24,16},{28,20},{1,9},{5... | collective-permute-start | bytes 884744 | tf_op jit(solution)/shard_map/ppermute | solution.py:338
  19.8 16.8 %collective-permute-start.10 = (bf16[2,2,288,128]{3,2,1,0:T(8,128)(2,1)S(1)}, bf16[2,2,288,128]{3,2,1,0:T(8,128)(2,1)S(1)}, u32[]{:S(2)}, u32[]{:S(2)}) collective-permute-start(bf16[2,2,288,128]{3,2,1,0:T(8,128)(2,1)S(1)} %get-tuple-element.32), channel_id=1, source_target_pairs={{0,16},{4,20},{8,24},{12,28},{16,0},{20,4},{24,8},{28,12},{1,17},{... | collective-permute-start | bytes 884744 | tf_op jit(solution)/shard_map/ppermute | solution.py:338
  21.0 15.6 %collective-permute-start.11 = (bf16[2,2,288,128]{3,2,1,0:T(8,128)(2,1)S(1)}, bf16[2,2,288,128]{3,2,1,0:T(8,128)(2,1)S(1)}, u32[]{:S(2)}, u32[]{:S(2)}) collective-permute-start(bf16[2,2,288,128]{3,2,1,0:T(8,128)(2,1)S(1)} %get-tuple-element.33), channel_id=1, source_target_pairs={{0,24},{4,28},{8,16},{12,20},{16,8},{20,12},{24,0},{28,4},{1,25},{... | collective-permute-start | bytes 884744 | tf_op jit(solution)/shard_map/ppermute | solution.py:338
  23.3 6.7 %copy-start = (bf16[2304,512]{1,0:T(8,128)(2,1)S(1)}, bf16[2304,512]{1,0:T(8,128)(2,1)}, u32[]{:S(2)}) copy-start(bf16[2304,512]{1,0:T(8,128)(2,1)} %wq_ref.3) | copy-start | bytes 7077892
  23.3 6.7 %copy-start.1 = (bf16[2304,256]{1,0:T(8,128)(2,1)S(1)}, bf16[2304,256]{1,0:T(8,128)(2,1)}, u32[]{:S(2)}) copy-start(bf16[2304,256]{1,0:T(8,128)(2,1)} %wk_ref.3) | copy-start | bytes 3538948
  23.3 6.7 %copy-start.2 = (bf16[2304,256]{1,0:T(8,128)(2,1)S(1)}, bf16[2304,256]{1,0:T(8,128)(2,1)}, u32[]{:S(2)}) copy-start(bf16[2304,256]{1,0:T(8,128)(2,1)} %wv_ref.3) | copy-start | bytes 3538948
  28.6 1.4 %collective-permute-start.7 = (bf16[128,512]{1,0:T(8,128)(2,1)S(1)}, bf16[128,512]{1,0:T(8,128)(2,1)S(1)}, u32[]{:S(2)}, u32[]{:S(2)}) collective-permute-start(bf16[128,512]{1,0:T(8,128)(2,1)S(1)} %get-tuple-element.28), channel_id=1, source_target_pairs={{0,4},{4,0},{8,12},{12,8},{16,20},{20,16},{24,28},{28,24},{1,5},{5... | collective-permute-start | bytes 393224 | tf_op jit(solution)/shard_map/ppermute | solution.py:338
  30.6 6.0 %collective-permute-start.8 = (bf16[576,128]{1,0:T(8,128)(2,1)S(1)}, bf16[576,128]{1,0:T(8,128)(2,1)S(1)}, u32[]{:S(2)}, u32[]{:S(2)}) collective-permute-start(bf16[576,128]{1,0:T(8,128)(2,1)S(1)} %shard_map.117), channel_id=1, source_target_pairs={{0,1},{1,0},{2,3},{3,2},{4,5},{5,4},{6,7},{7,6},{8,9},{9,8},{10,11... | collective-permute-start | bytes 442376 | tf_op jit(solution)/shard_map/ppermute | solution.py:338
  36.8 4.3 %collective-permute-start.12 = (bf16[5376,128]{1,0:T(8,128)(2,1)S(1)}, bf16[5376,128]{1,0:T(8,128)(2,1)S(1)}, u32[]{:S(2)}, u32[]{:S(2)}) collective-permute-start(bf16[5376,128]{1,0:T(8,128)(2,1)S(1)} %shard_map.119), channel_id=1, source_target_pairs={{0,4},{4,0},{8,12},{12,8},{16,20},{20,16},{24,28},{28,24},{1,5},{5... | collective-permute-start | bytes 4128776 | tf_op jit(solution)/shard_map/ppermute | solution.py:338
  36.9 10.4 %collective-permute-start.13 = (bf16[576,128]{1,0:T(8,128)(2,1)S(1)}, bf16[576,128]{1,0:T(8,128)(2,1)S(1)}, u32[]{:S(2)}, u32[]{:S(2)}) collective-permute-start(bf16[576,128]{1,0:T(8,128)(2,1)S(1)} %shard_map.118._), channel_id=1, source_target_pairs={{0,2},{1,3},{2,0},{3,1},{4,6},{5,7},{6,4},{7,5},{8,10},{9,11},{10,... | collective-permute-start | bytes 442376 | tf_op jit(solution)/shard_map/ppermute | solution.py:338
  39.5 8.0 %collective-permute-start.14 = (bf16[576,128]{1,0:T(8,128)(2,1)S(1)}, bf16[576,128]{1,0:T(8,128)(2,1)S(1)}, u32[]{:S(2)}, u32[]{:S(2)}) collective-permute-start(bf16[576,128]{1,0:T(8,128)(2,1)S(1)} %get-tuple-element.36), channel_id=1, source_target_pairs={{0,1},{1,0},{2,3},{3,2},{4,5},{5,4},{6,7},{7,6},{8,9},{9,8},{10,11... | collective-permute-start | bytes 442376 | tf_op jit(solution)/shard_map/ppermute | solution.py:338

commit v19 on v18

--- a/solution.py
+++ b/solution.py
@@ -39,12 +39,12 @@
 
 
 def out_grad_kernel(
-    cot_hbm, weight_hbm, q_hbm, k_hbm, v_hbm, same_ref, other_ref, cot_ref, weight_ref, sem
+    cot_hbm, weight_hbm, q_hbm, k_hbm, v_hbm, same_hbm, other_hbm, cot_ref, weight_ref, half_ref, sem
 ):
     core = lax.axis_index("seq") % 2
-    halves = ((other_ref, 1 - core), (same_ref, core))
+    halves = ((other_hbm, 1 - core), (same_hbm, core))
     rows = weight_ref.shape[0] // 2
-    pieces = (sem.shape[0] - 6) // 3
+    pieces = (sem.shape[0] - 10) // 3
     cut = weight_ref.shape[1] // pieces
     model_copies = []
     for piece in range(pieces):
@@ -74,12 +74,22 @@
             plain_copies.append(
                 pltpu.make_async_copy(
                     source.at[:, at(half, cols)],
-                    target.at[:, pl.ds(first, cols)],
+                    half_ref.at[place, :, pl.ds(first, cols)],
                     sem.at[3 * place + which],
                 )
             )
             plain_copies[-1].start()
             first += cols
+    out_copies = []
+    for place, (target, _) in enumerate(halves):
+        for which, cols in enumerate((pl.ds(0, first), pl.ds(first, target.shape[1] - first))):
+            out_copies.append(
+                pltpu.make_async_copy(
+                    half_ref.at[place, :, cols],
+                    target.at[:, cols],
+                    sem.at[6 + 3 * pieces + 2 * place + which],
+                )
+            )
     total = None
     for piece in range(pieces):
         for copy in model_copies[piece]:
@@ -87,13 +97,18 @@
         part = slice(piece * cut, (piece + 1) * cut)
         product = dot_nt(weight_ref[:, part], cot_ref[:, part])
         total = product if total is None else total + product
-    for place, (target, _) in enumerate(halves):
+    for copy in plain_copies:
+        copy.wait()
+    out_copies[0].start()
+    out_copies[2].start()
+    for place in range(2):
         for head in range(rows // HEAD_SIZE):
             row = place * rows + head * HEAD_SIZE
-            target[:, first + head * HEAD_SIZE : first + (head + 1) * HEAD_SIZE] = total[
+            half_ref[place, :, first + head * HEAD_SIZE : first + (head + 1) * HEAD_SIZE] = total[
                 row : row + HEAD_SIZE
             ].astype(jnp.bfloat16)
-    for copy in plain_copies:
+        out_copies[2 * place + 1].start()
+    for copy in out_copies:
         copy.wait()
 
 
@@ -164,15 +179,13 @@
     query_place = lax.broadcasted_iota(jnp.int32, (size, wide), 1) % size
     allowed = key_place <= query_place
 
-    for step in range(steps):
-        span = (step + 1) * size
-        own = slice(step * size, span)
-        lanes = slice(step * wide, (step + 1) * wide)
+    def scored(step):
+        own = slice(step * size, (step + 1) * size)
         score_ref = score_odd_ref if step % 2 else score_even_ref
         queries = jnp.concatenate(
             [gathered_ref[own, h * HEAD_SIZE : (h + 1) * HEAD_SIZE] for h in range(heads)], axis=0
         )
-        query_ref[lanes] = queries
+        query_ref[step * wide : (step + 1) * wide] = queries
         top = None
         for piece in range(step + 1):
             part = slice(piece * size, (piece + 1) * size)
@@ -182,6 +195,17 @@
             score_ref[part] = scores
             largest = jnp.max(scores.reshape(size // 8, 8, wide), axis=0)
             top = largest if top is None else jnp.maximum(top, largest)
+        return top
+
+    next_top = scored(steps - 1)
+    for step in range(steps - 1, -1, -1):
+        span = (step + 1) * size
+        own = slice(step * size, span)
+        lanes = slice(step * wide, (step + 1) * wide)
+        score_ref = score_odd_ref if step % 2 else score_even_ref
+        top = next_top
+        if step:
+            next_top = scored(step - 1)
         top = jnp.max(top, axis=0, keepdims=True)
         total = None
         for piece in range(step + 1):
@@ -318,7 +342,7 @@
 
 
 def kernel_call(
-    body, outs, operands, in_vmem=(), scratch=(), flops=0, moved=0, room=16
+    body, outs, operands, in_vmem=(), scratch=(), flops=0, moved=0, room=16, out_vmem=True
 ):
     vmem = pl.BlockSpec(memory_space=pltpu.VMEM)
     hbm = pl.BlockSpec(memory_space=pltpu.HBM)
@@ -326,7 +350,7 @@
         body,
         out_shape=outs,
         in_specs=[vmem if place in in_vmem else hbm for place in range(len(operands))],
-        out_specs=(vmem,) * len(outs),
+        out_specs=(vmem if out_vmem else hbm,) * len(outs),
         scratch_shapes=list(scratch),
         compiler_params=pltpu.CompilerParams(vmem_limit_bytes=room * 1024 * 1024),
         cost_estimate=pl.CostEstimate(flops=flops, bytes_accessed=moved, transcendentals=0),
@@ -367,11 +391,13 @@
         scratch=(
             pltpu.VMEM(out_cotangent.shape, bf16),
             pltpu.VMEM(output_weight.shape, bf16),
-            pltpu.SemaphoreType.DMA((6 + 3 * pieces,)),
+            pltpu.VMEM((2, rows, packed_cols), bf16),
+            pltpu.SemaphoreType.DMA((10 + 3 * pieces,)),
         ),
         flops=4 * rows * model * q_cols,
         moved=2 * model * (rows + 2 * q_cols),
         room=63,
+        out_vmem=False,
     )
     held = {0: same}
     for apart in range(2, blocks):

time: 48.4 us -> 48 us (level)
  transfers between devices with their start and end apart: 15 -> 15, of which waited for: 6 -> 6; matrix products, arithmetic and copies ran while one was open for 0% -> 0% of each run, Pallas kernels for 22% -> 21%
where the time goes in v19:
time: 48 us; the launch traced here: 47.8 us
  starting transfers between devices  18.7 us (39%)
  Pallas kernels  14.8 us (31%)
  waiting for transfers between devices  11.6 us (24%)
  local copies, waits for them, and re-layouts  2.01 us (4%)
  between operations  0.77 us (2%)
    ppermute x15, starting transfers between devices, swapped(): lax.ppermute(value, axis, [(place, place ^ apart) for place in range(coun...  18.7 us
    pallas_call x11, Pallas kernels, kernel_call(): pl.pallas_call(body, out_shape=outs, in_specs=[vmem if place in in_vmem e...  14.8 us
    ppermute x15, waiting for transfers between devices, swapped(): lax.ppermute(value, axis, [(place, place ^ apart) for place in range(coun...  11.6 us
    unnamed x12, local copies, waits for them, and re-layouts  2.01 us
  transfers between devices with their start and end apart: 15, of which 6 were waited for; matrix products, arithmetic and copies ran while one was open for 0% of the time, Pallas kernels for 21%

profile of v19, /device:TPU:0, one launch (start us, length us, event | category | flops | bytes accessed | tf_op | source)
XLA Modules:
  0.0 47.8 jit_solution(12753767766991809181)
XLA Ops:
  0.6 3.8 %shard_map.112 = (bf16[128,768]{1,0:T(8,128)(2,1)}, bf16[128,768]{1,0:T(8,128)(2,1)}) custom-call(bf16[128,2304]{1,0:T(8,128)(2,1)} %cot_ref.1, bf16[512,2304]{1,0:T(8,128)(2,1)} %weight_hbm.1, bf16[128,512]{1,0:T(8,128)(2,1)} %q_hbm.1, bf16[128,256]{1,0:T(8,128)(2,1)} %k_hbm.1, bf16[128,256]{1,0:T(8,128)(2,1)} %v_hbm.1), custom_call_target="tpu_custom_call" | custom-call | flops 301989888 | bytes 2949120 | tf_op jit(solution)/shard_map/pallas_call | solution.py:349
  4.5 3.0 %collective-permute-start = (bf16[128,768]{1,0:T(8,128)(2,1)}, bf16[128,768]{1,0:T(8,128)(2,1)S(1)}, u32[]{:S(2)}, u32[]{:S(2)}) collective-permute-start(bf16[128,768]{1,0:T(8,128)(2,1)} %get-tuple-element.21.block_ref), channel_id=1, source_target_pairs={{0,8},{4,12},{8,0},{12,4},{16,24},{20,28},{24,16},{28,20},{1,9},{5... | collective-permute-start | bytes 589832 | tf_op jit(solution)/shard_map/ppermute | solution.py:362
  7.5 0.7 %collective-permute-start.1 = (bf16[128,768]{1,0:T(8,128)(2,1)}, bf16[128,768]{1,0:T(8,128)(2,1)S(1)}, u32[]{:S(2)}, u32[]{:S(2)}) collective-permute-start(bf16[128,768]{1,0:T(8,128)(2,1)} %get-tuple-element.22), channel_id=1, source_target_pairs={{0,20},{4,16},{8,28},{12,24},{16,4},{20,0},{24,12},{28,8},{1,21},{... | collective-permute-start | bytes 589832 | tf_op jit(solution)/shard_map/ppermute | solution.py:362
  8.1 0.9 %collective-permute-start.4 = (bf16[128,768]{1,0:T(8,128)(2,1)}, bf16[128,768]{1,0:T(8,128)(2,1)S(1)}, u32[]{:S(2)}, u32[]{:S(2)}) collective-permute-start(bf16[128,768]{1,0:T(8,128)(2,1)} %get-tuple-element.21.block_ref), channel_id=1, source_target_pairs={{0,16},{4,20},{8,24},{12,28},{16,0},{20,4},{24,8},{28,12},{1,17},{... | collective-permute-start | bytes 589832 | tf_op jit(solution)/shard_map/ppermute | solution.py:362
  9.7 3.4 %collective-permute-done._.refs_2_ = bf16[128,768]{1,0:T(8,128)(2,1)S(1)} collective-permute-done((bf16[128,768]{1,0:T(8,128)(2,1)}, bf16[128,768]{1,0:T(8,128)(2,1)S(1)}, u32[]{:S(2)}, u32[]{:S(2)}) %collective-permute-start) | collective-permute-done | bytes 196640 | tf_op jit(solution)/shard_map/ppermute | solution.py:362
  13.1 2.2 %collective-permute-start.5 = (bf16[128,768]{1,0:T(8,128)(2,1)S(1)}, bf16[128,768]{1,0:T(8,128)(2,1)S(1)}, u32[]{:S(2)}, u32[]{:S(2)}) collective-permute-start(bf16[128,768]{1,0:T(8,128)(2,1)S(1)} %collective-permute-done._.refs_2_), channel_id=1, source_target_pairs={{0,16},{4,20},{8,24},{12,28},{16,0},{20,4},{24,8},{28,12},{1,17},{... | collective-permute-start | bytes 589832 | tf_op jit(solution)/shard_map/ppermute | solution.py:362
  15.2 1.7 %collective-permute-start.6 = (bf16[128,768]{1,0:T(8,128)(2,1)S(1)}, bf16[128,768]{1,0:T(8,128)(2,1)S(1)}, u32[]{:S(2)}, u32[]{:S(2)}) collective-permute-start(bf16[128,768]{1,0:T(8,128)(2,1)S(1)} %collective-permute-done.1.__.refs_5_), channel_id=1, source_target_pairs={{0,8},{4,12},{8,0},{12,4},{16,24},{20,28},{24,16},{28,20},{1,9},{5... | collective-permute-start | bytes 589832 | tf_op jit(solution)/shard_map/ppermute | solution.py:362
  17.0 1.1 %copy-done.4 = bf16[128,2304]{1,0:T(8,128)(2,1)S(1)} copy-done((bf16[128,2304]{1,0:T(8,128)(2,1)S(1)}, bf16[128,2304]{1,0:T(8,128)(2,1)}, u32[]{:S(2)}) %copy-start.4) | copy-done | bytes 589848
  18.1 0.9 %copy-done.5 = bf16[128,768]{1,0:T(8,128)(2,1)S(1)} copy-done((bf16[128,768]{1,0:T(8,128)(2,1)S(1)}, bf16[128,768]{1,0:T(8,128)(2,1)}, u32[]{:S(2)}) %copy-start.5) | copy-done | bytes 196632
  19.0 0.5 %shard_map.113 = (bf16[2,2,288,128]{3,2,1,0:T(8,128)(2,1)S(1)}, bf16[2,2,288,128]{3,2,1,0:T(8,128)(2,1)S(1)}, bf16[2,2,288,128]{3,2,1,0:T(8,128)(2,1)S(1)}, bf16...) custom-call(bf16[128,2304]{1,0:T(8,128)(2,1)S(1)} %copy-done.4, bf16[128,2304]{1,0:T(8,128)(2,1)S(1)} %copy-done.3, ...), custom_call_target="tpu_custom_call" | custom-call | bytes 2359296 | tf_op jit(solution)/shard_map/pallas_call | solution.py:349
  19.8 1.1 %collective-permute-start.10 = (bf16[2,2,288,128]{3,2,1,0:T(8,128)(2,1)S(1)}, bf16[2,2,288,128]{3,2,1,0:T(8,128)(2,1)S(1)}, u32[]{:S(2)}, u32[]{:S(2)}) collective-permute-start(bf16[2,2,288,128]{3,2,1,0:T(8,128)(2,1)S(1)} %get-tuple-element.32), channel_id=1, source_target_pairs={{0,16},{4,20},{8,24},{12,28},{16,0},{20,4},{24,8},{28,12},{1,17},{... | collective-permute-start | bytes 884744 | tf_op jit(solution)/shard_map/ppermute | solution.py:362
  21.0 2.1 %collective-permute-start.11 = (bf16[2,2,288,128]{3,2,1,0:T(8,128)(2,1)S(1)}, bf16[2,2,288,128]{3,2,1,0:T(8,128)(2,1)S(1)}, u32[]{:S(2)}, u32[]{:S(2)}) collective-permute-start(bf16[2,2,288,128]{3,2,1,0:T(8,128)(2,1)S(1)} %get-tuple-element.33), channel_id=1, source_target_pairs={{0,24},{4,28},{8,16},{12,20},{16,8},{20,12},{24,0},{28,4},{1,25},{... | collective-permute-start | bytes 884744 | tf_op jit(solution)/shard_map/ppermute | solution.py:362
  23.4 4.9 %shard_map.114 = (bf16[128,512]{1,0:T(8,128)(2,1)S(1)}, bf16[128,512]{1,0:T(8,128)(2,1)S(1)}, bf16[256,1024]{1,0:T(8,128)(2,1)S(1)}, bf16[1024,2048]{1,0:T(8,128)(2,1)S(1)}, bf16[128,2048]{1,0:T(8,128)(2,1)S(1)}) custom-call(bf16[128,768]{1,0:T(8,128)(2,1)S(1)} %get-tuple-element.23.refs_0_, bf16[128,768]{1,0:T(8,128)(2,1)S(1)} %collective-permute-done.2.refs_1_, ...), custom_call_target="tpu_custom_call" | custom-call | flops 2147483648 | bytes 1572864 | tf_op jit(solution)/shard_map/pallas_call | solution.py:349
  28.4 1.3 %collective-permute-done.7.far_ref = bf16[128,512]{1,0:T(8,128)(2,1)S(1)} collective-permute-done((bf16[128,512]{1,0:T(8,128)(2,1)S(1)}, bf16[128,512]{1,0:T(8,128)(2,1)S(1)}, u32[]{:S(2)}, u32[]{:S(2)}) %collective-permute-start.7) | collective-permute-done | bytes 131104 | tf_op jit(solution)/shard_map/ppermute | solution.py:362
  29.7 0.5 %shard_map.117 = bf16[576,128]{1,0:T(8,128)(2,1)S(1)} custom-call(bf16[128,512]{1,0:T(8,128)(2,1)S(1)} %get-tuple-element.27.own_ref, bf16[128,512]{1,0:T(8,128)(2,1)S(1)} %collective-permute-done.7.far_ref, bf16[2304,512]{1,0:T(8,128)(2,1)S(1)} %copy-done, bf16[2304,256]{1,0:T(8,128)(2,1)S(1)} %copy-done.1, bf16[2304,256]{1,0:T(8,128)(2,1)S(1)} %copy-done.2), custom_call_target="tpu_custom_call" | custom-call | flops 150994944 | bytes 1179648 | tf_op jit(solution)/shard_map/pallas_call | solution.py:349
  30.2 1.6 %collective-permute-start.8 = (bf16[576,128]{1,0:T(8,128)(2,1)S(1)}, bf16[576,128]{1,0:T(8,128)(2,1)S(1)}, u32[]{:S(2)}, u32[]{:S(2)}) collective-permute-start(bf16[576,128]{1,0:T(8,128)(2,1)S(1)} %shard_map.117), channel_id=1, source_target_pairs={{0,1},{1,0},{2,3},{3,2},{4,5},{5,4},{6,7},{7,6},{8,9},{9,8},{10,11... | collective-permute-start | bytes 442376 | tf_op jit(solution)/shard_map/ppermute | solution.py:362
  31.9 1.0 %shard_map.115._.dv_t_ref = bf16[128,1024]{1,0:T(8,128)(2,1)S(1)} custom-call(bf16[1024,2048]{1,0:T(8,128)(2,1)S(1)} %get-tuple-element.25.prob_ref, bf16[128,2048]{1,0:T(8,128)(2,1)S(1)} %get-tuple-element.26.grad_t_ref), custom_call_target="tpu_custom_call" | custom-call | flops 268435456 | bytes 4194304 | tf_op jit(solution)/shard_map/pallas_call | solution.py:349
  32.9 1.1 %shard_map.116 = (bf16[576,128]{1,0:T(8,128)(2,1)S(1)}, bf16[576,128]{1,0:T(8,128)(2,1)S(1)}, f32[576,128]{1,0:T(8,128)S(1)}) custom-call(bf16[128,512]{1,0:T(8,128)(2,1)S(1)} %get-tuple-element.27.own_ref, bf16[128,512]{1,0:T(8,128)(2,1)S(1)} %collective-permute-done.7.far_ref, bf16[2304,512]{1,0:T(8,128)(2,1)S(1)} %copy-done, ...), custom_call_target="tpu_custom_call" | custom-call | flops 452984832 | bytes 3538944 | tf_op jit(solution)/shard_map/pallas_call | solution.py:349
  34.0 2.2 %collective-permute-done.8.arrived_ref = bf16[576,128]{1,0:T(8,128)(2,1)S(1)} collective-permute-done((bf16[576,128]{1,0:T(8,128)(2,1)S(1)}, bf16[576,128]{1,0:T(8,128)(2,1)S(1)}, u32[]{:S(2)}, u32[]{:S(2)}) %collective-permute-start.8) | collective-permute-done | bytes 147488 | tf_op jit(solution)/shard_map/ppermute | solution.py:362
  36.5 2.6 %collective-permute-start.13 = (bf16[576,128]{1,0:T(8,128)(2,1)S(1)}, bf16[576,128]{1,0:T(8,128)(2,1)S(1)}, u32[]{:S(2)}, u32[]{:S(2)}) collective-permute-start(bf16[576,128]{1,0:T(8,128)(2,1)S(1)} %shard_map.118._), channel_id=1, source_target_pairs={{0,2},{1,3},{2,0},{3,1},{4,6},{5,7},{6,4},{7,5},{8,10},{9,11},{10,... | collective-permute-start | bytes 442376 | tf_op jit(solution)/shard_map/ppermute | solution.py:362
  39.2 1.6 %collective-permute-start.14 = (bf16[576,128]{1,0:T(8,128)(2,1)S(1)}, bf16[576,128]{1,0:T(8,128)(2,1)S(1)}, u32[]{:S(2)}, u32[]{:S(2)}) collective-permute-start(bf16[576,128]{1,0:T(8,128)(2,1)S(1)} %get-tuple-element.36), channel_id=1, source_target_pairs={{0,1},{1,0},{2,3},{3,2},{4,5},{5,4},{6,7},{7,6},{8,9},{9,8},{10,11... | collective-permute-start | bytes 442376 | tf_op jit(solution)/shard_map/ppermute | solution.py:362
  40.8 2.0 %shard_map.120 = (f32[288,256]{1,0:T(8,128)}, f32[288,512]{1,0:T(8,128)}, f32[8,128]{1,0:T(8,128)S(1)}) custom-call(bf16[256,1024]{1,0:T(8,128)(2,1)S(1)} %get-tuple-element.24.attn_ref, bf16[128,1024]{1,0:T(8,128)(2,1)S(1)} %shard_map.115._.dv_t_ref, bf16[5376,128]{1,0:T(8,128)(2,1)S(1)} %collective-permute-done.12.got_ref, ...), custom_call_target="tpu_custom_call" | custom-call | tf_op jit(solution)/shard_map/pallas_call | solution.py:349
  42.8 4.2 %collective-permute-done.13.arrived_ref = bf16[576,128]{1,0:T(8,128)(2,1)S(1)} collective-permute-done((bf16[576,128]{1,0:T(8,128)(2,1)S(1)}, bf16[576,128]{1,0:T(8,128)(2,1)S(1)}, u32[]{:S(2)}, u32[]{:S(2)}) %collective-permute-start.13) | collective-permute-done | bytes 147488 | tf_op jit(solution)/shard_map/ppermute | solution.py:362
  47.1 0.7 %shard_map.122 = bf16[576,128]{1,0:T(8,128)(2,1)} custom-call(f32[576,128]{1,0:T(8,128)S(1)} %shard_map.121.own_ref, bf16[576,128]{1,0:T(8,128)(2,1)S(1)} %collective-permute-done.14.refs_0_), custom_call_target="tpu_custom_call" | custom-call | bytes 1179648 | tf_op jit(solution)/shard_map/pallas_call | solution.py:349
  (29 shorter events, 1.9 us)
Async XLA Ops:
  0.6 16.4 %copy-start.3 = (bf16[128,2304]{1,0:T(8,128)(2,1)S(1)}, bf16[128,2304]{1,0:T(8,128)(2,1)}, u32[]{:S(2)}) copy-start(bf16[128,2304]{1,0:T(8,128)(2,1)} %cot_ref.1) | copy-start | bytes 1769476
  4.5 8.6 %collective-permute-start = (bf16[128,768]{1,0:T(8,128)(2,1)}, bf16[128,768]{1,0:T(8,128)(2,1)S(1)}, u32[]{:S(2)}, u32[]{:S(2)}) collective-permute-start(bf16[128,768]{1,0:T(8,128)(2,1)} %get-tuple-element.21.block_ref), channel_id=1, source_target_pairs={{0,8},{4,12},{8,0},{12,4},{16,24},{20,28},{24,16},{28,20},{1,9},{5... | collective-permute-start | bytes 589832 | tf_op jit(solution)/shard_map/ppermute | solution.py:362
  7.5 7.8 %collective-permute-start.1 = (bf16[128,768]{1,0:T(8,128)(2,1)}, bf16[128,768]{1,0:T(8,128)(2,1)S(1)}, u32[]{:S(2)}, u32[]{:S(2)}) collective-permute-start(bf16[128,768]{1,0:T(8,128)(2,1)} %get-tuple-element.22), channel_id=1, source_target_pairs={{0,20},{4,16},{8,28},{12,24},{16,4},{20,0},{24,12},{28,8},{1,21},{... | collective-permute-start | bytes 589832 | tf_op jit(solution)/shard_map/ppermute | solution.py:362
  8.1 11.3 %collective-permute-start.4 = (bf16[128,768]{1,0:T(8,128)(2,1)}, bf16[128,768]{1,0:T(8,128)(2,1)S(1)}, u32[]{:S(2)}, u32[]{:S(2)}) collective-permute-start(bf16[128,768]{1,0:T(8,128)(2,1)} %get-tuple-element.21.block_ref), channel_id=1, source_target_pairs={{0,16},{4,20},{8,24},{12,28},{16,0},{20,4},{24,8},{28,12},{1,17},{... | collective-permute-start | bytes 589832 | tf_op jit(solution)/shard_map/ppermute | solution.py:362
  9.0 10.8 %collective-permute-start.3 = (bf16[128,768]{1,0:T(8,128)(2,1)}, bf16[128,768]{1,0:T(8,128)(2,1)S(1)}, u32[]{:S(2)}, u32[]{:S(2)}) collective-permute-start(bf16[128,768]{1,0:T(8,128)(2,1)} %get-tuple-element.22), channel_id=1, source_target_pairs={{0,12},{4,8},{8,4},{12,0},{16,28},{20,24},{24,20},{28,16},{1,13},{... | collective-permute-start | bytes 589832 | tf_op jit(solution)/shard_map/ppermute | solution.py:362
  9.2 11.8 %collective-permute-start.2 = (bf16[128,768]{1,0:T(8,128)(2,1)}, bf16[128,768]{1,0:T(8,128)(2,1)S(1)}, u32[]{:S(2)}, u32[]{:S(2)}) collective-permute-start(bf16[128,768]{1,0:T(8,128)(2,1)} %get-tuple-element.22), channel_id=1, source_target_pairs={{0,4},{4,0},{8,12},{12,8},{16,20},{20,16},{24,28},{28,24},{1,5},{5... | collective-permute-start | bytes 589832 | tf_op jit(solution)/shard_map/ppermute | solution.py:362
  13.1 10.3 %collective-permute-start.5 = (bf16[128,768]{1,0:T(8,128)(2,1)S(1)}, bf16[128,768]{1,0:T(8,128)(2,1)S(1)}, u32[]{:S(2)}, u32[]{:S(2)}) collective-permute-start(bf16[128,768]{1,0:T(8,128)(2,1)S(1)} %collective-permute-done._.refs_2_), channel_id=1, source_target_pairs={{0,16},{4,20},{8,24},{12,28},{16,0},{20,4},{24,8},{28,12},{1,17},{... | collective-permute-start | bytes 589832 | tf_op jit(solution)/shard_map/ppermute | solution.py:362
  15.2 8.1 %collective-permute-start.6 = (bf16[128,768]{1,0:T(8,128)(2,1)S(1)}, bf16[128,768]{1,0:T(8,128)(2,1)S(1)}, u32[]{:S(2)}, u32[]{:S(2)}) collective-permute-start(bf16[128,768]{1,0:T(8,128)(2,1)S(1)} %collective-permute-done.1.__.refs_5_), channel_id=1, source_target_pairs={{0,8},{4,12},{8,0},{12,4},{16,24},{20,28},{24,16},{28,20},{1,9},{5... | collective-permute-start | bytes 589832 | tf_op jit(solution)/shard_map/ppermute | solution.py:362
  17.0 1.1 %copy-start.4 = (bf16[128,2304]{1,0:T(8,128)(2,1)S(1)}, bf16[128,2304]{1,0:T(8,128)(2,1)}, u32[]{:S(2)}) copy-start(bf16[128,2304]{1,0:T(8,128)(2,1)} %normed_ref.1) | copy-start | bytes 1769476
  18.1 0.9 %copy-start.5 = (bf16[128,768]{1,0:T(8,128)(2,1)S(1)}, bf16[128,768]{1,0:T(8,128)(2,1)}, u32[]{:S(2)}) copy-start(bf16[128,768]{1,0:T(8,128)(2,1)} %get-tuple-element.21.block_ref) | copy-start | bytes 589828
  19.5 16.8 %collective-permute-start.9 = (bf16[2,2,288,128]{3,2,1,0:T(8,128)(2,1)S(1)}, bf16[2,2,288,128]{3,2,1,0:T(8,128)(2,1)S(1)}, u32[]{:S(2)}, u32[]{:S(2)}) collective-permute-start(bf16[2,2,288,128]{3,2,1,0:T(8,128)(2,1)S(1)} %get-tuple-element.31), channel_id=1, source_target_pairs={{0,8},{4,12},{8,0},{12,4},{16,24},{20,28},{24,16},{28,20},{1,9},{5... | collective-permute-start | bytes 884744 | tf_op jit(solution)/shard_map/ppermute | solution.py:362
  19.8 16.4 %collective-permute-start.10 = (bf16[2,2,288,128]{3,2,1,0:T(8,128)(2,1)S(1)}, bf16[2,2,288,128]{3,2,1,0:T(8,128)(2,1)S(1)}, u32[]{:S(2)}, u32[]{:S(2)}) collective-permute-start(bf16[2,2,288,128]{3,2,1,0:T(8,128)(2,1)S(1)} %get-tuple-element.32), channel_id=1, source_target_pairs={{0,16},{4,20},{8,24},{12,28},{16,0},{20,4},{24,8},{28,12},{1,17},{... | collective-permute-start | bytes 884744 | tf_op jit(solution)/shard_map/ppermute | solution.py:362
  21.0 15.3 %collective-permute-start.11 = (bf16[2,2,288,128]{3,2,1,0:T(8,128)(2,1)S(1)}, bf16[2,2,288,128]{3,2,1,0:T(8,128)(2,1)S(1)}, u32[]{:S(2)}, u32[]{:S(2)}) collective-permute-start(bf16[2,2,288,128]{3,2,1,0:T(8,128)(2,1)S(1)} %get-tuple-element.33), channel_id=1, source_target_pairs={{0,24},{4,28},{8,16},{12,20},{16,8},{20,12},{24,0},{28,4},{1,25},{... | collective-permute-start | bytes 884744 | tf_op jit(solution)/shard_map/ppermute | solution.py:362
  23.4 6.3 %copy-start = (bf16[2304,512]{1,0:T(8,128)(2,1)S(1)}, bf16[2304,512]{1,0:T(8,128)(2,1)}, u32[]{:S(2)}) copy-start(bf16[2304,512]{1,0:T(8,128)(2,1)} %wq_ref.3) | copy-start | bytes 7077892
  23.4 6.3 %copy-start.1 = (bf16[2304,256]{1,0:T(8,128)(2,1)S(1)}, bf16[2304,256]{1,0:T(8,128)(2,1)}, u32[]{:S(2)}) copy-start(bf16[2304,256]{1,0:T(8,128)(2,1)} %wk_ref.3) | copy-start | bytes 3538948
  23.4 6.3 %copy-start.2 = (bf16[2304,256]{1,0:T(8,128)(2,1)S(1)}, bf16[2304,256]{1,0:T(8,128)(2,1)}, u32[]{:S(2)}) copy-start(bf16[2304,256]{1,0:T(8,128)(2,1)} %wv_ref.3) | copy-start | bytes 3538948
  28.3 1.4 %collective-permute-start.7 = (bf16[128,512]{1,0:T(8,128)(2,1)S(1)}, bf16[128,512]{1,0:T(8,128)(2,1)S(1)}, u32[]{:S(2)}, u32[]{:S(2)}) collective-permute-start(bf16[128,512]{1,0:T(8,128)(2,1)S(1)} %get-tuple-element.28), channel_id=1, source_target_pairs={{0,4},{4,0},{8,12},{12,8},{16,20},{20,16},{24,28},{28,24},{1,5},{5... | collective-permute-start | bytes 393224 | tf_op jit(solution)/shard_map/ppermute | solution.py:362
  30.2 6.0 %collective-permute-start.8 = (bf16[576,128]{1,0:T(8,128)(2,1)S(1)}, bf16[576,128]{1,0:T(8,128)(2,1)S(1)}, u32[]{:S(2)}, u32[]{:S(2)}) collective-permute-start(bf16[576,128]{1,0:T(8,128)(2,1)S(1)} %shard_map.117), channel_id=1, source_target_pairs={{0,1},{1,0},{2,3},{3,2},{4,5},{5,4},{6,7},{7,6},{8,9},{9,8},{10,11... | collective-permute-start | bytes 442376 | tf_op jit(solution)/shard_map/ppermute | solution.py:362
  36.5 4.3 %collective-permute-start.12 = (bf16[5376,128]{1,0:T(8,128)(2,1)S(1)}, bf16[5376,128]{1,0:T(8,128)(2,1)S(1)}, u32[]{:S(2)}, u32[]{:S(2)}) collective-permute-start(bf16[5376,128]{1,0:T(8,128)(2,1)S(1)} %shard_map.119), channel_id=1, source_target_pairs={{0,4},{4,0},{8,12},{12,8},{16,20},{20,16},{24,28},{28,24},{1,5},{5... | collective-permute-start | bytes 4128776 | tf_op jit(solution)/shard_map/ppermute | solution.py:362
  36.5 10.4 %collective-permute-start.13 = (bf16[576,128]{1,0:T(8,128)(2,1)S(1)}, bf16[576,128]{1,0:T(8,128)(2,1)S(1)}, u32[]{:S(2)}, u32[]{:S(2)}) collective-permute-start(bf16[576,128]{1,0:T(8,128)(2,1)S(1)} %shard_map.118._), channel_id=1, source_target_pairs={{0,2},{1,3},{2,0},{3,1},{4,6},{5,7},{6,4},{7,5},{8,10},{9,11},{10,... | collective-permute-start | bytes 442376 | tf_op jit(solution)/shard_map/ppermute | solution.py:362
  39.2 8.0 %collective-permute-start.14 = (bf16[576,128]{1,0:T(8,128)(2,1)S(1)}, bf16[576,128]{1,0:T(8,128)(2,1)S(1)}, u32[]{:S(2)}, u32[]{:S(2)}) collective-permute-start(bf16[576,128]{1,0:T(8,128)(2,1)S(1)} %get-tuple-element.36), channel_id=1, source_target_pairs={{0,1},{1,0},{2,3},{3,2},{4,5},{5,4},{6,7},{7,6},{8,9},{9,8},{10,11... | collective-permute-start | bytes 442376 | tf_op jit(solution)/shard_map/ppermute | solution.py:362

commit v20 on v18

--- a/solution.py
+++ b/solution.py
@@ -164,15 +164,13 @@
     query_place = lax.broadcasted_iota(jnp.int32, (size, wide), 1) % size
     allowed = key_place <= query_place
 
-    for step in range(steps):
-        span = (step + 1) * size
-        own = slice(step * size, span)
-        lanes = slice(step * wide, (step + 1) * wide)
+    def scored(step):
+        own = slice(step * size, (step + 1) * size)
         score_ref = score_odd_ref if step % 2 else score_even_ref
         queries = jnp.concatenate(
             [gathered_ref[own, h * HEAD_SIZE : (h + 1) * HEAD_SIZE] for h in range(heads)], axis=0
         )
-        query_ref[lanes] = queries
+        query_ref[step * wide : (step + 1) * wide] = queries
         top = None
         for piece in range(step + 1):
             part = slice(piece * size, (piece + 1) * size)
@@ -182,6 +180,17 @@
             score_ref[part] = scores
             largest = jnp.max(scores.reshape(size // 8, 8, wide), axis=0)
             top = largest if top is None else jnp.maximum(top, largest)
+        return top
+
+    next_top = scored(steps - 1)
+    for step in range(steps - 1, -1, -1):
+        span = (step + 1) * size
+        own = slice(step * size, span)
+        lanes = slice(step * wide, (step + 1) * wide)
+        score_ref = score_odd_ref if step % 2 else score_even_ref
+        top = next_top
+        if step:
+            next_top = scored(step - 1)
         top = jnp.max(top, axis=0, keepdims=True)
         total = None
         for piece in range(step + 1):
@@ -328,7 +337,7 @@
         in_specs=[vmem if place in in_vmem else hbm for place in range(len(operands))],
         out_specs=(vmem,) * len(outs),
         scratch_shapes=list(scratch),
-        compiler_params=pltpu.CompilerParams(vmem_limit_bytes=room * 1024 * 1024),
+        compiler_params=pltpu.CompilerParams(vmem_limit_bytes=int(room * 1024 * 1024)),
         cost_estimate=pl.CostEstimate(flops=flops, bytes_accessed=moved, transcendentals=0),
     )(*operands)
 
@@ -358,7 +367,7 @@
     kv_cols = HEAD_SIZE
     wide = 2 * QUERIES_PER_KEY * rows
     packed_cols = 2 * q_cols + 2 * kv_cols
-    pieces = 3 if model % (6 * HEAD_SIZE) == 0 else 1
+    pieces = model // (2 * HEAD_SIZE) if model % (2 * HEAD_SIZE) == 0 else 1
     shape = jax.ShapeDtypeStruct
     same, other = kernel_call(
         out_grad_kernel,
@@ -371,7 +380,7 @@
         ),
         flops=4 * rows * model * q_cols,
         moved=2 * model * (rows + 2 * q_cols),
-        room=63,
+        room=62,
     )
     held = {0: same}
     for apart in range(2, blocks):

time: 48.4 us -> 48.2 us (level)
  waiting for transfers between devices: 11.6 us -> 12.8 us
  local copies, waits for them, and re-layouts: 2.01 us -> 0.95 us
    ppermute x15, waiting for transfers between devices: 11.6 us -> 12.8 us  [swapped(): lax.ppermute(value, axis, [(place, place ^ apart) for place in range(coun...]
    unnamed x12, local copies, waits for them, and re-layouts: 2.01 us -> 0.95 us
  transfers between devices with their start and end apart: 15 -> 15, of which waited for: 6 -> 7; matrix products, arithmetic and copies ran while one was open for 0% -> 0% of each run, Pallas kernels for 22% -> 21%
where the time goes in v20:
time: 48.2 us; the launch traced here: 48.1 us
  starting transfers between devices  18.6 us (39%)
  Pallas kernels  15 us (31%)
  waiting for transfers between devices  12.8 us (27%)
  local copies, waits for them, and re-layouts  0.95 us (2%)
  between operations  0.77 us (2%)
    ppermute x15, starting transfers between devices, swapped(): lax.ppermute(value, axis, [(place, place ^ apart) for place in range(coun...  18.6 us
    pallas_call x11, Pallas kernels, kernel_call(): pl.pallas_call(body, out_shape=outs, in_specs=[vmem if place in in_vmem e...  15 us
    ppermute x15, waiting for transfers between devices, swapped(): lax.ppermute(value, axis, [(place, place ^ apart) for place in range(coun...  12.8 us
  transfers between devices with their start and end apart: 15, of which 7 were waited for; matrix products, arithmetic and copies ran while one was open for 0% of the time, Pallas kernels for 21%

profile of v20, /device:TPU:0, one launch (start us, length us, event | category | flops | bytes accessed | tf_op | source)
XLA Modules:
  0.0 48.1 jit_solution(13152574125351252023)
XLA Ops:
  0.7 4.0 %shard_map.112 = (bf16[128,768]{1,0:T(8,128)(2,1)}, bf16[128,768]{1,0:T(8,128)(2,1)}) custom-call(bf16[128,2304]{1,0:T(8,128)(2,1)} %cot_ref.1, bf16[512,2304]{1,0:T(8,128)(2,1)} %weight_hbm.1, bf16[128,512]{1,0:T(8,128)(2,1)} %q_hbm.1, bf16[128,256]{1,0:T(8,128)(2,1)} %k_hbm.1, bf16[128,256]{1,0:T(8,128)(2,1)} %v_hbm.1), custom_call_target="tpu_custom_call" | custom-call | flops 301989888 | bytes 2949120 | tf_op jit(solution)/shard_map/pallas_call | solution.py:334
  4.7 3.0 %collective-permute-start = (bf16[128,768]{1,0:T(8,128)(2,1)}, bf16[128,768]{1,0:T(8,128)(2,1)S(1)}, u32[]{:S(2)}, u32[]{:S(2)}) collective-permute-start(bf16[128,768]{1,0:T(8,128)(2,1)} %get-tuple-element.21.block_ref), channel_id=1, source_target_pairs={{0,8},{4,12},{8,0},{12,4},{16,24},{20,28},{24,16},{28,20},{1,9},{5... | collective-permute-start | bytes 589832 | tf_op jit(solution)/shard_map/ppermute | solution.py:347
  7.7 0.7 %collective-permute-start.1 = (bf16[128,768]{1,0:T(8,128)(2,1)}, bf16[128,768]{1,0:T(8,128)(2,1)S(1)}, u32[]{:S(2)}, u32[]{:S(2)}) collective-permute-start(bf16[128,768]{1,0:T(8,128)(2,1)} %get-tuple-element.22), channel_id=1, source_target_pairs={{0,20},{4,16},{8,28},{12,24},{16,4},{20,0},{24,12},{28,8},{1,21},{... | collective-permute-start | bytes 589832 | tf_op jit(solution)/shard_map/ppermute | solution.py:347
  8.4 0.9 %collective-permute-start.4 = (bf16[128,768]{1,0:T(8,128)(2,1)}, bf16[128,768]{1,0:T(8,128)(2,1)S(1)}, u32[]{:S(2)}, u32[]{:S(2)}) collective-permute-start(bf16[128,768]{1,0:T(8,128)(2,1)} %get-tuple-element.21.block_ref), channel_id=1, source_target_pairs={{0,16},{4,20},{8,24},{12,28},{16,0},{20,4},{24,8},{28,12},{1,17},{... | collective-permute-start | bytes 589832 | tf_op jit(solution)/shard_map/ppermute | solution.py:347
  9.9 3.4 %collective-permute-done._.refs_2_ = bf16[128,768]{1,0:T(8,128)(2,1)S(1)} collective-permute-done((bf16[128,768]{1,0:T(8,128)(2,1)}, bf16[128,768]{1,0:T(8,128)(2,1)S(1)}, u32[]{:S(2)}, u32[]{:S(2)}) %collective-permute-start) | collective-permute-done | bytes 196640 | tf_op jit(solution)/shard_map/ppermute | solution.py:347
  13.3 2.2 %collective-permute-start.5 = (bf16[128,768]{1,0:T(8,128)(2,1)S(1)}, bf16[128,768]{1,0:T(8,128)(2,1)S(1)}, u32[]{:S(2)}, u32[]{:S(2)}) collective-permute-start(bf16[128,768]{1,0:T(8,128)(2,1)S(1)} %collective-permute-done._.refs_2_), channel_id=1, source_target_pairs={{0,16},{4,20},{8,24},{12,28},{16,0},{20,4},{24,8},{28,12},{1,17},{... | collective-permute-start | bytes 589832 | tf_op jit(solution)/shard_map/ppermute | solution.py:347
  15.5 1.7 %collective-permute-start.6 = (bf16[128,768]{1,0:T(8,128)(2,1)S(1)}, bf16[128,768]{1,0:T(8,128)(2,1)S(1)}, u32[]{:S(2)}, u32[]{:S(2)}) collective-permute-start(bf16[128,768]{1,0:T(8,128)(2,1)S(1)} %collective-permute-done.1.__.refs_5_), channel_id=1, source_target_pairs={{0,8},{4,12},{8,0},{12,4},{16,24},{20,28},{24,16},{28,20},{1,9},{5... | collective-permute-start | bytes 589832 | tf_op jit(solution)/shard_map/ppermute | solution.py:347
  17.2 0.9 %copy-done.5 = bf16[128,768]{1,0:T(8,128)(2,1)S(1)} copy-done((bf16[128,768]{1,0:T(8,128)(2,1)S(1)}, bf16[128,768]{1,0:T(8,128)(2,1)}, u32[]{:S(2)}) %copy-start.5) | copy-done | bytes 196632
  18.6 0.7 %collective-permute-done.4.refs_4_ = bf16[128,768]{1,0:T(8,128)(2,1)S(1)} collective-permute-done((bf16[128,768]{1,0:T(8,128)(2,1)}, bf16[128,768]{1,0:T(8,128)(2,1)S(1)}, u32[]{:S(2)}, u32[]{:S(2)}) %collective-permute-start.4) | collective-permute-done | bytes 196640 | tf_op jit(solution)/shard_map/ppermute | solution.py:347
  19.9 1.0 %collective-permute-start.10 = (bf16[2,2,288,128]{3,2,1,0:T(8,128)(2,1)S(1)}, bf16[2,2,288,128]{3,2,1,0:T(8,128)(2,1)S(1)}, u32[]{:S(2)}, u32[]{:S(2)}) collective-permute-start(bf16[2,2,288,128]{3,2,1,0:T(8,128)(2,1)S(1)} %get-tuple-element.32), channel_id=1, source_target_pairs={{0,16},{4,20},{8,24},{12,28},{16,0},{20,4},{24,8},{28,12},{1,17},{... | collective-permute-start | bytes 884744 | tf_op jit(solution)/shard_map/ppermute | solution.py:347
  20.9 2.0 %collective-permute-start.11 = (bf16[2,2,288,128]{3,2,1,0:T(8,128)(2,1)S(1)}, bf16[2,2,288,128]{3,2,1,0:T(8,128)(2,1)S(1)}, u32[]{:S(2)}, u32[]{:S(2)}) collective-permute-start(bf16[2,2,288,128]{3,2,1,0:T(8,128)(2,1)S(1)} %get-tuple-element.33), channel_id=1, source_target_pairs={{0,24},{4,28},{8,16},{12,20},{16,8},{20,12},{24,0},{28,4},{1,25},{... | collective-permute-start | bytes 884744 | tf_op jit(solution)/shard_map/ppermute | solution.py:347
  22.9 0.7 %collective-permute-done.5.refs_6_ = bf16[128,768]{1,0:T(8,128)(2,1)S(1)} collective-permute-done((bf16[128,768]{1,0:T(8,128)(2,1)S(1)}, bf16[128,768]{1,0:T(8,128)(2,1)S(1)}, u32[]{:S(2)}, u32[]{:S(2)}) %collective-permute-start.5) | collective-permute-done | bytes 196640 | tf_op jit(solution)/shard_map/ppermute | solution.py:347
  23.6 4.9 %shard_map.114 = (bf16[128,512]{1,0:T(8,128)(2,1)S(1)}, bf16[128,512]{1,0:T(8,128)(2,1)S(1)}, bf16[256,1024]{1,0:T(8,128)(2,1)S(1)}, bf16[1024,2048]{1,0:T(8,128)(2,1)S(1)}, bf16[128,2048]{1,0:T(8,128)(2,1)S(1)}) custom-call(bf16[128,768]{1,0:T(8,128)(2,1)S(1)} %get-tuple-element.23.refs_0_, bf16[128,768]{1,0:T(8,128)(2,1)S(1)} %collective-permute-done.2.refs_1_, ...), custom_call_target="tpu_custom_call" | custom-call | flops 2147483648 | bytes 1572864 | tf_op jit(solution)/shard_map/pallas_call | solution.py:334
  28.6 1.3 %collective-permute-done.7.far_ref = bf16[128,512]{1,0:T(8,128)(2,1)S(1)} collective-permute-done((bf16[128,512]{1,0:T(8,128)(2,1)S(1)}, bf16[128,512]{1,0:T(8,128)(2,1)S(1)}, u32[]{:S(2)}, u32[]{:S(2)}) %collective-permute-start.7) | collective-permute-done | bytes 131104 | tf_op jit(solution)/shard_map/ppermute | solution.py:347
  29.9 0.5 %shard_map.117 = bf16[576,128]{1,0:T(8,128)(2,1)S(1)} custom-call(bf16[128,512]{1,0:T(8,128)(2,1)S(1)} %get-tuple-element.27.own_ref, bf16[128,512]{1,0:T(8,128)(2,1)S(1)} %collective-permute-done.7.far_ref, bf16[2304,512]{1,0:T(8,128)(2,1)S(1)} %copy-done, bf16[2304,256]{1,0:T(8,128)(2,1)S(1)} %copy-done.1, bf16[2304,256]{1,0:T(8,128)(2,1)S(1)} %copy-done.2), custom_call_target="tpu_custom_call" | custom-call | flops 150994944 | bytes 1179648 | tf_op jit(solution)/shard_map/pallas_call | solution.py:334
  30.5 1.6 %collective-permute-start.8 = (bf16[576,128]{1,0:T(8,128)(2,1)S(1)}, bf16[576,128]{1,0:T(8,128)(2,1)S(1)}, u32[]{:S(2)}, u32[]{:S(2)}) collective-permute-start(bf16[576,128]{1,0:T(8,128)(2,1)S(1)} %shard_map.117), channel_id=1, source_target_pairs={{0,1},{1,0},{2,3},{3,2},{4,5},{5,4},{6,7},{7,6},{8,9},{9,8},{10,11... | collective-permute-start | bytes 442376 | tf_op jit(solution)/shard_map/ppermute | solution.py:347
  32.1 1.0 %shard_map.115._.dv_t_ref = bf16[128,1024]{1,0:T(8,128)(2,1)S(1)} custom-call(bf16[1024,2048]{1,0:T(8,128)(2,1)S(1)} %get-tuple-element.25.prob_ref, bf16[128,2048]{1,0:T(8,128)(2,1)S(1)} %get-tuple-element.26.grad_t_ref), custom_call_target="tpu_custom_call" | custom-call | flops 268435456 | bytes 4194304 | tf_op jit(solution)/shard_map/pallas_call | solution.py:334
  33.1 1.1 %shard_map.116 = (bf16[576,128]{1,0:T(8,128)(2,1)S(1)}, bf16[576,128]{1,0:T(8,128)(2,1)S(1)}, f32[576,128]{1,0:T(8,128)S(1)}) custom-call(bf16[128,512]{1,0:T(8,128)(2,1)S(1)} %get-tuple-element.27.own_ref, bf16[128,512]{1,0:T(8,128)(2,1)S(1)} %collective-permute-done.7.far_ref, bf16[2304,512]{1,0:T(8,128)(2,1)S(1)} %copy-done, ...), custom_call_target="tpu_custom_call" | custom-call | flops 452984832 | bytes 3538944 | tf_op jit(solution)/shard_map/pallas_call | solution.py:334
  34.2 2.2 %collective-permute-done.8.arrived_ref = bf16[576,128]{1,0:T(8,128)(2,1)S(1)} collective-permute-done((bf16[576,128]{1,0:T(8,128)(2,1)S(1)}, bf16[576,128]{1,0:T(8,128)(2,1)S(1)}, u32[]{:S(2)}, u32[]{:S(2)}) %collective-permute-start.8) | collective-permute-done | bytes 147488 | tf_op jit(solution)/shard_map/ppermute | solution.py:347
  36.8 2.6 %collective-permute-start.13 = (bf16[576,128]{1,0:T(8,128)(2,1)S(1)}, bf16[576,128]{1,0:T(8,128)(2,1)S(1)}, u32[]{:S(2)}, u32[]{:S(2)}) collective-permute-start(bf16[576,128]{1,0:T(8,128)(2,1)S(1)} %shard_map.118._), channel_id=1, source_target_pairs={{0,2},{1,3},{2,0},{3,1},{4,6},{5,7},{6,4},{7,5},{8,10},{9,11},{10,... | collective-permute-start | bytes 442376 | tf_op jit(solution)/shard_map/ppermute | solution.py:347
  39.4 1.6 %collective-permute-start.14 = (bf16[576,128]{1,0:T(8,128)(2,1)S(1)}, bf16[576,128]{1,0:T(8,128)(2,1)S(1)}, u32[]{:S(2)}, u32[]{:S(2)}) collective-permute-start(bf16[576,128]{1,0:T(8,128)(2,1)S(1)} %get-tuple-element.36), channel_id=1, source_target_pairs={{0,1},{1,0},{2,3},{3,2},{4,5},{5,4},{6,7},{7,6},{8,9},{9,8},{10,11... | collective-permute-start | bytes 442376 | tf_op jit(solution)/shard_map/ppermute | solution.py:347
  41.0 2.0 %shard_map.120 = (f32[288,256]{1,0:T(8,128)}, f32[288,512]{1,0:T(8,128)}, f32[8,128]{1,0:T(8,128)S(1)}) custom-call(bf16[256,1024]{1,0:T(8,128)(2,1)S(1)} %get-tuple-element.24.attn_ref, bf16[128,1024]{1,0:T(8,128)(2,1)S(1)} %shard_map.115._.dv_t_ref, bf16[5376,128]{1,0:T(8,128)(2,1)S(1)} %collective-permute-done.12.got_ref, ...), custom_call_target="tpu_custom_call" | custom-call | tf_op jit(solution)/shard_map/pallas_call | solution.py:334
  43.0 4.2 %collective-permute-done.13.arrived_ref = bf16[576,128]{1,0:T(8,128)(2,1)S(1)} collective-permute-done((bf16[576,128]{1,0:T(8,128)(2,1)S(1)}, bf16[576,128]{1,0:T(8,128)(2,1)S(1)}, u32[]{:S(2)}, u32[]{:S(2)}) %collective-permute-start.13) | collective-permute-done | bytes 147488 | tf_op jit(solution)/shard_map/ppermute | solution.py:347
  47.4 0.7 %shard_map.122 = bf16[576,128]{1,0:T(8,128)(2,1)} custom-call(f32[576,128]{1,0:T(8,128)S(1)} %shard_map.121.own_ref, bf16[576,128]{1,0:T(8,128)(2,1)S(1)} %collective-permute-done.14.refs_0_), custom_call_target="tpu_custom_call" | custom-call | bytes 1179648 | tf_op jit(solution)/shard_map/pallas_call | solution.py:334
  (29 shorter events, 2.2 us)
Async XLA Ops:
  0.6 16.6 %copy-start.3 = (bf16[128,2304]{1,0:T(8,128)(2,1)S(1)}, bf16[128,2304]{1,0:T(8,128)(2,1)}, u32[]{:S(2)}) copy-start(bf16[128,2304]{1,0:T(8,128)(2,1)} %cot_ref.1) | copy-start | bytes 1769476
  0.6 16.6 %copy-start.4 = (bf16[128,2304]{1,0:T(8,128)(2,1)S(1)}, bf16[128,2304]{1,0:T(8,128)(2,1)}, u32[]{:S(2)}) copy-start(bf16[128,2304]{1,0:T(8,128)(2,1)} %normed_ref.1) | copy-start | bytes 1769476
  4.7 8.6 %collective-permute-start = (bf16[128,768]{1,0:T(8,128)(2,1)}, bf16[128,768]{1,0:T(8,128)(2,1)S(1)}, u32[]{:S(2)}, u32[]{:S(2)}) collective-permute-start(bf16[128,768]{1,0:T(8,128)(2,1)} %get-tuple-element.21.block_ref), channel_id=1, source_target_pairs={{0,8},{4,12},{8,0},{12,4},{16,24},{20,28},{24,16},{28,20},{1,9},{5... | collective-permute-start | bytes 589832 | tf_op jit(solution)/shard_map/ppermute | solution.py:347
  7.7 7.8 %collective-permute-start.1 = (bf16[128,768]{1,0:T(8,128)(2,1)}, bf16[128,768]{1,0:T(8,128)(2,1)S(1)}, u32[]{:S(2)}, u32[]{:S(2)}) collective-permute-start(bf16[128,768]{1,0:T(8,128)(2,1)} %get-tuple-element.22), channel_id=1, source_target_pairs={{0,20},{4,16},{8,28},{12,24},{16,4},{20,0},{24,12},{28,8},{1,21},{... | collective-permute-start | bytes 589832 | tf_op jit(solution)/shard_map/ppermute | solution.py:347
  8.4 11.0 %collective-permute-start.4 = (bf16[128,768]{1,0:T(8,128)(2,1)}, bf16[128,768]{1,0:T(8,128)(2,1)S(1)}, u32[]{:S(2)}, u32[]{:S(2)}) collective-permute-start(bf16[128,768]{1,0:T(8,128)(2,1)} %get-tuple-element.21.block_ref), channel_id=1, source_target_pairs={{0,16},{4,20},{8,24},{12,28},{16,0},{20,4},{24,8},{28,12},{1,17},{... | collective-permute-start | bytes 589832 | tf_op jit(solution)/shard_map/ppermute | solution.py:347
  9.2 10.6 %collective-permute-start.3 = (bf16[128,768]{1,0:T(8,128)(2,1)}, bf16[128,768]{1,0:T(8,128)(2,1)S(1)}, u32[]{:S(2)}, u32[]{:S(2)}) collective-permute-start(bf16[128,768]{1,0:T(8,128)(2,1)} %get-tuple-element.22), channel_id=1, source_target_pairs={{0,12},{4,8},{8,4},{12,0},{16,28},{20,24},{24,20},{28,16},{1,13},{... | collective-permute-start | bytes 589832 | tf_op jit(solution)/shard_map/ppermute | solution.py:347
  9.5 11.4 %collective-permute-start.2 = (bf16[128,768]{1,0:T(8,128)(2,1)}, bf16[128,768]{1,0:T(8,128)(2,1)S(1)}, u32[]{:S(2)}, u32[]{:S(2)}) collective-permute-start(bf16[128,768]{1,0:T(8,128)(2,1)} %get-tuple-element.22), channel_id=1, source_target_pairs={{0,4},{4,0},{8,12},{12,8},{16,20},{20,16},{24,28},{28,24},{1,5},{5... | collective-permute-start | bytes 589832 | tf_op jit(solution)/shard_map/ppermute | solution.py:347
  13.3 10.3 %collective-permute-start.5 = (bf16[128,768]{1,0:T(8,128)(2,1)S(1)}, bf16[128,768]{1,0:T(8,128)(2,1)S(1)}, u32[]{:S(2)}, u32[]{:S(2)}) collective-permute-start(bf16[128,768]{1,0:T(8,128)(2,1)S(1)} %collective-permute-done._.refs_2_), channel_id=1, source_target_pairs={{0,16},{4,20},{8,24},{12,28},{16,0},{20,4},{24,8},{28,12},{1,17},{... | collective-permute-start | bytes 589832 | tf_op jit(solution)/shard_map/ppermute | solution.py:347
  15.5 8.1 %collective-permute-start.6 = (bf16[128,768]{1,0:T(8,128)(2,1)S(1)}, bf16[128,768]{1,0:T(8,128)(2,1)S(1)}, u32[]{:S(2)}, u32[]{:S(2)}) collective-permute-start(bf16[128,768]{1,0:T(8,128)(2,1)S(1)} %collective-permute-done.1.__.refs_5_), channel_id=1, source_target_pairs={{0,8},{4,12},{8,0},{12,4},{16,24},{20,28},{24,16},{28,20},{1,9},{5... | collective-permute-start | bytes 589832 | tf_op jit(solution)/shard_map/ppermute | solution.py:347
  17.2 0.9 %copy-start.5 = (bf16[128,768]{1,0:T(8,128)(2,1)S(1)}, bf16[128,768]{1,0:T(8,128)(2,1)}, u32[]{:S(2)}) copy-start(bf16[128,768]{1,0:T(8,128)(2,1)} %get-tuple-element.21.block_ref) | copy-start | bytes 589828
  19.4 17.1 %collective-permute-start.9 = (bf16[2,2,288,128]{3,2,1,0:T(8,128)(2,1)S(1)}, bf16[2,2,288,128]{3,2,1,0:T(8,128)(2,1)S(1)}, u32[]{:S(2)}, u32[]{:S(2)}) collective-permute-start(bf16[2,2,288,128]{3,2,1,0:T(8,128)(2,1)S(1)} %get-tuple-element.31), channel_id=1, source_target_pairs={{0,8},{4,12},{8,0},{12,4},{16,24},{20,28},{24,16},{28,20},{1,9},{5... | collective-permute-start | bytes 884744 | tf_op jit(solution)/shard_map/ppermute | solution.py:347
  19.9 16.6 %collective-permute-start.10 = (bf16[2,2,288,128]{3,2,1,0:T(8,128)(2,1)S(1)}, bf16[2,2,288,128]{3,2,1,0:T(8,128)(2,1)S(1)}, u32[]{:S(2)}, u32[]{:S(2)}) collective-permute-start(bf16[2,2,288,128]{3,2,1,0:T(8,128)(2,1)S(1)} %get-tuple-element.32), channel_id=1, source_target_pairs={{0,16},{4,20},{8,24},{12,28},{16,0},{20,4},{24,8},{28,12},{1,17},{... | collective-permute-start | bytes 884744 | tf_op jit(solution)/shard_map/ppermute | solution.py:347
  20.9 15.6 %collective-permute-start.11 = (bf16[2,2,288,128]{3,2,1,0:T(8,128)(2,1)S(1)}, bf16[2,2,288,128]{3,2,1,0:T(8,128)(2,1)S(1)}, u32[]{:S(2)}, u32[]{:S(2)}) collective-permute-start(bf16[2,2,288,128]{3,2,1,0:T(8,128)(2,1)S(1)} %get-tuple-element.33), channel_id=1, source_target_pairs={{0,24},{4,28},{8,16},{12,20},{16,8},{20,12},{24,0},{28,4},{1,25},{... | collective-permute-start | bytes 884744 | tf_op jit(solution)/shard_map/ppermute | solution.py:347
  23.6 6.3 %copy-start = (bf16[2304,512]{1,0:T(8,128)(2,1)S(1)}, bf16[2304,512]{1,0:T(8,128)(2,1)}, u32[]{:S(2)}) copy-start(bf16[2304,512]{1,0:T(8,128)(2,1)} %wq_ref.3) | copy-start | bytes 7077892
  23.6 6.3 %copy-start.1 = (bf16[2304,256]{1,0:T(8,128)(2,1)S(1)}, bf16[2304,256]{1,0:T(8,128)(2,1)}, u32[]{:S(2)}) copy-start(bf16[2304,256]{1,0:T(8,128)(2,1)} %wk_ref.3) | copy-start | bytes 3538948
  23.6 6.3 %copy-start.2 = (bf16[2304,256]{1,0:T(8,128)(2,1)S(1)}, bf16[2304,256]{1,0:T(8,128)(2,1)}, u32[]{:S(2)}) copy-start(bf16[2304,256]{1,0:T(8,128)(2,1)} %wv_ref.3) | copy-start | bytes 3538948
  28.5 1.4 %collective-permute-start.7 = (bf16[128,512]{1,0:T(8,128)(2,1)S(1)}, bf16[128,512]{1,0:T(8,128)(2,1)S(1)}, u32[]{:S(2)}, u32[]{:S(2)}) collective-permute-start(bf16[128,512]{1,0:T(8,128)(2,1)S(1)} %get-tuple-element.28), channel_id=1, source_target_pairs={{0,4},{4,0},{8,12},{12,8},{16,20},{20,16},{24,28},{28,24},{1,5},{5... | collective-permute-start | bytes 393224 | tf_op jit(solution)/shard_map/ppermute | solution.py:347
  30.5 6.0 %collective-permute-start.8 = (bf16[576,128]{1,0:T(8,128)(2,1)S(1)}, bf16[576,128]{1,0:T(8,128)(2,1)S(1)}, u32[]{:S(2)}, u32[]{:S(2)}) collective-permute-start(bf16[576,128]{1,0:T(8,128)(2,1)S(1)} %shard_map.117), channel_id=1, source_target_pairs={{0,1},{1,0},{2,3},{3,2},{4,5},{5,4},{6,7},{7,6},{8,9},{9,8},{10,11... | collective-permute-start | bytes 442376 | tf_op jit(solution)/shard_map/ppermute | solution.py:347
  36.7 4.3 %collective-permute-start.12 = (bf16[5376,128]{1,0:T(8,128)(2,1)S(1)}, bf16[5376,128]{1,0:T(8,128)(2,1)S(1)}, u32[]{:S(2)}, u32[]{:S(2)}) collective-permute-start(bf16[5376,128]{1,0:T(8,128)(2,1)S(1)} %shard_map.119), channel_id=1, source_target_pairs={{0,4},{4,0},{8,12},{12,8},{16,20},{20,16},{24,28},{28,24},{1,5},{5... | collective-permute-start | bytes 4128776 | tf_op jit(solution)/shard_map/ppermute | solution.py:347
  36.8 10.4 %collective-permute-start.13 = (bf16[576,128]{1,0:T(8,128)(2,1)S(1)}, bf16[576,128]{1,0:T(8,128)(2,1)S(1)}, u32[]{:S(2)}, u32[]{:S(2)}) collective-permute-start(bf16[576,128]{1,0:T(8,128)(2,1)S(1)} %shard_map.118._), channel_id=1, source_target_pairs={{0,2},{1,3},{2,0},{3,1},{4,6},{5,7},{6,4},{7,5},{8,10},{9,11},{10,... | collective-permute-start | bytes 442376 | tf_op jit(solution)/shard_map/ppermute | solution.py:347
  39.4 8.0 %collective-permute-start.14 = (bf16[576,128]{1,0:T(8,128)(2,1)S(1)}, bf16[576,128]{1,0:T(8,128)(2,1)S(1)}, u32[]{:S(2)}, u32[]{:S(2)}) collective-permute-start(bf16[576,128]{1,0:T(8,128)(2,1)S(1)} %get-tuple-element.36), channel_id=1, source_target_pairs={{0,1},{1,0},{2,3},{3,2},{4,5},{5,4},{6,7},{7,6},{8,9},{9,8},{10,11... | collective-permute-start | bytes 442376 | tf_op jit(solution)/shard_map/ppermute | solution.py:347

commit v21 on v20

--- a/solution.py
+++ b/solution.py
@@ -85,14 +85,14 @@
         for copy in model_copies[piece]:
             copy.wait()
         part = slice(piece * cut, (piece + 1) * cut)
-        product = dot_nt(weight_ref[:, part], cot_ref[:, part])
+        product = dot_nt(cot_ref[:, part], weight_ref[:, part])
         total = product if total is None else total + product
     for place, (target, _) in enumerate(halves):
         for head in range(rows // HEAD_SIZE):
             row = place * rows + head * HEAD_SIZE
             target[:, first + head * HEAD_SIZE : first + (head + 1) * HEAD_SIZE] = total[
-                row : row + HEAD_SIZE
-            ].astype(jnp.bfloat16)
+                :, row : row + HEAD_SIZE
+            ].T.astype(jnp.bfloat16)
     for copy in plain_copies:
         copy.wait()
 
@@ -367,7 +367,7 @@
     kv_cols = HEAD_SIZE
     wide = 2 * QUERIES_PER_KEY * rows
     packed_cols = 2 * q_cols + 2 * kv_cols
-    pieces = model // (2 * HEAD_SIZE) if model % (2 * HEAD_SIZE) == 0 else 1
+    pieces = 3 if model % (6 * HEAD_SIZE) == 0 else 1
     shape = jax.ShapeDtypeStruct
     same, other = kernel_call(
         out_grad_kernel,
@@ -380,7 +380,7 @@
         ),
         flops=4 * rows * model * q_cols,
         moved=2 * model * (rows + 2 * q_cols),
-        room=62,
+        room=63,
     )
     held = {0: same}
     for apart in range(2, blocks):

time: 48.2 us -> 47.7 us (0.990)
  waiting for transfers between devices: 12.8 us -> 11.7 us
  local copies, waits for them, and re-layouts: 0.95 us -> 2.01 us
  Pallas kernels: 15 us -> 14.4 us
    ppermute x15, waiting for transfers between devices: 12.8 us -> 11.7 us  [swapped(): lax.ppermute(value, axis, [(place, place ^ apart) for place in range(coun...]
    unnamed x12, local copies, waits for them, and re-layouts: 0.95 us -> 2.01 us
    pallas_call x11, Pallas kernels: 15 us -> 14.4 us  [kernel_call(): pl.pallas_call(body, out_shape=outs, in_specs=[vmem if place in in_vmem e...]
  transfers between devices with their start and end apart: 15 -> 15, of which waited for: 7 -> 6; matrix products, arithmetic and copies ran while one was open for 0% -> 0% of each run, Pallas kernels for 21% -> 21%
where the time goes in v21:
time: 47.7 us; the launch traced here: 47.5 us
  starting transfers between devices  18.7 us (39%)
  Pallas kernels  14.4 us (30%)
  waiting for transfers between devices  11.7 us (25%)
  local copies, waits for them, and re-layouts  2.01 us (4%)
  between operations  0.77 us (2%)
    ppermute x15, starting transfers between devices, swapped(): lax.ppermute(value, axis, [(place, place ^ apart) for place in range(coun...  18.7 us
    pallas_call x11, Pallas kernels, kernel_call(): pl.pallas_call(body, out_shape=outs, in_specs=[vmem if place in in_vmem e...  14.4 us
    ppermute x15, waiting for transfers between devices, swapped(): lax.ppermute(value, axis, [(place, place ^ apart) for place in range(coun...  11.7 us
    unnamed x12, local copies, waits for them, and re-layouts  2.01 us
  transfers between devices with their start and end apart: 15, of which 6 were waited for; matrix products, arithmetic and copies ran while one was open for 0% of the time, Pallas kernels for 21%

profile of v21, /device:TPU:0, one launch (start us, length us, event | category | flops | bytes accessed | tf_op | source)
XLA Modules:
  0.0 47.5 jit_solution(11025335459068929025)
XLA Ops:
  0.6 3.5 %shard_map.112 = (bf16[128,768]{1,0:T(8,128)(2,1)}, bf16[128,768]{1,0:T(8,128)(2,1)}) custom-call(bf16[128,2304]{1,0:T(8,128)(2,1)} %cot_ref.1, bf16[512,2304]{1,0:T(8,128)(2,1)} %weight_hbm.1, bf16[128,512]{1,0:T(8,128)(2,1)} %q_hbm.1, bf16[128,256]{1,0:T(8,128)(2,1)} %k_hbm.1, bf16[128,256]{1,0:T(8,128)(2,1)} %v_hbm.1), custom_call_target="tpu_custom_call" | custom-call | flops 301989888 | bytes 2949120 | tf_op jit(solution)/shard_map/pallas_call | solution.py:334
  4.1 3.0 %collective-permute-start = (bf16[128,768]{1,0:T(8,128)(2,1)}, bf16[128,768]{1,0:T(8,128)(2,1)S(1)}, u32[]{:S(2)}, u32[]{:S(2)}) collective-permute-start(bf16[128,768]{1,0:T(8,128)(2,1)} %get-tuple-element.21.block_ref), channel_id=1, source_target_pairs={{0,8},{4,12},{8,0},{12,4},{16,24},{20,28},{24,16},{28,20},{1,9},{5... | collective-permute-start | bytes 589832 | tf_op jit(solution)/shard_map/ppermute | solution.py:347
  7.1 0.7 %collective-permute-start.1 = (bf16[128,768]{1,0:T(8,128)(2,1)}, bf16[128,768]{1,0:T(8,128)(2,1)S(1)}, u32[]{:S(2)}, u32[]{:S(2)}) collective-permute-start(bf16[128,768]{1,0:T(8,128)(2,1)} %get-tuple-element.22), channel_id=1, source_target_pairs={{0,20},{4,16},{8,28},{12,24},{16,4},{20,0},{24,12},{28,8},{1,21},{... | collective-permute-start | bytes 589832 | tf_op jit(solution)/shard_map/ppermute | solution.py:347
  7.8 0.9 %collective-permute-start.4 = (bf16[128,768]{1,0:T(8,128)(2,1)}, bf16[128,768]{1,0:T(8,128)(2,1)S(1)}, u32[]{:S(2)}, u32[]{:S(2)}) collective-permute-start(bf16[128,768]{1,0:T(8,128)(2,1)} %get-tuple-element.21.block_ref), channel_id=1, source_target_pairs={{0,16},{4,20},{8,24},{12,28},{16,0},{20,4},{24,8},{28,12},{1,17},{... | collective-permute-start | bytes 589832 | tf_op jit(solution)/shard_map/ppermute | solution.py:347
  9.3 3.4 %collective-permute-done._.refs_2_ = bf16[128,768]{1,0:T(8,128)(2,1)S(1)} collective-permute-done((bf16[128,768]{1,0:T(8,128)(2,1)}, bf16[128,768]{1,0:T(8,128)(2,1)S(1)}, u32[]{:S(2)}, u32[]{:S(2)}) %collective-permute-start) | collective-permute-done | bytes 196640 | tf_op jit(solution)/shard_map/ppermute | solution.py:347
  12.7 2.2 %collective-permute-start.5 = (bf16[128,768]{1,0:T(8,128)(2,1)S(1)}, bf16[128,768]{1,0:T(8,128)(2,1)S(1)}, u32[]{:S(2)}, u32[]{:S(2)}) collective-permute-start(bf16[128,768]{1,0:T(8,128)(2,1)S(1)} %collective-permute-done._.refs_2_), channel_id=1, source_target_pairs={{0,16},{4,20},{8,24},{12,28},{16,0},{20,4},{24,8},{28,12},{1,17},{... | collective-permute-start | bytes 589832 | tf_op jit(solution)/shard_map/ppermute | solution.py:347
  14.9 1.7 %collective-permute-start.6 = (bf16[128,768]{1,0:T(8,128)(2,1)S(1)}, bf16[128,768]{1,0:T(8,128)(2,1)S(1)}, u32[]{:S(2)}, u32[]{:S(2)}) collective-permute-start(bf16[128,768]{1,0:T(8,128)(2,1)S(1)} %collective-permute-done.1.__.refs_5_), channel_id=1, source_target_pairs={{0,8},{4,12},{8,0},{12,4},{16,24},{20,28},{24,16},{28,20},{1,9},{5... | collective-permute-start | bytes 589832 | tf_op jit(solution)/shard_map/ppermute | solution.py:347
  16.6 1.1 %copy-done.4 = bf16[128,2304]{1,0:T(8,128)(2,1)S(1)} copy-done((bf16[128,2304]{1,0:T(8,128)(2,1)S(1)}, bf16[128,2304]{1,0:T(8,128)(2,1)}, u32[]{:S(2)}) %copy-start.4) | copy-done | bytes 589848
  17.7 0.9 %copy-done.5 = bf16[128,768]{1,0:T(8,128)(2,1)S(1)} copy-done((bf16[128,768]{1,0:T(8,128)(2,1)S(1)}, bf16[128,768]{1,0:T(8,128)(2,1)}, u32[]{:S(2)}) %copy-start.5) | copy-done | bytes 196632
  18.6 0.5 %shard_map.113 = (bf16[2,2,288,128]{3,2,1,0:T(8,128)(2,1)S(1)}, bf16[2,2,288,128]{3,2,1,0:T(8,128)(2,1)S(1)}, bf16[2,2,288,128]{3,2,1,0:T(8,128)(2,1)S(1)}, bf16...) custom-call(bf16[128,2304]{1,0:T(8,128)(2,1)S(1)} %copy-done.4, bf16[128,2304]{1,0:T(8,128)(2,1)S(1)} %copy-done.3, ...), custom_call_target="tpu_custom_call" | custom-call | bytes 2359296 | tf_op jit(solution)/shard_map/pallas_call | solution.py:334
  19.5 1.1 %collective-permute-start.10 = (bf16[2,2,288,128]{3,2,1,0:T(8,128)(2,1)S(1)}, bf16[2,2,288,128]{3,2,1,0:T(8,128)(2,1)S(1)}, u32[]{:S(2)}, u32[]{:S(2)}) collective-permute-start(bf16[2,2,288,128]{3,2,1,0:T(8,128)(2,1)S(1)} %get-tuple-element.32), channel_id=1, source_target_pairs={{0,16},{4,20},{8,24},{12,28},{16,0},{20,4},{24,8},{28,12},{1,17},{... | collective-permute-start | bytes 884744 | tf_op jit(solution)/shard_map/ppermute | solution.py:347
  20.6 2.1 %collective-permute-start.11 = (bf16[2,2,288,128]{3,2,1,0:T(8,128)(2,1)S(1)}, bf16[2,2,288,128]{3,2,1,0:T(8,128)(2,1)S(1)}, u32[]{:S(2)}, u32[]{:S(2)}) collective-permute-start(bf16[2,2,288,128]{3,2,1,0:T(8,128)(2,1)S(1)} %get-tuple-element.33), channel_id=1, source_target_pairs={{0,24},{4,28},{8,16},{12,20},{16,8},{20,12},{24,0},{28,4},{1,25},{... | collective-permute-start | bytes 884744 | tf_op jit(solution)/shard_map/ppermute | solution.py:347
  23.0 4.9 %shard_map.114 = (bf16[128,512]{1,0:T(8,128)(2,1)S(1)}, bf16[128,512]{1,0:T(8,128)(2,1)S(1)}, bf16[256,1024]{1,0:T(8,128)(2,1)S(1)}, bf16[1024,2048]{1,0:T(8,128)(2,1)S(1)}, bf16[128,2048]{1,0:T(8,128)(2,1)S(1)}) custom-call(bf16[128,768]{1,0:T(8,128)(2,1)S(1)} %get-tuple-element.23.refs_0_, bf16[128,768]{1,0:T(8,128)(2,1)S(1)} %collective-permute-done.2.refs_1_, ...), custom_call_target="tpu_custom_call" | custom-call | flops 2147483648 | bytes 1572864 | tf_op jit(solution)/shard_map/pallas_call | solution.py:334
  28.0 1.3 %collective-permute-done.7.far_ref = bf16[128,512]{1,0:T(8,128)(2,1)S(1)} collective-permute-done((bf16[128,512]{1,0:T(8,128)(2,1)S(1)}, bf16[128,512]{1,0:T(8,128)(2,1)S(1)}, u32[]{:S(2)}, u32[]{:S(2)}) %collective-permute-start.7) | collective-permute-done | bytes 131104 | tf_op jit(solution)/shard_map/ppermute | solution.py:347
  29.4 0.5 %shard_map.117 = bf16[576,128]{1,0:T(8,128)(2,1)S(1)} custom-call(bf16[128,512]{1,0:T(8,128)(2,1)S(1)} %get-tuple-element.27.own_ref, bf16[128,512]{1,0:T(8,128)(2,1)S(1)} %collective-permute-done.7.far_ref, bf16[2304,512]{1,0:T(8,128)(2,1)S(1)} %copy-done, bf16[2304,256]{1,0:T(8,128)(2,1)S(1)} %copy-done.1, bf16[2304,256]{1,0:T(8,128)(2,1)S(1)} %copy-done.2), custom_call_target="tpu_custom_call" | custom-call | flops 150994944 | bytes 1179648 | tf_op jit(solution)/shard_map/pallas_call | solution.py:334
  29.9 1.6 %collective-permute-start.8 = (bf16[576,128]{1,0:T(8,128)(2,1)S(1)}, bf16[576,128]{1,0:T(8,128)(2,1)S(1)}, u32[]{:S(2)}, u32[]{:S(2)}) collective-permute-start(bf16[576,128]{1,0:T(8,128)(2,1)S(1)} %shard_map.117), channel_id=1, source_target_pairs={{0,1},{1,0},{2,3},{3,2},{4,5},{5,4},{6,7},{7,6},{8,9},{9,8},{10,11... | collective-permute-start | bytes 442376 | tf_op jit(solution)/shard_map/ppermute | solution.py:347
  31.5 1.0 %shard_map.115._.dv_t_ref = bf16[128,1024]{1,0:T(8,128)(2,1)S(1)} custom-call(bf16[1024,2048]{1,0:T(8,128)(2,1)S(1)} %get-tuple-element.25.prob_ref, bf16[128,2048]{1,0:T(8,128)(2,1)S(1)} %get-tuple-element.26.grad_t_ref), custom_call_target="tpu_custom_call" | custom-call | flops 268435456 | bytes 4194304 | tf_op jit(solution)/shard_map/pallas_call | solution.py:334
  32.5 1.1 %shard_map.116 = (bf16[576,128]{1,0:T(8,128)(2,1)S(1)}, bf16[576,128]{1,0:T(8,128)(2,1)S(1)}, f32[576,128]{1,0:T(8,128)S(1)}) custom-call(bf16[128,512]{1,0:T(8,128)(2,1)S(1)} %get-tuple-element.27.own_ref, bf16[128,512]{1,0:T(8,128)(2,1)S(1)} %collective-permute-done.7.far_ref, bf16[2304,512]{1,0:T(8,128)(2,1)S(1)} %copy-done, ...), custom_call_target="tpu_custom_call" | custom-call | flops 452984832 | bytes 3538944 | tf_op jit(solution)/shard_map/pallas_call | solution.py:334
  33.6 2.2 %collective-permute-done.8.arrived_ref = bf16[576,128]{1,0:T(8,128)(2,1)S(1)} collective-permute-done((bf16[576,128]{1,0:T(8,128)(2,1)S(1)}, bf16[576,128]{1,0:T(8,128)(2,1)S(1)}, u32[]{:S(2)}, u32[]{:S(2)}) %collective-permute-start.8) | collective-permute-done | bytes 147488 | tf_op jit(solution)/shard_map/ppermute | solution.py:347
  36.2 2.6 %collective-permute-start.13 = (bf16[576,128]{1,0:T(8,128)(2,1)S(1)}, bf16[576,128]{1,0:T(8,128)(2,1)S(1)}, u32[]{:S(2)}, u32[]{:S(2)}) collective-permute-start(bf16[576,128]{1,0:T(8,128)(2,1)S(1)} %shard_map.118._), channel_id=1, source_target_pairs={{0,2},{1,3},{2,0},{3,1},{4,6},{5,7},{6,4},{7,5},{8,10},{9,11},{10,... | collective-permute-start | bytes 442376 | tf_op jit(solution)/shard_map/ppermute | solution.py:347
  38.8 1.6 %collective-permute-start.14 = (bf16[576,128]{1,0:T(8,128)(2,1)S(1)}, bf16[576,128]{1,0:T(8,128)(2,1)S(1)}, u32[]{:S(2)}, u32[]{:S(2)}) collective-permute-start(bf16[576,128]{1,0:T(8,128)(2,1)S(1)} %get-tuple-element.36), channel_id=1, source_target_pairs={{0,1},{1,0},{2,3},{3,2},{4,5},{5,4},{6,7},{7,6},{8,9},{9,8},{10,11... | collective-permute-start | bytes 442376 | tf_op jit(solution)/shard_map/ppermute | solution.py:347
  40.4 2.0 %shard_map.120 = (f32[288,256]{1,0:T(8,128)}, f32[288,512]{1,0:T(8,128)}, f32[8,128]{1,0:T(8,128)S(1)}) custom-call(bf16[256,1024]{1,0:T(8,128)(2,1)S(1)} %get-tuple-element.24.attn_ref, bf16[128,1024]{1,0:T(8,128)(2,1)S(1)} %shard_map.115._.dv_t_ref, bf16[5376,128]{1,0:T(8,128)(2,1)S(1)} %collective-permute-done.12.got_ref, ...), custom_call_target="tpu_custom_call" | custom-call | tf_op jit(solution)/shard_map/pallas_call | solution.py:334
  42.4 4.2 %collective-permute-done.13.arrived_ref = bf16[576,128]{1,0:T(8,128)(2,1)S(1)} collective-permute-done((bf16[576,128]{1,0:T(8,128)(2,1)S(1)}, bf16[576,128]{1,0:T(8,128)(2,1)S(1)}, u32[]{:S(2)}, u32[]{:S(2)}) %collective-permute-start.13) | collective-permute-done | bytes 147488 | tf_op jit(solution)/shard_map/ppermute | solution.py:347
  46.8 0.7 %shard_map.122 = bf16[576,128]{1,0:T(8,128)(2,1)} custom-call(f32[576,128]{1,0:T(8,128)S(1)} %shard_map.121.own_ref, bf16[576,128]{1,0:T(8,128)(2,1)S(1)} %collective-permute-done.14.refs_0_), custom_call_target="tpu_custom_call" | custom-call | bytes 1179648 | tf_op jit(solution)/shard_map/pallas_call | solution.py:334
  (29 shorter events, 1.9 us)
Async XLA Ops:
  0.6 16.0 %copy-start.3 = (bf16[128,2304]{1,0:T(8,128)(2,1)S(1)}, bf16[128,2304]{1,0:T(8,128)(2,1)}, u32[]{:S(2)}) copy-start(bf16[128,2304]{1,0:T(8,128)(2,1)} %cot_ref.1) | copy-start | bytes 1769476
  4.1 8.6 %collective-permute-start = (bf16[128,768]{1,0:T(8,128)(2,1)}, bf16[128,768]{1,0:T(8,128)(2,1)S(1)}, u32[]{:S(2)}, u32[]{:S(2)}) collective-permute-start(bf16[128,768]{1,0:T(8,128)(2,1)} %get-tuple-element.21.block_ref), channel_id=1, source_target_pairs={{0,8},{4,12},{8,0},{12,4},{16,24},{20,28},{24,16},{28,20},{1,9},{5... | collective-permute-start | bytes 589832 | tf_op jit(solution)/shard_map/ppermute | solution.py:347
  7.1 7.8 %collective-permute-start.1 = (bf16[128,768]{1,0:T(8,128)(2,1)}, bf16[128,768]{1,0:T(8,128)(2,1)S(1)}, u32[]{:S(2)}, u32[]{:S(2)}) collective-permute-start(bf16[128,768]{1,0:T(8,128)(2,1)} %get-tuple-element.22), channel_id=1, source_target_pairs={{0,20},{4,16},{8,28},{12,24},{16,4},{20,0},{24,12},{28,8},{1,21},{... | collective-permute-start | bytes 589832 | tf_op jit(solution)/shard_map/ppermute | solution.py:347
  7.8 11.3 %collective-permute-start.4 = (bf16[128,768]{1,0:T(8,128)(2,1)}, bf16[128,768]{1,0:T(8,128)(2,1)S(1)}, u32[]{:S(2)}, u32[]{:S(2)}) collective-permute-start(bf16[128,768]{1,0:T(8,128)(2,1)} %get-tuple-element.21.block_ref), channel_id=1, source_target_pairs={{0,16},{4,20},{8,24},{12,28},{16,0},{20,4},{24,8},{28,12},{1,17},{... | collective-permute-start | bytes 589832 | tf_op jit(solution)/shard_map/ppermute | solution.py:347
  8.7 10.8 %collective-permute-start.3 = (bf16[128,768]{1,0:T(8,128)(2,1)}, bf16[128,768]{1,0:T(8,128)(2,1)S(1)}, u32[]{:S(2)}, u32[]{:S(2)}) collective-permute-start(bf16[128,768]{1,0:T(8,128)(2,1)} %get-tuple-element.22), channel_id=1, source_target_pairs={{0,12},{4,8},{8,4},{12,0},{16,28},{20,24},{24,20},{28,16},{1,13},{... | collective-permute-start | bytes 589832 | tf_op jit(solution)/shard_map/ppermute | solution.py:347
  8.9 11.8 %collective-permute-start.2 = (bf16[128,768]{1,0:T(8,128)(2,1)}, bf16[128,768]{1,0:T(8,128)(2,1)S(1)}, u32[]{:S(2)}, u32[]{:S(2)}) collective-permute-start(bf16[128,768]{1,0:T(8,128)(2,1)} %get-tuple-element.22), channel_id=1, source_target_pairs={{0,4},{4,0},{8,12},{12,8},{16,20},{20,16},{24,28},{28,24},{1,5},{5... | collective-permute-start | bytes 589832 | tf_op jit(solution)/shard_map/ppermute | solution.py:347
  12.7 10.3 %collective-permute-start.5 = (bf16[128,768]{1,0:T(8,128)(2,1)S(1)}, bf16[128,768]{1,0:T(8,128)(2,1)S(1)}, u32[]{:S(2)}, u32[]{:S(2)}) collective-permute-start(bf16[128,768]{1,0:T(8,128)(2,1)S(1)} %collective-permute-done._.refs_2_), channel_id=1, source_target_pairs={{0,16},{4,20},{8,24},{12,28},{16,0},{20,4},{24,8},{28,12},{1,17},{... | collective-permute-start | bytes 589832 | tf_op jit(solution)/shard_map/ppermute | solution.py:347
  14.9 8.1 %collective-permute-start.6 = (bf16[128,768]{1,0:T(8,128)(2,1)S(1)}, bf16[128,768]{1,0:T(8,128)(2,1)S(1)}, u32[]{:S(2)}, u32[]{:S(2)}) collective-permute-start(bf16[128,768]{1,0:T(8,128)(2,1)S(1)} %collective-permute-done.1.__.refs_5_), channel_id=1, source_target_pairs={{0,8},{4,12},{8,0},{12,4},{16,24},{20,28},{24,16},{28,20},{1,9},{5... | collective-permute-start | bytes 589832 | tf_op jit(solution)/shard_map/ppermute | solution.py:347
  16.6 1.1 %copy-start.4 = (bf16[128,2304]{1,0:T(8,128)(2,1)S(1)}, bf16[128,2304]{1,0:T(8,128)(2,1)}, u32[]{:S(2)}) copy-start(bf16[128,2304]{1,0:T(8,128)(2,1)} %normed_ref.1) | copy-start | bytes 1769476
  17.7 0.9 %copy-start.5 = (bf16[128,768]{1,0:T(8,128)(2,1)S(1)}, bf16[128,768]{1,0:T(8,128)(2,1)}, u32[]{:S(2)}) copy-start(bf16[128,768]{1,0:T(8,128)(2,1)} %get-tuple-element.21.block_ref) | copy-start | bytes 589828
  19.1 16.8 %collective-permute-start.9 = (bf16[2,2,288,128]{3,2,1,0:T(8,128)(2,1)S(1)}, bf16[2,2,288,128]{3,2,1,0:T(8,128)(2,1)S(1)}, u32[]{:S(2)}, u32[]{:S(2)}) collective-permute-start(bf16[2,2,288,128]{3,2,1,0:T(8,128)(2,1)S(1)} %get-tuple-element.31), channel_id=1, source_target_pairs={{0,8},{4,12},{8,0},{12,4},{16,24},{20,28},{24,16},{28,20},{1,9},{5... | collective-permute-start | bytes 884744 | tf_op jit(solution)/shard_map/ppermute | solution.py:347
  19.5 16.4 %collective-permute-start.10 = (bf16[2,2,288,128]{3,2,1,0:T(8,128)(2,1)S(1)}, bf16[2,2,288,128]{3,2,1,0:T(8,128)(2,1)S(1)}, u32[]{:S(2)}, u32[]{:S(2)}) collective-permute-start(bf16[2,2,288,128]{3,2,1,0:T(8,128)(2,1)S(1)} %get-tuple-element.32), channel_id=1, source_target_pairs={{0,16},{4,20},{8,24},{12,28},{16,0},{20,4},{24,8},{28,12},{1,17},{... | collective-permute-start | bytes 884744 | tf_op jit(solution)/shard_map/ppermute | solution.py:347
  20.6 15.3 %collective-permute-start.11 = (bf16[2,2,288,128]{3,2,1,0:T(8,128)(2,1)S(1)}, bf16[2,2,288,128]{3,2,1,0:T(8,128)(2,1)S(1)}, u32[]{:S(2)}, u32[]{:S(2)}) collective-permute-start(bf16[2,2,288,128]{3,2,1,0:T(8,128)(2,1)S(1)} %get-tuple-element.33), channel_id=1, source_target_pairs={{0,24},{4,28},{8,16},{12,20},{16,8},{20,12},{24,0},{28,4},{1,25},{... | collective-permute-start | bytes 884744 | tf_op jit(solution)/shard_map/ppermute | solution.py:347
  23.0 6.3 %copy-start = (bf16[2304,512]{1,0:T(8,128)(2,1)S(1)}, bf16[2304,512]{1,0:T(8,128)(2,1)}, u32[]{:S(2)}) copy-start(bf16[2304,512]{1,0:T(8,128)(2,1)} %wq_ref.3) | copy-start | bytes 7077892
  23.0 6.3 %copy-start.1 = (bf16[2304,256]{1,0:T(8,128)(2,1)S(1)}, bf16[2304,256]{1,0:T(8,128)(2,1)}, u32[]{:S(2)}) copy-start(bf16[2304,256]{1,0:T(8,128)(2,1)} %wk_ref.3) | copy-start | bytes 3538948
  23.0 6.3 %copy-start.2 = (bf16[2304,256]{1,0:T(8,128)(2,1)S(1)}, bf16[2304,256]{1,0:T(8,128)(2,1)}, u32[]{:S(2)}) copy-start(bf16[2304,256]{1,0:T(8,128)(2,1)} %wv_ref.3) | copy-start | bytes 3538948
  27.9 1.4 %collective-permute-start.7 = (bf16[128,512]{1,0:T(8,128)(2,1)S(1)}, bf16[128,512]{1,0:T(8,128)(2,1)S(1)}, u32[]{:S(2)}, u32[]{:S(2)}) collective-permute-start(bf16[128,512]{1,0:T(8,128)(2,1)S(1)} %get-tuple-element.28), channel_id=1, source_target_pairs={{0,4},{4,0},{8,12},{12,8},{16,20},{20,16},{24,28},{28,24},{1,5},{5... | collective-permute-start | bytes 393224 | tf_op jit(solution)/shard_map/ppermute | solution.py:347
  29.9 6.0 %collective-permute-start.8 = (bf16[576,128]{1,0:T(8,128)(2,1)S(1)}, bf16[576,128]{1,0:T(8,128)(2,1)S(1)}, u32[]{:S(2)}, u32[]{:S(2)}) collective-permute-start(bf16[576,128]{1,0:T(8,128)(2,1)S(1)} %shard_map.117), channel_id=1, source_target_pairs={{0,1},{1,0},{2,3},{3,2},{4,5},{5,4},{6,7},{7,6},{8,9},{9,8},{10,11... | collective-permute-start | bytes 442376 | tf_op jit(solution)/shard_map/ppermute | solution.py:347
  36.1 4.3 %collective-permute-start.12 = (bf16[5376,128]{1,0:T(8,128)(2,1)S(1)}, bf16[5376,128]{1,0:T(8,128)(2,1)S(1)}, u32[]{:S(2)}, u32[]{:S(2)}) collective-permute-start(bf16[5376,128]{1,0:T(8,128)(2,1)S(1)} %shard_map.119), channel_id=1, source_target_pairs={{0,4},{4,0},{8,12},{12,8},{16,20},{20,16},{24,28},{28,24},{1,5},{5... | collective-permute-start | bytes 4128776 | tf_op jit(solution)/shard_map/ppermute | solution.py:347
  36.2 10.4 %collective-permute-start.13 = (bf16[576,128]{1,0:T(8,128)(2,1)S(1)}, bf16[576,128]{1,0:T(8,128)(2,1)S(1)}, u32[]{:S(2)}, u32[]{:S(2)}) collective-permute-start(bf16[576,128]{1,0:T(8,128)(2,1)S(1)} %shard_map.118._), channel_id=1, source_target_pairs={{0,2},{1,3},{2,0},{3,1},{4,6},{5,7},{6,4},{7,5},{8,10},{9,11},{10,... | collective-permute-start | bytes 442376 | tf_op jit(solution)/shard_map/ppermute | solution.py:347
  38.8 8.0 %collective-permute-start.14 = (bf16[576,128]{1,0:T(8,128)(2,1)S(1)}, bf16[576,128]{1,0:T(8,128)(2,1)S(1)}, u32[]{:S(2)}, u32[]{:S(2)}) collective-permute-start(bf16[576,128]{1,0:T(8,128)(2,1)S(1)} %get-tuple-element.36), channel_id=1, source_target_pairs={{0,1},{1,0},{2,3},{3,2},{4,5},{5,4},{6,7},{7,6},{8,9},{9,8},{10,11... | collective-permute-start | bytes 442376 | tf_op jit(solution)/shard_map/ppermute | solution.py:347

commit v22 on v21

--- a/solution.py
+++ b/solution.py
@@ -109,7 +109,7 @@
                 target[far, which] = turned_ref[which, at(me ^ (2 * chip + far), cut)]
 
 
-def pass_on_kernel(_, attn_ref, dv_t_ref, *refs):
+def pass_on_kernel(_, __, attn_ref, dv_t_ref, *refs):
     *column_refs, give_ref = refs
     cut, rows = column_refs[0].shape[2:]
     for chip, ref in enumerate(column_refs):
@@ -315,11 +315,7 @@
     sum_ref[...] = total.astype(jnp.bfloat16)
 
 
-def far_sum_kernel(_, own_ref, arrived_ref, sum_ref):
-    sum_ref[...] = own_ref[...] + arrived_ref[...].astype(jnp.float32)
-
-
-def sum_kernel(own_ref, *refs):
+def sum_kernel(_, own_ref, *refs):
     total = own_ref[...]
     for arrived_ref in refs[:-1]:
         total = total + arrived_ref[...].astype(jnp.float32)
@@ -463,12 +459,13 @@
         in_vmem=range(2),
         room=4,
     )
+    near_got = swapped(near_term, "head", 1)
     part_rows = q_cols + kv_cols
     (give,) = kernel_call(
         pass_on_kernel,
         (shape((blocks * (cut + part_rows), rows), bf16),),
-        (pair_sum, attn, dv_t, *columns),
-        in_vmem=range(1, 3 + blocks // 2),
+        (pair_sum, near_got, attn, dv_t, *columns),
+        in_vmem=range(2, 4 + blocks // 2),
         room=4,
     )
     grad_wvalue, grad_woutput, weights_done = kernel_call(
@@ -487,19 +484,11 @@
         ),
         room=8,
     )
-    (far_sum,) = kernel_call(
-        far_sum_kernel,
-        (shape((model // groups, rows), f32),),
-        (weights_done, own_term, swapped(pair_sum, "head", 2)),
-        in_vmem=range(1, 3),
-        moved=10 * rows * (model // groups),
-        room=4,
-    )
     (grad_input,) = kernel_call(
         sum_kernel,
         (shape((model // groups, rows), bf16),),
-        (far_sum, swapped(near_term, "head", 1)),
-        in_vmem=range(2),
+        (weights_done, own_term, near_got, swapped(pair_sum, "head", 2)),
+        in_vmem=range(1, 4),
         moved=4 * groups * (model // groups) * rows,
     )
     return (grad_input.T, grad_wvalue, grad_woutput.T)

time: 47.7 us -> 55.3 us (1.16)
  waiting for transfers between devices: 11.7 us -> 20.3 us
  starting transfers between devices: 18.7 us -> 17.7 us
    ppermute x15, waiting for transfers between devices: 11.7 us -> 20.3 us  [swapped(): lax.ppermute(value, axis, [(place, place ^ apart) for place in range(coun...]
    ppermute x15, starting transfers between devices: 18.7 us -> 17.7 us  [swapped(): lax.ppermute(value, axis, [(place, place ^ apart) for place in range(coun...]
    pallas_call x11 -> x10, Pallas kernels: 14.4 us -> 14.4 us  [kernel_call(): pl.pallas_call(body, out_shape=outs, in_specs=[vmem if place in in_vmem e...]
  transfers between devices with their start and end apart: 15 -> 15, of which waited for: 6 -> 6; matrix products, arithmetic and copies ran while one was open for 0% -> 0% of each run, Pallas kernels for 21% -> 9%
where the time goes in v22:
time: 55.3 us; the launch traced here: 55.1 us
  waiting for transfers between devices  20.3 us (37%)
  starting transfers between devices  17.7 us (32%)
  Pallas kernels  14.4 us (26%)
  local copies, waits for them, and re-layouts  2.01 us (4%)
  between operations  0.78 us (1%)
    ppermute x15, waiting for transfers between devices, swapped(): lax.ppermute(value, axis, [(place, place ^ apart) for place in range(coun...  20.3 us
    ppermute x15, starting transfers between devices, swapped(): lax.ppermute(value, axis, [(place, place ^ apart) for place in range(coun...  17.7 us
    pallas_call x10, Pallas kernels, kernel_call(): pl.pallas_call(body, out_shape=outs, in_specs=[vmem if place in in_vmem e...  14.4 us
    unnamed x12, local copies, waits for them, and re-layouts  2.01 us
  transfers between devices with their start and end apart: 15, of which 6 were waited for; matrix products, arithmetic and copies ran while one was open for 0% of the time, Pallas kernels for 9%

profile of v22, /device:TPU:0, one launch (start us, length us, event | category | flops | bytes accessed | tf_op | source)
XLA Modules:
  0.0 55.1 jit_solution(14643863664973547545)
XLA Ops:
  0.6 3.5 %shard_map.112 = (bf16[128,768]{1,0:T(8,128)(2,1)}, bf16[128,768]{1,0:T(8,128)(2,1)}) custom-call(bf16[128,2304]{1,0:T(8,128)(2,1)} %cot_ref.1, bf16[512,2304]{1,0:T(8,128)(2,1)} %weight_hbm.1, bf16[128,512]{1,0:T(8,128)(2,1)} %q_hbm.1, bf16[128,256]{1,0:T(8,128)(2,1)} %k_hbm.1, bf16[128,256]{1,0:T(8,128)(2,1)} %v_hbm.1), custom_call_target="tpu_custom_call" | custom-call | flops 301989888 | bytes 2949120 | tf_op jit(solution)/shard_map/pallas_call | solution.py:330
  4.1 3.0 %collective-permute-start = (bf16[128,768]{1,0:T(8,128)(2,1)}, bf16[128,768]{1,0:T(8,128)(2,1)S(1)}, u32[]{:S(2)}, u32[]{:S(2)}) collective-permute-start(bf16[128,768]{1,0:T(8,128)(2,1)} %get-tuple-element.21.block_ref), channel_id=1, source_target_pairs={{0,8},{4,12},{8,0},{12,4},{16,24},{20,28},{24,16},{28,20},{1,9},{5... | collective-permute-start | bytes 589832 | tf_op jit(solution)/shard_map/ppermute | solution.py:343
  7.1 0.7 %collective-permute-start.1 = (bf16[128,768]{1,0:T(8,128)(2,1)}, bf16[128,768]{1,0:T(8,128)(2,1)S(1)}, u32[]{:S(2)}, u32[]{:S(2)}) collective-permute-start(bf16[128,768]{1,0:T(8,128)(2,1)} %get-tuple-element.22), channel_id=1, source_target_pairs={{0,20},{4,16},{8,28},{12,24},{16,4},{20,0},{24,12},{28,8},{1,21},{... | collective-permute-start | bytes 589832 | tf_op jit(solution)/shard_map/ppermute | solution.py:343
  7.8 0.9 %collective-permute-start.4 = (bf16[128,768]{1,0:T(8,128)(2,1)}, bf16[128,768]{1,0:T(8,128)(2,1)S(1)}, u32[]{:S(2)}, u32[]{:S(2)}) collective-permute-start(bf16[128,768]{1,0:T(8,128)(2,1)} %get-tuple-element.21.block_ref), channel_id=1, source_target_pairs={{0,16},{4,20},{8,24},{12,28},{16,0},{20,4},{24,8},{28,12},{1,17},{... | collective-permute-start | bytes 589832 | tf_op jit(solution)/shard_map/ppermute | solution.py:343
  9.3 3.4 %collective-permute-done._.refs_2_ = bf16[128,768]{1,0:T(8,128)(2,1)S(1)} collective-permute-done((bf16[128,768]{1,0:T(8,128)(2,1)}, bf16[128,768]{1,0:T(8,128)(2,1)S(1)}, u32[]{:S(2)}, u32[]{:S(2)}) %collective-permute-start) | collective-permute-done | bytes 196640 | tf_op jit(solution)/shard_map/ppermute | solution.py:343
  12.7 2.2 %collective-permute-start.5 = (bf16[128,768]{1,0:T(8,128)(2,1)S(1)}, bf16[128,768]{1,0:T(8,128)(2,1)S(1)}, u32[]{:S(2)}, u32[]{:S(2)}) collective-permute-start(bf16[128,768]{1,0:T(8,128)(2,1)S(1)} %collective-permute-done._.refs_2_), channel_id=1, source_target_pairs={{0,16},{4,20},{8,24},{12,28},{16,0},{20,4},{24,8},{28,12},{1,17},{... | collective-permute-start | bytes 589832 | tf_op jit(solution)/shard_map/ppermute | solution.py:343
  14.9 1.7 %collective-permute-start.6 = (bf16[128,768]{1,0:T(8,128)(2,1)S(1)}, bf16[128,768]{1,0:T(8,128)(2,1)S(1)}, u32[]{:S(2)}, u32[]{:S(2)}) collective-permute-start(bf16[128,768]{1,0:T(8,128)(2,1)S(1)} %collective-permute-done.1.__.refs_5_), channel_id=1, source_target_pairs={{0,8},{4,12},{8,0},{12,4},{16,24},{20,28},{24,16},{28,20},{1,9},{5... | collective-permute-start | bytes 589832 | tf_op jit(solution)/shard_map/ppermute | solution.py:343
  16.6 1.1 %copy-done.4 = bf16[128,2304]{1,0:T(8,128)(2,1)S(1)} copy-done((bf16[128,2304]{1,0:T(8,128)(2,1)S(1)}, bf16[128,2304]{1,0:T(8,128)(2,1)}, u32[]{:S(2)}) %copy-start.4) | copy-done | bytes 589848
  17.7 0.9 %copy-done.5 = bf16[128,768]{1,0:T(8,128)(2,1)S(1)} copy-done((bf16[128,768]{1,0:T(8,128)(2,1)S(1)}, bf16[128,768]{1,0:T(8,128)(2,1)}, u32[]{:S(2)}) %copy-start.5) | copy-done | bytes 196632
  19.2 3.8 %collective-permute-done.5.refs_6_ = bf16[128,768]{1,0:T(8,128)(2,1)S(1)} collective-permute-done((bf16[128,768]{1,0:T(8,128)(2,1)S(1)}, bf16[128,768]{1,0:T(8,128)(2,1)S(1)}, u32[]{:S(2)}, u32[]{:S(2)}) %collective-permute-start.5) | collective-permute-done | bytes 196640 | tf_op jit(solution)/shard_map/ppermute | solution.py:343
  23.0 4.9 %shard_map.114 = (bf16[128,512]{1,0:T(8,128)(2,1)S(1)}, bf16[128,512]{1,0:T(8,128)(2,1)S(1)}, bf16[256,1024]{1,0:T(8,128)(2,1)S(1)}, bf16[1024,2048]{1,0:T(8,128)(2,1)S(1)}, bf16[128,2048]{1,0:T(8,128)(2,1)S(1)}) custom-call(bf16[128,768]{1,0:T(8,128)(2,1)S(1)} %get-tuple-element.23.refs_0_, bf16[128,768]{1,0:T(8,128)(2,1)S(1)} %collective-permute-done.2.refs_1_, ...), custom_call_target="tpu_custom_call" | custom-call | flops 2147483648 | bytes 1572864 | tf_op jit(solution)/shard_map/pallas_call | solution.py:330
  28.0 1.2 %collective-permute-start.11 = (bf16[2,2,288,128]{3,2,1,0:T(8,128)(2,1)S(1)}, bf16[2,2,288,128]{3,2,1,0:T(8,128)(2,1)S(1)}, u32[]{:S(2)}, u32[]{:S(2)}) collective-permute-start(bf16[2,2,288,128]{3,2,1,0:T(8,128)(2,1)S(1)} %get-tuple-element.33), channel_id=1, source_target_pairs={{0,16},{4,20},{8,24},{12,28},{16,0},{20,4},{24,8},{28,12},{1,17},{... | collective-permute-start | bytes 884744 | tf_op jit(solution)/shard_map/ppermute | solution.py:343
  29.3 2.2 %collective-permute-start.12 = (bf16[2,2,288,128]{3,2,1,0:T(8,128)(2,1)S(1)}, bf16[2,2,288,128]{3,2,1,0:T(8,128)(2,1)S(1)}, u32[]{:S(2)}, u32[]{:S(2)}) collective-permute-start(bf16[2,2,288,128]{3,2,1,0:T(8,128)(2,1)S(1)} %get-tuple-element.34), channel_id=1, source_target_pairs={{0,24},{4,28},{8,16},{12,20},{16,8},{20,12},{24,0},{28,4},{1,25},{... | collective-permute-start | bytes 884744 | tf_op jit(solution)/shard_map/ppermute | solution.py:343
  31.5 0.5 shard_map.117
  32.1 1.6 %collective-permute-start.8 = (bf16[576,128]{1,0:T(8,128)(2,1)S(1)}, bf16[576,128]{1,0:T(8,128)(2,1)S(1)}, u32[]{:S(2)}, u32[]{:S(2)}) collective-permute-start(bf16[576,128]{1,0:T(8,128)(2,1)S(1)} %shard_map.117), channel_id=1, source_target_pairs={{0,1},{1,0},{2,3},{3,2},{4,5},{5,4},{6,7},{7,6},{8,9},{9,8},{10,11... | collective-permute-start | bytes 442376 | tf_op jit(solution)/shard_map/ppermute | solution.py:343
  33.7 1.1 %shard_map.116 = (bf16[576,128]{1,0:T(8,128)(2,1)S(1)}, bf16[576,128]{1,0:T(8,128)(2,1)S(1)}, f32[576,128]{1,0:T(8,128)S(1)}) custom-call(bf16[128,512]{1,0:T(8,128)(2,1)S(1)} %get-tuple-element.27.own_ref, bf16[128,512]{1,0:T(8,128)(2,1)S(1)} %collective-permute-done.7.far_ref, bf16[2304,512]{1,0:T(8,128)(2,1)S(1)} %copy-done, ...), custom_call_target="tpu_custom_call" | custom-call | flops 452984832 | bytes 3538944 | tf_op jit(solution)/shard_map/pallas_call | solution.py:330
  34.8 0.5 collective-permute-start.9
  35.3 1.0 %shard_map.115._.dv_t_ref = bf16[128,1024]{1,0:T(8,128)(2,1)S(1)} custom-call(bf16[1024,2048]{1,0:T(8,128)(2,1)S(1)} %get-tuple-element.25.prob_ref, bf16[128,2048]{1,0:T(8,128)(2,1)S(1)} %get-tuple-element.26.grad_t_ref), custom_call_target="tpu_custom_call" | custom-call | flops 268435456 | bytes 4194304 | tf_op jit(solution)/shard_map/pallas_call | solution.py:330
  36.3 1.8 %collective-permute-done.8.arrived_ref = bf16[576,128]{1,0:T(8,128)(2,1)S(1)} collective-permute-done((bf16[576,128]{1,0:T(8,128)(2,1)S(1)}, bf16[576,128]{1,0:T(8,128)(2,1)S(1)}, u32[]{:S(2)}, u32[]{:S(2)}) %collective-permute-start.8) | collective-permute-done | bytes 147488 | tf_op jit(solution)/shard_map/ppermute | solution.py:343
  38.2 5.7 %collective-permute-done.12.refs_3_ = bf16[2,2,288,128]{3,2,1,0:T(8,128)(2,1)S(1)} collective-permute-done((bf16[2,2,288,128]{3,2,1,0:T(8,128)(2,1)S(1)}, bf16[2,2,288,128]{3,2,1,0:T(8,128)(2,1)S(1)}, u32[]{:S(2)}, u32[]{:S(2)}) %collective-permute-start.12) | collective-permute-done | bytes 294944 | tf_op jit(solution)/shard_map/ppermute | solution.py:343
  44.1 2.7 %collective-permute-start.14 = (bf16[576,128]{1,0:T(8,128)(2,1)S(1)}, bf16[576,128]{1,0:T(8,128)(2,1)S(1)}, u32[]{:S(2)}, u32[]{:S(2)}) collective-permute-start(bf16[576,128]{1,0:T(8,128)(2,1)S(1)} %shard_map.118._), channel_id=1, source_target_pairs={{0,2},{1,3},{2,0},{3,1},{4,6},{5,7},{6,4},{7,5},{8,10},{9,11},{10,... | collective-permute-start | bytes 442376 | tf_op jit(solution)/shard_map/ppermute | solution.py:343
  47.2 2.1 %shard_map.120 = (f32[288,256]{1,0:T(8,128)}, f32[288,512]{1,0:T(8,128)}, f32[8,128]{1,0:T(8,128)S(1)}) custom-call(bf16[256,1024]{1,0:T(8,128)(2,1)S(1)} %get-tuple-element.24.attn_ref, bf16[128,1024]{1,0:T(8,128)(2,1)S(1)} %shard_map.115._.dv_t_ref, bf16[5376,128]{1,0:T(8,128)(2,1)S(1)} %collective-permute-done.13.got_ref, ...), custom_call_target="tpu_custom_call" | custom-call | tf_op jit(solution)/shard_map/pallas_call | solution.py:330
  49.3 5.2 %collective-permute-done.14.refs_1_ = bf16[576,128]{1,0:T(8,128)(2,1)S(1)} collective-permute-done((bf16[576,128]{1,0:T(8,128)(2,1)S(1)}, bf16[576,128]{1,0:T(8,128)(2,1)S(1)}, u32[]{:S(2)}, u32[]{:S(2)}) %collective-permute-start.14) | collective-permute-done | bytes 147488 | tf_op jit(solution)/shard_map/ppermute | solution.py:343
  54.4 0.7 %shard_map.121 = bf16[576,128]{1,0:T(8,128)(2,1)} custom-call(f32[8,128]{1,0:T(8,128)S(1)} %get-tuple-element.35._, f32[576,128]{1,0:T(8,128)S(1)} %get-tuple-element.36.own_ref, bf16[576,128]{1,0:T(8,128)(2,1)S(1)} %collective-permute-done.9.__.refs_0_, bf16[576,128]{1,0:T(8,128)(2,1)S(1)} %collective-permute-done.14.refs_1_), custom_call_target="tpu_custom_call" | custom-call | bytes 1179648 | tf_op jit(solution)/shard_map/pallas_call | solution.py:330
  (28 shorter events, 2.0 us)
Async XLA Ops:
  0.6 16.0 %copy-start.3 = (bf16[128,2304]{1,0:T(8,128)(2,1)S(1)}, bf16[128,2304]{1,0:T(8,128)(2,1)}, u32[]{:S(2)}) copy-start(bf16[128,2304]{1,0:T(8,128)(2,1)} %cot_ref.1) | copy-start | bytes 1769476
  4.1 8.6 %collective-permute-start = (bf16[128,768]{1,0:T(8,128)(2,1)}, bf16[128,768]{1,0:T(8,128)(2,1)S(1)}, u32[]{:S(2)}, u32[]{:S(2)}) collective-permute-start(bf16[128,768]{1,0:T(8,128)(2,1)} %get-tuple-element.21.block_ref), channel_id=1, source_target_pairs={{0,8},{4,12},{8,0},{12,4},{16,24},{20,28},{24,16},{28,20},{1,9},{5... | collective-permute-start | bytes 589832 | tf_op jit(solution)/shard_map/ppermute | solution.py:343
  7.1 7.8 %collective-permute-start.1 = (bf16[128,768]{1,0:T(8,128)(2,1)}, bf16[128,768]{1,0:T(8,128)(2,1)S(1)}, u32[]{:S(2)}, u32[]{:S(2)}) collective-permute-start(bf16[128,768]{1,0:T(8,128)(2,1)} %get-tuple-element.22), channel_id=1, source_target_pairs={{0,20},{4,16},{8,28},{12,24},{16,4},{20,0},{24,12},{28,8},{1,21},{... | collective-permute-start | bytes 589832 | tf_op jit(solution)/shard_map/ppermute | solution.py:343
  7.8 11.3 %collective-permute-start.4 = (bf16[128,768]{1,0:T(8,128)(2,1)}, bf16[128,768]{1,0:T(8,128)(2,1)S(1)}, u32[]{:S(2)}, u32[]{:S(2)}) collective-permute-start(bf16[128,768]{1,0:T(8,128)(2,1)} %get-tuple-element.21.block_ref), channel_id=1, source_target_pairs={{0,16},{4,20},{8,24},{12,28},{16,0},{20,4},{24,8},{28,12},{1,17},{... | collective-permute-start | bytes 589832 | tf_op jit(solution)/shard_map/ppermute | solution.py:343
  8.7 10.5 %collective-permute-start.3 = (bf16[128,768]{1,0:T(8,128)(2,1)}, bf16[128,768]{1,0:T(8,128)(2,1)S(1)}, u32[]{:S(2)}, u32[]{:S(2)}) collective-permute-start(bf16[128,768]{1,0:T(8,128)(2,1)} %get-tuple-element.22), channel_id=1, source_target_pairs={{0,12},{4,8},{8,4},{12,0},{16,28},{20,24},{24,20},{28,16},{1,13},{... | collective-permute-start | bytes 589832 | tf_op jit(solution)/shard_map/ppermute | solution.py:343
  8.9 10.3 %collective-permute-start.2 = (bf16[128,768]{1,0:T(8,128)(2,1)}, bf16[128,768]{1,0:T(8,128)(2,1)S(1)}, u32[]{:S(2)}, u32[]{:S(2)}) collective-permute-start(bf16[128,768]{1,0:T(8,128)(2,1)} %get-tuple-element.22), channel_id=1, source_target_pairs={{0,4},{4,0},{8,12},{12,8},{16,20},{20,16},{24,28},{28,24},{1,5},{5... | collective-permute-start | bytes 589832 | tf_op jit(solution)/shard_map/ppermute | solution.py:343
  12.7 10.2 %collective-permute-start.5 = (bf16[128,768]{1,0:T(8,128)(2,1)S(1)}, bf16[128,768]{1,0:T(8,128)(2,1)S(1)}, u32[]{:S(2)}, u32[]{:S(2)}) collective-permute-start(bf16[128,768]{1,0:T(8,128)(2,1)S(1)} %collective-permute-done._.refs_2_), channel_id=1, source_target_pairs={{0,16},{4,20},{8,24},{12,28},{16,0},{20,4},{24,8},{28,12},{1,17},{... | collective-permute-start | bytes 589832 | tf_op jit(solution)/shard_map/ppermute | solution.py:343
  14.9 8.1 %collective-permute-start.6 = (bf16[128,768]{1,0:T(8,128)(2,1)S(1)}, bf16[128,768]{1,0:T(8,128)(2,1)S(1)}, u32[]{:S(2)}, u32[]{:S(2)}) collective-permute-start(bf16[128,768]{1,0:T(8,128)(2,1)S(1)} %collective-permute-done.1.__.refs_5_), channel_id=1, source_target_pairs={{0,8},{4,12},{8,0},{12,4},{16,24},{20,28},{24,16},{28,20},{1,9},{5... | collective-permute-start | bytes 589832 | tf_op jit(solution)/shard_map/ppermute | solution.py:343
  16.6 1.1 %copy-start.4 = (bf16[128,2304]{1,0:T(8,128)(2,1)S(1)}, bf16[128,2304]{1,0:T(8,128)(2,1)}, u32[]{:S(2)}) copy-start(bf16[128,2304]{1,0:T(8,128)(2,1)} %normed_ref.1) | copy-start | bytes 1769476
  17.7 0.9 %copy-start.5 = (bf16[128,768]{1,0:T(8,128)(2,1)S(1)}, bf16[128,768]{1,0:T(8,128)(2,1)}, u32[]{:S(2)}) copy-start(bf16[128,768]{1,0:T(8,128)(2,1)} %get-tuple-element.21.block_ref) | copy-start | bytes 589828
  23.0 8.5 %copy-start = (bf16[2304,512]{1,0:T(8,128)(2,1)S(1)}, bf16[2304,512]{1,0:T(8,128)(2,1)}, u32[]{:S(2)}) copy-start(bf16[2304,512]{1,0:T(8,128)(2,1)} %wq_ref.3) | copy-start | bytes 7077892
  23.0 8.5 %copy-start.1 = (bf16[2304,256]{1,0:T(8,128)(2,1)S(1)}, bf16[2304,256]{1,0:T(8,128)(2,1)}, u32[]{:S(2)}) copy-start(bf16[2304,256]{1,0:T(8,128)(2,1)} %wk_ref.3) | copy-start | bytes 3538948
  23.0 8.6 %copy-start.2 = (bf16[2304,256]{1,0:T(8,128)(2,1)S(1)}, bf16[2304,256]{1,0:T(8,128)(2,1)}, u32[]{:S(2)}) copy-start(bf16[2304,256]{1,0:T(8,128)(2,1)} %wv_ref.3) | copy-start | bytes 3538948
  27.9 3.6 %collective-permute-start.7 = (bf16[128,512]{1,0:T(8,128)(2,1)S(1)}, bf16[128,512]{1,0:T(8,128)(2,1)S(1)}, u32[]{:S(2)}, u32[]{:S(2)}) collective-permute-start(bf16[128,512]{1,0:T(8,128)(2,1)S(1)} %get-tuple-element.28), channel_id=1, source_target_pairs={{0,4},{4,0},{8,12},{12,8},{16,20},{20,16},{24,28},{28,24},{1,5},{5... | collective-permute-start | bytes 393224 | tf_op jit(solution)/shard_map/ppermute | solution.py:343
  28.0 10.2 %collective-permute-start.10 = (bf16[2,2,288,128]{3,2,1,0:T(8,128)(2,1)S(1)}, bf16[2,2,288,128]{3,2,1,0:T(8,128)(2,1)S(1)}, u32[]{:S(2)}, u32[]{:S(2)}) collective-permute-start(bf16[2,2,288,128]{3,2,1,0:T(8,128)(2,1)S(1)} %get-tuple-element.32), channel_id=1, source_target_pairs={{0,8},{4,12},{8,0},{12,4},{16,24},{20,28},{24,16},{28,20},{1,9},{5... | collective-permute-start | bytes 884744 | tf_op jit(solution)/shard_map/ppermute | solution.py:343
  28.0 10.2 %collective-permute-start.11 = (bf16[2,2,288,128]{3,2,1,0:T(8,128)(2,1)S(1)}, bf16[2,2,288,128]{3,2,1,0:T(8,128)(2,1)S(1)}, u32[]{:S(2)}, u32[]{:S(2)}) collective-permute-start(bf16[2,2,288,128]{3,2,1,0:T(8,128)(2,1)S(1)} %get-tuple-element.33), channel_id=1, source_target_pairs={{0,16},{4,20},{8,24},{12,28},{16,0},{20,4},{24,8},{28,12},{1,17},{... | collective-permute-start | bytes 884744 | tf_op jit(solution)/shard_map/ppermute | solution.py:343
  29.3 14.6 %collective-permute-start.12 = (bf16[2,2,288,128]{3,2,1,0:T(8,128)(2,1)S(1)}, bf16[2,2,288,128]{3,2,1,0:T(8,128)(2,1)S(1)}, u32[]{:S(2)}, u32[]{:S(2)}) collective-permute-start(bf16[2,2,288,128]{3,2,1,0:T(8,128)(2,1)S(1)} %get-tuple-element.34), channel_id=1, source_target_pairs={{0,24},{4,28},{8,16},{12,20},{16,8},{20,12},{24,0},{28,4},{1,25},{... | collective-permute-start | bytes 884744 | tf_op jit(solution)/shard_map/ppermute | solution.py:343
  32.1 6.1 %collective-permute-start.8 = (bf16[576,128]{1,0:T(8,128)(2,1)S(1)}, bf16[576,128]{1,0:T(8,128)(2,1)S(1)}, u32[]{:S(2)}, u32[]{:S(2)}) collective-permute-start(bf16[576,128]{1,0:T(8,128)(2,1)S(1)} %shard_map.117), channel_id=1, source_target_pairs={{0,1},{1,0},{2,3},{3,2},{4,5},{5,4},{6,7},{7,6},{8,9},{9,8},{10,11... | collective-permute-start | bytes 442376 | tf_op jit(solution)/shard_map/ppermute | solution.py:343
  34.8 9.0 %collective-permute-start.9 = (bf16[576,128]{1,0:T(8,128)(2,1)S(1)}, bf16[576,128]{1,0:T(8,128)(2,1)S(1)}, u32[]{:S(2)}, u32[]{:S(2)}) collective-permute-start(bf16[576,128]{1,0:T(8,128)(2,1)S(1)} %get-tuple-element.30), channel_id=1, source_target_pairs={{0,1},{1,0},{2,3},{3,2},{4,5},{5,4},{6,7},{7,6},{8,9},{9,8},{10,11... | collective-permute-start | bytes 442376 | tf_op jit(solution)/shard_map/ppermute | solution.py:343
  44.0 3.2 %collective-permute-start.13 = (bf16[5376,128]{1,0:T(8,128)(2,1)S(1)}, bf16[5376,128]{1,0:T(8,128)(2,1)S(1)}, u32[]{:S(2)}, u32[]{:S(2)}) collective-permute-start(bf16[5376,128]{1,0:T(8,128)(2,1)S(1)} %shard_map.119), channel_id=1, source_target_pairs={{0,4},{4,0},{8,12},{12,8},{16,20},{20,16},{24,28},{28,24},{1,5},{5... | collective-permute-start | bytes 4128776 | tf_op jit(solution)/shard_map/ppermute | solution.py:343
  44.1 10.3 %collective-permute-start.14 = (bf16[576,128]{1,0:T(8,128)(2,1)S(1)}, bf16[576,128]{1,0:T(8,128)(2,1)S(1)}, u32[]{:S(2)}, u32[]{:S(2)}) collective-permute-start(bf16[576,128]{1,0:T(8,128)(2,1)S(1)} %shard_map.118._), channel_id=1, source_target_pairs={{0,2},{1,3},{2,0},{3,1},{4,6},{5,7},{6,4},{7,5},{8,10},{9,11},{10,... | collective-permute-start | bytes 442376 | tf_op jit(solution)/shard_map/ppermute | solution.py:343

commit v23 on v21

--- a/solution.py
+++ b/solution.py
@@ -123,8 +123,9 @@
             first += ref.shape[0]
 
 
-def attention_kernel(blocks, *refs):
-    attention_body(refs[:blocks], *refs[blocks:])
+def attention_kernel(blocks, late, *refs):
+    first = blocks + late
+    attention_body(refs[:blocks], *refs[first : first + 5], *refs[first + 5 + late :])
 
 
 def attention_body(
@@ -327,7 +328,7 @@
 
 
 def kernel_call(
-    body, outs, operands, in_vmem=(), scratch=(), flops=0, moved=0, room=16
+    body, outs, operands, in_vmem=(), scratch=(), flops=0, moved=0, room=16, aliases={}
 ):
     vmem = pl.BlockSpec(memory_space=pltpu.VMEM)
     hbm = pl.BlockSpec(memory_space=pltpu.HBM)
@@ -335,7 +336,8 @@
         body,
         out_shape=outs,
         in_specs=[vmem if place in in_vmem else hbm for place in range(len(operands))],
-        out_specs=(vmem,) * len(outs),
+        out_specs=tuple(hbm if place in aliases.values() else vmem for place in range(len(outs))),
+        input_output_aliases=aliases,
         scratch_shapes=list(scratch),
         compiler_params=pltpu.CompilerParams(vmem_limit_bytes=int(room * 1024 * 1024)),
         cost_estimate=pl.CostEstimate(flops=flops, bytes_accessed=moved, transcendentals=0),
@@ -403,20 +405,20 @@
         moved=8 * rows * model,
         room=8,
     )
-    columns = [columns[0]] + [
-        swapped(columns[chip], "seq", 2 * chip) for chip in range(1, blocks // 2)
-    ]
-    dx_own, dx_far, attn, prob, grad_t = kernel_call(
-        functools.partial(attention_kernel, blocks),
+    late = [chip for chip in range(1, blocks // 2) if not power_of_two(chip)]
+    dx_own, dx_far, attn, prob, grad_t, *passed = kernel_call(
+        functools.partial(attention_kernel, blocks, len(late)),
         (
             shape((rows, q_cols + 2 * kv_cols), bf16),
             shape((rows, q_cols + 2 * kv_cols), bf16),
             shape((q_cols, tokens), bf16),
             shape((tokens, tokens * QUERIES_PER_KEY), bf16),
             shape((HEAD_SIZE, tokens * QUERIES_PER_KEY), bf16),
-        ),
-        [held[apart] for apart in range(blocks)],
+        )
+        + tuple(shape(columns[chip].shape, bf16) for chip in late),
+        [held[apart] for apart in range(blocks)] + [columns[chip] for chip in late],
         in_vmem=range(blocks),
+        aliases={blocks + place: 5 + place for place in range(len(late))},
         scratch=(
             pltpu.VMEM((tokens, packed_cols), bf16),
             pltpu.VMEM((tokens, wide), f32),
@@ -433,6 +435,11 @@
         moved=2 * tokens * packed_cols,
     )
     dx_got = swapped(dx_far, "seq", 1)
+    for place, chip in enumerate(late):
+        columns[chip] = passed[place]
+    columns = [columns[0]] + [
+        swapped(columns[chip], "seq", 2 * chip) for chip in range(1, blocks // 2)
+    ]
     def terms_of(chosen):
         return kernel_call(
             functools.partial(input_terms_kernel, chosen),

time: 47.7 us -> 49.6 us (1.040)
  waiting for transfers between devices: 11.7 us -> 14.9 us
  starting transfers between devices: 18.7 us -> 17.3 us
    ppermute x15, waiting for transfers between devices: 11.7 us -> 14.9 us  [swapped(): lax.ppermute(value, axis, [(place, place ^ apart) for place in range(coun...]
    ppermute x15, starting transfers between devices: 18.7 us -> 17.3 us  [swapped(): lax.ppermute(value, axis, [(place, place ^ apart) for place in range(coun...]
  transfers between devices with their start and end apart: 15 -> 15, of which waited for: 6 -> 7; matrix products, arithmetic and copies ran while one was open for 0% -> 0% of each run, Pallas kernels for 21% -> 20%
where the time goes in v23:
time: 49.6 us; the launch traced here: 49.4 us
  starting transfers between devices  17.3 us (35%)
  waiting for transfers between devices  14.9 us (30%)
  Pallas kernels  14.4 us (29%)
  local copies, waits for them, and re-layouts  2.01 us (4%)
  between operations  0.75 us (2%)
    ppermute x15, starting transfers between devices, swapped(): lax.ppermute(value, axis, [(place, place ^ apart) for place in range(coun...  17.3 us
    ppermute x15, waiting for transfers between devices, swapped(): lax.ppermute(value, axis, [(place, place ^ apart) for place in range(coun...  14.9 us
    pallas_call x11, Pallas kernels, kernel_call(): pl.pallas_call(body, out_shape=outs, in_specs=[vmem if place in in_vmem e...  14.4 us
    unnamed x12, local copies, waits for them, and re-layouts  2.01 us
  transfers between devices with their start and end apart: 15, of which 7 were waited for; matrix products, arithmetic and copies ran while one was open for 0% of the time, Pallas kernels for 20%

profile of v23, /device:TPU:0, one launch (start us, length us, event | category | flops | bytes accessed | tf_op | source)
XLA Modules:
  0.0 49.4 jit_solution(10524942167056354751)
XLA Ops:
  0.6 3.5 %shard_map.112 = (bf16[128,768]{1,0:T(8,128)(2,1)}, bf16[128,768]{1,0:T(8,128)(2,1)}) custom-call(bf16[128,2304]{1,0:T(8,128)(2,1)} %cot_ref.1, bf16[512,2304]{1,0:T(8,128)(2,1)} %weight_hbm.1, bf16[128,512]{1,0:T(8,128)(2,1)} %q_hbm.1, bf16[128,256]{1,0:T(8,128)(2,1)} %k_hbm.1, bf16[128,256]{1,0:T(8,128)(2,1)} %v_hbm.1), custom_call_target="tpu_custom_call" | custom-call | flops 301989888 | bytes 2949120 | tf_op jit(solution)/shard_map/pallas_call | solution.py:335
  4.1 3.0 %collective-permute-start = (bf16[128,768]{1,0:T(8,128)(2,1)}, bf16[128,768]{1,0:T(8,128)(2,1)S(1)}, u32[]{:S(2)}, u32[]{:S(2)}) collective-permute-start(bf16[128,768]{1,0:T(8,128)(2,1)} %get-tuple-element.22.block_ref), channel_id=1, source_target_pairs={{0,8},{4,12},{8,0},{12,4},{16,24},{20,28},{24,16},{28,20},{1,9},{5... | collective-permute-start | bytes 589832 | tf_op jit(solution)/shard_map/ppermute | solution.py:349
  7.1 0.7 %collective-permute-start.1 = (bf16[128,768]{1,0:T(8,128)(2,1)}, bf16[128,768]{1,0:T(8,128)(2,1)S(1)}, u32[]{:S(2)}, u32[]{:S(2)}) collective-permute-start(bf16[128,768]{1,0:T(8,128)(2,1)} %get-tuple-element.23), channel_id=1, source_target_pairs={{0,20},{4,16},{8,28},{12,24},{16,4},{20,0},{24,12},{28,8},{1,21},{... | collective-permute-start | bytes 589832 | tf_op jit(solution)/shard_map/ppermute | solution.py:349
  7.8 0.9 %collective-permute-start.4 = (bf16[128,768]{1,0:T(8,128)(2,1)}, bf16[128,768]{1,0:T(8,128)(2,1)S(1)}, u32[]{:S(2)}, u32[]{:S(2)}) collective-permute-start(bf16[128,768]{1,0:T(8,128)(2,1)} %get-tuple-element.22.block_ref), channel_id=1, source_target_pairs={{0,16},{4,20},{8,24},{12,28},{16,0},{20,4},{24,8},{28,12},{1,17},{... | collective-permute-start | bytes 589832 | tf_op jit(solution)/shard_map/ppermute | solution.py:349
  9.3 3.4 %collective-permute-done._.refs_2_ = bf16[128,768]{1,0:T(8,128)(2,1)S(1)} collective-permute-done((bf16[128,768]{1,0:T(8,128)(2,1)}, bf16[128,768]{1,0:T(8,128)(2,1)S(1)}, u32[]{:S(2)}, u32[]{:S(2)}) %collective-permute-start) | collective-permute-done | bytes 196640 | tf_op jit(solution)/shard_map/ppermute | solution.py:349
  12.7 2.2 %collective-permute-start.5 = (bf16[128,768]{1,0:T(8,128)(2,1)S(1)}, bf16[128,768]{1,0:T(8,128)(2,1)S(1)}, u32[]{:S(2)}, u32[]{:S(2)}) collective-permute-start(bf16[128,768]{1,0:T(8,128)(2,1)S(1)} %collective-permute-done._.refs_2_), channel_id=1, source_target_pairs={{0,16},{4,20},{8,24},{12,28},{16,0},{20,4},{24,8},{28,12},{1,17},{... | collective-permute-start | bytes 589832 | tf_op jit(solution)/shard_map/ppermute | solution.py:349
  14.9 1.7 %collective-permute-start.6 = (bf16[128,768]{1,0:T(8,128)(2,1)S(1)}, bf16[128,768]{1,0:T(8,128)(2,1)S(1)}, u32[]{:S(2)}, u32[]{:S(2)}) collective-permute-start(bf16[128,768]{1,0:T(8,128)(2,1)S(1)} %collective-permute-done.1.__.refs_5_), channel_id=1, source_target_pairs={{0,8},{4,12},{8,0},{12,4},{16,24},{20,28},{24,16},{28,20},{1,9},{5... | collective-permute-start | bytes 589832 | tf_op jit(solution)/shard_map/ppermute | solution.py:349
  16.6 1.1 %copy-done.4 = bf16[128,2304]{1,0:T(8,128)(2,1)S(1)} copy-done((bf16[128,2304]{1,0:T(8,128)(2,1)S(1)}, bf16[128,2304]{1,0:T(8,128)(2,1)}, u32[]{:S(2)}) %copy-start.4) | copy-done | bytes 589848
  17.7 0.9 %copy-done.5 = bf16[128,768]{1,0:T(8,128)(2,1)S(1)} copy-done((bf16[128,768]{1,0:T(8,128)(2,1)S(1)}, bf16[128,768]{1,0:T(8,128)(2,1)}, u32[]{:S(2)}) %copy-start.5) | copy-done | bytes 196632
  19.5 1.1 %collective-permute-start.10 = (bf16[2,2,288,128]{3,2,1,0:T(8,128)(2,1)S(1)}, bf16[2,2,288,128]{3,2,1,0:T(8,128)(2,1)S(1)}, u32[]{:S(2)}, u32[]{:S(2)}) collective-permute-start(bf16[2,2,288,128]{3,2,1,0:T(8,128)(2,1)S(1)} %get-tuple-element.34), channel_id=1, source_target_pairs={{0,16},{4,20},{8,24},{12,28},{16,0},{20,4},{24,8},{28,12},{1,17},{... | collective-permute-start | bytes 884744 | tf_op jit(solution)/shard_map/ppermute | solution.py:349
  20.6 2.4 %collective-permute-done.5.refs_6_ = bf16[128,768]{1,0:T(8,128)(2,1)S(1)} collective-permute-done((bf16[128,768]{1,0:T(8,128)(2,1)S(1)}, bf16[128,768]{1,0:T(8,128)(2,1)S(1)}, u32[]{:S(2)}, u32[]{:S(2)}) %collective-permute-start.5) | collective-permute-done | bytes 196640 | tf_op jit(solution)/shard_map/ppermute | solution.py:349
  23.0 4.9 %shard_map.114 = (bf16[128,512]{1,0:T(8,128)(2,1)S(1)}, bf16[128,512]{1,0:T(8,128)(2,1)S(1)}, bf16[256,1024]{1,0:T(8,128)(2,1)S(1)}, bf16[1024,2048]{1,0:T(8,128...) custom-call(bf16[128,768]{1,0:T(8,128)(2,1)S(1)} %get-tuple-element., ...), custom_call_target="tpu_custom_call", output_to_operand_aliasing={{5}: (8, {})} | custom-call | flops 2147483648 | bytes 1572864 | tf_op jit(solution)/shard_map/pallas_call | solution.py:335
  27.9 0.7 %collective-permute-start.11 = (bf16[2,2,288,128]{3,2,1,0:T(8,128)(2,1)S(1)}, bf16[2,2,288,128]{3,2,1,0:T(8,128)(2,1)S(1)}, u32[]{:S(2)}, u32[]{:S(2)}) collective-permute-start(bf16[2,2,288,128]{3,2,1,0:T(8,128)(2,1)S(1)} %get-tuple-element.35), channel_id=1, source_target_pairs={{0,24},{4,28},{8,16},{12,20},{16,8},{20,12},{24,0},{28,4},{1,25},{... | collective-permute-start | bytes 884744 | tf_op jit(solution)/shard_map/ppermute | solution.py:349
  28.7 1.3 %collective-permute-done.7.far_ref = bf16[128,512]{1,0:T(8,128)(2,1)S(1)} collective-permute-done((bf16[128,512]{1,0:T(8,128)(2,1)S(1)}, bf16[128,512]{1,0:T(8,128)(2,1)S(1)}, u32[]{:S(2)}, u32[]{:S(2)}) %collective-permute-start.7) | collective-permute-done | bytes 131104 | tf_op jit(solution)/shard_map/ppermute | solution.py:349
  30.5 1.6 %collective-permute-start.8 = (bf16[576,128]{1,0:T(8,128)(2,1)S(1)}, bf16[576,128]{1,0:T(8,128)(2,1)S(1)}, u32[]{:S(2)}, u32[]{:S(2)}) collective-permute-start(bf16[576,128]{1,0:T(8,128)(2,1)S(1)} %shard_map.117), channel_id=1, source_target_pairs={{0,1},{1,0},{2,3},{3,2},{4,5},{5,4},{6,7},{7,6},{8,9},{9,8},{10,11... | collective-permute-start | bytes 442376 | tf_op jit(solution)/shard_map/ppermute | solution.py:349
  32.1 1.0 %shard_map.115._.dv_t_ref = bf16[128,1024]{1,0:T(8,128)(2,1)S(1)} custom-call(bf16[1024,2048]{1,0:T(8,128)(2,1)S(1)} %get-tuple-element.27.prob_ref, bf16[128,2048]{1,0:T(8,128)(2,1)S(1)} %get-tuple-element.28.grad_t_ref), custom_call_target="tpu_custom_call" | custom-call | flops 268435456 | bytes 4194304 | tf_op jit(solution)/shard_map/pallas_call | solution.py:335
  33.1 1.1 %shard_map.116 = (bf16[576,128]{1,0:T(8,128)(2,1)S(1)}, bf16[576,128]{1,0:T(8,128)(2,1)S(1)}, f32[576,128]{1,0:T(8,128)S(1)}) custom-call(bf16[128,512]{1,0:T(8,128)(2,1)S(1)} %get-tuple-element.29.own_ref, bf16[128,512]{1,0:T(8,128)(2,1)S(1)} %collective-permute-done.7.far_ref, bf16[2304,512]{1,0:T(8,128)(2,1)S(1)} %copy-done, ...), custom_call_target="tpu_custom_call" | custom-call | flops 452984832 | bytes 3538944 | tf_op jit(solution)/shard_map/pallas_call | solution.py:335
  34.2 2.2 %collective-permute-done.8.arrived_ref = bf16[576,128]{1,0:T(8,128)(2,1)S(1)} collective-permute-done((bf16[576,128]{1,0:T(8,128)(2,1)S(1)}, bf16[576,128]{1,0:T(8,128)(2,1)S(1)}, u32[]{:S(2)}, u32[]{:S(2)}) %collective-permute-start.8) | collective-permute-done | bytes 147488 | tf_op jit(solution)/shard_map/ppermute | solution.py:349
  36.5 1.3 %collective-permute-done.11.refs_3_ = bf16[2,2,288,128]{3,2,1,0:T(8,128)(2,1)S(1)} collective-permute-done((bf16[2,2,288,128]{3,2,1,0:T(8,128)(2,1)S(1)}, bf16[2,2,288,128]{3,2,1,0:T(8,128)(2,1)S(1)}, u32[]{:S(2)}, u32[]{:S(2)}) %collective-permute-start.11) | collective-permute-done | bytes 294944 | tf_op jit(solution)/shard_map/ppermute | solution.py:349
  38.0 2.6 %collective-permute-start.13 = (bf16[576,128]{1,0:T(8,128)(2,1)S(1)}, bf16[576,128]{1,0:T(8,128)(2,1)S(1)}, u32[]{:S(2)}, u32[]{:S(2)}) collective-permute-start(bf16[576,128]{1,0:T(8,128)(2,1)S(1)} %shard_map.118._), channel_id=1, source_target_pairs={{0,2},{1,3},{2,0},{3,1},{4,6},{5,7},{6,4},{7,5},{8,10},{9,11},{10,... | collective-permute-start | bytes 442376 | tf_op jit(solution)/shard_map/ppermute | solution.py:349
  40.7 1.6 %collective-permute-start.14 = (bf16[576,128]{1,0:T(8,128)(2,1)S(1)}, bf16[576,128]{1,0:T(8,128)(2,1)S(1)}, u32[]{:S(2)}, u32[]{:S(2)}) collective-permute-start(bf16[576,128]{1,0:T(8,128)(2,1)S(1)} %get-tuple-element.38), channel_id=1, source_target_pairs={{0,1},{1,0},{2,3},{3,2},{4,5},{5,4},{6,7},{7,6},{8,9},{9,8},{10,11... | collective-permute-start | bytes 442376 | tf_op jit(solution)/shard_map/ppermute | solution.py:349
  42.3 2.0 %shard_map.120 = (f32[288,256]{1,0:T(8,128)}, f32[288,512]{1,0:T(8,128)}, f32[8,128]{1,0:T(8,128)S(1)}) custom-call(bf16[256,1024]{1,0:T(8,128)(2,1)S(1)} %get-tuple-element.26.attn_ref, bf16[128,1024]{1,0:T(8,128)(2,1)S(1)} %shard_map.115._.dv_t_ref, bf16[5376,128]{1,0:T(8,128)(2,1)S(1)} %collective-permute-done.12.got_ref, ...), custom_call_target="tpu_custom_call" | custom-call | tf_op jit(solution)/shard_map/pallas_call | solution.py:335
  44.3 4.2 %collective-permute-done.13.arrived_ref = bf16[576,128]{1,0:T(8,128)(2,1)S(1)} collective-permute-done((bf16[576,128]{1,0:T(8,128)(2,1)S(1)}, bf16[576,128]{1,0:T(8,128)(2,1)S(1)}, u32[]{:S(2)}, u32[]{:S(2)}) %collective-permute-start.13) | collective-permute-done | bytes 147488 | tf_op jit(solution)/shard_map/ppermute | solution.py:349
  48.7 0.7 %shard_map.122 = bf16[576,128]{1,0:T(8,128)(2,1)} custom-call(f32[576,128]{1,0:T(8,128)S(1)} %shard_map.121.own_ref, bf16[576,128]{1,0:T(8,128)(2,1)S(1)} %collective-permute-done.14.refs_0_), custom_call_target="tpu_custom_call" | custom-call | bytes 1179648 | tf_op jit(solution)/shard_map/pallas_call | solution.py:335
  (29 shorter events, 2.6 us)
Async XLA Ops:
  0.6 16.0 %copy-start.3 = (bf16[128,2304]{1,0:T(8,128)(2,1)S(1)}, bf16[128,2304]{1,0:T(8,128)(2,1)}, u32[]{:S(2)}) copy-start(bf16[128,2304]{1,0:T(8,128)(2,1)} %cot_ref.1) | copy-start | bytes 1769476
  4.1 8.6 %collective-permute-start = (bf16[128,768]{1,0:T(8,128)(2,1)}, bf16[128,768]{1,0:T(8,128)(2,1)S(1)}, u32[]{:S(2)}, u32[]{:S(2)}) collective-permute-start(bf16[128,768]{1,0:T(8,128)(2,1)} %get-tuple-element.22.block_ref), channel_id=1, source_target_pairs={{0,8},{4,12},{8,0},{12,4},{16,24},{20,28},{24,16},{28,20},{1,9},{5... | collective-permute-start | bytes 589832 | tf_op jit(solution)/shard_map/ppermute | solution.py:349
  7.1 7.8 %collective-permute-start.1 = (bf16[128,768]{1,0:T(8,128)(2,1)}, bf16[128,768]{1,0:T(8,128)(2,1)S(1)}, u32[]{:S(2)}, u32[]{:S(2)}) collective-permute-start(bf16[128,768]{1,0:T(8,128)(2,1)} %get-tuple-element.23), channel_id=1, source_target_pairs={{0,20},{4,16},{8,28},{12,24},{16,4},{20,0},{24,12},{28,8},{1,21},{... | collective-permute-start | bytes 589832 | tf_op jit(solution)/shard_map/ppermute | solution.py:349
  7.8 11.3 %collective-permute-start.4 = (bf16[128,768]{1,0:T(8,128)(2,1)}, bf16[128,768]{1,0:T(8,128)(2,1)S(1)}, u32[]{:S(2)}, u32[]{:S(2)}) collective-permute-start(bf16[128,768]{1,0:T(8,128)(2,1)} %get-tuple-element.22.block_ref), channel_id=1, source_target_pairs={{0,16},{4,20},{8,24},{12,28},{16,0},{20,4},{24,8},{28,12},{1,17},{... | collective-permute-start | bytes 589832 | tf_op jit(solution)/shard_map/ppermute | solution.py:349
  8.7 10.8 %collective-permute-start.3 = (bf16[128,768]{1,0:T(8,128)(2,1)}, bf16[128,768]{1,0:T(8,128)(2,1)S(1)}, u32[]{:S(2)}, u32[]{:S(2)}) collective-permute-start(bf16[128,768]{1,0:T(8,128)(2,1)} %get-tuple-element.23), channel_id=1, source_target_pairs={{0,12},{4,8},{8,4},{12,0},{16,28},{20,24},{24,20},{28,16},{1,13},{... | collective-permute-start | bytes 589832 | tf_op jit(solution)/shard_map/ppermute | solution.py:349
  8.9 11.8 %collective-permute-start.2 = (bf16[128,768]{1,0:T(8,128)(2,1)}, bf16[128,768]{1,0:T(8,128)(2,1)S(1)}, u32[]{:S(2)}, u32[]{:S(2)}) collective-permute-start(bf16[128,768]{1,0:T(8,128)(2,1)} %get-tuple-element.23), channel_id=1, source_target_pairs={{0,4},{4,0},{8,12},{12,8},{16,20},{20,16},{24,28},{28,24},{1,5},{5... | collective-permute-start | bytes 589832 | tf_op jit(solution)/shard_map/ppermute | solution.py:349
  12.7 10.3 %collective-permute-start.5 = (bf16[128,768]{1,0:T(8,128)(2,1)S(1)}, bf16[128,768]{1,0:T(8,128)(2,1)S(1)}, u32[]{:S(2)}, u32[]{:S(2)}) collective-permute-start(bf16[128,768]{1,0:T(8,128)(2,1)S(1)} %collective-permute-done._.refs_2_), channel_id=1, source_target_pairs={{0,16},{4,20},{8,24},{12,28},{16,0},{20,4},{24,8},{28,12},{1,17},{... | collective-permute-start | bytes 589832 | tf_op jit(solution)/shard_map/ppermute | solution.py:349
  14.9 8.1 %collective-permute-start.6 = (bf16[128,768]{1,0:T(8,128)(2,1)S(1)}, bf16[128,768]{1,0:T(8,128)(2,1)S(1)}, u32[]{:S(2)}, u32[]{:S(2)}) collective-permute-start(bf16[128,768]{1,0:T(8,128)(2,1)S(1)} %collective-permute-done.1.__.refs_5_), channel_id=1, source_target_pairs={{0,8},{4,12},{8,0},{12,4},{16,24},{20,28},{24,16},{28,20},{1,9},{5... | collective-permute-start | bytes 589832 | tf_op jit(solution)/shard_map/ppermute | solution.py:349
  16.6 1.1 %copy-start.4 = (bf16[128,2304]{1,0:T(8,128)(2,1)S(1)}, bf16[128,2304]{1,0:T(8,128)(2,1)}, u32[]{:S(2)}) copy-start(bf16[128,2304]{1,0:T(8,128)(2,1)} %normed_ref.1) | copy-start | bytes 1769476
  17.7 0.9 %copy-start.5 = (bf16[128,768]{1,0:T(8,128)(2,1)S(1)}, bf16[128,768]{1,0:T(8,128)(2,1)}, u32[]{:S(2)}) copy-start(bf16[128,768]{1,0:T(8,128)(2,1)} %get-tuple-element.22.block_ref) | copy-start | bytes 589828
  19.1 17.3 %collective-permute-start.9 = (bf16[2,2,288,128]{3,2,1,0:T(8,128)(2,1)S(1)}, bf16[2,2,288,128]{3,2,1,0:T(8,128)(2,1)S(1)}, u32[]{:S(2)}, u32[]{:S(2)}) collective-permute-start(bf16[2,2,288,128]{3,2,1,0:T(8,128)(2,1)S(1)} %get-tuple-element.33), channel_id=1, source_target_pairs={{0,8},{4,12},{8,0},{12,4},{16,24},{20,28},{24,16},{28,20},{1,9},{5... | collective-permute-start | bytes 884744 | tf_op jit(solution)/shard_map/ppermute | solution.py:349
  19.5 17.0 %collective-permute-start.10 = (bf16[2,2,288,128]{3,2,1,0:T(8,128)(2,1)S(1)}, bf16[2,2,288,128]{3,2,1,0:T(8,128)(2,1)S(1)}, u32[]{:S(2)}, u32[]{:S(2)}) collective-permute-start(bf16[2,2,288,128]{3,2,1,0:T(8,128)(2,1)S(1)} %get-tuple-element.34), channel_id=1, source_target_pairs={{0,16},{4,20},{8,24},{12,28},{16,0},{20,4},{24,8},{28,12},{1,17},{... | collective-permute-start | bytes 884744 | tf_op jit(solution)/shard_map/ppermute | solution.py:349
  23.0 6.9 %copy-start = (bf16[2304,512]{1,0:T(8,128)(2,1)S(1)}, bf16[2304,512]{1,0:T(8,128)(2,1)}, u32[]{:S(2)}) copy-start(bf16[2304,512]{1,0:T(8,128)(2,1)} %wq_ref.3) | copy-start | bytes 7077892
  23.0 6.9 %copy-start.1 = (bf16[2304,256]{1,0:T(8,128)(2,1)S(1)}, bf16[2304,256]{1,0:T(8,128)(2,1)}, u32[]{:S(2)}) copy-start(bf16[2304,256]{1,0:T(8,128)(2,1)} %wk_ref.3) | copy-start | bytes 3538948
  23.0 6.9 %copy-start.2 = (bf16[2304,256]{1,0:T(8,128)(2,1)S(1)}, bf16[2304,256]{1,0:T(8,128)(2,1)}, u32[]{:S(2)}) copy-start(bf16[2304,256]{1,0:T(8,128)(2,1)} %wv_ref.3) | copy-start | bytes 3538948
  27.9 9.9 %collective-permute-start.11 = (bf16[2,2,288,128]{3,2,1,0:T(8,128)(2,1)S(1)}, bf16[2,2,288,128]{3,2,1,0:T(8,128)(2,1)S(1)}, u32[]{:S(2)}, u32[]{:S(2)}) collective-permute-start(bf16[2,2,288,128]{3,2,1,0:T(8,128)(2,1)S(1)} %get-tuple-element.35), channel_id=1, source_target_pairs={{0,24},{4,28},{8,16},{12,20},{16,8},{20,12},{24,0},{28,4},{1,25},{... | collective-permute-start | bytes 884744 | tf_op jit(solution)/shard_map/ppermute | solution.py:349
  28.6 1.3 %collective-permute-start.7 = (bf16[128,512]{1,0:T(8,128)(2,1)S(1)}, bf16[128,512]{1,0:T(8,128)(2,1)S(1)}, u32[]{:S(2)}, u32[]{:S(2)}) collective-permute-start(bf16[128,512]{1,0:T(8,128)(2,1)S(1)} %get-tuple-element.30), channel_id=1, source_target_pairs={{0,4},{4,0},{8,12},{12,8},{16,20},{20,16},{24,28},{28,24},{1,5},{5... | collective-permute-start | bytes 393224 | tf_op jit(solution)/shard_map/ppermute | solution.py:349
  30.5 6.0 %collective-permute-start.8 = (bf16[576,128]{1,0:T(8,128)(2,1)S(1)}, bf16[576,128]{1,0:T(8,128)(2,1)S(1)}, u32[]{:S(2)}, u32[]{:S(2)}) collective-permute-start(bf16[576,128]{1,0:T(8,128)(2,1)S(1)} %shard_map.117), channel_id=1, source_target_pairs={{0,1},{1,0},{2,3},{3,2},{4,5},{5,4},{6,7},{7,6},{8,9},{9,8},{10,11... | collective-permute-start | bytes 442376 | tf_op jit(solution)/shard_map/ppermute | solution.py:349
  38.0 4.3 %collective-permute-start.12 = (bf16[5376,128]{1,0:T(8,128)(2,1)S(1)}, bf16[5376,128]{1,0:T(8,128)(2,1)S(1)}, u32[]{:S(2)}, u32[]{:S(2)}) collective-permute-start(bf16[5376,128]{1,0:T(8,128)(2,1)S(1)} %shard_map.119), channel_id=1, source_target_pairs={{0,4},{4,0},{8,12},{12,8},{16,20},{20,16},{24,28},{28,24},{1,5},{5... | collective-permute-start | bytes 4128776 | tf_op jit(solution)/shard_map/ppermute | solution.py:349
  38.0 10.4 %collective-permute-start.13 = (bf16[576,128]{1,0:T(8,128)(2,1)S(1)}, bf16[576,128]{1,0:T(8,128)(2,1)S(1)}, u32[]{:S(2)}, u32[]{:S(2)}) collective-permute-start(bf16[576,128]{1,0:T(8,128)(2,1)S(1)} %shard_map.118._), channel_id=1, source_target_pairs={{0,2},{1,3},{2,0},{3,1},{4,6},{5,7},{6,4},{7,5},{8,10},{9,11},{10,... | collective-permute-start | bytes 442376 | tf_op jit(solution)/shard_map/ppermute | solution.py:349
  40.7 8.0 %collective-permute-start.14 = (bf16[576,128]{1,0:T(8,128)(2,1)S(1)}, bf16[576,128]{1,0:T(8,128)(2,1)S(1)}, u32[]{:S(2)}, u32[]{:S(2)}) collective-permute-start(bf16[576,128]{1,0:T(8,128)(2,1)S(1)} %get-tuple-element.38), channel_id=1, source_target_pairs={{0,1},{1,0},{2,3},{3,2},{4,5},{5,4},{6,7},{7,6},{8,9},{9,8},{10,11... | collective-permute-start | bytes 442376 | tf_op jit(solution)/shard_map/ppermute | solution.py:349

commit v24 on v21

--- a/solution.py
+++ b/solution.py
@@ -24,6 +24,7 @@
 
 
 NT = (((1,), (1,)), ((), ()))
+ones_rows = 16
 
 
 def dot_nt(left, right):
@@ -158,7 +159,8 @@
     key_cols = slice(heads * HEAD_SIZE, (heads + 1) * HEAD_SIZE)
     value_cols = slice((heads + 1) * HEAD_SIZE, (heads + 2) * HEAD_SIZE)
     grad_base = (heads + 2) * HEAD_SIZE
-    value_t_ref[...] = gathered_ref[:, value_cols].T
+    value_t_ref[:HEAD_SIZE] = gathered_ref[:, value_cols].T
+    value_t_ref[HEAD_SIZE:] = jnp.ones((ones_rows, tokens), jnp.bfloat16)
     key_t_ref[...] = gathered_ref[:, key_cols].T
     key_place = lax.broadcasted_iota(jnp.int32, (size, wide), 0)
     query_place = lax.broadcasted_iota(jnp.int32, (size, wide), 1) % size
@@ -192,15 +194,13 @@
         if step:
             next_top = scored(step - 1)
         top = jnp.max(top, axis=0, keepdims=True)
-        total = None
         for piece in range(step + 1):
             part = slice(piece * size, (piece + 1) * size)
             weights = jnp.exp2((score_ref[part] - top) * log2_scale)
             prob_ref[part, lanes] = weights.astype(jnp.bfloat16)
-            summed = jnp.sum(weights.reshape(size // 8, 8, wide), axis=0)
-            total = summed if total is None else total + summed
-        inverse = 1.0 / jnp.sum(total, axis=0, keepdims=True)
-        attn = dot_nn(value_t_ref[:, :span], prob_ref[:span, lanes]) * inverse
+        product = dot_nn(value_t_ref[:, :span], prob_ref[:span, lanes])
+        inverse = 1.0 / product[HEAD_SIZE : HEAD_SIZE + 1]
+        attn = product[:HEAD_SIZE] * inverse
         for h in range(heads):
             attn_ref[h * HEAD_SIZE : (h + 1) * HEAD_SIZE, own] = attn[
                 :, h * size : (h + 1) * size
@@ -423,7 +423,7 @@
             pltpu.VMEM((tokens, wide), f32),
             pltpu.VMEM((1, tokens * QUERIES_PER_KEY), f32),
             pltpu.VMEM((tokens * QUERIES_PER_KEY, HEAD_SIZE), bf16),
-            pltpu.VMEM((HEAD_SIZE, tokens), bf16),
+            pltpu.VMEM((HEAD_SIZE + ones_rows, tokens), bf16),
             pltpu.VMEM((HEAD_SIZE, tokens), bf16),
             pltpu.VMEM((HEAD_SIZE, wide), f32),
             pltpu.VMEM((2 * rows, HEAD_SIZE), f32),

time: 47.7 us -> 47.6 us (level)
  no operation moved by 1% of the time
where the time goes in v24:
time: 47.6 us; the launch traced here: 47.5 us
  starting transfers between devices  18.7 us (39%)
  Pallas kernels  14.4 us (30%)
  waiting for transfers between devices  11.6 us (24%)
  local copies, waits for them, and re-layouts  2.01 us (4%)
  between operations  0.77 us (2%)
    ppermute x15, starting transfers between devices, swapped(): lax.ppermute(value, axis, [(place, place ^ apart) for place in range(coun...  18.7 us
    pallas_call x11, Pallas kernels, kernel_call(): pl.pallas_call(body, out_shape=outs, in_specs=[vmem if place in in_vmem e...  14.4 us
    ppermute x15, waiting for transfers between devices, swapped(): lax.ppermute(value, axis, [(place, place ^ apart) for place in range(coun...  11.6 us
    unnamed x12, local copies, waits for them, and re-layouts  2.01 us
  transfers between devices with their start and end apart: 15, of which 6 were waited for; matrix products, arithmetic and copies ran while one was open for 0% of the time, Pallas kernels for 21%

profile of v24, /device:TPU:0, one launch (start us, length us, event | category | flops | bytes accessed | tf_op | source)
XLA Modules:
  0.0 47.5 jit_solution(1674512935349449234)
XLA Ops:
  0.6 3.5 %shard_map.112 = (bf16[128,768]{1,0:T(8,128)(2,1)}, bf16[128,768]{1,0:T(8,128)(2,1)}) custom-call(bf16[128,2304]{1,0:T(8,128)(2,1)} %cot_ref.1, bf16[512,2304]{1,0:T(8,128)(2,1)} %weight_hbm.1, bf16[128,512]{1,0:T(8,128)(2,1)} %q_hbm.1, bf16[128,256]{1,0:T(8,128)(2,1)} %k_hbm.1, bf16[128,256]{1,0:T(8,128)(2,1)} %v_hbm.1), custom_call_target="tpu_custom_call" | custom-call | flops 301989888 | bytes 2949120 | tf_op jit(solution)/shard_map/pallas_call | solution.py:334
  4.1 3.0 %collective-permute-start = (bf16[128,768]{1,0:T(8,128)(2,1)}, bf16[128,768]{1,0:T(8,128)(2,1)S(1)}, u32[]{:S(2)}, u32[]{:S(2)}) collective-permute-start(bf16[128,768]{1,0:T(8,128)(2,1)} %get-tuple-element.21.block_ref), channel_id=1, source_target_pairs={{0,8},{4,12},{8,0},{12,4},{16,24},{20,28},{24,16},{28,20},{1,9},{5... | collective-permute-start | bytes 589832 | tf_op jit(solution)/shard_map/ppermute | solution.py:347
  7.1 0.7 %collective-permute-start.1 = (bf16[128,768]{1,0:T(8,128)(2,1)}, bf16[128,768]{1,0:T(8,128)(2,1)S(1)}, u32[]{:S(2)}, u32[]{:S(2)}) collective-permute-start(bf16[128,768]{1,0:T(8,128)(2,1)} %get-tuple-element.22), channel_id=1, source_target_pairs={{0,20},{4,16},{8,28},{12,24},{16,4},{20,0},{24,12},{28,8},{1,21},{... | collective-permute-start | bytes 589832 | tf_op jit(solution)/shard_map/ppermute | solution.py:347
  7.8 0.9 %collective-permute-start.4 = (bf16[128,768]{1,0:T(8,128)(2,1)}, bf16[128,768]{1,0:T(8,128)(2,1)S(1)}, u32[]{:S(2)}, u32[]{:S(2)}) collective-permute-start(bf16[128,768]{1,0:T(8,128)(2,1)} %get-tuple-element.21.block_ref), channel_id=1, source_target_pairs={{0,16},{4,20},{8,24},{12,28},{16,0},{20,4},{24,8},{28,12},{1,17},{... | collective-permute-start | bytes 589832 | tf_op jit(solution)/shard_map/ppermute | solution.py:347
  9.3 3.4 %collective-permute-done._.refs_2_ = bf16[128,768]{1,0:T(8,128)(2,1)S(1)} collective-permute-done((bf16[128,768]{1,0:T(8,128)(2,1)}, bf16[128,768]{1,0:T(8,128)(2,1)S(1)}, u32[]{:S(2)}, u32[]{:S(2)}) %collective-permute-start) | collective-permute-done | bytes 196640 | tf_op jit(solution)/shard_map/ppermute | solution.py:347
  12.7 2.2 %collective-permute-start.5 = (bf16[128,768]{1,0:T(8,128)(2,1)S(1)}, bf16[128,768]{1,0:T(8,128)(2,1)S(1)}, u32[]{:S(2)}, u32[]{:S(2)}) collective-permute-start(bf16[128,768]{1,0:T(8,128)(2,1)S(1)} %collective-permute-done._.refs_2_), channel_id=1, source_target_pairs={{0,16},{4,20},{8,24},{12,28},{16,0},{20,4},{24,8},{28,12},{1,17},{... | collective-permute-start | bytes 589832 | tf_op jit(solution)/shard_map/ppermute | solution.py:347
  14.9 1.7 %collective-permute-start.6 = (bf16[128,768]{1,0:T(8,128)(2,1)S(1)}, bf16[128,768]{1,0:T(8,128)(2,1)S(1)}, u32[]{:S(2)}, u32[]{:S(2)}) collective-permute-start(bf16[128,768]{1,0:T(8,128)(2,1)S(1)} %collective-permute-done.1.__.refs_5_), channel_id=1, source_target_pairs={{0,8},{4,12},{8,0},{12,4},{16,24},{20,28},{24,16},{28,20},{1,9},{5... | collective-permute-start | bytes 589832 | tf_op jit(solution)/shard_map/ppermute | solution.py:347
  16.6 1.1 %copy-done.4 = bf16[128,2304]{1,0:T(8,128)(2,1)S(1)} copy-done((bf16[128,2304]{1,0:T(8,128)(2,1)S(1)}, bf16[128,2304]{1,0:T(8,128)(2,1)}, u32[]{:S(2)}) %copy-start.4) | copy-done | bytes 589848
  17.7 0.9 %copy-done.5 = bf16[128,768]{1,0:T(8,128)(2,1)S(1)} copy-done((bf16[128,768]{1,0:T(8,128)(2,1)S(1)}, bf16[128,768]{1,0:T(8,128)(2,1)}, u32[]{:S(2)}) %copy-start.5) | copy-done | bytes 196632
  18.6 0.5 %shard_map.113 = (bf16[2,2,288,128]{3,2,1,0:T(8,128)(2,1)S(1)}, bf16[2,2,288,128]{3,2,1,0:T(8,128)(2,1)S(1)}, bf16[2,2,288,128]{3,2,1,0:T(8,128)(2,1)S(1)}, bf16...) custom-call(bf16[128,2304]{1,0:T(8,128)(2,1)S(1)} %copy-done.4, bf16[128,2304]{1,0:T(8,128)(2,1)S(1)} %copy-done.3, ...), custom_call_target="tpu_custom_call" | custom-call | bytes 2359296 | tf_op jit(solution)/shard_map/pallas_call | solution.py:334
  19.5 1.1 %collective-permute-start.10 = (bf16[2,2,288,128]{3,2,1,0:T(8,128)(2,1)S(1)}, bf16[2,2,288,128]{3,2,1,0:T(8,128)(2,1)S(1)}, u32[]{:S(2)}, u32[]{:S(2)}) collective-permute-start(bf16[2,2,288,128]{3,2,1,0:T(8,128)(2,1)S(1)} %get-tuple-element.32), channel_id=1, source_target_pairs={{0,16},{4,20},{8,24},{12,28},{16,0},{20,4},{24,8},{28,12},{1,17},{... | collective-permute-start | bytes 884744 | tf_op jit(solution)/shard_map/ppermute | solution.py:347
  20.6 2.1 %collective-permute-start.11 = (bf16[2,2,288,128]{3,2,1,0:T(8,128)(2,1)S(1)}, bf16[2,2,288,128]{3,2,1,0:T(8,128)(2,1)S(1)}, u32[]{:S(2)}, u32[]{:S(2)}) collective-permute-start(bf16[2,2,288,128]{3,2,1,0:T(8,128)(2,1)S(1)} %get-tuple-element.33), channel_id=1, source_target_pairs={{0,24},{4,28},{8,16},{12,20},{16,8},{20,12},{24,0},{28,4},{1,25},{... | collective-permute-start | bytes 884744 | tf_op jit(solution)/shard_map/ppermute | solution.py:347
  23.0 4.9 %shard_map.114 = (bf16[128,512]{1,0:T(8,128)(2,1)S(1)}, bf16[128,512]{1,0:T(8,128)(2,1)S(1)}, bf16[256,1024]{1,0:T(8,128)(2,1)S(1)}, bf16[1024,2048]{1,0:T(8,128)(2,1)S(1)}, bf16[128,2048]{1,0:T(8,128)(2,1)S(1)}) custom-call(bf16[128,768]{1,0:T(8,128)(2,1)S(1)} %get-tuple-element.23.refs_0_, bf16[128,768]{1,0:T(8,128)(2,1)S(1)} %collective-permute-done.2.refs_1_, ...), custom_call_target="tpu_custom_call" | custom-call | flops 2147483648 | bytes 1572864 | tf_op jit(solution)/shard_map/pallas_call | solution.py:334
  28.0 1.3 %collective-permute-done.7.far_ref = bf16[128,512]{1,0:T(8,128)(2,1)S(1)} collective-permute-done((bf16[128,512]{1,0:T(8,128)(2,1)S(1)}, bf16[128,512]{1,0:T(8,128)(2,1)S(1)}, u32[]{:S(2)}, u32[]{:S(2)}) %collective-permute-start.7) | collective-permute-done | bytes 131104 | tf_op jit(solution)/shard_map/ppermute | solution.py:347
  29.3 0.5 %shard_map.117 = bf16[576,128]{1,0:T(8,128)(2,1)S(1)} custom-call(bf16[128,512]{1,0:T(8,128)(2,1)S(1)} %get-tuple-element.27.own_ref, bf16[128,512]{1,0:T(8,128)(2,1)S(1)} %collective-permute-done.7.far_ref, bf16[2304,512]{1,0:T(8,128)(2,1)S(1)} %copy-done, bf16[2304,256]{1,0:T(8,128)(2,1)S(1)} %copy-done.1, bf16[2304,256]{1,0:T(8,128)(2,1)S(1)} %copy-done.2), custom_call_target="tpu_custom_call" | custom-call | flops 150994944 | bytes 1179648 | tf_op jit(solution)/shard_map/pallas_call | solution.py:334
  29.9 1.6 %collective-permute-start.8 = (bf16[576,128]{1,0:T(8,128)(2,1)S(1)}, bf16[576,128]{1,0:T(8,128)(2,1)S(1)}, u32[]{:S(2)}, u32[]{:S(2)}) collective-permute-start(bf16[576,128]{1,0:T(8,128)(2,1)S(1)} %shard_map.117), channel_id=1, source_target_pairs={{0,1},{1,0},{2,3},{3,2},{4,5},{5,4},{6,7},{7,6},{8,9},{9,8},{10,11... | collective-permute-start | bytes 442376 | tf_op jit(solution)/shard_map/ppermute | solution.py:347
  31.5 1.0 %shard_map.115._.dv_t_ref = bf16[128,1024]{1,0:T(8,128)(2,1)S(1)} custom-call(bf16[1024,2048]{1,0:T(8,128)(2,1)S(1)} %get-tuple-element.25.prob_ref, bf16[128,2048]{1,0:T(8,128)(2,1)S(1)} %get-tuple-element.26.grad_t_ref), custom_call_target="tpu_custom_call" | custom-call | flops 268435456 | bytes 4194304 | tf_op jit(solution)/shard_map/pallas_call | solution.py:334
  32.5 1.1 %shard_map.116 = (bf16[576,128]{1,0:T(8,128)(2,1)S(1)}, bf16[576,128]{1,0:T(8,128)(2,1)S(1)}, f32[576,128]{1,0:T(8,128)S(1)}) custom-call(bf16[128,512]{1,0:T(8,128)(2,1)S(1)} %get-tuple-element.27.own_ref, bf16[128,512]{1,0:T(8,128)(2,1)S(1)} %collective-permute-done.7.far_ref, bf16[2304,512]{1,0:T(8,128)(2,1)S(1)} %copy-done, ...), custom_call_target="tpu_custom_call" | custom-call | flops 452984832 | bytes 3538944 | tf_op jit(solution)/shard_map/pallas_call | solution.py:334
  33.6 2.2 %collective-permute-done.8.arrived_ref = bf16[576,128]{1,0:T(8,128)(2,1)S(1)} collective-permute-done((bf16[576,128]{1,0:T(8,128)(2,1)S(1)}, bf16[576,128]{1,0:T(8,128)(2,1)S(1)}, u32[]{:S(2)}, u32[]{:S(2)}) %collective-permute-start.8) | collective-permute-done | bytes 147488 | tf_op jit(solution)/shard_map/ppermute | solution.py:347
  36.2 2.6 %collective-permute-start.13 = (bf16[576,128]{1,0:T(8,128)(2,1)S(1)}, bf16[576,128]{1,0:T(8,128)(2,1)S(1)}, u32[]{:S(2)}, u32[]{:S(2)}) collective-permute-start(bf16[576,128]{1,0:T(8,128)(2,1)S(1)} %shard_map.118._), channel_id=1, source_target_pairs={{0,2},{1,3},{2,0},{3,1},{4,6},{5,7},{6,4},{7,5},{8,10},{9,11},{10,... | collective-permute-start | bytes 442376 | tf_op jit(solution)/shard_map/ppermute | solution.py:347
  38.8 1.6 %collective-permute-start.14 = (bf16[576,128]{1,0:T(8,128)(2,1)S(1)}, bf16[576,128]{1,0:T(8,128)(2,1)S(1)}, u32[]{:S(2)}, u32[]{:S(2)}) collective-permute-start(bf16[576,128]{1,0:T(8,128)(2,1)S(1)} %get-tuple-element.36), channel_id=1, source_target_pairs={{0,1},{1,0},{2,3},{3,2},{4,5},{5,4},{6,7},{7,6},{8,9},{9,8},{10,11... | collective-permute-start | bytes 442376 | tf_op jit(solution)/shard_map/ppermute | solution.py:347
  40.4 2.0 %shard_map.120 = (f32[288,256]{1,0:T(8,128)}, f32[288,512]{1,0:T(8,128)}, f32[8,128]{1,0:T(8,128)S(1)}) custom-call(bf16[256,1024]{1,0:T(8,128)(2,1)S(1)} %get-tuple-element.24.attn_ref, bf16[128,1024]{1,0:T(8,128)(2,1)S(1)} %shard_map.115._.dv_t_ref, bf16[5376,128]{1,0:T(8,128)(2,1)S(1)} %collective-permute-done.12.got_ref, ...), custom_call_target="tpu_custom_call" | custom-call | tf_op jit(solution)/shard_map/pallas_call | solution.py:334
  42.4 4.2 %collective-permute-done.13.arrived_ref = bf16[576,128]{1,0:T(8,128)(2,1)S(1)} collective-permute-done((bf16[576,128]{1,0:T(8,128)(2,1)S(1)}, bf16[576,128]{1,0:T(8,128)(2,1)S(1)}, u32[]{:S(2)}, u32[]{:S(2)}) %collective-permute-start.13) | collective-permute-done | bytes 147488 | tf_op jit(solution)/shard_map/ppermute | solution.py:347
  46.8 0.7 %shard_map.122 = bf16[576,128]{1,0:T(8,128)(2,1)} custom-call(f32[576,128]{1,0:T(8,128)S(1)} %shard_map.121.own_ref, bf16[576,128]{1,0:T(8,128)(2,1)S(1)} %collective-permute-done.14.refs_0_), custom_call_target="tpu_custom_call" | custom-call | bytes 1179648 | tf_op jit(solution)/shard_map/pallas_call | solution.py:334
  (29 shorter events, 1.9 us)
Async XLA Ops:
  0.6 16.0 %copy-start.3 = (bf16[128,2304]{1,0:T(8,128)(2,1)S(1)}, bf16[128,2304]{1,0:T(8,128)(2,1)}, u32[]{:S(2)}) copy-start(bf16[128,2304]{1,0:T(8,128)(2,1)} %cot_ref.1) | copy-start | bytes 1769476
  4.1 8.6 %collective-permute-start = (bf16[128,768]{1,0:T(8,128)(2,1)}, bf16[128,768]{1,0:T(8,128)(2,1)S(1)}, u32[]{:S(2)}, u32[]{:S(2)}) collective-permute-start(bf16[128,768]{1,0:T(8,128)(2,1)} %get-tuple-element.21.block_ref), channel_id=1, source_target_pairs={{0,8},{4,12},{8,0},{12,4},{16,24},{20,28},{24,16},{28,20},{1,9},{5... | collective-permute-start | bytes 589832 | tf_op jit(solution)/shard_map/ppermute | solution.py:347
  7.1 7.8 %collective-permute-start.1 = (bf16[128,768]{1,0:T(8,128)(2,1)}, bf16[128,768]{1,0:T(8,128)(2,1)S(1)}, u32[]{:S(2)}, u32[]{:S(2)}) collective-permute-start(bf16[128,768]{1,0:T(8,128)(2,1)} %get-tuple-element.22), channel_id=1, source_target_pairs={{0,20},{4,16},{8,28},{12,24},{16,4},{20,0},{24,12},{28,8},{1,21},{... | collective-permute-start | bytes 589832 | tf_op jit(solution)/shard_map/ppermute | solution.py:347
  7.8 11.3 %collective-permute-start.4 = (bf16[128,768]{1,0:T(8,128)(2,1)}, bf16[128,768]{1,0:T(8,128)(2,1)S(1)}, u32[]{:S(2)}, u32[]{:S(2)}) collective-permute-start(bf16[128,768]{1,0:T(8,128)(2,1)} %get-tuple-element.21.block_ref), channel_id=1, source_target_pairs={{0,16},{4,20},{8,24},{12,28},{16,0},{20,4},{24,8},{28,12},{1,17},{... | collective-permute-start | bytes 589832 | tf_op jit(solution)/shard_map/ppermute | solution.py:347
  8.7 10.8 %collective-permute-start.3 = (bf16[128,768]{1,0:T(8,128)(2,1)}, bf16[128,768]{1,0:T(8,128)(2,1)S(1)}, u32[]{:S(2)}, u32[]{:S(2)}) collective-permute-start(bf16[128,768]{1,0:T(8,128)(2,1)} %get-tuple-element.22), channel_id=1, source_target_pairs={{0,12},{4,8},{8,4},{12,0},{16,28},{20,24},{24,20},{28,16},{1,13},{... | collective-permute-start | bytes 589832 | tf_op jit(solution)/shard_map/ppermute | solution.py:347
  8.9 11.8 %collective-permute-start.2 = (bf16[128,768]{1,0:T(8,128)(2,1)}, bf16[128,768]{1,0:T(8,128)(2,1)S(1)}, u32[]{:S(2)}, u32[]{:S(2)}) collective-permute-start(bf16[128,768]{1,0:T(8,128)(2,1)} %get-tuple-element.22), channel_id=1, source_target_pairs={{0,4},{4,0},{8,12},{12,8},{16,20},{20,16},{24,28},{28,24},{1,5},{5... | collective-permute-start | bytes 589832 | tf_op jit(solution)/shard_map/ppermute | solution.py:347
  12.7 10.3 %collective-permute-start.5 = (bf16[128,768]{1,0:T(8,128)(2,1)S(1)}, bf16[128,768]{1,0:T(8,128)(2,1)S(1)}, u32[]{:S(2)}, u32[]{:S(2)}) collective-permute-start(bf16[128,768]{1,0:T(8,128)(2,1)S(1)} %collective-permute-done._.refs_2_), channel_id=1, source_target_pairs={{0,16},{4,20},{8,24},{12,28},{16,0},{20,4},{24,8},{28,12},{1,17},{... | collective-permute-start | bytes 589832 | tf_op jit(solution)/shard_map/ppermute | solution.py:347
  14.9 8.1 %collective-permute-start.6 = (bf16[128,768]{1,0:T(8,128)(2,1)S(1)}, bf16[128,768]{1,0:T(8,128)(2,1)S(1)}, u32[]{:S(2)}, u32[]{:S(2)}) collective-permute-start(bf16[128,768]{1,0:T(8,128)(2,1)S(1)} %collective-permute-done.1.__.refs_5_), channel_id=1, source_target_pairs={{0,8},{4,12},{8,0},{12,4},{16,24},{20,28},{24,16},{28,20},{1,9},{5... | collective-permute-start | bytes 589832 | tf_op jit(solution)/shard_map/ppermute | solution.py:347
  16.6 1.1 %copy-start.4 = (bf16[128,2304]{1,0:T(8,128)(2,1)S(1)}, bf16[128,2304]{1,0:T(8,128)(2,1)}, u32[]{:S(2)}) copy-start(bf16[128,2304]{1,0:T(8,128)(2,1)} %normed_ref.1) | copy-start | bytes 1769476
  17.7 0.9 %copy-start.5 = (bf16[128,768]{1,0:T(8,128)(2,1)S(1)}, bf16[128,768]{1,0:T(8,128)(2,1)}, u32[]{:S(2)}) copy-start(bf16[128,768]{1,0:T(8,128)(2,1)} %get-tuple-element.21.block_ref) | copy-start | bytes 589828
  19.1 16.7 %collective-permute-start.9 = (bf16[2,2,288,128]{3,2,1,0:T(8,128)(2,1)S(1)}, bf16[2,2,288,128]{3,2,1,0:T(8,128)(2,1)S(1)}, u32[]{:S(2)}, u32[]{:S(2)}) collective-permute-start(bf16[2,2,288,128]{3,2,1,0:T(8,128)(2,1)S(1)} %get-tuple-element.31), channel_id=1, source_target_pairs={{0,8},{4,12},{8,0},{12,4},{16,24},{20,28},{24,16},{28,20},{1,9},{5... | collective-permute-start | bytes 884744 | tf_op jit(solution)/shard_map/ppermute | solution.py:347
  19.5 16.4 %collective-permute-start.10 = (bf16[2,2,288,128]{3,2,1,0:T(8,128)(2,1)S(1)}, bf16[2,2,288,128]{3,2,1,0:T(8,128)(2,1)S(1)}, u32[]{:S(2)}, u32[]{:S(2)}) collective-permute-start(bf16[2,2,288,128]{3,2,1,0:T(8,128)(2,1)S(1)} %get-tuple-element.32), channel_id=1, source_target_pairs={{0,16},{4,20},{8,24},{12,28},{16,0},{20,4},{24,8},{28,12},{1,17},{... | collective-permute-start | bytes 884744 | tf_op jit(solution)/shard_map/ppermute | solution.py:347
  20.6 15.2 %collective-permute-start.11 = (bf16[2,2,288,128]{3,2,1,0:T(8,128)(2,1)S(1)}, bf16[2,2,288,128]{3,2,1,0:T(8,128)(2,1)S(1)}, u32[]{:S(2)}, u32[]{:S(2)}) collective-permute-start(bf16[2,2,288,128]{3,2,1,0:T(8,128)(2,1)S(1)} %get-tuple-element.33), channel_id=1, source_target_pairs={{0,24},{4,28},{8,16},{12,20},{16,8},{20,12},{24,0},{28,4},{1,25},{... | collective-permute-start | bytes 884744 | tf_op jit(solution)/shard_map/ppermute | solution.py:347
  23.0 6.3 %copy-start = (bf16[2304,512]{1,0:T(8,128)(2,1)S(1)}, bf16[2304,512]{1,0:T(8,128)(2,1)}, u32[]{:S(2)}) copy-start(bf16[2304,512]{1,0:T(8,128)(2,1)} %wq_ref.3) | copy-start | bytes 7077892
  23.0 6.3 %copy-start.1 = (bf16[2304,256]{1,0:T(8,128)(2,1)S(1)}, bf16[2304,256]{1,0:T(8,128)(2,1)}, u32[]{:S(2)}) copy-start(bf16[2304,256]{1,0:T(8,128)(2,1)} %wk_ref.3) | copy-start | bytes 3538948
  23.0 6.3 %copy-start.2 = (bf16[2304,256]{1,0:T(8,128)(2,1)S(1)}, bf16[2304,256]{1,0:T(8,128)(2,1)}, u32[]{:S(2)}) copy-start(bf16[2304,256]{1,0:T(8,128)(2,1)} %wv_ref.3) | copy-start | bytes 3538948
  27.9 1.4 %collective-permute-start.7 = (bf16[128,512]{1,0:T(8,128)(2,1)S(1)}, bf16[128,512]{1,0:T(8,128)(2,1)S(1)}, u32[]{:S(2)}, u32[]{:S(2)}) collective-permute-start(bf16[128,512]{1,0:T(8,128)(2,1)S(1)} %get-tuple-element.28), channel_id=1, source_target_pairs={{0,4},{4,0},{8,12},{12,8},{16,20},{20,16},{24,28},{28,24},{1,5},{5... | collective-permute-start | bytes 393224 | tf_op jit(solution)/shard_map/ppermute | solution.py:347
  29.9 6.0 %collective-permute-start.8 = (bf16[576,128]{1,0:T(8,128)(2,1)S(1)}, bf16[576,128]{1,0:T(8,128)(2,1)S(1)}, u32[]{:S(2)}, u32[]{:S(2)}) collective-permute-start(bf16[576,128]{1,0:T(8,128)(2,1)S(1)} %shard_map.117), channel_id=1, source_target_pairs={{0,1},{1,0},{2,3},{3,2},{4,5},{5,4},{6,7},{7,6},{8,9},{9,8},{10,11... | collective-permute-start | bytes 442376 | tf_op jit(solution)/shard_map/ppermute | solution.py:347
  36.1 4.3 %collective-permute-start.12 = (bf16[5376,128]{1,0:T(8,128)(2,1)S(1)}, bf16[5376,128]{1,0:T(8,128)(2,1)S(1)}, u32[]{:S(2)}, u32[]{:S(2)}) collective-permute-start(bf16[5376,128]{1,0:T(8,128)(2,1)S(1)} %shard_map.119), channel_id=1, source_target_pairs={{0,4},{4,0},{8,12},{12,8},{16,20},{20,16},{24,28},{28,24},{1,5},{5... | collective-permute-start | bytes 4128776 | tf_op jit(solution)/shard_map/ppermute | solution.py:347
  36.2 10.4 %collective-permute-start.13 = (bf16[576,128]{1,0:T(8,128)(2,1)S(1)}, bf16[576,128]{1,0:T(8,128)(2,1)S(1)}, u32[]{:S(2)}, u32[]{:S(2)}) collective-permute-start(bf16[576,128]{1,0:T(8,128)(2,1)S(1)} %shard_map.118._), channel_id=1, source_target_pairs={{0,2},{1,3},{2,0},{3,1},{4,6},{5,7},{6,4},{7,5},{8,10},{9,11},{10,... | collective-permute-start | bytes 442376 | tf_op jit(solution)/shard_map/ppermute | solution.py:347
  38.8 8.0 %collective-permute-start.14 = (bf16[576,128]{1,0:T(8,128)(2,1)S(1)}, bf16[576,128]{1,0:T(8,128)(2,1)S(1)}, u32[]{:S(2)}, u32[]{:S(2)}) collective-permute-start(bf16[576,128]{1,0:T(8,128)(2,1)S(1)} %get-tuple-element.36), channel_id=1, source_target_pairs={{0,1},{1,0},{2,3},{3,2},{4,5},{5,4},{6,7},{7,6},{8,9},{9,8},{10,11... | collective-permute-start | bytes 442376 | tf_op jit(solution)/shard_map/ppermute | solution.py:347

commit v25 on v19

--- a/solution.py
+++ b/solution.py
@@ -95,18 +95,19 @@
         for copy in model_copies[piece]:
             copy.wait()
         part = slice(piece * cut, (piece + 1) * cut)
-        product = dot_nt(weight_ref[:, part], cot_ref[:, part])
+        product = dot_nt(cot_ref[:, part], weight_ref[:, part])
         total = product if total is None else total + product
-    for copy in plain_copies:
-        copy.wait()
-    out_copies[0].start()
-    out_copies[2].start()
+        if piece == 0:
+            for copy in plain_copies:
+                copy.wait()
+            out_copies[0].start()
+            out_copies[2].start()
     for place in range(2):
         for head in range(rows // HEAD_SIZE):
             row = place * rows + head * HEAD_SIZE
             half_ref[place, :, first + head * HEAD_SIZE : first + (head + 1) * HEAD_SIZE] = total[
-                row : row + HEAD_SIZE
-            ].astype(jnp.bfloat16)
+                :, row : row + HEAD_SIZE
+            ].T.astype(jnp.bfloat16)
         out_copies[2 * place + 1].start()
     for copy in out_copies:
         copy.wait()
@@ -352,7 +353,7 @@
         in_specs=[vmem if place in in_vmem else hbm for place in range(len(operands))],
         out_specs=(vmem if out_vmem else hbm,) * len(outs),
         scratch_shapes=list(scratch),
-        compiler_params=pltpu.CompilerParams(vmem_limit_bytes=room * 1024 * 1024),
+        compiler_params=pltpu.CompilerParams(vmem_limit_bytes=int(room * 1024 * 1024)),
         cost_estimate=pl.CostEstimate(flops=flops, bytes_accessed=moved, transcendentals=0),
     )(*operands)
 

time: 48 us -> 47.9 us (level)
  no operation moved by 1% of the time
where the time goes in v25:
time: 47.9 us; the launch traced here: 47.7 us
  starting transfers between devices  18.7 us (39%)
  Pallas kernels  14.7 us (31%)
  waiting for transfers between devices  11.6 us (24%)
  local copies, waits for them, and re-layouts  2.01 us (4%)
  between operations  0.77 us (2%)
    ppermute x15, starting transfers between devices, swapped(): lax.ppermute(value, axis, [(place, place ^ apart) for place in range(coun...  18.7 us
    pallas_call x11, Pallas kernels, kernel_call(): pl.pallas_call(body, out_shape=outs, in_specs=[vmem if place in in_vmem e...  14.7 us
    ppermute x15, waiting for transfers between devices, swapped(): lax.ppermute(value, axis, [(place, place ^ apart) for place in range(coun...  11.6 us
    unnamed x12, local copies, waits for them, and re-layouts  2.01 us
  transfers between devices with their start and end apart: 15, of which 6 were waited for; matrix products, arithmetic and copies ran while one was open for 0% of the time, Pallas kernels for 21%

profile of v25, /device:TPU:0, one launch (start us, length us, event | category | flops | bytes accessed | tf_op | source)
XLA Modules:
  0.0 47.7 jit_solution(6427079082706475646)
XLA Ops:
  0.6 3.7 %shard_map.112 = (bf16[128,768]{1,0:T(8,128)(2,1)}, bf16[128,768]{1,0:T(8,128)(2,1)}) custom-call(bf16[128,2304]{1,0:T(8,128)(2,1)} %cot_ref.1, bf16[512,2304]{1,0:T(8,128)(2,1)} %weight_hbm.1, bf16[128,512]{1,0:T(8,128)(2,1)} %q_hbm.1, bf16[128,256]{1,0:T(8,128)(2,1)} %k_hbm.1, bf16[128,256]{1,0:T(8,128)(2,1)} %v_hbm.1), custom_call_target="tpu_custom_call" | custom-call | flops 301989888 | bytes 2949120 | tf_op jit(solution)/shard_map/pallas_call | solution.py:350
  4.4 3.0 %collective-permute-start = (bf16[128,768]{1,0:T(8,128)(2,1)}, bf16[128,768]{1,0:T(8,128)(2,1)S(1)}, u32[]{:S(2)}, u32[]{:S(2)}) collective-permute-start(bf16[128,768]{1,0:T(8,128)(2,1)} %get-tuple-element.21.block_ref), channel_id=1, source_target_pairs={{0,8},{4,12},{8,0},{12,4},{16,24},{20,28},{24,16},{28,20},{1,9},{5... | collective-permute-start | bytes 589832 | tf_op jit(solution)/shard_map/ppermute | solution.py:363
  7.4 0.7 %collective-permute-start.1 = (bf16[128,768]{1,0:T(8,128)(2,1)}, bf16[128,768]{1,0:T(8,128)(2,1)S(1)}, u32[]{:S(2)}, u32[]{:S(2)}) collective-permute-start(bf16[128,768]{1,0:T(8,128)(2,1)} %get-tuple-element.22), channel_id=1, source_target_pairs={{0,20},{4,16},{8,28},{12,24},{16,4},{20,0},{24,12},{28,8},{1,21},{... | collective-permute-start | bytes 589832 | tf_op jit(solution)/shard_map/ppermute | solution.py:363
  8.0 0.9 %collective-permute-start.4 = (bf16[128,768]{1,0:T(8,128)(2,1)}, bf16[128,768]{1,0:T(8,128)(2,1)S(1)}, u32[]{:S(2)}, u32[]{:S(2)}) collective-permute-start(bf16[128,768]{1,0:T(8,128)(2,1)} %get-tuple-element.21.block_ref), channel_id=1, source_target_pairs={{0,16},{4,20},{8,24},{12,28},{16,0},{20,4},{24,8},{28,12},{1,17},{... | collective-permute-start | bytes 589832 | tf_op jit(solution)/shard_map/ppermute | solution.py:363
  9.6 3.4 %collective-permute-done._.refs_2_ = bf16[128,768]{1,0:T(8,128)(2,1)S(1)} collective-permute-done((bf16[128,768]{1,0:T(8,128)(2,1)}, bf16[128,768]{1,0:T(8,128)(2,1)S(1)}, u32[]{:S(2)}, u32[]{:S(2)}) %collective-permute-start) | collective-permute-done | bytes 196640 | tf_op jit(solution)/shard_map/ppermute | solution.py:363
  13.0 2.1 %collective-permute-start.5 = (bf16[128,768]{1,0:T(8,128)(2,1)S(1)}, bf16[128,768]{1,0:T(8,128)(2,1)S(1)}, u32[]{:S(2)}, u32[]{:S(2)}) collective-permute-start(bf16[128,768]{1,0:T(8,128)(2,1)S(1)} %collective-permute-done._.refs_2_), channel_id=1, source_target_pairs={{0,16},{4,20},{8,24},{12,28},{16,0},{20,4},{24,8},{28,12},{1,17},{... | collective-permute-start | bytes 589832 | tf_op jit(solution)/shard_map/ppermute | solution.py:363
  15.1 1.8 %collective-permute-start.6 = (bf16[128,768]{1,0:T(8,128)(2,1)S(1)}, bf16[128,768]{1,0:T(8,128)(2,1)S(1)}, u32[]{:S(2)}, u32[]{:S(2)}) collective-permute-start(bf16[128,768]{1,0:T(8,128)(2,1)S(1)} %collective-permute-done.1.__.refs_5_), channel_id=1, source_target_pairs={{0,8},{4,12},{8,0},{12,4},{16,24},{20,28},{24,16},{28,20},{1,9},{5... | collective-permute-start | bytes 589832 | tf_op jit(solution)/shard_map/ppermute | solution.py:363
  16.9 1.1 %copy-done.4 = bf16[128,2304]{1,0:T(8,128)(2,1)S(1)} copy-done((bf16[128,2304]{1,0:T(8,128)(2,1)S(1)}, bf16[128,2304]{1,0:T(8,128)(2,1)}, u32[]{:S(2)}) %copy-start.4) | copy-done | bytes 589848
  17.9 0.9 %copy-done.5 = bf16[128,768]{1,0:T(8,128)(2,1)S(1)} copy-done((bf16[128,768]{1,0:T(8,128)(2,1)S(1)}, bf16[128,768]{1,0:T(8,128)(2,1)}, u32[]{:S(2)}) %copy-start.5) | copy-done | bytes 196632
  18.9 0.5 %shard_map.113 = (bf16[2,2,288,128]{3,2,1,0:T(8,128)(2,1)S(1)}, bf16[2,2,288,128]{3,2,1,0:T(8,128)(2,1)S(1)}, bf16[2,2,288,128]{3,2,1,0:T(8,128)(2,1)S(1)}, bf16...) custom-call(bf16[128,2304]{1,0:T(8,128)(2,1)S(1)} %copy-done.4, bf16[128,2304]{1,0:T(8,128)(2,1)S(1)} %copy-done.3, ...), custom_call_target="tpu_custom_call" | custom-call | bytes 2359296 | tf_op jit(solution)/shard_map/pallas_call | solution.py:350
  19.7 1.2 %collective-permute-start.10 = (bf16[2,2,288,128]{3,2,1,0:T(8,128)(2,1)S(1)}, bf16[2,2,288,128]{3,2,1,0:T(8,128)(2,1)S(1)}, u32[]{:S(2)}, u32[]{:S(2)}) collective-permute-start(bf16[2,2,288,128]{3,2,1,0:T(8,128)(2,1)S(1)} %get-tuple-element.32), channel_id=1, source_target_pairs={{0,16},{4,20},{8,24},{12,28},{16,0},{20,4},{24,8},{28,12},{1,17},{... | collective-permute-start | bytes 884744 | tf_op jit(solution)/shard_map/ppermute | solution.py:363
  20.9 2.1 %collective-permute-start.11 = (bf16[2,2,288,128]{3,2,1,0:T(8,128)(2,1)S(1)}, bf16[2,2,288,128]{3,2,1,0:T(8,128)(2,1)S(1)}, u32[]{:S(2)}, u32[]{:S(2)}) collective-permute-start(bf16[2,2,288,128]{3,2,1,0:T(8,128)(2,1)S(1)} %get-tuple-element.33), channel_id=1, source_target_pairs={{0,24},{4,28},{8,16},{12,20},{16,8},{20,12},{24,0},{28,4},{1,25},{... | collective-permute-start | bytes 884744 | tf_op jit(solution)/shard_map/ppermute | solution.py:363
  23.3 4.9 %shard_map.114 = (bf16[128,512]{1,0:T(8,128)(2,1)S(1)}, bf16[128,512]{1,0:T(8,128)(2,1)S(1)}, bf16[256,1024]{1,0:T(8,128)(2,1)S(1)}, bf16[1024,2048]{1,0:T(8,128)(2,1)S(1)}, bf16[128,2048]{1,0:T(8,128)(2,1)S(1)}) custom-call(bf16[128,768]{1,0:T(8,128)(2,1)S(1)} %get-tuple-element.23.refs_0_, bf16[128,768]{1,0:T(8,128)(2,1)S(1)} %collective-permute-done.2.refs_1_, ...), custom_call_target="tpu_custom_call" | custom-call | flops 2147483648 | bytes 1572864 | tf_op jit(solution)/shard_map/pallas_call | solution.py:350
  28.2 1.3 %collective-permute-done.7.far_ref = bf16[128,512]{1,0:T(8,128)(2,1)S(1)} collective-permute-done((bf16[128,512]{1,0:T(8,128)(2,1)S(1)}, bf16[128,512]{1,0:T(8,128)(2,1)S(1)}, u32[]{:S(2)}, u32[]{:S(2)}) %collective-permute-start.7) | collective-permute-done | bytes 131104 | tf_op jit(solution)/shard_map/ppermute | solution.py:363
  29.6 0.5 %shard_map.117 = bf16[576,128]{1,0:T(8,128)(2,1)S(1)} custom-call(bf16[128,512]{1,0:T(8,128)(2,1)S(1)} %get-tuple-element.27.own_ref, bf16[128,512]{1,0:T(8,128)(2,1)S(1)} %collective-permute-done.7.far_ref, bf16[2304,512]{1,0:T(8,128)(2,1)S(1)} %copy-done, bf16[2304,256]{1,0:T(8,128)(2,1)S(1)} %copy-done.1, bf16[2304,256]{1,0:T(8,128)(2,1)S(1)} %copy-done.2), custom_call_target="tpu_custom_call" | custom-call | flops 150994944 | bytes 1179648 | tf_op jit(solution)/shard_map/pallas_call | solution.py:350
  30.1 1.7 %collective-permute-start.8 = (bf16[576,128]{1,0:T(8,128)(2,1)S(1)}, bf16[576,128]{1,0:T(8,128)(2,1)S(1)}, u32[]{:S(2)}, u32[]{:S(2)}) collective-permute-start(bf16[576,128]{1,0:T(8,128)(2,1)S(1)} %shard_map.117), channel_id=1, source_target_pairs={{0,1},{1,0},{2,3},{3,2},{4,5},{5,4},{6,7},{7,6},{8,9},{9,8},{10,11... | collective-permute-start | bytes 442376 | tf_op jit(solution)/shard_map/ppermute | solution.py:363
  31.8 1.0 %shard_map.115._.dv_t_ref = bf16[128,1024]{1,0:T(8,128)(2,1)S(1)} custom-call(bf16[1024,2048]{1,0:T(8,128)(2,1)S(1)} %get-tuple-element.25.prob_ref, bf16[128,2048]{1,0:T(8,128)(2,1)S(1)} %get-tuple-element.26.grad_t_ref), custom_call_target="tpu_custom_call" | custom-call | flops 268435456 | bytes 4194304 | tf_op jit(solution)/shard_map/pallas_call | solution.py:350
  32.7 1.1 %shard_map.116 = (bf16[576,128]{1,0:T(8,128)(2,1)S(1)}, bf16[576,128]{1,0:T(8,128)(2,1)S(1)}, f32[576,128]{1,0:T(8,128)S(1)}) custom-call(bf16[128,512]{1,0:T(8,128)(2,1)S(1)} %get-tuple-element.27.own_ref, bf16[128,512]{1,0:T(8,128)(2,1)S(1)} %collective-permute-done.7.far_ref, bf16[2304,512]{1,0:T(8,128)(2,1)S(1)} %copy-done, ...), custom_call_target="tpu_custom_call" | custom-call | flops 452984832 | bytes 3538944 | tf_op jit(solution)/shard_map/pallas_call | solution.py:350
  33.9 2.2 %collective-permute-done.8.arrived_ref = bf16[576,128]{1,0:T(8,128)(2,1)S(1)} collective-permute-done((bf16[576,128]{1,0:T(8,128)(2,1)S(1)}, bf16[576,128]{1,0:T(8,128)(2,1)S(1)}, u32[]{:S(2)}, u32[]{:S(2)}) %collective-permute-start.8) | collective-permute-done | bytes 147488 | tf_op jit(solution)/shard_map/ppermute | solution.py:363
  36.4 2.7 %collective-permute-start.13 = (bf16[576,128]{1,0:T(8,128)(2,1)S(1)}, bf16[576,128]{1,0:T(8,128)(2,1)S(1)}, u32[]{:S(2)}, u32[]{:S(2)}) collective-permute-start(bf16[576,128]{1,0:T(8,128)(2,1)S(1)} %shard_map.118._), channel_id=1, source_target_pairs={{0,2},{1,3},{2,0},{3,1},{4,6},{5,7},{6,4},{7,5},{8,10},{9,11},{10,... | collective-permute-start | bytes 442376 | tf_op jit(solution)/shard_map/ppermute | solution.py:363
  39.1 1.6 %collective-permute-start.14 = (bf16[576,128]{1,0:T(8,128)(2,1)S(1)}, bf16[576,128]{1,0:T(8,128)(2,1)S(1)}, u32[]{:S(2)}, u32[]{:S(2)}) collective-permute-start(bf16[576,128]{1,0:T(8,128)(2,1)S(1)} %get-tuple-element.36), channel_id=1, source_target_pairs={{0,1},{1,0},{2,3},{3,2},{4,5},{5,4},{6,7},{7,6},{8,9},{9,8},{10,11... | collective-permute-start | bytes 442376 | tf_op jit(solution)/shard_map/ppermute | solution.py:363
  40.7 2.0 %shard_map.120 = (f32[288,256]{1,0:T(8,128)}, f32[288,512]{1,0:T(8,128)}, f32[8,128]{1,0:T(8,128)S(1)}) custom-call(bf16[256,1024]{1,0:T(8,128)(2,1)S(1)} %get-tuple-element.24.attn_ref, bf16[128,1024]{1,0:T(8,128)(2,1)S(1)} %shard_map.115._.dv_t_ref, bf16[5376,128]{1,0:T(8,128)(2,1)S(1)} %collective-permute-done.12.got_ref, ...), custom_call_target="tpu_custom_call" | custom-call | tf_op jit(solution)/shard_map/pallas_call | solution.py:350
  42.7 4.2 %collective-permute-done.13.arrived_ref = bf16[576,128]{1,0:T(8,128)(2,1)S(1)} collective-permute-done((bf16[576,128]{1,0:T(8,128)(2,1)S(1)}, bf16[576,128]{1,0:T(8,128)(2,1)S(1)}, u32[]{:S(2)}, u32[]{:S(2)}) %collective-permute-start.13) | collective-permute-done | bytes 147488 | tf_op jit(solution)/shard_map/ppermute | solution.py:363
  47.0 0.7 %shard_map.122 = bf16[576,128]{1,0:T(8,128)(2,1)} custom-call(f32[576,128]{1,0:T(8,128)S(1)} %shard_map.121.own_ref, bf16[576,128]{1,0:T(8,128)(2,1)S(1)} %collective-permute-done.14.refs_0_), custom_call_target="tpu_custom_call" | custom-call | bytes 1179648 | tf_op jit(solution)/shard_map/pallas_call | solution.py:350
  (29 shorter events, 1.9 us)
Async XLA Ops:
  0.6 16.2 %copy-start.3 = (bf16[128,2304]{1,0:T(8,128)(2,1)S(1)}, bf16[128,2304]{1,0:T(8,128)(2,1)}, u32[]{:S(2)}) copy-start(bf16[128,2304]{1,0:T(8,128)(2,1)} %cot_ref.1) | copy-start | bytes 1769476
  4.4 8.6 %collective-permute-start = (bf16[128,768]{1,0:T(8,128)(2,1)}, bf16[128,768]{1,0:T(8,128)(2,1)S(1)}, u32[]{:S(2)}, u32[]{:S(2)}) collective-permute-start(bf16[128,768]{1,0:T(8,128)(2,1)} %get-tuple-element.21.block_ref), channel_id=1, source_target_pairs={{0,8},{4,12},{8,0},{12,4},{16,24},{20,28},{24,16},{28,20},{1,9},{5... | collective-permute-start | bytes 589832 | tf_op jit(solution)/shard_map/ppermute | solution.py:363
  7.4 7.8 %collective-permute-start.1 = (bf16[128,768]{1,0:T(8,128)(2,1)}, bf16[128,768]{1,0:T(8,128)(2,1)S(1)}, u32[]{:S(2)}, u32[]{:S(2)}) collective-permute-start(bf16[128,768]{1,0:T(8,128)(2,1)} %get-tuple-element.22), channel_id=1, source_target_pairs={{0,20},{4,16},{8,28},{12,24},{16,4},{20,0},{24,12},{28,8},{1,21},{... | collective-permute-start | bytes 589832 | tf_op jit(solution)/shard_map/ppermute | solution.py:363
  8.0 11.3 %collective-permute-start.4 = (bf16[128,768]{1,0:T(8,128)(2,1)}, bf16[128,768]{1,0:T(8,128)(2,1)S(1)}, u32[]{:S(2)}, u32[]{:S(2)}) collective-permute-start(bf16[128,768]{1,0:T(8,128)(2,1)} %get-tuple-element.21.block_ref), channel_id=1, source_target_pairs={{0,16},{4,20},{8,24},{12,28},{16,0},{20,4},{24,8},{28,12},{1,17},{... | collective-permute-start | bytes 589832 | tf_op jit(solution)/shard_map/ppermute | solution.py:363
  8.9 10.8 %collective-permute-start.3 = (bf16[128,768]{1,0:T(8,128)(2,1)}, bf16[128,768]{1,0:T(8,128)(2,1)S(1)}, u32[]{:S(2)}, u32[]{:S(2)}) collective-permute-start(bf16[128,768]{1,0:T(8,128)(2,1)} %get-tuple-element.22), channel_id=1, source_target_pairs={{0,12},{4,8},{8,4},{12,0},{16,28},{20,24},{24,20},{28,16},{1,13},{... | collective-permute-start | bytes 589832 | tf_op jit(solution)/shard_map/ppermute | solution.py:363
  9.1 11.7 %collective-permute-start.2 = (bf16[128,768]{1,0:T(8,128)(2,1)}, bf16[128,768]{1,0:T(8,128)(2,1)S(1)}, u32[]{:S(2)}, u32[]{:S(2)}) collective-permute-start(bf16[128,768]{1,0:T(8,128)(2,1)} %get-tuple-element.22), channel_id=1, source_target_pairs={{0,4},{4,0},{8,12},{12,8},{16,20},{20,16},{24,28},{28,24},{1,5},{5... | collective-permute-start | bytes 589832 | tf_op jit(solution)/shard_map/ppermute | solution.py:363
  13.0 10.3 %collective-permute-start.5 = (bf16[128,768]{1,0:T(8,128)(2,1)S(1)}, bf16[128,768]{1,0:T(8,128)(2,1)S(1)}, u32[]{:S(2)}, u32[]{:S(2)}) collective-permute-start(bf16[128,768]{1,0:T(8,128)(2,1)S(1)} %collective-permute-done._.refs_2_), channel_id=1, source_target_pairs={{0,16},{4,20},{8,24},{12,28},{16,0},{20,4},{24,8},{28,12},{1,17},{... | collective-permute-start | bytes 589832 | tf_op jit(solution)/shard_map/ppermute | solution.py:363
  15.1 8.1 %collective-permute-start.6 = (bf16[128,768]{1,0:T(8,128)(2,1)S(1)}, bf16[128,768]{1,0:T(8,128)(2,1)S(1)}, u32[]{:S(2)}, u32[]{:S(2)}) collective-permute-start(bf16[128,768]{1,0:T(8,128)(2,1)S(1)} %collective-permute-done.1.__.refs_5_), channel_id=1, source_target_pairs={{0,8},{4,12},{8,0},{12,4},{16,24},{20,28},{24,16},{28,20},{1,9},{5... | collective-permute-start | bytes 589832 | tf_op jit(solution)/shard_map/ppermute | solution.py:363
  16.9 1.1 %copy-start.4 = (bf16[128,2304]{1,0:T(8,128)(2,1)S(1)}, bf16[128,2304]{1,0:T(8,128)(2,1)}, u32[]{:S(2)}) copy-start(bf16[128,2304]{1,0:T(8,128)(2,1)} %normed_ref.1) | copy-start | bytes 1769476
  17.9 0.9 %copy-start.5 = (bf16[128,768]{1,0:T(8,128)(2,1)S(1)}, bf16[128,768]{1,0:T(8,128)(2,1)}, u32[]{:S(2)}) copy-start(bf16[128,768]{1,0:T(8,128)(2,1)} %get-tuple-element.21.block_ref) | copy-start | bytes 589828
  19.4 16.7 %collective-permute-start.9 = (bf16[2,2,288,128]{3,2,1,0:T(8,128)(2,1)S(1)}, bf16[2,2,288,128]{3,2,1,0:T(8,128)(2,1)S(1)}, u32[]{:S(2)}, u32[]{:S(2)}) collective-permute-start(bf16[2,2,288,128]{3,2,1,0:T(8,128)(2,1)S(1)} %get-tuple-element.31), channel_id=1, source_target_pairs={{0,8},{4,12},{8,0},{12,4},{16,24},{20,28},{24,16},{28,20},{1,9},{5... | collective-permute-start | bytes 884744 | tf_op jit(solution)/shard_map/ppermute | solution.py:363
  19.7 16.4 %collective-permute-start.10 = (bf16[2,2,288,128]{3,2,1,0:T(8,128)(2,1)S(1)}, bf16[2,2,288,128]{3,2,1,0:T(8,128)(2,1)S(1)}, u32[]{:S(2)}, u32[]{:S(2)}) collective-permute-start(bf16[2,2,288,128]{3,2,1,0:T(8,128)(2,1)S(1)} %get-tuple-element.32), channel_id=1, source_target_pairs={{0,16},{4,20},{8,24},{12,28},{16,0},{20,4},{24,8},{28,12},{1,17},{... | collective-permute-start | bytes 884744 | tf_op jit(solution)/shard_map/ppermute | solution.py:363
  20.9 15.3 %collective-permute-start.11 = (bf16[2,2,288,128]{3,2,1,0:T(8,128)(2,1)S(1)}, bf16[2,2,288,128]{3,2,1,0:T(8,128)(2,1)S(1)}, u32[]{:S(2)}, u32[]{:S(2)}) collective-permute-start(bf16[2,2,288,128]{3,2,1,0:T(8,128)(2,1)S(1)} %get-tuple-element.33), channel_id=1, source_target_pairs={{0,24},{4,28},{8,16},{12,20},{16,8},{20,12},{24,0},{28,4},{1,25},{... | collective-permute-start | bytes 884744 | tf_op jit(solution)/shard_map/ppermute | solution.py:363
  23.3 6.3 %copy-start = (bf16[2304,512]{1,0:T(8,128)(2,1)S(1)}, bf16[2304,512]{1,0:T(8,128)(2,1)}, u32[]{:S(2)}) copy-start(bf16[2304,512]{1,0:T(8,128)(2,1)} %wq_ref.3) | copy-start | bytes 7077892
  23.3 6.3 %copy-start.1 = (bf16[2304,256]{1,0:T(8,128)(2,1)S(1)}, bf16[2304,256]{1,0:T(8,128)(2,1)}, u32[]{:S(2)}) copy-start(bf16[2304,256]{1,0:T(8,128)(2,1)} %wk_ref.3) | copy-start | bytes 3538948
  23.3 6.3 %copy-start.2 = (bf16[2304,256]{1,0:T(8,128)(2,1)S(1)}, bf16[2304,256]{1,0:T(8,128)(2,1)}, u32[]{:S(2)}) copy-start(bf16[2304,256]{1,0:T(8,128)(2,1)} %wv_ref.3) | copy-start | bytes 3538948
  28.2 1.4 %collective-permute-start.7 = (bf16[128,512]{1,0:T(8,128)(2,1)S(1)}, bf16[128,512]{1,0:T(8,128)(2,1)S(1)}, u32[]{:S(2)}, u32[]{:S(2)}) collective-permute-start(bf16[128,512]{1,0:T(8,128)(2,1)S(1)} %get-tuple-element.28), channel_id=1, source_target_pairs={{0,4},{4,0},{8,12},{12,8},{16,20},{20,16},{24,28},{28,24},{1,5},{5... | collective-permute-start | bytes 393224 | tf_op jit(solution)/shard_map/ppermute | solution.py:363
  30.1 6.0 %collective-permute-start.8 = (bf16[576,128]{1,0:T(8,128)(2,1)S(1)}, bf16[576,128]{1,0:T(8,128)(2,1)S(1)}, u32[]{:S(2)}, u32[]{:S(2)}) collective-permute-start(bf16[576,128]{1,0:T(8,128)(2,1)S(1)} %shard_map.117), channel_id=1, source_target_pairs={{0,1},{1,0},{2,3},{3,2},{4,5},{5,4},{6,7},{7,6},{8,9},{9,8},{10,11... | collective-permute-start | bytes 442376 | tf_op jit(solution)/shard_map/ppermute | solution.py:363
  36.3 4.3 %collective-permute-start.12 = (bf16[5376,128]{1,0:T(8,128)(2,1)S(1)}, bf16[5376,128]{1,0:T(8,128)(2,1)S(1)}, u32[]{:S(2)}, u32[]{:S(2)}) collective-permute-start(bf16[5376,128]{1,0:T(8,128)(2,1)S(1)} %shard_map.119), channel_id=1, source_target_pairs={{0,4},{4,0},{8,12},{12,8},{16,20},{20,16},{24,28},{28,24},{1,5},{5... | collective-permute-start | bytes 4128776 | tf_op jit(solution)/shard_map/ppermute | solution.py:363
  36.4 10.4 %collective-permute-start.13 = (bf16[576,128]{1,0:T(8,128)(2,1)S(1)}, bf16[576,128]{1,0:T(8,128)(2,1)S(1)}, u32[]{:S(2)}, u32[]{:S(2)}) collective-permute-start(bf16[576,128]{1,0:T(8,128)(2,1)S(1)} %shard_map.118._), channel_id=1, source_target_pairs={{0,2},{1,3},{2,0},{3,1},{4,6},{5,7},{6,4},{7,5},{8,10},{9,11},{10,... | collective-permute-start | bytes 442376 | tf_op jit(solution)/shard_map/ppermute | solution.py:363
  39.1 7.9 %collective-permute-start.14 = (bf16[576,128]{1,0:T(8,128)(2,1)S(1)}, bf16[576,128]{1,0:T(8,128)(2,1)S(1)}, u32[]{:S(2)}, u32[]{:S(2)}) collective-permute-start(bf16[576,128]{1,0:T(8,128)(2,1)S(1)} %get-tuple-element.36), channel_id=1, source_target_pairs={{0,1},{1,0},{2,3},{3,2},{4,5},{5,4},{6,7},{7,6},{8,9},{9,8},{10,11... | collective-permute-start | bytes 442376 | tf_op jit(solution)/shard_map/ppermute | solution.py:363

commit v26 on v21

--- a/solution.py
+++ b/solution.py
@@ -97,11 +97,15 @@
         copy.wait()
 
 
-def turn_kernel(normed_ref, cot_ref, block_ref, _, __, *refs):
-    *column_refs, own_ref, turned_ref = refs
+def hold_kernel(same_ref, other_ref, kept_same_ref, kept_other_ref):
+    kept_same_ref[...] = same_ref[...]
+    kept_other_ref[...] = other_ref[...]
+
+
+def turn_kernel(normed_ref, cot_ref, _, __, *refs):
+    *column_refs, turned_ref = refs
     me = lax.axis_index("seq")
     cut = column_refs[0].shape[2]
-    own_ref[...] = block_ref[...]
     for which, ref in enumerate((normed_ref, cot_ref)):
         turned_ref[which] = ref[...].astype(jnp.float32).T.astype(jnp.bfloat16)
         for chip, target in enumerate(column_refs):
@@ -382,23 +386,33 @@
         moved=2 * model * (rows + 2 * q_cols),
         room=63,
     )
-    held = {0: same}
+    kept_same, kept_other = kernel_call(
+        hold_kernel,
+        (shape(same.shape, bf16),) * 2,
+        (same, other),
+        in_vmem=range(2),
+        moved=8 * rows * packed_cols,
+        room=4,
+    )
+    held = {0: kept_same}
     for apart in range(2, blocks):
         lowest, highest = 2, 1 << (apart.bit_length() - 1)
         while not apart & lowest:
             lowest *= 2
         through = lowest if apart % 2 else highest
         if lowest == highest:
-            held[apart] = swapped(other if apart % 2 else same, "seq", apart)
+            first = apart in (2, blocks // 2 + 1)
+            even, odd = (same, other) if first else (kept_same, kept_other)
+            held[apart] = swapped(odd if apart % 2 else even, "seq", apart)
         else:
             held[apart] = swapped(held[apart ^ through], "seq", through)
     held[1] = swapped(other, "seq", 1)
     cut = model // blocks
-    *columns, held[0] = kernel_call(
+    columns = kernel_call(
         turn_kernel,
-        (shape((2, 2, cut, rows), bf16),) * (blocks // 2) + (shape(same.shape, bf16),),
-        (normed_input, out_cotangent, same, held[2], held[blocks // 2 + 1]),
-        in_vmem=range(3),
+        (shape((2, 2, cut, rows), bf16),) * (blocks // 2),
+        (normed_input, out_cotangent, held[2], held[blocks // 2 + 1]),
+        in_vmem=range(2),
         scratch=(pltpu.VMEM((2, model, rows), bf16),),
         moved=8 * rows * model,
         room=8,

time: 47.7 us -> 47.7 us (level)
  waiting for transfers between devices: 11.7 us -> 10.7 us
  Pallas kernels: 14.4 us -> 15.3 us
    ppermute x15, waiting for transfers between devices: 11.7 us -> 10.7 us  [swapped(): lax.ppermute(value, axis, [(place, place ^ apart) for place in range(coun...]
    pallas_call x11 -> x12, Pallas kernels: 14.4 us -> 15.3 us  [kernel_call(): pl.pallas_call(body, out_shape=outs, in_specs=[vmem if place in in_vmem e...]
  transfers between devices with their start and end apart: 15 -> 15, of which waited for: 6 -> 7; matrix products, arithmetic and copies ran while one was open for 0% -> 0% of each run, Pallas kernels for 21% -> 23%
where the time goes in v26:
time: 47.7 us; the launch traced here: 47.5 us
  starting transfers between devices  18.6 us (39%)
  Pallas kernels  15.3 us (32%)
  waiting for transfers between devices  10.7 us (22%)
  local copies, waits for them, and re-layouts  2.04 us (4%)
  between operations  0.77 us (2%)
    ppermute x15, starting transfers between devices, swapped(): lax.ppermute(value, axis, [(place, place ^ apart) for place in range(coun...  18.6 us
    pallas_call x12, Pallas kernels, kernel_call(): pl.pallas_call(body, out_shape=outs, in_specs=[vmem if place in in_vmem e...  15.3 us
    ppermute x15, waiting for transfers between devices, swapped(): lax.ppermute(value, axis, [(place, place ^ apart) for place in range(coun...  10.7 us
    unnamed x12, local copies, waits for them, and re-layouts  2.04 us
  transfers between devices with their start and end apart: 15, of which 7 were waited for; matrix products, arithmetic and copies ran while one was open for 0% of the time, Pallas kernels for 23%

profile of v26, /device:TPU:0, one launch (start us, length us, event | category | flops | bytes accessed | tf_op | source)
XLA Modules:
  0.0 47.5 jit_solution(5965605267944449023)
XLA Ops:
  0.6 3.5 %shard_map.112 = (bf16[128,768]{1,0:T(8,128)(2,1)}, bf16[128,768]{1,0:T(8,128)(2,1)}) custom-call(bf16[128,2304]{1,0:T(8,128)(2,1)} %cot_ref.1, bf16[512,2304]{1,0:T(8,128)(2,1)} %weight_hbm.1, bf16[128,512]{1,0:T(8,128)(2,1)} %q_hbm.1, bf16[128,256]{1,0:T(8,128)(2,1)} %k_hbm.1, bf16[128,256]{1,0:T(8,128)(2,1)} %v_hbm.1), custom_call_target="tpu_custom_call" | custom-call | flops 301989888 | bytes 2949120 | tf_op jit(solution)/shard_map/pallas_call | solution.py:338
  4.1 2.5 %collective-permute-start.4 = (bf16[128,768]{1,0:T(8,128)(2,1)}, bf16[128,768]{1,0:T(8,128)(2,1)S(1)}, u32[]{:S(2)}, u32[]{:S(2)}) collective-permute-start(bf16[128,768]{1,0:T(8,128)(2,1)} %get-tuple-element.23.other_ref), channel_id=1, source_target_pairs={{0,20},{4,16},{8,28},{12,24},{16,4},{20,0},{24,12},{28,8},{1,21},{... | collective-permute-start | bytes 589832 | tf_op jit(solution)/shard_map/ppermute | solution.py:351
  6.6 1.5 %collective-permute-start.1 = (bf16[128,768]{1,0:T(8,128)(2,1)}, bf16[128,768]{1,0:T(8,128)(2,1)S(1)}, u32[]{:S(2)}, u32[]{:S(2)}) collective-permute-start(bf16[128,768]{1,0:T(8,128)(2,1)} %get-tuple-element.22.same_ref), channel_id=1, source_target_pairs={{0,8},{4,12},{8,0},{12,4},{16,24},{20,28},{24,16},{28,20},{1,9},{5... | collective-permute-start | bytes 589832 | tf_op jit(solution)/shard_map/ppermute | solution.py:351
  8.1 1.0 %copy-done.5 = bf16[128,768]{1,0:T(8,128)(2,1)S(1)} copy-done((bf16[128,768]{1,0:T(8,128)(2,1)S(1)}, bf16[128,768]{1,0:T(8,128)(2,1)}, u32[]{:S(2)}) %copy-start.5) | copy-done | bytes 196632
  9.0 1.0 %shard_map.113 = (bf16[128,768]{1,0:T(8,128)(2,1)S(1)}, bf16[128,768]{1,0:T(8,128)(2,1)S(1)}) custom-call(bf16[128,768]{1,0:T(8,128)(2,1)S(1)} %copy-done.5, bf16[128,768]{1,0:T(8,128)(2,1)} %get-tuple-element.23.other_ref), custom_call_target="tpu_custom_call" | custom-call | bytes 786432 | tf_op jit(solution)/shard_map/pallas_call | solution.py:338
  10.0 0.7 %collective-permute-start.3 = (bf16[128,768]{1,0:T(8,128)(2,1)S(1)}, bf16[128,768]{1,0:T(8,128)(2,1)S(1)}, u32[]{:S(2)}, u32[]{:S(2)}) collective-permute-start(bf16[128,768]{1,0:T(8,128)(2,1)S(1)} %get-tuple-element.24.refs_0_), channel_id=1, source_target_pairs={{0,16},{4,20},{8,24},{12,28},{16,0},{20,4},{24,8},{28,12},{1,17},{... | collective-permute-start | bytes 589832 | tf_op jit(solution)/shard_map/ppermute | solution.py:351
  11.3 0.9 %collective-permute-done.4.refs_5_.__ = bf16[128,768]{1,0:T(8,128)(2,1)S(1)} collective-permute-done((bf16[128,768]{1,0:T(8,128)(2,1)}, bf16[128,768]{1,0:T(8,128)(2,1)S(1)}, u32[]{:S(2)}, u32[]{:S(2)}) %collective-permute-start.4) | collective-permute-done | bytes 196640 | tf_op jit(solution)/shard_map/ppermute | solution.py:351
  12.2 2.3 %collective-permute-start.6 = (bf16[128,768]{1,0:T(8,128)(2,1)S(1)}, bf16[128,768]{1,0:T(8,128)(2,1)S(1)}, u32[]{:S(2)}, u32[]{:S(2)}) collective-permute-start(bf16[128,768]{1,0:T(8,128)(2,1)S(1)} %collective-permute-done.4.refs_5_.__), channel_id=1, source_target_pairs={{0,8},{4,12},{8,0},{12,4},{16,24},{20,28},{24,16},{28,20},{1,9},{5... | collective-permute-start | bytes 589832 | tf_op jit(solution)/shard_map/ppermute | solution.py:351
  14.6 1.5 %collective-permute-start.5 = (bf16[128,768]{1,0:T(8,128)(2,1)S(1)}, bf16[128,768]{1,0:T(8,128)(2,1)S(1)}, u32[]{:S(2)}, u32[]{:S(2)}) collective-permute-start(bf16[128,768]{1,0:T(8,128)(2,1)S(1)} %collective-permute-done.1.refs_2_._), channel_id=1, source_target_pairs={{0,16},{4,20},{8,24},{12,28},{16,0},{20,4},{24,8},{28,12},{1,17},{... | collective-permute-start | bytes 589832 | tf_op jit(solution)/shard_map/ppermute | solution.py:351
  16.0 1.1 %copy-done.4 = bf16[128,2304]{1,0:T(8,128)(2,1)S(1)} copy-done((bf16[128,2304]{1,0:T(8,128)(2,1)S(1)}, bf16[128,2304]{1,0:T(8,128)(2,1)}, u32[]{:S(2)}) %copy-start.4) | copy-done | bytes 589848
  17.6 1.2 %collective-permute-start.10 = (bf16[2,2,288,128]{3,2,1,0:T(8,128)(2,1)S(1)}, bf16[2,2,288,128]{3,2,1,0:T(8,128)(2,1)S(1)}, u32[]{:S(2)}, u32[]{:S(2)}) collective-permute-start(bf16[2,2,288,128]{3,2,1,0:T(8,128)(2,1)S(1)} %get-tuple-element.34), channel_id=1, source_target_pairs={{0,16},{4,20},{8,24},{12,28},{16,0},{20,4},{24,8},{28,12},{1,17},{... | collective-permute-start | bytes 884744 | tf_op jit(solution)/shard_map/ppermute | solution.py:351
  18.8 1.5 %collective-permute-start.11 = (bf16[2,2,288,128]{3,2,1,0:T(8,128)(2,1)S(1)}, bf16[2,2,288,128]{3,2,1,0:T(8,128)(2,1)S(1)}, u32[]{:S(2)}, u32[]{:S(2)}) collective-permute-start(bf16[2,2,288,128]{3,2,1,0:T(8,128)(2,1)S(1)} %get-tuple-element.35), channel_id=1, source_target_pairs={{0,24},{4,28},{8,16},{12,20},{16,8},{20,12},{24,0},{28,4},{1,25},{... | collective-permute-start | bytes 884744 | tf_op jit(solution)/shard_map/ppermute | solution.py:351
  20.3 0.9 %collective-permute-start.9 = (bf16[2,2,288,128]{3,2,1,0:T(8,128)(2,1)S(1)}, bf16[2,2,288,128]{3,2,1,0:T(8,128)(2,1)S(1)}, u32[]{:S(2)}, u32[]{:S(2)}) collective-permute-start(bf16[2,2,288,128]{3,2,1,0:T(8,128)(2,1)S(1)} %get-tuple-element.33), channel_id=1, source_target_pairs={{0,8},{4,12},{8,0},{12,4},{16,24},{20,28},{24,16},{28,20},{1,9},{5... | collective-permute-start | bytes 884744 | tf_op jit(solution)/shard_map/ppermute | solution.py:351
  21.2 1.8 %collective-permute-done.6.refs_7_ = bf16[128,768]{1,0:T(8,128)(2,1)S(1)} collective-permute-done((bf16[128,768]{1,0:T(8,128)(2,1)S(1)}, bf16[128,768]{1,0:T(8,128)(2,1)S(1)}, u32[]{:S(2)}, u32[]{:S(2)}) %collective-permute-start.6) | collective-permute-done | bytes 196640 | tf_op jit(solution)/shard_map/ppermute | solution.py:351
  23.0 4.9 %shard_map.114 = (bf16[128,512]{1,0:T(8,128)(2,1)S(1)}, bf16[128,512]{1,0:T(8,128)(2,1)S(1)}, bf16[256,1024]{1,0:T(8,128)(2,1)S(1)}, bf16[1024,2048]{1,0:T(8,128)(2,1)S(1)}, bf16[128,2048]{1,0:T(8,128)(2,1)S(1)}) custom-call(bf16[128,768]{1,0:T(8,128)(2,1)S(1)} %get-tuple-element.24.refs_0_, bf16[128,768]{1,0:T(8,128)(2,1)S(1)} %collective-permute-done.refs_1_, ...), custom_call_target="tpu_custom_call" | custom-call | flops 2147483648 | bytes 1572864 | tf_op jit(solution)/shard_map/pallas_call | solution.py:338
  28.0 1.3 %collective-permute-done.7.far_ref = bf16[128,512]{1,0:T(8,128)(2,1)S(1)} collective-permute-done((bf16[128,512]{1,0:T(8,128)(2,1)S(1)}, bf16[128,512]{1,0:T(8,128)(2,1)S(1)}, u32[]{:S(2)}, u32[]{:S(2)}) %collective-permute-start.7) | collective-permute-done | bytes 131104 | tf_op jit(solution)/shard_map/ppermute | solution.py:351
  29.8 1.6 %collective-permute-start.8 = (bf16[576,128]{1,0:T(8,128)(2,1)S(1)}, bf16[576,128]{1,0:T(8,128)(2,1)S(1)}, u32[]{:S(2)}, u32[]{:S(2)}) collective-permute-start(bf16[576,128]{1,0:T(8,128)(2,1)S(1)} %shard_map.117), channel_id=1, source_target_pairs={{0,1},{1,0},{2,3},{3,2},{4,5},{5,4},{6,7},{7,6},{8,9},{9,8},{10,11... | collective-permute-start | bytes 442376 | tf_op jit(solution)/shard_map/ppermute | solution.py:351
  31.5 1.0 %shard_map.115._.dv_t_ref = bf16[128,1024]{1,0:T(8,128)(2,1)S(1)} custom-call(bf16[1024,2048]{1,0:T(8,128)(2,1)S(1)} %get-tuple-element.27.prob_ref, bf16[128,2048]{1,0:T(8,128)(2,1)S(1)} %get-tuple-element.28.grad_t_ref), custom_call_target="tpu_custom_call" | custom-call | flops 268435456 | bytes 4194304 | tf_op jit(solution)/shard_map/pallas_call | solution.py:338
  32.5 1.1 %shard_map.116 = (bf16[576,128]{1,0:T(8,128)(2,1)S(1)}, bf16[576,128]{1,0:T(8,128)(2,1)S(1)}, f32[576,128]{1,0:T(8,128)S(1)}) custom-call(bf16[128,512]{1,0:T(8,128)(2,1)S(1)} %get-tuple-element.29.own_ref, bf16[128,512]{1,0:T(8,128)(2,1)S(1)} %collective-permute-done.7.far_ref, bf16[2304,512]{1,0:T(8,128)(2,1)S(1)} %copy-done, ...), custom_call_target="tpu_custom_call" | custom-call | flops 452984832 | bytes 3538944 | tf_op jit(solution)/shard_map/pallas_call | solution.py:338
  33.6 2.2 %collective-permute-done.8.arrived_ref = bf16[576,128]{1,0:T(8,128)(2,1)S(1)} collective-permute-done((bf16[576,128]{1,0:T(8,128)(2,1)S(1)}, bf16[576,128]{1,0:T(8,128)(2,1)S(1)}, u32[]{:S(2)}, u32[]{:S(2)}) %collective-permute-start.8) | collective-permute-done | bytes 147488 | tf_op jit(solution)/shard_map/ppermute | solution.py:351
  36.1 2.7 %collective-permute-start.13 = (bf16[576,128]{1,0:T(8,128)(2,1)S(1)}, bf16[576,128]{1,0:T(8,128)(2,1)S(1)}, u32[]{:S(2)}, u32[]{:S(2)}) collective-permute-start(bf16[576,128]{1,0:T(8,128)(2,1)S(1)} %shard_map.118._), channel_id=1, source_target_pairs={{0,2},{1,3},{2,0},{3,1},{4,6},{5,7},{6,4},{7,5},{8,10},{9,11},{10,... | collective-permute-start | bytes 442376 | tf_op jit(solution)/shard_map/ppermute | solution.py:351
  38.8 1.6 %collective-permute-start.14 = (bf16[576,128]{1,0:T(8,128)(2,1)S(1)}, bf16[576,128]{1,0:T(8,128)(2,1)S(1)}, u32[]{:S(2)}, u32[]{:S(2)}) collective-permute-start(bf16[576,128]{1,0:T(8,128)(2,1)S(1)} %get-tuple-element.38), channel_id=1, source_target_pairs={{0,1},{1,0},{2,3},{3,2},{4,5},{5,4},{6,7},{7,6},{8,9},{9,8},{10,11... | collective-permute-start | bytes 442376 | tf_op jit(solution)/shard_map/ppermute | solution.py:351
  40.4 2.0 %shard_map.121 = (f32[288,256]{1,0:T(8,128)}, f32[288,512]{1,0:T(8,128)}, f32[8,128]{1,0:T(8,128)S(1)}) custom-call(bf16[256,1024]{1,0:T(8,128)(2,1)S(1)} %get-tuple-element.26.attn_ref, bf16[128,1024]{1,0:T(8,128)(2,1)S(1)} %shard_map.115._.dv_t_ref, bf16[5376,128]{1,0:T(8,128)(2,1)S(1)} %collective-permute-done.12.got_ref, ...), custom_call_target="tpu_custom_call" | custom-call | tf_op jit(solution)/shard_map/pallas_call | solution.py:338
  42.4 4.2 %collective-permute-done.13.arrived_ref = bf16[576,128]{1,0:T(8,128)(2,1)S(1)} collective-permute-done((bf16[576,128]{1,0:T(8,128)(2,1)S(1)}, bf16[576,128]{1,0:T(8,128)(2,1)S(1)}, u32[]{:S(2)}, u32[]{:S(2)}) %collective-permute-start.13) | collective-permute-done | bytes 147488 | tf_op jit(solution)/shard_map/ppermute | solution.py:351
  (30 shorter events, 3.1 us)
Async XLA Ops:
  0.6 15.4 %copy-start.3 = (bf16[128,2304]{1,0:T(8,128)(2,1)S(1)}, bf16[128,2304]{1,0:T(8,128)(2,1)}, u32[]{:S(2)}) copy-start(bf16[128,2304]{1,0:T(8,128)(2,1)} %cot_ref.1) | copy-start | bytes 1769476
  4.1 8.1 %collective-permute-start.4 = (bf16[128,768]{1,0:T(8,128)(2,1)}, bf16[128,768]{1,0:T(8,128)(2,1)S(1)}, u32[]{:S(2)}, u32[]{:S(2)}) collective-permute-start(bf16[128,768]{1,0:T(8,128)(2,1)} %get-tuple-element.23.other_ref), channel_id=1, source_target_pairs={{0,20},{4,16},{8,28},{12,24},{16,4},{20,0},{24,12},{28,8},{1,21},{... | collective-permute-start | bytes 589832 | tf_op jit(solution)/shard_map/ppermute | solution.py:351
  6.6 8.0 %collective-permute-start.1 = (bf16[128,768]{1,0:T(8,128)(2,1)}, bf16[128,768]{1,0:T(8,128)(2,1)S(1)}, u32[]{:S(2)}, u32[]{:S(2)}) collective-permute-start(bf16[128,768]{1,0:T(8,128)(2,1)} %get-tuple-element.22.same_ref), channel_id=1, source_target_pairs={{0,8},{4,12},{8,0},{12,4},{16,24},{20,28},{24,16},{28,20},{1,9},{5... | collective-permute-start | bytes 589832 | tf_op jit(solution)/shard_map/ppermute | solution.py:351
  8.1 1.0 %copy-start.5 = (bf16[128,768]{1,0:T(8,128)(2,1)S(1)}, bf16[128,768]{1,0:T(8,128)(2,1)}, u32[]{:S(2)}) copy-start(bf16[128,768]{1,0:T(8,128)(2,1)} %get-tuple-element.22.same_ref) | copy-start | bytes 589828
  10.0 7.6 %collective-permute-start.3 = (bf16[128,768]{1,0:T(8,128)(2,1)S(1)}, bf16[128,768]{1,0:T(8,128)(2,1)S(1)}, u32[]{:S(2)}, u32[]{:S(2)}) collective-permute-start(bf16[128,768]{1,0:T(8,128)(2,1)S(1)} %get-tuple-element.24.refs_0_), channel_id=1, source_target_pairs={{0,16},{4,20},{8,24},{12,28},{16,0},{20,4},{24,8},{28,12},{1,17},{... | collective-permute-start | bytes 589832 | tf_op jit(solution)/shard_map/ppermute | solution.py:351
  10.7 8.1 %collective-permute-start.2 = (bf16[128,768]{1,0:T(8,128)(2,1)S(1)}, bf16[128,768]{1,0:T(8,128)(2,1)S(1)}, u32[]{:S(2)}, u32[]{:S(2)}) collective-permute-start(bf16[128,768]{1,0:T(8,128)(2,1)S(1)} %get-tuple-element.25), channel_id=1, source_target_pairs={{0,12},{4,8},{8,4},{12,0},{16,28},{20,24},{24,20},{28,16},{1,13},{... | collective-permute-start | bytes 589832 | tf_op jit(solution)/shard_map/ppermute | solution.py:351
  10.7 9.6 %collective-permute-start = (bf16[128,768]{1,0:T(8,128)(2,1)}, bf16[128,768]{1,0:T(8,128)(2,1)S(1)}, u32[]{:S(2)}, u32[]{:S(2)}) collective-permute-start(bf16[128,768]{1,0:T(8,128)(2,1)} %get-tuple-element.23.other_ref), channel_id=1, source_target_pairs={{0,4},{4,0},{8,12},{12,8},{16,20},{20,16},{24,28},{28,24},{1,5},{5... | collective-permute-start | bytes 589832 | tf_op jit(solution)/shard_map/ppermute | solution.py:351
  12.2 10.8 %collective-permute-start.6 = (bf16[128,768]{1,0:T(8,128)(2,1)S(1)}, bf16[128,768]{1,0:T(8,128)(2,1)S(1)}, u32[]{:S(2)}, u32[]{:S(2)}) collective-permute-start(bf16[128,768]{1,0:T(8,128)(2,1)S(1)} %collective-permute-done.4.refs_5_.__), channel_id=1, source_target_pairs={{0,8},{4,12},{8,0},{12,4},{16,24},{20,28},{24,16},{28,20},{1,9},{5... | collective-permute-start | bytes 589832 | tf_op jit(solution)/shard_map/ppermute | solution.py:351
  14.6 8.4 %collective-permute-start.5 = (bf16[128,768]{1,0:T(8,128)(2,1)S(1)}, bf16[128,768]{1,0:T(8,128)(2,1)S(1)}, u32[]{:S(2)}, u32[]{:S(2)}) collective-permute-start(bf16[128,768]{1,0:T(8,128)(2,1)S(1)} %collective-permute-done.1.refs_2_._), channel_id=1, source_target_pairs={{0,16},{4,20},{8,24},{12,28},{16,0},{20,4},{24,8},{28,12},{1,17},{... | collective-permute-start | bytes 589832 | tf_op jit(solution)/shard_map/ppermute | solution.py:351
  16.0 1.1 %copy-start.4 = (bf16[128,2304]{1,0:T(8,128)(2,1)S(1)}, bf16[128,2304]{1,0:T(8,128)(2,1)}, u32[]{:S(2)}) copy-start(bf16[128,2304]{1,0:T(8,128)(2,1)} %normed_ref.1) | copy-start | bytes 1769476
  17.6 18.2 %collective-permute-start.10 = (bf16[2,2,288,128]{3,2,1,0:T(8,128)(2,1)S(1)}, bf16[2,2,288,128]{3,2,1,0:T(8,128)(2,1)S(1)}, u32[]{:S(2)}, u32[]{:S(2)}) collective-permute-start(bf16[2,2,288,128]{3,2,1,0:T(8,128)(2,1)S(1)} %get-tuple-element.34), channel_id=1, source_target_pairs={{0,16},{4,20},{8,24},{12,28},{16,0},{20,4},{24,8},{28,12},{1,17},{... | collective-permute-start | bytes 884744 | tf_op jit(solution)/shard_map/ppermute | solution.py:351
  18.8 17.1 %collective-permute-start.11 = (bf16[2,2,288,128]{3,2,1,0:T(8,128)(2,1)S(1)}, bf16[2,2,288,128]{3,2,1,0:T(8,128)(2,1)S(1)}, u32[]{:S(2)}, u32[]{:S(2)}) collective-permute-start(bf16[2,2,288,128]{3,2,1,0:T(8,128)(2,1)S(1)} %get-tuple-element.35), channel_id=1, source_target_pairs={{0,24},{4,28},{8,16},{12,20},{16,8},{20,12},{24,0},{28,4},{1,25},{... | collective-permute-start | bytes 884744 | tf_op jit(solution)/shard_map/ppermute | solution.py:351
  20.3 9.0 %copy-start.1 = (bf16[2304,256]{1,0:T(8,128)(2,1)S(1)}, bf16[2304,256]{1,0:T(8,128)(2,1)}, u32[]{:S(2)}) copy-start(bf16[2304,256]{1,0:T(8,128)(2,1)} %wk_ref.3) | copy-start | bytes 3538948
  20.3 9.0 %copy-start.2 = (bf16[2304,256]{1,0:T(8,128)(2,1)S(1)}, bf16[2304,256]{1,0:T(8,128)(2,1)}, u32[]{:S(2)}) copy-start(bf16[2304,256]{1,0:T(8,128)(2,1)} %wv_ref.3) | copy-start | bytes 3538948
  20.3 15.6 %collective-permute-start.9 = (bf16[2,2,288,128]{3,2,1,0:T(8,128)(2,1)S(1)}, bf16[2,2,288,128]{3,2,1,0:T(8,128)(2,1)S(1)}, u32[]{:S(2)}, u32[]{:S(2)}) collective-permute-start(bf16[2,2,288,128]{3,2,1,0:T(8,128)(2,1)S(1)} %get-tuple-element.33), channel_id=1, source_target_pairs={{0,8},{4,12},{8,0},{12,4},{16,24},{20,28},{24,16},{28,20},{1,9},{5... | collective-permute-start | bytes 884744 | tf_op jit(solution)/shard_map/ppermute | solution.py:351
  23.0 6.3 %copy-start = (bf16[2304,512]{1,0:T(8,128)(2,1)S(1)}, bf16[2304,512]{1,0:T(8,128)(2,1)}, u32[]{:S(2)}) copy-start(bf16[2304,512]{1,0:T(8,128)(2,1)} %wq_ref.3) | copy-start | bytes 7077892
  27.9 1.4 %collective-permute-start.7 = (bf16[128,512]{1,0:T(8,128)(2,1)S(1)}, bf16[128,512]{1,0:T(8,128)(2,1)S(1)}, u32[]{:S(2)}, u32[]{:S(2)}) collective-permute-start(bf16[128,512]{1,0:T(8,128)(2,1)S(1)} %get-tuple-element.30), channel_id=1, source_target_pairs={{0,4},{4,0},{8,12},{12,8},{16,20},{20,16},{24,28},{28,24},{1,5},{5... | collective-permute-start | bytes 393224 | tf_op jit(solution)/shard_map/ppermute | solution.py:351
  29.8 6.0 %collective-permute-start.8 = (bf16[576,128]{1,0:T(8,128)(2,1)S(1)}, bf16[576,128]{1,0:T(8,128)(2,1)S(1)}, u32[]{:S(2)}, u32[]{:S(2)}) collective-permute-start(bf16[576,128]{1,0:T(8,128)(2,1)S(1)} %shard_map.117), channel_id=1, source_target_pairs={{0,1},{1,0},{2,3},{3,2},{4,5},{5,4},{6,7},{7,6},{8,9},{9,8},{10,11... | collective-permute-start | bytes 442376 | tf_op jit(solution)/shard_map/ppermute | solution.py:351
  36.1 4.3 %collective-permute-start.12 = (bf16[5376,128]{1,0:T(8,128)(2,1)S(1)}, bf16[5376,128]{1,0:T(8,128)(2,1)S(1)}, u32[]{:S(2)}, u32[]{:S(2)}) collective-permute-start(bf16[5376,128]{1,0:T(8,128)(2,1)S(1)} %shard_map.120), channel_id=1, source_target_pairs={{0,4},{4,0},{8,12},{12,8},{16,20},{20,16},{24,28},{28,24},{1,5},{5... | collective-permute-start | bytes 4128776 | tf_op jit(solution)/shard_map/ppermute | solution.py:351
  36.1 10.4 %collective-permute-start.13 = (bf16[576,128]{1,0:T(8,128)(2,1)S(1)}, bf16[576,128]{1,0:T(8,128)(2,1)S(1)}, u32[]{:S(2)}, u32[]{:S(2)}) collective-permute-start(bf16[576,128]{1,0:T(8,128)(2,1)S(1)} %shard_map.118._), channel_id=1, source_target_pairs={{0,2},{1,3},{2,0},{3,1},{4,6},{5,7},{6,4},{7,5},{8,10},{9,11},{10,... | collective-permute-start | bytes 442376 | tf_op jit(solution)/shard_map/ppermute | solution.py:351
  38.8 8.0 %collective-permute-start.14 = (bf16[576,128]{1,0:T(8,128)(2,1)S(1)}, bf16[576,128]{1,0:T(8,128)(2,1)S(1)}, u32[]{:S(2)}, u32[]{:S(2)}) collective-permute-start(bf16[576,128]{1,0:T(8,128)(2,1)S(1)} %get-tuple-element.38), channel_id=1, source_target_pairs={{0,1},{1,0},{2,3},{3,2},{4,5},{5,4},{6,7},{7,6},{8,9},{9,8},{10,11... | collective-permute-start | bytes 442376 | tf_op jit(solution)/shard_map/ppermute | solution.py:351

commit v27 on v26

--- a/solution.py
+++ b/solution.py
@@ -411,7 +411,7 @@
     columns = kernel_call(
         turn_kernel,
         (shape((2, 2, cut, rows), bf16),) * (blocks // 2),
-        (normed_input, out_cotangent, held[2], held[blocks // 2 + 1]),
+        (normed_input, out_cotangent, held[3], held[blocks // 2]),
         in_vmem=range(2),
         scratch=(pltpu.VMEM((2, model, rows), bf16),),
         moved=8 * rows * model,

time: 47.7 us -> 48.8 us (1.023)
  waiting for transfers between devices: 10.7 us -> 11.8 us
    ppermute x15, waiting for transfers between devices: 10.7 us -> 11.8 us  [swapped(): lax.ppermute(value, axis, [(place, place ^ apart) for place in range(coun...]
  transfers between devices with their start and end apart: 15 -> 15, of which waited for: 7 -> 9; matrix products, arithmetic and copies ran while one was open for 0% -> 0% of each run, Pallas kernels for 23% -> 23%
where the time goes in v27:
time: 48.8 us; the launch traced here: 48.6 us
  starting transfers between devices  18.6 us (38%)
  Pallas kernels  15.3 us (31%)
  waiting for transfers between devices  11.8 us (24%)
  local copies, waits for them, and re-layouts  2.04 us (4%)
  between operations  0.75 us (2%)
    ppermute x15, starting transfers between devices, swapped(): lax.ppermute(value, axis, [(place, place ^ apart) for place in range(coun...  18.6 us
    pallas_call x12, Pallas kernels, kernel_call(): pl.pallas_call(body, out_shape=outs, in_specs=[vmem if place in in_vmem e...  15.3 us
    ppermute x15, waiting for transfers between devices, swapped(): lax.ppermute(value, axis, [(place, place ^ apart) for place in range(coun...  11.8 us
    unnamed x12, local copies, waits for them, and re-layouts  2.04 us
  transfers between devices with their start and end apart: 15, of which 9 were waited for; matrix products, arithmetic and copies ran while one was open for 0% of the time, Pallas kernels for 23%

profile of v27, /device:TPU:0, one launch (start us, length us, event | category | flops | bytes accessed | tf_op | source)
XLA Modules:
  0.0 48.6 jit_solution(5444919271213347873)
XLA Ops:
  0.6 3.5 %shard_map.112 = (bf16[128,768]{1,0:T(8,128)(2,1)}, bf16[128,768]{1,0:T(8,128)(2,1)}) custom-call(bf16[128,2304]{1,0:T(8,128)(2,1)} %cot_ref.1, bf16[512,2304]{1,0:T(8,128)(2,1)} %weight_hbm.1, bf16[128,512]{1,0:T(8,128)(2,1)} %q_hbm.1, bf16[128,256]{1,0:T(8,128)(2,1)} %k_hbm.1, bf16[128,256]{1,0:T(8,128)(2,1)} %v_hbm.1), custom_call_target="tpu_custom_call" | custom-call | flops 301989888 | bytes 2949120 | tf_op jit(solution)/shard_map/pallas_call | solution.py:338
  4.1 2.5 %collective-permute-start.4 = (bf16[128,768]{1,0:T(8,128)(2,1)}, bf16[128,768]{1,0:T(8,128)(2,1)S(1)}, u32[]{:S(2)}, u32[]{:S(2)}) collective-permute-start(bf16[128,768]{1,0:T(8,128)(2,1)} %get-tuple-element.23.other_ref), channel_id=1, source_target_pairs={{0,20},{4,16},{8,28},{12,24},{16,4},{20,0},{24,12},{28,8},{1,21},{... | collective-permute-start | bytes 589832 | tf_op jit(solution)/shard_map/ppermute | solution.py:351
  6.6 1.5 %collective-permute-start.1 = (bf16[128,768]{1,0:T(8,128)(2,1)}, bf16[128,768]{1,0:T(8,128)(2,1)S(1)}, u32[]{:S(2)}, u32[]{:S(2)}) collective-permute-start(bf16[128,768]{1,0:T(8,128)(2,1)} %get-tuple-element.22.same_ref), channel_id=1, source_target_pairs={{0,8},{4,12},{8,0},{12,4},{16,24},{20,28},{24,16},{28,20},{1,9},{5... | collective-permute-start | bytes 589832 | tf_op jit(solution)/shard_map/ppermute | solution.py:351
  8.1 1.0 %copy-done.5 = bf16[128,768]{1,0:T(8,128)(2,1)S(1)} copy-done((bf16[128,768]{1,0:T(8,128)(2,1)S(1)}, bf16[128,768]{1,0:T(8,128)(2,1)}, u32[]{:S(2)}) %copy-start.5) | copy-done | bytes 196632
  9.0 1.0 %shard_map.113 = (bf16[128,768]{1,0:T(8,128)(2,1)S(1)}, bf16[128,768]{1,0:T(8,128)(2,1)S(1)}) custom-call(bf16[128,768]{1,0:T(8,128)(2,1)S(1)} %copy-done.5, bf16[128,768]{1,0:T(8,128)(2,1)} %get-tuple-element.23.other_ref), custom_call_target="tpu_custom_call" | custom-call | bytes 786432 | tf_op jit(solution)/shard_map/pallas_call | solution.py:338
  11.3 0.9 %collective-permute-done.4.refs_5_ = bf16[128,768]{1,0:T(8,128)(2,1)S(1)} collective-permute-done((bf16[128,768]{1,0:T(8,128)(2,1)}, bf16[128,768]{1,0:T(8,128)(2,1)S(1)}, u32[]{:S(2)}, u32[]{:S(2)}) %collective-permute-start.4) | collective-permute-done | bytes 196640 | tf_op jit(solution)/shard_map/ppermute | solution.py:351
  12.2 2.3 %collective-permute-start.6 = (bf16[128,768]{1,0:T(8,128)(2,1)S(1)}, bf16[128,768]{1,0:T(8,128)(2,1)S(1)}, u32[]{:S(2)}, u32[]{:S(2)}) collective-permute-start(bf16[128,768]{1,0:T(8,128)(2,1)S(1)} %collective-permute-done.4.refs_5_), channel_id=1, source_target_pairs={{0,8},{4,12},{8,0},{12,4},{16,24},{20,28},{24,16},{28,20},{1,9},{5... | collective-permute-start | bytes 589832 | tf_op jit(solution)/shard_map/ppermute | solution.py:351
  14.6 1.5 %collective-permute-start.5 = (bf16[128,768]{1,0:T(8,128)(2,1)S(1)}, bf16[128,768]{1,0:T(8,128)(2,1)S(1)}, u32[]{:S(2)}, u32[]{:S(2)}) collective-permute-start(bf16[128,768]{1,0:T(8,128)(2,1)S(1)} %collective-permute-done.1.refs_2_), channel_id=1, source_target_pairs={{0,16},{4,20},{8,24},{12,28},{16,0},{20,4},{24,8},{28,12},{1,17},{... | collective-permute-start | bytes 589832 | tf_op jit(solution)/shard_map/ppermute | solution.py:351
  16.0 1.4 %collective-permute-done.3.refs_4_.__ = bf16[128,768]{1,0:T(8,128)(2,1)S(1)} collective-permute-done((bf16[128,768]{1,0:T(8,128)(2,1)S(1)}, bf16[128,768]{1,0:T(8,128)(2,1)S(1)}, u32[]{:S(2)}, u32[]{:S(2)}) %collective-permute-start.3) | collective-permute-done | bytes 196640 | tf_op jit(solution)/shard_map/ppermute | solution.py:351
  17.4 0.8 %collective-permute-done.2.refs_3_._ = bf16[128,768]{1,0:T(8,128)(2,1)S(1)} collective-permute-done((bf16[128,768]{1,0:T(8,128)(2,1)S(1)}, bf16[128,768]{1,0:T(8,128)(2,1)S(1)}, u32[]{:S(2)}, u32[]{:S(2)}) %collective-permute-start.2) | collective-permute-done | bytes 196640 | tf_op jit(solution)/shard_map/ppermute | solution.py:351
  18.2 1.1 %copy-done.4 = bf16[128,2304]{1,0:T(8,128)(2,1)S(1)} copy-done((bf16[128,2304]{1,0:T(8,128)(2,1)S(1)}, bf16[128,2304]{1,0:T(8,128)(2,1)}, u32[]{:S(2)}) %copy-start.4) | copy-done | bytes 589848
  19.7 0.9 %collective-permute-start.10 = (bf16[2,2,288,128]{3,2,1,0:T(8,128)(2,1)S(1)}, bf16[2,2,288,128]{3,2,1,0:T(8,128)(2,1)S(1)}, u32[]{:S(2)}, u32[]{:S(2)}) collective-permute-start(bf16[2,2,288,128]{3,2,1,0:T(8,128)(2,1)S(1)} %get-tuple-element.34), channel_id=1, source_target_pairs={{0,16},{4,20},{8,24},{12,28},{16,0},{20,4},{24,8},{28,12},{1,17},{... | collective-permute-start | bytes 884744 | tf_op jit(solution)/shard_map/ppermute | solution.py:351
  20.7 2.1 %collective-permute-start.11 = (bf16[2,2,288,128]{3,2,1,0:T(8,128)(2,1)S(1)}, bf16[2,2,288,128]{3,2,1,0:T(8,128)(2,1)S(1)}, u32[]{:S(2)}, u32[]{:S(2)}) collective-permute-start(bf16[2,2,288,128]{3,2,1,0:T(8,128)(2,1)S(1)} %get-tuple-element.35), channel_id=1, source_target_pairs={{0,24},{4,28},{8,16},{12,20},{16,8},{20,12},{24,0},{28,4},{1,25},{... | collective-permute-start | bytes 884744 | tf_op jit(solution)/shard_map/ppermute | solution.py:351
  23.3 4.9 %shard_map.114 = (bf16[128,512]{1,0:T(8,128)(2,1)S(1)}, bf16[128,512]{1,0:T(8,128)(2,1)S(1)}, bf16[256,1024]{1,0:T(8,128)(2,1)S(1)}, bf16[1024,2048]{1,0:T(8,128)(2,1)S(1)}, bf16[128,2048]{1,0:T(8,128)(2,1)S(1)}) custom-call(bf16[128,768]{1,0:T(8,128)(2,1)S(1)} %get-tuple-element.24.refs_0_, bf16[128,768]{1,0:T(8,128)(2,1)S(1)} %collective-permute-done.refs_1_, ...), custom_call_target="tpu_custom_call" | custom-call | flops 2147483648 | bytes 1572864 | tf_op jit(solution)/shard_map/pallas_call | solution.py:338
  28.3 1.3 %collective-permute-done.7.far_ref = bf16[128,512]{1,0:T(8,128)(2,1)S(1)} collective-permute-done((bf16[128,512]{1,0:T(8,128)(2,1)S(1)}, bf16[128,512]{1,0:T(8,128)(2,1)S(1)}, u32[]{:S(2)}, u32[]{:S(2)}) %collective-permute-start.7) | collective-permute-done | bytes 131104 | tf_op jit(solution)/shard_map/ppermute | solution.py:351
  30.2 1.7 %collective-permute-start.8 = (bf16[576,128]{1,0:T(8,128)(2,1)S(1)}, bf16[576,128]{1,0:T(8,128)(2,1)S(1)}, u32[]{:S(2)}, u32[]{:S(2)}) collective-permute-start(bf16[576,128]{1,0:T(8,128)(2,1)S(1)} %shard_map.117), channel_id=1, source_target_pairs={{0,1},{1,0},{2,3},{3,2},{4,5},{5,4},{6,7},{7,6},{8,9},{9,8},{10,11... | collective-permute-start | bytes 442376 | tf_op jit(solution)/shard_map/ppermute | solution.py:351
  31.8 1.0 %shard_map.115._.dv_t_ref = bf16[128,1024]{1,0:T(8,128)(2,1)S(1)} custom-call(bf16[1024,2048]{1,0:T(8,128)(2,1)S(1)} %get-tuple-element.27.prob_ref, bf16[128,2048]{1,0:T(8,128)(2,1)S(1)} %get-tuple-element.28.grad_t_ref), custom_call_target="tpu_custom_call" | custom-call | flops 268435456 | bytes 4194304 | tf_op jit(solution)/shard_map/pallas_call | solution.py:338
  32.8 1.1 %shard_map.116 = (bf16[576,128]{1,0:T(8,128)(2,1)S(1)}, bf16[576,128]{1,0:T(8,128)(2,1)S(1)}, f32[576,128]{1,0:T(8,128)S(1)}) custom-call(bf16[128,512]{1,0:T(8,128)(2,1)S(1)} %get-tuple-element.29.own_ref, bf16[128,512]{1,0:T(8,128)(2,1)S(1)} %collective-permute-done.7.far_ref, bf16[2304,512]{1,0:T(8,128)(2,1)S(1)} %copy-done, ...), custom_call_target="tpu_custom_call" | custom-call | flops 452984832 | bytes 3538944 | tf_op jit(solution)/shard_map/pallas_call | solution.py:338
  33.9 2.2 %collective-permute-done.8.arrived_ref = bf16[576,128]{1,0:T(8,128)(2,1)S(1)} collective-permute-done((bf16[576,128]{1,0:T(8,128)(2,1)S(1)}, bf16[576,128]{1,0:T(8,128)(2,1)S(1)}, u32[]{:S(2)}, u32[]{:S(2)}) %collective-permute-start.8) | collective-permute-done | bytes 147488 | tf_op jit(solution)/shard_map/ppermute | solution.py:351
  36.2 0.8 %collective-permute-done.9.refs_1_ = bf16[2,2,288,128]{3,2,1,0:T(8,128)(2,1)S(1)} collective-permute-done((bf16[2,2,288,128]{3,2,1,0:T(8,128)(2,1)S(1)}, bf16[2,2,288,128]{3,2,1,0:T(8,128)(2,1)S(1)}, u32[]{:S(2)}, u32[]{:S(2)}) %collective-permute-start.9) | collective-permute-done | bytes 294944 | tf_op jit(solution)/shard_map/ppermute | solution.py:351
  37.2 2.7 %collective-permute-start.13 = (bf16[576,128]{1,0:T(8,128)(2,1)S(1)}, bf16[576,128]{1,0:T(8,128)(2,1)S(1)}, u32[]{:S(2)}, u32[]{:S(2)}) collective-permute-start(bf16[576,128]{1,0:T(8,128)(2,1)S(1)} %shard_map.118._), channel_id=1, source_target_pairs={{0,2},{1,3},{2,0},{3,1},{4,6},{5,7},{6,4},{7,5},{8,10},{9,11},{10,... | collective-permute-start | bytes 442376 | tf_op jit(solution)/shard_map/ppermute | solution.py:351
  39.9 1.6 %collective-permute-start.14 = (bf16[576,128]{1,0:T(8,128)(2,1)S(1)}, bf16[576,128]{1,0:T(8,128)(2,1)S(1)}, u32[]{:S(2)}, u32[]{:S(2)}) collective-permute-start(bf16[576,128]{1,0:T(8,128)(2,1)S(1)} %get-tuple-element.38), channel_id=1, source_target_pairs={{0,1},{1,0},{2,3},{3,2},{4,5},{5,4},{6,7},{7,6},{8,9},{9,8},{10,11... | collective-permute-start | bytes 442376 | tf_op jit(solution)/shard_map/ppermute | solution.py:351
  41.5 2.0 %shard_map.121 = (f32[288,256]{1,0:T(8,128)}, f32[288,512]{1,0:T(8,128)}, f32[8,128]{1,0:T(8,128)S(1)}) custom-call(bf16[256,1024]{1,0:T(8,128)(2,1)S(1)} %get-tuple-element.26.attn_ref, bf16[128,1024]{1,0:T(8,128)(2,1)S(1)} %shard_map.115._.dv_t_ref, bf16[5376,128]{1,0:T(8,128)(2,1)S(1)} %collective-permute-done.12.got_ref, ...), custom_call_target="tpu_custom_call" | custom-call | tf_op jit(solution)/shard_map/pallas_call | solution.py:338
  43.5 4.2 %collective-permute-done.13.arrived_ref = bf16[576,128]{1,0:T(8,128)(2,1)S(1)} collective-permute-done((bf16[576,128]{1,0:T(8,128)(2,1)S(1)}, bf16[576,128]{1,0:T(8,128)(2,1)S(1)}, u32[]{:S(2)}, u32[]{:S(2)}) %collective-permute-start.13) | collective-permute-done | bytes 147488 | tf_op jit(solution)/shard_map/ppermute | solution.py:351
  (30 shorter events, 4.3 us)
Async XLA Ops:
  0.6 17.5 %copy-start.3 = (bf16[128,2304]{1,0:T(8,128)(2,1)S(1)}, bf16[128,2304]{1,0:T(8,128)(2,1)}, u32[]{:S(2)}) copy-start(bf16[128,2304]{1,0:T(8,128)(2,1)} %cot_ref.1) | copy-start | bytes 1769476
  4.1 8.1 %collective-permute-start.4 = (bf16[128,768]{1,0:T(8,128)(2,1)}, bf16[128,768]{1,0:T(8,128)(2,1)S(1)}, u32[]{:S(2)}, u32[]{:S(2)}) collective-permute-start(bf16[128,768]{1,0:T(8,128)(2,1)} %get-tuple-element.23.other_ref), channel_id=1, source_target_pairs={{0,20},{4,16},{8,28},{12,24},{16,4},{20,0},{24,12},{28,8},{1,21},{... | collective-permute-start | bytes 589832 | tf_op jit(solution)/shard_map/ppermute | solution.py:351
  6.6 8.0 %collective-permute-start.1 = (bf16[128,768]{1,0:T(8,128)(2,1)}, bf16[128,768]{1,0:T(8,128)(2,1)S(1)}, u32[]{:S(2)}, u32[]{:S(2)}) collective-permute-start(bf16[128,768]{1,0:T(8,128)(2,1)} %get-tuple-element.22.same_ref), channel_id=1, source_target_pairs={{0,8},{4,12},{8,0},{12,4},{16,24},{20,28},{24,16},{28,20},{1,9},{5... | collective-permute-start | bytes 589832 | tf_op jit(solution)/shard_map/ppermute | solution.py:351
  8.1 1.0 %copy-start.5 = (bf16[128,768]{1,0:T(8,128)(2,1)S(1)}, bf16[128,768]{1,0:T(8,128)(2,1)}, u32[]{:S(2)}) copy-start(bf16[128,768]{1,0:T(8,128)(2,1)} %get-tuple-element.22.same_ref) | copy-start | bytes 589828
  10.0 7.4 %collective-permute-start.3 = (bf16[128,768]{1,0:T(8,128)(2,1)S(1)}, bf16[128,768]{1,0:T(8,128)(2,1)S(1)}, u32[]{:S(2)}, u32[]{:S(2)}) collective-permute-start(bf16[128,768]{1,0:T(8,128)(2,1)S(1)} %get-tuple-element.24.refs_0_), channel_id=1, source_target_pairs={{0,16},{4,20},{8,24},{12,28},{16,0},{20,4},{24,8},{28,12},{1,17},{... | collective-permute-start | bytes 589832 | tf_op jit(solution)/shard_map/ppermute | solution.py:351
  10.7 7.5 %collective-permute-start.2 = (bf16[128,768]{1,0:T(8,128)(2,1)S(1)}, bf16[128,768]{1,0:T(8,128)(2,1)S(1)}, u32[]{:S(2)}, u32[]{:S(2)}) collective-permute-start(bf16[128,768]{1,0:T(8,128)(2,1)S(1)} %get-tuple-element.25), channel_id=1, source_target_pairs={{0,12},{4,8},{8,4},{12,0},{16,28},{20,24},{24,20},{28,16},{1,13},{... | collective-permute-start | bytes 589832 | tf_op jit(solution)/shard_map/ppermute | solution.py:351
  10.7 12.1 %collective-permute-start = (bf16[128,768]{1,0:T(8,128)(2,1)}, bf16[128,768]{1,0:T(8,128)(2,1)S(1)}, u32[]{:S(2)}, u32[]{:S(2)}) collective-permute-start(bf16[128,768]{1,0:T(8,128)(2,1)} %get-tuple-element.23.other_ref), channel_id=1, source_target_pairs={{0,4},{4,0},{8,12},{12,8},{16,20},{20,16},{24,28},{28,24},{1,5},{5... | collective-permute-start | bytes 589832 | tf_op jit(solution)/shard_map/ppermute | solution.py:351
  12.2 11.1 %collective-permute-start.6 = (bf16[128,768]{1,0:T(8,128)(2,1)S(1)}, bf16[128,768]{1,0:T(8,128)(2,1)S(1)}, u32[]{:S(2)}, u32[]{:S(2)}) collective-permute-start(bf16[128,768]{1,0:T(8,128)(2,1)S(1)} %collective-permute-done.4.refs_5_), channel_id=1, source_target_pairs={{0,8},{4,12},{8,0},{12,4},{16,24},{20,28},{24,16},{28,20},{1,9},{5... | collective-permute-start | bytes 589832 | tf_op jit(solution)/shard_map/ppermute | solution.py:351
  14.6 8.7 %collective-permute-start.5 = (bf16[128,768]{1,0:T(8,128)(2,1)S(1)}, bf16[128,768]{1,0:T(8,128)(2,1)S(1)}, u32[]{:S(2)}, u32[]{:S(2)}) collective-permute-start(bf16[128,768]{1,0:T(8,128)(2,1)S(1)} %collective-permute-done.1.refs_2_), channel_id=1, source_target_pairs={{0,16},{4,20},{8,24},{12,28},{16,0},{20,4},{24,8},{28,12},{1,17},{... | collective-permute-start | bytes 589832 | tf_op jit(solution)/shard_map/ppermute | solution.py:351
  18.2 1.1 %copy-start.4 = (bf16[128,2304]{1,0:T(8,128)(2,1)S(1)}, bf16[128,2304]{1,0:T(8,128)(2,1)}, u32[]{:S(2)}) copy-start(bf16[128,2304]{1,0:T(8,128)(2,1)} %normed_ref.1) | copy-start | bytes 1769476
  19.7 16.4 %collective-permute-start.10 = (bf16[2,2,288,128]{3,2,1,0:T(8,128)(2,1)S(1)}, bf16[2,2,288,128]{3,2,1,0:T(8,128)(2,1)S(1)}, u32[]{:S(2)}, u32[]{:S(2)}) collective-permute-start(bf16[2,2,288,128]{3,2,1,0:T(8,128)(2,1)S(1)} %get-tuple-element.34), channel_id=1, source_target_pairs={{0,16},{4,20},{8,24},{12,28},{16,0},{20,4},{24,8},{28,12},{1,17},{... | collective-permute-start | bytes 884744 | tf_op jit(solution)/shard_map/ppermute | solution.py:351
  20.7 15.5 %collective-permute-start.11 = (bf16[2,2,288,128]{3,2,1,0:T(8,128)(2,1)S(1)}, bf16[2,2,288,128]{3,2,1,0:T(8,128)(2,1)S(1)}, u32[]{:S(2)}, u32[]{:S(2)}) collective-permute-start(bf16[2,2,288,128]{3,2,1,0:T(8,128)(2,1)S(1)} %get-tuple-element.35), channel_id=1, source_target_pairs={{0,24},{4,28},{8,16},{12,20},{16,8},{20,12},{24,0},{28,4},{1,25},{... | collective-permute-start | bytes 884744 | tf_op jit(solution)/shard_map/ppermute | solution.py:351
  22.8 6.8 %copy-start.1 = (bf16[2304,256]{1,0:T(8,128)(2,1)S(1)}, bf16[2304,256]{1,0:T(8,128)(2,1)}, u32[]{:S(2)}) copy-start(bf16[2304,256]{1,0:T(8,128)(2,1)} %wk_ref.3) | copy-start | bytes 3538948
  22.8 6.8 %copy-start.2 = (bf16[2304,256]{1,0:T(8,128)(2,1)S(1)}, bf16[2304,256]{1,0:T(8,128)(2,1)}, u32[]{:S(2)}) copy-start(bf16[2304,256]{1,0:T(8,128)(2,1)} %wv_ref.3) | copy-start | bytes 3538948
  22.8 14.2 %collective-permute-start.9 = (bf16[2,2,288,128]{3,2,1,0:T(8,128)(2,1)S(1)}, bf16[2,2,288,128]{3,2,1,0:T(8,128)(2,1)S(1)}, u32[]{:S(2)}, u32[]{:S(2)}) collective-permute-start(bf16[2,2,288,128]{3,2,1,0:T(8,128)(2,1)S(1)} %get-tuple-element.33), channel_id=1, source_target_pairs={{0,8},{4,12},{8,0},{12,4},{16,24},{20,28},{24,16},{28,20},{1,9},{5... | collective-permute-start | bytes 884744 | tf_op jit(solution)/shard_map/ppermute | solution.py:351
  23.3 6.3 %copy-start = (bf16[2304,512]{1,0:T(8,128)(2,1)S(1)}, bf16[2304,512]{1,0:T(8,128)(2,1)}, u32[]{:S(2)}) copy-start(bf16[2304,512]{1,0:T(8,128)(2,1)} %wq_ref.3) | copy-start | bytes 7077892
  28.2 1.4 %collective-permute-start.7 = (bf16[128,512]{1,0:T(8,128)(2,1)S(1)}, bf16[128,512]{1,0:T(8,128)(2,1)S(1)}, u32[]{:S(2)}, u32[]{:S(2)}) collective-permute-start(bf16[128,512]{1,0:T(8,128)(2,1)S(1)} %get-tuple-element.30), channel_id=1, source_target_pairs={{0,4},{4,0},{8,12},{12,8},{16,20},{20,16},{24,28},{28,24},{1,5},{5... | collective-permute-start | bytes 393224 | tf_op jit(solution)/shard_map/ppermute | solution.py:351
  30.2 6.0 %collective-permute-start.8 = (bf16[576,128]{1,0:T(8,128)(2,1)S(1)}, bf16[576,128]{1,0:T(8,128)(2,1)S(1)}, u32[]{:S(2)}, u32[]{:S(2)}) collective-permute-start(bf16[576,128]{1,0:T(8,128)(2,1)S(1)} %shard_map.117), channel_id=1, source_target_pairs={{0,1},{1,0},{2,3},{3,2},{4,5},{5,4},{6,7},{7,6},{8,9},{9,8},{10,11... | collective-permute-start | bytes 442376 | tf_op jit(solution)/shard_map/ppermute | solution.py:351
  37.2 4.3 %collective-permute-start.12 = (bf16[5376,128]{1,0:T(8,128)(2,1)S(1)}, bf16[5376,128]{1,0:T(8,128)(2,1)S(1)}, u32[]{:S(2)}, u32[]{:S(2)}) collective-permute-start(bf16[5376,128]{1,0:T(8,128)(2,1)S(1)} %shard_map.120), channel_id=1, source_target_pairs={{0,4},{4,0},{8,12},{12,8},{16,20},{20,16},{24,28},{28,24},{1,5},{5... | collective-permute-start | bytes 4128776 | tf_op jit(solution)/shard_map/ppermute | solution.py:351
  37.2 10.4 %collective-permute-start.13 = (bf16[576,128]{1,0:T(8,128)(2,1)S(1)}, bf16[576,128]{1,0:T(8,128)(2,1)S(1)}, u32[]{:S(2)}, u32[]{:S(2)}) collective-permute-start(bf16[576,128]{1,0:T(8,128)(2,1)S(1)} %shard_map.118._), channel_id=1, source_target_pairs={{0,2},{1,3},{2,0},{3,1},{4,6},{5,7},{6,4},{7,5},{8,10},{9,11},{10,... | collective-permute-start | bytes 442376 | tf_op jit(solution)/shard_map/ppermute | solution.py:351
  39.9 8.0 %collective-permute-start.14 = (bf16[576,128]{1,0:T(8,128)(2,1)S(1)}, bf16[576,128]{1,0:T(8,128)(2,1)S(1)}, u32[]{:S(2)}, u32[]{:S(2)}) collective-permute-start(bf16[576,128]{1,0:T(8,128)(2,1)S(1)} %get-tuple-element.38), channel_id=1, source_target_pairs={{0,1},{1,0},{2,3},{3,2},{4,5},{5,4},{6,7},{7,6},{8,9},{9,8},{10,11... | collective-permute-start | bytes 442376 | tf_op jit(solution)/shard_map/ppermute | solution.py:351
